TPU v7x, 32 devices: a whole 2x2x4 slice. The times are simulated.
32 devices in a mesh: dp: 8 (over z, x), table: 4 (over y, core).
Axes of the slice: x: 2, y: 2, z: 4, core: 2. Of those that a mesh axis runs over, the one named last changes fastest.
Arguments:
- touched_rows: bfloat16 [8192, 512], P(('dp', 'table')), may hold values from -6 to 6
- row_of_token: int32 [16384], P(('dp', 'table')), may hold values from 0 to 255
- row_owner: int32 [8192, 1], P(('dp', 'table')), may hold values from 0 to 31; in each aligned block of 256 rows (0 to 255, 256 to 511, ...) at most 16 rows name the same one
- owner_row: int32 [8192], P(('dp', 'table')), may hold values from 0 to 1023
- seq_blocks: int32 [256], P(('dp', 'table')), may hold values from 1 to 4, as said below
- seq_dest: int32 [256], P(('dp', 'table')), may hold values from 0 to 7, as said below
- grad_out: bfloat16 [8192, 512], P(('dp', 'table')), may hold values from -6 to 6
- w_in: bfloat16 [512, 2048], replicated, may hold values from -0.25 to 0.25
- w_out: bfloat16 [512, 512], replicated, may hold values from -0.25 to 0.25
- gain_in: float32 [512], replicated, may hold values from 0.25 to 1.75
- gain_out: float32 [512], replicated, may hold values from 0.25 to 1.75
Outputs:
- table_grad: float32 [32768, 512], P(('dp', 'table'))
- grad_w_in: float32 [512, 2048], replicated
- grad_w_out: float32 [512, 512], replicated
- grad_gain_in: float32 [512], replicated
- grad_gain_out: float32 [512], replicated
Inputs may be any that keep to these rules, and one draw needn't show every extreme that they name: `seq_blocks`: lengths in blocks of 16 tokens. The sequences that one device receives total exactly 16 blocks, and among them one has exactly 4 blocks. `seq_dest`: the 8 slots of a device go to 8 different dp indices, so every device receives exactly one sequence from each device with its table index. `row_owner`: at most 16 of one device's touched rows have the same owner.
All inputs are finite; a program needn't handle non-finite values.
Results may differ from a plain program's by a relative error of at most 0.0091.
Values may be sent and summed in bfloat16 or wider, within the bound.
No kernel may reach another device: no remote copies, remote signals or barrier semaphores. Data moves between devices by JAX's collectives and lax.ppermute only.
A program may use at most 128 MiB of HBM per device.

v0:
```python
import math

import jax
import jax.numpy as jnp
from jax import lax
from jax.sharding import PartitionSpec as P

HEADS = 4
HDIM = 128
BLK = 16
LMAXB = 4
ROWS_DEV = 1024


EPSILON = 1e-05


def norm_rows(values, row_gain):
    centre = jnp.mean(values, axis=-1, keepdims=True)
    shifted = values - centre
    spread = jnp.mean(shifted * shifted, axis=-1, keepdims=True)
    return shifted * lax.rsqrt(spread + EPSILON) * row_gain


def silu_slope(values):
    sigma_v = jax.nn.sigmoid(values)
    return sigma_v * (1.0 + values * (1.0 - sigma_v))


def group_size(blocks_total):
    limit_blocks = max(1, 1024 // BLK)
    chosen = 1
    for candidate in range(1, min(blocks_total, limit_blocks) + 1):
        if blocks_total % candidate == 0:
            chosen = candidate
    return chosen


def group_window(slab, per_group):
    return jnp.stack([slab[offset : offset + per_group] for offset in range(LMAXB)], axis=1)


def window_sum(parts):
    per_group = parts.shape[0]
    summed = jnp.zeros((per_group + LMAXB - 1,) + parts.shape[2:], parts.dtype)
    for offset in range(LMAXB):
        summed = summed.at[offset : offset + per_group].add(parts[:, offset])
    return summed


def group_mask(segment_slab, per_group):
    seg_windows = group_window(segment_slab, per_group)
    own_segment = segment_slab[LMAXB - 1 :]
    same_segment = jnp.repeat(seg_windows == own_segment[:, None], BLK, axis=1)
    key_offsets = (
        (jnp.arange(LMAXB) - (LMAXB - 1))[:, None] * BLK + jnp.arange(BLK)[None, :]
    ).reshape(-1)
    causal = key_offsets[None, :] <= jnp.arange(BLK)[:, None]
    return same_segment[:, None, :] & causal[None]


def attend_forward(query_g, keys_g, vals_g, allowed):
    scores = jnp.einsum(
        "bqhd,bkhd->bhqk", query_g, keys_g, preferred_element_type=jnp.float32
    ) * HDIM ** (-0.5)
    weights = jnp.where(allowed[:, None], scores * jax.nn.sigmoid(scores), 0.0).astype(jnp.bfloat16)
    return jnp.einsum("bhqk,bkhd->bqhd", weights, vals_g, preferred_element_type=jnp.float32)


def attend_backward(query_g, keys_g, vals_g, allowed, grad_o):
    scores = jnp.einsum(
        "bqhd,bkhd->bhqk", query_g, keys_g, preferred_element_type=jnp.float32
    ) * HDIM ** (-0.5)
    allowed_heads = allowed[:, None]
    weights = jnp.where(allowed_heads, scores * jax.nn.sigmoid(scores), 0.0).astype(jnp.bfloat16)
    grad_weight = jnp.einsum("bqhd,bkhd->bhqk", grad_o, vals_g, preferred_element_type=jnp.float32)
    grad_score = jnp.where(
        allowed_heads, grad_weight * silu_slope(scores) * HDIM ** (-0.5), 0.0
    ).astype(jnp.bfloat16)
    grad_query = jnp.einsum(
        "bhqk,bkhd->bqhd", grad_score, keys_g, preferred_element_type=jnp.float32
    )
    grad_keywin = jnp.einsum(
        "bhqk,bqhd->bkhd", grad_score, query_g, preferred_element_type=jnp.float32
    )
    grad_valwin = jnp.einsum("bhqk,bqhd->bkhd", weights, grad_o, preferred_element_type=jnp.float32)
    return (grad_query, grad_keywin, grad_valwin)


def layer_grads(tokens, grad_y, segment, w_in, w_out, gain_in, gain_out):
    row_count, model_width = tokens.shape
    blocks_total = row_count // BLK
    per_group = group_size(blocks_total)
    group_ids = jnp.arange(blocks_total // per_group, dtype=jnp.int32)
    normed, back_in = jax.vjp(norm_rows, tokens.astype(jnp.float32), gain_in)
    normed_half = normed.astype(jnp.bfloat16)
    hidden = jnp.dot(normed_half, w_in, preferred_element_type=jnp.float32)
    active = hidden * jax.nn.sigmoid(hidden)
    gate_part = active[:, :model_width]
    head_shape = (blocks_total, BLK, HEADS, HDIM)
    value_blocks = active[:, model_width : 2 * model_width].astype(jnp.bfloat16).reshape(head_shape)
    query_blocks = (
        active[:, 2 * model_width : 3 * model_width].astype(jnp.bfloat16).reshape(head_shape)
    )
    key_blocks = active[:, 3 * model_width :].astype(jnp.bfloat16).reshape(head_shape)
    leading = jnp.zeros((LMAXB - 1, BLK, HEADS, HDIM), jnp.bfloat16)
    key_padded = jnp.concatenate([leading, key_blocks], axis=0)
    value_padded = jnp.concatenate([leading, value_blocks], axis=0)
    segment_padded = jnp.concatenate([jnp.full((LMAXB - 1,), -1, jnp.int32), segment], axis=0)

    def pieces_of():
        keys_g = group_window(key_padded, per_group).reshape(per_group, LMAXB * BLK, HEADS, HDIM)
        vals_g = group_window(value_padded, per_group).reshape(per_group, LMAXB * BLK, HEADS, HDIM)
        allowed = group_mask(segment_padded, per_group)
        return (query_blocks, keys_g, vals_g, allowed)

    def forward_group(group_id):
        query_g, keys_g, vals_g, allowed = pieces_of()
        return attend_forward(query_g, keys_g, vals_g, allowed)

    attended = lax.map(forward_group, group_ids).reshape(row_count, model_width)
    out_norm, back_out = jax.vjp(norm_rows, attended, gain_out)
    mixed = (out_norm * gate_part).astype(jnp.bfloat16)
    grad_mixed = jnp.dot(grad_y, w_out.T, preferred_element_type=jnp.float32)
    sum_w_out = jnp.dot(mixed.T, grad_y, preferred_element_type=jnp.float32)
    grad_gate = grad_mixed * out_norm
    grad_attended, sum_gain_out = back_out(grad_mixed * gate_part)
    grad_att_blocks = grad_attended.astype(jnp.bfloat16).reshape(head_shape)
    zero_slab = jnp.zeros((blocks_total + LMAXB - 1, BLK, HEADS, HDIM), jnp.float32)

    def back_step(running, group_id):
        acc_keys, acc_vals = running
        query_g, keys_g, vals_g, allowed = pieces_of()
        grad_query, grad_keywin, grad_valwin = attend_backward(
            query_g, keys_g, vals_g, allowed, grad_att_blocks
        )
        slab_keys = window_sum(grad_keywin.reshape(per_group, LMAXB, BLK, HEADS, HDIM))
        slab_vals = window_sum(grad_valwin.reshape(per_group, LMAXB, BLK, HEADS, HDIM))
        acc_keys = acc_keys + slab_keys
        acc_vals = acc_vals + slab_vals
        return ((acc_keys, acc_vals), grad_query)

    (acc_keys, acc_vals), grad_queries = lax.scan(back_step, (zero_slab, zero_slab), group_ids)
    grad_keys = acc_keys[LMAXB - 1 :].reshape(row_count, model_width)
    grad_values = acc_vals[LMAXB - 1 :].reshape(row_count, model_width)
    grad_queries = grad_queries.reshape(row_count, model_width)
    grad_active = jnp.concatenate([grad_gate, grad_values, grad_queries, grad_keys], axis=1)
    grad_hidden = (grad_active * silu_slope(hidden)).astype(jnp.bfloat16)
    sum_w_in = jnp.dot(normed_half.T, grad_hidden, preferred_element_type=jnp.float32)
    grad_normed = jnp.dot(grad_hidden, w_in.T, preferred_element_type=jnp.float32)
    grad_inner, sum_gain_in = back_in(grad_normed)
    grad_tokens = (grad_inner + grad_y.astype(jnp.float32)).astype(jnp.bfloat16)
    return (grad_tokens, (sum_w_in, sum_w_out, sum_gain_in, sum_gain_out))


def return_plan(lengths):
    starts = jnp.cumsum(lengths) - lengths
    inner = jnp.arange(LMAXB, dtype=jnp.int32)
    live = inner[None, :] < lengths[:, None]
    picks = jnp.where(live, starts[:, None] + inner[None, :], 0).astype(jnp.int32)
    return (starts, live.reshape(-1), picks.reshape(-1))


def take_blocks(rows_in, picks, live):
    blocks_in = rows_in.reshape(-1, BLK, rows_in.shape[1])
    chosen = jnp.take(blocks_in, picks, axis=0)
    return jnp.where(live[:, None, None], chosen, jnp.zeros((), chosen.dtype))


def on_device(
    touched_rows,
    row_of_token,
    row_owner,
    owner_row,
    seq_blocks,
    seq_dest,
    grad_out,
    w_in,
    w_out,
    gain_in,
    gain_out,
):
    dp_size = lax.axis_size("dp")
    table_size = lax.axis_size("table")
    devices_all = dp_size * table_size
    model_width = touched_rows.shape[1]
    slot_rows = LMAXB * BLK
    tokens = jnp.take(touched_rows, row_of_token, axis=0)
    peers = jnp.arange(dp_size, dtype=jnp.int32)
    matches = seq_dest[None, :] == peers[:, None]
    slot_for_peer = jnp.sum(jnp.where(matches, peers[None, :], 0), axis=1)
    send_lengths = jnp.take(seq_blocks, slot_for_peer)[:, None]
    send_tokens = jnp.take(tokens.reshape(dp_size, slot_rows, model_width), slot_for_peer, axis=0)
    got_tokens, got_lengths = (
        lax.all_to_all(send_tokens, "dp", split_axis=0, concat_axis=0, tiled=True),
        lax.all_to_all(send_lengths, "dp", split_axis=0, concat_axis=0, tiled=True),
    )
    lengths = got_lengths[:, 0]
    starts, live, picks = return_plan(lengths)
    bal_blocks = grad_out.shape[0] // BLK
    block_ids = jnp.arange(bal_blocks, dtype=jnp.int32)
    source = jnp.sum((starts + lengths)[None, :] <= block_ids[:, None], axis=1)
    begins = jnp.sum(jnp.where(source[:, None] == peers[None, :], starts[None, :], 0), axis=1)
    gather_ids = (source * LMAXB + block_ids - begins).astype(jnp.int32)
    bal_tokens = jnp.take(
        got_tokens.reshape(dp_size * LMAXB, BLK, model_width), gather_ids, axis=0
    ).reshape(-1, model_width)
    grad_bal, local_sums = layer_grads(bal_tokens, grad_out, source, w_in, w_out, gain_in, gain_out)
    back_blocks = take_blocks(grad_bal, picks, live).reshape(dp_size, slot_rows, model_width)
    returned = lax.all_to_all(back_blocks, "dp", split_axis=0, concat_axis=0, tiled=True)
    grad_tokens = jnp.take(returned, seq_dest, axis=0).reshape(-1, model_width)
    row_sums = jax.ops.segment_sum(
        grad_tokens.astype(jnp.float32), row_of_token, num_segments=touched_rows.shape[0]
    )
    owners = row_owner[:, 0]
    capacity = 2 * touched_rows.shape[0] // devices_all
    owner_ids = jnp.arange(devices_all, dtype=jnp.int32)
    owner_hits = (owners[:, None] == owner_ids[None, :]).astype(jnp.int32)
    ranked = jnp.sum(owner_hits * (jnp.cumsum(owner_hits, axis=0) - 1), axis=1)
    send_grad = (
        jnp.zeros((devices_all, capacity, model_width), jnp.float32)
        .at[owners, ranked]
        .set(row_sums)
    )
    send_rows = jnp.zeros((devices_all, capacity), jnp.int32).at[owners, ranked].set(owner_row)
    got_grad, got_rows = (
        lax.all_to_all(send_grad, ("dp", "table"), split_axis=0, concat_axis=0, tiled=True),
        lax.all_to_all(send_rows, ("dp", "table"), split_axis=0, concat_axis=0, tiled=True),
    )
    table_part = jax.ops.segment_sum(
        got_grad.reshape(-1, model_width), got_rows.reshape(-1), num_segments=ROWS_DEV
    )
    sum_w_in, sum_w_out, sum_gain_in, sum_gain_out = local_sums
    total_w_in, total_w_out, total_gain_in, total_gain_out = lax.psum(
        (sum_w_in, sum_w_out, sum_gain_in, sum_gain_out), ("dp", "table")
    )
    factor = 1.0 / math.sqrt(grad_out.shape[0] * devices_all)
    return (
        table_part,
        total_w_in * factor,
        total_w_out * factor,
        total_gain_in * factor,
        total_gain_out * factor,
    )


def solution(mesh):
    in_specs = (
        P(("dp", "table"), None),
        P(("dp", "table")),
        P(("dp", "table"), None),
        P(("dp", "table")),
        P(("dp", "table")),
        P(("dp", "table")),
        P(("dp", "table"), None),
        P(),
        P(),
        P(),
        P(),
    )
    out_specs = (P(("dp", "table"), None), P(), P(), P(), P())
    return jax.shard_map(
        on_device, mesh=mesh, in_specs=in_specs, out_specs=out_specs, check_vma=False
    )
```

profile of v0, /device:TPU:0, one launch (start us, length us, event | category | flops | bytes accessed | tf_op | source)
XLA Modules:
  0.0 262.9 jit_solution(743702972523533164)
XLA Ops:
  7.2 0.9 select_reduce_fusion.1
  8.1 1.3 gather_fusion
  9.4 0.7 copy.94
  10.1 7.3 %all-to-all-start.1 = ((s32[8,1,1]{2,1,0:T(1,128)}), s32[8,1,1]{2,1,0:T(1,128)S(1)}, u32[]{:S(2)}, u32[]{:S(2)}) async-start(s32[8,1,1]{2,1,0:T(1,128)} %copy.94), calls=%async_computation.1 | async-start | bytes 8192 | tf_op jit(solution)/shard_map/all_to_all | solution.py:196
  17.4 0.7 compare_and_fusion.3
  18.1 0.7 compare_select_fusion.3
  19.1 0.7 fusion.32
  19.8 2.0 gather_fusion.1
  22.5 0.9 broadcast_select_fusion.1
  24.0 6.0 %all-to-all-start.2 = ((bf16[8,64,512]{2,1,0:T(8,128)(2,1)}), bf16[8,64,512]{2,1,0:T(8,128)(2,1)S(1)}, u32[]{:S(2)}, u32[]{:S(2)}) async-start(bf16[8,64,512]{2,1,0:T(8,128)(2,1)} %broadcast_select_fusion.1), calls=%async_computation.2 | async-start | bytes 1048576 | tf_op jit(solution)/shard_map/all_to_all | solution.py:195
  31.8 12.1 %all-to-all-done.2 = bf16[8,64,512]{2,1,0:T(8,128)(2,1)S(1)} async-done(((bf16[8,64,512]{2,1,0:T(8,128)(2,1)}), bf16[8,64,512]{2,1,0:T(8,128)(2,1)S(1)}, u32[]{:S(2)}, u32[]{:S(2)}) %all-to-all-start.2) | async-done | bytes 524320 | tf_op jit(solution)/shard_map/all_to_all | solution.py:195
  45.3 2.8 %fusion.41 = (bf16[256,2048]{1,0:T(8,128)(2,1)S(1)}, f32[256,2048]{1,0:T(8,128)}, f32[256,2048]{1,0:T(8,128)}) fusion(bf16[512,2048]{1,0:T(8,128)(2,1)S(1)} %copy-done, bf16[256,512]{1,0:T(8,128)(2,1)S(1)} %bitcast_select_fusion.1, f32[512]{0:T(512)S(1)} %copy-done.17, f32[256]{0:T(256)S(1)} %rsqrt.20, f32[256]{0:T(256)S(1)} %div.52), kind=kOutput, calls=%fused_computation.166 | convolution fusion | flops 540147712 | bytes 7606272 | tf_op jit(solution)/shard_map/dot_general | solution.py:97
  48.2 0.8 stack_reshape.13
  49.0 0.8 stack_reshape.12
  49.8 0.8 reshape.883
  50.9 1.9 pad_maximum_fusion.1
  53.8 1.0 pad_maximum_fusion
  55.7 0.8 copy-done.9
  56.5 1.2 fusion.46
  57.8 1.2 multiply_reduce_fusion.4
  59.0 2.1 copy.99
  61.2 2.8 %fusion.19 = f32[512,512]{1,0:T(8,128)} fusion(bf16[256,512]{1,0:T(8,128)(2,1)} %param.35, f32[256,2048]{1,0:T(8,128)} %get-tuple-element.216, f32[32,8,4,128]{3,2,1,0:T(4,128)} %bitcast.173, f32[512]{0:T(512)S(1)} %copy-done.18, f32[256]{0:T(256)S(1)} %rsqrt.21, f32[256]{0:T(256)S(1)} %div.57), kind=kOutput, calls=%fused_computation.77 | convolution fusion | flops 134873088 | bytes 2363392 | tf_op jit(solution)/shard_map/dot_general | solution.py:125
  64.0 2.3 multiply_reduce_fusion
  66.3 1.3 fusion.40
  67.6 0.8 add_convert_fusion.1
  68.4 1.7 reshape.887
  70.2 2.2 fusion.4
  78.0 1.0 copy-done.7
  79.1 0.8 fusion
  80.0 0.8 multiply_reduce_fusion.2
  80.9 2.9 %fusion.37 = f32[512,2048]{1,0:T(8,128)} fusion(bf16[256,2048]{1,0:T(8,128)(2,1)S(1)} %fusion, bf16[256,512]{1,0:T(8,128)(2,1)S(1)} %copy-done.12, f32[512]{0:T(512)S(1)} %copy-done.17, f32[256]{0:T(256)S(1)} %rsqrt.20, f32[256]{0:T(256)S(1)} %div.52), kind=kOutput, calls=%fused_computation.162 | convolution fusion | flops 537526272 | bytes 5509120 | tf_op jit(solution)/shard_map/dot_general | solution.py:149
  84.2 0.9 copy-done.4
  86.0 1.0 fusion.17
  87.0 3.6 %all-to-all-start.3 = ((bf16[8,64,512]{2,1,0:T(8,128)(2,1)}), bf16[8,64,512]{2,1,0:T(8,128)(2,1)S(1)}, u32[]{:S(2)}, u32[]{:S(2)}) async-start(bf16[8,64,512]{2,1,0:T(8,128)(2,1)} %fusion.17), calls=%async_computation.3 | async-start | bytes 1048576 | tf_op jit(solution)/shard_map/all_to_all | solution.py:210
  91.0 12.7 %scatter_fusion = s32[32,16]{0,1:T(8,128)S(1)} fusion(s32[32,16]{0,1:T(8,128)S(1)} %broadcast_in_dim.214, s32[256]{0:T(256)S(1)} %bitcast.167, s32[256]{0:T(256)S(1)} %copy-done.20), kind=kCustom, calls=%fused_computation.6 | custom fusion | bytes 5120 | tf_op jit(solution)/shard_map/scatter | solution.py:225
  104.4 6.7 %all-to-all-done.3 = bf16[8,64,512]{2,1,0:T(8,128)(2,1)S(1)} async-done(((bf16[8,64,512]{2,1,0:T(8,128)(2,1)}), bf16[8,64,512]{2,1,0:T(8,128)(2,1)S(1)}, u32[]{:S(2)}, u32[]{:S(2)}) %all-to-all-start.3) | async-done | bytes 524320 | tf_op jit(solution)/shard_map/all_to_all | solution.py:210
  111.1 3.7 %all-to-all-start = ((s32[32,1,16]{2,1,0:T(1,128)}), s32[32,1,16]{2,1,0:T(1,128)S(1)}, u32[]{:S(2)}, u32[]{:S(2)}) async-start(s32[32,1,16]{2,1,0:T(1,128)} %copy.93), calls=%async_computation | async-start | bytes 32768 | tf_op jit(solution)/shard_map/all_to_all | solution.py:228
  115.4 0.9 broadcast_select_fusion
  116.3 4.3 %scatter_custom_fusion.1 = f32[256,512]{1,0:T(8,128)S(1)} fusion(s32[512]{0:T(512)} %param.30, bf16[512,512]{1,0:T(8,128)(2,1)} %bitcast.185, f32[]{:T(128)} %constant.359.clone.1), kind=kCustom, calls=%fused_computation.24 | custom fusion | flops 524288 | bytes 1049088 | tf_op jit(solution)/shard_map/scatter-add | solution.py:212
  120.6 1.1 broadcast_in_dim.215
  121.7 32.1 %scatter_fusion.1 = f32[32,16,512]{2,1,0:T(8,128)} fusion(f32[32,16,512]{2,1,0:T(8,128)} %broadcast_in_dim.215, s32[256]{0:T(256)S(1)} %bitcast.168, f32[256,512]{1,0:T(8,128)S(1)} %scatter_custom_fusion.1), kind=kCustom, calls=%fused_computation.8 | custom fusion | bytes 1574912 | tf_op jit(solution)/shard_map/scatter | solution.py:223
  153.8 6.0 %all-to-all-start.4 = ((f32[32,16,512]{2,1,0:T(8,128)}), f32[32,16,512]{2,1,0:T(8,128)S(1)}, u32[]{:S(2)}, u32[]{:S(2)}) async-start(f32[32,16,512]{2,1,0:T(8,128)} %scatter_fusion.1), calls=%async_computation.4 | async-start | bytes 2097152 | tf_op jit(solution)/shard_map/all_to_all | solution.py:227
  160.3 0.7 reduce.35
  161.1 48.5 %all-reduce.5 = (f32[512]{0:T(512)S(1)}, f32[512]{0:T(512)S(1)}) all-reduce(f32[512]{0:T(512)S(1)} %get-tuple-element.207, f32[512]{0:T(512)S(1)} %get-tuple-element.205), channel_id=1, replica_groups=mesh['dp'=8,'table'=4] {'dp','table'}, use_global_device_ids=true, to_apply=%region_22.24 | all-reduce | flops 1024 | bytes 8192 | tf_op jit(solution)/shard_map/psum | solution.py:234
  210.7 33.0 %all-reduce.9.cloned.1.call-done = (f32[512,2048]{1,0:T(8,128)}, f32[512,512]{1,0:T(8,128)}) async-done(((f32[512,2048]{1,0:T(8,128)}, f32[512,512]{1,0:T(8,128)}), (f32[512,2048]{1,0:T(8,128)}, f32[512,512]{1,0:T(8,128)})) %all-reduce.9.cloned.1.call-update) | async-done | bytes 5242896 | tf_op jit(solution)/shard_map/psum | solution.py:234
  243.8 2.3 broadcast_multiply_fusion.1
  246.1 5.0 %broadcast_multiply_fusion = f32[512,2048]{1,0:T(8,128)} fusion(f32[512,2048]{1,0:T(8,128)} %get-tuple-element.211), kind=kLoop, calls=%fused_computation.12 | loop fusion | flops 1048576 | bytes 8388608 | tf_op jit(solution)/shard_map/mul | solution.py:240
  251.0 5.0 %scatter_custom_fusion.3 = f32[1024,512]{1,0:T(8,128)} fusion(s32[512]{0:T(512)S(1)} %reshape.972, f32[512,512]{1,0:T(8,128)S(1)} %bitcast.189, f32[]{:T(128)} %constant.359.clone.1), kind=kCustom, calls=%fused_computation.26 | custom fusion | flops 262144 | bytes 2097156 | tf_op jit(solution)/shard_map/scatter-add | solution.py:230
  (148 shorter events, 17.6 us)
Async XLA Ops:
  7.2 38.1 %copy-start = (bf16[512,2048]{1,0:T(8,128)(2,1)S(1)}, bf16[512,2048]{1,0:T(8,128)(2,1)}, u32[]{:S(2)}) copy-start(bf16[512,2048]{1,0:T(8,128)(2,1)} %param.36) | copy-start | bytes 6291460
  7.2 12.6 %copy-start.1 = (bf16[256,512]{1,0:T(8,128)(2,1)S(1)}, bf16[256,512]{1,0:T(8,128)(2,1)}, u32[]{:S(2)}) copy-start(bf16[256,512]{1,0:T(8,128)(2,1)} %param.29) | copy-start | bytes 786436
  10.1 13.8 %all-to-all-start.1 = ((s32[8,1,1]{2,1,0:T(1,128)}), s32[8,1,1]{2,1,0:T(1,128)S(1)}, u32[]{:S(2)}, u32[]{:S(2)}) async-start(s32[8,1,1]{2,1,0:T(1,128)} %copy.94), calls=%async_computation.1 | async-start | bytes 8192 | tf_op jit(solution)/shard_map/all_to_all | solution.py:196
  22.5 22.8 %copy-start.17 = (f32[512]{0:T(512)S(1)}, f32[512]{0:T(512)}, u32[]{:S(2)}) copy-start(f32[512]{0:T(512)} %param.38) | copy-start | bytes 6148
  24.0 20.0 %all-to-all-start.2 = ((bf16[8,64,512]{2,1,0:T(8,128)(2,1)}), bf16[8,64,512]{2,1,0:T(8,128)(2,1)S(1)}, u32[]{:S(2)}, u32[]{:S(2)}) async-start(bf16[8,64,512]{2,1,0:T(8,128)(2,1)} %broadcast_select_fusion.1), calls=%async_computation.2 | async-start | bytes 1048576 | tf_op jit(solution)/shard_map/all_to_all | solution.py:195
  30.0 213.8 %all-reduce.9.cloned.1.call-start = ((), (), s32[]{:S(2)}) async-start(), calls=%async_computation.5 | async-start | bytes 10485760 | tf_op jit(solution)/shard_map/psum | solution.py:234
  45.3 2.9 %copy-start.11 = (bf16[256,512]{1,0:T(8,128)(2,1)}, bf16[256,512]{1,0:T(8,128)(2,1)S(1)}, u32[]{:S(2)}) copy-start(bf16[256,512]{1,0:T(8,128)(2,1)S(1)} %bitcast_select_fusion.1) | copy-start | bytes 786436
  52.8 1.0 copy-start.15
  53.1 2.6 copy-start.14
  53.8 1.2 copy-start.5
  55.7 0.8 copy-start.9
  56.5 4.7 %copy-start.18 = (f32[512]{0:T(512)S(1)}, f32[512]{0:T(512)}, u32[]{:S(2)}) copy-start(f32[512]{0:T(512)} %param.39) | copy-start | bytes 6148
  61.2 2.8 %copy-start.2 = (f32[16,16,4,128]{3,2,1,0:T(4,128)S(1)}, f32[16,16,4,128]{3,2,1,0:T(4,128)}, u32[]{:S(2)}) copy-start(f32[16,16,4,128]{3,2,1,0:T(4,128)} %copy.99) | copy-start | bytes 1572868
  61.2 2.8 %copy-start.3 = (bf16[256,512]{1,0:T(8,128)(2,1)S(1)}, bf16[256,512]{1,0:T(8,128)(2,1)}, u32[]{:S(2)}) copy-start(bf16[256,512]{1,0:T(8,128)(2,1)} %param.35) | copy-start | bytes 786436
  61.2 2.8 %copy-start.16 = (bf16[512,512]{1,0:T(8,128)(2,1)S(1)}, bf16[512,512]{1,0:T(8,128)(2,1)}, u32[]{:S(2)}) copy-start(bf16[512,512]{1,0:T(8,128)(2,1)} %param.37) | copy-start | bytes 1572868
  70.2 2.2 copy-start.10
  70.2 2.2 copy-start.13
  72.4 1.0 copy-start.6
  77.4 1.6 copy-start.7
  77.4 1.7 copy-start.8
  79.1 0.9 copy-start.12
  84.1 1.0 copy-start.4
  85.1 5.8 %copy-start.19 = (s32[256,1]{0,1:T(1,128)S(1)}, s32[256,1]{0,1:T(1,128)}, u32[]{:S(2)}) copy-start(s32[256,1]{0,1:T(1,128)} %param.31) | copy-start | bytes 3076
  85.1 5.9 %copy-start.20 = (s32[256]{0:T(256)S(1)}, s32[256]{0:T(256)}, u32[]{:S(2)}) copy-start(s32[256]{0:T(256)} %param.32) | copy-start | bytes 3076
  86.0 18.4 %copy-start.21 = (s32[8]{0:T(128)S(1)}, s32[8]{0:T(128)}, u32[]{:S(2)}) copy-start(s32[8]{0:T(128)} %param.34) | copy-start | bytes 100
  87.0 24.1 %all-to-all-start.3 = ((bf16[8,64,512]{2,1,0:T(8,128)(2,1)}), bf16[8,64,512]{2,1,0:T(8,128)(2,1)S(1)}, u32[]{:S(2)}, u32[]{:S(2)}) async-start(bf16[8,64,512]{2,1,0:T(8,128)(2,1)} %fusion.17), calls=%async_computation.3 | async-start | bytes 1048576 | tf_op jit(solution)/shard_map/all_to_all | solution.py:210
  111.1 42.7 %all-to-all-start = ((s32[32,1,16]{2,1,0:T(1,128)}), s32[32,1,16]{2,1,0:T(1,128)S(1)}, u32[]{:S(2)}, u32[]{:S(2)}) async-start(s32[32,1,16]{2,1,0:T(1,128)} %copy.93), calls=%async_computation | async-start | bytes 32768 | tf_op jit(solution)/shard_map/all_to_all | solution.py:228
  153.8 97.3 %all-to-all-start.4 = ((f32[32,16,512]{2,1,0:T(8,128)}), f32[32,16,512]{2,1,0:T(8,128)S(1)}, u32[]{:S(2)}, u32[]{:S(2)}) async-start(f32[32,16,512]{2,1,0:T(8,128)} %scatter_fusion.1), calls=%async_computation.4 | async-start | bytes 2097152 | tf_op jit(solution)/shard_map/all_to_all | solution.py:227
Sparse Core Ops, SparseCore 0:
  84.3 159.4 all-reduce.8
where the time goes:
time: 265 us; the launch traced here: 263 us
  local copies, waits for them, and re-layouts  67.6 us (26%)
  waiting for transfers between devices  51.9 us (20%)
  blocking collectives  48.5 us (18%)
  other arithmetic  36.5 us (14%)
  starting transfers between devices  26.6 us (10%)
  matrix products  17.1 us (6%)
  between operations  14.7 us (6%)
    psum x1, blocking collectives, on_device(): lax.psum((sum_w_in, sum_w_out, sum_gain_in, sum_gain_out), ('dp', 'table'))  48.5 us
    psum x1, waiting for transfers between devices, on_device(): lax.psum((sum_w_in, sum_w_out, sum_gain_in, sum_gain_out), ('dp', 'table'))  33 us
    scatter x1, local copies, waits for them, and re-layouts, on_device(): send_grad = jnp.zeros((devices_all, capacity, model_width), jnp.float32)....  32.1 us
    scatter x1, local copies, waits for them, and re-layouts, on_device(): jnp.zeros((devices_all, capacity), jnp.int32).at[owners, ranked]  12.7 us
    all_to_all x1, waiting for transfers between devices, on_device(): lax.all_to_all(send_tokens, 'dp', split_axis=0, concat_axis=0, tiled=True)  12.1 us
    all_to_all x1, starting transfers between devices, on_device(): lax.all_to_all(send_lengths, 'dp', split_axis=0, concat_axis=0, tiled=True)  7.25 us
    all_to_all x1, waiting for transfers between devices, on_device(): lax.all_to_all(back_blocks, 'dp', split_axis=0, concat_axis=0, tiled=True)  6.67 us
    all_to_all x1, starting transfers between devices, on_device(): lax.all_to_all(send_tokens, 'dp', split_axis=0, concat_axis=0, tiled=True)  6.01 us
  transfers between devices with their start and end apart: 6, of which 3 were waited for; matrix products, arithmetic and copies ran while one was open for 28% of the time, Pallas kernels for 0%

commit v1 on v0

v1 whole, which is shorter than its diff:
```python
import functools
import math

import jax
import jax.numpy as jnp
from jax import lax
from jax.experimental import pallas as pl
from jax.experimental.pallas import tpu as pltpu
from jax.sharding import PartitionSpec as P

HEADS = 4
HDIM = 128
BLK = 16
LMAXB = 4
SLOT = LMAXB * BLK
ROWS_DEV = 1024
TILE = 2 * SLOT
EPSILON = 1e-05
F32 = jnp.float32
BF16 = jnp.bfloat16
VMEM = pl.BlockSpec(memory_space=pltpu.VMEM)
SMEM = pl.BlockSpec(memory_space=pltpu.SMEM)


def call(body, out_shape, in_specs, flops=0, moved=0, scratch=()):
    outs = jax.tree.map(lambda _: VMEM, out_shape)
    return pl.pallas_call(
        body,
        out_shape=out_shape,
        in_specs=in_specs,
        out_specs=outs,
        scratch_shapes=scratch,
        compiler_params=pltpu.CompilerParams(vmem_limit_bytes=40 * 1024 * 1024),
        cost_estimate=pl.CostEstimate(flops=flops, bytes_accessed=moved, transcendentals=0),
    )


def shape_of(dims, dtype):
    return jax.ShapeDtypeStruct(dims, dtype)


def sigmoid(values):
    return 0.5 * jnp.tanh(0.5 * values) + 0.5


def dot(left, right, contract=((1,), (0,))):
    return lax.dot_general(left, right, (contract, ((), ())), preferred_element_type=F32)


NT = ((1,), (1,))
TN = ((0,), (0,))


def send_body(packed_ref, me_ref, grad_ref, out_ref):
    peers, slots = packed_ref.shape
    blocks = grad_ref.shape[0] // BLK
    me = me_ref[0]
    begin = jnp.int32(0)
    for peer in range(peers):

        def find(slot, length):
            entry = packed_ref[peer, slot]
            return length + jnp.where(entry >> 3 == me, entry & 7, 0)

        length = lax.fori_loop(0, slots, find, jnp.int32(0), unroll=True)
        for inner in range(LMAXB):
            block = jnp.minimum(begin + inner, blocks - 1)
            rows = grad_ref[pl.ds(pl.multiple_of(block * BLK, BLK), BLK), :]
            live = jnp.full(rows.shape, inner, jnp.int32) < length
            out_ref[peer, inner * BLK : (inner + 1) * BLK, :] = jnp.where(
                live, rows.astype(F32), 0.0
            ).astype(BF16)
        begin = begin + length


def plan_body(capacity, owner_col_ref, owner_row_ref, rows_col_ref, place_ref, ids_ref):
    count = owner_col_ref.shape[0]
    places = ids_ref.shape[1]
    across = jnp.broadcast_to(owner_row_ref[...], (count, count))
    down = jnp.broadcast_to(owner_col_ref[...], (count, count))
    same = across == down
    sub = lax.broadcasted_iota(jnp.int32, (count, count), 0)
    lane = lax.broadcasted_iota(jnp.int32, (count, count), 1)
    before_row = jnp.sum(jnp.where(same & (sub < lane), 1.0, 0.0), axis=0, keepdims=True)
    before_col = jnp.sum(jnp.where(same & (lane < sub), 1.0, 0.0), axis=1, keepdims=True)
    place_ref[...] = owner_row_ref[...] * capacity + before_row.astype(jnp.int32)
    place_col = owner_col_ref[...] * capacity + before_col.astype(jnp.int32)
    spots = lax.broadcasted_iota(jnp.int32, (count, places), 1)
    hit = spots == jnp.broadcast_to(place_col, (count, places))
    numbers = jnp.broadcast_to(rows_col_ref[...], (count, places)) + 1
    found = jnp.sum(jnp.where(hit, numbers.astype(F32), 0.0), axis=0, keepdims=True)
    ids_ref[...] = found.astype(jnp.int32) - 1


def tile_mask():
    sub = lax.broadcasted_iota(jnp.int32, (TILE, TILE), 0)
    lane = lax.broadcasted_iota(jnp.int32, (TILE, TILE), 1)
    return (sub // SLOT == lane // SLOT) & (lane <= sub)


def forward_body(
    rows_ref,
    item_ref,
    w_in_ref,
    gain_in_ref,
    gain_out_ref,
    qkv_ref,
    gate_ref,
    hat_ref,
    hat_scale_ref,
    mixed_ref,
    weight_ref,
    slope_ref,
    normed_ref,
    rows_hat_ref,
    rows_scale_ref,
    rows_slope_ref,
):
    count, width = rows_ref.shape
    tokens = item_ref.shape[0]
    values = rows_ref[...].astype(F32)
    shifted = values - jnp.mean(values, axis=-1, keepdims=True)
    scale = lax.rsqrt(jnp.mean(shifted * shifted, axis=-1, keepdims=True) + EPSILON)
    hat = shifted * scale
    rows_hat_ref[...] = hat
    rows_scale_ref[...] = scale
    normed = (hat * gain_in_ref[...]).astype(BF16)
    normed_ref[...] = normed
    lane = lax.broadcasted_iota(jnp.int32, (tokens, count), 1)
    pick = jnp.where(lane == jnp.broadcast_to(item_ref[...], (tokens, count)), 1.0, 0.0)
    pick = pick.astype(BF16)
    for part in range(4):
        columns = slice(part * width, (part + 1) * width)
        hidden = dot(normed, w_in_ref[:, columns])
        sigma = sigmoid(hidden)
        active = hidden * sigma
        rows_slope_ref[:, columns] = sigma * (1.0 + hidden * (1.0 - sigma))
        if part == 0:
            high = active.astype(BF16)
            low = (active - high.astype(F32)).astype(BF16)
            gate_ref[...] = dot(pick, high) + dot(pick, low)
        else:
            qkv_ref[:, (part - 1) * width : part * width] = dot(pick, active.astype(BF16)).astype(
                BF16
            )
    mask = tile_mask()
    factor = HDIM ** (-0.5)
    for tile in range(tokens // TILE):
        rows = slice(tile * TILE, (tile + 1) * TILE)
        parts = []
        for head in range(HEADS):
            vals, queries, keys = (
                qkv_ref[rows, part * width + head * HDIM : part * width + (head + 1) * HDIM]
                for part in range(3)
            )
            score = dot(queries, keys, NT) * factor
            sigma = sigmoid(score)
            weight = jnp.where(mask, score * sigma, 0.0).astype(BF16)
            slope = sigma * (1.0 + score * (1.0 - sigma)) * factor
            slope_ref[tile * HEADS + head] = jnp.where(mask, slope, 0.0)
            weight_ref[tile * HEADS + head] = weight
            parts.append(dot(weight, vals))
        attended = jnp.concatenate(parts, axis=1)
        shifted = attended - jnp.mean(attended, axis=-1, keepdims=True)
        scale = lax.rsqrt(jnp.mean(shifted * shifted, axis=-1, keepdims=True) + EPSILON)
        hat = shifted * scale
        hat_ref[rows, :] = hat
        hat_scale_ref[rows, :] = scale
        mixed_ref[rows, :] = (hat * gain_out_ref[...] * gate_ref[rows, :]).astype(BF16)


def backward_body(
    total_factor,
    dest_ref,
    got_ref,
    item_ref,
    place_ref,
    w_in_ref,
    w_out_ref,
    gain_in_ref,
    gain_out_ref,
    qkv_ref,
    gate_ref,
    hat_ref,
    hat_scale_ref,
    mixed_ref,
    weight_ref,
    slope_ref,
    normed_ref,
    rows_hat_ref,
    rows_scale_ref,
    rows_slope_ref,
    sums_ref,
    table_ref,
    gains_ref,
    active_ref,
    grad_y_ref,
):
    count, width = rows_hat_ref.shape
    tokens = hat_ref.shape[0]
    for slot in range(got_ref.shape[0]):
        grad_y_ref[slot * SLOT : (slot + 1) * SLOT, :] = got_ref[dest_ref[slot]]
    gain_total = jnp.zeros((1, width), F32)
    for tile in range(tokens // TILE):
        rows = slice(tile * TILE, (tile + 1) * TILE)
        grad_mixed = dot(grad_y_ref[rows, :], w_out_ref[...], NT)
        hat = hat_ref[rows, :]
        active_ref[rows, :width] = (grad_mixed * hat * gain_out_ref[...]).astype(BF16)
        inner = grad_mixed * gate_ref[rows, :]
        gain_total = gain_total + jnp.sum(inner * hat, axis=0, keepdims=True)
        inner = inner * gain_out_ref[...]
        mean = jnp.mean(inner, axis=-1, keepdims=True)
        along = jnp.mean(inner * hat, axis=-1, keepdims=True)
        grad_att = ((inner - mean - hat * along) * hat_scale_ref[rows, :]).astype(BF16)
        for head in range(HEADS):
            columns = slice(head * HDIM, (head + 1) * HDIM)
            vals, queries, keys = (
                qkv_ref[rows, part * width + head * HDIM : part * width + (head + 1) * HDIM]
                for part in range(3)
            )
            grad_o = grad_att[:, columns]
            grad_weight = dot(grad_o, vals, NT)
            grad_score = (grad_weight * slope_ref[tile * HEADS + head]).astype(BF16)
            for part, value in (
                (1, dot(weight_ref[tile * HEADS + head], grad_o, TN)),
                (2, dot(grad_score, keys)),
                (3, dot(grad_score, queries, TN)),
            ):
                first = part * width + head * HDIM
                active_ref[rows, first : first + HDIM] = value.astype(BF16)
    gains_ref[1:2, :] = gain_total * total_factor
    grad_y = grad_y_ref[...]
    sums_ref[:, 4 * width :] = (dot(mixed_ref[...], grad_y, TN) * total_factor).astype(BF16)
    sub = lax.broadcasted_iota(jnp.int32, (count, tokens), 0)
    gather = jnp.where(sub == jnp.broadcast_to(item_ref[...], (count, tokens)), 1.0, 0.0)
    gather = gather.astype(BF16)
    grad_normed = jnp.zeros((count, width), F32)
    for part in range(4):
        columns = slice(part * width, (part + 1) * width)
        summed = dot(gather, active_ref[:, columns])
        grad_hidden = (summed * rows_slope_ref[:, columns]).astype(BF16)
        sums_ref[:, columns] = (dot(normed_ref[...], grad_hidden, TN) * total_factor).astype(BF16)
        grad_normed = grad_normed + dot(grad_hidden, w_in_ref[:, columns], NT)
    hat = rows_hat_ref[...]
    gains_ref[0:1, :] = jnp.sum(grad_normed * hat, axis=0, keepdims=True) * total_factor
    inner = grad_normed * gain_in_ref[...]
    mean = jnp.mean(inner, axis=-1, keepdims=True)
    along = jnp.mean(inner * hat, axis=-1, keepdims=True)
    row_grad = (inner - mean - hat * along) * rows_scale_ref[...] + dot(gather, grad_y)
    places = table_ref.shape[0]
    spots = lax.broadcasted_iota(jnp.int32, (places, count), 0)
    spread = jnp.where(spots == jnp.broadcast_to(place_ref[...], (places, count)), 1.0, 0.0)
    table_ref[...] = dot(spread.astype(BF16), row_grad.astype(BF16)).astype(BF16)


def table_body(got_ref, ids_ref, out_ref):
    places = got_ref.shape[0]
    step = 256
    for first in range(0, out_ref.shape[0], step):
        sub = lax.broadcasted_iota(jnp.int32, (step, places), 0) + first
        hit = jnp.where(sub == jnp.broadcast_to(ids_ref[...], (step, places)), 1.0, 0.0)
        out_ref[first : first + step, :] = dot(hit.astype(BF16), got_ref[...])


def widen_body(full_ref, w_in_ref, w_out_ref):
    split = w_in_ref.shape[1]
    w_in_ref[...] = full_ref[:, :split].astype(F32)
    w_out_ref[...] = full_ref[:, split:].astype(F32)


def on_device(
    touched_rows,
    row_of_token,
    row_owner,
    owner_row,
    seq_blocks,
    seq_dest,
    grad_out,
    w_in,
    w_out,
    gain_in,
    gain_out,
):
    dp_size = lax.axis_size("dp")
    devices_all = dp_size * lax.axis_size("table")
    both = ("dp", "table")
    count, width = touched_rows.shape
    tokens = row_of_token.shape[0]
    capacity = 2 * count // devices_all
    places = devices_all * capacity
    total_factor = 1.0 / math.sqrt(grad_out.shape[0] * devices_all)
    gain_in, gain_out = gain_in[None, :], gain_out[None, :]

    packed = lax.all_gather(seq_dest * 8 + seq_blocks, "dp")
    me = lax.axis_index("dp").astype(jnp.int32)[None]
    send = call(
        send_body,
        shape_of((dp_size, SLOT, width), BF16),
        [SMEM, SMEM, VMEM],
    )(packed, me, grad_out)
    got = lax.all_to_all(send, "dp", split_axis=0, concat_axis=0, tiled=True)

    place, ids = call(
        functools.partial(plan_body, capacity),
        (shape_of((1, count), jnp.int32), shape_of((1, places), jnp.int32)),
        [VMEM] * 3,
    )(row_owner, row_owner.reshape(1, count), owner_row.reshape(count, 1))
    got_ids = lax.all_to_all(
        ids.reshape(devices_all, capacity), both, split_axis=0, concat_axis=0, tiled=True
    ).reshape(1, places)

    pairs = tokens // TILE * HEADS
    saved = call(
        forward_body,
        (
            shape_of((tokens, 3 * width), BF16),
            shape_of((tokens, width), F32),
            shape_of((tokens, width), F32),
            shape_of((tokens, 1), F32),
            shape_of((tokens, width), BF16),
            shape_of((pairs, TILE, TILE), BF16),
            shape_of((pairs, TILE, TILE), F32),
            shape_of((count, width), BF16),
            shape_of((count, width), F32),
            shape_of((count, 1), F32),
            shape_of((count, 4 * width), F32),
        ),
        [VMEM] * 5,
        flops=4 * count * width * width * 8,
        moved=10_000_000,
    )(touched_rows, row_of_token.reshape(tokens, 1), w_in, gain_in, gain_out)

    sums, table_send, gains = call(
        functools.partial(backward_body, total_factor),
        (
            shape_of((width, 5 * width), BF16),
            shape_of((places, width), BF16),
            shape_of((2, width), F32),
        ),
        [SMEM] + [VMEM] * 18,
        flops=4 * count * width * width * 20,
        moved=12_000_000,
        scratch=[pltpu.VMEM((tokens, 4 * width), BF16), pltpu.VMEM((tokens, width), BF16)],
    )(
        seq_dest,
        got,
        row_of_token.reshape(1, tokens),
        place,
        w_in,
        w_out,
        gain_in,
        gain_out,
        *saved,
    )

    shard = lax.psum_scatter(sums, both, scatter_dimension=0, tiled=True)
    full = lax.all_gather(shard, both, axis=0, tiled=True)
    table_got = lax.all_to_all(
        table_send.reshape(devices_all, capacity, width),
        both,
        split_axis=0,
        concat_axis=0,
        tiled=True,
    )
    table_part = call(
        table_body,
        shape_of((ROWS_DEV, width), F32),
        [VMEM] * 2,
    )(table_got.reshape(places, width), got_ids)
    gain_sums = jnp.sum(lax.all_gather(gains, both), axis=0)
    grad_w_in, grad_w_out = call(
        widen_body,
        (shape_of(w_in.shape, F32), shape_of(w_out.shape, F32)),
        [VMEM],
    )(full)
    return (table_part, grad_w_in, grad_w_out, gain_sums[0], gain_sums[1])


def solution(mesh):
    rows = P(("dp", "table"), None)
    flat = P(("dp", "table"))
    in_specs = (rows, flat, rows, flat, flat, flat, rows, P(), P(), P(), P())
    out_specs = (rows, P(), P(), P(), P())
    return jax.shard_map(
        on_device, mesh=mesh, in_specs=in_specs, out_specs=out_specs, check_vma=False
    )
```

time: 265 us -> 279 us (1.053)
  waiting for transfers between devices: 51.9 us -> 139 us
  local copies, waits for them, and re-layouts: 67.6 us -> 29 us
  other arithmetic: 36.5 us -> 2.19 us
  Pallas kernels: 0 us -> 20.9 us
  starting transfers between devices: 26.6 us -> 6.18 us
  blocking collectives: 48.5 us -> 66.1 us
  matrix products: 17.1 us -> 0 us
    reduce_scatter x0 -> x1, waiting for transfers between devices: none -> 139 us  [on_device(): shard = lax.psum_scatter(sums, both, scatter_dimension=0, tiled=True)]
    psum x1 -> x0, blocking collectives: 48.5 us -> none  [on_device(): lax.psum((sum_w_in, sum_w_out, sum_gain_in, sum_gain_out), ('dp', 'table'))]
    scatter x2 -> x0, local copies, waits for them, and re-layouts: 44.8 us -> none  [the longest x1 32.1 us: on_device(): send_grad = jnp.zeros((devices_all, capacity, model_width), jnp.float32)....]
    all_gather x0 -> x1, blocking collectives: none -> 44.2 us  [on_device(): gain_sums = jnp.sum(lax.all_gather(gains, both), axis=0)]
    psum x1 -> x0, waiting for transfers between devices: 33 us -> none  [on_device(): lax.psum((sum_w_in, sum_w_out, sum_gain_in, sum_gain_out), ('dp', 'table'))]
    unnamed x47 -> x63, local copies, waits for them, and re-layouts: 4.14 us -> 26.7 us
    pallas_call x0 -> x6, Pallas kernels: none -> 20.9 us  [the longest x1 9.05 us: on_device(): call(functools.partial(backward_body, total_factor), (shape_of((width, 5...]
    all_to_all x5 -> x2, starting transfers between devices: 26.6 us -> 6.1 us  [the longest x1 3.49 us: on_device(): got = lax.all_to_all(send, 'dp', split_axis=0, concat_axis=0, tiled=True)]
  transfers between devices with their start and end apart: 6 -> 4, of which waited for: 3 -> 1; matrix products, arithmetic and copies ran while one was open for 28% -> 2% of each run, Pallas kernels for 0% -> 3%
where the time goes in v1:
time: 279 us
  waiting for transfers between devices  139 us (50%)
  blocking collectives  66.1 us (24%)
  local copies, waits for them, and re-layouts  29 us (10%)
  Pallas kernels  20.9 us (7%)
  between operations  14.9 us (5%)
  starting transfers between devices  6.18 us (2%)
    reduce_scatter x1, waiting for transfers between devices, on_device(): shard = lax.psum_scatter(sums, both, scatter_dimension=0, tiled=True)  139 us
    all_gather x1, blocking collectives, on_device(): gain_sums = jnp.sum(lax.all_gather(gains, both), axis=0)  44.2 us
    unnamed x63, local copies, waits for them, and re-layouts  26.7 us
    unnamed x1, blocking collectives  13.1 us
    pallas_call x1, Pallas kernels, on_device(): call(functools.partial(backward_body, total_factor), (shape_of((width, 5...  9.05 us
    all_to_all x1, blocking collectives, on_device(): lax.all_to_all(ids.reshape(devices_all, capacity), both, split_axis=0, co...  8.83 us
  transfers between devices with their start and end apart: 4, of which 1 were waited for; matrix products, arithmetic and copies ran while one was open for 2% of the time, Pallas kernels for 3%

profile of v1, /device:TPU:0, one launch (start us, length us, event | category | flops | bytes accessed | tf_op | source)
XLA Modules:
  0.0 278.5 jit_solution(5257349450119827447)
XLA Ops:
  7.2 1.3 dynamic-slice
  9.1 0.8 add_dynamic-update-slice_fusion
  9.9 13.1 %all-reduce = s32[64]{0:T(128)S(1)} all-reduce(s32[64]{0:T(128)S(1)} %add_dynamic-update-slice_fusion), channel_id=2, replica_groups=mesh['dp'=8,'table'=4] {'dp'}, use_global_device_ids=true, to_apply=%add | all-reduce | flops 64 | bytes 512
  23.0 0.1 reshape.43.packed_ref
  23.0 1.0 copy-done.1
  24.0 1.6 shard_map.146
  25.6 3.5 %all-to-all-start = ((bf16[8,64,512]{2,1,0:T(8,128)(2,1)}), bf16[8,64,512]{2,1,0:T(8,128)(2,1)S(1)}, u32[]{:S(2)}, u32[]{:S(2)}) async-start(bf16[8,64,512]{2,1,0:T(8,128)(2,1)} %shard_map.146), calls=%async_computation | async-start | bytes 1048576 | tf_op jit(solution)/shard_map/all_to_all | solution.py:301
  29.1 0.8 copy.21.rows_col_ref
  29.9 0.8 copy.20.owner_col_ref
  30.8 0.1 copy.22.item_ref
  30.9 0.3 shard_map.147
  31.3 5.3 %shard_map.148 = (bf16[512,1536]{1,0:T(8,128)(2,1)S(1)}, f32[512,512]{1,0:T(8,128)S(1)}, f32[512,512]{1,0:T(8,128)S(1)}, f32[512,1]{1,0:T(8,128)S(1)}, bf16[512,...) custom-call(bf16[256,512]{1,0:T(8,128)(2,1)S(1)} %copy-done.7, ...), custom_call_target="tpu_custom_call" | custom-call | flops 2147483648 | bytes 10000000 | tf_op jit(solution)/shard_map/pallas_call | solution.py:313
  36.6 1.3 copy-done.10
  37.9 1.1 copy-done.12
  39.1 1.0 copy-done.14
  40.0 1.0 copy-done.16
  41.0 1.0 copy-done.18
  42.0 0.8 copy-done.20
  42.8 0.8 copy-done.22
  43.6 0.8 copy-done.24
  44.4 0.7 copy-done.26
  45.1 0.7 copy-done.28
  45.8 1.0 copy-done.6
  46.9 1.6 copy-done.11
  48.5 1.4 copy-done.13
  49.9 1.2 copy-done.15
  51.1 1.2 copy-done.17
  52.3 1.2 copy-done.19
  53.6 1.0 copy-done.21
  54.6 1.0 copy-done.23
  55.6 1.0 copy-done.25
  56.7 0.9 copy-done.27
  57.6 0.9 copy-done.29
  58.6 9.1 %shard_map.149 = (bf16[512,2560]{1,0:T(8,128)(2,1)}, bf16[512,512]{1,0:T(8,128)(2,1)}, f32[2,512]{1,0:T(2,128)S(1)}) custom-call(s32[8]{0:T(128)S(1)} %copy-done.4, bf16[8,64,512]{2,1,0:T(8,128)(2,1)S(1)} %all-to-all-done.got_ref, s32[1,512]{1,0:T(1,128)S(1)} %bitcast.18, s32[1,256]{1,0:T(1,128)S(1)} %get-tuple-element.23.place_ref, ...), custom_call_target="tpu_custom_call" | custom-call | flops 5368709120 | bytes 12000000 | tf_op jit(solution)/shard_map/pallas_call | solution.py:333
  67.7 139.2 %reduce-scatter.2.cloned.1.call-done = bf16[16,2560]{1,0:T(8,128)(2,1)} async-done(((bf16[512,2560]{1,0:T(8,128)(2,1)}), bf16[16,2560]{1,0:T(8,128)(2,1)}) %reduce-scatter.2.cloned.1.call-update) | async-done | bytes 81936 | tf_op jit(solution)/shard_map/reduce_scatter | solution.py:356
  207.0 0.5 broadcast.12
  207.5 0.7 reduce.7
  208.1 0.1 all_to_all.14
  208.2 8.8 %all_to_all.19 = s32[32,1,16]{2,1,0:T(1,128)S(1)} all-to-all(s32[32,1,16]{2,1,0:T(1,128)S(1)} %bitcast.23), channel_id=1, replica_groups=mesh['dp'=8,'table'=4] {'dp','table'}, dimensions={0} | all-to-all | bytes 4096 | tf_op jit(solution)/shard_map/all_to_all | solution.py:308
  217.1 2.6 all-to-all-start.1
  219.7 0.7 reduce.8
  220.4 0.1 reshape.42.ids_ref
  220.4 44.2 %all-gather.2 = f32[32,2,512]{2,1,0:T(2,128)S(1)} all-gather(f32[1,2,512]{2,1,0:T(2,128)S(1)} %bitcast.16), channel_id=3, replica_groups=mesh['dp'=8,'table'=4] {'dp','table'}, dimensions={0}, use_global_device_ids=true | all-gather | bytes 135168 | tf_op jit(solution)/shard_map/all_gather | solution.py:370
  264.6 0.1 reduce_sum.9
  264.7 0.6 fusion
  265.3 2.0 shard_map.150
  267.3 1.7 copy-done
  269.0 2.6 shard_map.151
  (45 shorter events, 0.2 us)
Async XLA Ops:
  7.2 23.8 %copy-start.2 = (s32[256,1]{0,1:T(1,128)S(1)}, s32[256,1]{0,1:T(1,128)}, u32[]{:S(2)}) copy-start(s32[256,1]{0,1:T(1,128)} %param.13) | copy-start | bytes 3076
  7.2 23.6 %copy-start.3 = (s32[512]{0:T(512)S(1)}, s32[512]{0:T(512)}, u32[]{:S(2)}) copy-start(s32[512]{0:T(512)} %param.12) | copy-start | bytes 6148
  7.2 24.0 %copy-start.9 = (f32[512]{0:T(512)S(1)}, f32[512]{0:T(512)}, u32[]{:S(2)}) copy-start(f32[512]{0:T(512)} %param.21) | copy-start | bytes 6148
  7.2 24.0 %copy-start.8 = (f32[512]{0:T(512)S(1)}, f32[512]{0:T(512)}, u32[]{:S(2)}) copy-start(f32[512]{0:T(512)} %param.20) | copy-start | bytes 6148
  23.0 1.0 copy-start.1
  24.0 7.2 %copy-start.5 = (bf16[512,2048]{1,0:T(8,128)(2,1)S(1)}, bf16[512,2048]{1,0:T(8,128)(2,1)}, u32[]{:S(2)}) copy-start(bf16[512,2048]{1,0:T(8,128)(2,1)} %w_in_ref.3) | copy-start | bytes 6291460
  24.0 7.3 %copy-start.7 = (bf16[256,512]{1,0:T(8,128)(2,1)S(1)}, bf16[256,512]{1,0:T(8,128)(2,1)}, u32[]{:S(2)}) copy-start(bf16[256,512]{1,0:T(8,128)(2,1)} %rows_ref.1) | copy-start | bytes 786436
  25.6 20.3 %all-to-all-start = ((bf16[8,64,512]{2,1,0:T(8,128)(2,1)}), bf16[8,64,512]{2,1,0:T(8,128)(2,1)S(1)}, u32[]{:S(2)}, u32[]{:S(2)}) async-start(bf16[8,64,512]{2,1,0:T(8,128)(2,1)} %shard_map.146), calls=%async_computation | async-start | bytes 1048576 | tf_op jit(solution)/shard_map/all_to_all | solution.py:301
  29.1 177.9 %reduce-scatter.2.cloned.1.call-start = ((), (), s32[]{:S(2)}) async-start(), calls=%async_computation.4 | async-start | bytes 2703360 | tf_op jit(solution)/shard_map/reduce_scatter | solution.py:356
  31.3 14.6 %copy-start.4 = (s32[8]{0:T(128)S(1)}, s32[8]{0:T(128)}, u32[]{:S(2)}) copy-start(s32[8]{0:T(128)} %dest_ref.1) | copy-start | bytes 100
  36.6 1.3 copy-start.10
  37.9 1.1 copy-start.12
  39.1 1.0 copy-start.14
  40.0 1.0 copy-start.16
  41.0 1.0 copy-start.18
  42.0 0.8 copy-start.20
  42.8 0.8 copy-start.22
  43.6 0.8 copy-start.24
  44.4 0.7 copy-start.26
  45.1 0.7 copy-start.28
  45.8 1.0 copy-start.6
  46.9 1.6 copy-start.11
  48.5 1.4 copy-start.13
  49.9 1.2 copy-start.15
  51.1 1.2 copy-start.17
  52.3 1.2 copy-start.19
  53.6 1.0 copy-start.21
  54.6 1.0 copy-start.23
  55.6 1.0 copy-start.25
  56.7 0.9 copy-start.27
  57.6 0.9 copy-start.29
  67.7 199.6 %all-gather.5.cloned.1.call-start = ((), (), s32[]{:S(2)}) async-start(), calls=%async_computation.5 | async-start | bytes 2703360 | tf_op jit(solution)/shard_map/all_gather | solution.py:357
  217.1 48.2 %all-to-all-start.1 = ((bf16[32,16,512]{2,1,0:T(8,128)(2,1)}), bf16[32,16,512]{2,1,0:T(8,128)(2,1)S(1)}, u32[]{:S(2)}, u32[]{:S(2)}) async-start(bf16[32,16,512]{2,1,0:T(8,128)(2,1)} %bitcast.8), calls=%async_computation.1 | async-start | bytes 1048576 | tf_op jit(solution)/shard_map/all_to_all | solution.py:358
  267.3 1.7 copy-start
Sparse Core Ops, SparseCore 0:
  67.8 139.1 reduce-scatter.1
  209.8 54.8 all-gather.4

commit v2 on v1

--- a/solution.py
+++ b/solution.py
@@ -15,6 +15,8 @@
 SLOT = LMAXB * BLK
 ROWS_DEV = 1024
 TILE = 2 * SLOT
+LANES = 128
+CHUNK_ROWS = 16
 EPSILON = 1e-05
 F32 = jnp.float32
 BF16 = jnp.bfloat16
@@ -30,7 +32,7 @@
         in_specs=in_specs,
         out_specs=outs,
         scratch_shapes=scratch,
-        compiler_params=pltpu.CompilerParams(vmem_limit_bytes=40 * 1024 * 1024),
+        compiler_params=pltpu.CompilerParams(vmem_limit_bytes=24 * 1024 * 1024),
         cost_estimate=pl.CostEstimate(flops=flops, bytes_accessed=moved, transcendentals=0),
     )
 
@@ -51,45 +53,38 @@
 TN = ((0,), (0,))
 
 
-def send_body(packed_ref, me_ref, grad_ref, out_ref):
-    peers, slots = packed_ref.shape
+def send_body(table_size, me_ref, *refs):
+    peers = (len(refs) - 2) // 2
+    packed_refs, grad_ref, out_refs, lengths_ref = (
+        refs[:peers],
+        refs[peers],
+        refs[peers + 1 : 2 * peers + 1],
+        refs[-1],
+    )
     blocks = grad_ref.shape[0] // BLK
-    me = me_ref[0]
-    begin = jnp.int32(0)
-    for peer in range(peers):
-
-        def find(slot, length):
-            entry = packed_ref[peer, slot]
+    me = me_ref[0] // table_size
+    for apart, packed_ref in enumerate(packed_refs):
+
+        def find(slot, length, packed_ref=packed_ref):
+            entry = packed_ref[slot]
             return length + jnp.where(entry >> 3 == me, entry & 7, 0)
 
-        length = lax.fori_loop(0, slots, find, jnp.int32(0), unroll=True)
+        length = lax.fori_loop(0, peers, find, jnp.int32(0), unroll=True)
+        lengths_ref[me ^ apart] = length
+    for apart, out_ref in enumerate(out_refs):
+        peer = me ^ apart
+
+        def before(other, begin, peer=peer):
+            return begin + jnp.where(other < peer, lengths_ref[other], 0)
+
+        begin = lax.fori_loop(0, peers, before, jnp.int32(0), unroll=True)
         for inner in range(LMAXB):
             block = jnp.minimum(begin + inner, blocks - 1)
             rows = grad_ref[pl.ds(pl.multiple_of(block * BLK, BLK), BLK), :]
-            live = jnp.full(rows.shape, inner, jnp.int32) < length
-            out_ref[peer, inner * BLK : (inner + 1) * BLK, :] = jnp.where(
+            live = jnp.full(rows.shape, inner, jnp.int32) < lengths_ref[peer]
+            out_ref[inner * BLK : (inner + 1) * BLK, :] = jnp.where(
                 live, rows.astype(F32), 0.0
             ).astype(BF16)
-        begin = begin + length
-
-
-def plan_body(capacity, owner_col_ref, owner_row_ref, rows_col_ref, place_ref, ids_ref):
-    count = owner_col_ref.shape[0]
-    places = ids_ref.shape[1]
-    across = jnp.broadcast_to(owner_row_ref[...], (count, count))
-    down = jnp.broadcast_to(owner_col_ref[...], (count, count))
-    same = across == down
-    sub = lax.broadcasted_iota(jnp.int32, (count, count), 0)
-    lane = lax.broadcasted_iota(jnp.int32, (count, count), 1)
-    before_row = jnp.sum(jnp.where(same & (sub < lane), 1.0, 0.0), axis=0, keepdims=True)
-    before_col = jnp.sum(jnp.where(same & (lane < sub), 1.0, 0.0), axis=1, keepdims=True)
-    place_ref[...] = owner_row_ref[...] * capacity + before_row.astype(jnp.int32)
-    place_col = owner_col_ref[...] * capacity + before_col.astype(jnp.int32)
-    spots = lax.broadcasted_iota(jnp.int32, (count, places), 1)
-    hit = spots == jnp.broadcast_to(place_col, (count, places))
-    numbers = jnp.broadcast_to(rows_col_ref[...], (count, places)) + 1
-    found = jnp.sum(jnp.where(hit, numbers.astype(F32), 0.0), axis=0, keepdims=True)
-    ids_ref[...] = found.astype(jnp.int32) - 1
 
 
 def tile_mask():
@@ -104,6 +99,9 @@
     w_in_ref,
     gain_in_ref,
     gain_out_ref,
+    owner_col_ref,
+    owner_row_ref,
+    number_ref,
     qkv_ref,
     gate_ref,
     hat_ref,
@@ -115,9 +113,21 @@
     rows_hat_ref,
     rows_scale_ref,
     rows_slope_ref,
+    rank_ref,
+    digits_ref,
 ):
     count, width = rows_ref.shape
     tokens = item_ref.shape[0]
+    across = jnp.broadcast_to(owner_row_ref[...], (count, count))
+    down = jnp.broadcast_to(owner_col_ref[...], (count, count))
+    sub = lax.broadcasted_iota(jnp.int32, (count, count), 0)
+    lane = lax.broadcasted_iota(jnp.int32, (count, count), 1)
+    earlier = jnp.where((across == down) & (sub < lane), 1.0, 0.0)
+    rank_ref[...] = jnp.sum(earlier, axis=0, keepdims=True).astype(jnp.int32)
+    number = jnp.broadcast_to(number_ref[...], (count, LANES))
+    lane = lax.broadcasted_iota(jnp.int32, (count, LANES), 1)
+    digits = jnp.where(lane == 0, number >> 5, jnp.where(lane == 1, number & 31, 0))
+    digits_ref[...] = digits.astype(F32).astype(BF16)
     values = rows_ref[...].astype(F32)
     shifted = values - jnp.mean(values, axis=-1, keepdims=True)
     scale = lax.rsqrt(jnp.mean(shifted * shifted, axis=-1, keepdims=True) + EPSILON)
@@ -170,11 +180,12 @@
 
 
 def backward_body(
+    plan,
     total_factor,
+    me_ref,
     dest_ref,
-    got_ref,
     item_ref,
-    place_ref,
+    owner_row_ref,
     w_in_ref,
     w_out_ref,
     gain_in_ref,
@@ -190,16 +201,21 @@
     rows_hat_ref,
     rows_scale_ref,
     rows_slope_ref,
-    sums_ref,
-    table_ref,
-    gains_ref,
-    active_ref,
-    grad_y_ref,
+    rank_ref,
+    digits_ref,
+    *refs,
 ):
     count, width = rows_hat_ref.shape
     tokens = hat_ref.shape[0]
-    for slot in range(got_ref.shape[0]):
-        grad_y_ref[slot * SLOT : (slot + 1) * SLOT, :] = got_ref[dest_ref[slot]]
+    peers, table_size = plan.dp_size, plan.table_size
+    got_refs, refs = refs[:peers], refs[peers:]
+    table_refs, refs = refs[:table_size], refs[table_size:]
+    part_refs, (sums_ref, active_ref, grad_y_ref, wide_ref) = refs[:4], refs[4:]
+    me = me_ref[0]
+    for slot in range(peers):
+        wide_ref[me // table_size ^ slot] = got_refs[slot][...]
+    for slot in range(peers):
+        grad_y_ref[slot * SLOT : (slot + 1) * SLOT, :] = wide_ref[dest_ref[slot]]
     gain_total = jnp.zeros((1, width), F32)
     for tile in range(tokens // TILE):
         rows = slice(tile * TILE, (tile + 1) * TILE)
@@ -228,9 +244,10 @@
             ):
                 first = part * width + head * HDIM
                 active_ref[rows, first : first + HDIM] = value.astype(BF16)
-    gains_ref[1:2, :] = gain_total * total_factor
     grad_y = grad_y_ref[...]
-    sums_ref[:, 4 * width :] = (dot(mixed_ref[...], grad_y, TN) * total_factor).astype(BF16)
+    sums_ref[:, 4 * width : 5 * width] = (dot(mixed_ref[...], grad_y, TN) * total_factor).astype(
+        BF16
+    )
     sub = lax.broadcasted_iota(jnp.int32, (count, tokens), 0)
     gather = jnp.where(sub == jnp.broadcast_to(item_ref[...], (count, tokens)), 1.0, 0.0)
     gather = gather.astype(BF16)
@@ -242,30 +259,141 @@
         sums_ref[:, columns] = (dot(normed_ref[...], grad_hidden, TN) * total_factor).astype(BF16)
         grad_normed = grad_normed + dot(grad_hidden, w_in_ref[:, columns], NT)
     hat = rows_hat_ref[...]
-    gains_ref[0:1, :] = jnp.sum(grad_normed * hat, axis=0, keepdims=True) * total_factor
+    gain_rows = jnp.concatenate(
+        [jnp.sum(grad_normed * hat, axis=0, keepdims=True), gain_total]
+        + [jnp.zeros((14, width), F32)],
+        axis=0,
+    )
+    gains = (gain_rows * total_factor).astype(BF16)
+    sums_ref[:, 5 * width : 5 * width + LANES] = dot(gains, unit(16), TN).astype(BF16)
+    if sums_ref.shape[1] > 5 * width + LANES:
+        rest = sums_ref.shape[1] - 5 * width - LANES
+        sums_ref[:, 5 * width + LANES :] = jnp.zeros((width, rest), BF16)
     inner = grad_normed * gain_in_ref[...]
     mean = jnp.mean(inner, axis=-1, keepdims=True)
     along = jnp.mean(inner * hat, axis=-1, keepdims=True)
     row_grad = (inner - mean - hat * along) * rows_scale_ref[...] + dot(gather, grad_y)
-    places = table_ref.shape[0]
-    spots = lax.broadcasted_iota(jnp.int32, (places, count), 0)
-    spread = jnp.where(spots == jnp.broadcast_to(place_ref[...], (places, count)), 1.0, 0.0)
-    table_ref[...] = dot(spread.astype(BF16), row_grad.astype(BF16)).astype(BF16)
-
-
-def table_body(got_ref, ids_ref, out_ref):
-    places = got_ref.shape[0]
+    owner = owner_row_ref[...] ^ me
+    shift = table_size.bit_length() - 1
+    place = (owner & (table_size - 1)) * peers + (owner >> shift)
+    place = place * plan.capacity + rank_ref[...]
+    row_grad = row_grad.astype(BF16)
+    held = table_refs[0].shape[0]
+    for apart, table_ref in enumerate(table_refs):
+        spots = lax.broadcasted_iota(jnp.int32, (held, count), 0) + apart * held
+        spread = jnp.where(spots == jnp.broadcast_to(place, (held, count)), 1.0, 0.0)
+        spread = spread.astype(BF16)
+        table_ref[:, :width] = dot(spread, row_grad).astype(BF16)
+        table_ref[:, width:] = dot(spread, digits_ref[...]).astype(BF16)
+    for half in range(2):
+        for place_now in range(plan.chunks):
+            out_ref = part_refs[2 * half + place_now // (plan.chunks // 2)]
+            out_ref[place_now % (plan.chunks // 2)] = sums_ref[
+                chunk_at(plan, me ^ plan.mask_of(half, place_now), half)
+            ]
+
+
+def unit(rows):
+    sub = lax.broadcasted_iota(jnp.int32, (rows, LANES), 0)
+    lane = lax.broadcasted_iota(jnp.int32, (rows, LANES), 1)
+    return jnp.where(sub == lane, 1.0, 0.0).astype(BF16)
+
+
+def chunk_at(plan, chunk, half):
+    first = pl.multiple_of((chunk & (plan.row_groups - 1)) * CHUNK_ROWS, CHUNK_ROWS)
+    begin, wide = plan.halves[half]
+    if plan.column_groups == 1:
+        return pl.ds(first, CHUNK_ROWS), slice(begin, begin + wide)
+    group = chunk >> (plan.row_groups.bit_length() - 1)
+    column = pl.multiple_of(group * wide + begin, LANES)
+    return pl.ds(first, CHUNK_ROWS), pl.ds(column, wide)
+
+
+class Plan:
+    def __init__(self, dp_size, table_size, count, width):
+        self.dp_size, self.table_size = dp_size, table_size
+        self.chunks = dp_size * table_size
+        self.capacity = 2 * count // self.chunks
+        self.row_groups = min(self.chunks, width // CHUNK_ROWS)
+        self.column_groups = self.chunks // self.row_groups
+        block = self.column_groups * LANES
+        blocks = -(-(5 * width + LANES) // block)
+        left = -(-blocks // 2)
+        self.columns = blocks * block
+        self.halves = ((0, left * LANES), (left * block, (blocks - left) * LANES))
+        table_bits = [1 << bit for bit in range(table_size.bit_length() - 1)]
+        dp_bits = [table_size << bit for bit in range(dp_size.bit_length() - 1)]
+        self.orders = (
+            table_bits + dp_bits,
+            table_bits[:1] + dp_bits[:1] + table_bits[1:] + dp_bits[1:],
+        )
+
+    def mask_of(self, half, place):
+        order = self.orders[half]
+        mask = 0
+        for step, bit in enumerate(order):
+            if place >> (len(order) - 1 - step) & 1:
+                mask ^= bit
+        return mask
+
+
+def regroup_body(plan, *refs):
+    in_refs, out_refs = refs[: plan.table_size], refs[plan.table_size :]
+    rows = out_refs[0].shape[0]
+    held = in_refs[0].shape[0]
+    capacity = plan.capacity
+    if capacity % 16 == 0:
+        for apart, out_ref in enumerate(out_refs):
+            for side, in_ref in enumerate(in_refs):
+                out_ref[side * capacity : (side + 1) * capacity, :] = in_ref[
+                    apart * capacity : (apart + 1) * capacity, :
+                ]
+        return
+    for apart, out_ref in enumerate(out_refs):
+        total = jnp.zeros(out_ref.shape, F32)
+        for side, in_ref in enumerate(in_refs):
+            sub = lax.broadcasted_iota(jnp.int32, (rows, held), 0) - side * capacity
+            lane = lax.broadcasted_iota(jnp.int32, (rows, held), 1) - apart * capacity
+            hit = (sub == lane) & (sub >= 0) & (sub < capacity)
+            total = total + dot(jnp.where(hit, 1.0, 0.0).astype(BF16), in_ref[...])
+        out_ref[...] = total.astype(BF16)
+
+
+def table_body(*refs):
+    got_refs, out_ref, full_ref = refs[:-2], refs[-2], refs[-1]
+    held = got_refs[0].shape[0]
+    for index, got_ref in enumerate(got_refs):
+        full_ref[index * held : (index + 1) * held, :] = got_ref[...]
+    places, width = full_ref.shape[0], out_ref.shape[1]
+    lane = lax.broadcasted_iota(jnp.int32, (16, LANES), 1)
+    scale = jnp.where(lane == 0, 32.0, jnp.where(lane == 1, 1.0, 0.0)).astype(BF16)
+    numbers = dot(scale, full_ref[:, width:], NT)[0:1].astype(jnp.int32)
     step = 256
     for first in range(0, out_ref.shape[0], step):
         sub = lax.broadcasted_iota(jnp.int32, (step, places), 0) + first
-        hit = jnp.where(sub == jnp.broadcast_to(ids_ref[...], (step, places)), 1.0, 0.0)
-        out_ref[first : first + step, :] = dot(hit.astype(BF16), got_ref[...])
-
-
-def widen_body(full_ref, w_in_ref, w_out_ref):
-    split = w_in_ref.shape[1]
-    w_in_ref[...] = full_ref[:, :split].astype(F32)
-    w_out_ref[...] = full_ref[:, split:].astype(F32)
+        hit = jnp.where(sub == jnp.broadcast_to(numbers, (step, places)), 1.0, 0.0)
+        out_ref[first : first + step, :] = dot(hit.astype(BF16), full_ref[:, :width])
+
+
+def widen_body(plan, me_ref, *refs):
+    part_refs, (w_in_ref, w_out_ref, gain_in_ref, gain_out_ref, sums_ref) = refs[:4], refs[4:]
+    me = me_ref[0]
+    for half in range(2):
+        for place in range(plan.chunks):
+            in_ref = part_refs[2 * half + place // (plan.chunks // 2)]
+            sums_ref[chunk_at(plan, me ^ plan.mask_of(half, place), half)] = in_ref[
+                place % (plan.chunks // 2)
+            ]
+    split, end = w_in_ref.shape[1], w_in_ref.shape[1] + w_out_ref.shape[1]
+    w_in_ref[...] = sums_ref[:, :split].astype(F32)
+    w_out_ref[...] = sums_ref[:, split:end].astype(F32)
+    gains = dot(unit(16), sums_ref[:, end : end + LANES], NT)
+    gain_in_ref[...] = gains[0:1]
+    gain_out_ref[...] = gains[1:2]
+
+
+def add(left, right):
+    return (left.astype(F32) + right.astype(F32)).astype(BF16)
 
 
 def on_device(
@@ -281,33 +409,28 @@
     gain_in,
     gain_out,
 ):
-    dp_size = lax.axis_size("dp")
-    devices_all = dp_size * lax.axis_size("table")
+    dp_size, table_size = lax.axis_size("dp"), lax.axis_size("table")
     both = ("dp", "table")
     count, width = touched_rows.shape
     tokens = row_of_token.shape[0]
-    capacity = 2 * count // devices_all
-    places = devices_all * capacity
+    plan = Plan(dp_size, table_size, count, width)
+    devices_all = plan.chunks
     total_factor = 1.0 / math.sqrt(grad_out.shape[0] * devices_all)
     gain_in, gain_out = gain_in[None, :], gain_out[None, :]
-
-    packed = lax.all_gather(seq_dest * 8 + seq_blocks, "dp")
-    me = lax.axis_index("dp").astype(jnp.int32)[None]
+    me = lax.axis_index(both).astype(jnp.int32)[None]
+
+    def swap(values, mask):
+        return lax.ppermute(values, both, [(here, here ^ mask) for here in range(devices_all)])
+
+    packed = seq_dest * 8 + seq_blocks
+    all_packed = [packed] + [swap(packed, apart * table_size) for apart in range(1, dp_size)]
     send = call(
-        send_body,
-        shape_of((dp_size, SLOT, width), BF16),
-        [SMEM, SMEM, VMEM],
-    )(packed, me, grad_out)
-    got = lax.all_to_all(send, "dp", split_axis=0, concat_axis=0, tiled=True)
-
-    place, ids = call(
-        functools.partial(plan_body, capacity),
-        (shape_of((1, count), jnp.int32), shape_of((1, places), jnp.int32)),
-        [VMEM] * 3,
-    )(row_owner, row_owner.reshape(1, count), owner_row.reshape(count, 1))
-    got_ids = lax.all_to_all(
-        ids.reshape(devices_all, capacity), both, split_axis=0, concat_axis=0, tiled=True
-    ).reshape(1, places)
+        functools.partial(send_body, table_size),
+        [shape_of((SLOT, width), BF16)] * dp_size,
+        [SMEM] * (dp_size + 1) + [VMEM],
+        scratch=[pltpu.SMEM((dp_size,), jnp.int32)],
+    )(me, *all_packed, grad_out)
+    got = [send[0]] + [swap(send[apart], apart * table_size) for apart in range(1, dp_size)]
 
     pairs = tokens // TILE * HEADS
     saved = call(
@@ -324,56 +447,97 @@
             shape_of((count, width), F32),
             shape_of((count, 1), F32),
             shape_of((count, 4 * width), F32),
+            shape_of((1, count), jnp.int32),
+            shape_of((count, LANES), BF16),
         ),
-        [VMEM] * 5,
+        [VMEM] * 8,
         flops=4 * count * width * width * 8,
         moved=10_000_000,
-    )(touched_rows, row_of_token.reshape(tokens, 1), w_in, gain_in, gain_out)
-
-    sums, table_send, gains = call(
-        functools.partial(backward_body, total_factor),
-        (
-            shape_of((width, 5 * width), BF16),
-            shape_of((places, width), BF16),
-            shape_of((2, width), F32),
-        ),
-        [SMEM] + [VMEM] * 18,
+    )(
+        touched_rows,
+        row_of_token.reshape(tokens, 1),
+        w_in,
+        gain_in,
+        gain_out,
+        row_owner,
+        row_owner.reshape(1, count),
+        owner_row.reshape(count, 1),
+    )
+
+    half_shapes = [
+        shape_of((devices_all // 2, CHUNK_ROWS, wide), BF16) for _, wide in plan.halves
+    ]
+    held = dp_size * plan.capacity
+    outs = call(
+        functools.partial(backward_body, plan, total_factor),
+        [shape_of((held, width + LANES), BF16)] * table_size
+        + [half_shapes[0], half_shapes[0], half_shapes[1], half_shapes[1]],
+        [SMEM] * 2 + [VMEM] * (19 + dp_size),
         flops=4 * count * width * width * 20,
         moved=12_000_000,
-        scratch=[pltpu.VMEM((tokens, 4 * width), BF16), pltpu.VMEM((tokens, width), BF16)],
+        scratch=[
+            pltpu.VMEM((width, plan.columns), BF16),
+            pltpu.VMEM((tokens, 4 * width), BF16),
+            pltpu.VMEM((tokens, width), BF16),
+            pltpu.VMEM((dp_size, SLOT, width), BF16),
+        ],
     )(
+        me,
         seq_dest,
-        got,
         row_of_token.reshape(1, tokens),
-        place,
+        row_owner.reshape(1, count),
         w_in,
         w_out,
         gain_in,
         gain_out,
         *saved,
-    )
-
-    shard = lax.psum_scatter(sums, both, scatter_dimension=0, tiled=True)
-    full = lax.all_gather(shard, both, axis=0, tiled=True)
-    table_got = lax.all_to_all(
-        table_send.reshape(devices_all, capacity, width),
-        both,
-        split_axis=0,
-        concat_axis=0,
-        tiled=True,
-    )
+        *got,
+    )
+    table_send, parts = outs[:table_size], outs[table_size:]
+
+    steps = len(plan.orders[0])
+    kept, sent = [parts[0], parts[2]], [parts[1], parts[3]]
+    for step in range(steps):
+        came = [swap(sent[half], plan.orders[half][step]) for half in range(2)]
+        middle = kept[0].shape[0] // 2
+        for half in range(2):
+            if middle:
+                sent[half] = add(kept[half][middle:], came[half][middle:])
+                kept[half] = add(kept[half][:middle], came[half][:middle])
+            else:
+                kept[half] = add(kept[half], came[half])
+    for step in reversed(range(steps)):
+        came = [swap(kept[half], plan.orders[half][step]) for half in range(2)]
+        if step:
+            kept = [jnp.concatenate([kept[half], came[half]]) for half in range(2)]
+
+    table_mid = [table_send[0]] + [swap(table_send[apart], apart) for apart in range(1, table_size)]
+    table_mid = call(
+        functools.partial(regroup_body, plan),
+        [shape_of((table_size * plan.capacity, width + LANES), BF16)] * dp_size,
+        [VMEM] * table_size,
+    )(*table_mid)
+    table_got = [table_mid[0]] + [
+        swap(table_mid[apart], apart * table_size) for apart in range(1, dp_size)
+    ]
     table_part = call(
         table_body,
         shape_of((ROWS_DEV, width), F32),
-        [VMEM] * 2,
-    )(table_got.reshape(places, width), got_ids)
-    gain_sums = jnp.sum(lax.all_gather(gains, both), axis=0)
-    grad_w_in, grad_w_out = call(
-        widen_body,
-        (shape_of(w_in.shape, F32), shape_of(w_out.shape, F32)),
-        [VMEM],
-    )(full)
-    return (table_part, grad_w_in, grad_w_out, gain_sums[0], gain_sums[1])
+        [VMEM] * dp_size,
+        scratch=[pltpu.VMEM((devices_all * plan.capacity, width + LANES), BF16)],
+    )(*table_got)
+    grad_w_in, grad_w_out, grad_gain_in, grad_gain_out = call(
+        functools.partial(widen_body, plan),
+        (
+            shape_of(w_in.shape, F32),
+            shape_of(w_out.shape, F32),
+            shape_of((1, width), F32),
+            shape_of((1, width), F32),
+        ),
+        [SMEM] + [VMEM] * 4,
+        scratch=[pltpu.VMEM((width, plan.columns), BF16)],
+    )(me, kept[0], came[0], kept[1], came[1])
+    return (table_part, grad_w_in, grad_w_out, grad_gain_in[0], grad_gain_out[0])
 
 
 def solution(mesh):

time: 279 us -> 157 us (0.56)
  waiting for transfers between devices: 139 us -> 63.3 us
  blocking collectives: 66.1 us -> 0 us
  starting transfers between devices: 6.18 us -> 63.1 us
  local copies, waits for them, and re-layouts: 29 us -> 8.13 us
  between operations: 14.9 us -> 0.99 us
    reduce_scatter x1 -> x0, waiting for transfers between devices: 139 us -> none  [on_device(): shard = lax.psum_scatter(sums, both, scatter_dimension=0, tiled=True)]
    ppermute x0 -> x44, waiting for transfers between devices: none -> 63.3 us  [swap(): lax.ppermute(values, both, [(here, here ^ mask) for here in range(devices...]
    ppermute x0 -> x44, starting transfers between devices: none -> 63.1 us  [swap(): lax.ppermute(values, both, [(here, here ^ mask) for here in range(devices...]
    all_gather x1 -> x0, blocking collectives: 44.2 us -> none  [on_device(): gain_sums = jnp.sum(lax.all_gather(gains, both), axis=0)]
    unnamed x63 -> x33, local copies, waits for them, and re-layouts: 26.7 us -> 6.44 us
    unnamed x1 -> x0, blocking collectives: 13.1 us -> none
    all_to_all x1 -> x0, blocking collectives: 8.83 us -> none  [on_device(): lax.all_to_all(ids.reshape(devices_all, capacity), both, split_axis=0, co...]
    all_to_all x2 -> x0, starting transfers between devices: 6.1 us -> none  [the longest x1 3.49 us: on_device(): got = lax.all_to_all(send, 'dp', split_axis=0, concat_axis=0, tiled=True)]
  transfers between devices with their start and end apart: 4 -> 44, of which waited for: 1 -> 21; matrix products, arithmetic and copies ran while one was open for 2% -> 2% of each run, Pallas kernels for 3% -> 5%
where the time goes in v2:
time: 157 us
  waiting for transfers between devices  63.3 us (40%)
  starting transfers between devices  63.1 us (40%)
  Pallas kernels  19.5 us (12%)
  local copies, waits for them, and re-layouts  8.13 us (5%)
  other arithmetic  1.67 us (1%)
    ppermute x44, waiting for transfers between devices, swap(): lax.ppermute(values, both, [(here, here ^ mask) for here in range(devices...  63.3 us
    ppermute x44, starting transfers between devices, swap(): lax.ppermute(values, both, [(here, here ^ mask) for here in range(devices...  63.1 us
    pallas_call x1, Pallas kernels, on_device(): call(functools.partial(backward_body, plan, total_factor), [shape_of((hel...  8.18 us
    unnamed x33, local copies, waits for them, and re-layouts  6.44 us
    pallas_call x1, Pallas kernels, on_device(): call(forward_body, (shape_of((tokens, 3 * width), BF16), shape_of((tokens...  5.43 us
  transfers between devices with their start and end apart: 44, of which 21 were waited for; matrix products, arithmetic and copies ran while one was open for 2% of the time, Pallas kernels for 5%

profile of v2, /device:TPU:0, one launch (start us, length us, event | category | flops | bytes accessed | tf_op | source)
XLA Modules:
  0.0 156.6 jit_solution(5408373669714545785)
XLA Ops:
  1.3 6.0 %collective-permute-start.6 = (s32[8]{0:T(128)S(1)}, s32[8]{0:T(128)S(1)}, u32[]{:S(2)}, u32[]{:S(2)}) collective-permute-start(s32[8]{0:T(128)S(1)} %multiply_add_fusion.refs_0_), channel_id=1, source_target_pairs={{0,28},{1,29},{2,30},{3,31},{4,24},{5,25},{6,26},{7,27},{8,20},{9,... | collective-permute-start | bytes 104 | tf_op jit(solution)/shard_map/ppermute | solution.py:423
  8.3 1.9 %collective-permute-start.3 = (s32[8]{0:T(128)S(1)}, s32[8]{0:T(128)S(1)}, u32[]{:S(2)}, u32[]{:S(2)}) collective-permute-start(s32[8]{0:T(128)S(1)} %multiply_add_fusion.refs_0_), channel_id=1, source_target_pairs={{0,16},{1,17},{2,18},{3,19},{4,20},{5,21},{6,22},{7,23},{8,24},{9,... | collective-permute-start | bytes 104 | tf_op jit(solution)/shard_map/ppermute | solution.py:423
  10.2 2.4 %collective-permute-start.2 = (s32[8]{0:T(128)S(1)}, s32[8]{0:T(128)S(1)}, u32[]{:S(2)}, u32[]{:S(2)}) collective-permute-start(s32[8]{0:T(128)S(1)} %multiply_add_fusion.refs_0_), channel_id=1, source_target_pairs={{0,12},{1,13},{2,14},{3,15},{4,8},{5,9},{6,10},{7,11},{8,4},{9,5},... | collective-permute-start | bytes 104 | tf_op jit(solution)/shard_map/ppermute | solution.py:423
  14.7 1.5 collective-permute-done.1.refs_2_
  16.9 0.9 copy-done
  19.1 1.5 collective-permute-start.8
  23.1 1.7 %collective-permute-start.9 = (bf16[64,512]{1,0:T(8,128)(2,1)S(1)}, bf16[64,512]{1,0:T(8,128)(2,1)S(1)}, u32[]{:S(2)}, u32[]{:S(2)}) collective-permute-start(bf16[64,512]{1,0:T(8,128)(2,1)S(1)} %get-tuple-element.62), channel_id=1, source_target_pairs={{0,12},{1,13},{2,14},{3,15},{4,8},{5,9},{6,10},{7,11},{8,4},{9,5},... | collective-permute-start | bytes 196616 | tf_op jit(solution)/shard_map/ppermute | solution.py:423
  24.8 2.2 %collective-permute-start.10 = (bf16[64,512]{1,0:T(8,128)(2,1)S(1)}, bf16[64,512]{1,0:T(8,128)(2,1)S(1)}, u32[]{:S(2)}, u32[]{:S(2)}) collective-permute-start(bf16[64,512]{1,0:T(8,128)(2,1)S(1)} %get-tuple-element.63), channel_id=1, source_target_pairs={{0,16},{1,17},{2,18},{3,19},{4,20},{5,21},{6,22},{7,23},{8,24},{9,... | collective-permute-start | bytes 196616 | tf_op jit(solution)/shard_map/ppermute | solution.py:423
  27.5 3.8 %collective-permute-start.12 = (bf16[64,512]{1,0:T(8,128)(2,1)S(1)}, bf16[64,512]{1,0:T(8,128)(2,1)S(1)}, u32[]{:S(2)}, u32[]{:S(2)}) collective-permute-start(bf16[64,512]{1,0:T(8,128)(2,1)S(1)} %get-tuple-element.65), channel_id=1, source_target_pairs={{0,24},{1,25},{2,26},{3,27},{4,28},{5,29},{6,30},{7,31},{8,16},{9,... | collective-permute-start | bytes 196616 | tf_op jit(solution)/shard_map/ppermute | solution.py:423
  31.3 1.1 collective-permute-start.13
  33.1 1.6 %copy-done.4 = bf16[512,2048]{1,0:T(8,128)(2,1)S(1)} copy-done((bf16[512,2048]{1,0:T(8,128)(2,1)S(1)}, bf16[512,2048]{1,0:T(8,128)(2,1)}, u32[]{:S(2)}) %copy-start.4) | copy-done | bytes 2097176
  34.7 0.9 copy-done.7
  37.1 5.4 %shard_map.146 = (bf16[512,1536]{1,0:T(8,128)(2,1)S(1)}, f32[512,512]{1,0:T(8,128)S(1)}, f32[512,512]{1,0:T(8,128)S(1)}, f32[512,1]{1,0:T(8,128)S(1)}, bf16[512,...) custom-call(bf16[256,512]{1,0:T(8,128)(2,1)S(1)} %copy-done.7, ...), custom_call_target="tpu_custom_call" | custom-call | flops 2147483648 | bytes 10000000 | tf_op jit(solution)/shard_map/pallas_call | solution.py:436
  42.6 8.2 %shard_map.148 = (bf16[128,640]{1,0:T(8,128)(2,1)S(1)}, bf16[128,640]{1,0:T(8,128)(2,1)S(1)}, bf16[128,640]{1,0:T(8,128)(2,1)S(1)}, bf16[128,640]{1,0:T(8,128)(2...) custom-call(s32[1]{0:T(128)} %bitcast.me_ref, ...), custom_call_target="tpu_custom_call" | custom-call | flops 5368709120 | bytes 12000000 | tf_op jit(solution)/shard_map/pallas_call | solution.py:471
  50.9 2.1 %collective-permute-done.34 = bf16[16,16,1280]{2,1,0:T(8,128)(2,1)S(1)} collective-permute-done((bf16[16,16,1280]{2,1,0:T(8,128)(2,1)S(1)}, bf16[16,16,1280]{2,1,0:T(8,128)(2,1)S(1)}, u32[]{:S(2)}, u32[]{:S(2)}) %collective-permute-start.34) | collective-permute-done | bytes 655392 | tf_op jit(solution)/shard_map/ppermute | solution.py:423
  53.6 9.4 %collective-permute-done.35 = bf16[8,16,1280]{2,1,0:T(8,128)(2,1)S(1)} collective-permute-done((bf16[8,16,1280]{2,1,0:T(8,128)(2,1)S(1)}, bf16[8,16,1280]{2,1,0:T(8,128)(2,1)S(1)}, u32[]{:S(2)}, u32[]{:S(2)}) %collective-permute-start.35) | collective-permute-done | bytes 327712 | tf_op jit(solution)/shard_map/ppermute | solution.py:423
  63.1 1.6 %collective-permute-start.36 = (bf16[4,16,1280]{2,1,0:T(8,128)(2,1)S(1)}, bf16[4,16,1280]{2,1,0:T(8,128)(2,1)S(1)}, u32[]{:S(2)}, u32[]{:S(2)}) collective-permute-start(bf16[4,16,1280]{2,1,0:T(8,128)(2,1)S(1)} %get-tuple-element.98), channel_id=1, source_target_pairs={{0,2},{1,3},{2,0},{3,1},{4,6},{5,7},{6,4},{7,5},{8,10},{9,11},{10,... | collective-permute-start | bytes 491528 | tf_op jit(solution)/shard_map/ppermute | solution.py:423
  64.6 3.9 %collective-permute-done.36 = bf16[4,16,1280]{2,1,0:T(8,128)(2,1)S(1)} collective-permute-done((bf16[4,16,1280]{2,1,0:T(8,128)(2,1)S(1)}, bf16[4,16,1280]{2,1,0:T(8,128)(2,1)S(1)}, u32[]{:S(2)}, u32[]{:S(2)}) %collective-permute-start.36) | collective-permute-done | bytes 163872 | tf_op jit(solution)/shard_map/ppermute | solution.py:423
  68.9 1.6 %collective-permute-start.25 = (bf16[8,16,1408]{2,1,0:T(8,128)(2,1)S(1)}, bf16[8,16,1408]{2,1,0:T(8,128)(2,1)S(1)}, u32[]{:S(2)}, u32[]{:S(2)}) collective-permute-start(bf16[8,16,1408]{2,1,0:T(8,128)(2,1)S(1)} %get-tuple-element.92), channel_id=1, source_target_pairs={{0,2},{1,3},{2,0},{3,1},{4,6},{5,7},{6,4},{7,5},{8,10},{9,11},{10,... | collective-permute-start | bytes 1081352 | tf_op jit(solution)/shard_map/ppermute | solution.py:423
  70.4 2.6 %collective-permute-done.37 = bf16[2,16,1280]{2,1,0:T(8,128)(2,1)S(1)} collective-permute-done((bf16[2,16,1280]{2,1,0:T(8,128)(2,1)S(1)}, bf16[2,16,1280]{2,1,0:T(8,128)(2,1)S(1)}, u32[]{:S(2)}, u32[]{:S(2)}) %collective-permute-start.37) | collective-permute-done | bytes 81952 | tf_op jit(solution)/shard_map/ppermute | solution.py:423
  73.1 2.2 %collective-permute-start.38 = (bf16[1,16,1280]{2,1,0:T(8,128)(2,1)S(1)}, bf16[1,16,1280]{2,1,0:T(8,128)(2,1)S(1)}, u32[]{:S(2)}, u32[]{:S(2)}) collective-permute-start(bf16[1,16,1280]{2,1,0:T(8,128)(2,1)S(1)} %add_convert_fusion.16), channel_id=1, source_target_pairs={{0,16},{1,17},{2,18},{3,19},{4,20},{5,21},{6,22},{7,23},{8,24},{9,... | collective-permute-start | bytes 122888 | tf_op jit(solution)/shard_map/ppermute | solution.py:423
  75.3 2.3 %collective-permute-done.25 = bf16[8,16,1408]{2,1,0:T(8,128)(2,1)S(1)} collective-permute-done((bf16[8,16,1408]{2,1,0:T(8,128)(2,1)S(1)}, bf16[8,16,1408]{2,1,0:T(8,128)(2,1)S(1)}, u32[]{:S(2)}, u32[]{:S(2)}) %collective-permute-start.25) | collective-permute-done | bytes 360480 | tf_op jit(solution)/shard_map/ppermute | solution.py:423
  78.4 4.1 %collective-permute-start.39 = (bf16[1,16,1280]{2,1,0:T(8,128)(2,1)S(1)}, bf16[1,16,1280]{2,1,0:T(8,128)(2,1)S(1)}, u32[]{:S(2)}, u32[]{:S(2)}) collective-permute-start(bf16[1,16,1280]{2,1,0:T(8,128)(2,1)S(1)} %get-tuple-element.88), channel_id=1, source_target_pairs={{0,16},{1,17},{2,18},{3,19},{4,20},{5,21},{6,22},{7,23},{8,24},{9,... | collective-permute-start | bytes 122888 | tf_op jit(solution)/shard_map/ppermute | solution.py:423
  82.5 1.0 collective-permute-done.26
  83.5 1.8 %collective-permute-start.27 = (bf16[2,16,1408]{2,1,0:T(8,128)(2,1)S(1)}, bf16[2,16,1408]{2,1,0:T(8,128)(2,1)S(1)}, u32[]{:S(2)}, u32[]{:S(2)}) collective-permute-start(bf16[2,16,1408]{2,1,0:T(8,128)(2,1)S(1)} %get-tuple-element.100), channel_id=1, source_target_pairs={{0,8},{1,9},{2,10},{3,11},{4,12},{5,13},{6,14},{7,15},{8,0},{9,1},... | collective-permute-start | bytes 270344 | tf_op jit(solution)/shard_map/ppermute | solution.py:423
  85.7 2.4 %collective-permute-done.27 = bf16[2,16,1408]{2,1,0:T(8,128)(2,1)S(1)} collective-permute-done((bf16[2,16,1408]{2,1,0:T(8,128)(2,1)S(1)}, bf16[2,16,1408]{2,1,0:T(8,128)(2,1)S(1)}, u32[]{:S(2)}, u32[]{:S(2)}) %collective-permute-start.27) | collective-permute-done | bytes 90144 | tf_op jit(solution)/shard_map/ppermute | solution.py:423
  88.1 3.9 %collective-permute-start.28 = (bf16[1,16,1408]{2,1,0:T(8,128)(2,1)S(1)}, bf16[1,16,1408]{2,1,0:T(8,128)(2,1)S(1)}, u32[]{:S(2)}, u32[]{:S(2)}) collective-permute-start(bf16[1,16,1408]{2,1,0:T(8,128)(2,1)S(1)} %add_convert_fusion.13), channel_id=1, source_target_pairs={{0,16},{1,17},{2,18},{3,19},{4,20},{5,21},{6,22},{7,23},{8,24},{9,... | collective-permute-start | bytes 135176 | tf_op jit(solution)/shard_map/ppermute | solution.py:423
  92.1 1.6 %collective-permute-start.41 = (bf16[4,16,1280]{2,1,0:T(8,128)(2,1)S(1)}, bf16[4,16,1280]{2,1,0:T(8,128)(2,1)S(1)}, u32[]{:S(2)}, u32[]{:S(2)}) collective-permute-start(bf16[4,16,1280]{2,1,0:T(8,128)(2,1)S(1)} %pad_maximum_fusion.3), channel_id=1, source_target_pairs={{0,2},{1,3},{2,0},{3,1},{4,6},{5,7},{6,4},{7,5},{8,10},{9,11},{10,... | collective-permute-start | bytes 491528 | tf_op jit(solution)/shard_map/ppermute | solution.py:423
  94.6 2.6 %collective-permute-start.29 = (bf16[1,16,1408]{2,1,0:T(8,128)(2,1)S(1)}, bf16[1,16,1408]{2,1,0:T(8,128)(2,1)S(1)}, u32[]{:S(2)}, u32[]{:S(2)}) collective-permute-start(bf16[1,16,1408]{2,1,0:T(8,128)(2,1)S(1)} %get-tuple-element.90), channel_id=1, source_target_pairs={{0,16},{1,17},{2,18},{3,19},{4,20},{5,21},{6,22},{7,23},{8,24},{9,... | collective-permute-start | bytes 135176 | tf_op jit(solution)/shard_map/ppermute | solution.py:423
  97.3 2.7 %collective-permute-done.29 = bf16[1,16,1408]{2,1,0:T(8,128)(2,1)S(1)} collective-permute-done((bf16[1,16,1408]{2,1,0:T(8,128)(2,1)S(1)}, bf16[1,16,1408]{2,1,0:T(8,128)(2,1)S(1)}, u32[]{:S(2)}, u32[]{:S(2)}) %collective-permute-start.29) | collective-permute-done | bytes 45088 | tf_op jit(solution)/shard_map/ppermute | solution.py:423
  100.1 4.4 %collective-permute-done.30 = bf16[2,16,1408]{2,1,0:T(8,128)(2,1)S(1)} collective-permute-done((bf16[2,16,1408]{2,1,0:T(8,128)(2,1)S(1)}, bf16[2,16,1408]{2,1,0:T(8,128)(2,1)S(1)}, u32[]{:S(2)}, u32[]{:S(2)}) %collective-permute-start.30) | collective-permute-done | bytes 90144 | tf_op jit(solution)/shard_map/ppermute | solution.py:423
  105.2 1.6 collective-permute-start.42
  106.8 3.3 %collective-permute-done.31 = bf16[4,16,1408]{2,1,0:T(8,128)(2,1)S(1)} collective-permute-done((bf16[4,16,1408]{2,1,0:T(8,128)(2,1)S(1)}, bf16[4,16,1408]{2,1,0:T(8,128)(2,1)S(1)}, u32[]{:S(2)}, u32[]{:S(2)}) %collective-permute-start.31) | collective-permute-done | bytes 180256 | tf_op jit(solution)/shard_map/ppermute | solution.py:423
  110.2 1.6 %collective-permute-start.32 = (bf16[8,16,1408]{2,1,0:T(8,128)(2,1)S(1)}, bf16[8,16,1408]{2,1,0:T(8,128)(2,1)S(1)}, u32[]{:S(2)}, u32[]{:S(2)}) collective-permute-start(bf16[8,16,1408]{2,1,0:T(8,128)(2,1)S(1)} %pad_maximum_fusion), channel_id=1, source_target_pairs={{0,2},{1,3},{2,0},{3,1},{4,6},{5,7},{6,4},{7,5},{8,10},{9,11},{10,... | collective-permute-start | bytes 1081352 | tf_op jit(solution)/shard_map/ppermute | solution.py:423
  111.8 5.9 %collective-permute-done.32 = bf16[8,16,1408]{2,1,0:T(8,128)(2,1)S(1)} collective-permute-done((bf16[8,16,1408]{2,1,0:T(8,128)(2,1)S(1)}, bf16[8,16,1408]{2,1,0:T(8,128)(2,1)S(1)}, u32[]{:S(2)}, u32[]{:S(2)}) %collective-permute-start.32) | collective-permute-done | bytes 360480 | tf_op jit(solution)/shard_map/ppermute | solution.py:423
  118.5 1.5 collective-permute-start.15
  121.1 4.3 %collective-permute-done.15.refs_2_ = bf16[128,640]{1,0:T(8,128)(2,1)S(1)} collective-permute-done((bf16[128,640]{1,0:T(8,128)(2,1)S(1)}, bf16[128,640]{1,0:T(8,128)(2,1)S(1)}, u32[]{:S(2)}, u32[]{:S(2)}) %collective-permute-start.15) | collective-permute-done | bytes 163872 | tf_op jit(solution)/shard_map/ppermute | solution.py:423
  125.5 2.6 %collective-permute-done.16.refs_3_ = bf16[128,640]{1,0:T(8,128)(2,1)S(1)} collective-permute-done((bf16[128,640]{1,0:T(8,128)(2,1)S(1)}, bf16[128,640]{1,0:T(8,128)(2,1)S(1)}, u32[]{:S(2)}, u32[]{:S(2)}) %collective-permute-start.16) | collective-permute-done | bytes 163872 | tf_op jit(solution)/shard_map/ppermute | solution.py:423
  128.8 2.8 %collective-permute-start.19 = (bf16[64,640]{1,0:T(8,128)(2,1)S(1)}, bf16[64,640]{1,0:T(8,128)(2,1)S(1)}, u32[]{:S(2)}, u32[]{:S(2)}) collective-permute-start(bf16[64,640]{1,0:T(8,128)(2,1)S(1)} %get-tuple-element.74), channel_id=1, source_target_pairs={{0,12},{1,13},{2,14},{3,15},{4,8},{5,9},{6,10},{7,11},{8,4},{9,5},... | collective-permute-start | bytes 245768 | tf_op jit(solution)/shard_map/ppermute | solution.py:423
  131.7 1.1 collective-permute-done.17.refs_1_
  132.8 2.3 %collective-permute-start.20 = (bf16[64,640]{1,0:T(8,128)(2,1)S(1)}, bf16[64,640]{1,0:T(8,128)(2,1)S(1)}, u32[]{:S(2)}, u32[]{:S(2)}) collective-permute-start(bf16[64,640]{1,0:T(8,128)(2,1)S(1)} %get-tuple-element.75), channel_id=1, source_target_pairs={{0,16},{1,17},{2,18},{3,19},{4,20},{5,21},{6,22},{7,23},{8,24},{9,... | collective-permute-start | bytes 245768 | tf_op jit(solution)/shard_map/ppermute | solution.py:423
  135.1 2.1 %collective-permute-start.21 = (bf16[64,640]{1,0:T(8,128)(2,1)S(1)}, bf16[64,640]{1,0:T(8,128)(2,1)S(1)}, u32[]{:S(2)}, u32[]{:S(2)}) collective-permute-start(bf16[64,640]{1,0:T(8,128)(2,1)S(1)} %get-tuple-element.76), channel_id=1, source_target_pairs={{0,20},{1,21},{2,22},{3,23},{4,16},{5,17},{6,18},{7,19},{8,28},{9,... | collective-permute-start | bytes 245768 | tf_op jit(solution)/shard_map/ppermute | solution.py:423
  137.2 1.8 %collective-permute-start.22 = (bf16[64,640]{1,0:T(8,128)(2,1)S(1)}, bf16[64,640]{1,0:T(8,128)(2,1)S(1)}, u32[]{:S(2)}, u32[]{:S(2)}) collective-permute-start(bf16[64,640]{1,0:T(8,128)(2,1)S(1)} %get-tuple-element.77), channel_id=1, source_target_pairs={{0,24},{1,25},{2,26},{3,27},{4,28},{5,29},{6,30},{7,31},{8,16},{9,... | collective-permute-start | bytes 245768 | tf_op jit(solution)/shard_map/ppermute | solution.py:423
  139.1 5.5 %collective-permute-done.20.refs_4_ = bf16[64,640]{1,0:T(8,128)(2,1)S(1)} collective-permute-done((bf16[64,640]{1,0:T(8,128)(2,1)S(1)}, bf16[64,640]{1,0:T(8,128)(2,1)S(1)}, u32[]{:S(2)}, u32[]{:S(2)}) %collective-permute-start.20) | collective-permute-done | bytes 81952 | tf_op jit(solution)/shard_map/ppermute | solution.py:423
  144.5 2.4 %collective-permute-start.23 = (bf16[64,640]{1,0:T(8,128)(2,1)S(1)}, bf16[64,640]{1,0:T(8,128)(2,1)S(1)}, u32[]{:S(2)}, u32[]{:S(2)}) collective-permute-start(bf16[64,640]{1,0:T(8,128)(2,1)S(1)} %get-tuple-element.78), channel_id=1, source_target_pairs={{0,28},{1,29},{2,30},{3,31},{4,24},{5,25},{6,26},{7,27},{8,20},{9,... | collective-permute-start | bytes 245768 | tf_op jit(solution)/shard_map/ppermute | solution.py:423
  146.9 4.8 %collective-permute-done.23.refs_7_ = bf16[64,640]{1,0:T(8,128)(2,1)S(1)} collective-permute-done((bf16[64,640]{1,0:T(8,128)(2,1)S(1)}, bf16[64,640]{1,0:T(8,128)(2,1)S(1)}, u32[]{:S(2)}, u32[]{:S(2)}) %collective-permute-start.23) | collective-permute-done | bytes 81952 | tf_op jit(solution)/shard_map/ppermute | solution.py:423
  151.7 2.2 %shard_map.150 = f32[1024,512]{1,0:T(8,128)} custom-call(bf16[64,640]{1,0:T(8,128)(2,1)S(1)} %get-tuple-element.71.refs_0_, bf16[64,640]{1,0:T(8,128)(2,1)S(1)} %collective-permute-done.17.refs_1_, bf16[64,640]{1,0:T(8,128)(2,1)S(1)} %collective-permute-done.18.refs_2_, bf16[64,640]{1,0:T(8,128)(2,1)S(1)} %collective-permute-done.19.refs_3_, ...), custom_call_target="tpu_custom_call" | custom-call | tf_op jit(solution)/shard_map/pallas_call | solution.py:523
  153.8 2.8 %shard_map.151 = (f32[512,2048]{1,0:T(8,128)}, f32[512,512]{1,0:T(8,128)}, f32[1,512]{1,0:T(1,128)}, f32[1,512]{1,0:T(1,128)}) custom-call(s32[1]{0:T(128)} %bitcast.me_ref, bf16[16,16,1408]{2,1,0:T(8,128)(2,1)S(1)} %constant_dynamic-update-slice_fusion.refs_0_, bf16[16,16,1408]{2,1,0:T(8,128)(2,1)S(1)} %collective-permute-done.33.refs_1_, ...), custom_call_target="tpu_custom_call" | custom-call | tf_op jit(solution)/shard_map/pallas_call | solution.py:529
  (100 shorter events, 17.7 us)
Async XLA Ops:
  1.3 11.3 %collective-permute-start.6 = (s32[8]{0:T(128)S(1)}, s32[8]{0:T(128)S(1)}, u32[]{:S(2)}, u32[]{:S(2)}) collective-permute-start(s32[8]{0:T(128)S(1)} %multiply_add_fusion.refs_0_), channel_id=1, source_target_pairs={{0,28},{1,29},{2,30},{3,31},{4,24},{5,25},{6,26},{7,27},{8,20},{9,... | collective-permute-start | bytes 104 | tf_op jit(solution)/shard_map/ppermute | solution.py:423
  7.3 6.1 %collective-permute-start.5 = (s32[8]{0:T(128)S(1)}, s32[8]{0:T(128)S(1)}, u32[]{:S(2)}, u32[]{:S(2)}) collective-permute-start(s32[8]{0:T(128)S(1)} %multiply_add_fusion.refs_0_), channel_id=1, source_target_pairs={{0,24},{1,25},{2,26},{3,27},{4,28},{5,29},{6,30},{7,31},{8,16},{9,... | collective-permute-start | bytes 104 | tf_op jit(solution)/shard_map/ppermute | solution.py:423
  7.5 6.2 %collective-permute-start.4 = (s32[8]{0:T(128)S(1)}, s32[8]{0:T(128)S(1)}, u32[]{:S(2)}, u32[]{:S(2)}) collective-permute-start(s32[8]{0:T(128)S(1)} %multiply_add_fusion.refs_0_), channel_id=1, source_target_pairs={{0,20},{1,21},{2,22},{3,23},{4,16},{5,17},{6,18},{7,19},{8,28},{9,... | collective-permute-start | bytes 104 | tf_op jit(solution)/shard_map/ppermute | solution.py:423
  8.3 5.4 %collective-permute-start.3 = (s32[8]{0:T(128)S(1)}, s32[8]{0:T(128)S(1)}, u32[]{:S(2)}, u32[]{:S(2)}) collective-permute-start(s32[8]{0:T(128)S(1)} %multiply_add_fusion.refs_0_), channel_id=1, source_target_pairs={{0,16},{1,17},{2,18},{3,19},{4,20},{5,21},{6,22},{7,23},{8,24},{9,... | collective-permute-start | bytes 104 | tf_op jit(solution)/shard_map/ppermute | solution.py:423
  10.2 4.4 %collective-permute-start.2 = (s32[8]{0:T(128)S(1)}, s32[8]{0:T(128)S(1)}, u32[]{:S(2)}, u32[]{:S(2)}) collective-permute-start(s32[8]{0:T(128)S(1)} %multiply_add_fusion.refs_0_), channel_id=1, source_target_pairs={{0,12},{1,13},{2,14},{3,15},{4,8},{5,9},{6,10},{7,11},{8,4},{9,5},... | collective-permute-start | bytes 104 | tf_op jit(solution)/shard_map/ppermute | solution.py:423
  12.6 3.5 %collective-permute-start.1 = (s32[8]{0:T(128)S(1)}, s32[8]{0:T(128)S(1)}, u32[]{:S(2)}, u32[]{:S(2)}) collective-permute-start(s32[8]{0:T(128)S(1)} %multiply_add_fusion.refs_0_), channel_id=1, source_target_pairs={{0,8},{1,9},{2,10},{3,11},{4,12},{5,13},{6,14},{7,15},{8,0},{9,1},... | collective-permute-start | bytes 104 | tf_op jit(solution)/shard_map/ppermute | solution.py:423
  13.4 3.5 %collective-permute-start = (s32[8]{0:T(128)S(1)}, s32[8]{0:T(128)S(1)}, u32[]{:S(2)}, u32[]{:S(2)}) collective-permute-start(s32[8]{0:T(128)S(1)} %multiply_add_fusion.refs_0_), channel_id=1, source_target_pairs={{0,4},{1,5},{2,6},{3,7},{4,0},{5,1},{6,2},{7,3},{8,12},{9,13},{10,... | collective-permute-start | bytes 104 | tf_op jit(solution)/shard_map/ppermute | solution.py:423
  18.7 8.8 %collective-permute-start.7 = (bf16[64,512]{1,0:T(8,128)(2,1)S(1)}, bf16[64,512]{1,0:T(8,128)(2,1)S(1)}, u32[]{:S(2)}, u32[]{:S(2)}) collective-permute-start(bf16[64,512]{1,0:T(8,128)(2,1)S(1)} %get-tuple-element.60), channel_id=1, source_target_pairs={{0,4},{1,5},{2,6},{3,7},{4,0},{5,1},{6,2},{7,3},{8,12},{9,13},{10,... | collective-permute-start | bytes 196616 | tf_op jit(solution)/shard_map/ppermute | solution.py:423
  19.1 12.2 %collective-permute-start.8 = (bf16[64,512]{1,0:T(8,128)(2,1)S(1)}, bf16[64,512]{1,0:T(8,128)(2,1)S(1)}, u32[]{:S(2)}, u32[]{:S(2)}) collective-permute-start(bf16[64,512]{1,0:T(8,128)(2,1)S(1)} %get-tuple-element.61), channel_id=1, source_target_pairs={{0,8},{1,9},{2,10},{3,11},{4,12},{5,13},{6,14},{7,15},{8,0},{9,1},... | collective-permute-start | bytes 196616 | tf_op jit(solution)/shard_map/ppermute | solution.py:423
  23.1 19.5 %collective-permute-start.9 = (bf16[64,512]{1,0:T(8,128)(2,1)S(1)}, bf16[64,512]{1,0:T(8,128)(2,1)S(1)}, u32[]{:S(2)}, u32[]{:S(2)}) collective-permute-start(bf16[64,512]{1,0:T(8,128)(2,1)S(1)} %get-tuple-element.62), channel_id=1, source_target_pairs={{0,12},{1,13},{2,14},{3,15},{4,8},{5,9},{6,10},{7,11},{8,4},{9,5},... | collective-permute-start | bytes 196616 | tf_op jit(solution)/shard_map/ppermute | solution.py:423
  24.8 17.7 %collective-permute-start.10 = (bf16[64,512]{1,0:T(8,128)(2,1)S(1)}, bf16[64,512]{1,0:T(8,128)(2,1)S(1)}, u32[]{:S(2)}, u32[]{:S(2)}) collective-permute-start(bf16[64,512]{1,0:T(8,128)(2,1)S(1)} %get-tuple-element.63), channel_id=1, source_target_pairs={{0,16},{1,17},{2,18},{3,19},{4,20},{5,21},{6,22},{7,23},{8,24},{9,... | collective-permute-start | bytes 196616 | tf_op jit(solution)/shard_map/ppermute | solution.py:423
  27.0 15.5 %collective-permute-start.11 = (bf16[64,512]{1,0:T(8,128)(2,1)S(1)}, bf16[64,512]{1,0:T(8,128)(2,1)S(1)}, u32[]{:S(2)}, u32[]{:S(2)}) collective-permute-start(bf16[64,512]{1,0:T(8,128)(2,1)S(1)} %get-tuple-element.64), channel_id=1, source_target_pairs={{0,20},{1,21},{2,22},{3,23},{4,16},{5,17},{6,18},{7,19},{8,28},{9,... | collective-permute-start | bytes 196616 | tf_op jit(solution)/shard_map/ppermute | solution.py:423
  27.5 15.0 %collective-permute-start.12 = (bf16[64,512]{1,0:T(8,128)(2,1)S(1)}, bf16[64,512]{1,0:T(8,128)(2,1)S(1)}, u32[]{:S(2)}, u32[]{:S(2)}) collective-permute-start(bf16[64,512]{1,0:T(8,128)(2,1)S(1)} %get-tuple-element.65), channel_id=1, source_target_pairs={{0,24},{1,25},{2,26},{3,27},{4,28},{5,29},{6,30},{7,31},{8,16},{9,... | collective-permute-start | bytes 196616 | tf_op jit(solution)/shard_map/ppermute | solution.py:423
  31.3 11.3 %collective-permute-start.13 = (bf16[64,512]{1,0:T(8,128)(2,1)S(1)}, bf16[64,512]{1,0:T(8,128)(2,1)S(1)}, u32[]{:S(2)}, u32[]{:S(2)}) collective-permute-start(bf16[64,512]{1,0:T(8,128)(2,1)S(1)} %get-tuple-element.66), channel_id=1, source_target_pairs={{0,28},{1,29},{2,30},{3,31},{4,24},{5,25},{6,26},{7,27},{8,20},{9,... | collective-permute-start | bytes 196616 | tf_op jit(solution)/shard_map/ppermute | solution.py:423
  37.1 5.6 %copy-start.6 = (bf16[512,512]{1,0:T(8,128)(2,1)S(1)}, bf16[512,512]{1,0:T(8,128)(2,1)}, u32[]{:S(2)}) copy-start(bf16[512,512]{1,0:T(8,128)(2,1)} %w_out_ref.1) | copy-start | bytes 1572868
  37.1 5.6 %copy-start.9 = (f32[512]{0:T(512)S(1)}, f32[512]{0:T(512)}, u32[]{:S(2)}) copy-start(f32[512]{0:T(512)} %param.20) | copy-start | bytes 6148
  37.1 5.6 %copy-start.11 = (f32[512]{0:T(512)S(1)}, f32[512]{0:T(512)}, u32[]{:S(2)}) copy-start(f32[512]{0:T(512)} %param.21) | copy-start | bytes 6148
  37.1 5.6 %copy-start.12 = (s32[8]{0:T(128)S(1)}, s32[8]{0:T(128)}, u32[]{:S(2)}) copy-start(s32[8]{0:T(128)} %dest_ref.1) | copy-start | bytes 100
  50.8 2.2 %collective-permute-start.34 = (bf16[16,16,1280]{2,1,0:T(8,128)(2,1)S(1)}, bf16[16,16,1280]{2,1,0:T(8,128)(2,1)S(1)}, u32[]{:S(2)}, u32[]{:S(2)}) collective-permute-start(bf16[16,16,1280]{2,1,0:T(8,128)(2,1)S(1)} %get-tuple-element.82), channel_id=1, source_target_pairs={{0,1},{1,0},{2,3},{3,2},{4,5},{5,4},{6,7},{7,6},{8,9},{9,8},{10,11... | collective-permute-start | bytes 1966088 | tf_op jit(solution)/shard_map/ppermute | solution.py:423
  53.2 9.8 %collective-permute-start.35 = (bf16[8,16,1280]{2,1,0:T(8,128)(2,1)S(1)}, bf16[8,16,1280]{2,1,0:T(8,128)(2,1)S(1)}, u32[]{:S(2)}, u32[]{:S(2)}) collective-permute-start(bf16[8,16,1280]{2,1,0:T(8,128)(2,1)S(1)} %get-tuple-element.94), channel_id=1, source_target_pairs={{0,4},{1,5},{2,6},{3,7},{4,0},{5,1},{6,2},{7,3},{8,12},{9,13},{10,... | collective-permute-start | bytes 983048 | tf_op jit(solution)/shard_map/ppermute | solution.py:423
  53.6 15.1 %collective-permute-start.24 = (bf16[16,16,1408]{2,1,0:T(8,128)(2,1)S(1)}, bf16[16,16,1408]{2,1,0:T(8,128)(2,1)S(1)}, u32[]{:S(2)}, u32[]{:S(2)}) collective-permute-start(bf16[16,16,1408]{2,1,0:T(8,128)(2,1)S(1)} %get-tuple-element.80), channel_id=1, source_target_pairs={{0,1},{1,0},{2,3},{3,2},{4,5},{5,4},{6,7},{7,6},{8,9},{9,8},{10,11... | collective-permute-start | bytes 2162696 | tf_op jit(solution)/shard_map/ppermute | solution.py:423
  63.1 5.5 %collective-permute-start.36 = (bf16[4,16,1280]{2,1,0:T(8,128)(2,1)S(1)}, bf16[4,16,1280]{2,1,0:T(8,128)(2,1)S(1)}, u32[]{:S(2)}, u32[]{:S(2)}) collective-permute-start(bf16[4,16,1280]{2,1,0:T(8,128)(2,1)S(1)} %get-tuple-element.98), channel_id=1, source_target_pairs={{0,2},{1,3},{2,0},{3,1},{4,6},{5,7},{6,4},{7,5},{8,10},{9,11},{10,... | collective-permute-start | bytes 491528 | tf_op jit(solution)/shard_map/ppermute | solution.py:423
  68.6 4.5 %collective-permute-start.37 = (bf16[2,16,1280]{2,1,0:T(8,128)(2,1)S(1)}, bf16[2,16,1280]{2,1,0:T(8,128)(2,1)S(1)}, u32[]{:S(2)}, u32[]{:S(2)}) collective-permute-start(bf16[2,16,1280]{2,1,0:T(8,128)(2,1)S(1)} %get-tuple-element.102), channel_id=1, source_target_pairs={{0,8},{1,9},{2,10},{3,11},{4,12},{5,13},{6,14},{7,15},{8,0},{9,1},... | collective-permute-start | bytes 245768 | tf_op jit(solution)/shard_map/ppermute | solution.py:423
  68.9 8.8 %collective-permute-start.25 = (bf16[8,16,1408]{2,1,0:T(8,128)(2,1)S(1)}, bf16[8,16,1408]{2,1,0:T(8,128)(2,1)S(1)}, u32[]{:S(2)}, u32[]{:S(2)}) collective-permute-start(bf16[8,16,1408]{2,1,0:T(8,128)(2,1)S(1)} %get-tuple-element.92), channel_id=1, source_target_pairs={{0,2},{1,3},{2,0},{3,1},{4,6},{5,7},{6,4},{7,5},{8,10},{9,11},{10,... | collective-permute-start | bytes 1081352 | tf_op jit(solution)/shard_map/ppermute | solution.py:423
  73.1 5.2 %collective-permute-start.38 = (bf16[1,16,1280]{2,1,0:T(8,128)(2,1)S(1)}, bf16[1,16,1280]{2,1,0:T(8,128)(2,1)S(1)}, u32[]{:S(2)}, u32[]{:S(2)}) collective-permute-start(bf16[1,16,1280]{2,1,0:T(8,128)(2,1)S(1)} %add_convert_fusion.16), channel_id=1, source_target_pairs={{0,16},{1,17},{2,18},{3,19},{4,20},{5,21},{6,22},{7,23},{8,24},{9,... | collective-permute-start | bytes 122888 | tf_op jit(solution)/shard_map/ppermute | solution.py:423
  77.9 5.6 %collective-permute-start.26 = (bf16[4,16,1408]{2,1,0:T(8,128)(2,1)S(1)}, bf16[4,16,1408]{2,1,0:T(8,128)(2,1)S(1)}, u32[]{:S(2)}, u32[]{:S(2)}) collective-permute-start(bf16[4,16,1408]{2,1,0:T(8,128)(2,1)S(1)} %get-tuple-element.96), channel_id=1, source_target_pairs={{0,4},{1,5},{2,6},{3,7},{4,0},{5,1},{6,2},{7,3},{8,12},{9,13},{10,... | collective-permute-start | bytes 540680 | tf_op jit(solution)/shard_map/ppermute | solution.py:423
  78.4 6.9 %collective-permute-start.39 = (bf16[1,16,1280]{2,1,0:T(8,128)(2,1)S(1)}, bf16[1,16,1280]{2,1,0:T(8,128)(2,1)S(1)}, u32[]{:S(2)}, u32[]{:S(2)}) collective-permute-start(bf16[1,16,1280]{2,1,0:T(8,128)(2,1)S(1)} %get-tuple-element.88), channel_id=1, source_target_pairs={{0,16},{1,17},{2,18},{3,19},{4,20},{5,21},{6,22},{7,23},{8,24},{9,... | collective-permute-start | bytes 122888 | tf_op jit(solution)/shard_map/ppermute | solution.py:423
  83.5 4.6 %collective-permute-start.27 = (bf16[2,16,1408]{2,1,0:T(8,128)(2,1)S(1)}, bf16[2,16,1408]{2,1,0:T(8,128)(2,1)S(1)}, u32[]{:S(2)}, u32[]{:S(2)}) collective-permute-start(bf16[2,16,1408]{2,1,0:T(8,128)(2,1)S(1)} %get-tuple-element.100), channel_id=1, source_target_pairs={{0,8},{1,9},{2,10},{3,11},{4,12},{5,13},{6,14},{7,15},{8,0},{9,1},... | collective-permute-start | bytes 270344 | tf_op jit(solution)/shard_map/ppermute | solution.py:423
  85.3 6.7 %collective-permute-start.40 = (bf16[2,16,1280]{2,1,0:T(8,128)(2,1)S(1)}, bf16[2,16,1280]{2,1,0:T(8,128)(2,1)S(1)}, u32[]{:S(2)}, u32[]{:S(2)}) collective-permute-start(bf16[2,16,1280]{2,1,0:T(8,128)(2,1)S(1)} %pad_maximum_fusion.5), channel_id=1, source_target_pairs={{0,8},{1,9},{2,10},{3,11},{4,12},{5,13},{6,14},{7,15},{8,0},{9,1},... | collective-permute-start | bytes 245768 | tf_op jit(solution)/shard_map/ppermute | solution.py:423
  88.1 6.4 %collective-permute-start.28 = (bf16[1,16,1408]{2,1,0:T(8,128)(2,1)S(1)}, bf16[1,16,1408]{2,1,0:T(8,128)(2,1)S(1)}, u32[]{:S(2)}, u32[]{:S(2)}) collective-permute-start(bf16[1,16,1408]{2,1,0:T(8,128)(2,1)S(1)} %add_convert_fusion.13), channel_id=1, source_target_pairs={{0,16},{1,17},{2,18},{3,19},{4,20},{5,21},{6,22},{7,23},{8,24},{9,... | collective-permute-start | bytes 135176 | tf_op jit(solution)/shard_map/ppermute | solution.py:423
  92.1 13.1 %collective-permute-start.41 = (bf16[4,16,1280]{2,1,0:T(8,128)(2,1)S(1)}, bf16[4,16,1280]{2,1,0:T(8,128)(2,1)S(1)}, u32[]{:S(2)}, u32[]{:S(2)}) collective-permute-start(bf16[4,16,1280]{2,1,0:T(8,128)(2,1)S(1)} %pad_maximum_fusion.3), channel_id=1, source_target_pairs={{0,2},{1,3},{2,0},{3,1},{4,6},{5,7},{6,4},{7,5},{8,10},{9,11},{10,... | collective-permute-start | bytes 491528 | tf_op jit(solution)/shard_map/ppermute | solution.py:423
  94.6 5.3 %collective-permute-start.29 = (bf16[1,16,1408]{2,1,0:T(8,128)(2,1)S(1)}, bf16[1,16,1408]{2,1,0:T(8,128)(2,1)S(1)}, u32[]{:S(2)}, u32[]{:S(2)}) collective-permute-start(bf16[1,16,1408]{2,1,0:T(8,128)(2,1)S(1)} %get-tuple-element.90), channel_id=1, source_target_pairs={{0,16},{1,17},{2,18},{3,19},{4,20},{5,21},{6,22},{7,23},{8,24},{9,... | collective-permute-start | bytes 135176 | tf_op jit(solution)/shard_map/ppermute | solution.py:423
  99.9 4.6 %collective-permute-start.30 = (bf16[2,16,1408]{2,1,0:T(8,128)(2,1)S(1)}, bf16[2,16,1408]{2,1,0:T(8,128)(2,1)S(1)}, u32[]{:S(2)}, u32[]{:S(2)}) collective-permute-start(bf16[2,16,1408]{2,1,0:T(8,128)(2,1)S(1)} %pad_maximum_fusion.4), channel_id=1, source_target_pairs={{0,8},{1,9},{2,10},{3,11},{4,12},{5,13},{6,14},{7,15},{8,0},{9,1},... | collective-permute-start | bytes 270344 | tf_op jit(solution)/shard_map/ppermute | solution.py:423
  104.6 5.6 %collective-permute-start.31 = (bf16[4,16,1408]{2,1,0:T(8,128)(2,1)S(1)}, bf16[4,16,1408]{2,1,0:T(8,128)(2,1)S(1)}, u32[]{:S(2)}, u32[]{:S(2)}) collective-permute-start(bf16[4,16,1408]{2,1,0:T(8,128)(2,1)S(1)} %pad_maximum_fusion.2), channel_id=1, source_target_pairs={{0,4},{1,5},{2,6},{3,7},{4,0},{5,1},{6,2},{7,3},{8,12},{9,13},{10,... | collective-permute-start | bytes 540680 | tf_op jit(solution)/shard_map/ppermute | solution.py:423
  105.2 12.6 %collective-permute-start.42 = (bf16[8,16,1280]{2,1,0:T(8,128)(2,1)S(1)}, bf16[8,16,1280]{2,1,0:T(8,128)(2,1)S(1)}, u32[]{:S(2)}, u32[]{:S(2)}) collective-permute-start(bf16[8,16,1280]{2,1,0:T(8,128)(2,1)S(1)} %pad_maximum_fusion.1), channel_id=1, source_target_pairs={{0,4},{1,5},{2,6},{3,7},{4,0},{5,1},{6,2},{7,3},{8,12},{9,13},{10,... | collective-permute-start | bytes 983048 | tf_op jit(solution)/shard_map/ppermute | solution.py:423
  110.2 7.5 %collective-permute-start.32 = (bf16[8,16,1408]{2,1,0:T(8,128)(2,1)S(1)}, bf16[8,16,1408]{2,1,0:T(8,128)(2,1)S(1)}, u32[]{:S(2)}, u32[]{:S(2)}) collective-permute-start(bf16[8,16,1408]{2,1,0:T(8,128)(2,1)S(1)} %pad_maximum_fusion), channel_id=1, source_target_pairs={{0,2},{1,3},{2,0},{3,1},{4,6},{5,7},{6,4},{7,5},{8,10},{9,11},{10,... | collective-permute-start | bytes 1081352 | tf_op jit(solution)/shard_map/ppermute | solution.py:423
  117.7 36.1 %collective-permute-start.33 = (bf16[16,16,1408]{2,1,0:T(8,128)(2,1)S(1)}, bf16[16,16,1408]{2,1,0:T(8,128)(2,1)S(1)}, u32[]{:S(2)}, u32[]{:S(2)}) collective-permute-start(bf16[16,16,1408]{2,1,0:T(8,128)(2,1)S(1)} %constant_dynamic-update-slice_fusion.refs_0_), channel_id=1, source_target_pairs={{0,1},{1,0},{2,3},{3,2},{4,5},{5,4},{6,7},{7,6},{8,9},{9,8},{10,11... | collective-permute-start | bytes 2162696 | tf_op jit(solution)/shard_map/ppermute | solution.py:423
  117.8 36.0 %collective-permute-start.43 = (bf16[16,16,1280]{2,1,0:T(8,128)(2,1)S(1)}, bf16[16,16,1280]{2,1,0:T(8,128)(2,1)S(1)}, u32[]{:S(2)}, u32[]{:S(2)}) collective-permute-start(bf16[16,16,1280]{2,1,0:T(8,128)(2,1)S(1)} %constant_dynamic-update-slice_fusion.5.refs_2_), channel_id=1, source_target_pairs={{0,1},{1,0},{2,3},{3,2},{4,5},{5,4},{6,7},{7,6},{8,9},{9,8},{10,11... | collective-permute-start | bytes 1966088 | tf_op jit(solution)/shard_map/ppermute | solution.py:423
  118.4 2.8 %collective-permute-start.14 = (bf16[128,640]{1,0:T(8,128)(2,1)S(1)}, bf16[128,640]{1,0:T(8,128)(2,1)S(1)}, u32[]{:S(2)}, u32[]{:S(2)}) collective-permute-start(bf16[128,640]{1,0:T(8,128)(2,1)S(1)} %get-tuple-element.68), channel_id=1, source_target_pairs={{0,1},{1,0},{2,3},{3,2},{4,5},{5,4},{6,7},{7,6},{8,9},{9,8},{10,11... | collective-permute-start | bytes 491528 | tf_op jit(solution)/shard_map/ppermute | solution.py:423
  118.5 7.0 %collective-permute-start.15 = (bf16[128,640]{1,0:T(8,128)(2,1)S(1)}, bf16[128,640]{1,0:T(8,128)(2,1)S(1)}, u32[]{:S(2)}, u32[]{:S(2)}) collective-permute-start(bf16[128,640]{1,0:T(8,128)(2,1)S(1)} %get-tuple-element.69), channel_id=1, source_target_pairs={{0,2},{1,3},{2,0},{3,1},{4,6},{5,7},{6,4},{7,5},{8,10},{9,11},{10,... | collective-permute-start | bytes 491528 | tf_op jit(solution)/shard_map/ppermute | solution.py:423
  120.0 8.1 %collective-permute-start.16 = (bf16[128,640]{1,0:T(8,128)(2,1)S(1)}, bf16[128,640]{1,0:T(8,128)(2,1)S(1)}, u32[]{:S(2)}, u32[]{:S(2)}) collective-permute-start(bf16[128,640]{1,0:T(8,128)(2,1)S(1)} %get-tuple-element.70), channel_id=1, source_target_pairs={{0,3},{1,2},{2,1},{3,0},{4,7},{5,6},{6,5},{7,4},{8,11},{9,10},{10,... | collective-permute-start | bytes 491528 | tf_op jit(solution)/shard_map/ppermute | solution.py:423
  128.1 4.7 %collective-permute-start.17 = (bf16[64,640]{1,0:T(8,128)(2,1)S(1)}, bf16[64,640]{1,0:T(8,128)(2,1)S(1)}, u32[]{:S(2)}, u32[]{:S(2)}) collective-permute-start(bf16[64,640]{1,0:T(8,128)(2,1)S(1)} %get-tuple-element.72), channel_id=1, source_target_pairs={{0,4},{1,5},{2,6},{3,7},{4,0},{5,1},{6,2},{7,3},{8,12},{9,13},{10,... | collective-permute-start | bytes 245768 | tf_op jit(solution)/shard_map/ppermute | solution.py:423
  128.7 6.4 %collective-permute-start.18 = (bf16[64,640]{1,0:T(8,128)(2,1)S(1)}, bf16[64,640]{1,0:T(8,128)(2,1)S(1)}, u32[]{:S(2)}, u32[]{:S(2)}) collective-permute-start(bf16[64,640]{1,0:T(8,128)(2,1)S(1)} %get-tuple-element.73), channel_id=1, source_target_pairs={{0,8},{1,9},{2,10},{3,11},{4,12},{5,13},{6,14},{7,15},{8,0},{9,1},... | collective-permute-start | bytes 245768 | tf_op jit(solution)/shard_map/ppermute | solution.py:423
  128.8 8.4 %collective-permute-start.19 = (bf16[64,640]{1,0:T(8,128)(2,1)S(1)}, bf16[64,640]{1,0:T(8,128)(2,1)S(1)}, u32[]{:S(2)}, u32[]{:S(2)}) collective-permute-start(bf16[64,640]{1,0:T(8,128)(2,1)S(1)} %get-tuple-element.74), channel_id=1, source_target_pairs={{0,12},{1,13},{2,14},{3,15},{4,8},{5,9},{6,10},{7,11},{8,4},{9,5},... | collective-permute-start | bytes 245768 | tf_op jit(solution)/shard_map/ppermute | solution.py:423
  132.8 11.7 %collective-permute-start.20 = (bf16[64,640]{1,0:T(8,128)(2,1)S(1)}, bf16[64,640]{1,0:T(8,128)(2,1)S(1)}, u32[]{:S(2)}, u32[]{:S(2)}) collective-permute-start(bf16[64,640]{1,0:T(8,128)(2,1)S(1)} %get-tuple-element.75), channel_id=1, source_target_pairs={{0,16},{1,17},{2,18},{3,19},{4,20},{5,21},{6,22},{7,23},{8,24},{9,... | collective-permute-start | bytes 245768 | tf_op jit(solution)/shard_map/ppermute | solution.py:423
  135.1 11.8 %collective-permute-start.21 = (bf16[64,640]{1,0:T(8,128)(2,1)S(1)}, bf16[64,640]{1,0:T(8,128)(2,1)S(1)}, u32[]{:S(2)}, u32[]{:S(2)}) collective-permute-start(bf16[64,640]{1,0:T(8,128)(2,1)S(1)} %get-tuple-element.76), channel_id=1, source_target_pairs={{0,20},{1,21},{2,22},{3,23},{4,16},{5,17},{6,18},{7,19},{8,28},{9,... | collective-permute-start | bytes 245768 | tf_op jit(solution)/shard_map/ppermute | solution.py:423
  137.2 9.7 %collective-permute-start.22 = (bf16[64,640]{1,0:T(8,128)(2,1)S(1)}, bf16[64,640]{1,0:T(8,128)(2,1)S(1)}, u32[]{:S(2)}, u32[]{:S(2)}) collective-permute-start(bf16[64,640]{1,0:T(8,128)(2,1)S(1)} %get-tuple-element.77), channel_id=1, source_target_pairs={{0,24},{1,25},{2,26},{3,27},{4,28},{5,29},{6,30},{7,31},{8,16},{9,... | collective-permute-start | bytes 245768 | tf_op jit(solution)/shard_map/ppermute | solution.py:423
  144.5 7.1 %collective-permute-start.23 = (bf16[64,640]{1,0:T(8,128)(2,1)S(1)}, bf16[64,640]{1,0:T(8,128)(2,1)S(1)}, u32[]{:S(2)}, u32[]{:S(2)}) collective-permute-start(bf16[64,640]{1,0:T(8,128)(2,1)S(1)} %get-tuple-element.78), channel_id=1, source_target_pairs={{0,28},{1,29},{2,30},{3,31},{4,24},{5,25},{6,26},{7,27},{8,20},{9,... | collective-permute-start | bytes 245768 | tf_op jit(solution)/shard_map/ppermute | solution.py:423
  (9 other events, 22.2 us)

commit v3 on v2

--- a/solution.py
+++ b/solution.py
@@ -53,38 +53,26 @@
 TN = ((0,), (0,))
 
 
-def send_body(table_size, me_ref, *refs):
-    peers = (len(refs) - 2) // 2
-    packed_refs, grad_ref, out_refs, lengths_ref = (
-        refs[:peers],
-        refs[peers],
-        refs[peers + 1 : 2 * peers + 1],
-        refs[-1],
-    )
+def send_body(table_size, me_ref, packed_ref, grad_ref, out_ref):
+    peers = out_ref.shape[0]
     blocks = grad_ref.shape[0] // BLK
     me = me_ref[0] // table_size
-    for apart, packed_ref in enumerate(packed_refs):
-
-        def find(slot, length, packed_ref=packed_ref):
-            entry = packed_ref[slot]
+    begin = jnp.int32(0)
+    for peer in range(peers):
+
+        def find(slot, length, peer=peer):
+            entry = packed_ref[peer, 0, slot]
             return length + jnp.where(entry >> 3 == me, entry & 7, 0)
 
         length = lax.fori_loop(0, peers, find, jnp.int32(0), unroll=True)
-        lengths_ref[me ^ apart] = length
-    for apart, out_ref in enumerate(out_refs):
-        peer = me ^ apart
-
-        def before(other, begin, peer=peer):
-            return begin + jnp.where(other < peer, lengths_ref[other], 0)
-
-        begin = lax.fori_loop(0, peers, before, jnp.int32(0), unroll=True)
         for inner in range(LMAXB):
             block = jnp.minimum(begin + inner, blocks - 1)
             rows = grad_ref[pl.ds(pl.multiple_of(block * BLK, BLK), BLK), :]
-            live = jnp.full(rows.shape, inner, jnp.int32) < lengths_ref[peer]
-            out_ref[inner * BLK : (inner + 1) * BLK, :] = jnp.where(
+            live = jnp.full(rows.shape, inner, jnp.int32) < length
+            out_ref[peer, inner * BLK : (inner + 1) * BLK, :] = jnp.where(
                 live, rows.astype(F32), 0.0
             ).astype(BF16)
+        begin = begin + length
 
 
 def tile_mask():
@@ -203,19 +191,19 @@
     rows_slope_ref,
     rank_ref,
     digits_ref,
-    *refs,
+    got_ref,
+    table_ref,
+    keep_ref,
+    give_ref,
+    sums_ref,
+    active_ref,
+    grad_y_ref,
 ):
     count, width = rows_hat_ref.shape
     tokens = hat_ref.shape[0]
-    peers, table_size = plan.dp_size, plan.table_size
-    got_refs, refs = refs[:peers], refs[peers:]
-    table_refs, refs = refs[:table_size], refs[table_size:]
-    part_refs, (sums_ref, active_ref, grad_y_ref, wide_ref) = refs[:4], refs[4:]
     me = me_ref[0]
-    for slot in range(peers):
-        wide_ref[me // table_size ^ slot] = got_refs[slot][...]
-    for slot in range(peers):
-        grad_y_ref[slot * SLOT : (slot + 1) * SLOT, :] = wide_ref[dest_ref[slot]]
+    for slot in range(got_ref.shape[0]):
+        grad_y_ref[slot * SLOT : (slot + 1) * SLOT, :] = got_ref[dest_ref[slot]]
     gain_total = jnp.zeros((1, width), F32)
     for tile in range(tokens // TILE):
         rows = slice(tile * TILE, (tile + 1) * TILE)
@@ -273,24 +261,15 @@
     mean = jnp.mean(inner, axis=-1, keepdims=True)
     along = jnp.mean(inner * hat, axis=-1, keepdims=True)
     row_grad = (inner - mean - hat * along) * rows_scale_ref[...] + dot(gather, grad_y)
-    owner = owner_row_ref[...] ^ me
-    shift = table_size.bit_length() - 1
-    place = (owner & (table_size - 1)) * peers + (owner >> shift)
-    place = place * plan.capacity + rank_ref[...]
-    row_grad = row_grad.astype(BF16)
-    held = table_refs[0].shape[0]
-    for apart, table_ref in enumerate(table_refs):
-        spots = lax.broadcasted_iota(jnp.int32, (held, count), 0) + apart * held
-        spread = jnp.where(spots == jnp.broadcast_to(place, (held, count)), 1.0, 0.0)
-        spread = spread.astype(BF16)
-        table_ref[:, :width] = dot(spread, row_grad).astype(BF16)
-        table_ref[:, width:] = dot(spread, digits_ref[...]).astype(BF16)
-    for half in range(2):
-        for place_now in range(plan.chunks):
-            out_ref = part_refs[2 * half + place_now // (plan.chunks // 2)]
-            out_ref[place_now % (plan.chunks // 2)] = sums_ref[
-                chunk_at(plan, me ^ plan.mask_of(half, place_now), half)
-            ]
+    places = table_ref.shape[0]
+    place = owner_row_ref[...] * plan.capacity + rank_ref[...]
+    spots = lax.broadcasted_iota(jnp.int32, (places, count), 0)
+    spread = jnp.where(spots == jnp.broadcast_to(place, (places, count)), 1.0, 0.0).astype(BF16)
+    table_ref[:, :width] = dot(spread, row_grad.astype(BF16)).astype(BF16)
+    table_ref[:, width:] = dot(spread, digits_ref[...]).astype(BF16)
+    for place_now in range(plan.chunks):
+        out_ref = (keep_ref, give_ref)[place_now // (plan.chunks // 2)]
+        out_ref[place_now % (plan.chunks // 2)] = sums_ref[plan.chunk_at(me, place_now)]
 
 
 def unit(rows):
@@ -299,91 +278,58 @@
     return jnp.where(sub == lane, 1.0, 0.0).astype(BF16)
 
 
-def chunk_at(plan, chunk, half):
-    first = pl.multiple_of((chunk & (plan.row_groups - 1)) * CHUNK_ROWS, CHUNK_ROWS)
-    begin, wide = plan.halves[half]
-    if plan.column_groups == 1:
-        return pl.ds(first, CHUNK_ROWS), slice(begin, begin + wide)
-    group = chunk >> (plan.row_groups.bit_length() - 1)
-    column = pl.multiple_of(group * wide + begin, LANES)
-    return pl.ds(first, CHUNK_ROWS), pl.ds(column, wide)
-
-
 class Plan:
     def __init__(self, dp_size, table_size, count, width):
-        self.dp_size, self.table_size = dp_size, table_size
         self.chunks = dp_size * table_size
         self.capacity = 2 * count // self.chunks
         self.row_groups = min(self.chunks, width // CHUNK_ROWS)
         self.column_groups = self.chunks // self.row_groups
         block = self.column_groups * LANES
         blocks = -(-(5 * width + LANES) // block)
-        left = -(-blocks // 2)
         self.columns = blocks * block
-        self.halves = ((0, left * LANES), (left * block, (blocks - left) * LANES))
-        table_bits = [1 << bit for bit in range(table_size.bit_length() - 1)]
+        self.wide = blocks * LANES
+        table_bits = [1 << bit for bit in range(1, table_size.bit_length() - 1)]
         dp_bits = [table_size << bit for bit in range(dp_size.bit_length() - 1)]
-        self.orders = (
-            table_bits + dp_bits,
-            table_bits[:1] + dp_bits[:1] + table_bits[1:] + dp_bits[1:],
-        )
-
-    def mask_of(self, half, place):
-        order = self.orders[half]
+        self.orders = (table_bits + dp_bits, dp_bits[:2] + table_bits + dp_bits[2:])
+        self.steps = len(self.orders[0])
+
+    def low_mask(self, core, place):
         mask = 0
-        for step, bit in enumerate(order):
-            if place >> (len(order) - 1 - step) & 1:
+        for step, bit in enumerate(self.orders[core]):
+            if place >> (self.steps - 1 - step) & 1:
                 mask ^= bit
         return mask
 
-
-def regroup_body(plan, *refs):
-    in_refs, out_refs = refs[: plan.table_size], refs[plan.table_size :]
-    rows = out_refs[0].shape[0]
-    held = in_refs[0].shape[0]
-    capacity = plan.capacity
-    if capacity % 16 == 0:
-        for apart, out_ref in enumerate(out_refs):
-            for side, in_ref in enumerate(in_refs):
-                out_ref[side * capacity : (side + 1) * capacity, :] = in_ref[
-                    apart * capacity : (apart + 1) * capacity, :
-                ]
-        return
-    for apart, out_ref in enumerate(out_refs):
-        total = jnp.zeros(out_ref.shape, F32)
-        for side, in_ref in enumerate(in_refs):
-            sub = lax.broadcasted_iota(jnp.int32, (rows, held), 0) - side * capacity
-            lane = lax.broadcasted_iota(jnp.int32, (rows, held), 1) - apart * capacity
-            hit = (sub == lane) & (sub >= 0) & (sub < capacity)
-            total = total + dot(jnp.where(hit, 1.0, 0.0).astype(BF16), in_ref[...])
-        out_ref[...] = total.astype(BF16)
-
-
-def table_body(*refs):
-    got_refs, out_ref, full_ref = refs[:-2], refs[-2], refs[-1]
-    held = got_refs[0].shape[0]
-    for index, got_ref in enumerate(got_refs):
-        full_ref[index * held : (index + 1) * held, :] = got_ref[...]
-    places, width = full_ref.shape[0], out_ref.shape[1]
+    def chunk_at(self, me, place):
+        top, low = divmod(place, self.chunks // 2)
+        masks = [top ^ self.low_mask(core ^ top, low) for core in range(2)]
+        chunk = me ^ jnp.where((me & 1) == 0, masks[0], masks[1])
+        first = pl.multiple_of((chunk & (self.row_groups - 1)) * CHUNK_ROWS, CHUNK_ROWS)
+        if self.column_groups == 1:
+            return pl.ds(first, CHUNK_ROWS), slice(0, self.wide)
+        group = chunk >> (self.row_groups.bit_length() - 1)
+        return pl.ds(first, CHUNK_ROWS), pl.ds(pl.multiple_of(group * self.wide, LANES), self.wide)
+
+
+def table_body(got_ref, out_ref):
+    places, width = got_ref.shape[0], out_ref.shape[1]
     lane = lax.broadcasted_iota(jnp.int32, (16, LANES), 1)
     scale = jnp.where(lane == 0, 32.0, jnp.where(lane == 1, 1.0, 0.0)).astype(BF16)
-    numbers = dot(scale, full_ref[:, width:], NT)[0:1].astype(jnp.int32)
+    numbers = dot(scale, got_ref[:, width:], NT)[0:1].astype(jnp.int32)
     step = 256
     for first in range(0, out_ref.shape[0], step):
         sub = lax.broadcasted_iota(jnp.int32, (step, places), 0) + first
         hit = jnp.where(sub == jnp.broadcast_to(numbers, (step, places)), 1.0, 0.0)
-        out_ref[first : first + step, :] = dot(hit.astype(BF16), full_ref[:, :width])
-
-
-def widen_body(plan, me_ref, *refs):
-    part_refs, (w_in_ref, w_out_ref, gain_in_ref, gain_out_ref, sums_ref) = refs[:4], refs[4:]
+        out_ref[first : first + step, :] = dot(hit.astype(BF16), got_ref[:, :width])
+
+
+def widen_body(
+    plan, me_ref, own_ref, came_ref, w_in_ref, w_out_ref, gain_in_ref, gain_out_ref, sums_ref
+):
     me = me_ref[0]
-    for half in range(2):
-        for place in range(plan.chunks):
-            in_ref = part_refs[2 * half + place // (plan.chunks // 2)]
-            sums_ref[chunk_at(plan, me ^ plan.mask_of(half, place), half)] = in_ref[
-                place % (plan.chunks // 2)
-            ]
+    for place in range(plan.chunks):
+        in_ref = (own_ref, came_ref)[place // (plan.chunks // 2)]
+        sums_ref[plan.chunk_at(me, place)] = in_ref[place % (plan.chunks // 2)]
     split, end = w_in_ref.shape[1], w_in_ref.shape[1] + w_out_ref.shape[1]
     w_in_ref[...] = sums_ref[:, :split].astype(F32)
     w_out_ref[...] = sums_ref[:, split:end].astype(F32)
@@ -419,18 +365,20 @@
     gain_in, gain_out = gain_in[None, :], gain_out[None, :]
     me = lax.axis_index(both).astype(jnp.int32)[None]
 
-    def swap(values, mask):
-        return lax.ppermute(values, both, [(here, here ^ mask) for here in range(devices_all)])
-
-    packed = seq_dest * 8 + seq_blocks
-    all_packed = [packed] + [swap(packed, apart * table_size) for apart in range(1, dp_size)]
+    def swap(values, masks):
+        pairs = [(here, here ^ masks[here & 1]) for here in range(devices_all)]
+        return lax.ppermute(values, both, pairs)
+
+    def exchange(values, axes):
+        return lax.all_to_all(values, axes, split_axis=0, concat_axis=0, tiled=True)
+
+    packed = jnp.broadcast_to(seq_dest * 8 + seq_blocks, (dp_size, 1, dp_size))
     send = call(
         functools.partial(send_body, table_size),
-        [shape_of((SLOT, width), BF16)] * dp_size,
-        [SMEM] * (dp_size + 1) + [VMEM],
-        scratch=[pltpu.SMEM((dp_size,), jnp.int32)],
-    )(me, *all_packed, grad_out)
-    got = [send[0]] + [swap(send[apart], apart * table_size) for apart in range(1, dp_size)]
+        shape_of((dp_size, SLOT, width), BF16),
+        [SMEM] * 2 + [VMEM],
+    )(me, exchange(packed, "dp"), grad_out)
+    got = exchange(send, "dp")
 
     pairs = tokens // TILE * HEADS
     saved = call(
@@ -464,22 +412,17 @@
         owner_row.reshape(count, 1),
     )
 
-    half_shapes = [
-        shape_of((devices_all // 2, CHUNK_ROWS, wide), BF16) for _, wide in plan.halves
-    ]
-    held = dp_size * plan.capacity
-    outs = call(
+    half = shape_of((devices_all // 2, CHUNK_ROWS, plan.wide), BF16)
+    table_send, kept, sent = call(
         functools.partial(backward_body, plan, total_factor),
-        [shape_of((held, width + LANES), BF16)] * table_size
-        + [half_shapes[0], half_shapes[0], half_shapes[1], half_shapes[1]],
-        [SMEM] * 2 + [VMEM] * (19 + dp_size),
+        [shape_of((devices_all * plan.capacity, width + LANES), BF16), half, half],
+        [SMEM] * 2 + [VMEM] * 20,
         flops=4 * count * width * width * 20,
         moved=12_000_000,
         scratch=[
             pltpu.VMEM((width, plan.columns), BF16),
             pltpu.VMEM((tokens, 4 * width), BF16),
             pltpu.VMEM((tokens, width), BF16),
-            pltpu.VMEM((dp_size, SLOT, width), BF16),
         ],
     )(
         me,
@@ -491,41 +434,24 @@
         gain_in,
         gain_out,
         *saved,
-        *got,
-    )
-    table_send, parts = outs[:table_size], outs[table_size:]
-
-    steps = len(plan.orders[0])
-    kept, sent = [parts[0], parts[2]], [parts[1], parts[3]]
-    for step in range(steps):
-        came = [swap(sent[half], plan.orders[half][step]) for half in range(2)]
-        middle = kept[0].shape[0] // 2
-        for half in range(2):
-            if middle:
-                sent[half] = add(kept[half][middle:], came[half][middle:])
-                kept[half] = add(kept[half][:middle], came[half][:middle])
-            else:
-                kept[half] = add(kept[half], came[half])
-    for step in reversed(range(steps)):
-        came = [swap(kept[half], plan.orders[half][step]) for half in range(2)]
-        if step:
-            kept = [jnp.concatenate([kept[half], came[half]]) for half in range(2)]
-
-    table_mid = [table_send[0]] + [swap(table_send[apart], apart) for apart in range(1, table_size)]
-    table_mid = call(
-        functools.partial(regroup_body, plan),
-        [shape_of((table_size * plan.capacity, width + LANES), BF16)] * dp_size,
-        [VMEM] * table_size,
-    )(*table_mid)
-    table_got = [table_mid[0]] + [
-        swap(table_mid[apart], apart * table_size) for apart in range(1, dp_size)
-    ]
+        got,
+    )
+
+    kept = add(kept, swap(sent, (1, 1)))
+    for masks in zip(*plan.orders):
+        middle = kept.shape[0] // 2
+        came = swap(kept[middle:], masks)
+        kept = add(kept[:middle], came)
+    for masks in reversed(list(zip(*plan.orders))):
+        kept = jnp.concatenate([kept, swap(kept, masks)])
+    came = swap(kept, (1, 1))
+
+    table_got = exchange(table_send.reshape(devices_all, plan.capacity, width + LANES), both)
     table_part = call(
         table_body,
         shape_of((ROWS_DEV, width), F32),
-        [VMEM] * dp_size,
-        scratch=[pltpu.VMEM((devices_all * plan.capacity, width + LANES), BF16)],
-    )(*table_got)
+        [VMEM],
+    )(table_got.reshape(devices_all * plan.capacity, width + LANES))
     grad_w_in, grad_w_out, grad_gain_in, grad_gain_out = call(
         functools.partial(widen_body, plan),
         (
@@ -534,9 +460,9 @@
             shape_of((1, width), F32),
             shape_of((1, width), F32),
         ),
-        [SMEM] + [VMEM] * 4,
+        [SMEM] + [VMEM] * 2,
         scratch=[pltpu.VMEM((width, plan.columns), BF16)],
-    )(me, kept[0], came[0], kept[1], came[1])
+    )(me, kept, came)
     return (table_part, grad_w_in, grad_w_out, grad_gain_in[0], grad_gain_out[0])
 
 

time: 157 us -> 160 us (1.019)
  starting transfers between devices: 63.1 us -> 29.5 us
  blocking collectives: 0 us -> 24.4 us
  local copies, waits for them, and re-layouts: 8.13 us -> 25.8 us
  waiting for transfers between devices: 63.3 us -> 56.9 us
    ppermute x44 -> x10, starting transfers between devices: 63.1 us -> 18.8 us  [swap(): return lax.ppermute(values, both, pairs)]
    all_to_all x0 -> x1, blocking collectives: none -> 24.4 us  [exchange(): return lax.all_to_all(values, axes, split_axis=0, concat_axis=0, tiled=True)]
    unnamed x33 -> x68, local copies, waits for them, and re-layouts: 6.44 us -> 24.7 us
    ppermute x44 -> x10, waiting for transfers between devices: 63.3 us -> 50.5 us  [swap(): return lax.ppermute(values, both, pairs)]
    all_to_all x0 -> x2, starting transfers between devices: none -> 10.7 us  [exchange(): return lax.all_to_all(values, axes, split_axis=0, concat_axis=0, tiled=True)]
    all_to_all x0 -> x2, waiting for transfers between devices: none -> 6.39 us  [exchange(): return lax.all_to_all(values, axes, split_axis=0, concat_axis=0, tiled=True)]
    pallas_call x4 -> x3, Pallas kernels: 11.3 us -> 11.9 us  [the longest x1 8.15 us: on_device(): call(functools.partial(backward_body, plan, total_factor), [shape_of((dev...]
  transfers between devices with their start and end apart: 44 -> 12, of which waited for: 21 -> 10; matrix products, arithmetic and copies ran while one was open for 2% -> 0% of each run, Pallas kernels for 5% -> 5%
where the time goes in v3:
time: 160 us; the launch traced here: 159 us
  waiting for transfers between devices  56.9 us (36%)
  starting transfers between devices  29.5 us (18%)
  local copies, waits for them, and re-layouts  25.8 us (16%)
  blocking collectives  24.4 us (15%)
  Pallas kernels  20.1 us (13%)
    ppermute x10, waiting for transfers between devices, swap(): return lax.ppermute(values, both, pairs)  50.5 us
    unnamed x68, local copies, waits for them, and re-layouts  24.7 us
    all_to_all x1, blocking collectives, exchange(): return lax.all_to_all(values, axes, split_axis=0, concat_axis=0, tiled=True)  24.4 us
    ppermute x10, starting transfers between devices, swap(): return lax.ppermute(values, both, pairs)  18.8 us
    all_to_all x2, starting transfers between devices, exchange(): return lax.all_to_all(values, axes, split_axis=0, concat_axis=0, tiled=True)  10.7 us
    pallas_call x1, Pallas kernels, on_device(): call(functools.partial(backward_body, plan, total_factor), [shape_of((dev...  8.15 us
    all_to_all x2, waiting for transfers between devices, exchange(): return lax.all_to_all(values, axes, split_axis=0, concat_axis=0, tiled=True)  6.39 us
    pallas_call x1, Pallas kernels, on_device(): call(forward_body, (shape_of((tokens, 3 * width), BF16), shape_of((tokens...  5.39 us
  transfers between devices with their start and end apart: 12, of which 10 were waited for; matrix products, arithmetic and copies ran while one was open for 0% of the time, Pallas kernels for 5%

profile of v3, /device:TPU:0, one launch (start us, length us, event | category | flops | bytes accessed | tf_op | source)
XLA Modules:
  0.0 159.1 jit_solution(5976620538848196294)
XLA Ops:
  2.0 7.3 %all-to-all-start = ((s32[8,1,8]{2,1,0:T(1,128)}), s32[8,1,8]{2,1,0:T(1,128)S(1)}, u32[]{:S(2)}, u32[]{:S(2)}) async-start(s32[8,1,8]{2,1,0:T(1,128)} %broadcast_in_dim.15), calls=%async_computation | async-start | bytes 8192 | tf_op jit(solution)/shard_map/all_to_all | solution.py:373
  9.2 6.4 %all-to-all-done.packed_ref = s32[8,1,8]{2,1,0:T(1,128)S(1)} async-done(((s32[8,1,8]{2,1,0:T(1,128)}), s32[8,1,8]{2,1,0:T(1,128)S(1)}, u32[]{:S(2)}, u32[]{:S(2)}) %all-to-all-start) | async-done | bytes 288 | tf_op jit(solution)/shard_map/all_to_all | solution.py:373
  15.6 0.9 copy-done
  16.6 1.6 shard_map.147
  18.1 3.5 %all-to-all-start.1 = ((bf16[8,64,512]{2,1,0:T(8,128)(2,1)}), bf16[8,64,512]{2,1,0:T(8,128)(2,1)S(1)}, u32[]{:S(2)}, u32[]{:S(2)}) async-start(bf16[8,64,512]{2,1,0:T(8,128)(2,1)} %shard_map.147), calls=%async_computation.1 | async-start | bytes 1048576 | tf_op jit(solution)/shard_map/all_to_all | solution.py:373
  22.2 5.4 %shard_map.146 = (bf16[512,1536]{1,0:T(8,128)(2,1)S(1)}, f32[512,512]{1,0:T(8,128)S(1)}, f32[512,512]{1,0:T(8,128)S(1)}, f32[512,1]{1,0:T(8,128)S(1)}, bf16[512,...) custom-call(bf16[256,512]{1,0:T(8,128)(2,1)S(1)} %copy-done.5, ...), custom_call_target="tpu_custom_call" | custom-call | flops 2147483648 | bytes 10000000 | tf_op jit(solution)/shard_map/pallas_call | solution.py:384
  27.6 1.3 copy-done.9
  28.9 1.1 copy-done.11
  30.0 1.0 copy-done.13
  31.0 1.0 copy-done.15
  32.0 1.0 copy-done.17
  33.0 0.8 copy-done.19
  33.8 0.8 copy-done.21
  34.6 0.8 copy-done.23
  36.1 0.7 copy-done.27
  37.5 1.0 copy-done.4
  38.5 1.6 copy-done.10
  40.1 1.4 copy-done.12
  41.5 1.2 copy-done.14
  42.8 1.2 copy-done.16
  44.0 1.2 copy-done.18
  45.2 1.0 copy-done.20
  46.3 1.0 copy-done.22
  47.3 1.0 copy-done.24
  48.3 0.9 copy-done.26
  49.3 0.9 copy-done.28
  50.2 0.9 copy-done.30
  51.1 8.1 %shard_map.148 = (bf16[512,640]{1,0:T(8,128)(2,1)S(1)}, bf16[16,16,2688]{2,1,0:T(8,128)(2,1)S(1)}, bf16[16,16,2688]{2,1,0:T(8,128)(2,1)S(1)}) custom-call(s32[1]{0:T(128)} %bitcast.me_ref, s32[8]{0:T(128)S(1)} %copy-done.8, s32[1,512]{1,0:T(1,128)S(1)} %bitcast.14, s32[1,256]{1,0:T(1,128)S(1)} %bitcast.16, bf16[512,2048]{1,0:T(8,128)(2,1)S(1)} %copy-done.3, ...), custom_call_target="tpu_custom_call" | custom-call | flops 5368709120 | bytes 12000000 | tf_op jit(solution)/shard_map/pallas_call | solution.py:416
  59.4 3.1 %collective-permute-done = bf16[16,16,2688]{2,1,0:T(8,128)(2,1)S(1)} collective-permute-done((bf16[16,16,2688]{2,1,0:T(8,128)(2,1)S(1)}, bf16[16,16,2688]{2,1,0:T(8,128)(2,1)S(1)}, u32[]{:S(2)}, u32[]{:S(2)}) %collective-permute-start) | collective-permute-done | bytes 1376288 | tf_op jit(solution)/shard_map/ppermute | solution.py:370
  62.9 1.6 collective-permute-start.1
  64.5 9.4 %collective-permute-done.1 = bf16[8,16,2688]{2,1,0:T(8,128)(2,1)S(1)} collective-permute-done((bf16[8,16,2688]{2,1,0:T(8,128)(2,1)S(1)}, bf16[8,16,2688]{2,1,0:T(8,128)(2,1)S(1)}, u32[]{:S(2)}, u32[]{:S(2)}) %collective-permute-start.1) | collective-permute-done | bytes 688160 | tf_op jit(solution)/shard_map/ppermute | solution.py:370
  74.1 2.0 %collective-permute-start.2 = (bf16[4,16,2688]{2,1,0:T(8,128)(2,1)S(1)}, bf16[4,16,2688]{2,1,0:T(8,128)(2,1)S(1)}, u32[]{:S(2)}, u32[]{:S(2)}) collective-permute-start(bf16[4,16,2688]{2,1,0:T(8,128)(2,1)S(1)} %slice.35), channel_id=1, source_target_pairs={{0,4},{1,9},{2,6},{3,11},{4,0},{5,13},{6,2},{7,15},{8,12},{9,1},{1... | collective-permute-start | bytes 1032200 | tf_op jit(solution)/shard_map/ppermute | solution.py:370
  76.1 5.3 %collective-permute-done.2 = bf16[4,16,2688]{2,1,0:T(8,128)(2,1)S(1)} collective-permute-done((bf16[4,16,2688]{2,1,0:T(8,128)(2,1)S(1)}, bf16[4,16,2688]{2,1,0:T(8,128)(2,1)S(1)}, u32[]{:S(2)}, u32[]{:S(2)}) %collective-permute-start.2) | collective-permute-done | bytes 344096 | tf_op jit(solution)/shard_map/ppermute | solution.py:370
  81.5 2.0 %collective-permute-start.3 = (bf16[2,16,2688]{2,1,0:T(8,128)(2,1)S(1)}, bf16[2,16,2688]{2,1,0:T(8,128)(2,1)S(1)}, u32[]{:S(2)}, u32[]{:S(2)}) collective-permute-start(bf16[2,16,2688]{2,1,0:T(8,128)(2,1)S(1)} %slice.37), channel_id=1, source_target_pairs={{0,8},{1,3},{2,10},{3,1},{4,12},{5,7},{6,14},{7,5},{8,0},{9,11},{1... | collective-permute-start | bytes 516104 | tf_op jit(solution)/shard_map/ppermute | solution.py:370
  83.5 3.5 %collective-permute-done.3 = bf16[2,16,2688]{2,1,0:T(8,128)(2,1)S(1)} collective-permute-done((bf16[2,16,2688]{2,1,0:T(8,128)(2,1)S(1)}, bf16[2,16,2688]{2,1,0:T(8,128)(2,1)S(1)}, u32[]{:S(2)}, u32[]{:S(2)}) %collective-permute-start.3) | collective-permute-done | bytes 172064 | tf_op jit(solution)/shard_map/ppermute | solution.py:370
  87.1 2.9 %collective-permute-start.4 = (bf16[1,16,2688]{2,1,0:T(8,128)(2,1)S(1)}, bf16[1,16,2688]{2,1,0:T(8,128)(2,1)S(1)}, u32[]{:S(2)}, u32[]{:S(2)}) collective-permute-start(bf16[1,16,2688]{2,1,0:T(8,128)(2,1)S(1)} %slice.39), channel_id=1, source_target_pairs={{0,16},{1,17},{2,18},{3,19},{4,20},{5,21},{6,22},{7,23},{8,24},{9,... | collective-permute-start | bytes 258056 | tf_op jit(solution)/shard_map/ppermute | solution.py:370
  90.0 2.6 %collective-permute-done.4 = bf16[1,16,2688]{2,1,0:T(8,128)(2,1)S(1)} collective-permute-done((bf16[1,16,2688]{2,1,0:T(8,128)(2,1)S(1)}, bf16[1,16,2688]{2,1,0:T(8,128)(2,1)S(1)}, u32[]{:S(2)}, u32[]{:S(2)}) %collective-permute-start.4) | collective-permute-done | bytes 86048 | tf_op jit(solution)/shard_map/ppermute | solution.py:370
  92.5 3.2 %collective-permute-start.5 = (bf16[1,16,2688]{2,1,0:T(8,128)(2,1)S(1)}, bf16[1,16,2688]{2,1,0:T(8,128)(2,1)S(1)}, u32[]{:S(2)}, u32[]{:S(2)}) collective-permute-start(bf16[1,16,2688]{2,1,0:T(8,128)(2,1)S(1)} %get-tuple-element.46), channel_id=1, source_target_pairs={{0,16},{1,17},{2,18},{3,19},{4,20},{5,21},{6,22},{7,23},{8,24},{9,... | collective-permute-start | bytes 258056 | tf_op jit(solution)/shard_map/ppermute | solution.py:370
  95.8 2.5 %collective-permute-done.5 = bf16[1,16,2688]{2,1,0:T(8,128)(2,1)S(1)} collective-permute-done((bf16[1,16,2688]{2,1,0:T(8,128)(2,1)S(1)}, bf16[1,16,2688]{2,1,0:T(8,128)(2,1)S(1)}, u32[]{:S(2)}, u32[]{:S(2)}) %collective-permute-start.5) | collective-permute-done | bytes 86048 | tf_op jit(solution)/shard_map/ppermute | solution.py:370
  98.2 3.9 %collective-permute-start.6 = (bf16[2,16,2688]{2,1,0:T(8,128)(2,1)S(1)}, bf16[2,16,2688]{2,1,0:T(8,128)(2,1)S(1)}, u32[]{:S(2)}, u32[]{:S(2)}) collective-permute-start(bf16[2,16,2688]{2,1,0:T(8,128)(2,1)S(1)} %pad_maximum_fusion.2), channel_id=1, source_target_pairs={{0,8},{1,3},{2,10},{3,1},{4,12},{5,7},{6,14},{7,5},{8,0},{9,11},{1... | collective-permute-start | bytes 516104 | tf_op jit(solution)/shard_map/ppermute | solution.py:370
  102.1 5.3 %collective-permute-done.6 = bf16[2,16,2688]{2,1,0:T(8,128)(2,1)S(1)} collective-permute-done((bf16[2,16,2688]{2,1,0:T(8,128)(2,1)S(1)}, bf16[2,16,2688]{2,1,0:T(8,128)(2,1)S(1)}, u32[]{:S(2)}, u32[]{:S(2)}) %collective-permute-start.6) | collective-permute-done | bytes 172064 | tf_op jit(solution)/shard_map/ppermute | solution.py:370
  107.5 1.5 collective-permute-start.7
  108.9 9.5 %collective-permute-done.7 = bf16[4,16,2688]{2,1,0:T(8,128)(2,1)S(1)} collective-permute-done((bf16[4,16,2688]{2,1,0:T(8,128)(2,1)S(1)}, bf16[4,16,2688]{2,1,0:T(8,128)(2,1)S(1)}, u32[]{:S(2)}, u32[]{:S(2)}) %collective-permute-start.7) | collective-permute-done | bytes 344096 | tf_op jit(solution)/shard_map/ppermute | solution.py:370
  118.5 1.6 %collective-permute-start.8 = (bf16[8,16,2688]{2,1,0:T(8,128)(2,1)S(1)}, bf16[8,16,2688]{2,1,0:T(8,128)(2,1)S(1)}, u32[]{:S(2)}, u32[]{:S(2)}) collective-permute-start(bf16[8,16,2688]{2,1,0:T(8,128)(2,1)S(1)} %pad_maximum_fusion), channel_id=1, source_target_pairs={{0,2},{1,5},{2,0},{3,7},{4,6},{5,1},{6,4},{7,3},{8,10},{9,13},{10,... | collective-permute-start | bytes 2064392 | tf_op jit(solution)/shard_map/ppermute | solution.py:370
  120.2 9.3 %collective-permute-done.8 = bf16[8,16,2688]{2,1,0:T(8,128)(2,1)S(1)} collective-permute-done((bf16[8,16,2688]{2,1,0:T(8,128)(2,1)S(1)}, bf16[8,16,2688]{2,1,0:T(8,128)(2,1)S(1)}, u32[]{:S(2)}, u32[]{:S(2)}) %collective-permute-start.8) | collective-permute-done | bytes 688160 | tf_op jit(solution)/shard_map/ppermute | solution.py:370
  129.7 24.4 %all_to_all.15 = bf16[32,16,640]{2,1,0:T(8,128)(2,1)S(1)} all-to-all(bf16[32,16,640]{2,1,0:T(8,128)(2,1)S(1)} %bitcast.12), channel_id=1, replica_groups=mesh['dp'=8,'table'=4] {'dp','table'}, dimensions={0} | all-to-all | bytes 1310720 | tf_op jit(solution)/shard_map/all_to_all | solution.py:373
  154.1 2.2 %shard_map.149 = f32[1024,512]{1,0:T(8,128)} custom-call(bf16[512,640]{1,0:T(8,128)(2,1)S(1)} %bitcast.11), custom_call_target="tpu_custom_call" | custom-call | tf_op jit(solution)/shard_map/pallas_call | solution.py:450
  156.3 2.8 %shard_map.150 = (f32[512,2048]{1,0:T(8,128)}, f32[512,512]{1,0:T(8,128)}, f32[1,512]{1,0:T(1,128)}, f32[1,512]{1,0:T(1,128)}) custom-call(s32[1]{0:T(128)} %bitcast.me_ref, bf16[16,16,2688]{2,1,0:T(8,128)(2,1)S(1)} %constant_dynamic-update-slice_fusion.own_ref, bf16[16,16,2688]{2,1,0:T(8,128)(2,1)S(1)} %collective-permute-done.9.came_ref), custom_call_target="tpu_custom_call" | custom-call | tf_op jit(solution)/shard_map/pallas_call | solution.py:455
  (67 shorter events, 4.4 us)
Async XLA Ops:
  0.6 21.0 %copy-start.31 = (s32[256]{0:T(256)S(1)}, s32[256]{0:T(256)}, u32[]{:S(2)}) copy-start(s32[256]{0:T(256)} %param.14) | copy-start | bytes 3076
  0.6 21.2 %copy-start.2 = (s32[256,1]{0,1:T(1,128)S(1)}, s32[256,1]{0,1:T(1,128)}, u32[]{:S(2)}) copy-start(s32[256,1]{0,1:T(1,128)} %param.13) | copy-start | bytes 3076
  0.7 21.3 %copy-start.1 = (s32[512]{0:T(512)S(1)}, s32[512]{0:T(512)}, u32[]{:S(2)}) copy-start(s32[512]{0:T(512)} %param.12) | copy-start | bytes 6148
  0.7 21.5 %copy-start.7 = (f32[512]{0:T(512)S(1)}, f32[512]{0:T(512)}, u32[]{:S(2)}) copy-start(f32[512]{0:T(512)} %param.21) | copy-start | bytes 6148
  0.7 21.5 %copy-start.6 = (f32[512]{0:T(512)S(1)}, f32[512]{0:T(512)}, u32[]{:S(2)}) copy-start(f32[512]{0:T(512)} %param.20) | copy-start | bytes 6148
  2.0 13.6 %all-to-all-start = ((s32[8,1,8]{2,1,0:T(1,128)}), s32[8,1,8]{2,1,0:T(1,128)S(1)}, u32[]{:S(2)}, u32[]{:S(2)}) async-start(s32[8,1,8]{2,1,0:T(1,128)} %broadcast_in_dim.15), calls=%async_computation | async-start | bytes 8192 | tf_op jit(solution)/shard_map/all_to_all | solution.py:373
  15.6 1.0 copy-start
  16.6 5.6 %copy-start.3 = (bf16[512,2048]{1,0:T(8,128)(2,1)S(1)}, bf16[512,2048]{1,0:T(8,128)(2,1)}, u32[]{:S(2)}) copy-start(bf16[512,2048]{1,0:T(8,128)(2,1)} %w_in_ref.3) | copy-start | bytes 6291460
  16.6 5.6 %copy-start.5 = (bf16[256,512]{1,0:T(8,128)(2,1)S(1)}, bf16[256,512]{1,0:T(8,128)(2,1)}, u32[]{:S(2)}) copy-start(bf16[256,512]{1,0:T(8,128)(2,1)} %rows_ref.1) | copy-start | bytes 786436
  18.1 19.3 %all-to-all-start.1 = ((bf16[8,64,512]{2,1,0:T(8,128)(2,1)}), bf16[8,64,512]{2,1,0:T(8,128)(2,1)S(1)}, u32[]{:S(2)}, u32[]{:S(2)}) async-start(bf16[8,64,512]{2,1,0:T(8,128)(2,1)} %shard_map.147), calls=%async_computation.1 | async-start | bytes 1048576 | tf_op jit(solution)/shard_map/all_to_all | solution.py:373
  22.2 15.3 %copy-start.8 = (s32[8]{0:T(128)S(1)}, s32[8]{0:T(128)}, u32[]{:S(2)}) copy-start(s32[8]{0:T(128)} %dest_ref.1) | copy-start | bytes 100
  27.6 1.3 copy-start.9
  28.9 1.1 copy-start.11
  30.0 1.0 copy-start.13
  31.0 1.0 copy-start.15
  32.0 1.0 copy-start.17
  33.0 0.8 copy-start.19
  33.8 0.8 copy-start.21
  34.6 0.8 copy-start.23
  35.4 0.7 copy-start.25
  36.1 0.7 copy-start.27
  36.8 0.7 copy-start.29
  37.5 1.0 copy-start.4
  38.5 1.6 %copy-start.10 = (f32[256,2048]{1,0:T(8,128)S(1)}, f32[256,2048]{1,0:T(8,128)}, u32[]{:S(2)}) copy-start(f32[256,2048]{1,0:T(8,128)} %copy-done.9) | copy-start | bytes 6291460
  40.1 1.4 copy-start.12
  41.5 1.2 copy-start.14
  42.8 1.2 copy-start.16
  44.0 1.2 copy-start.18
  45.2 1.0 copy-start.20
  46.3 1.0 copy-start.22
  47.3 1.0 copy-start.24
  48.3 0.9 copy-start.26
  49.3 0.9 copy-start.28
  50.2 0.9 copy-start.30
  59.3 3.2 %collective-permute-start = (bf16[16,16,2688]{2,1,0:T(8,128)(2,1)S(1)}, bf16[16,16,2688]{2,1,0:T(8,128)(2,1)S(1)}, u32[]{:S(2)}, u32[]{:S(2)}) collective-permute-start(bf16[16,16,2688]{2,1,0:T(8,128)(2,1)S(1)} %get-tuple-element.40), channel_id=1, source_target_pairs={{0,1},{1,0},{2,3},{3,2},{4,5},{5,4},{6,7},{7,6},{8,9},{9,8},{10,11... | collective-permute-start | bytes 4128776 | tf_op jit(solution)/shard_map/ppermute | solution.py:370
  62.9 11.0 %collective-permute-start.1 = (bf16[8,16,2688]{2,1,0:T(8,128)(2,1)S(1)}, bf16[8,16,2688]{2,1,0:T(8,128)(2,1)S(1)}, u32[]{:S(2)}, u32[]{:S(2)}) collective-permute-start(bf16[8,16,2688]{2,1,0:T(8,128)(2,1)S(1)} %slice.33), channel_id=1, source_target_pairs={{0,2},{1,5},{2,0},{3,7},{4,6},{5,1},{6,4},{7,3},{8,10},{9,13},{10,... | collective-permute-start | bytes 2064392 | tf_op jit(solution)/shard_map/ppermute | solution.py:370
  74.1 7.3 %collective-permute-start.2 = (bf16[4,16,2688]{2,1,0:T(8,128)(2,1)S(1)}, bf16[4,16,2688]{2,1,0:T(8,128)(2,1)S(1)}, u32[]{:S(2)}, u32[]{:S(2)}) collective-permute-start(bf16[4,16,2688]{2,1,0:T(8,128)(2,1)S(1)} %slice.35), channel_id=1, source_target_pairs={{0,4},{1,9},{2,6},{3,11},{4,0},{5,13},{6,2},{7,15},{8,12},{9,1},{1... | collective-permute-start | bytes 1032200 | tf_op jit(solution)/shard_map/ppermute | solution.py:370
  81.5 5.5 %collective-permute-start.3 = (bf16[2,16,2688]{2,1,0:T(8,128)(2,1)S(1)}, bf16[2,16,2688]{2,1,0:T(8,128)(2,1)S(1)}, u32[]{:S(2)}, u32[]{:S(2)}) collective-permute-start(bf16[2,16,2688]{2,1,0:T(8,128)(2,1)S(1)} %slice.37), channel_id=1, source_target_pairs={{0,8},{1,3},{2,10},{3,1},{4,12},{5,7},{6,14},{7,5},{8,0},{9,11},{1... | collective-permute-start | bytes 516104 | tf_op jit(solution)/shard_map/ppermute | solution.py:370
  87.1 5.4 %collective-permute-start.4 = (bf16[1,16,2688]{2,1,0:T(8,128)(2,1)S(1)}, bf16[1,16,2688]{2,1,0:T(8,128)(2,1)S(1)}, u32[]{:S(2)}, u32[]{:S(2)}) collective-permute-start(bf16[1,16,2688]{2,1,0:T(8,128)(2,1)S(1)} %slice.39), channel_id=1, source_target_pairs={{0,16},{1,17},{2,18},{3,19},{4,20},{5,21},{6,22},{7,23},{8,24},{9,... | collective-permute-start | bytes 258056 | tf_op jit(solution)/shard_map/ppermute | solution.py:370
  92.5 5.7 %collective-permute-start.5 = (bf16[1,16,2688]{2,1,0:T(8,128)(2,1)S(1)}, bf16[1,16,2688]{2,1,0:T(8,128)(2,1)S(1)}, u32[]{:S(2)}, u32[]{:S(2)}) collective-permute-start(bf16[1,16,2688]{2,1,0:T(8,128)(2,1)S(1)} %get-tuple-element.46), channel_id=1, source_target_pairs={{0,16},{1,17},{2,18},{3,19},{4,20},{5,21},{6,22},{7,23},{8,24},{9,... | collective-permute-start | bytes 258056 | tf_op jit(solution)/shard_map/ppermute | solution.py:370
  98.2 9.2 %collective-permute-start.6 = (bf16[2,16,2688]{2,1,0:T(8,128)(2,1)S(1)}, bf16[2,16,2688]{2,1,0:T(8,128)(2,1)S(1)}, u32[]{:S(2)}, u32[]{:S(2)}) collective-permute-start(bf16[2,16,2688]{2,1,0:T(8,128)(2,1)S(1)} %pad_maximum_fusion.2), channel_id=1, source_target_pairs={{0,8},{1,3},{2,10},{3,1},{4,12},{5,7},{6,14},{7,5},{8,0},{9,11},{1... | collective-permute-start | bytes 516104 | tf_op jit(solution)/shard_map/ppermute | solution.py:370
  107.5 10.9 %collective-permute-start.7 = (bf16[4,16,2688]{2,1,0:T(8,128)(2,1)S(1)}, bf16[4,16,2688]{2,1,0:T(8,128)(2,1)S(1)}, u32[]{:S(2)}, u32[]{:S(2)}) collective-permute-start(bf16[4,16,2688]{2,1,0:T(8,128)(2,1)S(1)} %pad_maximum_fusion.1), channel_id=1, source_target_pairs={{0,4},{1,9},{2,6},{3,11},{4,0},{5,13},{6,2},{7,15},{8,12},{9,1},{1... | collective-permute-start | bytes 1032200 | tf_op jit(solution)/shard_map/ppermute | solution.py:370
  118.5 11.0 %collective-permute-start.8 = (bf16[8,16,2688]{2,1,0:T(8,128)(2,1)S(1)}, bf16[8,16,2688]{2,1,0:T(8,128)(2,1)S(1)}, u32[]{:S(2)}, u32[]{:S(2)}) collective-permute-start(bf16[8,16,2688]{2,1,0:T(8,128)(2,1)S(1)} %pad_maximum_fusion), channel_id=1, source_target_pairs={{0,2},{1,5},{2,0},{3,7},{4,6},{5,1},{6,4},{7,3},{8,10},{9,13},{10,... | collective-permute-start | bytes 2064392 | tf_op jit(solution)/shard_map/ppermute | solution.py:370
  129.6 26.7 %collective-permute-start.9 = (bf16[16,16,2688]{2,1,0:T(8,128)(2,1)S(1)}, bf16[16,16,2688]{2,1,0:T(8,128)(2,1)S(1)}, u32[]{:S(2)}, u32[]{:S(2)}) collective-permute-start(bf16[16,16,2688]{2,1,0:T(8,128)(2,1)S(1)} %constant_dynamic-update-slice_fusion.own_ref), channel_id=1, source_target_pairs={{0,1},{1,0},{2,3},{3,2},{4,5},{5,4},{6,7},{7,6},{8,9},{9,8},{10,11... | collective-permute-start | bytes 4128776 | tf_op jit(solution)/shard_map/ppermute | solution.py:370

commit v4 on v3

--- a/solution.py
+++ b/solution.py
@@ -22,17 +22,18 @@
 BF16 = jnp.bfloat16
 VMEM = pl.BlockSpec(memory_space=pltpu.VMEM)
 SMEM = pl.BlockSpec(memory_space=pltpu.SMEM)
-
-
-def call(body, out_shape, in_specs, flops=0, moved=0, scratch=()):
-    outs = jax.tree.map(lambda _: VMEM, out_shape)
+HBM = pl.BlockSpec(memory_space=pltpu.HBM)
+
+
+def call(body, out_shape, in_specs, flops=0, moved=0, scratch=(), out_space=VMEM, mebibytes=24):
+    outs = jax.tree.map(lambda _: out_space, out_shape)
     return pl.pallas_call(
         body,
         out_shape=out_shape,
         in_specs=in_specs,
         out_specs=outs,
         scratch_shapes=scratch,
-        compiler_params=pltpu.CompilerParams(vmem_limit_bytes=24 * 1024 * 1024),
+        compiler_params=pltpu.CompilerParams(vmem_limit_bytes=mebibytes * 1024 * 1024),
         cost_estimate=pl.CostEstimate(flops=flops, bytes_accessed=moved, transcendentals=0),
     )
 
@@ -81,7 +82,44 @@
     return (sub // SLOT == lane // SLOT) & (lane <= sub)
 
 
+SAVED = (
+    "gate",
+    "hat",
+    "hat_scale",
+    "qkv",
+    "slope",
+    "weight",
+    "mixed",
+    "normed",
+    "rows_slope",
+    "rows_hat",
+    "rows_scale",
+    "place",
+    "digits",
+)
+
+
+def saved_shapes(tokens, count, width):
+    pairs = tokens // TILE * HEADS
+    return dict(
+        gate=shape_of((tokens, width), F32),
+        hat=shape_of((tokens, width), F32),
+        hat_scale=shape_of((tokens, 1), F32),
+        qkv=shape_of((tokens, 3 * width), BF16),
+        slope=shape_of((pairs, TILE, TILE), F32),
+        weight=shape_of((pairs, TILE, TILE), BF16),
+        mixed=shape_of((tokens, width), BF16),
+        normed=shape_of((count, width), BF16),
+        rows_slope=shape_of((count, 4 * width), F32),
+        rows_hat=shape_of((count, width), F32),
+        rows_scale=shape_of((count, 1), F32),
+        place=shape_of((1, count), jnp.int32),
+        digits=shape_of((count, LANES), BF16),
+    )
+
+
 def forward_body(
+    capacity,
     rows_ref,
     item_ref,
     w_in_ref,
@@ -90,20 +128,21 @@
     owner_col_ref,
     owner_row_ref,
     number_ref,
-    qkv_ref,
-    gate_ref,
-    hat_ref,
-    hat_scale_ref,
-    mixed_ref,
-    weight_ref,
-    slope_ref,
-    normed_ref,
-    rows_hat_ref,
-    rows_scale_ref,
-    rows_slope_ref,
-    rank_ref,
-    digits_ref,
+    *refs,
 ):
+    size = len(SAVED)
+    held = dict(zip(SAVED, refs[size : 2 * size]))
+    sems = refs[-1]
+    copies = {
+        name: pltpu.make_async_copy(held[name], refs[index], sems.at[index])
+        for index, name in enumerate(SAVED)
+    }
+    gate_ref, hat_ref, hat_scale_ref, qkv_ref, slope_ref, weight_ref, mixed_ref = (
+        held[name] for name in SAVED[:7]
+    )
+    normed_ref, rows_slope_ref, rows_hat_ref, rows_scale_ref, place_ref, digits_ref = (
+        held[name] for name in SAVED[7:]
+    )
     count, width = rows_ref.shape
     tokens = item_ref.shape[0]
     across = jnp.broadcast_to(owner_row_ref[...], (count, count))
@@ -111,11 +150,14 @@
     sub = lax.broadcasted_iota(jnp.int32, (count, count), 0)
     lane = lax.broadcasted_iota(jnp.int32, (count, count), 1)
     earlier = jnp.where((across == down) & (sub < lane), 1.0, 0.0)
-    rank_ref[...] = jnp.sum(earlier, axis=0, keepdims=True).astype(jnp.int32)
+    rank = jnp.sum(earlier, axis=0, keepdims=True).astype(jnp.int32)
+    place_ref[...] = owner_row_ref[...] * capacity + rank
     number = jnp.broadcast_to(number_ref[...], (count, LANES))
     lane = lax.broadcasted_iota(jnp.int32, (count, LANES), 1)
     digits = jnp.where(lane == 0, number >> 5, jnp.where(lane == 1, number & 31, 0))
     digits_ref[...] = digits.astype(F32).astype(BF16)
+    copies["place"].start()
+    copies["digits"].start()
     values = rows_ref[...].astype(F32)
     shifted = values - jnp.mean(values, axis=-1, keepdims=True)
     scale = lax.rsqrt(jnp.mean(shifted * shifted, axis=-1, keepdims=True) + EPSILON)
@@ -124,6 +166,8 @@
     rows_scale_ref[...] = scale
     normed = (hat * gain_in_ref[...]).astype(BF16)
     normed_ref[...] = normed
+    for name in ("rows_hat", "rows_scale", "normed"):
+        copies[name].start()
     lane = lax.broadcasted_iota(jnp.int32, (tokens, count), 1)
     pick = jnp.where(lane == jnp.broadcast_to(item_ref[...], (tokens, count)), 1.0, 0.0)
     pick = pick.astype(BF16)
@@ -141,6 +185,8 @@
             qkv_ref[:, (part - 1) * width : part * width] = dot(pick, active.astype(BF16)).astype(
                 BF16
             )
+    for name in ("gate", "qkv", "rows_slope"):
+        copies[name].start()
     mask = tile_mask()
     factor = HDIM ** (-0.5)
     for tile in range(tokens // TILE):
@@ -165,45 +211,38 @@
         hat_ref[rows, :] = hat
         hat_scale_ref[rows, :] = scale
         mixed_ref[rows, :] = (hat * gain_out_ref[...] * gate_ref[rows, :]).astype(BF16)
+    for name in ("hat", "hat_scale", "slope", "weight", "mixed"):
+        copies[name].start()
+    for copy in copies.values():
+        copy.wait()
 
 
 def backward_body(
-    plan,
-    total_factor,
-    me_ref,
-    dest_ref,
-    item_ref,
-    owner_row_ref,
-    w_in_ref,
-    w_out_ref,
-    gain_in_ref,
-    gain_out_ref,
-    qkv_ref,
-    gate_ref,
-    hat_ref,
-    hat_scale_ref,
-    mixed_ref,
-    weight_ref,
-    slope_ref,
-    normed_ref,
-    rows_hat_ref,
-    rows_scale_ref,
-    rows_slope_ref,
-    rank_ref,
-    digits_ref,
-    got_ref,
-    table_ref,
-    keep_ref,
-    give_ref,
-    sums_ref,
-    active_ref,
-    grad_y_ref,
+    plan, total_factor, me_ref, dest_ref, item_ref, gain_in_ref, gain_out_ref, got_ref, *refs
 ):
+    size = len(SAVED) + 2
+    far_refs, (table_ref, keep_ref, give_ref), near_refs = (
+        refs[:size],
+        refs[size : size + 3],
+        refs[size + 3 : 2 * size + 3],
+    )
+    sums_ref, active_ref, grad_y_ref, sems = refs[2 * size + 3 :]
+    copies = [
+        pltpu.make_async_copy(far, near, sems.at[index])
+        for index, (far, near) in enumerate(zip(far_refs, near_refs))
+    ]
+    for copy in copies:
+        copy.start()
+    w_out_ref, gate_ref, hat_ref, hat_scale_ref, qkv_ref, slope_ref, weight_ref = near_refs[:7]
+    mixed_ref, normed_ref, rows_slope_ref, rows_hat_ref, rows_scale_ref = near_refs[7:12]
+    place_ref, digits_ref, w_in_ref = near_refs[12:]
     count, width = rows_hat_ref.shape
     tokens = hat_ref.shape[0]
     me = me_ref[0]
     for slot in range(got_ref.shape[0]):
         grad_y_ref[slot * SLOT : (slot + 1) * SLOT, :] = got_ref[dest_ref[slot]]
+    for copy in copies[:7]:
+        copy.wait()
     gain_total = jnp.zeros((1, width), F32)
     for tile in range(tokens // TILE):
         rows = slice(tile * TILE, (tile + 1) * TILE)
@@ -232,6 +271,8 @@
             ):
                 first = part * width + head * HDIM
                 active_ref[rows, first : first + HDIM] = value.astype(BF16)
+    for copy in copies[7:]:
+        copy.wait()
     grad_y = grad_y_ref[...]
     sums_ref[:, 4 * width : 5 * width] = (dot(mixed_ref[...], grad_y, TN) * total_factor).astype(
         BF16
@@ -262,7 +303,7 @@
     along = jnp.mean(inner * hat, axis=-1, keepdims=True)
     row_grad = (inner - mean - hat * along) * rows_scale_ref[...] + dot(gather, grad_y)
     places = table_ref.shape[0]
-    place = owner_row_ref[...] * plan.capacity + rank_ref[...]
+    place = place_ref[...]
     spots = lax.broadcasted_iota(jnp.int32, (places, count), 0)
     spread = jnp.where(spots == jnp.broadcast_to(place, (places, count)), 1.0, 0.0).astype(BF16)
     table_ref[:, :width] = dot(spread, row_grad.astype(BF16)).astype(BF16)
@@ -380,27 +421,18 @@
     )(me, exchange(packed, "dp"), grad_out)
     got = exchange(send, "dp")
 
-    pairs = tokens // TILE * HEADS
+    shapes = saved_shapes(tokens, count, width)
+    shapes = [shapes[name] for name in SAVED]
+    held = [pltpu.VMEM(item.shape, item.dtype) for item in shapes]
     saved = call(
-        forward_body,
-        (
-            shape_of((tokens, 3 * width), BF16),
-            shape_of((tokens, width), F32),
-            shape_of((tokens, width), F32),
-            shape_of((tokens, 1), F32),
-            shape_of((tokens, width), BF16),
-            shape_of((pairs, TILE, TILE), BF16),
-            shape_of((pairs, TILE, TILE), F32),
-            shape_of((count, width), BF16),
-            shape_of((count, width), F32),
-            shape_of((count, 1), F32),
-            shape_of((count, 4 * width), F32),
-            shape_of((1, count), jnp.int32),
-            shape_of((count, LANES), BF16),
-        ),
+        functools.partial(forward_body, plan.capacity),
+        shapes,
         [VMEM] * 8,
         flops=4 * count * width * width * 8,
         moved=10_000_000,
+        mebibytes=12 + tokens // 32,
+        scratch=held + [pltpu.SemaphoreType.DMA((len(SAVED),))],
+        out_space=HBM,
     )(
         touched_rows,
         row_of_token.reshape(tokens, 1),
@@ -416,25 +448,29 @@
     table_send, kept, sent = call(
         functools.partial(backward_body, plan, total_factor),
         [shape_of((devices_all * plan.capacity, width + LANES), BF16), half, half],
-        [SMEM] * 2 + [VMEM] * 20,
+        [SMEM] * 2 + [VMEM] * 4 + [HBM] * (len(SAVED) + 2),
         flops=4 * count * width * width * 20,
         moved=12_000_000,
-        scratch=[
+        mebibytes=12 + tokens // 32,
+        scratch=[pltpu.VMEM(w_out.shape, BF16)]
+        + held
+        + [
+            pltpu.VMEM(w_in.shape, BF16),
             pltpu.VMEM((width, plan.columns), BF16),
             pltpu.VMEM((tokens, 4 * width), BF16),
             pltpu.VMEM((tokens, width), BF16),
+            pltpu.SemaphoreType.DMA((len(SAVED) + 2,)),
         ],
     )(
         me,
         seq_dest,
         row_of_token.reshape(1, tokens),
-        row_owner.reshape(1, count),
-        w_in,
-        w_out,
         gain_in,
         gain_out,
+        got,
+        w_out,
         *saved,
-        got,
+        w_in,
     )
 
     kept = add(kept, swap(sent, (1, 1)))
@@ -442,16 +478,17 @@
         middle = kept.shape[0] // 2
         came = swap(kept[middle:], masks)
         kept = add(kept[:middle], came)
+    table_got = exchange(table_send.reshape(devices_all, plan.capacity, width + LANES), both)
+    kept, table_got = lax.optimization_barrier((kept, table_got))
     for masks in reversed(list(zip(*plan.orders))):
         kept = jnp.concatenate([kept, swap(kept, masks)])
-    came = swap(kept, (1, 1))
-
-    table_got = exchange(table_send.reshape(devices_all, plan.capacity, width + LANES), both)
     table_part = call(
         table_body,
         shape_of((ROWS_DEV, width), F32),
         [VMEM],
     )(table_got.reshape(devices_all * plan.capacity, width + LANES))
+    came = swap(kept, (1, 1))
+
     grad_w_in, grad_w_out, grad_gain_in, grad_gain_out = call(
         functools.partial(widen_body, plan),
         (

time: 160 us -> 150 us (0.938)
  blocking collectives: 24.4 us -> 0 us
  waiting for transfers between devices: 56.9 us -> 71.3 us
  Pallas kernels: 20.1 us -> 23.6 us
  starting transfers between devices: 29.5 us -> 26.5 us
    all_to_all x1 -> x0, blocking collectives: 24.4 us -> none  [exchange(): return lax.all_to_all(values, axes, split_axis=0, concat_axis=0, tiled=True)]
    ppermute x10, waiting for transfers between devices: 50.5 us -> 64.9 us  [swap(): return lax.ppermute(values, both, pairs)]
    ppermute x10, starting transfers between devices: 18.8 us -> 11.1 us  [swap(): return lax.ppermute(values, both, pairs)]
    all_to_all x2 -> x3, starting transfers between devices: 10.7 us -> 15.4 us  [exchange(): return lax.all_to_all(values, axes, split_axis=0, concat_axis=0, tiled=True)]
    pallas_call x1, Pallas kernels: 8.15 us -> 10.4 us  [on_device(): call(functools.partial(backward_body, plan, total_factor), [shape_of((dev...]
    unnamed x68 -> x69, local copies, waits for them, and re-layouts: 24.7 us -> 24.7 us
    all_to_all x2 -> x3, waiting for transfers between devices: 6.39 us -> 6.39 us  [exchange(): return lax.all_to_all(values, axes, split_axis=0, concat_axis=0, tiled=True)]
  transfers between devices with their start and end apart: 12 -> 13, of which waited for: 10 -> 10; matrix products, arithmetic and copies ran while one was open for 0% -> 0% of each run, Pallas kernels for 5% -> 6%
where the time goes in v4:
time: 150 us
  waiting for transfers between devices  71.3 us (48%)
  starting transfers between devices  26.5 us (18%)
  local copies, waits for them, and re-layouts  25.8 us (17%)
  Pallas kernels  23.6 us (16%)
  other arithmetic  1.51 us (1%)
    ppermute x10, waiting for transfers between devices, swap(): return lax.ppermute(values, both, pairs)  64.9 us
    unnamed x69, local copies, waits for them, and re-layouts  24.7 us
    all_to_all x3, starting transfers between devices, exchange(): return lax.all_to_all(values, axes, split_axis=0, concat_axis=0, tiled=True)  15.4 us
    ppermute x10, starting transfers between devices, swap(): return lax.ppermute(values, both, pairs)  11.1 us
    pallas_call x1, Pallas kernels, on_device(): call(functools.partial(backward_body, plan, total_factor), [shape_of((dev...  10.4 us
    pallas_call x1, Pallas kernels, on_device(): call(functools.partial(forward_body, plan.capacity), shapes, [VMEM] * 8,...  6.64 us
    all_to_all x3, waiting for transfers between devices, exchange(): return lax.all_to_all(values, axes, split_axis=0, concat_axis=0, tiled=True)  6.39 us
  transfers between devices with their start and end apart: 13, of which 10 were waited for; matrix products, arithmetic and copies ran while one was open for 0% of the time, Pallas kernels for 6%

profile of v4, /device:TPU:0, one launch (start us, length us, event | category | flops | bytes accessed | tf_op | source)
XLA Modules:
  0.0 149.5 jit_solution(17512719752588653862)
XLA Ops:
  0.7 0.7 multiply_add_fusion
  2.0 7.3 %all-to-all-start = ((s32[8,1,8]{2,1,0:T(1,128)}), s32[8,1,8]{2,1,0:T(1,128)S(1)}, u32[]{:S(2)}, u32[]{:S(2)}) async-start(s32[8,1,8]{2,1,0:T(1,128)} %broadcast_in_dim.15), calls=%async_computation | async-start | bytes 8192 | tf_op jit(solution)/shard_map/all_to_all | solution.py:414
  9.2 6.4 %all-to-all-done.packed_ref = s32[8,1,8]{2,1,0:T(1,128)S(1)} async-done(((s32[8,1,8]{2,1,0:T(1,128)}), s32[8,1,8]{2,1,0:T(1,128)S(1)}, u32[]{:S(2)}, u32[]{:S(2)}) %all-to-all-start) | async-done | bytes 288 | tf_op jit(solution)/shard_map/all_to_all | solution.py:414
  15.6 0.9 copy-done
  16.6 1.6 %shard_map.146 = bf16[8,64,512]{2,1,0:T(8,128)(2,1)} custom-call(s32[1]{0:T(128)} %bitcast.me_ref, s32[8,1,8]{2,1,0:T(1,128)S(1)} %all-to-all-done.packed_ref, bf16[256,512]{1,0:T(8,128)(2,1)S(1)} %copy-done), custom_call_target="tpu_custom_call" | custom-call | tf_op jit(solution)/shard_map/pallas_call | solution.py:417
  18.2 3.5 %all-to-all-start.1 = ((bf16[8,64,512]{2,1,0:T(8,128)(2,1)}), bf16[8,64,512]{2,1,0:T(8,128)(2,1)S(1)}, u32[]{:S(2)}, u32[]{:S(2)}) async-start(bf16[8,64,512]{2,1,0:T(8,128)(2,1)} %shard_map.146), calls=%async_computation.1 | async-start | bytes 1048576 | tf_op jit(solution)/shard_map/all_to_all | solution.py:414
  22.2 6.6 %shard_map.147 = (f32[512,512]{1,0:T(8,128)S(1)}, f32[512,512]{1,0:T(8,128)S(1)}, f32[512,1]{1,0:T(8,128)S(1)}, bf16[512,1536]{1,0:T(8,128)(2,1)S(1)}, f32[16,12...) custom-call(bf16[256,512]{1,0:T(8,128)(2,1)S(1)} %copy-done.5, ...), custom_call_target="tpu_custom_call" | custom-call | flops 2147483648 | bytes 10000000 | tf_op jit(solution)/shard_map/pallas_call | solution.py:427
  28.8 1.3 copy-done.9
  30.1 1.1 copy-done.11
  31.3 1.0 copy-done.13
  32.3 1.0 copy-done.15
  33.2 1.0 copy-done.17
  34.2 0.8 copy-done.19
  35.0 0.8 copy-done.21
  35.8 0.8 copy-done.23
  36.6 0.7 copy-done.25
  37.3 0.7 copy-done.27
  38.7 1.0 copy-done.4
  39.8 1.6 %copy-done.10 = f32[256,2048]{1,0:T(8,128)S(1)} copy-done((f32[256,2048]{1,0:T(8,128)S(1)}, f32[256,2048]{1,0:T(8,128)}, u32[]{:S(2)}) %copy-start.10) | copy-done | bytes 2097176
  41.4 1.4 copy-done.12
  42.8 1.2 copy-done.14
  44.0 1.2 copy-done.16
  45.2 1.2 copy-done.18
  46.4 1.0 copy-done.20
  47.5 1.0 copy-done.22
  48.5 1.0 copy-done.24
  49.6 0.9 copy-done.26
  50.5 0.9 copy-done.28
  51.5 0.9 copy-done.30
  52.4 10.4 %shard_map.148 = (bf16[512,640]{1,0:T(8,128)(2,1)}, bf16[16,16,2688]{2,1,0:T(8,128)(2,1)S(1)}, bf16[16,16,2688]{2,1,0:T(8,128)(2,1)S(1)}) custom-call(s32[1]{0:T(128)} %bitcast.me_ref, s32[8]{0:T(128)S(1)} %copy-done.8, s32[1,512]{1,0:T(1,128)S(1)} %bitcast.13, f32[1,512]{1,0:T(1,128)S(1)} %bitcast.16, f32[1,512]{1,0:T(1,128)S(1)} %bitcast.18, ...), custom_call_target="tpu_custom_call" | custom-call | flops 5368709120 | bytes 12000000 | tf_op jit(solution)/shard_map/pallas_call | solution.py:448
  62.9 3.1 %collective-permute-done = bf16[16,16,2688]{2,1,0:T(8,128)(2,1)S(1)} collective-permute-done((bf16[16,16,2688]{2,1,0:T(8,128)(2,1)S(1)}, bf16[16,16,2688]{2,1,0:T(8,128)(2,1)S(1)}, u32[]{:S(2)}, u32[]{:S(2)}) %collective-permute-start) | collective-permute-done | bytes 1376288 | tf_op jit(solution)/shard_map/ppermute | solution.py:411
  66.4 1.6 %collective-permute-start.1 = (bf16[8,16,2688]{2,1,0:T(8,128)(2,1)S(1)}, bf16[8,16,2688]{2,1,0:T(8,128)(2,1)S(1)}, u32[]{:S(2)}, u32[]{:S(2)}) collective-permute-start(bf16[8,16,2688]{2,1,0:T(8,128)(2,1)S(1)} %slice.33), channel_id=1, source_target_pairs={{0,2},{1,5},{2,0},{3,7},{4,6},{5,1},{6,4},{7,3},{8,10},{9,13},{10,... | collective-permute-start | bytes 2064392 | tf_op jit(solution)/shard_map/ppermute | solution.py:411
  67.9 9.4 %collective-permute-done.1 = bf16[8,16,2688]{2,1,0:T(8,128)(2,1)S(1)} collective-permute-done((bf16[8,16,2688]{2,1,0:T(8,128)(2,1)S(1)}, bf16[8,16,2688]{2,1,0:T(8,128)(2,1)S(1)}, u32[]{:S(2)}, u32[]{:S(2)}) %collective-permute-start.1) | collective-permute-done | bytes 688160 | tf_op jit(solution)/shard_map/ppermute | solution.py:411
  77.6 2.0 %collective-permute-start.2 = (bf16[4,16,2688]{2,1,0:T(8,128)(2,1)S(1)}, bf16[4,16,2688]{2,1,0:T(8,128)(2,1)S(1)}, u32[]{:S(2)}, u32[]{:S(2)}) collective-permute-start(bf16[4,16,2688]{2,1,0:T(8,128)(2,1)S(1)} %slice.35), channel_id=1, source_target_pairs={{0,4},{1,9},{2,6},{3,11},{4,0},{5,13},{6,2},{7,15},{8,12},{9,1},{1... | collective-permute-start | bytes 1032200 | tf_op jit(solution)/shard_map/ppermute | solution.py:411
  79.6 5.3 %collective-permute-done.2 = bf16[4,16,2688]{2,1,0:T(8,128)(2,1)S(1)} collective-permute-done((bf16[4,16,2688]{2,1,0:T(8,128)(2,1)S(1)}, bf16[4,16,2688]{2,1,0:T(8,128)(2,1)S(1)}, u32[]{:S(2)}, u32[]{:S(2)}) %collective-permute-start.2) | collective-permute-done | bytes 344096 | tf_op jit(solution)/shard_map/ppermute | solution.py:411
  85.0 2.0 %collective-permute-start.3 = (bf16[2,16,2688]{2,1,0:T(8,128)(2,1)S(1)}, bf16[2,16,2688]{2,1,0:T(8,128)(2,1)S(1)}, u32[]{:S(2)}, u32[]{:S(2)}) collective-permute-start(bf16[2,16,2688]{2,1,0:T(8,128)(2,1)S(1)} %slice.37), channel_id=1, source_target_pairs={{0,8},{1,3},{2,10},{3,1},{4,12},{5,7},{6,14},{7,5},{8,0},{9,11},{1... | collective-permute-start | bytes 516104 | tf_op jit(solution)/shard_map/ppermute | solution.py:411
  87.0 4.6 %all-to-all-start.2 = ((bf16[32,16,640]{2,1,0:T(8,128)(2,1)}), bf16[32,16,640]{2,1,0:T(8,128)(2,1)S(1)}, u32[]{:S(2)}, u32[]{:S(2)}) async-start(bf16[32,16,640]{2,1,0:T(8,128)(2,1)} %bitcast.7), calls=%async_computation.2 | async-start | bytes 1310720 | tf_op jit(solution)/shard_map/all_to_all | solution.py:414
  91.7 2.7 %collective-permute-start.4 = (bf16[1,16,2688]{2,1,0:T(8,128)(2,1)S(1)}, bf16[1,16,2688]{2,1,0:T(8,128)(2,1)S(1)}, u32[]{:S(2)}, u32[]{:S(2)}) collective-permute-start(bf16[1,16,2688]{2,1,0:T(8,128)(2,1)S(1)} %slice.39), channel_id=1, source_target_pairs={{0,16},{1,17},{2,18},{3,19},{4,20},{5,21},{6,22},{7,23},{8,24},{9,... | collective-permute-start | bytes 258056 | tf_op jit(solution)/shard_map/ppermute | solution.py:411
  94.4 18.7 %collective-permute-done.4 = bf16[1,16,2688]{2,1,0:T(8,128)(2,1)S(1)} collective-permute-done((bf16[1,16,2688]{2,1,0:T(8,128)(2,1)S(1)}, bf16[1,16,2688]{2,1,0:T(8,128)(2,1)S(1)}, u32[]{:S(2)}, u32[]{:S(2)}) %collective-permute-start.4) | collective-permute-done | bytes 86048 | tf_op jit(solution)/shard_map/ppermute | solution.py:411
  113.2 6.3 %collective-permute-done.5 = bf16[1,16,2688]{2,1,0:T(8,128)(2,1)S(1)} collective-permute-done((bf16[1,16,2688]{2,1,0:T(8,128)(2,1)S(1)}, bf16[1,16,2688]{2,1,0:T(8,128)(2,1)S(1)}, u32[]{:S(2)}, u32[]{:S(2)}) %collective-permute-start.5) | collective-permute-done | bytes 86048 | tf_op jit(solution)/shard_map/ppermute | solution.py:411
  119.6 5.4 %collective-permute-done.6 = bf16[2,16,2688]{2,1,0:T(8,128)(2,1)S(1)} collective-permute-done((bf16[2,16,2688]{2,1,0:T(8,128)(2,1)S(1)}, bf16[2,16,2688]{2,1,0:T(8,128)(2,1)S(1)}, u32[]{:S(2)}, u32[]{:S(2)}) %collective-permute-start.6) | collective-permute-done | bytes 172064 | tf_op jit(solution)/shard_map/ppermute | solution.py:411
  125.0 1.2 collective-permute-start.7
  126.3 6.1 %collective-permute-done.7 = bf16[4,16,2688]{2,1,0:T(8,128)(2,1)S(1)} collective-permute-done((bf16[4,16,2688]{2,1,0:T(8,128)(2,1)S(1)}, bf16[4,16,2688]{2,1,0:T(8,128)(2,1)S(1)}, u32[]{:S(2)}, u32[]{:S(2)}) %collective-permute-start.7) | collective-permute-done | bytes 344096 | tf_op jit(solution)/shard_map/ppermute | solution.py:411
  132.4 1.3 collective-permute-start.8
  133.8 9.7 %collective-permute-done.8 = bf16[8,16,2688]{2,1,0:T(8,128)(2,1)S(1)} collective-permute-done((bf16[8,16,2688]{2,1,0:T(8,128)(2,1)S(1)}, bf16[8,16,2688]{2,1,0:T(8,128)(2,1)S(1)}, u32[]{:S(2)}, u32[]{:S(2)}) %collective-permute-start.8) | collective-permute-done | bytes 688160 | tf_op jit(solution)/shard_map/ppermute | solution.py:411
  143.6 2.2 %shard_map.149 = f32[1024,512]{1,0:T(8,128)} custom-call(bf16[512,640]{1,0:T(8,128)(2,1)S(1)} %bitcast.11), custom_call_target="tpu_custom_call" | custom-call | tf_op jit(solution)/shard_map/pallas_call | solution.py:485
  145.8 1.0 collective-permute-done.9.came_ref
  146.7 2.8 %shard_map.150 = (f32[512,2048]{1,0:T(8,128)}, f32[512,512]{1,0:T(8,128)}, f32[1,512]{1,0:T(1,128)}, f32[1,512]{1,0:T(1,128)}) custom-call(s32[1]{0:T(128)} %bitcast.me_ref, bf16[16,16,2688]{2,1,0:T(8,128)(2,1)S(1)} %constant_dynamic-update-slice_fusion.own_ref, bf16[16,16,2688]{2,1,0:T(8,128)(2,1)S(1)} %collective-permute-done.9.came_ref), custom_call_target="tpu_custom_call" | custom-call | tf_op jit(solution)/shard_map/pallas_call | solution.py:492
  (69 shorter events, 3.1 us)
Async XLA Ops:
  0.6 21.0 %copy-start.31 = (s32[256]{0:T(256)S(1)}, s32[256]{0:T(256)}, u32[]{:S(2)}) copy-start(s32[256]{0:T(256)} %param.14) | copy-start | bytes 3076
  0.6 21.2 %copy-start.2 = (s32[256,1]{0,1:T(1,128)S(1)}, s32[256,1]{0,1:T(1,128)}, u32[]{:S(2)}) copy-start(s32[256,1]{0,1:T(1,128)} %param.13) | copy-start | bytes 3076
  0.7 21.3 %copy-start.1 = (s32[512]{0:T(512)S(1)}, s32[512]{0:T(512)}, u32[]{:S(2)}) copy-start(s32[512]{0:T(512)} %param.12) | copy-start | bytes 6148
  0.7 21.5 %copy-start.7 = (f32[512]{0:T(512)S(1)}, f32[512]{0:T(512)}, u32[]{:S(2)}) copy-start(f32[512]{0:T(512)} %param.21) | copy-start | bytes 6148
  0.7 21.5 %copy-start.6 = (f32[512]{0:T(512)S(1)}, f32[512]{0:T(512)}, u32[]{:S(2)}) copy-start(f32[512]{0:T(512)} %param.20) | copy-start | bytes 6148
  2.0 13.6 %all-to-all-start = ((s32[8,1,8]{2,1,0:T(1,128)}), s32[8,1,8]{2,1,0:T(1,128)S(1)}, u32[]{:S(2)}, u32[]{:S(2)}) async-start(s32[8,1,8]{2,1,0:T(1,128)} %broadcast_in_dim.15), calls=%async_computation | async-start | bytes 8192 | tf_op jit(solution)/shard_map/all_to_all | solution.py:414
  15.6 1.0 copy-start
  16.6 5.6 %copy-start.3 = (bf16[512,2048]{1,0:T(8,128)(2,1)S(1)}, bf16[512,2048]{1,0:T(8,128)(2,1)}, u32[]{:S(2)}) copy-start(bf16[512,2048]{1,0:T(8,128)(2,1)} %refs_14_.1) | copy-start | bytes 6291460
  16.6 5.6 %copy-start.5 = (bf16[256,512]{1,0:T(8,128)(2,1)S(1)}, bf16[256,512]{1,0:T(8,128)(2,1)}, u32[]{:S(2)}) copy-start(bf16[256,512]{1,0:T(8,128)(2,1)} %rows_ref.1) | copy-start | bytes 786436
  18.2 20.6 %all-to-all-start.1 = ((bf16[8,64,512]{2,1,0:T(8,128)(2,1)}), bf16[8,64,512]{2,1,0:T(8,128)(2,1)S(1)}, u32[]{:S(2)}, u32[]{:S(2)}) async-start(bf16[8,64,512]{2,1,0:T(8,128)(2,1)} %shard_map.146), calls=%async_computation.1 | async-start | bytes 1048576 | tf_op jit(solution)/shard_map/all_to_all | solution.py:414
  22.2 16.6 %copy-start.8 = (s32[8]{0:T(128)S(1)}, s32[8]{0:T(128)}, u32[]{:S(2)}) copy-start(s32[8]{0:T(128)} %dest_ref.1) | copy-start | bytes 100
  28.8 1.3 copy-start.9
  30.1 1.1 copy-start.11
  31.3 1.0 copy-start.13
  32.2 1.0 copy-start.15
  33.2 1.0 copy-start.17
  34.2 0.8 copy-start.19
  35.0 0.8 copy-start.21
  35.8 0.8 copy-start.23
  36.6 0.7 copy-start.25
  37.3 0.7 copy-start.27
  38.0 0.7 copy-start.29
  38.7 1.0 copy-start.4
  39.8 1.6 %copy-start.10 = (f32[256,2048]{1,0:T(8,128)S(1)}, f32[256,2048]{1,0:T(8,128)}, u32[]{:S(2)}) copy-start(f32[256,2048]{1,0:T(8,128)} %copy-done.9) | copy-start | bytes 6291460
  41.4 1.4 copy-start.12
  42.8 1.2 copy-start.14
  44.0 1.2 copy-start.16
  45.2 1.2 copy-start.18
  46.4 1.0 copy-start.20
  47.5 1.0 copy-start.22
  48.5 1.0 copy-start.24
  49.6 0.9 copy-start.26
  50.5 0.9 copy-start.28
  51.5 0.9 copy-start.30
  62.8 3.2 %collective-permute-start = (bf16[16,16,2688]{2,1,0:T(8,128)(2,1)S(1)}, bf16[16,16,2688]{2,1,0:T(8,128)(2,1)S(1)}, u32[]{:S(2)}, u32[]{:S(2)}) collective-permute-start(bf16[16,16,2688]{2,1,0:T(8,128)(2,1)S(1)} %get-tuple-element.41), channel_id=1, source_target_pairs={{0,1},{1,0},{2,3},{3,2},{4,5},{5,4},{6,7},{7,6},{8,9},{9,8},{10,11... | collective-permute-start | bytes 4128776 | tf_op jit(solution)/shard_map/ppermute | solution.py:411
  66.4 11.0 %collective-permute-start.1 = (bf16[8,16,2688]{2,1,0:T(8,128)(2,1)S(1)}, bf16[8,16,2688]{2,1,0:T(8,128)(2,1)S(1)}, u32[]{:S(2)}, u32[]{:S(2)}) collective-permute-start(bf16[8,16,2688]{2,1,0:T(8,128)(2,1)S(1)} %slice.33), channel_id=1, source_target_pairs={{0,2},{1,5},{2,0},{3,7},{4,6},{5,1},{6,4},{7,3},{8,10},{9,13},{10,... | collective-permute-start | bytes 2064392 | tf_op jit(solution)/shard_map/ppermute | solution.py:411
  77.6 7.3 %collective-permute-start.2 = (bf16[4,16,2688]{2,1,0:T(8,128)(2,1)S(1)}, bf16[4,16,2688]{2,1,0:T(8,128)(2,1)S(1)}, u32[]{:S(2)}, u32[]{:S(2)}) collective-permute-start(bf16[4,16,2688]{2,1,0:T(8,128)(2,1)S(1)} %slice.35), channel_id=1, source_target_pairs={{0,4},{1,9},{2,6},{3,11},{4,0},{5,13},{6,2},{7,15},{8,12},{9,1},{1... | collective-permute-start | bytes 1032200 | tf_op jit(solution)/shard_map/ppermute | solution.py:411
  85.0 6.6 %collective-permute-start.3 = (bf16[2,16,2688]{2,1,0:T(8,128)(2,1)S(1)}, bf16[2,16,2688]{2,1,0:T(8,128)(2,1)S(1)}, u32[]{:S(2)}, u32[]{:S(2)}) collective-permute-start(bf16[2,16,2688]{2,1,0:T(8,128)(2,1)S(1)} %slice.37), channel_id=1, source_target_pairs={{0,8},{1,3},{2,10},{3,1},{4,12},{5,7},{6,14},{7,5},{8,0},{9,11},{1... | collective-permute-start | bytes 516104 | tf_op jit(solution)/shard_map/ppermute | solution.py:411
  87.0 26.1 %all-to-all-start.2 = ((bf16[32,16,640]{2,1,0:T(8,128)(2,1)}), bf16[32,16,640]{2,1,0:T(8,128)(2,1)S(1)}, u32[]{:S(2)}, u32[]{:S(2)}) async-start(bf16[32,16,640]{2,1,0:T(8,128)(2,1)} %bitcast.7), calls=%async_computation.2 | async-start | bytes 1310720 | tf_op jit(solution)/shard_map/all_to_all | solution.py:414
  91.7 21.4 %collective-permute-start.4 = (bf16[1,16,2688]{2,1,0:T(8,128)(2,1)S(1)}, bf16[1,16,2688]{2,1,0:T(8,128)(2,1)S(1)}, u32[]{:S(2)}, u32[]{:S(2)}) collective-permute-start(bf16[1,16,2688]{2,1,0:T(8,128)(2,1)S(1)} %slice.39), channel_id=1, source_target_pairs={{0,16},{1,17},{2,18},{3,19},{4,20},{5,21},{6,22},{7,23},{8,24},{9,... | collective-permute-start | bytes 258056 | tf_op jit(solution)/shard_map/ppermute | solution.py:411
  113.1 6.3 %collective-permute-start.5 = (bf16[1,16,2688]{2,1,0:T(8,128)(2,1)S(1)}, bf16[1,16,2688]{2,1,0:T(8,128)(2,1)S(1)}, u32[]{:S(2)}, u32[]{:S(2)}) collective-permute-start(bf16[1,16,2688]{2,1,0:T(8,128)(2,1)S(1)} %add_convert_fusion.4), channel_id=1, source_target_pairs={{0,16},{1,17},{2,18},{3,19},{4,20},{5,21},{6,22},{7,23},{8,24},{9,... | collective-permute-start | bytes 258056 | tf_op jit(solution)/shard_map/ppermute | solution.py:411
  119.5 5.5 %collective-permute-start.6 = (bf16[2,16,2688]{2,1,0:T(8,128)(2,1)S(1)}, bf16[2,16,2688]{2,1,0:T(8,128)(2,1)S(1)}, u32[]{:S(2)}, u32[]{:S(2)}) collective-permute-start(bf16[2,16,2688]{2,1,0:T(8,128)(2,1)S(1)} %pad_maximum_fusion.2), channel_id=1, source_target_pairs={{0,8},{1,3},{2,10},{3,1},{4,12},{5,7},{6,14},{7,5},{8,0},{9,11},{1... | collective-permute-start | bytes 516104 | tf_op jit(solution)/shard_map/ppermute | solution.py:411
  125.0 7.3 %collective-permute-start.7 = (bf16[4,16,2688]{2,1,0:T(8,128)(2,1)S(1)}, bf16[4,16,2688]{2,1,0:T(8,128)(2,1)S(1)}, u32[]{:S(2)}, u32[]{:S(2)}) collective-permute-start(bf16[4,16,2688]{2,1,0:T(8,128)(2,1)S(1)} %pad_maximum_fusion.1), channel_id=1, source_target_pairs={{0,4},{1,9},{2,6},{3,11},{4,0},{5,13},{6,2},{7,15},{8,12},{9,1},{1... | collective-permute-start | bytes 1032200 | tf_op jit(solution)/shard_map/ppermute | solution.py:411
  132.4 11.0 %collective-permute-start.8 = (bf16[8,16,2688]{2,1,0:T(8,128)(2,1)S(1)}, bf16[8,16,2688]{2,1,0:T(8,128)(2,1)S(1)}, u32[]{:S(2)}, u32[]{:S(2)}) collective-permute-start(bf16[8,16,2688]{2,1,0:T(8,128)(2,1)S(1)} %pad_maximum_fusion), channel_id=1, source_target_pairs={{0,2},{1,5},{2,0},{3,7},{4,6},{5,1},{6,4},{7,3},{8,10},{9,13},{10,... | collective-permute-start | bytes 2064392 | tf_op jit(solution)/shard_map/ppermute | solution.py:411
  143.5 3.2 %collective-permute-start.9 = (bf16[16,16,2688]{2,1,0:T(8,128)(2,1)S(1)}, bf16[16,16,2688]{2,1,0:T(8,128)(2,1)S(1)}, u32[]{:S(2)}, u32[]{:S(2)}) collective-permute-start(bf16[16,16,2688]{2,1,0:T(8,128)(2,1)S(1)} %constant_dynamic-update-slice_fusion.own_ref), channel_id=1, source_target_pairs={{0,1},{1,0},{2,3},{3,2},{4,5},{5,4},{6,7},{7,6},{8,9},{9,8},{10,11... | collective-permute-start | bytes 4128776 | tf_op jit(solution)/shard_map/ppermute | solution.py:411

commit v5 on v4

--- a/solution.py
+++ b/solution.py
@@ -430,7 +430,7 @@
         [VMEM] * 8,
         flops=4 * count * width * width * 8,
         moved=10_000_000,
-        mebibytes=12 + tokens // 32,
+        mebibytes=58,
         scratch=held + [pltpu.SemaphoreType.DMA((len(SAVED),))],
         out_space=HBM,
     )(
@@ -451,7 +451,7 @@
         [SMEM] * 2 + [VMEM] * 4 + [HBM] * (len(SAVED) + 2),
         flops=4 * count * width * width * 20,
         moved=12_000_000,
-        mebibytes=12 + tokens // 32,
+        mebibytes=58,
         scratch=[pltpu.VMEM(w_out.shape, BF16)]
         + held
         + [
@@ -474,12 +474,13 @@
     )
 
     kept = add(kept, swap(sent, (1, 1)))
-    for masks in zip(*plan.orders):
+    table_got = exchange(table_send.reshape(devices_all, plan.capacity, width + LANES), both)
+    for step, masks in enumerate(zip(*plan.orders)):
+        if step == 2:
+            kept, table_got = lax.optimization_barrier((kept, table_got))
         middle = kept.shape[0] // 2
         came = swap(kept[middle:], masks)
         kept = add(kept[:middle], came)
-    table_got = exchange(table_send.reshape(devices_all, plan.capacity, width + LANES), both)
-    kept, table_got = lax.optimization_barrier((kept, table_got))
     for masks in reversed(list(zip(*plan.orders))):
         kept = jnp.concatenate([kept, swap(kept, masks)])
     table_part = call(

time: 150 us -> 133 us (0.89)
  local copies, waits for them, and re-layouts: 25.8 us -> 5.03 us
  Pallas kernels: 23.6 us -> 28.8 us
  starting transfers between devices: 26.5 us -> 23.6 us
    unnamed x69 -> x14, local copies, waits for them, and re-layouts: 24.7 us -> 2.62 us
    pallas_call x1, Pallas kernels: 10.4 us -> 13.1 us  [on_device(): call(functools.partial(backward_body, plan, total_factor), [shape_of((dev...]
    pallas_call x1, Pallas kernels: 6.64 us -> 9.11 us  [on_device(): call(functools.partial(forward_body, plan.capacity), shapes, [VMEM] * 8,...]
    ppermute x10, starting transfers between devices: 11.1 us -> 9.3 us  [swap(): return lax.ppermute(values, both, pairs)]
    all_to_all x3, waiting for transfers between devices: 6.39 us -> 8.07 us  [exchange(): return lax.all_to_all(values, axes, split_axis=0, concat_axis=0, tiled=True)]
    ppermute x10, waiting for transfers between devices: 64.9 us -> 63.2 us  [swap(): return lax.ppermute(values, both, pairs)]
  transfers between devices with their start and end apart: 13 -> 13, of which waited for: 10 -> 12; matrix products, arithmetic and copies ran while one was open for 0% -> 2% of each run, Pallas kernels for 6% -> 9%
where the time goes in v5:
time: 133 us; the launch traced here: 132 us
  waiting for transfers between devices  71.3 us (54%)
  Pallas kernels  28.8 us (22%)
  starting transfers between devices  23.6 us (18%)
  local copies, waits for them, and re-layouts  5.03 us (4%)
  other arithmetic  2.87 us (2%)
    ppermute x10, waiting for transfers between devices, swap(): return lax.ppermute(values, both, pairs)  63.2 us
    all_to_all x3, starting transfers between devices, exchange(): return lax.all_to_all(values, axes, split_axis=0, concat_axis=0, tiled=True)  14.3 us
    pallas_call x1, Pallas kernels, on_device(): call(functools.partial(backward_body, plan, total_factor), [shape_of((dev...  13.1 us
    ppermute x10, starting transfers between devices, swap(): return lax.ppermute(values, both, pairs)  9.3 us
    pallas_call x1, Pallas kernels, on_device(): call(functools.partial(forward_body, plan.capacity), shapes, [VMEM] * 8,...  9.11 us
    all_to_all x3, waiting for transfers between devices, exchange(): return lax.all_to_all(values, axes, split_axis=0, concat_axis=0, tiled=True)  8.07 us
    pallas_call x1, Pallas kernels, on_device(): call(functools.partial(widen_body, plan), (shape_of(w_in.shape, F32), sha...  2.81 us
  transfers between devices with their start and end apart: 13, of which 12 were waited for; matrix products, arithmetic and copies ran while one was open for 2% of the time, Pallas kernels for 9%

profile of v5, /device:TPU:0, one launch (start us, length us, event | category | flops | bytes accessed | tf_op | source)
XLA Modules:
  0.0 132.4 jit_solution(17223996805120405258)
XLA Ops:
  0.6 0.0 copy-start.3
  0.6 0.0 copy-start.4
  0.7 0.0 copy-start.2
  0.7 0.7 multiply_add_fusion
  1.4 0.6 broadcast_in_dim.15
  2.0 7.3 %all-to-all-start = ((s32[8,1,8]{2,1,0:T(1,128)}), s32[8,1,8]{2,1,0:T(1,128)S(1)}, u32[]{:S(2)}, u32[]{:S(2)}) async-start(s32[8,1,8]{2,1,0:T(1,128)} %broadcast_in_dim.15), calls=%async_computation | async-start | bytes 8192 | tf_op jit(solution)/shard_map/all_to_all | solution.py:414
  9.2 6.4 %all-to-all-done.packed_ref = s32[8,1,8]{2,1,0:T(1,128)S(1)} async-done(((s32[8,1,8]{2,1,0:T(1,128)}), s32[8,1,8]{2,1,0:T(1,128)S(1)}, u32[]{:S(2)}, u32[]{:S(2)}) %all-to-all-start) | async-done | bytes 288 | tf_op jit(solution)/shard_map/all_to_all | solution.py:414
  15.6 0.9 copy-done
  16.5 1.6 %shard_map.146 = bf16[8,64,512]{2,1,0:T(8,128)(2,1)} custom-call(s32[1]{0:T(128)} %bitcast.me_ref, s32[8,1,8]{2,1,0:T(1,128)S(1)} %all-to-all-done.packed_ref, bf16[256,512]{1,0:T(8,128)(2,1)S(1)} %copy-done), custom_call_target="tpu_custom_call" | custom-call | tf_op jit(solution)/shard_map/pallas_call | solution.py:417
  18.1 3.5 %all-to-all-start.1 = ((bf16[8,64,512]{2,1,0:T(8,128)(2,1)}), bf16[8,64,512]{2,1,0:T(8,128)(2,1)S(1)}, u32[]{:S(2)}, u32[]{:S(2)}) async-start(bf16[8,64,512]{2,1,0:T(8,128)(2,1)} %shard_map.146), calls=%async_computation.1 | async-start | bytes 1048576 | tf_op jit(solution)/shard_map/all_to_all | solution.py:414
  21.6 0.0 copy-done.3
  21.6 0.8 copy.19.number_ref
  22.4 0.0 copy-done.4
  22.4 0.8 copy.18.owner_col_ref
  23.2 0.9 copy.17.item_ref
  24.1 9.1 %shard_map.147 = (f32[512,512]{1,0:T(8,128)}, f32[512,512]{1,0:T(8,128)}, f32[512,1]{1,0:T(8,128)}, bf16[512,1536]{1,0:T(8,128)(2,1)}, f32[16,128,128]{2,1,0:T(8...) custom-call(bf16[256,512]{1,0:T(8,128)(2,1)} %rows_ref.1, ...), custom_call_target="tpu_custom_call" | custom-call | flops 2147483648 | bytes 10000000 | tf_op jit(solution)/shard_map/pallas_call | solution.py:427
  33.2 1.7 %all-to-all-done.1.got_ref = bf16[8,64,512]{2,1,0:T(8,128)(2,1)S(1)} async-done(((bf16[8,64,512]{2,1,0:T(8,128)(2,1)}), bf16[8,64,512]{2,1,0:T(8,128)(2,1)S(1)}, u32[]{:S(2)}, u32[]{:S(2)}) %all-to-all-start.1) | async-done | bytes 524320 | tf_op jit(solution)/shard_map/all_to_all | solution.py:414
  34.9 0.8 copy-done.1
  35.7 13.1 %shard_map.148 = (bf16[512,640]{1,0:T(8,128)(2,1)}, bf16[16,16,2688]{2,1,0:T(8,128)(2,1)}, bf16[16,16,2688]{2,1,0:T(8,128)(2,1)}) custom-call(s32[1]{0:T(128)} %bitcast.me_ref, s32[8]{0:T(128)} %dest_ref.1, s32[1,512]{1,0:T(1,128)} %bitcast.13, f32[1,512]{1,0:T(1,128)} %bitcast.18, f32[1,512]{1,0:T(1,128)} %bitcast.20, bf16[8,64,512]{2,1,0:T(8,128)(2,1)} %copy-done.1, ...), custom_call_target="tpu_custom_call" | custom-call | flops 5368709120 | bytes 12000000 | tf_op jit(solution)/shard_map/pallas_call | solution.py:448
  48.8 0.1 collective-permute-start
  48.9 3.3 %collective-permute-done = bf16[16,16,2688]{2,1,0:T(8,128)(2,1)S(1)} collective-permute-done((bf16[16,16,2688]{2,1,0:T(8,128)(2,1)}, bf16[16,16,2688]{2,1,0:T(8,128)(2,1)S(1)}, u32[]{:S(2)}, u32[]{:S(2)}) %collective-permute-start) | collective-permute-done | bytes 1376288 | tf_op jit(solution)/shard_map/ppermute | solution.py:411
  52.2 1.7 %add_convert_fusion = bf16[16,16,2688]{2,1,0:T(8,128)(2,1)S(1)} fusion(bf16[16,16,2688]{2,1,0:T(8,128)(2,1)S(1)} %collective-permute-done, bf16[16,16,2688]{2,1,0:T(8,128)(2,1)} %get-tuple-element.40), kind=kLoop, calls=%fused_computation | loop fusion | flops 2752512 | bytes 4128768 | tf_op jit(solution)/shard_map/convert_element_type | solution.py:383
  54.0 1.6 %collective-permute-start.1 = (bf16[8,16,2688]{2,1,0:T(8,128)(2,1)S(1)}, bf16[8,16,2688]{2,1,0:T(8,128)(2,1)S(1)}, u32[]{:S(2)}, u32[]{:S(2)}) collective-permute-start(bf16[8,16,2688]{2,1,0:T(8,128)(2,1)S(1)} %slice.33), channel_id=1, source_target_pairs={{0,2},{1,5},{2,0},{3,7},{4,6},{5,1},{6,4},{7,3},{8,10},{9,13},{10,... | collective-permute-start | bytes 2064392 | tf_op jit(solution)/shard_map/ppermute | solution.py:411
  55.5 3.5 %all-to-all-start.2 = ((bf16[32,16,640]{2,1,0:T(8,128)(2,1)}), bf16[32,16,640]{2,1,0:T(8,128)(2,1)S(1)}, u32[]{:S(2)}, u32[]{:S(2)}) async-start(bf16[32,16,640]{2,1,0:T(8,128)(2,1)} %bitcast.12), calls=%async_computation.2 | async-start | bytes 1310720 | tf_op jit(solution)/shard_map/all_to_all | solution.py:414
  59.1 10.3 %collective-permute-done.1 = bf16[8,16,2688]{2,1,0:T(8,128)(2,1)S(1)} collective-permute-done((bf16[8,16,2688]{2,1,0:T(8,128)(2,1)S(1)}, bf16[8,16,2688]{2,1,0:T(8,128)(2,1)S(1)}, u32[]{:S(2)}, u32[]{:S(2)}) %collective-permute-start.1) | collective-permute-done | bytes 688160 | tf_op jit(solution)/shard_map/ppermute | solution.py:411
  69.3 0.2 add_convert_fusion.1
  69.5 1.7 %collective-permute-start.2 = (bf16[4,16,2688]{2,1,0:T(8,128)(2,1)S(1)}, bf16[4,16,2688]{2,1,0:T(8,128)(2,1)S(1)}, u32[]{:S(2)}, u32[]{:S(2)}) collective-permute-start(bf16[4,16,2688]{2,1,0:T(8,128)(2,1)S(1)} %slice.35), channel_id=1, source_target_pairs={{0,4},{1,9},{2,6},{3,11},{4,0},{5,13},{6,2},{7,15},{8,12},{9,1},{1... | collective-permute-start | bytes 1032200 | tf_op jit(solution)/shard_map/ppermute | solution.py:411
  71.2 6.5 %collective-permute-done.2 = bf16[4,16,2688]{2,1,0:T(8,128)(2,1)S(1)} collective-permute-done((bf16[4,16,2688]{2,1,0:T(8,128)(2,1)S(1)}, bf16[4,16,2688]{2,1,0:T(8,128)(2,1)S(1)}, u32[]{:S(2)}, u32[]{:S(2)}) %collective-permute-start.2) | collective-permute-done | bytes 344096 | tf_op jit(solution)/shard_map/ppermute | solution.py:411
  77.7 0.1 add_convert_fusion.2
  77.8 0.0 all-to-all-done.2
  77.9 0.6 collective-permute-start.3
  78.4 4.9 %collective-permute-done.3 = bf16[2,16,2688]{2,1,0:T(8,128)(2,1)S(1)} collective-permute-done((bf16[2,16,2688]{2,1,0:T(8,128)(2,1)S(1)}, bf16[2,16,2688]{2,1,0:T(8,128)(2,1)S(1)}, u32[]{:S(2)}, u32[]{:S(2)}) %collective-permute-start.3) | collective-permute-done | bytes 172064 | tf_op jit(solution)/shard_map/ppermute | solution.py:411
  83.4 0.8 collective-permute-start.4
  84.2 5.5 %collective-permute-done.4 = bf16[1,16,2688]{2,1,0:T(8,128)(2,1)S(1)} collective-permute-done((bf16[1,16,2688]{2,1,0:T(8,128)(2,1)S(1)}, bf16[1,16,2688]{2,1,0:T(8,128)(2,1)S(1)}, u32[]{:S(2)}, u32[]{:S(2)}) %collective-permute-start.4) | collective-permute-done | bytes 86048 | tf_op jit(solution)/shard_map/ppermute | solution.py:411
  89.7 0.1 collective-permute-start.5
  89.8 5.5 %collective-permute-done.5 = bf16[1,16,2688]{2,1,0:T(8,128)(2,1)S(1)} collective-permute-done((bf16[1,16,2688]{2,1,0:T(8,128)(2,1)S(1)}, bf16[1,16,2688]{2,1,0:T(8,128)(2,1)S(1)}, u32[]{:S(2)}, u32[]{:S(2)}) %collective-permute-start.5) | collective-permute-done | bytes 86048 | tf_op jit(solution)/shard_map/ppermute | solution.py:411
  95.3 0.1 collective-permute-start.6
  95.4 7.2 %collective-permute-done.6 = bf16[2,16,2688]{2,1,0:T(8,128)(2,1)S(1)} collective-permute-done((bf16[2,16,2688]{2,1,0:T(8,128)(2,1)S(1)}, bf16[2,16,2688]{2,1,0:T(8,128)(2,1)S(1)}, u32[]{:S(2)}, u32[]{:S(2)}) %collective-permute-start.6) | collective-permute-done | bytes 172064 | tf_op jit(solution)/shard_map/ppermute | solution.py:411
  102.7 0.1 collective-permute-start.7
  102.7 10.2 %collective-permute-done.7 = bf16[4,16,2688]{2,1,0:T(8,128)(2,1)S(1)} collective-permute-done((bf16[4,16,2688]{2,1,0:T(8,128)(2,1)S(1)}, bf16[4,16,2688]{2,1,0:T(8,128)(2,1)S(1)}, u32[]{:S(2)}, u32[]{:S(2)}) %collective-permute-start.7) | collective-permute-done | bytes 344096 | tf_op jit(solution)/shard_map/ppermute | solution.py:411
  113.0 0.1 pad_maximum_fusion
  113.1 4.3 %collective-permute-start.8 = (bf16[8,16,2688]{2,1,0:T(8,128)(2,1)S(1)}, bf16[8,16,2688]{2,1,0:T(8,128)(2,1)S(1)}, u32[]{:S(2)}, u32[]{:S(2)}) collective-permute-start(bf16[8,16,2688]{2,1,0:T(8,128)(2,1)S(1)} %pad_maximum_fusion), channel_id=1, source_target_pairs={{0,2},{1,5},{2,0},{3,7},{4,6},{5,1},{6,4},{7,3},{8,10},{9,13},{10,... | collective-permute-start | bytes 2064392 | tf_op jit(solution)/shard_map/ppermute | solution.py:411
  117.4 8.8 %collective-permute-done.8 = bf16[8,16,2688]{2,1,0:T(8,128)(2,1)S(1)} collective-permute-done((bf16[8,16,2688]{2,1,0:T(8,128)(2,1)S(1)}, bf16[8,16,2688]{2,1,0:T(8,128)(2,1)S(1)}, u32[]{:S(2)}, u32[]{:S(2)}) %collective-permute-start.8) | collective-permute-done | bytes 688160 | tf_op jit(solution)/shard_map/ppermute | solution.py:411
  126.3 0.1 constant_dynamic-update-slice_fusion.own_ref
  126.4 0.1 collective-permute-start.9
  126.4 2.2 %shard_map.149 = f32[1024,512]{1,0:T(8,128)} custom-call(bf16[512,640]{1,0:T(8,128)(2,1)S(1)} %bitcast.11), custom_call_target="tpu_custom_call" | custom-call | tf_op jit(solution)/shard_map/pallas_call | solution.py:486
  128.6 1.0 collective-permute-done.9.came_ref
  129.5 2.8 %shard_map.150 = (f32[512,2048]{1,0:T(8,128)}, f32[512,512]{1,0:T(8,128)}, f32[1,512]{1,0:T(1,128)}, f32[1,512]{1,0:T(1,128)}) custom-call(s32[1]{0:T(128)} %bitcast.me_ref, bf16[16,16,2688]{2,1,0:T(8,128)(2,1)S(1)} %constant_dynamic-update-slice_fusion.own_ref, bf16[16,16,2688]{2,1,0:T(8,128)(2,1)S(1)} %collective-permute-done.9.came_ref), custom_call_target="tpu_custom_call" | custom-call | tf_op jit(solution)/shard_map/pallas_call | solution.py:493
  (14 shorter events, 0.3 us)
Async XLA Ops:
  0.6 21.0 %copy-start.3 = (s32[256]{0:T(256)S(1)}, s32[256]{0:T(256)}, u32[]{:S(2)}) copy-start(s32[256]{0:T(256)} %param.14) | copy-start | bytes 3076
  0.6 21.8 %copy-start.4 = (s32[256,1]{0,1:T(1,128)S(1)}, s32[256,1]{0,1:T(1,128)}, u32[]{:S(2)}) copy-start(s32[256,1]{0,1:T(1,128)} %param.13) | copy-start | bytes 3076
  0.7 22.6 %copy-start.2 = (s32[512]{0:T(512)S(1)}, s32[512]{0:T(512)}, u32[]{:S(2)}) copy-start(s32[512]{0:T(512)} %param.12) | copy-start | bytes 6148
  2.0 13.6 %all-to-all-start = ((s32[8,1,8]{2,1,0:T(1,128)}), s32[8,1,8]{2,1,0:T(1,128)S(1)}, u32[]{:S(2)}, u32[]{:S(2)}) async-start(s32[8,1,8]{2,1,0:T(1,128)} %broadcast_in_dim.15), calls=%async_computation | async-start | bytes 8192 | tf_op jit(solution)/shard_map/all_to_all | solution.py:414
  15.6 1.0 copy-start
  18.1 16.8 %all-to-all-start.1 = ((bf16[8,64,512]{2,1,0:T(8,128)(2,1)}), bf16[8,64,512]{2,1,0:T(8,128)(2,1)S(1)}, u32[]{:S(2)}, u32[]{:S(2)}) async-start(bf16[8,64,512]{2,1,0:T(8,128)(2,1)} %shard_map.146), calls=%async_computation.1 | async-start | bytes 1048576 | tf_op jit(solution)/shard_map/all_to_all | solution.py:414
  34.9 0.8 copy-start.1
  48.8 3.4 %collective-permute-start = (bf16[16,16,2688]{2,1,0:T(8,128)(2,1)}, bf16[16,16,2688]{2,1,0:T(8,128)(2,1)S(1)}, u32[]{:S(2)}, u32[]{:S(2)}) collective-permute-start(bf16[16,16,2688]{2,1,0:T(8,128)(2,1)} %get-tuple-element.41), channel_id=1, source_target_pairs={{0,1},{1,0},{2,3},{3,2},{4,5},{5,4},{6,7},{7,6},{8,9},{9,8},{10,11... | collective-permute-start | bytes 4128776 | tf_op jit(solution)/shard_map/ppermute | solution.py:411
  54.0 15.4 %collective-permute-start.1 = (bf16[8,16,2688]{2,1,0:T(8,128)(2,1)S(1)}, bf16[8,16,2688]{2,1,0:T(8,128)(2,1)S(1)}, u32[]{:S(2)}, u32[]{:S(2)}) collective-permute-start(bf16[8,16,2688]{2,1,0:T(8,128)(2,1)S(1)} %slice.33), channel_id=1, source_target_pairs={{0,2},{1,5},{2,0},{3,7},{4,6},{5,1},{6,4},{7,3},{8,10},{9,13},{10,... | collective-permute-start | bytes 2064392 | tf_op jit(solution)/shard_map/ppermute | solution.py:411
  55.5 22.3 %all-to-all-start.2 = ((bf16[32,16,640]{2,1,0:T(8,128)(2,1)}), bf16[32,16,640]{2,1,0:T(8,128)(2,1)S(1)}, u32[]{:S(2)}, u32[]{:S(2)}) async-start(bf16[32,16,640]{2,1,0:T(8,128)(2,1)} %bitcast.12), calls=%async_computation.2 | async-start | bytes 1310720 | tf_op jit(solution)/shard_map/all_to_all | solution.py:414
  69.5 8.2 %collective-permute-start.2 = (bf16[4,16,2688]{2,1,0:T(8,128)(2,1)S(1)}, bf16[4,16,2688]{2,1,0:T(8,128)(2,1)S(1)}, u32[]{:S(2)}, u32[]{:S(2)}) collective-permute-start(bf16[4,16,2688]{2,1,0:T(8,128)(2,1)S(1)} %slice.35), channel_id=1, source_target_pairs={{0,4},{1,9},{2,6},{3,11},{4,0},{5,13},{6,2},{7,15},{8,12},{9,1},{1... | collective-permute-start | bytes 1032200 | tf_op jit(solution)/shard_map/ppermute | solution.py:411
  77.9 5.5 %collective-permute-start.3 = (bf16[2,16,2688]{2,1,0:T(8,128)(2,1)S(1)}, bf16[2,16,2688]{2,1,0:T(8,128)(2,1)S(1)}, u32[]{:S(2)}, u32[]{:S(2)}) collective-permute-start(bf16[2,16,2688]{2,1,0:T(8,128)(2,1)S(1)} %slice.29), channel_id=1, source_target_pairs={{0,8},{1,3},{2,10},{3,1},{4,12},{5,7},{6,14},{7,5},{8,0},{9,11},{1... | collective-permute-start | bytes 516104 | tf_op jit(solution)/shard_map/ppermute | solution.py:411
  83.4 6.3 %collective-permute-start.4 = (bf16[1,16,2688]{2,1,0:T(8,128)(2,1)S(1)}, bf16[1,16,2688]{2,1,0:T(8,128)(2,1)S(1)}, u32[]{:S(2)}, u32[]{:S(2)}) collective-permute-start(bf16[1,16,2688]{2,1,0:T(8,128)(2,1)S(1)} %slice.37), channel_id=1, source_target_pairs={{0,16},{1,17},{2,18},{3,19},{4,20},{5,21},{6,22},{7,23},{8,24},{9,... | collective-permute-start | bytes 258056 | tf_op jit(solution)/shard_map/ppermute | solution.py:411
  89.7 5.5 %collective-permute-start.5 = (bf16[1,16,2688]{2,1,0:T(8,128)(2,1)S(1)}, bf16[1,16,2688]{2,1,0:T(8,128)(2,1)S(1)}, u32[]{:S(2)}, u32[]{:S(2)}) collective-permute-start(bf16[1,16,2688]{2,1,0:T(8,128)(2,1)S(1)} %get-tuple-element.50), channel_id=1, source_target_pairs={{0,16},{1,17},{2,18},{3,19},{4,20},{5,21},{6,22},{7,23},{8,24},{9,... | collective-permute-start | bytes 258056 | tf_op jit(solution)/shard_map/ppermute | solution.py:411
  95.3 7.3 %collective-permute-start.6 = (bf16[2,16,2688]{2,1,0:T(8,128)(2,1)S(1)}, bf16[2,16,2688]{2,1,0:T(8,128)(2,1)S(1)}, u32[]{:S(2)}, u32[]{:S(2)}) collective-permute-start(bf16[2,16,2688]{2,1,0:T(8,128)(2,1)S(1)} %pad_maximum_fusion.2), channel_id=1, source_target_pairs={{0,8},{1,3},{2,10},{3,1},{4,12},{5,7},{6,14},{7,5},{8,0},{9,11},{1... | collective-permute-start | bytes 516104 | tf_op jit(solution)/shard_map/ppermute | solution.py:411
  102.7 10.3 %collective-permute-start.7 = (bf16[4,16,2688]{2,1,0:T(8,128)(2,1)S(1)}, bf16[4,16,2688]{2,1,0:T(8,128)(2,1)S(1)}, u32[]{:S(2)}, u32[]{:S(2)}) collective-permute-start(bf16[4,16,2688]{2,1,0:T(8,128)(2,1)S(1)} %pad_maximum_fusion.1), channel_id=1, source_target_pairs={{0,4},{1,9},{2,6},{3,11},{4,0},{5,13},{6,2},{7,15},{8,12},{9,1},{1... | collective-permute-start | bytes 1032200 | tf_op jit(solution)/shard_map/ppermute | solution.py:411
  113.1 13.2 %collective-permute-start.8 = (bf16[8,16,2688]{2,1,0:T(8,128)(2,1)S(1)}, bf16[8,16,2688]{2,1,0:T(8,128)(2,1)S(1)}, u32[]{:S(2)}, u32[]{:S(2)}) collective-permute-start(bf16[8,16,2688]{2,1,0:T(8,128)(2,1)S(1)} %pad_maximum_fusion), channel_id=1, source_target_pairs={{0,2},{1,5},{2,0},{3,7},{4,6},{5,1},{6,4},{7,3},{8,10},{9,13},{10,... | collective-permute-start | bytes 2064392 | tf_op jit(solution)/shard_map/ppermute | solution.py:411
  126.4 3.2 %collective-permute-start.9 = (bf16[16,16,2688]{2,1,0:T(8,128)(2,1)S(1)}, bf16[16,16,2688]{2,1,0:T(8,128)(2,1)S(1)}, u32[]{:S(2)}, u32[]{:S(2)}) collective-permute-start(bf16[16,16,2688]{2,1,0:T(8,128)(2,1)S(1)} %constant_dynamic-update-slice_fusion.own_ref), channel_id=1, source_target_pairs={{0,1},{1,0},{2,3},{3,2},{4,5},{5,4},{6,7},{7,6},{8,9},{9,8},{10,11... | collective-permute-start | bytes 4128776 | tf_op jit(solution)/shard_map/ppermute | solution.py:411

commit v6 on v5

--- a/solution.py
+++ b/solution.py
@@ -106,11 +106,11 @@
         hat=shape_of((tokens, width), F32),
         hat_scale=shape_of((tokens, 1), F32),
         qkv=shape_of((tokens, 3 * width), BF16),
-        slope=shape_of((pairs, TILE, TILE), F32),
+        slope=shape_of((pairs, TILE, TILE), BF16),
         weight=shape_of((pairs, TILE, TILE), BF16),
         mixed=shape_of((tokens, width), BF16),
         normed=shape_of((count, width), BF16),
-        rows_slope=shape_of((count, 4 * width), F32),
+        rows_slope=shape_of((count, 4 * width), BF16),
         rows_hat=shape_of((count, width), F32),
         rows_scale=shape_of((count, 1), F32),
         place=shape_of((1, count), jnp.int32),
@@ -176,7 +176,8 @@
         hidden = dot(normed, w_in_ref[:, columns])
         sigma = sigmoid(hidden)
         active = hidden * sigma
-        rows_slope_ref[:, columns] = sigma * (1.0 + hidden * (1.0 - sigma))
+        slope = sigma * (1.0 + hidden * (1.0 - sigma))
+        rows_slope_ref[:, columns] = slope.astype(BF16)
         if part == 0:
             high = active.astype(BF16)
             low = (active - high.astype(F32)).astype(BF16)
@@ -201,7 +202,7 @@
             sigma = sigmoid(score)
             weight = jnp.where(mask, score * sigma, 0.0).astype(BF16)
             slope = sigma * (1.0 + score * (1.0 - sigma)) * factor
-            slope_ref[tile * HEADS + head] = jnp.where(mask, slope, 0.0)
+            slope_ref[tile * HEADS + head] = jnp.where(mask, slope, 0.0).astype(BF16)
             weight_ref[tile * HEADS + head] = weight
             parts.append(dot(weight, vals))
         attended = jnp.concatenate(parts, axis=1)
@@ -241,7 +242,7 @@
     me = me_ref[0]
     for slot in range(got_ref.shape[0]):
         grad_y_ref[slot * SLOT : (slot + 1) * SLOT, :] = got_ref[dest_ref[slot]]
-    for copy in copies[:7]:
+    for copy in copies[:4]:
         copy.wait()
     gain_total = jnp.zeros((1, width), F32)
     for tile in range(tokens // TILE):
@@ -255,6 +256,9 @@
         mean = jnp.mean(inner, axis=-1, keepdims=True)
         along = jnp.mean(inner * hat, axis=-1, keepdims=True)
         grad_att = ((inner - mean - hat * along) * hat_scale_ref[rows, :]).astype(BF16)
+        if tile == 0:
+            for copy in copies[4:7]:
+                copy.wait()
         for head in range(HEADS):
             columns = slice(head * HDIM, (head + 1) * HDIM)
             vals, queries, keys = (
@@ -263,7 +267,9 @@
             )
             grad_o = grad_att[:, columns]
             grad_weight = dot(grad_o, vals, NT)
-            grad_score = (grad_weight * slope_ref[tile * HEADS + head]).astype(BF16)
+            grad_score = (grad_weight * slope_ref[tile * HEADS + head].astype(F32)).astype(
+                BF16
+            )
             for part, value in (
                 (1, dot(weight_ref[tile * HEADS + head], grad_o, TN)),
                 (2, dot(grad_score, keys)),
@@ -284,7 +290,7 @@
     for part in range(4):
         columns = slice(part * width, (part + 1) * width)
         summed = dot(gather, active_ref[:, columns])
-        grad_hidden = (summed * rows_slope_ref[:, columns]).astype(BF16)
+        grad_hidden = (summed * rows_slope_ref[:, columns].astype(F32)).astype(BF16)
         sums_ref[:, columns] = (dot(normed_ref[...], grad_hidden, TN) * total_factor).astype(BF16)
         grad_normed = grad_normed + dot(grad_hidden, w_in_ref[:, columns], NT)
     hat = rows_hat_ref[...]
@@ -331,7 +337,7 @@
         self.wide = blocks * LANES
         table_bits = [1 << bit for bit in range(1, table_size.bit_length() - 1)]
         dp_bits = [table_size << bit for bit in range(dp_size.bit_length() - 1)]
-        self.orders = (table_bits + dp_bits, dp_bits[:2] + table_bits + dp_bits[2:])
+        self.orders = (table_bits + dp_bits, dp_bits[:1] + table_bits + dp_bits[1:])
         self.steps = len(self.orders[0])
 
     def low_mask(self, core, place):
@@ -481,13 +487,15 @@
         middle = kept.shape[0] // 2
         came = swap(kept[middle:], masks)
         kept = add(kept[:middle], came)
-    for masks in reversed(list(zip(*plan.orders))):
-        kept = jnp.concatenate([kept, swap(kept, masks)])
     table_part = call(
         table_body,
         shape_of((ROWS_DEV, width), F32),
         [VMEM],
     )(table_got.reshape(devices_all * plan.capacity, width + LANES))
+    for step, masks in reversed(list(enumerate(zip(*plan.orders)))):
+        if step == 0:
+            kept, table_part = lax.optimization_barrier((kept, table_part))
+        kept = jnp.concatenate([kept, swap(kept, masks)])
     came = swap(kept, (1, 1))
 
     grad_w_in, grad_w_out, grad_gain_in, grad_gain_out = call(

time: 133 us -> 131 us (0.985)
  waiting for transfers between devices: 71.3 us -> 68.6 us
    ppermute x10, waiting for transfers between devices: 63.2 us -> 60.4 us  [swap(): return lax.ppermute(values, both, pairs)]
where the time goes in v6:
time: 131 us; the launch traced here: 130 us
  waiting for transfers between devices  68.6 us (52%)
  Pallas kernels  28.1 us (21%)
  starting transfers between devices  24.7 us (19%)
  local copies, waits for them, and re-layouts  5.03 us (4%)
  other arithmetic  2.87 us (2%)
    ppermute x10, waiting for transfers between devices, swap(): return lax.ppermute(values, both, pairs)  60.4 us
    all_to_all x3, starting transfers between devices, exchange(): return lax.all_to_all(values, axes, split_axis=0, concat_axis=0, tiled=True)  14.2 us
    pallas_call x1, Pallas kernels, on_device(): call(functools.partial(backward_body, plan, total_factor), [shape_of((dev...  12.6 us
    ppermute x10, starting transfers between devices, swap(): return lax.ppermute(values, both, pairs)  10.5 us
    pallas_call x1, Pallas kernels, on_device(): call(functools.partial(forward_body, plan.capacity), shapes, [VMEM] * 8,...  8.99 us
    all_to_all x3, waiting for transfers between devices, exchange(): return lax.all_to_all(values, axes, split_axis=0, concat_axis=0, tiled=True)  8.19 us
    pallas_call x1, Pallas kernels, on_device(): call(functools.partial(widen_body, plan), (shape_of(w_in.shape, F32), sha...  2.81 us
  transfers between devices with their start and end apart: 13, of which 12 were waited for; matrix products, arithmetic and copies ran while one was open for 2% of the time, Pallas kernels for 9%

profile of v6, /device:TPU:0, one launch (start us, length us, event | category | flops | bytes accessed | tf_op | source)
XLA Modules:
  0.0 130.2 jit_solution(11650947412636422820)
XLA Ops:
  0.6 0.0 copy-start.3
  0.6 0.0 copy-start.4
  0.7 0.0 copy-start.2
  0.7 0.7 multiply_add_fusion
  1.4 0.6 broadcast_in_dim.15
  2.0 7.3 %all-to-all-start = ((s32[8,1,8]{2,1,0:T(1,128)}), s32[8,1,8]{2,1,0:T(1,128)S(1)}, u32[]{:S(2)}, u32[]{:S(2)}) async-start(s32[8,1,8]{2,1,0:T(1,128)} %broadcast_in_dim.15), calls=%async_computation | async-start | bytes 8192 | tf_op jit(solution)/shard_map/all_to_all | solution.py:420
  9.2 6.4 %all-to-all-done.packed_ref = s32[8,1,8]{2,1,0:T(1,128)S(1)} async-done(((s32[8,1,8]{2,1,0:T(1,128)}), s32[8,1,8]{2,1,0:T(1,128)S(1)}, u32[]{:S(2)}, u32[]{:S(2)}) %all-to-all-start) | async-done | bytes 288 | tf_op jit(solution)/shard_map/all_to_all | solution.py:420
  15.6 0.9 copy-done
  16.5 1.6 %shard_map.146 = bf16[8,64,512]{2,1,0:T(8,128)(2,1)} custom-call(s32[1]{0:T(128)} %bitcast.me_ref, s32[8,1,8]{2,1,0:T(1,128)S(1)} %all-to-all-done.packed_ref, bf16[256,512]{1,0:T(8,128)(2,1)S(1)} %copy-done), custom_call_target="tpu_custom_call" | custom-call | tf_op jit(solution)/shard_map/pallas_call | solution.py:423
  18.1 3.5 %all-to-all-start.1 = ((bf16[8,64,512]{2,1,0:T(8,128)(2,1)}), bf16[8,64,512]{2,1,0:T(8,128)(2,1)S(1)}, u32[]{:S(2)}, u32[]{:S(2)}) async-start(bf16[8,64,512]{2,1,0:T(8,128)(2,1)} %shard_map.146), calls=%async_computation.1 | async-start | bytes 1048576 | tf_op jit(solution)/shard_map/all_to_all | solution.py:420
  21.6 0.0 copy-done.3
  21.6 0.8 copy.19.number_ref
  22.4 0.0 copy-done.4
  22.4 0.8 copy.18.owner_col_ref
  23.2 0.9 copy.17.item_ref
  24.1 9.0 %shard_map.147 = (f32[512,512]{1,0:T(8,128)}, f32[512,512]{1,0:T(8,128)}, f32[512,1]{1,0:T(8,128)}, bf16[512,1536]{1,0:T(8,128)(2,1)}, bf16[16,128,128]{2,1,0:T(...) custom-call(bf16[256,512]{1,0:T(8,128)(2,1)} %rows_ref.1, ...), custom_call_target="tpu_custom_call" | custom-call | flops 2147483648 | bytes 10000000 | tf_op jit(solution)/shard_map/pallas_call | solution.py:433
  33.1 1.8 %all-to-all-done.1.got_ref = bf16[8,64,512]{2,1,0:T(8,128)(2,1)S(1)} async-done(((bf16[8,64,512]{2,1,0:T(8,128)(2,1)}), bf16[8,64,512]{2,1,0:T(8,128)(2,1)S(1)}, u32[]{:S(2)}, u32[]{:S(2)}) %all-to-all-start.1) | async-done | bytes 524320 | tf_op jit(solution)/shard_map/all_to_all | solution.py:420
  34.9 0.8 copy-done.1
  35.7 12.6 %shard_map.148 = (bf16[512,640]{1,0:T(8,128)(2,1)}, bf16[16,16,2688]{2,1,0:T(8,128)(2,1)}, bf16[16,16,2688]{2,1,0:T(8,128)(2,1)}) custom-call(s32[1]{0:T(128)} %bitcast.me_ref, s32[8]{0:T(128)} %dest_ref.1, s32[1,512]{1,0:T(1,128)} %bitcast.13, f32[1,512]{1,0:T(1,128)} %bitcast.18, f32[1,512]{1,0:T(1,128)} %bitcast.20, bf16[8,64,512]{2,1,0:T(8,128)(2,1)} %copy-done.1, ...), custom_call_target="tpu_custom_call" | custom-call | flops 5368709120 | bytes 12000000 | tf_op jit(solution)/shard_map/pallas_call | solution.py:454
  48.3 0.1 collective-permute-start
  48.3 3.3 %collective-permute-done = bf16[16,16,2688]{2,1,0:T(8,128)(2,1)S(1)} collective-permute-done((bf16[16,16,2688]{2,1,0:T(8,128)(2,1)}, bf16[16,16,2688]{2,1,0:T(8,128)(2,1)S(1)}, u32[]{:S(2)}, u32[]{:S(2)}) %collective-permute-start) | collective-permute-done | bytes 1376288 | tf_op jit(solution)/shard_map/ppermute | solution.py:417
  51.7 1.7 %add_convert_fusion = bf16[16,16,2688]{2,1,0:T(8,128)(2,1)S(1)} fusion(bf16[16,16,2688]{2,1,0:T(8,128)(2,1)S(1)} %collective-permute-done, bf16[16,16,2688]{2,1,0:T(8,128)(2,1)} %get-tuple-element.42), kind=kLoop, calls=%fused_computation | loop fusion | flops 2752512 | bytes 4128768 | tf_op jit(solution)/shard_map/convert_element_type | solution.py:389
  53.4 1.6 %collective-permute-start.1 = (bf16[8,16,2688]{2,1,0:T(8,128)(2,1)S(1)}, bf16[8,16,2688]{2,1,0:T(8,128)(2,1)S(1)}, u32[]{:S(2)}, u32[]{:S(2)}) collective-permute-start(bf16[8,16,2688]{2,1,0:T(8,128)(2,1)S(1)} %slice.33), channel_id=1, source_target_pairs={{0,2},{1,5},{2,0},{3,7},{4,6},{5,1},{6,4},{7,3},{8,10},{9,13},{10,... | collective-permute-start | bytes 2064392 | tf_op jit(solution)/shard_map/ppermute | solution.py:417
  55.0 3.4 %all-to-all-start.2 = ((bf16[32,16,640]{2,1,0:T(8,128)(2,1)}), bf16[32,16,640]{2,1,0:T(8,128)(2,1)S(1)}, u32[]{:S(2)}, u32[]{:S(2)}) async-start(bf16[32,16,640]{2,1,0:T(8,128)(2,1)} %bitcast.12), calls=%async_computation.2 | async-start | bytes 1310720 | tf_op jit(solution)/shard_map/all_to_all | solution.py:420
  58.4 10.3 %collective-permute-done.1 = bf16[8,16,2688]{2,1,0:T(8,128)(2,1)S(1)} collective-permute-done((bf16[8,16,2688]{2,1,0:T(8,128)(2,1)S(1)}, bf16[8,16,2688]{2,1,0:T(8,128)(2,1)S(1)}, u32[]{:S(2)}, u32[]{:S(2)}) %collective-permute-start.1) | collective-permute-done | bytes 688160 | tf_op jit(solution)/shard_map/ppermute | solution.py:417
  68.8 0.2 add_convert_fusion.1
  69.0 1.6 %collective-permute-start.2 = (bf16[4,16,2688]{2,1,0:T(8,128)(2,1)S(1)}, bf16[4,16,2688]{2,1,0:T(8,128)(2,1)S(1)}, u32[]{:S(2)}, u32[]{:S(2)}) collective-permute-start(bf16[4,16,2688]{2,1,0:T(8,128)(2,1)S(1)} %slice.35), channel_id=1, source_target_pairs={{0,4},{1,3},{2,6},{3,1},{4,0},{5,7},{6,2},{7,5},{8,12},{9,11},{10,... | collective-permute-start | bytes 1032200 | tf_op jit(solution)/shard_map/ppermute | solution.py:417
  70.6 6.6 %collective-permute-done.2 = bf16[4,16,2688]{2,1,0:T(8,128)(2,1)S(1)} collective-permute-done((bf16[4,16,2688]{2,1,0:T(8,128)(2,1)S(1)}, bf16[4,16,2688]{2,1,0:T(8,128)(2,1)S(1)}, u32[]{:S(2)}, u32[]{:S(2)}) %collective-permute-start.2) | collective-permute-done | bytes 344096 | tf_op jit(solution)/shard_map/ppermute | solution.py:417
  77.1 0.1 add_convert_fusion.2
  77.2 0.0 all-to-all-done.2
  77.3 0.6 collective-permute-start.3
  77.9 4.8 %collective-permute-done.3 = bf16[2,16,2688]{2,1,0:T(8,128)(2,1)S(1)} collective-permute-done((bf16[2,16,2688]{2,1,0:T(8,128)(2,1)S(1)}, bf16[2,16,2688]{2,1,0:T(8,128)(2,1)S(1)}, u32[]{:S(2)}, u32[]{:S(2)}) %collective-permute-start.3) | collective-permute-done | bytes 172064 | tf_op jit(solution)/shard_map/ppermute | solution.py:417
  82.8 1.6 %collective-permute-start.4 = (bf16[1,16,2688]{2,1,0:T(8,128)(2,1)S(1)}, bf16[1,16,2688]{2,1,0:T(8,128)(2,1)S(1)}, u32[]{:S(2)}, u32[]{:S(2)}) collective-permute-start(bf16[1,16,2688]{2,1,0:T(8,128)(2,1)S(1)} %slice.37), channel_id=1, source_target_pairs={{0,16},{1,17},{2,18},{3,19},{4,20},{5,21},{6,22},{7,23},{8,24},{9,... | collective-permute-start | bytes 258056 | tf_op jit(solution)/shard_map/ppermute | solution.py:417
  84.4 5.0 %collective-permute-done.4 = bf16[1,16,2688]{2,1,0:T(8,128)(2,1)S(1)} collective-permute-done((bf16[1,16,2688]{2,1,0:T(8,128)(2,1)S(1)}, bf16[1,16,2688]{2,1,0:T(8,128)(2,1)S(1)}, u32[]{:S(2)}, u32[]{:S(2)}) %collective-permute-start.4) | collective-permute-done | bytes 86048 | tf_op jit(solution)/shard_map/ppermute | solution.py:417
  89.5 0.5 collective-permute-start.5
  90.0 5.4 %collective-permute-done.5 = bf16[1,16,2688]{2,1,0:T(8,128)(2,1)S(1)} collective-permute-done((bf16[1,16,2688]{2,1,0:T(8,128)(2,1)S(1)}, bf16[1,16,2688]{2,1,0:T(8,128)(2,1)S(1)}, u32[]{:S(2)}, u32[]{:S(2)}) %collective-permute-start.5) | collective-permute-done | bytes 86048 | tf_op jit(solution)/shard_map/ppermute | solution.py:417
  95.4 0.1 collective-permute-start.6
  95.5 5.4 %collective-permute-done.6 = bf16[2,16,2688]{2,1,0:T(8,128)(2,1)S(1)} collective-permute-done((bf16[2,16,2688]{2,1,0:T(8,128)(2,1)S(1)}, bf16[2,16,2688]{2,1,0:T(8,128)(2,1)S(1)}, u32[]{:S(2)}, u32[]{:S(2)}) %collective-permute-start.6) | collective-permute-done | bytes 172064 | tf_op jit(solution)/shard_map/ppermute | solution.py:417
  100.9 0.8 collective-permute-start.7
  101.7 2.2 %shard_map.149 = f32[1024,512]{1,0:T(8,128)} custom-call(bf16[512,640]{1,0:T(8,128)(2,1)S(1)} %bitcast.11), custom_call_target="tpu_custom_call" | custom-call | tf_op jit(solution)/shard_map/pallas_call | solution.py:490
  103.8 7.6 %collective-permute-done.7 = bf16[4,16,2688]{2,1,0:T(8,128)(2,1)S(1)} collective-permute-done((bf16[4,16,2688]{2,1,0:T(8,128)(2,1)S(1)}, bf16[4,16,2688]{2,1,0:T(8,128)(2,1)S(1)}, u32[]{:S(2)}, u32[]{:S(2)}) %collective-permute-start.7) | collective-permute-done | bytes 344096 | tf_op jit(solution)/shard_map/ppermute | solution.py:417
  111.4 0.1 pad_maximum_fusion
  111.5 3.6 %collective-permute-start.8 = (bf16[8,16,2688]{2,1,0:T(8,128)(2,1)S(1)}, bf16[8,16,2688]{2,1,0:T(8,128)(2,1)S(1)}, u32[]{:S(2)}, u32[]{:S(2)}) collective-permute-start(bf16[8,16,2688]{2,1,0:T(8,128)(2,1)S(1)} %pad_maximum_fusion), channel_id=1, source_target_pairs={{0,2},{1,5},{2,0},{3,7},{4,6},{5,1},{6,4},{7,3},{8,10},{9,13},{10,... | collective-permute-start | bytes 2064392 | tf_op jit(solution)/shard_map/ppermute | solution.py:417
  115.2 8.9 %collective-permute-done.8 = bf16[8,16,2688]{2,1,0:T(8,128)(2,1)S(1)} collective-permute-done((bf16[8,16,2688]{2,1,0:T(8,128)(2,1)S(1)}, bf16[8,16,2688]{2,1,0:T(8,128)(2,1)S(1)}, u32[]{:S(2)}, u32[]{:S(2)}) %collective-permute-start.8) | collective-permute-done | bytes 688160 | tf_op jit(solution)/shard_map/ppermute | solution.py:417
  124.1 0.1 constant_dynamic-update-slice_fusion.own_ref
  124.1 0.1 collective-permute-start.9
  124.2 3.1 %collective-permute-done.9.came_ref = bf16[16,16,2688]{2,1,0:T(8,128)(2,1)S(1)} collective-permute-done((bf16[16,16,2688]{2,1,0:T(8,128)(2,1)S(1)}, bf16[16,16,2688]{2,1,0:T(8,128)(2,1)S(1)}, u32[]{:S(2)}, u32[]{:S(2)}) %collective-permute-start.9) | collective-permute-done | bytes 1376288 | tf_op jit(solution)/shard_map/ppermute | solution.py:417
  127.3 2.8 %shard_map.150 = (f32[512,2048]{1,0:T(8,128)}, f32[512,512]{1,0:T(8,128)}, f32[1,512]{1,0:T(1,128)}, f32[1,512]{1,0:T(1,128)}) custom-call(s32[1]{0:T(128)} %bitcast.me_ref, bf16[16,16,2688]{2,1,0:T(8,128)(2,1)S(1)} %constant_dynamic-update-slice_fusion.own_ref, bf16[16,16,2688]{2,1,0:T(8,128)(2,1)S(1)} %collective-permute-done.9.came_ref), custom_call_target="tpu_custom_call" | custom-call | tf_op jit(solution)/shard_map/pallas_call | solution.py:501
  (12 shorter events, 0.3 us)
Async XLA Ops:
  0.6 21.0 %copy-start.3 = (s32[256]{0:T(256)S(1)}, s32[256]{0:T(256)}, u32[]{:S(2)}) copy-start(s32[256]{0:T(256)} %param.14) | copy-start | bytes 3076
  0.6 21.8 %copy-start.4 = (s32[256,1]{0,1:T(1,128)S(1)}, s32[256,1]{0,1:T(1,128)}, u32[]{:S(2)}) copy-start(s32[256,1]{0,1:T(1,128)} %param.13) | copy-start | bytes 3076
  0.7 22.6 %copy-start.2 = (s32[512]{0:T(512)S(1)}, s32[512]{0:T(512)}, u32[]{:S(2)}) copy-start(s32[512]{0:T(512)} %param.12) | copy-start | bytes 6148
  2.0 13.6 %all-to-all-start = ((s32[8,1,8]{2,1,0:T(1,128)}), s32[8,1,8]{2,1,0:T(1,128)S(1)}, u32[]{:S(2)}, u32[]{:S(2)}) async-start(s32[8,1,8]{2,1,0:T(1,128)} %broadcast_in_dim.15), calls=%async_computation | async-start | bytes 8192 | tf_op jit(solution)/shard_map/all_to_all | solution.py:420
  15.6 1.0 copy-start
  18.1 16.8 %all-to-all-start.1 = ((bf16[8,64,512]{2,1,0:T(8,128)(2,1)}), bf16[8,64,512]{2,1,0:T(8,128)(2,1)S(1)}, u32[]{:S(2)}, u32[]{:S(2)}) async-start(bf16[8,64,512]{2,1,0:T(8,128)(2,1)} %shard_map.146), calls=%async_computation.1 | async-start | bytes 1048576 | tf_op jit(solution)/shard_map/all_to_all | solution.py:420
  34.9 0.8 copy-start.1
  48.3 3.4 %collective-permute-start = (bf16[16,16,2688]{2,1,0:T(8,128)(2,1)}, bf16[16,16,2688]{2,1,0:T(8,128)(2,1)S(1)}, u32[]{:S(2)}, u32[]{:S(2)}) collective-permute-start(bf16[16,16,2688]{2,1,0:T(8,128)(2,1)} %get-tuple-element.43), channel_id=1, source_target_pairs={{0,1},{1,0},{2,3},{3,2},{4,5},{5,4},{6,7},{7,6},{8,9},{9,8},{10,11... | collective-permute-start | bytes 4128776 | tf_op jit(solution)/shard_map/ppermute | solution.py:417
  53.4 15.3 %collective-permute-start.1 = (bf16[8,16,2688]{2,1,0:T(8,128)(2,1)S(1)}, bf16[8,16,2688]{2,1,0:T(8,128)(2,1)S(1)}, u32[]{:S(2)}, u32[]{:S(2)}) collective-permute-start(bf16[8,16,2688]{2,1,0:T(8,128)(2,1)S(1)} %slice.33), channel_id=1, source_target_pairs={{0,2},{1,5},{2,0},{3,7},{4,6},{5,1},{6,4},{7,3},{8,10},{9,13},{10,... | collective-permute-start | bytes 2064392 | tf_op jit(solution)/shard_map/ppermute | solution.py:417
  55.0 22.2 %all-to-all-start.2 = ((bf16[32,16,640]{2,1,0:T(8,128)(2,1)}), bf16[32,16,640]{2,1,0:T(8,128)(2,1)S(1)}, u32[]{:S(2)}, u32[]{:S(2)}) async-start(bf16[32,16,640]{2,1,0:T(8,128)(2,1)} %bitcast.12), calls=%async_computation.2 | async-start | bytes 1310720 | tf_op jit(solution)/shard_map/all_to_all | solution.py:420
  69.0 8.2 %collective-permute-start.2 = (bf16[4,16,2688]{2,1,0:T(8,128)(2,1)S(1)}, bf16[4,16,2688]{2,1,0:T(8,128)(2,1)S(1)}, u32[]{:S(2)}, u32[]{:S(2)}) collective-permute-start(bf16[4,16,2688]{2,1,0:T(8,128)(2,1)S(1)} %slice.35), channel_id=1, source_target_pairs={{0,4},{1,3},{2,6},{3,1},{4,0},{5,7},{6,2},{7,5},{8,12},{9,11},{10,... | collective-permute-start | bytes 1032200 | tf_op jit(solution)/shard_map/ppermute | solution.py:417
  77.3 5.5 %collective-permute-start.3 = (bf16[2,16,2688]{2,1,0:T(8,128)(2,1)S(1)}, bf16[2,16,2688]{2,1,0:T(8,128)(2,1)S(1)}, u32[]{:S(2)}, u32[]{:S(2)}) collective-permute-start(bf16[2,16,2688]{2,1,0:T(8,128)(2,1)S(1)} %slice.29), channel_id=1, source_target_pairs={{0,8},{1,9},{2,10},{3,11},{4,12},{5,13},{6,14},{7,15},{8,0},{9,1},... | collective-permute-start | bytes 516104 | tf_op jit(solution)/shard_map/ppermute | solution.py:417
  82.8 6.6 %collective-permute-start.4 = (bf16[1,16,2688]{2,1,0:T(8,128)(2,1)S(1)}, bf16[1,16,2688]{2,1,0:T(8,128)(2,1)S(1)}, u32[]{:S(2)}, u32[]{:S(2)}) collective-permute-start(bf16[1,16,2688]{2,1,0:T(8,128)(2,1)S(1)} %slice.37), channel_id=1, source_target_pairs={{0,16},{1,17},{2,18},{3,19},{4,20},{5,21},{6,22},{7,23},{8,24},{9,... | collective-permute-start | bytes 258056 | tf_op jit(solution)/shard_map/ppermute | solution.py:417
  89.5 5.9 %collective-permute-start.5 = (bf16[1,16,2688]{2,1,0:T(8,128)(2,1)S(1)}, bf16[1,16,2688]{2,1,0:T(8,128)(2,1)S(1)}, u32[]{:S(2)}, u32[]{:S(2)}) collective-permute-start(bf16[1,16,2688]{2,1,0:T(8,128)(2,1)S(1)} %add_convert_fusion.4), channel_id=1, source_target_pairs={{0,16},{1,17},{2,18},{3,19},{4,20},{5,21},{6,22},{7,23},{8,24},{9,... | collective-permute-start | bytes 258056 | tf_op jit(solution)/shard_map/ppermute | solution.py:417
  95.4 5.5 %collective-permute-start.6 = (bf16[2,16,2688]{2,1,0:T(8,128)(2,1)S(1)}, bf16[2,16,2688]{2,1,0:T(8,128)(2,1)S(1)}, u32[]{:S(2)}, u32[]{:S(2)}) collective-permute-start(bf16[2,16,2688]{2,1,0:T(8,128)(2,1)S(1)} %pad_maximum_fusion.2), channel_id=1, source_target_pairs={{0,8},{1,9},{2,10},{3,11},{4,12},{5,13},{6,14},{7,15},{8,0},{9,1},... | collective-permute-start | bytes 516104 | tf_op jit(solution)/shard_map/ppermute | solution.py:417
  100.9 10.5 %collective-permute-start.7 = (bf16[4,16,2688]{2,1,0:T(8,128)(2,1)S(1)}, bf16[4,16,2688]{2,1,0:T(8,128)(2,1)S(1)}, u32[]{:S(2)}, u32[]{:S(2)}) collective-permute-start(bf16[4,16,2688]{2,1,0:T(8,128)(2,1)S(1)} %pad_maximum_fusion.1), channel_id=1, source_target_pairs={{0,4},{1,3},{2,6},{3,1},{4,0},{5,7},{6,2},{7,5},{8,12},{9,11},{10,... | collective-permute-start | bytes 1032200 | tf_op jit(solution)/shard_map/ppermute | solution.py:417
  111.5 12.6 %collective-permute-start.8 = (bf16[8,16,2688]{2,1,0:T(8,128)(2,1)S(1)}, bf16[8,16,2688]{2,1,0:T(8,128)(2,1)S(1)}, u32[]{:S(2)}, u32[]{:S(2)}) collective-permute-start(bf16[8,16,2688]{2,1,0:T(8,128)(2,1)S(1)} %pad_maximum_fusion), channel_id=1, source_target_pairs={{0,2},{1,5},{2,0},{3,7},{4,6},{5,1},{6,4},{7,3},{8,10},{9,13},{10,... | collective-permute-start | bytes 2064392 | tf_op jit(solution)/shard_map/ppermute | solution.py:417
  124.1 3.2 %collective-permute-start.9 = (bf16[16,16,2688]{2,1,0:T(8,128)(2,1)S(1)}, bf16[16,16,2688]{2,1,0:T(8,128)(2,1)S(1)}, u32[]{:S(2)}, u32[]{:S(2)}) collective-permute-start(bf16[16,16,2688]{2,1,0:T(8,128)(2,1)S(1)} %constant_dynamic-update-slice_fusion.own_ref), channel_id=1, source_target_pairs={{0,1},{1,0},{2,3},{3,2},{4,5},{5,4},{6,7},{7,6},{8,9},{9,8},{10,11... | collective-permute-start | bytes 4128776 | tf_op jit(solution)/shard_map/ppermute | solution.py:417

commit v7 on v6

--- a/solution.py
+++ b/solution.py
@@ -218,105 +218,138 @@
         copy.wait()
 
 
-def backward_body(
-    plan, total_factor, me_ref, dest_ref, item_ref, gain_in_ref, gain_out_ref, got_ref, *refs
-):
-    size = len(SAVED) + 2
-    far_refs, (table_ref, keep_ref, give_ref), near_refs = (
-        refs[:size],
-        refs[size : size + 3],
-        refs[size + 3 : 2 * size + 3],
-    )
-    sums_ref, active_ref, grad_y_ref, sems = refs[2 * size + 3 :]
-    copies = [
-        pltpu.make_async_copy(far, near, sems.at[index])
-        for index, (far, near) in enumerate(zip(far_refs, near_refs))
-    ]
-    for copy in copies:
-        copy.start()
-    w_out_ref, gate_ref, hat_ref, hat_scale_ref, qkv_ref, slope_ref, weight_ref = near_refs[:7]
-    mixed_ref, normed_ref, rows_slope_ref, rows_hat_ref, rows_scale_ref = near_refs[7:12]
-    place_ref, digits_ref, w_in_ref = near_refs[12:]
-    count, width = rows_hat_ref.shape
-    tokens = hat_ref.shape[0]
-    me = me_ref[0]
+def fetch(names, far_refs, near_refs, sems):
+    copies = {}
+    for index, name in enumerate(names):
+        copies[name] = pltpu.make_async_copy(far_refs[index], near_refs[index], sems.at[index])
+        copies[name].start()
+
+    def get(name):
+        copies[name].wait()
+        return near_refs[names.index(name)]
+
+    return get
+
+
+def gather_of(item_ref, count):
+    tokens = item_ref.shape[1]
+    sub = lax.broadcasted_iota(jnp.int32, (count, tokens), 0)
+    hit = sub == jnp.broadcast_to(item_ref[...], (count, tokens))
+    return jnp.where(hit, 1.0, 0.0).astype(BF16)
+
+
+FIRST = ("w_out", "gate", "hat", "hat_scale", "mixed", "normed", "rows_slope")
+SECOND = (
+    "grad_att",
+    "qkv",
+    "slope",
+    "weight",
+    "normed",
+    "rows_slope",
+    "grad_hidden",
+    "w_in",
+    "rows_hat",
+    "rows_scale",
+    "grad_y",
+    "place",
+    "digits",
+)
+
+
+def first_body(plan, factor, me_ref, dest_ref, item_ref, gain_out_ref, got_ref, *refs):
+    size = len(FIRST)
+    far_refs, refs = refs[:size], refs[size:]
+    keep_ref, give_ref, grad_att_ref, grad_hidden_ref, grad_y_ref, gain_ref = refs[:6]
+    near_refs, (sums_ref, active_ref, sems) = refs[6 : 6 + size], refs[6 + size :]
+    get = fetch(FIRST, far_refs, near_refs, sems)
+    tokens, width = grad_att_ref.shape
+    count = grad_hidden_ref.shape[0]
     for slot in range(got_ref.shape[0]):
         grad_y_ref[slot * SLOT : (slot + 1) * SLOT, :] = got_ref[dest_ref[slot]]
-    for copy in copies[:4]:
-        copy.wait()
+    w_out_ref, gate_ref, hat_ref, hat_scale_ref = (get(name) for name in FIRST[:4])
     gain_total = jnp.zeros((1, width), F32)
     for tile in range(tokens // TILE):
         rows = slice(tile * TILE, (tile + 1) * TILE)
         grad_mixed = dot(grad_y_ref[rows, :], w_out_ref[...], NT)
         hat = hat_ref[rows, :]
-        active_ref[rows, :width] = (grad_mixed * hat * gain_out_ref[...]).astype(BF16)
+        active_ref[rows, :] = (grad_mixed * hat * gain_out_ref[...]).astype(BF16)
         inner = grad_mixed * gate_ref[rows, :]
         gain_total = gain_total + jnp.sum(inner * hat, axis=0, keepdims=True)
         inner = inner * gain_out_ref[...]
         mean = jnp.mean(inner, axis=-1, keepdims=True)
         along = jnp.mean(inner * hat, axis=-1, keepdims=True)
-        grad_att = ((inner - mean - hat * along) * hat_scale_ref[rows, :]).astype(BF16)
-        if tile == 0:
-            for copy in copies[4:7]:
-                copy.wait()
+        grad_att_ref[rows, :] = ((inner - mean - hat * along) * hat_scale_ref[rows, :]).astype(BF16)
+    gain_ref[...] = gain_total
+    mixed_ref, normed_ref, slope_ref = (get(name) for name in FIRST[4:])
+    sums_ref[:, :width] = (dot(mixed_ref[...], grad_y_ref[...], TN) * factor).astype(BF16)
+    summed = dot(gather_of(item_ref, count), active_ref[...])
+    grad_hidden = (summed * slope_ref[...].astype(F32)).astype(BF16)
+    grad_hidden_ref[...] = grad_hidden
+    sums_ref[:, width:] = (dot(normed_ref[...], grad_hidden, TN) * factor).astype(BF16)
+    plan.write(me_ref[0], plan.first, sums_ref, keep_ref, give_ref)
+
+
+def second_body(plan, factor, me_ref, item_ref, gain_in_ref, gain_ref, *refs):
+    size = len(SECOND)
+    far_refs, refs = refs[:size], refs[size:]
+    (table_ref, keep_ref, give_ref), near_refs = refs[:3], refs[3 : 3 + size]
+    sums_ref, active_ref, sems = refs[3 + size :]
+    get = fetch(SECOND, far_refs, near_refs, sems)
+    grad_att_ref, qkv_ref, slope_ref, weight_ref = (get(name) for name in SECOND[:4])
+    tokens, width = grad_att_ref.shape
+    for tile in range(tokens // TILE):
+        rows = slice(tile * TILE, (tile + 1) * TILE)
         for head in range(HEADS):
-            columns = slice(head * HDIM, (head + 1) * HDIM)
             vals, queries, keys = (
                 qkv_ref[rows, part * width + head * HDIM : part * width + (head + 1) * HDIM]
                 for part in range(3)
             )
-            grad_o = grad_att[:, columns]
+            grad_o = grad_att_ref[rows, head * HDIM : (head + 1) * HDIM]
             grad_weight = dot(grad_o, vals, NT)
-            grad_score = (grad_weight * slope_ref[tile * HEADS + head].astype(F32)).astype(
-                BF16
-            )
+            grad_score = (grad_weight * slope_ref[tile * HEADS + head].astype(F32)).astype(BF16)
             for part, value in (
-                (1, dot(weight_ref[tile * HEADS + head], grad_o, TN)),
-                (2, dot(grad_score, keys)),
-                (3, dot(grad_score, queries, TN)),
+                (0, dot(weight_ref[tile * HEADS + head], grad_o, TN)),
+                (1, dot(grad_score, keys)),
+                (2, dot(grad_score, queries, TN)),
             ):
                 first = part * width + head * HDIM
                 active_ref[rows, first : first + HDIM] = value.astype(BF16)
-    for copy in copies[7:]:
-        copy.wait()
-    grad_y = grad_y_ref[...]
-    sums_ref[:, 4 * width : 5 * width] = (dot(mixed_ref[...], grad_y, TN) * total_factor).astype(
-        BF16
-    )
-    sub = lax.broadcasted_iota(jnp.int32, (count, tokens), 0)
-    gather = jnp.where(sub == jnp.broadcast_to(item_ref[...], (count, tokens)), 1.0, 0.0)
-    gather = gather.astype(BF16)
-    grad_normed = jnp.zeros((count, width), F32)
-    for part in range(4):
+    normed_ref, rows_slope_ref, grad_hidden_ref, w_in_ref = (get(name) for name in SECOND[4:8])
+    count = normed_ref.shape[0]
+    gather = gather_of(item_ref, count)
+    grad_normed = dot(grad_hidden_ref[...], w_in_ref[:, :width], NT)
+    for part in range(3):
         columns = slice(part * width, (part + 1) * width)
+        inside = slice((part + 1) * width, (part + 2) * width)
         summed = dot(gather, active_ref[:, columns])
-        grad_hidden = (summed * rows_slope_ref[:, columns].astype(F32)).astype(BF16)
-        sums_ref[:, columns] = (dot(normed_ref[...], grad_hidden, TN) * total_factor).astype(BF16)
-        grad_normed = grad_normed + dot(grad_hidden, w_in_ref[:, columns], NT)
+        grad_hidden = (summed * rows_slope_ref[:, inside].astype(F32)).astype(BF16)
+        sums_ref[:, columns] = (dot(normed_ref[...], grad_hidden, TN) * factor).astype(BF16)
+        grad_normed = grad_normed + dot(grad_hidden, w_in_ref[:, inside], NT)
+    rows_hat_ref, rows_scale_ref, grad_y_ref, place_ref, digits_ref = (
+        get(name) for name in SECOND[8:]
+    )
     hat = rows_hat_ref[...]
     gain_rows = jnp.concatenate(
-        [jnp.sum(grad_normed * hat, axis=0, keepdims=True), gain_total]
+        [jnp.sum(grad_normed * hat, axis=0, keepdims=True), gain_ref[...]]
         + [jnp.zeros((14, width), F32)],
         axis=0,
     )
-    gains = (gain_rows * total_factor).astype(BF16)
-    sums_ref[:, 5 * width : 5 * width + LANES] = dot(gains, unit(16), TN).astype(BF16)
-    if sums_ref.shape[1] > 5 * width + LANES:
-        rest = sums_ref.shape[1] - 5 * width - LANES
-        sums_ref[:, 5 * width + LANES :] = jnp.zeros((width, rest), BF16)
+    gains = (gain_rows * factor).astype(BF16)
+    end = 3 * width + LANES
+    sums_ref[:, 3 * width : end] = dot(gains, unit(16), TN).astype(BF16)
+    if sums_ref.shape[1] > end:
+        sums_ref[:, end:] = jnp.zeros((width, sums_ref.shape[1] - end), BF16)
     inner = grad_normed * gain_in_ref[...]
     mean = jnp.mean(inner, axis=-1, keepdims=True)
     along = jnp.mean(inner * hat, axis=-1, keepdims=True)
-    row_grad = (inner - mean - hat * along) * rows_scale_ref[...] + dot(gather, grad_y)
+    row_grad = (inner - mean - hat * along) * rows_scale_ref[...] + dot(gather, grad_y_ref[...])
     places = table_ref.shape[0]
-    place = place_ref[...]
     spots = lax.broadcasted_iota(jnp.int32, (places, count), 0)
-    spread = jnp.where(spots == jnp.broadcast_to(place, (places, count)), 1.0, 0.0).astype(BF16)
+    hit = spots == jnp.broadcast_to(place_ref[...], (places, count))
+    spread = jnp.where(hit, 1.0, 0.0).astype(BF16)
     table_ref[:, :width] = dot(spread, row_grad.astype(BF16)).astype(BF16)
     table_ref[:, width:] = dot(spread, digits_ref[...]).astype(BF16)
-    for place_now in range(plan.chunks):
-        out_ref = (keep_ref, give_ref)[place_now // (plan.chunks // 2)]
-        out_ref[place_now % (plan.chunks // 2)] = sums_ref[plan.chunk_at(me, place_now)]
+    plan.write(me_ref[0], plan.second, sums_ref, keep_ref, give_ref)
 
 
 def unit(rows):
@@ -332,30 +365,60 @@
         self.row_groups = min(self.chunks, width // CHUNK_ROWS)
         self.column_groups = self.chunks // self.row_groups
         block = self.column_groups * LANES
-        blocks = -(-(5 * width + LANES) // block)
-        self.columns = blocks * block
-        self.wide = blocks * LANES
+        self.left = 2 * width // self.column_groups
+        self.right = -(-(3 * width + LANES) // block) * LANES
+        self.split = -(-(self.left + self.right) // (2 * LANES)) * LANES
         table_bits = [1 << bit for bit in range(1, table_size.bit_length() - 1)]
         dp_bits = [table_size << bit for bit in range(dp_size.bit_length() - 1)]
-        self.orders = (table_bits + dp_bits, dp_bits[:1] + table_bits + dp_bits[1:])
-        self.steps = len(self.orders[0])
-
-    def low_mask(self, core, place):
-        mask = 0
-        for step, bit in enumerate(self.orders[core]):
-            if place >> (self.steps - 1 - step) & 1:
-                mask ^= bit
-        return mask
-
-    def chunk_at(self, me, place):
+        far, near = table_bits + dp_bits[:1], dp_bits[:1] + table_bits
+        self.near_steps = len(far)
+        last = (dp_bits[1:], dp_bits[:0:-1])
+        self.first = (far + last[0], far + last[1])
+        self.second = (far + last[0], near + last[1])
+        self.third = (near + last[0], near + last[1])
+
+    def chunk(self, me, orders, place):
         top, low = divmod(place, self.chunks // 2)
-        masks = [top ^ self.low_mask(core ^ top, low) for core in range(2)]
-        chunk = me ^ jnp.where((me & 1) == 0, masks[0], masks[1])
-        first = pl.multiple_of((chunk & (self.row_groups - 1)) * CHUNK_ROWS, CHUNK_ROWS)
+        steps = len(orders[0])
+        masks = []
+        for core in range(2):
+            mask = top
+            for step, bit in enumerate(orders[core ^ top]):
+                if low >> (steps - 1 - step) & 1:
+                    mask ^= bit
+            masks.append(mask)
+        return me ^ jnp.where((me & 1) == 0, masks[0], masks[1])
+
+    def rows(self, chunk):
+        first = (chunk & (self.row_groups - 1)) * CHUNK_ROWS
+        return pl.ds(pl.multiple_of(first, CHUNK_ROWS), CHUNK_ROWS)
+
+    def columns(self, chunk, begin, group_width, first, size):
         if self.column_groups == 1:
-            return pl.ds(first, CHUNK_ROWS), slice(0, self.wide)
+            return slice(begin + first, begin + first + size)
         group = chunk >> (self.row_groups.bit_length() - 1)
-        return pl.ds(first, CHUNK_ROWS), pl.ds(pl.multiple_of(group * self.wide, LANES), self.wide)
+        return pl.ds(pl.multiple_of(group * group_width + begin + first, LANES), size)
+
+    def write(self, me, orders, sums_ref, keep_ref, give_ref):
+        half, _, wide = keep_ref.shape
+        for place in range(self.chunks):
+            chunk = self.chunk(me, orders, place)
+            columns = self.columns(chunk, 0, wide, 0, wide)
+            (keep_ref, give_ref)[place // half][place % half] = sums_ref[self.rows(chunk), columns]
+
+    def read(self, me, left_refs, right_refs, sums_ref):
+        half = self.chunks // 2
+        whole = self.left * self.column_groups
+        over = self.split - self.left
+        for place in range(self.chunks):
+            chunk = self.chunk(me, self.first, place)
+            rows = self.rows(chunk)
+            piece = left_refs[place // half].at[place % half]
+            sums_ref[rows, self.columns(chunk, 0, self.left, 0, self.left)] = piece[:, : self.left]
+            sums_ref[rows, self.columns(chunk, whole, self.right, 0, over)] = piece[:, self.left :]
+            chunk = self.chunk(me, self.third, place)
+            columns = self.columns(chunk, whole, self.right, over, self.right - over)
+            sums_ref[self.rows(chunk), columns] = right_refs[place // half][place % half]
 
 
 def table_body(got_ref, out_ref):
@@ -370,17 +433,17 @@
         out_ref[first : first + step, :] = dot(hit.astype(BF16), got_ref[:, :width])
 
 
-def widen_body(
-    plan, me_ref, own_ref, came_ref, w_in_ref, w_out_ref, gain_in_ref, gain_out_ref, sums_ref
-):
-    me = me_ref[0]
-    for place in range(plan.chunks):
-        in_ref = (own_ref, came_ref)[place // (plan.chunks // 2)]
-        sums_ref[plan.chunk_at(me, place)] = in_ref[place % (plan.chunks // 2)]
-    split, end = w_in_ref.shape[1], w_in_ref.shape[1] + w_out_ref.shape[1]
-    w_in_ref[...] = sums_ref[:, :split].astype(F32)
-    w_out_ref[...] = sums_ref[:, split:end].astype(F32)
-    gains = dot(unit(16), sums_ref[:, end : end + LANES], NT)
+def widen_body(plan, me_ref, *refs):
+    left_refs, right_refs, (w_in_ref, w_out_ref, gain_in_ref, gain_out_ref, sums_ref) = (
+        refs[:2],
+        refs[2:4],
+        refs[4:],
+    )
+    plan.read(me_ref[0], left_refs, right_refs, sums_ref)
+    width = w_out_ref.shape[0]
+    w_out_ref[...] = sums_ref[:, :width].astype(F32)
+    w_in_ref[...] = sums_ref[:, width : 5 * width].astype(F32)
+    gains = dot(unit(16), sums_ref[:, 5 * width : 5 * width + LANES], NT)
     gain_in_ref[...] = gains[0:1]
     gain_out_ref[...] = gains[1:2]
 
@@ -450,54 +513,87 @@
         owner_row.reshape(count, 1),
     )
 
-    half = shape_of((devices_all // 2, CHUNK_ROWS, plan.wide), BF16)
-    table_send, kept, sent = call(
-        functools.partial(backward_body, plan, total_factor),
-        [shape_of((devices_all * plan.capacity, width + LANES), BF16), half, half],
-        [SMEM] * 2 + [VMEM] * 4 + [HBM] * (len(SAVED) + 2),
-        flops=4 * count * width * width * 20,
-        moved=12_000_000,
+    saved = dict(zip(SAVED, saved), w_in=w_in, w_out=w_out)
+    items = row_of_token.reshape(1, tokens)
+
+    def near(names, **arrays):
+        arrays = saved | arrays
+        return [pltpu.VMEM(arrays[name].shape, arrays[name].dtype) for name in names] + [
+            pltpu.SemaphoreType.DMA((len(names),))
+        ]
+
+    def halves(wide):
+        return [shape_of((devices_all // 2, CHUNK_ROWS, wide), BF16)] * 2
+
+    first = dict(saved, rows_slope=saved["rows_slope"][:, :width])
+    scratch = near(FIRST, **first)
+    keep_left, give_left, grad_att, grad_hidden, grad_y, gain_total = call(
+        functools.partial(first_body, plan, total_factor),
+        halves(plan.left)
+        + [
+            shape_of((tokens, width), BF16),
+            shape_of((count, width), BF16),
+            shape_of((tokens, width), BF16),
+            shape_of((1, width), F32),
+        ],
+        [SMEM] * 2 + [VMEM] * 3 + [HBM] * len(FIRST),
+        flops=4 * count * width * width * 10,
+        moved=6_000_000,
         mebibytes=58,
-        scratch=[pltpu.VMEM(w_out.shape, BF16)]
-        + held
+        scratch=scratch[:-1]
+        + [pltpu.VMEM((width, 2 * width), BF16), pltpu.VMEM((tokens, width), BF16)]
+        + scratch[-1:],
+    )(me, seq_dest, items, gain_out, got, *(first[name] for name in FIRST))
+
+    left = add(keep_left, swap(give_left, (1, 1)))
+    left, grad_att = lax.optimization_barrier((left, grad_att))
+    second = dict(saved, grad_att=grad_att, grad_hidden=grad_hidden, grad_y=grad_y)
+    scratch = near(SECOND, **second)
+    table_send, keep_right, give_right = call(
+        functools.partial(second_body, plan, total_factor),
+        [shape_of((devices_all * plan.capacity, width + LANES), BF16)] + halves(plan.right),
+        [SMEM] + [VMEM] * 3 + [HBM] * len(SECOND),
+        flops=4 * count * width * width * 30,
+        moved=8_000_000,
+        mebibytes=58,
+        scratch=scratch[:-1]
         + [
-            pltpu.VMEM(w_in.shape, BF16),
-            pltpu.VMEM((width, plan.columns), BF16),
-            pltpu.VMEM((tokens, 4 * width), BF16),
-            pltpu.VMEM((tokens, width), BF16),
-            pltpu.SemaphoreType.DMA((len(SAVED) + 2,)),
-        ],
-    )(
-        me,
-        seq_dest,
-        row_of_token.reshape(1, tokens),
-        gain_in,
-        gain_out,
-        got,
-        w_out,
-        *saved,
-        w_in,
-    )
-
-    kept = add(kept, swap(sent, (1, 1)))
+            pltpu.VMEM((width, plan.column_groups * plan.right), BF16),
+            pltpu.VMEM((tokens, 3 * width), BF16),
+        ]
+        + scratch[-1:],
+    )(me, items, gain_in, gain_total, *(second[name] for name in SECOND))
+
+    def reduced(kept, masks):
+        middle = kept.shape[0] // 2
+        return add(kept[:middle], swap(kept[middle:], masks))
+
+    def gathered(kept, masks):
+        return jnp.concatenate([kept, swap(kept, masks)])
+
     table_got = exchange(table_send.reshape(devices_all, plan.capacity, width + LANES), both)
-    for step, masks in enumerate(zip(*plan.orders)):
-        if step == 2:
-            kept, table_got = lax.optimization_barrier((kept, table_got))
-        middle = kept.shape[0] // 2
-        came = swap(kept[middle:], masks)
-        kept = add(kept[:middle], came)
+    right = add(keep_right, swap(give_right, (1, 1)))
+    rounds = [list(zip(*orders)) for orders in (plan.first, plan.second, plan.third)]
+    for step in range(plan.near_steps):
+        left = reduced(left, rounds[0][step])
+        right = reduced(right, rounds[1][step])
+    kept = jnp.concatenate([left, right], axis=2)
+    kept, table_got = lax.optimization_barrier((kept, table_got))
     table_part = call(
         table_body,
         shape_of((ROWS_DEV, width), F32),
         [VMEM],
     )(table_got.reshape(devices_all * plan.capacity, width + LANES))
-    for step, masks in reversed(list(enumerate(zip(*plan.orders)))):
+    for masks in rounds[0][plan.near_steps :]:
+        kept = reduced(kept, masks)
+    for masks in reversed(rounds[0][plan.near_steps :]):
+        kept = gathered(kept, masks)
+    left, right = kept[..., : plan.split], kept[..., plan.split :]
+    for step in reversed(range(plan.near_steps)):
         if step == 0:
-            kept, table_part = lax.optimization_barrier((kept, table_part))
-        kept = jnp.concatenate([kept, swap(kept, masks)])
-    came = swap(kept, (1, 1))
-
+            left, right, table_part = lax.optimization_barrier((left, right, table_part))
+        left = gathered(left, rounds[0][step])
+        right = gathered(right, rounds[2][step])
     grad_w_in, grad_w_out, grad_gain_in, grad_gain_out = call(
         functools.partial(widen_body, plan),
         (
@@ -506,9 +602,9 @@
             shape_of((1, width), F32),
             shape_of((1, width), F32),
         ),
-        [SMEM] + [VMEM] * 2,
-        scratch=[pltpu.VMEM((width, plan.columns), BF16)],
-    )(me, kept, came)
+        [SMEM] + [VMEM] * 4,
+        scratch=[pltpu.VMEM((width, plan.column_groups * (plan.left + plan.right)), BF16)],
+    )(me, left, swap(left, (1, 1)), right, swap(right, (1, 1)))
     return (table_part, grad_w_in, grad_w_out, grad_gain_in[0], grad_gain_out[0])
 
 

time: 131 us -> 134 us (1.023)
  waiting for transfers between devices: 68.6 us -> 58.1 us
  starting transfers between devices: 24.7 us -> 33 us
  Pallas kernels: 28.1 us -> 30.7 us
  local copies, waits for them, and re-layouts: 5.03 us -> 6.7 us
    ppermute x10 -> x16, waiting for transfers between devices: 60.4 us -> 47.8 us  [swap(): return lax.ppermute(values, both, pairs)]
    ppermute x10 -> x16, starting transfers between devices: 10.5 us -> 17.2 us  [swap(): return lax.ppermute(values, both, pairs)]
    pallas_call x1 -> x2, Pallas kernels: 12.6 us -> 15.4 us  [the longest x1 9.27 us: on_device(): call(functools.partial(second_body, plan, total_factor), [shape_of((devic...]
    all_to_all x3, waiting for transfers between devices: 8.19 us -> 10.3 us  [exchange(): return lax.all_to_all(values, axes, split_axis=0, concat_axis=0, tiled=True)]
    slice x4 -> x8, local copies, waits for them, and re-layouts: 0.1 us -> 1.79 us  [the longest x1 1.68 us: on_device(): first = dict(saved, rows_slope=saved['rows_slope'][:, :width])]
    all_to_all x3, starting transfers between devices: 14.2 us -> 15.8 us  [exchange(): return lax.all_to_all(values, axes, split_axis=0, concat_axis=0, tiled=True)]
    convert_element_type x5 -> x8, other arithmetic: 2.03 us -> 2.93 us  [add(): return (left.astype(F32) + right.astype(F32)).astype(BF16)]
  transfers between devices with their start and end apart: 13 -> 19, of which waited for: 12 -> 16; matrix products, arithmetic and copies ran while one was open for 2% -> 5% of each run, Pallas kernels for 9% -> 8%
where the time goes in v7:
time: 134 us; the launch traced here: 133 us
  waiting for transfers between devices  58.1 us (43%)
  starting transfers between devices  33 us (25%)
  Pallas kernels  30.7 us (23%)
  local copies, waits for them, and re-layouts  6.7 us (5%)
  other arithmetic  3.79 us (3%)
    ppermute x16, waiting for transfers between devices, swap(): return lax.ppermute(values, both, pairs)  47.8 us
    ppermute x16, starting transfers between devices, swap(): return lax.ppermute(values, both, pairs)  17.2 us
    all_to_all x3, starting transfers between devices, exchange(): return lax.all_to_all(values, axes, split_axis=0, concat_axis=0, tiled=True)  15.8 us
    all_to_all x3, waiting for transfers between devices, exchange(): return lax.all_to_all(values, axes, split_axis=0, concat_axis=0, tiled=True)  10.3 us
    pallas_call x1, Pallas kernels, on_device(): call(functools.partial(second_body, plan, total_factor), [shape_of((devic...  9.27 us
    pallas_call x1, Pallas kernels, on_device(): call(functools.partial(forward_body, plan.capacity), shapes, [VMEM] * 8,...  8.96 us
    pallas_call x1, Pallas kernels, on_device(): call(functools.partial(first_body, plan, total_factor), halves(plan.left)...  6.17 us
    convert_element_type x8, other arithmetic, add(): return (left.astype(F32) + right.astype(F32)).astype(BF16)  2.93 us
  transfers between devices with their start and end apart: 19, of which 16 were waited for; matrix products, arithmetic and copies ran while one was open for 5% of the time, Pallas kernels for 8%

profile of v7, /device:TPU:0, one launch (start us, length us, event | category | flops | bytes accessed | tf_op | source)
XLA Modules:
  0.0 133.2 jit_solution(4794972410273394397)
XLA Ops:
  0.7 0.7 multiply_add_fusion
  1.4 0.6 broadcast_in_dim.14
  2.0 7.3 %all-to-all-start = ((s32[8,1,8]{2,1,0:T(1,128)}), s32[8,1,8]{2,1,0:T(1,128)S(1)}, u32[]{:S(2)}, u32[]{:S(2)}) async-start(s32[8,1,8]{2,1,0:T(1,128)} %broadcast_in_dim.14), calls=%async_computation | async-start | bytes 8192 | tf_op jit(solution)/shard_map/all_to_all | solution.py:483
  9.2 6.4 %all-to-all-done.packed_ref = s32[8,1,8]{2,1,0:T(1,128)S(1)} async-done(((s32[8,1,8]{2,1,0:T(1,128)}), s32[8,1,8]{2,1,0:T(1,128)S(1)}, u32[]{:S(2)}, u32[]{:S(2)}) %all-to-all-start) | async-done | bytes 288 | tf_op jit(solution)/shard_map/all_to_all | solution.py:483
  15.6 0.9 copy-done
  16.5 1.6 %shard_map.146 = bf16[8,64,512]{2,1,0:T(8,128)(2,1)} custom-call(s32[1]{0:T(128)} %bitcast.me_ref, s32[8,1,8]{2,1,0:T(1,128)S(1)} %all-to-all-done.packed_ref, bf16[256,512]{1,0:T(8,128)(2,1)S(1)} %copy-done), custom_call_target="tpu_custom_call" | custom-call | tf_op jit(solution)/shard_map/pallas_call | solution.py:486
  18.1 3.5 %all-to-all-start.1 = ((bf16[8,64,512]{2,1,0:T(8,128)(2,1)}), bf16[8,64,512]{2,1,0:T(8,128)(2,1)S(1)}, u32[]{:S(2)}, u32[]{:S(2)}) async-start(bf16[8,64,512]{2,1,0:T(8,128)(2,1)} %shard_map.146), calls=%async_computation.1 | async-start | bytes 1048576 | tf_op jit(solution)/shard_map/all_to_all | solution.py:483
  21.6 0.8 copy.19.number_ref
  22.4 0.8 copy.18.owner_col_ref
  23.2 0.9 copy.17.item_ref
  24.1 9.0 %shard_map.147 = (f32[512,512]{1,0:T(8,128)}, f32[512,512]{1,0:T(8,128)}, f32[512,1]{1,0:T(8,128)}, bf16[512,1536]{1,0:T(8,128)(2,1)}, bf16[16,128,128]{2,1,0:T(...) custom-call(bf16[256,512]{1,0:T(8,128)(2,1)} %rows_ref.1, ...), custom_call_target="tpu_custom_call" | custom-call | flops 2147483648 | bytes 10000000 | tf_op jit(solution)/shard_map/pallas_call | solution.py:496
  33.0 1.7 %slice.45.refs_6_ = bf16[256,512]{1,0:T(8,128)(2,1)} slice(bf16[256,2048]{1,0:T(8,128)(2,1)} %get-tuple-element.43.refs_5_), slice={[0:256], [0:512]} | slice | bytes 524288 | tf_op jit(solution)/shard_map/slice | solution.py:528
  34.7 0.1 all-to-all-done.1.got_ref
  34.9 0.8 copy-done.1
  35.7 6.2 %shard_map.148 = (bf16[16,16,1024]{2,1,0:T(8,128)(2,1)}, bf16[16,16,1024]{2,1,0:T(8,128)(2,1)}, bf16[512,512]{1,0:T(8,128)(2,1)}, bf16[256,512]{1,0:T(8,128)(2,1...) custom-call(s32[1]{0:T(128)} %bitcast.me_ref, s32[8]{0:T(128)} %dest_ref.1, s32[1,512]{1,0:T(1,128)} %bitcast.12, ...), custom_call_target="tpu_custom_call" | custom-call | flops 2684354560 | bytes 6000000 | tf_op jit(solution)/shard_map/pallas_call | solution.py:530
  41.9 2.1 %collective-permute-done = bf16[16,16,1024]{2,1,0:T(8,128)(2,1)S(1)} collective-permute-done((bf16[16,16,1024]{2,1,0:T(8,128)(2,1)}, bf16[16,16,1024]{2,1,0:T(8,128)(2,1)S(1)}, u32[]{:S(2)}, u32[]{:S(2)}) %collective-permute-start) | collective-permute-done | bytes 524320 | tf_op jit(solution)/shard_map/ppermute | solution.py:480
  44.0 1.2 add_convert_fusion.1
  45.3 9.3 %shard_map.149 = (bf16[512,640]{1,0:T(8,128)(2,1)}, bf16[16,16,1664]{2,1,0:T(8,128)(2,1)}, bf16[16,16,1664]{2,1,0:T(8,128)(2,1)}) custom-call(s32[1]{0:T(128)} %bitcast.me_ref, s32[1,512]{1,0:T(1,128)} %bitcast.13, f32[1,512]{1,0:T(1,128)} %bitcast.20, f32[1,512]{1,0:T(1,128)} %get-tuple-element.48.gain_ref, bf16[512,512]{1,0:T(8,128)(2,1)} %get-tuple-element.49.refs_0_, ...), custom_call_target="tpu_custom_call" | custom-call | flops 8053063680 | bytes 8000000 | tf_op jit(solution)/shard_map/pallas_call | solution.py:552
  54.5 0.2 collective-permute-start.3
  54.8 1.6 %collective-permute-start.1 = (bf16[8,16,1024]{2,1,0:T(8,128)(2,1)S(1)}, bf16[8,16,1024]{2,1,0:T(8,128)(2,1)S(1)}, u32[]{:S(2)}, u32[]{:S(2)}) collective-permute-start(bf16[8,16,1024]{2,1,0:T(8,128)(2,1)S(1)} %slice.47), channel_id=1, source_target_pairs={{0,2},{1,3},{2,0},{3,1},{4,6},{5,7},{6,4},{7,5},{8,10},{9,11},{10,... | collective-permute-start | bytes 786440 | tf_op jit(solution)/shard_map/ppermute | solution.py:480
  56.4 0.8 collective-permute-done.3
  57.2 1.4 %add_convert_fusion = bf16[16,16,1664]{2,1,0:T(8,128)(2,1)S(1)} fusion(bf16[16,16,1664]{2,1,0:T(8,128)(2,1)S(1)} %collective-permute-done.3, bf16[16,16,1664]{2,1,0:T(8,128)(2,1)} %get-tuple-element.59), kind=kLoop, calls=%fused_computation | loop fusion | flops 1703936 | bytes 2555904 | tf_op jit(solution)/shard_map/convert_element_type | solution.py:452
  58.6 1.6 %collective-permute-start.4 = (bf16[8,16,1664]{2,1,0:T(8,128)(2,1)S(1)}, bf16[8,16,1664]{2,1,0:T(8,128)(2,1)S(1)}, u32[]{:S(2)}, u32[]{:S(2)}) collective-permute-start(bf16[8,16,1664]{2,1,0:T(8,128)(2,1)S(1)} %slice.63), channel_id=1, source_target_pairs={{0,2},{1,5},{2,0},{3,7},{4,6},{5,1},{6,4},{7,3},{8,10},{9,13},{10,... | collective-permute-start | bytes 1277960 | tf_op jit(solution)/shard_map/ppermute | solution.py:480
  60.2 5.1 %all-to-all-start.2 = ((bf16[32,16,640]{2,1,0:T(8,128)(2,1)}), bf16[32,16,640]{2,1,0:T(8,128)(2,1)S(1)}, u32[]{:S(2)}, u32[]{:S(2)}) async-start(bf16[32,16,640]{2,1,0:T(8,128)(2,1)} %bitcast.7), calls=%async_computation.2 | async-start | bytes 1310720 | tf_op jit(solution)/shard_map/all_to_all | solution.py:483
  65.4 1.7 %collective-permute-start.2 = (bf16[4,16,1024]{2,1,0:T(8,128)(2,1)S(1)}, bf16[4,16,1024]{2,1,0:T(8,128)(2,1)S(1)}, u32[]{:S(2)}, u32[]{:S(2)}) collective-permute-start(bf16[4,16,1024]{2,1,0:T(8,128)(2,1)S(1)} %slice.61), channel_id=1, source_target_pairs={{0,4},{1,5},{2,6},{3,7},{4,0},{5,1},{6,2},{7,3},{8,12},{9,13},{10,... | collective-permute-start | bytes 393224 | tf_op jit(solution)/shard_map/ppermute | solution.py:480
  67.0 1.0 collective-permute-done.4
  68.0 0.1 add_convert_fusion.2
  68.1 5.7 %collective-permute-start.5 = (bf16[4,16,1664]{2,1,0:T(8,128)(2,1)S(1)}, bf16[4,16,1664]{2,1,0:T(8,128)(2,1)S(1)}, u32[]{:S(2)}, u32[]{:S(2)}) collective-permute-start(bf16[4,16,1664]{2,1,0:T(8,128)(2,1)S(1)} %slice.65), channel_id=1, source_target_pairs={{0,4},{1,3},{2,6},{3,1},{4,0},{5,7},{6,2},{7,5},{8,12},{9,11},{10,... | collective-permute-start | bytes 638984 | tf_op jit(solution)/shard_map/ppermute | solution.py:480
  73.8 2.3 %collective-permute-done.2 = bf16[4,16,1024]{2,1,0:T(8,128)(2,1)S(1)} collective-permute-done((bf16[4,16,1024]{2,1,0:T(8,128)(2,1)S(1)}, bf16[4,16,1024]{2,1,0:T(8,128)(2,1)S(1)}, u32[]{:S(2)}, u32[]{:S(2)}) %collective-permute-start.2) | collective-permute-done | bytes 131104 | tf_op jit(solution)/shard_map/ppermute | solution.py:480
  76.1 3.1 %collective-permute-done.5 = bf16[4,16,1664]{2,1,0:T(8,128)(2,1)S(1)} collective-permute-done((bf16[4,16,1664]{2,1,0:T(8,128)(2,1)S(1)}, bf16[4,16,1664]{2,1,0:T(8,128)(2,1)S(1)}, u32[]{:S(2)}, u32[]{:S(2)}) %collective-permute-start.5) | collective-permute-done | bytes 213024 | tf_op jit(solution)/shard_map/ppermute | solution.py:480
  79.3 3.7 %all-to-all-done.2 = bf16[32,16,640]{2,1,0:T(8,128)(2,1)S(1)} async-done(((bf16[32,16,640]{2,1,0:T(8,128)(2,1)}), bf16[32,16,640]{2,1,0:T(8,128)(2,1)S(1)}, u32[]{:S(2)}, u32[]{:S(2)}) %all-to-all-start.2) | async-done | bytes 655392 | tf_op jit(solution)/shard_map/all_to_all | solution.py:483
  83.0 1.5 %collective-permute-start.6 = (bf16[2,16,2688]{2,1,0:T(8,128)(2,1)S(1)}, bf16[2,16,2688]{2,1,0:T(8,128)(2,1)S(1)}, u32[]{:S(2)}, u32[]{:S(2)}) collective-permute-start(bf16[2,16,2688]{2,1,0:T(8,128)(2,1)S(1)} %slice.55), channel_id=1, source_target_pairs={{0,8},{1,17},{2,10},{3,19},{4,12},{5,21},{6,14},{7,23},{8,0},{9,25... | collective-permute-start | bytes 516104 | tf_op jit(solution)/shard_map/ppermute | solution.py:480
  84.5 5.8 %collective-permute-done.6 = bf16[2,16,2688]{2,1,0:T(8,128)(2,1)S(1)} collective-permute-done((bf16[2,16,2688]{2,1,0:T(8,128)(2,1)S(1)}, bf16[2,16,2688]{2,1,0:T(8,128)(2,1)S(1)}, u32[]{:S(2)}, u32[]{:S(2)}) %collective-permute-start.6) | collective-permute-done | bytes 172064 | tf_op jit(solution)/shard_map/ppermute | solution.py:480
  90.4 0.6 collective-permute-start.7
  91.0 5.9 %collective-permute-done.7 = bf16[1,16,2688]{2,1,0:T(8,128)(2,1)S(1)} collective-permute-done((bf16[1,16,2688]{2,1,0:T(8,128)(2,1)S(1)}, bf16[1,16,2688]{2,1,0:T(8,128)(2,1)S(1)}, u32[]{:S(2)}, u32[]{:S(2)}) %collective-permute-start.7) | collective-permute-done | bytes 86048 | tf_op jit(solution)/shard_map/ppermute | solution.py:480
  97.0 8.4 %collective-permute-done.8 = bf16[1,16,2688]{2,1,0:T(8,128)(2,1)S(1)} collective-permute-done((bf16[1,16,2688]{2,1,0:T(8,128)(2,1)S(1)}, bf16[1,16,2688]{2,1,0:T(8,128)(2,1)S(1)}, u32[]{:S(2)}, u32[]{:S(2)}) %collective-permute-start.8) | collective-permute-done | bytes 86048 | tf_op jit(solution)/shard_map/ppermute | solution.py:480
  105.4 0.1 collective-permute-start.9
  105.5 2.2 %shard_map.150 = f32[1024,512]{1,0:T(8,128)} custom-call(bf16[512,640]{1,0:T(8,128)(2,1)S(1)} %bitcast.11), custom_call_target="tpu_custom_call" | custom-call | tf_op jit(solution)/shard_map/pallas_call | solution.py:582
  107.7 3.2 %collective-permute-done.9 = bf16[2,16,2688]{2,1,0:T(8,128)(2,1)S(1)} collective-permute-done((bf16[2,16,2688]{2,1,0:T(8,128)(2,1)S(1)}, bf16[2,16,2688]{2,1,0:T(8,128)(2,1)S(1)}, u32[]{:S(2)}, u32[]{:S(2)}) %collective-permute-start.9) | collective-permute-done | bytes 172064 | tf_op jit(solution)/shard_map/ppermute | solution.py:480
  111.1 1.3 collective-permute-start.10
  112.4 5.6 %collective-permute-done.11 = bf16[4,16,1280]{2,1,0:T(8,128)(2,1)S(1)} collective-permute-done((bf16[4,16,1280]{2,1,0:T(8,128)(2,1)S(1)}, bf16[4,16,1280]{2,1,0:T(8,128)(2,1)S(1)}, u32[]{:S(2)}, u32[]{:S(2)}) %collective-permute-start.11) | collective-permute-done | bytes 163872 | tf_op jit(solution)/shard_map/ppermute | solution.py:480
  118.0 0.6 collective-permute-done.10
  118.6 1.3 collective-permute-start.14
  119.9 0.9 collective-permute-start.12
  120.9 6.5 %collective-permute-done.12 = bf16[8,16,1408]{2,1,0:T(8,128)(2,1)S(1)} collective-permute-done((bf16[8,16,1408]{2,1,0:T(8,128)(2,1)S(1)}, bf16[8,16,1408]{2,1,0:T(8,128)(2,1)S(1)}, u32[]{:S(2)}, u32[]{:S(2)}) %collective-permute-start.12) | collective-permute-done | bytes 360480 | tf_op jit(solution)/shard_map/ppermute | solution.py:480
  127.5 0.5 collective-permute-start.15
  128.0 2.5 %collective-permute-done.15.refs_3_ = bf16[16,16,1280]{2,1,0:T(8,128)(2,1)S(1)} collective-permute-done((bf16[16,16,1280]{2,1,0:T(8,128)(2,1)S(1)}, bf16[16,16,1280]{2,1,0:T(8,128)(2,1)S(1)}, u32[]{:S(2)}, u32[]{:S(2)}) %collective-permute-start.15) | collective-permute-done | bytes 655392 | tf_op jit(solution)/shard_map/ppermute | solution.py:480
  130.6 2.6 %shard_map.151 = (f32[512,2048]{1,0:T(8,128)}, f32[512,512]{1,0:T(8,128)}, f32[1,512]{1,0:T(1,128)}, f32[1,512]{1,0:T(1,128)}) custom-call(s32[1]{0:T(128)} %bitcast.me_ref, bf16[16,16,1408]{2,1,0:T(8,128)(2,1)S(1)} %constant_dynamic-update-slice_fusion.refs_0_, bf16[16,16,1408]{2,1,0:T(8,128)(2,1)S(1)} %collective-permute-done.13.refs_1_, ...), custom_call_target="tpu_custom_call" | custom-call | tf_op jit(solution)/shard_map/pallas_call | solution.py:597
  (37 shorter events, 0.9 us)
Async XLA Ops:
  0.6 21.0 %copy-start.3 = (s32[256]{0:T(256)S(1)}, s32[256]{0:T(256)}, u32[]{:S(2)}) copy-start(s32[256]{0:T(256)} %param.14) | copy-start | bytes 3076
  0.6 21.8 %copy-start.4 = (s32[256,1]{0,1:T(1,128)S(1)}, s32[256,1]{0,1:T(1,128)}, u32[]{:S(2)}) copy-start(s32[256,1]{0,1:T(1,128)} %param.13) | copy-start | bytes 3076
  0.7 22.6 %copy-start.2 = (s32[512]{0:T(512)S(1)}, s32[512]{0:T(512)}, u32[]{:S(2)}) copy-start(s32[512]{0:T(512)} %param.12) | copy-start | bytes 6148
  2.0 13.6 %all-to-all-start = ((s32[8,1,8]{2,1,0:T(1,128)}), s32[8,1,8]{2,1,0:T(1,128)S(1)}, u32[]{:S(2)}, u32[]{:S(2)}) async-start(s32[8,1,8]{2,1,0:T(1,128)} %broadcast_in_dim.14), calls=%async_computation | async-start | bytes 8192 | tf_op jit(solution)/shard_map/all_to_all | solution.py:483
  15.6 1.0 copy-start
  18.1 16.8 %all-to-all-start.1 = ((bf16[8,64,512]{2,1,0:T(8,128)(2,1)}), bf16[8,64,512]{2,1,0:T(8,128)(2,1)S(1)}, u32[]{:S(2)}, u32[]{:S(2)}) async-start(bf16[8,64,512]{2,1,0:T(8,128)(2,1)} %shard_map.146), calls=%async_computation.1 | async-start | bytes 1048576 | tf_op jit(solution)/shard_map/all_to_all | solution.py:483
  34.9 0.8 copy-start.1
  41.8 2.2 %collective-permute-start = (bf16[16,16,1024]{2,1,0:T(8,128)(2,1)}, bf16[16,16,1024]{2,1,0:T(8,128)(2,1)S(1)}, u32[]{:S(2)}, u32[]{:S(2)}) collective-permute-start(bf16[16,16,1024]{2,1,0:T(8,128)(2,1)} %get-tuple-element.45), channel_id=1, source_target_pairs={{0,1},{1,0},{2,3},{3,2},{4,5},{5,4},{6,7},{7,6},{8,9},{9,8},{10,11... | collective-permute-start | bytes 1572872 | tf_op jit(solution)/shard_map/ppermute | solution.py:480
  54.5 2.7 %collective-permute-start.3 = (bf16[16,16,1664]{2,1,0:T(8,128)(2,1)}, bf16[16,16,1664]{2,1,0:T(8,128)(2,1)S(1)}, u32[]{:S(2)}, u32[]{:S(2)}) collective-permute-start(bf16[16,16,1664]{2,1,0:T(8,128)(2,1)} %get-tuple-element.60), channel_id=1, source_target_pairs={{0,1},{1,0},{2,3},{3,2},{4,5},{5,4},{6,7},{7,6},{8,9},{9,8},{10,11... | collective-permute-start | bytes 2555912 | tf_op jit(solution)/shard_map/ppermute | solution.py:480
  54.8 10.5 %collective-permute-start.1 = (bf16[8,16,1024]{2,1,0:T(8,128)(2,1)S(1)}, bf16[8,16,1024]{2,1,0:T(8,128)(2,1)S(1)}, u32[]{:S(2)}, u32[]{:S(2)}) collective-permute-start(bf16[8,16,1024]{2,1,0:T(8,128)(2,1)S(1)} %slice.47), channel_id=1, source_target_pairs={{0,2},{1,3},{2,0},{3,1},{4,6},{5,7},{6,4},{7,5},{8,10},{9,11},{10,... | collective-permute-start | bytes 786440 | tf_op jit(solution)/shard_map/ppermute | solution.py:480
  58.6 9.4 %collective-permute-start.4 = (bf16[8,16,1664]{2,1,0:T(8,128)(2,1)S(1)}, bf16[8,16,1664]{2,1,0:T(8,128)(2,1)S(1)}, u32[]{:S(2)}, u32[]{:S(2)}) collective-permute-start(bf16[8,16,1664]{2,1,0:T(8,128)(2,1)S(1)} %slice.63), channel_id=1, source_target_pairs={{0,2},{1,5},{2,0},{3,7},{4,6},{5,1},{6,4},{7,3},{8,10},{9,13},{10,... | collective-permute-start | bytes 1277960 | tf_op jit(solution)/shard_map/ppermute | solution.py:480
  60.2 22.8 %all-to-all-start.2 = ((bf16[32,16,640]{2,1,0:T(8,128)(2,1)}), bf16[32,16,640]{2,1,0:T(8,128)(2,1)S(1)}, u32[]{:S(2)}, u32[]{:S(2)}) async-start(bf16[32,16,640]{2,1,0:T(8,128)(2,1)} %bitcast.7), calls=%async_computation.2 | async-start | bytes 1310720 | tf_op jit(solution)/shard_map/all_to_all | solution.py:483
  65.4 10.7 %collective-permute-start.2 = (bf16[4,16,1024]{2,1,0:T(8,128)(2,1)S(1)}, bf16[4,16,1024]{2,1,0:T(8,128)(2,1)S(1)}, u32[]{:S(2)}, u32[]{:S(2)}) collective-permute-start(bf16[4,16,1024]{2,1,0:T(8,128)(2,1)S(1)} %slice.61), channel_id=1, source_target_pairs={{0,4},{1,5},{2,6},{3,7},{4,0},{5,1},{6,2},{7,3},{8,12},{9,13},{10,... | collective-permute-start | bytes 393224 | tf_op jit(solution)/shard_map/ppermute | solution.py:480
  68.1 11.1 %collective-permute-start.5 = (bf16[4,16,1664]{2,1,0:T(8,128)(2,1)S(1)}, bf16[4,16,1664]{2,1,0:T(8,128)(2,1)S(1)}, u32[]{:S(2)}, u32[]{:S(2)}) collective-permute-start(bf16[4,16,1664]{2,1,0:T(8,128)(2,1)S(1)} %slice.65), channel_id=1, source_target_pairs={{0,4},{1,3},{2,6},{3,1},{4,0},{5,7},{6,2},{7,5},{8,12},{9,11},{10,... | collective-permute-start | bytes 638984 | tf_op jit(solution)/shard_map/ppermute | solution.py:480
  83.0 7.3 %collective-permute-start.6 = (bf16[2,16,2688]{2,1,0:T(8,128)(2,1)S(1)}, bf16[2,16,2688]{2,1,0:T(8,128)(2,1)S(1)}, u32[]{:S(2)}, u32[]{:S(2)}) collective-permute-start(bf16[2,16,2688]{2,1,0:T(8,128)(2,1)S(1)} %slice.55), channel_id=1, source_target_pairs={{0,8},{1,17},{2,10},{3,19},{4,12},{5,21},{6,14},{7,23},{8,0},{9,25... | collective-permute-start | bytes 516104 | tf_op jit(solution)/shard_map/ppermute | solution.py:480
  90.4 6.5 %collective-permute-start.7 = (bf16[1,16,2688]{2,1,0:T(8,128)(2,1)S(1)}, bf16[1,16,2688]{2,1,0:T(8,128)(2,1)S(1)}, u32[]{:S(2)}, u32[]{:S(2)}) collective-permute-start(bf16[1,16,2688]{2,1,0:T(8,128)(2,1)S(1)} %slice.67), channel_id=1, source_target_pairs={{0,16},{1,9},{2,18},{3,11},{4,20},{5,13},{6,22},{7,15},{8,24},{9,1... | collective-permute-start | bytes 258056 | tf_op jit(solution)/shard_map/ppermute | solution.py:480
  96.9 8.5 %collective-permute-start.8 = (bf16[1,16,2688]{2,1,0:T(8,128)(2,1)S(1)}, bf16[1,16,2688]{2,1,0:T(8,128)(2,1)S(1)}, u32[]{:S(2)}, u32[]{:S(2)}) collective-permute-start(bf16[1,16,2688]{2,1,0:T(8,128)(2,1)S(1)} %add_convert_fusion.7), channel_id=1, source_target_pairs={{0,16},{1,9},{2,18},{3,11},{4,20},{5,13},{6,22},{7,15},{8,24},{9,1... | collective-permute-start | bytes 258056 | tf_op jit(solution)/shard_map/ppermute | solution.py:480
  105.4 5.5 %collective-permute-start.9 = (bf16[2,16,2688]{2,1,0:T(8,128)(2,1)S(1)}, bf16[2,16,2688]{2,1,0:T(8,128)(2,1)S(1)}, u32[]{:S(2)}, u32[]{:S(2)}) collective-permute-start(bf16[2,16,2688]{2,1,0:T(8,128)(2,1)S(1)} %pad_maximum_fusion.4), channel_id=1, source_target_pairs={{0,8},{1,17},{2,10},{3,19},{4,12},{5,21},{6,14},{7,23},{8,0},{9,25... | collective-permute-start | bytes 516104 | tf_op jit(solution)/shard_map/ppermute | solution.py:480
  110.9 7.1 %collective-permute-start.11 = (bf16[4,16,1280]{2,1,0:T(8,128)(2,1)S(1)}, bf16[4,16,1280]{2,1,0:T(8,128)(2,1)S(1)}, u32[]{:S(2)}, u32[]{:S(2)}) collective-permute-start(bf16[4,16,1280]{2,1,0:T(8,128)(2,1)S(1)} %pad_maximum_fusion.5), channel_id=1, source_target_pairs={{0,2},{1,3},{2,0},{3,1},{4,6},{5,7},{6,4},{7,5},{8,10},{9,11},{10,... | collective-permute-start | bytes 491528 | tf_op jit(solution)/shard_map/ppermute | solution.py:480
  111.1 7.5 %collective-permute-start.10 = (bf16[4,16,1408]{2,1,0:T(8,128)(2,1)S(1)}, bf16[4,16,1408]{2,1,0:T(8,128)(2,1)S(1)}, u32[]{:S(2)}, u32[]{:S(2)}) collective-permute-start(bf16[4,16,1408]{2,1,0:T(8,128)(2,1)S(1)} %slice.68), channel_id=1, source_target_pairs={{0,4},{1,5},{2,6},{3,7},{4,0},{5,1},{6,2},{7,3},{8,12},{9,13},{10,... | collective-permute-start | bytes 540680 | tf_op jit(solution)/shard_map/ppermute | solution.py:480
  118.6 8.8 %collective-permute-start.14 = (bf16[8,16,1280]{2,1,0:T(8,128)(2,1)S(1)}, bf16[8,16,1280]{2,1,0:T(8,128)(2,1)S(1)}, u32[]{:S(2)}, u32[]{:S(2)}) collective-permute-start(bf16[8,16,1280]{2,1,0:T(8,128)(2,1)S(1)} %pad_maximum_fusion.3), channel_id=1, source_target_pairs={{0,4},{1,5},{2,6},{3,7},{4,0},{5,1},{6,2},{7,3},{8,12},{9,13},{10,... | collective-permute-start | bytes 983048 | tf_op jit(solution)/shard_map/ppermute | solution.py:480
  119.9 7.4 %collective-permute-start.12 = (bf16[8,16,1408]{2,1,0:T(8,128)(2,1)S(1)}, bf16[8,16,1408]{2,1,0:T(8,128)(2,1)S(1)}, u32[]{:S(2)}, u32[]{:S(2)}) collective-permute-start(bf16[8,16,1408]{2,1,0:T(8,128)(2,1)S(1)} %pad_maximum_fusion), channel_id=1, source_target_pairs={{0,2},{1,3},{2,0},{3,1},{4,6},{5,7},{6,4},{7,5},{8,10},{9,11},{10,... | collective-permute-start | bytes 1081352 | tf_op jit(solution)/shard_map/ppermute | solution.py:480
  127.4 3.2 %collective-permute-start.13 = (bf16[16,16,1408]{2,1,0:T(8,128)(2,1)S(1)}, bf16[16,16,1408]{2,1,0:T(8,128)(2,1)S(1)}, u32[]{:S(2)}, u32[]{:S(2)}) collective-permute-start(bf16[16,16,1408]{2,1,0:T(8,128)(2,1)S(1)} %constant_dynamic-update-slice_fusion.refs_0_), channel_id=1, source_target_pairs={{0,1},{1,0},{2,3},{3,2},{4,5},{5,4},{6,7},{7,6},{8,9},{9,8},{10,11... | collective-permute-start | bytes 2162696 | tf_op jit(solution)/shard_map/ppermute | solution.py:480
  127.5 3.1 %collective-permute-start.15 = (bf16[16,16,1280]{2,1,0:T(8,128)(2,1)S(1)}, bf16[16,16,1280]{2,1,0:T(8,128)(2,1)S(1)}, u32[]{:S(2)}, u32[]{:S(2)}) collective-permute-start(bf16[16,16,1280]{2,1,0:T(8,128)(2,1)S(1)} %constant_dynamic-update-slice_fusion.2.refs_2_), channel_id=1, source_target_pairs={{0,1},{1,0},{2,3},{3,2},{4,5},{5,4},{6,7},{7,6},{8,9},{9,8},{10,11... | collective-permute-start | bytes 1966088 | tf_op jit(solution)/shard_map/ppermute | solution.py:480

commit v8 on v6

--- a/solution.py
+++ b/solution.py
@@ -218,36 +218,67 @@
         copy.wait()
 
 
-def backward_body(
-    plan, total_factor, me_ref, dest_ref, item_ref, gain_in_ref, gain_out_ref, got_ref, *refs
-):
-    size = len(SAVED) + 2
-    far_refs, (table_ref, keep_ref, give_ref), near_refs = (
-        refs[:size],
-        refs[size : size + 3],
-        refs[size + 3 : 2 * size + 3],
-    )
-    sums_ref, active_ref, grad_y_ref, sems = refs[2 * size + 3 :]
-    copies = [
-        pltpu.make_async_copy(far, near, sems.at[index])
-        for index, (far, near) in enumerate(zip(far_refs, near_refs))
+def fetch(names, far_refs, near_refs, sems):
+    copies = {}
+    for index, name in enumerate(names):
+        copies[name] = pltpu.make_async_copy(far_refs[index], near_refs[index], sems.at[index])
+        copies[name].start()
+
+    def get(name):
+        copies[name].wait()
+        return near_refs[names.index(name)]
+
+    return get
+
+
+def gather_of(item_ref, count):
+    tokens = item_ref.shape[1]
+    sub = lax.broadcasted_iota(jnp.int32, (count, tokens), 0)
+    hit = sub == jnp.broadcast_to(item_ref[...], (count, tokens))
+    return jnp.where(hit, 1.0, 0.0).astype(BF16)
+
+
+FETCHED = (
+    "got",
+    "w_out",
+    "hat",
+    "gate",
+    "hat_scale",
+    "qkv",
+    "slope",
+    "weight",
+    "mixed",
+    "normed",
+    "rows_slope",
+    "w_in",
+    "rows_hat",
+    "rows_scale",
+    "place",
+    "digits",
+)
+
+
+def backward_body(plan, factor, me_ref, dest_ref, item_ref, gain_in_ref, gain_out_ref, *refs):
+    size = len(FETCHED)
+    far_refs, out_refs, refs = refs[:size], refs[size : size + 5], refs[size + 5 :]
+    near_refs, stage_refs, refs = refs[:size], refs[size : size + 5], refs[size + 5 :]
+    sums_ref, active_ref, grad_y_ref, in_sems, out_sems = refs
+    get = fetch(FETCHED, far_refs, near_refs, in_sems)
+    sends = [
+        pltpu.make_async_copy(stage, out, out_sems.at[index])
+        for index, (stage, out) in enumerate(zip(stage_refs, out_refs))
     ]
-    for copy in copies:
-        copy.start()
-    w_out_ref, gate_ref, hat_ref, hat_scale_ref, qkv_ref, slope_ref, weight_ref = near_refs[:7]
-    mixed_ref, normed_ref, rows_slope_ref, rows_hat_ref, rows_scale_ref = near_refs[7:12]
-    place_ref, digits_ref, w_in_ref = near_refs[12:]
-    count, width = rows_hat_ref.shape
-    tokens = hat_ref.shape[0]
-    me = me_ref[0]
+    got_ref = get("got")
     for slot in range(got_ref.shape[0]):
         grad_y_ref[slot * SLOT : (slot + 1) * SLOT, :] = got_ref[dest_ref[slot]]
-    for copy in copies[:4]:
-        copy.wait()
+    w_out_ref = get("w_out")
+    tokens, width = grad_y_ref.shape
     gain_total = jnp.zeros((1, width), F32)
     for tile in range(tokens // TILE):
         rows = slice(tile * TILE, (tile + 1) * TILE)
         grad_mixed = dot(grad_y_ref[rows, :], w_out_ref[...], NT)
+        if tile == 0:
+            hat_ref, gate_ref, hat_scale_ref = get("hat"), get("gate"), get("hat_scale")
         hat = hat_ref[rows, :]
         active_ref[rows, :width] = (grad_mixed * hat * gain_out_ref[...]).astype(BF16)
         inner = grad_mixed * gate_ref[rows, :]
@@ -257,19 +288,15 @@
         along = jnp.mean(inner * hat, axis=-1, keepdims=True)
         grad_att = ((inner - mean - hat * along) * hat_scale_ref[rows, :]).astype(BF16)
         if tile == 0:
-            for copy in copies[4:7]:
-                copy.wait()
+            qkv_ref, slope_ref, weight_ref = get("qkv"), get("slope"), get("weight")
         for head in range(HEADS):
-            columns = slice(head * HDIM, (head + 1) * HDIM)
             vals, queries, keys = (
                 qkv_ref[rows, part * width + head * HDIM : part * width + (head + 1) * HDIM]
                 for part in range(3)
             )
-            grad_o = grad_att[:, columns]
+            grad_o = grad_att[:, head * HDIM : (head + 1) * HDIM]
             grad_weight = dot(grad_o, vals, NT)
-            grad_score = (grad_weight * slope_ref[tile * HEADS + head].astype(F32)).astype(
-                BF16
-            )
+            grad_score = (grad_weight * slope_ref[tile * HEADS + head].astype(F32)).astype(BF16)
             for part, value in (
                 (1, dot(weight_ref[tile * HEADS + head], grad_o, TN)),
                 (2, dot(grad_score, keys)),
@@ -277,46 +304,49 @@
             ):
                 first = part * width + head * HDIM
                 active_ref[rows, first : first + HDIM] = value.astype(BF16)
-    for copy in copies[7:]:
-        copy.wait()
-    grad_y = grad_y_ref[...]
-    sums_ref[:, 4 * width : 5 * width] = (dot(mixed_ref[...], grad_y, TN) * total_factor).astype(
-        BF16
-    )
-    sub = lax.broadcasted_iota(jnp.int32, (count, tokens), 0)
-    gather = jnp.where(sub == jnp.broadcast_to(item_ref[...], (count, tokens)), 1.0, 0.0)
-    gather = gather.astype(BF16)
+    mixed_ref = get("mixed")
+    sums_ref[:, :width] = (dot(mixed_ref[...], grad_y_ref[...], TN) * factor).astype(BF16)
+    normed_ref, rows_slope_ref, w_in_ref = get("normed"), get("rows_slope"), get("w_in")
+    count = normed_ref.shape[0]
+    gather = gather_of(item_ref, count)
     grad_normed = jnp.zeros((count, width), F32)
     for part in range(4):
         columns = slice(part * width, (part + 1) * width)
         summed = dot(gather, active_ref[:, columns])
         grad_hidden = (summed * rows_slope_ref[:, columns].astype(F32)).astype(BF16)
-        sums_ref[:, columns] = (dot(normed_ref[...], grad_hidden, TN) * total_factor).astype(BF16)
+        sums_ref[:, (part + 1) * width : (part + 2) * width] = (
+            dot(normed_ref[...], grad_hidden, TN) * factor
+        ).astype(BF16)
         grad_normed = grad_normed + dot(grad_hidden, w_in_ref[:, columns], NT)
+    rows_hat_ref, rows_scale_ref, place_ref, digits_ref = (get(name) for name in FETCHED[12:])
     hat = rows_hat_ref[...]
     gain_rows = jnp.concatenate(
         [jnp.sum(grad_normed * hat, axis=0, keepdims=True), gain_total]
         + [jnp.zeros((14, width), F32)],
         axis=0,
     )
-    gains = (gain_rows * total_factor).astype(BF16)
-    sums_ref[:, 5 * width : 5 * width + LANES] = dot(gains, unit(16), TN).astype(BF16)
-    if sums_ref.shape[1] > 5 * width + LANES:
-        rest = sums_ref.shape[1] - 5 * width - LANES
-        sums_ref[:, 5 * width + LANES :] = jnp.zeros((width, rest), BF16)
+    gains = (gain_rows * factor).astype(BF16)
+    end = 5 * width + LANES
+    sums_ref[:, 5 * width : end] = dot(gains, unit(16), TN).astype(BF16)
+    if sums_ref.shape[1] > end:
+        sums_ref[:, end:] = jnp.zeros((width, sums_ref.shape[1] - end), BF16)
+    plan.write(me_ref[0], sums_ref, stage_refs[1:])
+    for copy in sends[1:]:
+        copy.start()
     inner = grad_normed * gain_in_ref[...]
     mean = jnp.mean(inner, axis=-1, keepdims=True)
     along = jnp.mean(inner * hat, axis=-1, keepdims=True)
-    row_grad = (inner - mean - hat * along) * rows_scale_ref[...] + dot(gather, grad_y)
+    row_grad = (inner - mean - hat * along) * rows_scale_ref[...] + dot(gather, grad_y_ref[...])
+    table_ref = stage_refs[0]
     places = table_ref.shape[0]
-    place = place_ref[...]
     spots = lax.broadcasted_iota(jnp.int32, (places, count), 0)
-    spread = jnp.where(spots == jnp.broadcast_to(place, (places, count)), 1.0, 0.0).astype(BF16)
+    hit = spots == jnp.broadcast_to(place_ref[...], (places, count))
+    spread = jnp.where(hit, 1.0, 0.0).astype(BF16)
     table_ref[:, :width] = dot(spread, row_grad.astype(BF16)).astype(BF16)
     table_ref[:, width:] = dot(spread, digits_ref[...]).astype(BF16)
-    for place_now in range(plan.chunks):
-        out_ref = (keep_ref, give_ref)[place_now // (plan.chunks // 2)]
-        out_ref[place_now % (plan.chunks // 2)] = sums_ref[plan.chunk_at(me, place_now)]
+    sends[0].start()
+    for copy in sends:
+        copy.wait()
 
 
 def unit(rows):
@@ -332,30 +362,42 @@
         self.row_groups = min(self.chunks, width // CHUNK_ROWS)
         self.column_groups = self.chunks // self.row_groups
         block = self.column_groups * LANES
-        blocks = -(-(5 * width + LANES) // block)
-        self.columns = blocks * block
-        self.wide = blocks * LANES
+        self.wide = -(-(5 * width + LANES) // block) * LANES
+        self.split = -(-self.wide // (2 * LANES)) * LANES
+        self.sides = ((0, self.split), (self.split, self.wide - self.split))
         table_bits = [1 << bit for bit in range(1, table_size.bit_length() - 1)]
         dp_bits = [table_size << bit for bit in range(dp_size.bit_length() - 1)]
+        self.near_steps = len(table_bits) + 1
         self.orders = (table_bits + dp_bits, dp_bits[:1] + table_bits + dp_bits[1:])
-        self.steps = len(self.orders[0])
-
-    def low_mask(self, core, place):
+
+    def chunk_at(self, me, side, place):
+        order = [1] + self.orders[side]
         mask = 0
-        for step, bit in enumerate(self.orders[core]):
-            if place >> (self.steps - 1 - step) & 1:
+        for step, bit in enumerate(order):
+            if place >> (len(order) - 1 - step) & 1:
                 mask ^= bit
-        return mask
-
-    def chunk_at(self, me, place):
-        top, low = divmod(place, self.chunks // 2)
-        masks = [top ^ self.low_mask(core ^ top, low) for core in range(2)]
-        chunk = me ^ jnp.where((me & 1) == 0, masks[0], masks[1])
-        first = pl.multiple_of((chunk & (self.row_groups - 1)) * CHUNK_ROWS, CHUNK_ROWS)
+        chunk = me ^ mask
+        begin, size = self.sides[side]
+        first = (chunk & (self.row_groups - 1)) * CHUNK_ROWS
+        rows = pl.ds(pl.multiple_of(first, CHUNK_ROWS), CHUNK_ROWS)
         if self.column_groups == 1:
-            return pl.ds(first, CHUNK_ROWS), slice(0, self.wide)
+            return rows, slice(begin, begin + size)
         group = chunk >> (self.row_groups.bit_length() - 1)
-        return pl.ds(first, CHUNK_ROWS), pl.ds(pl.multiple_of(group * self.wide, LANES), self.wide)
+        return rows, pl.ds(pl.multiple_of(group * self.wide + begin, LANES), size)
+
+    def write(self, me, sums_ref, part_refs):
+        half = self.chunks // 2
+        for side in range(2):
+            for place in range(self.chunks):
+                out_ref = part_refs[2 * side + place // half]
+                out_ref[place % half] = sums_ref[self.chunk_at(me, side, place)]
+
+    def read(self, me, part_refs, sums_ref):
+        half = self.chunks // 2
+        for side in range(2):
+            for place in range(self.chunks):
+                in_ref = part_refs[2 * side + place // half]
+                sums_ref[self.chunk_at(me, side, place)] = in_ref[place % half]
 
 
 def table_body(got_ref, out_ref):
@@ -370,17 +412,13 @@
         out_ref[first : first + step, :] = dot(hit.astype(BF16), got_ref[:, :width])
 
 
-def widen_body(
-    plan, me_ref, own_ref, came_ref, w_in_ref, w_out_ref, gain_in_ref, gain_out_ref, sums_ref
-):
-    me = me_ref[0]
-    for place in range(plan.chunks):
-        in_ref = (own_ref, came_ref)[place // (plan.chunks // 2)]
-        sums_ref[plan.chunk_at(me, place)] = in_ref[place % (plan.chunks // 2)]
-    split, end = w_in_ref.shape[1], w_in_ref.shape[1] + w_out_ref.shape[1]
-    w_in_ref[...] = sums_ref[:, :split].astype(F32)
-    w_out_ref[...] = sums_ref[:, split:end].astype(F32)
-    gains = dot(unit(16), sums_ref[:, end : end + LANES], NT)
+def widen_body(plan, me_ref, *refs):
+    w_in_ref, w_out_ref, gain_in_ref, gain_out_ref, sums_ref = refs[4:]
+    plan.read(me_ref[0], refs[:4], sums_ref)
+    width = w_out_ref.shape[0]
+    w_out_ref[...] = sums_ref[:, :width].astype(F32)
+    w_in_ref[...] = sums_ref[:, width : 5 * width].astype(F32)
+    gains = dot(unit(16), sums_ref[:, 5 * width : 5 * width + LANES], NT)
     gain_in_ref[...] = gains[0:1]
     gain_out_ref[...] = gains[1:2]
 
@@ -412,9 +450,8 @@
     gain_in, gain_out = gain_in[None, :], gain_out[None, :]
     me = lax.axis_index(both).astype(jnp.int32)[None]
 
-    def swap(values, masks):
-        pairs = [(here, here ^ masks[here & 1]) for here in range(devices_all)]
-        return lax.ppermute(values, both, pairs)
+    def swap(values, mask):
+        return lax.ppermute(values, both, [(here, here ^ mask) for here in range(devices_all)])
 
     def exchange(values, axes):
         return lax.all_to_all(values, axes, split_axis=0, concat_axis=0, tiled=True)
@@ -450,54 +487,56 @@
         owner_row.reshape(count, 1),
     )
 
-    half = shape_of((devices_all // 2, CHUNK_ROWS, plan.wide), BF16)
-    table_send, kept, sent = call(
+    saved = dict(zip(SAVED, saved), w_in=w_in, w_out=w_out)
+    saved = dict(saved, got=got)
+    fetched = [saved[name] for name in FETCHED]
+    outs = [shape_of((devices_all * plan.capacity, width + LANES), BF16)]
+    for _, wide in plan.sides:
+        outs += [shape_of((devices_all // 2, CHUNK_ROWS, wide), BF16)] * 2
+    table_send, *parts = call(
         functools.partial(backward_body, plan, total_factor),
-        [shape_of((devices_all * plan.capacity, width + LANES), BF16), half, half],
-        [SMEM] * 2 + [VMEM] * 4 + [HBM] * (len(SAVED) + 2),
-        flops=4 * count * width * width * 20,
+        outs,
+        [SMEM] * 2 + [VMEM] * 3 + [HBM] * len(FETCHED),
+        flops=4 * count * width * width * 40,
         moved=12_000_000,
         mebibytes=58,
-        scratch=[pltpu.VMEM(w_out.shape, BF16)]
-        + held
+        out_space=HBM,
+        scratch=[pltpu.VMEM(item.shape, item.dtype) for item in fetched + outs]
         + [
-            pltpu.VMEM(w_in.shape, BF16),
-            pltpu.VMEM((width, plan.columns), BF16),
+            pltpu.VMEM((width, plan.column_groups * plan.wide), BF16),
             pltpu.VMEM((tokens, 4 * width), BF16),
             pltpu.VMEM((tokens, width), BF16),
-            pltpu.SemaphoreType.DMA((len(SAVED) + 2,)),
+            pltpu.SemaphoreType.DMA((len(FETCHED),)),
+            pltpu.SemaphoreType.DMA((len(outs),)),
         ],
-    )(
-        me,
-        seq_dest,
-        row_of_token.reshape(1, tokens),
-        gain_in,
-        gain_out,
-        got,
-        w_out,
-        *saved,
-        w_in,
-    )
-
-    kept = add(kept, swap(sent, (1, 1)))
+    )(me, seq_dest, row_of_token.reshape(1, tokens), gain_in, gain_out, *fetched)
+
+    def reduced(kept, mask):
+        middle = kept.shape[0] // 2
+        return add(kept[:middle], swap(kept[middle:], mask))
+
+    def gathered(kept, mask):
+        return jnp.concatenate([kept, swap(kept, mask)])
+
     table_got = exchange(table_send.reshape(devices_all, plan.capacity, width + LANES), both)
-    for step, masks in enumerate(zip(*plan.orders)):
-        if step == 2:
-            kept, table_got = lax.optimization_barrier((kept, table_got))
-        middle = kept.shape[0] // 2
-        came = swap(kept[middle:], masks)
-        kept = add(kept[:middle], came)
+    sides = [add(parts[2 * side], swap(parts[2 * side + 1], 1)) for side in range(2)]
+    for step in range(plan.near_steps):
+        sides = [reduced(sides[side], plan.orders[side][step]) for side in range(2)]
+    kept = jnp.concatenate(sides, axis=2)
+    kept, table_got = lax.optimization_barrier((kept, table_got))
     table_part = call(
         table_body,
         shape_of((ROWS_DEV, width), F32),
         [VMEM],
     )(table_got.reshape(devices_all * plan.capacity, width + LANES))
-    for step, masks in reversed(list(enumerate(zip(*plan.orders)))):
-        if step == 0:
-            kept, table_part = lax.optimization_barrier((kept, table_part))
-        kept = jnp.concatenate([kept, swap(kept, masks)])
-    came = swap(kept, (1, 1))
-
+    for mask in plan.orders[0][plan.near_steps :]:
+        kept = reduced(kept, mask)
+    for mask in reversed(plan.orders[0][plan.near_steps :]):
+        kept = gathered(kept, mask)
+    kept, table_part = lax.optimization_barrier((kept, table_part))
+    sides = [kept[..., : plan.split], kept[..., plan.split :]]
+    for step in reversed(range(plan.near_steps)):
+        sides = [gathered(sides[side], plan.orders[side][step]) for side in range(2)]
     grad_w_in, grad_w_out, grad_gain_in, grad_gain_out = call(
         functools.partial(widen_body, plan),
         (
@@ -506,9 +545,9 @@
             shape_of((1, width), F32),
             shape_of((1, width), F32),
         ),
-        [SMEM] + [VMEM] * 2,
-        scratch=[pltpu.VMEM((width, plan.columns), BF16)],
-    )(me, kept, came)
+        [SMEM] + [VMEM] * 4,
+        scratch=[pltpu.VMEM((width, plan.column_groups * plan.wide), BF16)],
+    )(me, sides[0], swap(sides[0], 1), sides[1], swap(sides[1], 1))
     return (table_part, grad_w_in, grad_w_out, grad_gain_in[0], grad_gain_out[0])
 
 

time: 131 us -> 124 us (0.947)
  waiting for transfers between devices: 68.6 us -> 51.6 us
  starting transfers between devices: 24.7 us -> 36.2 us
    ppermute x10 -> x16, waiting for transfers between devices: 60.4 us -> 43.4 us  [swap(): lax.ppermute(values, both, [(here, here ^ mask) for here in range(devices...]
    ppermute x10 -> x16, starting transfers between devices: 10.5 us -> 21.1 us  [swap(): lax.ppermute(values, both, [(here, here ^ mask) for here in range(devices...]
    convert_element_type x5 -> x8, other arithmetic: 2.03 us -> 0.64 us  [add(): return (left.astype(F32) + right.astype(F32)).astype(BF16)]
  transfers between devices with their start and end apart: 13 -> 19, of which waited for: 12 -> 13; matrix products, arithmetic and copies ran while one was open for 2% -> 3% of each run, Pallas kernels for 9% -> 9%
where the time goes in v8:
time: 124 us; the launch traced here: 123 us
  waiting for transfers between devices  51.6 us (42%)
  starting transfers between devices  36.2 us (29%)
  Pallas kernels  28 us (23%)
  local copies, waits for them, and re-layouts  4.95 us (4%)
  other arithmetic  1.65 us (1%)
    ppermute x16, waiting for transfers between devices, swap(): lax.ppermute(values, both, [(here, here ^ mask) for here in range(devices...  43.4 us
    ppermute x16, starting transfers between devices, swap(): lax.ppermute(values, both, [(here, here ^ mask) for here in range(devices...  21.1 us
    all_to_all x3, starting transfers between devices, exchange(): return lax.all_to_all(values, axes, split_axis=0, concat_axis=0, tiled=True)  15.1 us
    pallas_call x1, Pallas kernels, on_device(): call(functools.partial(backward_body, plan, total_factor), outs, [SMEM] *...  12.6 us
    pallas_call x1, Pallas kernels, on_device(): call(functools.partial(forward_body, plan.capacity), shapes, [VMEM] * 8,...  8.97 us
    all_to_all x3, waiting for transfers between devices, exchange(): return lax.all_to_all(values, axes, split_axis=0, concat_axis=0, tiled=True)  8.2 us
    pallas_call x1, Pallas kernels, on_device(): call(functools.partial(widen_body, plan), (shape_of(w_in.shape, F32), sha...  2.62 us
    unnamed x15, local copies, waits for them, and re-layouts  2.56 us
  transfers between devices with their start and end apart: 19, of which 13 were waited for; matrix products, arithmetic and copies ran while one was open for 3% of the time, Pallas kernels for 9%

profile of v8, /device:TPU:0, one launch (start us, length us, event | category | flops | bytes accessed | tf_op | source)
XLA Modules:
  0.0 123.3 jit_solution(1455514576432359253)
XLA Ops:
  0.7 0.7 multiply_add_fusion
  1.4 0.6 broadcast_in_dim.15
  2.0 7.3 %all-to-all-start = ((s32[8,1,8]{2,1,0:T(1,128)}), s32[8,1,8]{2,1,0:T(1,128)S(1)}, u32[]{:S(2)}, u32[]{:S(2)}) async-start(s32[8,1,8]{2,1,0:T(1,128)} %broadcast_in_dim.15), calls=%async_computation | async-start | bytes 8192 | tf_op jit(solution)/shard_map/all_to_all | solution.py:457
  9.2 6.4 %all-to-all-done.packed_ref = s32[8,1,8]{2,1,0:T(1,128)S(1)} async-done(((s32[8,1,8]{2,1,0:T(1,128)}), s32[8,1,8]{2,1,0:T(1,128)S(1)}, u32[]{:S(2)}, u32[]{:S(2)}) %all-to-all-start) | async-done | bytes 288 | tf_op jit(solution)/shard_map/all_to_all | solution.py:457
  15.6 0.9 copy-done
  16.5 1.6 %shard_map.146 = bf16[8,64,512]{2,1,0:T(8,128)(2,1)} custom-call(s32[1]{0:T(128)} %bitcast.me_ref, s32[8,1,8]{2,1,0:T(1,128)S(1)} %all-to-all-done.packed_ref, bf16[256,512]{1,0:T(8,128)(2,1)S(1)} %copy-done), custom_call_target="tpu_custom_call" | custom-call | tf_op jit(solution)/shard_map/pallas_call | solution.py:460
  18.1 3.5 %all-to-all-start.1 = ((bf16[8,64,512]{2,1,0:T(8,128)(2,1)}), bf16[8,64,512]{2,1,0:T(8,128)(2,1)S(1)}, u32[]{:S(2)}, u32[]{:S(2)}) async-start(bf16[8,64,512]{2,1,0:T(8,128)(2,1)} %shard_map.146), calls=%async_computation.1 | async-start | bytes 1048576 | tf_op jit(solution)/shard_map/all_to_all | solution.py:457
  21.6 0.8 copy.19.number_ref
  22.4 0.8 copy.18.owner_col_ref
  23.2 0.9 copy.17.item_ref
  24.1 9.0 %shard_map.147 = (f32[512,512]{1,0:T(8,128)}, f32[512,512]{1,0:T(8,128)}, f32[512,1]{1,0:T(8,128)}, bf16[512,1536]{1,0:T(8,128)(2,1)}, bf16[16,128,128]{2,1,0:T(...) custom-call(bf16[256,512]{1,0:T(8,128)(2,1)} %rows_ref.1, ...), custom_call_target="tpu_custom_call" | custom-call | flops 2147483648 | bytes 10000000 | tf_op jit(solution)/shard_map/pallas_call | solution.py:470
  33.1 1.8 %all-to-all-done.1.refs_0_ = bf16[8,64,512]{2,1,0:T(8,128)(2,1)S(1)} async-done(((bf16[8,64,512]{2,1,0:T(8,128)(2,1)}), bf16[8,64,512]{2,1,0:T(8,128)(2,1)S(1)}, u32[]{:S(2)}, u32[]{:S(2)}) %all-to-all-start.1) | async-done | bytes 524320 | tf_op jit(solution)/shard_map/all_to_all | solution.py:457
  34.9 0.8 copy-done.3
  35.7 12.6 %shard_map.148 = (bf16[512,640]{1,0:T(8,128)(2,1)}, bf16[16,16,1408]{2,1,0:T(8,128)(2,1)}, bf16[16,16,1408]{2,1,0:T(8,128)(2,1)}, bf16[16,16,1280]{2,1,0:T(8,128)(2,1)}, bf16[16,16,1280]{2,1,0:T(8,128)(2,1)}) custom-call(s32[1]{0:T(128)} %bitcast.me_ref, s32[8]{0:T(128)} %dest_ref.1, s32[1,512]{1,0:T(1,128)} %bitcast.13, f32[1,512]{1,0:T(1,128)} %bitcast.18, ...), custom_call_target="tpu_custom_call" | custom-call | flops 10737418240 | bytes 12000000 | tf_op jit(solution)/shard_map/pallas_call | solution.py:496
  48.4 0.5 collective-permute-start
  48.9 4.4 %all-to-all-start.2 = ((bf16[32,16,640]{2,1,0:T(8,128)(2,1)}), bf16[32,16,640]{2,1,0:T(8,128)(2,1)S(1)}, u32[]{:S(2)}, u32[]{:S(2)}) async-start(bf16[32,16,640]{2,1,0:T(8,128)(2,1)} %bitcast.12), calls=%async_computation.2 | async-start | bytes 1310720 | tf_op jit(solution)/shard_map/all_to_all | solution.py:457
  53.3 0.2 add_convert_fusion.1
  53.5 1.7 %collective-permute-start.4 = (bf16[8,16,1280]{2,1,0:T(8,128)(2,1)S(1)}, bf16[8,16,1280]{2,1,0:T(8,128)(2,1)S(1)}, u32[]{:S(2)}, u32[]{:S(2)}) collective-permute-start(bf16[8,16,1280]{2,1,0:T(8,128)(2,1)S(1)} %slice.61), channel_id=1, source_target_pairs={{0,4},{1,5},{2,6},{3,7},{4,0},{5,1},{6,2},{7,3},{8,12},{9,13},{10,... | collective-permute-start | bytes 983048 | tf_op jit(solution)/shard_map/ppermute | solution.py:454
  55.2 0.2 add_convert_fusion
  55.4 1.5 %collective-permute-start.1 = (bf16[8,16,1408]{2,1,0:T(8,128)(2,1)S(1)}, bf16[8,16,1408]{2,1,0:T(8,128)(2,1)S(1)}, u32[]{:S(2)}, u32[]{:S(2)}) collective-permute-start(bf16[8,16,1408]{2,1,0:T(8,128)(2,1)S(1)} %slice.57), channel_id=1, source_target_pairs={{0,2},{1,3},{2,0},{3,1},{4,6},{5,7},{6,4},{7,5},{8,10},{9,11},{10,... | collective-permute-start | bytes 1081352 | tf_op jit(solution)/shard_map/ppermute | solution.py:454
  56.9 12.6 %collective-permute-done.4 = bf16[8,16,1280]{2,1,0:T(8,128)(2,1)S(1)} collective-permute-done((bf16[8,16,1280]{2,1,0:T(8,128)(2,1)S(1)}, bf16[8,16,1280]{2,1,0:T(8,128)(2,1)S(1)}, u32[]{:S(2)}, u32[]{:S(2)}) %collective-permute-start.4) | collective-permute-done | bytes 327712 | tf_op jit(solution)/shard_map/ppermute | solution.py:454
  69.5 0.1 add_convert_fusion.3
  69.6 1.6 %collective-permute-start.5 = (bf16[4,16,1280]{2,1,0:T(8,128)(2,1)S(1)}, bf16[4,16,1280]{2,1,0:T(8,128)(2,1)S(1)}, u32[]{:S(2)}, u32[]{:S(2)}) collective-permute-start(bf16[4,16,1280]{2,1,0:T(8,128)(2,1)S(1)} %slice.63), channel_id=1, source_target_pairs={{0,2},{1,3},{2,0},{3,1},{4,6},{5,7},{6,4},{7,5},{8,10},{9,11},{10,... | collective-permute-start | bytes 491528 | tf_op jit(solution)/shard_map/ppermute | solution.py:454
  71.2 0.1 add_convert_fusion.2
  71.3 0.8 collective-permute-start.2
  72.1 3.1 %collective-permute-done.5 = bf16[4,16,1280]{2,1,0:T(8,128)(2,1)S(1)} collective-permute-done((bf16[4,16,1280]{2,1,0:T(8,128)(2,1)S(1)}, bf16[4,16,1280]{2,1,0:T(8,128)(2,1)S(1)}, u32[]{:S(2)}, u32[]{:S(2)}) %collective-permute-start.5) | collective-permute-done | bytes 163872 | tf_op jit(solution)/shard_map/ppermute | solution.py:454
  75.3 1.9 %collective-permute-done.2 = bf16[4,16,1408]{2,1,0:T(8,128)(2,1)S(1)} collective-permute-done((bf16[4,16,1408]{2,1,0:T(8,128)(2,1)S(1)}, bf16[4,16,1408]{2,1,0:T(8,128)(2,1)S(1)}, u32[]{:S(2)}, u32[]{:S(2)}) %collective-permute-start.2) | collective-permute-done | bytes 180256 | tf_op jit(solution)/shard_map/ppermute | solution.py:454
  77.3 1.7 %collective-permute-start.6 = (bf16[2,16,2688]{2,1,0:T(8,128)(2,1)S(1)}, bf16[2,16,2688]{2,1,0:T(8,128)(2,1)S(1)}, u32[]{:S(2)}, u32[]{:S(2)}) collective-permute-start(bf16[2,16,2688]{2,1,0:T(8,128)(2,1)S(1)} %slice.51), channel_id=1, source_target_pairs={{0,8},{1,9},{2,10},{3,11},{4,12},{5,13},{6,14},{7,15},{8,0},{9,1},... | collective-permute-start | bytes 516104 | tf_op jit(solution)/shard_map/ppermute | solution.py:454
  79.0 3.8 %collective-permute-done.6 = bf16[2,16,2688]{2,1,0:T(8,128)(2,1)S(1)} collective-permute-done((bf16[2,16,2688]{2,1,0:T(8,128)(2,1)S(1)}, bf16[2,16,2688]{2,1,0:T(8,128)(2,1)S(1)}, u32[]{:S(2)}, u32[]{:S(2)}) %collective-permute-start.6) | collective-permute-done | bytes 172064 | tf_op jit(solution)/shard_map/ppermute | solution.py:454
  82.9 3.0 %collective-permute-start.7 = (bf16[1,16,2688]{2,1,0:T(8,128)(2,1)S(1)}, bf16[1,16,2688]{2,1,0:T(8,128)(2,1)S(1)}, u32[]{:S(2)}, u32[]{:S(2)}) collective-permute-start(bf16[1,16,2688]{2,1,0:T(8,128)(2,1)S(1)} %slice.65), channel_id=1, source_target_pairs={{0,16},{1,17},{2,18},{3,19},{4,20},{5,21},{6,22},{7,23},{8,24},{9,... | collective-permute-start | bytes 258056 | tf_op jit(solution)/shard_map/ppermute | solution.py:454
  85.9 2.5 %collective-permute-done.7 = bf16[1,16,2688]{2,1,0:T(8,128)(2,1)S(1)} collective-permute-done((bf16[1,16,2688]{2,1,0:T(8,128)(2,1)S(1)}, bf16[1,16,2688]{2,1,0:T(8,128)(2,1)S(1)}, u32[]{:S(2)}, u32[]{:S(2)}) %collective-permute-start.7) | collective-permute-done | bytes 86048 | tf_op jit(solution)/shard_map/ppermute | solution.py:454
  88.4 3.1 %collective-permute-start.8 = (bf16[1,16,2688]{2,1,0:T(8,128)(2,1)S(1)}, bf16[1,16,2688]{2,1,0:T(8,128)(2,1)S(1)}, u32[]{:S(2)}, u32[]{:S(2)}) collective-permute-start(bf16[1,16,2688]{2,1,0:T(8,128)(2,1)S(1)} %add_convert_fusion.7), channel_id=1, source_target_pairs={{0,16},{1,17},{2,18},{3,19},{4,20},{5,21},{6,22},{7,23},{8,24},{9,... | collective-permute-start | bytes 258056 | tf_op jit(solution)/shard_map/ppermute | solution.py:454
  91.5 2.9 %collective-permute-done.8 = bf16[1,16,2688]{2,1,0:T(8,128)(2,1)S(1)} collective-permute-done((bf16[1,16,2688]{2,1,0:T(8,128)(2,1)S(1)}, bf16[1,16,2688]{2,1,0:T(8,128)(2,1)S(1)}, u32[]{:S(2)}, u32[]{:S(2)}) %collective-permute-start.8) | collective-permute-done | bytes 86048 | tf_op jit(solution)/shard_map/ppermute | solution.py:454
  94.4 4.5 %collective-permute-start.9 = (bf16[2,16,2688]{2,1,0:T(8,128)(2,1)S(1)}, bf16[2,16,2688]{2,1,0:T(8,128)(2,1)S(1)}, u32[]{:S(2)}, u32[]{:S(2)}) collective-permute-start(bf16[2,16,2688]{2,1,0:T(8,128)(2,1)S(1)} %pad_maximum_fusion.6), channel_id=1, source_target_pairs={{0,8},{1,9},{2,10},{3,11},{4,12},{5,13},{6,14},{7,15},{8,0},{9,1},... | collective-permute-start | bytes 516104 | tf_op jit(solution)/shard_map/ppermute | solution.py:454
  98.9 2.2 %shard_map.149 = f32[1024,512]{1,0:T(8,128)} custom-call(bf16[512,640]{1,0:T(8,128)(2,1)S(1)} %bitcast.11), custom_call_target="tpu_custom_call" | custom-call | tf_op jit(solution)/shard_map/pallas_call | solution.py:527
  101.0 1.2 collective-permute-done.9
  102.3 0.1 collective-permute-start.10
  102.4 1.1 collective-permute-start.13
  103.5 6.4 %collective-permute-done.10 = bf16[4,16,1408]{2,1,0:T(8,128)(2,1)S(1)} collective-permute-done((bf16[4,16,1408]{2,1,0:T(8,128)(2,1)S(1)}, bf16[4,16,1408]{2,1,0:T(8,128)(2,1)S(1)}, u32[]{:S(2)}, u32[]{:S(2)}) %collective-permute-start.10) | collective-permute-done | bytes 180256 | tf_op jit(solution)/shard_map/ppermute | solution.py:454
  109.9 0.6 collective-permute-start.11
  110.6 0.4 collective-permute-start.14
  111.0 6.4 %collective-permute-done.11 = bf16[8,16,1408]{2,1,0:T(8,128)(2,1)S(1)} collective-permute-done((bf16[8,16,1408]{2,1,0:T(8,128)(2,1)S(1)}, bf16[8,16,1408]{2,1,0:T(8,128)(2,1)S(1)}, u32[]{:S(2)}, u32[]{:S(2)}) %collective-permute-start.11) | collective-permute-done | bytes 360480 | tf_op jit(solution)/shard_map/ppermute | solution.py:454
  117.4 0.1 pad_maximum_fusion.refs_0_
  117.5 0.1 collective-permute-start.12
  117.6 0.1 collective-permute-done.14
  117.8 0.4 collective-permute-start.15
  118.2 2.5 %collective-permute-done.15.refs_3_ = bf16[16,16,1280]{2,1,0:T(8,128)(2,1)S(1)} collective-permute-done((bf16[16,16,1280]{2,1,0:T(8,128)(2,1)S(1)}, bf16[16,16,1280]{2,1,0:T(8,128)(2,1)S(1)}, u32[]{:S(2)}, u32[]{:S(2)}) %collective-permute-start.15) | collective-permute-done | bytes 655392 | tf_op jit(solution)/shard_map/ppermute | solution.py:454
  120.7 2.6 %shard_map.150 = (f32[512,2048]{1,0:T(8,128)}, f32[512,512]{1,0:T(8,128)}, f32[1,512]{1,0:T(1,128)}, f32[1,512]{1,0:T(1,128)}) custom-call(s32[1]{0:T(128)} %bitcast.me_ref, bf16[16,16,1408]{2,1,0:T(8,128)(2,1)S(1)} %pad_maximum_fusion.refs_0_, bf16[16,16,1408]{2,1,0:T(8,128)(2,1)S(1)} %collective-permute-done.12.refs_1_, ...), custom_call_target="tpu_custom_call" | custom-call | tf_op jit(solution)/shard_map/pallas_call | solution.py:540
  (37 shorter events, 0.6 us)
Async XLA Ops:
  0.6 21.0 %copy-start.5 = (s32[256]{0:T(256)S(1)}, s32[256]{0:T(256)}, u32[]{:S(2)}) copy-start(s32[256]{0:T(256)} %param.14) | copy-start | bytes 3076
  0.6 21.8 %copy-start.6 = (s32[256,1]{0,1:T(1,128)S(1)}, s32[256,1]{0,1:T(1,128)}, u32[]{:S(2)}) copy-start(s32[256,1]{0,1:T(1,128)} %param.13) | copy-start | bytes 3076
  0.7 22.6 %copy-start.4 = (s32[512]{0:T(512)S(1)}, s32[512]{0:T(512)}, u32[]{:S(2)}) copy-start(s32[512]{0:T(512)} %param.12) | copy-start | bytes 6148
  2.0 13.6 %all-to-all-start = ((s32[8,1,8]{2,1,0:T(1,128)}), s32[8,1,8]{2,1,0:T(1,128)S(1)}, u32[]{:S(2)}, u32[]{:S(2)}) async-start(s32[8,1,8]{2,1,0:T(1,128)} %broadcast_in_dim.15), calls=%async_computation | async-start | bytes 8192 | tf_op jit(solution)/shard_map/all_to_all | solution.py:457
  15.6 1.0 copy-start
  18.1 16.8 %all-to-all-start.1 = ((bf16[8,64,512]{2,1,0:T(8,128)(2,1)}), bf16[8,64,512]{2,1,0:T(8,128)(2,1)S(1)}, u32[]{:S(2)}, u32[]{:S(2)}) async-start(bf16[8,64,512]{2,1,0:T(8,128)(2,1)} %shard_map.146), calls=%async_computation.1 | async-start | bytes 1048576 | tf_op jit(solution)/shard_map/all_to_all | solution.py:457
  34.9 0.8 copy-start.3
  48.3 5.0 %copy-start.2 = (bf16[16,16,1280]{2,1,0:T(8,128)(2,1)S(1)}, bf16[16,16,1280]{2,1,0:T(8,128)(2,1)}, u32[]{:S(2)}) copy-start(bf16[16,16,1280]{2,1,0:T(8,128)(2,1)} %get-tuple-element.46) | copy-start | bytes 1966084
  48.3 5.0 %collective-permute-start.3 = (bf16[16,16,1280]{2,1,0:T(8,128)(2,1)}, bf16[16,16,1280]{2,1,0:T(8,128)(2,1)S(1)}, u32[]{:S(2)}, u32[]{:S(2)}) collective-permute-start(bf16[16,16,1280]{2,1,0:T(8,128)(2,1)} %get-tuple-element.47), channel_id=1, source_target_pairs={{0,1},{1,0},{2,3},{3,2},{4,5},{5,4},{6,7},{7,6},{8,9},{9,8},{10,11... | collective-permute-start | bytes 1966088 | tf_op jit(solution)/shard_map/ppermute | solution.py:454
  48.4 6.8 %collective-permute-start = (bf16[16,16,1408]{2,1,0:T(8,128)(2,1)}, bf16[16,16,1408]{2,1,0:T(8,128)(2,1)S(1)}, u32[]{:S(2)}, u32[]{:S(2)}) collective-permute-start(bf16[16,16,1408]{2,1,0:T(8,128)(2,1)} %get-tuple-element.45), channel_id=1, source_target_pairs={{0,1},{1,0},{2,3},{3,2},{4,5},{5,4},{6,7},{7,6},{8,9},{9,8},{10,11... | collective-permute-start | bytes 2162696 | tf_op jit(solution)/shard_map/ppermute | solution.py:454
  48.9 28.4 %all-to-all-start.2 = ((bf16[32,16,640]{2,1,0:T(8,128)(2,1)}), bf16[32,16,640]{2,1,0:T(8,128)(2,1)S(1)}, u32[]{:S(2)}, u32[]{:S(2)}) async-start(bf16[32,16,640]{2,1,0:T(8,128)(2,1)} %bitcast.12), calls=%async_computation.2 | async-start | bytes 1310720 | tf_op jit(solution)/shard_map/all_to_all | solution.py:457
  53.3 1.9 %copy-start.1 = (bf16[16,16,1408]{2,1,0:T(8,128)(2,1)S(1)}, bf16[16,16,1408]{2,1,0:T(8,128)(2,1)}, u32[]{:S(2)}) copy-start(bf16[16,16,1408]{2,1,0:T(8,128)(2,1)} %get-tuple-element.44) | copy-start | bytes 2162692
  53.5 16.0 %collective-permute-start.4 = (bf16[8,16,1280]{2,1,0:T(8,128)(2,1)S(1)}, bf16[8,16,1280]{2,1,0:T(8,128)(2,1)S(1)}, u32[]{:S(2)}, u32[]{:S(2)}) collective-permute-start(bf16[8,16,1280]{2,1,0:T(8,128)(2,1)S(1)} %slice.61), channel_id=1, source_target_pairs={{0,4},{1,5},{2,6},{3,7},{4,0},{5,1},{6,2},{7,3},{8,12},{9,13},{10,... | collective-permute-start | bytes 983048 | tf_op jit(solution)/shard_map/ppermute | solution.py:454
  55.4 15.8 %collective-permute-start.1 = (bf16[8,16,1408]{2,1,0:T(8,128)(2,1)S(1)}, bf16[8,16,1408]{2,1,0:T(8,128)(2,1)S(1)}, u32[]{:S(2)}, u32[]{:S(2)}) collective-permute-start(bf16[8,16,1408]{2,1,0:T(8,128)(2,1)S(1)} %slice.57), channel_id=1, source_target_pairs={{0,2},{1,3},{2,0},{3,1},{4,6},{5,7},{6,4},{7,5},{8,10},{9,11},{10,... | collective-permute-start | bytes 1081352 | tf_op jit(solution)/shard_map/ppermute | solution.py:454
  69.6 5.7 %collective-permute-start.5 = (bf16[4,16,1280]{2,1,0:T(8,128)(2,1)S(1)}, bf16[4,16,1280]{2,1,0:T(8,128)(2,1)S(1)}, u32[]{:S(2)}, u32[]{:S(2)}) collective-permute-start(bf16[4,16,1280]{2,1,0:T(8,128)(2,1)S(1)} %slice.63), channel_id=1, source_target_pairs={{0,2},{1,3},{2,0},{3,1},{4,6},{5,7},{6,4},{7,5},{8,10},{9,11},{10,... | collective-permute-start | bytes 491528 | tf_op jit(solution)/shard_map/ppermute | solution.py:454
  71.3 5.9 %collective-permute-start.2 = (bf16[4,16,1408]{2,1,0:T(8,128)(2,1)S(1)}, bf16[4,16,1408]{2,1,0:T(8,128)(2,1)S(1)}, u32[]{:S(2)}, u32[]{:S(2)}) collective-permute-start(bf16[4,16,1408]{2,1,0:T(8,128)(2,1)S(1)} %slice.59), channel_id=1, source_target_pairs={{0,4},{1,5},{2,6},{3,7},{4,0},{5,1},{6,2},{7,3},{8,12},{9,13},{10,... | collective-permute-start | bytes 540680 | tf_op jit(solution)/shard_map/ppermute | solution.py:454
  77.3 5.5 %collective-permute-start.6 = (bf16[2,16,2688]{2,1,0:T(8,128)(2,1)S(1)}, bf16[2,16,2688]{2,1,0:T(8,128)(2,1)S(1)}, u32[]{:S(2)}, u32[]{:S(2)}) collective-permute-start(bf16[2,16,2688]{2,1,0:T(8,128)(2,1)S(1)} %slice.51), channel_id=1, source_target_pairs={{0,8},{1,9},{2,10},{3,11},{4,12},{5,13},{6,14},{7,15},{8,0},{9,1},... | collective-permute-start | bytes 516104 | tf_op jit(solution)/shard_map/ppermute | solution.py:454
  82.9 5.4 %collective-permute-start.7 = (bf16[1,16,2688]{2,1,0:T(8,128)(2,1)S(1)}, bf16[1,16,2688]{2,1,0:T(8,128)(2,1)S(1)}, u32[]{:S(2)}, u32[]{:S(2)}) collective-permute-start(bf16[1,16,2688]{2,1,0:T(8,128)(2,1)S(1)} %slice.65), channel_id=1, source_target_pairs={{0,16},{1,17},{2,18},{3,19},{4,20},{5,21},{6,22},{7,23},{8,24},{9,... | collective-permute-start | bytes 258056 | tf_op jit(solution)/shard_map/ppermute | solution.py:454
  88.4 6.0 %collective-permute-start.8 = (bf16[1,16,2688]{2,1,0:T(8,128)(2,1)S(1)}, bf16[1,16,2688]{2,1,0:T(8,128)(2,1)S(1)}, u32[]{:S(2)}, u32[]{:S(2)}) collective-permute-start(bf16[1,16,2688]{2,1,0:T(8,128)(2,1)S(1)} %add_convert_fusion.7), channel_id=1, source_target_pairs={{0,16},{1,17},{2,18},{3,19},{4,20},{5,21},{6,22},{7,23},{8,24},{9,... | collective-permute-start | bytes 258056 | tf_op jit(solution)/shard_map/ppermute | solution.py:454
  94.4 7.8 %collective-permute-start.9 = (bf16[2,16,2688]{2,1,0:T(8,128)(2,1)S(1)}, bf16[2,16,2688]{2,1,0:T(8,128)(2,1)S(1)}, u32[]{:S(2)}, u32[]{:S(2)}) collective-permute-start(bf16[2,16,2688]{2,1,0:T(8,128)(2,1)S(1)} %pad_maximum_fusion.6), channel_id=1, source_target_pairs={{0,8},{1,9},{2,10},{3,11},{4,12},{5,13},{6,14},{7,15},{8,0},{9,1},... | collective-permute-start | bytes 516104 | tf_op jit(solution)/shard_map/ppermute | solution.py:454
  102.3 7.5 %collective-permute-start.10 = (bf16[4,16,1408]{2,1,0:T(8,128)(2,1)S(1)}, bf16[4,16,1408]{2,1,0:T(8,128)(2,1)S(1)}, u32[]{:S(2)}, u32[]{:S(2)}) collective-permute-start(bf16[4,16,1408]{2,1,0:T(8,128)(2,1)S(1)} %slice.54), channel_id=1, source_target_pairs={{0,4},{1,5},{2,6},{3,7},{4,0},{5,1},{6,2},{7,3},{8,12},{9,13},{10,... | collective-permute-start | bytes 540680 | tf_op jit(solution)/shard_map/ppermute | solution.py:454
  102.4 8.1 %collective-permute-start.13 = (bf16[4,16,1280]{2,1,0:T(8,128)(2,1)S(1)}, bf16[4,16,1280]{2,1,0:T(8,128)(2,1)S(1)}, u32[]{:S(2)}, u32[]{:S(2)}) collective-permute-start(bf16[4,16,1280]{2,1,0:T(8,128)(2,1)S(1)} %slice.55), channel_id=1, source_target_pairs={{0,2},{1,3},{2,0},{3,1},{4,6},{5,7},{6,4},{7,5},{8,10},{9,11},{10,... | collective-permute-start | bytes 491528 | tf_op jit(solution)/shard_map/ppermute | solution.py:454
  109.9 7.5 %collective-permute-start.11 = (bf16[8,16,1408]{2,1,0:T(8,128)(2,1)S(1)}, bf16[8,16,1408]{2,1,0:T(8,128)(2,1)S(1)}, u32[]{:S(2)}, u32[]{:S(2)}) collective-permute-start(bf16[8,16,1408]{2,1,0:T(8,128)(2,1)S(1)} %pad_maximum_fusion.2), channel_id=1, source_target_pairs={{0,2},{1,3},{2,0},{3,1},{4,6},{5,7},{6,4},{7,5},{8,10},{9,11},{10,... | collective-permute-start | bytes 1081352 | tf_op jit(solution)/shard_map/ppermute | solution.py:454
  110.6 7.1 %collective-permute-start.14 = (bf16[8,16,1280]{2,1,0:T(8,128)(2,1)S(1)}, bf16[8,16,1280]{2,1,0:T(8,128)(2,1)S(1)}, u32[]{:S(2)}, u32[]{:S(2)}) collective-permute-start(bf16[8,16,1280]{2,1,0:T(8,128)(2,1)S(1)} %pad_maximum_fusion.5), channel_id=1, source_target_pairs={{0,4},{1,5},{2,6},{3,7},{4,0},{5,1},{6,2},{7,3},{8,12},{9,13},{10,... | collective-permute-start | bytes 983048 | tf_op jit(solution)/shard_map/ppermute | solution.py:454
  117.5 3.2 %collective-permute-start.12 = (bf16[16,16,1408]{2,1,0:T(8,128)(2,1)S(1)}, bf16[16,16,1408]{2,1,0:T(8,128)(2,1)S(1)}, u32[]{:S(2)}, u32[]{:S(2)}) collective-permute-start(bf16[16,16,1408]{2,1,0:T(8,128)(2,1)S(1)} %pad_maximum_fusion.refs_0_), channel_id=1, source_target_pairs={{0,1},{1,0},{2,3},{3,2},{4,5},{5,4},{6,7},{7,6},{8,9},{9,8},{10,11... | collective-permute-start | bytes 2162696 | tf_op jit(solution)/shard_map/ppermute | solution.py:454
  117.8 2.9 %collective-permute-start.15 = (bf16[16,16,1280]{2,1,0:T(8,128)(2,1)S(1)}, bf16[16,16,1280]{2,1,0:T(8,128)(2,1)S(1)}, u32[]{:S(2)}, u32[]{:S(2)}) collective-permute-start(bf16[16,16,1280]{2,1,0:T(8,128)(2,1)S(1)} %pad_maximum_fusion.1.refs_2_), channel_id=1, source_target_pairs={{0,1},{1,0},{2,3},{3,2},{4,5},{5,4},{6,7},{7,6},{8,9},{9,8},{10,11... | collective-permute-start | bytes 1966088 | tf_op jit(solution)/shard_map/ppermute | solution.py:454

commit v9 on v8

--- a/solution.py
+++ b/solution.py
@@ -17,12 +17,14 @@
 TILE = 2 * SLOT
 LANES = 128
 CHUNK_ROWS = 16
+GAIN_AT = 64
 EPSILON = 1e-05
 F32 = jnp.float32
 BF16 = jnp.bfloat16
 VMEM = pl.BlockSpec(memory_space=pltpu.VMEM)
 SMEM = pl.BlockSpec(memory_space=pltpu.SMEM)
 HBM = pl.BlockSpec(memory_space=pltpu.HBM)
+ANY = pl.BlockSpec(memory_space=pl.ANY)
 
 
 def call(body, out_shape, in_specs, flops=0, moved=0, scratch=(), out_space=VMEM, mebibytes=24):
@@ -54,26 +56,26 @@
 TN = ((0,), (0,))
 
 
-def send_body(table_size, me_ref, packed_ref, grad_ref, out_ref):
+def send_body(lengths_ref, grad_ref, out_ref, sems):
     peers = out_ref.shape[0]
     blocks = grad_ref.shape[0] // BLK
-    me = me_ref[0] // table_size
     begin = jnp.int32(0)
+    copies = []
     for peer in range(peers):
-
-        def find(slot, length, peer=peer):
-            entry = packed_ref[peer, 0, slot]
-            return length + jnp.where(entry >> 3 == me, entry & 7, 0)
-
-        length = lax.fori_loop(0, peers, find, jnp.int32(0), unroll=True)
         for inner in range(LMAXB):
             block = jnp.minimum(begin + inner, blocks - 1)
-            rows = grad_ref[pl.ds(pl.multiple_of(block * BLK, BLK), BLK), :]
-            live = jnp.full(rows.shape, inner, jnp.int32) < length
-            out_ref[peer, inner * BLK : (inner + 1) * BLK, :] = jnp.where(
-                live, rows.astype(F32), 0.0
-            ).astype(BF16)
-        begin = begin + length
+            copies.append(
+                pltpu.make_async_copy(
+                    grad_ref.at[pl.ds(pl.multiple_of(block * BLK, BLK), BLK)],
+                    out_ref.at[peer, pl.ds(inner * BLK, BLK)],
+                    sems.at[peer, inner],
+                )
+            )
+            copies[-1].start()
+        for slot in range(peers):
+            begin = begin + lengths_ref[peer, 0, slot]
+    for copy in copies:
+        copy.wait()
 
 
 def tile_mask():
@@ -88,9 +90,10 @@
     "hat_scale",
     "qkv",
     "slope",
-    "weight",
-    "mixed",
-    "normed",
+    "slope_t",
+    "weight_t",
+    "mixed_t",
+    "normed_t",
     "rows_slope",
     "rows_hat",
     "rows_scale",
@@ -107,9 +110,10 @@
         hat_scale=shape_of((tokens, 1), F32),
         qkv=shape_of((tokens, 3 * width), BF16),
         slope=shape_of((pairs, TILE, TILE), BF16),
-        weight=shape_of((pairs, TILE, TILE), BF16),
-        mixed=shape_of((tokens, width), BF16),
-        normed=shape_of((count, width), BF16),
+        slope_t=shape_of((pairs, TILE, TILE), BF16),
+        weight_t=shape_of((pairs, TILE, TILE), BF16),
+        mixed_t=shape_of((width, tokens), BF16),
+        normed_t=shape_of((width, count), BF16),
         rows_slope=shape_of((count, 4 * width), BF16),
         rows_hat=shape_of((count, width), F32),
         rows_scale=shape_of((count, 1), F32),
@@ -137,12 +141,11 @@
         name: pltpu.make_async_copy(held[name], refs[index], sems.at[index])
         for index, name in enumerate(SAVED)
     }
-    gate_ref, hat_ref, hat_scale_ref, qkv_ref, slope_ref, weight_ref, mixed_ref = (
-        held[name] for name in SAVED[:7]
+    gate_ref, hat_ref, hat_scale_ref, qkv_ref, slope_ref, slope_t_ref = (
+        held[name] for name in SAVED[:6]
     )
-    normed_ref, rows_slope_ref, rows_hat_ref, rows_scale_ref, place_ref, digits_ref = (
-        held[name] for name in SAVED[7:]
-    )
+    weight_t_ref, mixed_t_ref, normed_t_ref, rows_slope_ref = (held[name] for name in SAVED[6:10])
+    rows_hat_ref, rows_scale_ref, place_ref, digits_ref = (held[name] for name in SAVED[10:])
     count, width = rows_ref.shape
     tokens = item_ref.shape[0]
     across = jnp.broadcast_to(owner_row_ref[...], (count, count))
@@ -164,9 +167,10 @@
     hat = shifted * scale
     rows_hat_ref[...] = hat
     rows_scale_ref[...] = scale
-    normed = (hat * gain_in_ref[...]).astype(BF16)
-    normed_ref[...] = normed
-    for name in ("rows_hat", "rows_scale", "normed"):
+    normed = hat * gain_in_ref[...]
+    normed_t_ref[...] = normed.T.astype(BF16)
+    normed = normed.astype(BF16)
+    for name in ("rows_hat", "rows_scale", "normed_t"):
         copies[name].start()
     lane = lax.broadcasted_iota(jnp.int32, (tokens, count), 1)
     pick = jnp.where(lane == jnp.broadcast_to(item_ref[...], (tokens, count)), 1.0, 0.0)
@@ -200,19 +204,22 @@
             )
             score = dot(queries, keys, NT) * factor
             sigma = sigmoid(score)
-            weight = jnp.where(mask, score * sigma, 0.0).astype(BF16)
+            weight = jnp.where(mask, score * sigma, 0.0)
             slope = sigma * (1.0 + score * (1.0 - sigma)) * factor
-            slope_ref[tile * HEADS + head] = jnp.where(mask, slope, 0.0).astype(BF16)
-            weight_ref[tile * HEADS + head] = weight
-            parts.append(dot(weight, vals))
+            slope = jnp.where(mask, slope, 0.0)
+            slope_ref[tile * HEADS + head] = slope.astype(BF16)
+            slope_t_ref[tile * HEADS + head] = slope.T.astype(BF16)
+            weight_t_ref[tile * HEADS + head] = weight.T.astype(BF16)
+            parts.append(dot(weight.astype(BF16), vals))
         attended = jnp.concatenate(parts, axis=1)
         shifted = attended - jnp.mean(attended, axis=-1, keepdims=True)
         scale = lax.rsqrt(jnp.mean(shifted * shifted, axis=-1, keepdims=True) + EPSILON)
         hat = shifted * scale
         hat_ref[rows, :] = hat
         hat_scale_ref[rows, :] = scale
-        mixed_ref[rows, :] = (hat * gain_out_ref[...] * gate_ref[rows, :]).astype(BF16)
-    for name in ("hat", "hat_scale", "slope", "weight", "mixed"):
+        mixed = hat * gain_out_ref[...] * gate_ref[rows, :]
+        mixed_t_ref[:, rows] = mixed.T.astype(BF16)
+    for name in ("hat", "hat_scale", "slope", "slope_t", "weight_t", "mixed_t"):
         copies[name].start()
     for copy in copies.values():
         copy.wait()
@@ -246,9 +253,10 @@
     "hat_scale",
     "qkv",
     "slope",
-    "weight",
-    "mixed",
-    "normed",
+    "slope_t",
+    "weight_t",
+    "mixed_t",
+    "normed_t",
     "rows_slope",
     "w_in",
     "rows_hat",
@@ -258,7 +266,9 @@
 )
 
 
-def backward_body(plan, factor, me_ref, dest_ref, item_ref, gain_in_ref, gain_out_ref, *refs):
+def backward_body(
+    plan, factor, me_ref, dest_ref, blocks_ref, item_ref, gain_in_ref, gain_out_ref, *refs
+):
     size = len(FETCHED)
     far_refs, out_refs, refs = refs[:size], refs[size : size + 5], refs[size + 5 :]
     near_refs, stage_refs, refs = refs[:size], refs[size : size + 5], refs[size + 5 :]
@@ -270,7 +280,10 @@
     ]
     got_ref = get("got")
     for slot in range(got_ref.shape[0]):
-        grad_y_ref[slot * SLOT : (slot + 1) * SLOT, :] = got_ref[dest_ref[slot]]
+        rows = got_ref[dest_ref[slot]]
+        live = lax.broadcasted_iota(jnp.int32, rows.shape, 0) < blocks_ref[slot] * BLK
+        rows = jnp.where(live, rows.astype(F32), 0.0).astype(BF16)
+        grad_y_ref[slot * SLOT : (slot + 1) * SLOT, :] = rows
     w_out_ref = get("w_out")
     tokens, width = grad_y_ref.shape
     gain_total = jnp.zeros((1, width), F32)
@@ -288,7 +301,7 @@
         along = jnp.mean(inner * hat, axis=-1, keepdims=True)
         grad_att = ((inner - mean - hat * along) * hat_scale_ref[rows, :]).astype(BF16)
         if tile == 0:
-            qkv_ref, slope_ref, weight_ref = get("qkv"), get("slope"), get("weight")
+            qkv_ref, slope_ref, slope_t_ref, weight_t_ref = (get(name) for name in FETCHED[5:9])
         for head in range(HEADS):
             vals, queries, keys = (
                 qkv_ref[rows, part * width + head * HDIM : part * width + (head + 1) * HDIM]
@@ -297,17 +310,19 @@
             grad_o = grad_att[:, head * HDIM : (head + 1) * HDIM]
             grad_weight = dot(grad_o, vals, NT)
             grad_score = (grad_weight * slope_ref[tile * HEADS + head].astype(F32)).astype(BF16)
+            weight_t = dot(vals, grad_o, NT)
+            score_t = (weight_t * slope_t_ref[tile * HEADS + head].astype(F32)).astype(BF16)
             for part, value in (
-                (1, dot(weight_ref[tile * HEADS + head], grad_o, TN)),
+                (1, dot(weight_t_ref[tile * HEADS + head], grad_o)),
                 (2, dot(grad_score, keys)),
-                (3, dot(grad_score, queries, TN)),
+                (3, dot(score_t, queries)),
             ):
                 first = part * width + head * HDIM
                 active_ref[rows, first : first + HDIM] = value.astype(BF16)
-    mixed_ref = get("mixed")
-    sums_ref[:, :width] = (dot(mixed_ref[...], grad_y_ref[...], TN) * factor).astype(BF16)
-    normed_ref, rows_slope_ref, w_in_ref = get("normed"), get("rows_slope"), get("w_in")
-    count = normed_ref.shape[0]
+    mixed_t_ref = get("mixed_t")
+    sums_ref[:, :width] = (dot(mixed_t_ref[...], grad_y_ref[...]) * factor).astype(BF16)
+    normed_t_ref, rows_slope_ref, w_in_ref = get("normed_t"), get("rows_slope"), get("w_in")
+    count = normed_t_ref.shape[1]
     gather = gather_of(item_ref, count)
     grad_normed = jnp.zeros((count, width), F32)
     for part in range(4):
@@ -315,21 +330,12 @@
         summed = dot(gather, active_ref[:, columns])
         grad_hidden = (summed * rows_slope_ref[:, columns].astype(F32)).astype(BF16)
         sums_ref[:, (part + 1) * width : (part + 2) * width] = (
-            dot(normed_ref[...], grad_hidden, TN) * factor
+            dot(normed_t_ref[...], grad_hidden) * factor
         ).astype(BF16)
         grad_normed = grad_normed + dot(grad_hidden, w_in_ref[:, columns], NT)
-    rows_hat_ref, rows_scale_ref, place_ref, digits_ref = (get(name) for name in FETCHED[12:])
+    rows_hat_ref, rows_scale_ref, place_ref, digits_ref = (get(name) for name in FETCHED[13:])
     hat = rows_hat_ref[...]
-    gain_rows = jnp.concatenate(
-        [jnp.sum(grad_normed * hat, axis=0, keepdims=True), gain_total]
-        + [jnp.zeros((14, width), F32)],
-        axis=0,
-    )
-    gains = (gain_rows * factor).astype(BF16)
-    end = 5 * width + LANES
-    sums_ref[:, 5 * width : end] = dot(gains, unit(16), TN).astype(BF16)
-    if sums_ref.shape[1] > end:
-        sums_ref[:, end:] = jnp.zeros((width, sums_ref.shape[1] - end), BF16)
+    gains = (jnp.sum(grad_normed * hat, axis=0, keepdims=True) * factor, gain_total * factor)
     plan.write(me_ref[0], sums_ref, stage_refs[1:])
     for copy in sends[1:]:
         copy.start()
@@ -343,16 +349,23 @@
     hit = spots == jnp.broadcast_to(place_ref[...], (places, count))
     spread = jnp.where(hit, 1.0, 0.0).astype(BF16)
     table_ref[:, :width] = dot(spread, row_grad.astype(BF16)).astype(BF16)
-    table_ref[:, width:] = dot(spread, digits_ref[...]).astype(BF16)
+    extra = plan.extra
+    lanes = []
+    for row in range(plan.capacity):
+        first = row * plan.gain_lanes
+        gain = gains[first // width][:, first % width : first % width + plan.gain_lanes]
+        rest = extra - GAIN_AT - plan.gain_lanes
+        row_parts = [jnp.zeros((1, GAIN_AT), F32), gain]
+        lanes.append(jnp.concatenate(row_parts + [jnp.zeros((1, rest), F32)] * (rest > 0), axis=1))
+    lanes = jnp.concatenate(lanes, axis=0).astype(BF16)
+    repeat = lax.broadcasted_iota(jnp.int32, (places, plan.capacity), 0) % plan.capacity
+    lane = lax.broadcasted_iota(jnp.int32, (places, plan.capacity), 1)
+    repeat = jnp.where(repeat == lane, 1.0, 0.0).astype(BF16)
+    table_ref[:, width:] = dot(repeat, lanes).astype(BF16)
+    table_ref[:, width : width + LANES] += dot(spread, digits_ref[...]).astype(BF16)
     sends[0].start()
     for copy in sends:
         copy.wait()
-
-
-def unit(rows):
-    sub = lax.broadcasted_iota(jnp.int32, (rows, LANES), 0)
-    lane = lax.broadcasted_iota(jnp.int32, (rows, LANES), 1)
-    return jnp.where(sub == lane, 1.0, 0.0).astype(BF16)
 
 
 class Plan:
@@ -362,7 +375,9 @@
         self.row_groups = min(self.chunks, width // CHUNK_ROWS)
         self.column_groups = self.chunks // self.row_groups
         block = self.column_groups * LANES
-        self.wide = -(-(5 * width + LANES) // block) * LANES
+        self.wide = -(-5 * width // block) * LANES
+        self.gain_lanes = 2 * width // self.capacity
+        self.extra = -(-(GAIN_AT + self.gain_lanes) // LANES) * LANES
         self.split = -(-self.wide // (2 * LANES)) * LANES
         self.sides = ((0, self.split), (self.split, self.wide - self.split))
         table_bits = [1 << bit for bit in range(1, table_size.bit_length() - 1)]
@@ -400,27 +415,33 @@
                 sums_ref[self.chunk_at(me, side, place)] = in_ref[place % half]
 
 
-def table_body(got_ref, out_ref):
+def table_body(plan, got_ref, out_ref, gain_in_ref, gain_out_ref):
     places, width = got_ref.shape[0], out_ref.shape[1]
     lane = lax.broadcasted_iota(jnp.int32, (16, LANES), 1)
     scale = jnp.where(lane == 0, 32.0, jnp.where(lane == 1, 1.0, 0.0)).astype(BF16)
-    numbers = dot(scale, got_ref[:, width:], NT)[0:1].astype(jnp.int32)
+    numbers = dot(scale, got_ref[:, width : width + LANES], NT)[0:1].astype(jnp.int32)
     step = 256
     for first in range(0, out_ref.shape[0], step):
         sub = lax.broadcasted_iota(jnp.int32, (step, places), 0) + first
         hit = jnp.where(sub == jnp.broadcast_to(numbers, (step, places)), 1.0, 0.0)
         out_ref[first : first + step, :] = dot(hit.astype(BF16), got_ref[:, :width])
+    sub = lax.broadcasted_iota(jnp.int32, (16, places), 0)
+    lane = lax.broadcasted_iota(jnp.int32, (16, places), 1) % plan.capacity
+    total = dot(jnp.where(sub == lane, 1.0, 0.0).astype(BF16), got_ref[:, width:])
+    for row in range(plan.capacity):
+        first = row * plan.gain_lanes
+        gain_ref = (gain_in_ref, gain_out_ref)[first // width]
+        gain_ref[:, first % width : first % width + plan.gain_lanes] = total[
+            row : row + 1, GAIN_AT : GAIN_AT + plan.gain_lanes
+        ]
 
 
 def widen_body(plan, me_ref, *refs):
-    w_in_ref, w_out_ref, gain_in_ref, gain_out_ref, sums_ref = refs[4:]
+    w_in_ref, w_out_ref, sums_ref = refs[4:]
     plan.read(me_ref[0], refs[:4], sums_ref)
     width = w_out_ref.shape[0]
     w_out_ref[...] = sums_ref[:, :width].astype(F32)
     w_in_ref[...] = sums_ref[:, width : 5 * width].astype(F32)
-    gains = dot(unit(16), sums_ref[:, 5 * width : 5 * width + LANES], NT)
-    gain_in_ref[...] = gains[0:1]
-    gain_out_ref[...] = gains[1:2]
 
 
 def add(left, right):
@@ -456,12 +477,16 @@
     def exchange(values, axes):
         return lax.all_to_all(values, axes, split_axis=0, concat_axis=0, tiled=True)
 
-    packed = jnp.broadcast_to(seq_dest * 8 + seq_blocks, (dp_size, 1, dp_size))
+    peers = jnp.arange(dp_size, dtype=jnp.int32)[:, None, None]
+    lengths = jnp.where(seq_dest[None, None, :] == peers, seq_blocks[None, None, :], 0)
     send = call(
-        functools.partial(send_body, table_size),
+        send_body,
         shape_of((dp_size, SLOT, width), BF16),
-        [SMEM] * 2 + [VMEM],
-    )(me, exchange(packed, "dp"), grad_out)
+        [SMEM, HBM],
+        mebibytes=58,
+        out_space=HBM,
+        scratch=[pltpu.SemaphoreType.DMA((dp_size, LMAXB))],
+    )(exchange(lengths, "dp"), grad_out)
     got = exchange(send, "dp")
 
     shapes = saved_shapes(tokens, count, width)
@@ -490,13 +515,13 @@
     saved = dict(zip(SAVED, saved), w_in=w_in, w_out=w_out)
     saved = dict(saved, got=got)
     fetched = [saved[name] for name in FETCHED]
-    outs = [shape_of((devices_all * plan.capacity, width + LANES), BF16)]
+    outs = [shape_of((devices_all * plan.capacity, width + plan.extra), BF16)]
     for _, wide in plan.sides:
         outs += [shape_of((devices_all // 2, CHUNK_ROWS, wide), BF16)] * 2
     table_send, *parts = call(
         functools.partial(backward_body, plan, total_factor),
         outs,
-        [SMEM] * 2 + [VMEM] * 3 + [HBM] * len(FETCHED),
+        [SMEM] * 3 + [VMEM] * 3 + [ANY] + [HBM] * (len(FETCHED) - 1),
         flops=4 * count * width * width * 40,
         moved=12_000_000,
         mebibytes=58,
@@ -509,7 +534,7 @@
             pltpu.SemaphoreType.DMA((len(FETCHED),)),
             pltpu.SemaphoreType.DMA((len(outs),)),
         ],
-    )(me, seq_dest, row_of_token.reshape(1, tokens), gain_in, gain_out, *fetched)
+    )(me, seq_dest, seq_blocks, row_of_token.reshape(1, tokens), gain_in, gain_out, *fetched)
 
     def reduced(kept, mask):
         middle = kept.shape[0] // 2
@@ -518,17 +543,22 @@
     def gathered(kept, mask):
         return jnp.concatenate([kept, swap(kept, mask)])
 
-    table_got = exchange(table_send.reshape(devices_all, plan.capacity, width + LANES), both)
     sides = [add(parts[2 * side], swap(parts[2 * side + 1], 1)) for side in range(2)]
+    *sides, table_send = lax.optimization_barrier((*sides, table_send))
+    table_got = exchange(table_send.reshape(devices_all, plan.capacity, -1), both)
     for step in range(plan.near_steps):
         sides = [reduced(sides[side], plan.orders[side][step]) for side in range(2)]
     kept = jnp.concatenate(sides, axis=2)
     kept, table_got = lax.optimization_barrier((kept, table_got))
-    table_part = call(
-        table_body,
-        shape_of((ROWS_DEV, width), F32),
+    table_part, grad_gain_in, grad_gain_out = call(
+        functools.partial(table_body, plan),
+        (
+            shape_of((ROWS_DEV, width), F32),
+            shape_of((1, width), F32),
+            shape_of((1, width), F32),
+        ),
         [VMEM],
-    )(table_got.reshape(devices_all * plan.capacity, width + LANES))
+    )(table_got.reshape(devices_all * plan.capacity, -1))
     for mask in plan.orders[0][plan.near_steps :]:
         kept = reduced(kept, mask)
     for mask in reversed(plan.orders[0][plan.near_steps :]):
@@ -537,14 +567,9 @@
     sides = [kept[..., : plan.split], kept[..., plan.split :]]
     for step in reversed(range(plan.near_steps)):
         sides = [gathered(sides[side], plan.orders[side][step]) for side in range(2)]
-    grad_w_in, grad_w_out, grad_gain_in, grad_gain_out = call(
+    grad_w_in, grad_w_out = call(
         functools.partial(widen_body, plan),
-        (
-            shape_of(w_in.shape, F32),
-            shape_of(w_out.shape, F32),
-            shape_of((1, width), F32),
-            shape_of((1, width), F32),
-        ),
+        (shape_of(w_in.shape, F32), shape_of(w_out.shape, F32)),
         [SMEM] + [VMEM] * 4,
         scratch=[pltpu.VMEM((width, plan.column_groups * plan.wide), BF16)],
     )(me, sides[0], swap(sides[0], 1), sides[1], swap(sides[1], 1))

time: 124 us -> 140 us (1.13)
  Pallas kernels: 28 us -> 44.7 us
  blocking collectives: 0 us -> 13.5 us
  starting transfers between devices: 36.2 us -> 24.7 us
  local copies, waits for them, and re-layouts: 4.95 us -> 3.34 us
  waiting for transfers between devices: 51.6 us -> 50 us
    pallas_call x2, Pallas kernels: 3.73 us -> 20.1 us  [the longest x1 18 us: on_device(): call(send_body, shape_of((dp_size, SLOT, width), BF16), [SMEM, HBM], mebi...]
    all_to_all x0 -> x1, blocking collectives: none -> 13.5 us  [exchange(): return lax.all_to_all(values, axes, split_axis=0, concat_axis=0, tiled=True)]
    all_to_all x3 -> x2, starting transfers between devices: 15.1 us -> 6.95 us  [exchange(): return lax.all_to_all(values, axes, split_axis=0, concat_axis=0, tiled=True)]
    all_to_all x3 -> x2, waiting for transfers between devices: 8.2 us -> 1.81 us  [exchange(): return lax.all_to_all(values, axes, split_axis=0, concat_axis=0, tiled=True)]
    ppermute x16, waiting for transfers between devices: 43.4 us -> 48.2 us  [swap(): lax.ppermute(values, both, [(here, here ^ mask) for here in range(devices...]
    ppermute x16, starting transfers between devices: 21.1 us -> 17.8 us  [swap(): lax.ppermute(values, both, [(here, here ^ mask) for here in range(devices...]
  transfers between devices with their start and end apart: 19 -> 18, of which waited for: 13 -> 15; matrix products, arithmetic and copies ran while one was open for 3% -> 3% of each run, Pallas kernels for 9% -> 8%
where the time goes in v9:
time: 140 us
  waiting for transfers between devices  50 us (36%)
  Pallas kernels  44.7 us (32%)
  starting transfers between devices  24.7 us (18%)
  blocking collectives  13.5 us (10%)
  local copies, waits for them, and re-layouts  3.34 us (2%)
  other arithmetic  2.65 us (2%)
    ppermute x16, waiting for transfers between devices, swap(): lax.ppermute(values, both, [(here, here ^ mask) for here in range(devices...  48.2 us
    pallas_call x1, Pallas kernels, on_device(): call(send_body, shape_of((dp_size, SLOT, width), BF16), [SMEM, HBM], mebi...  18 us
    ppermute x16, starting transfers between devices, swap(): lax.ppermute(values, both, [(here, here ^ mask) for here in range(devices...  17.8 us
    all_to_all x1, blocking collectives, exchange(): return lax.all_to_all(values, axes, split_axis=0, concat_axis=0, tiled=True)  13.5 us
    pallas_call x1, Pallas kernels, on_device(): call(functools.partial(backward_body, plan, total_factor), outs, [SMEM] *...  12.9 us
    pallas_call x1, Pallas kernels, on_device(): call(functools.partial(forward_body, plan.capacity), shapes, [VMEM] * 8,...  9.14 us
    all_to_all x2, starting transfers between devices, exchange(): return lax.all_to_all(values, axes, split_axis=0, concat_axis=0, tiled=True)  6.95 us
  transfers between devices with their start and end apart: 18, of which 15 were waited for; matrix products, arithmetic and copies ran while one was open for 3% of the time, Pallas kernels for 8%

profile of v9, /device:TPU:0, one launch (start us, length us, event | category | flops | bytes accessed | tf_op | source)
XLA Modules:
  0.0 139.9 jit_solution(12439928358854667598)
XLA Ops:
  0.7 0.7 compare_select_fusion
  1.4 13.5 %all_to_all.15.lengths_ref = s32[8,1,8]{2,1,0:T(1,128)} all-to-all(s32[8,1,8]{2,1,0:T(1,128)S(1)} %compare_select_fusion), channel_id=1, replica_groups=mesh['dp'=8,'table'=4] {'dp'}, dimensions={0} | all-to-all | bytes 512 | tf_op jit(solution)/shard_map/all_to_all | solution.py:478
  14.8 18.0 %shard_map.146 = bf16[8,64,512]{2,1,0:T(8,128)(2,1)} custom-call(s32[8,1,8]{2,1,0:T(1,128)} %all_to_all.15.lengths_ref, bf16[256,512]{1,0:T(8,128)(2,1)} %grad_ref.1), custom_call_target="tpu_custom_call" | custom-call | tf_op jit(solution)/shard_map/pallas_call | solution.py:482
  32.8 3.5 %all-to-all-start.1 = ((bf16[8,64,512]{2,1,0:T(8,128)(2,1)}), bf16[8,64,512]{2,1,0:T(8,128)(2,1)S(1)}, u32[]{:S(2)}, u32[]{:S(2)}) async-start(bf16[8,64,512]{2,1,0:T(8,128)(2,1)} %shard_map.146), calls=%async_computation.1 | async-start | bytes 1048576 | tf_op jit(solution)/shard_map/all_to_all | solution.py:478
  36.3 0.8 copy.19.number_ref
  37.1 0.8 copy.18.owner_col_ref
  37.9 0.9 copy.17.item_ref
  38.8 9.1 %shard_map.147 = (f32[512,512]{1,0:T(8,128)}, f32[512,512]{1,0:T(8,128)}, f32[512,1]{1,0:T(8,128)}, bf16[512,1536]{1,0:T(8,128)(2,1)}, bf16[16,128,128]{2,1,0:T(...) custom-call(bf16[256,512]{1,0:T(8,128)(2,1)} %rows_ref.1, ...), custom_call_target="tpu_custom_call" | custom-call | flops 2147483648 | bytes 10000000 | tf_op jit(solution)/shard_map/pallas_call | solution.py:495
  47.9 1.8 %all-to-all-done.1.refs_0_ = bf16[8,64,512]{2,1,0:T(8,128)(2,1)S(1)} async-done(((bf16[8,64,512]{2,1,0:T(8,128)(2,1)}), bf16[8,64,512]{2,1,0:T(8,128)(2,1)S(1)}, u32[]{:S(2)}, u32[]{:S(2)}) %all-to-all-start.1) | async-done | bytes 524320 | tf_op jit(solution)/shard_map/all_to_all | solution.py:478
  49.7 0.8 copy-done.1
  50.5 12.9 %shard_map.148 = (bf16[512,640]{1,0:T(8,128)(2,1)}, bf16[16,16,1280]{2,1,0:T(8,128)(2,1)}, bf16[16,16,1280]{2,1,0:T(8,128)(2,1)}, bf16[16,16,1280]{2,1,0:T(8,128)(2,1)}, bf16[16,16,1280]{2,1,0:T(8,128)(2,1)}) custom-call(s32[1]{0:T(128)} %bitcast.me_ref, s32[8]{0:T(128)} %dest_ref.1, s32[8]{0:T(128)} %blocks_ref.1, s32[1,512]{1,0:T(1,128)} %bitcast.12, ...), custom_call_target="tpu_custom_call" | custom-call | flops 10737418240 | bytes 12000000 | tf_op jit(solution)/shard_map/pallas_call | solution.py:521
  63.4 0.1 collective-permute-start
  63.4 0.5 collective-permute-start.1
  63.9 1.8 %collective-permute-done = bf16[16,16,1280]{2,1,0:T(8,128)(2,1)S(1)} collective-permute-done((bf16[16,16,1280]{2,1,0:T(8,128)(2,1)}, bf16[16,16,1280]{2,1,0:T(8,128)(2,1)S(1)}, u32[]{:S(2)}, u32[]{:S(2)}) %collective-permute-start) | collective-permute-done | bytes 655392 | tf_op jit(solution)/shard_map/ppermute | solution.py:475
  65.7 1.2 add_convert_fusion.1
  67.0 0.2 add_convert_fusion
  67.2 1.5 %collective-permute-start.4 = (bf16[8,16,1280]{2,1,0:T(8,128)(2,1)S(1)}, bf16[8,16,1280]{2,1,0:T(8,128)(2,1)S(1)}, u32[]{:S(2)}, u32[]{:S(2)}) collective-permute-start(bf16[8,16,1280]{2,1,0:T(8,128)(2,1)S(1)} %slice.47), channel_id=1, source_target_pairs={{0,4},{1,5},{2,6},{3,7},{4,0},{5,1},{6,2},{7,3},{8,12},{9,13},{10,... | collective-permute-start | bytes 983048 | tf_op jit(solution)/shard_map/ppermute | solution.py:475
  68.7 3.4 %all-to-all-start.2 = ((bf16[32,16,640]{2,1,0:T(8,128)(2,1)}), bf16[32,16,640]{2,1,0:T(8,128)(2,1)S(1)}, u32[]{:S(2)}, u32[]{:S(2)}) async-start(bf16[32,16,640]{2,1,0:T(8,128)(2,1)} %bitcast.7), calls=%async_computation.2 | async-start | bytes 1310720 | tf_op jit(solution)/shard_map/all_to_all | solution.py:478
  72.2 1.7 %collective-permute-start.2 = (bf16[8,16,1280]{2,1,0:T(8,128)(2,1)S(1)}, bf16[8,16,1280]{2,1,0:T(8,128)(2,1)S(1)}, u32[]{:S(2)}, u32[]{:S(2)}) collective-permute-start(bf16[8,16,1280]{2,1,0:T(8,128)(2,1)S(1)} %slice.43), channel_id=1, source_target_pairs={{0,2},{1,3},{2,0},{3,1},{4,6},{5,7},{6,4},{7,5},{8,10},{9,11},{10,... | collective-permute-start | bytes 983048 | tf_op jit(solution)/shard_map/ppermute | solution.py:475
  73.9 5.9 %collective-permute-done.4 = bf16[8,16,1280]{2,1,0:T(8,128)(2,1)S(1)} collective-permute-done((bf16[8,16,1280]{2,1,0:T(8,128)(2,1)S(1)}, bf16[8,16,1280]{2,1,0:T(8,128)(2,1)S(1)}, u32[]{:S(2)}, u32[]{:S(2)}) %collective-permute-start.4) | collective-permute-done | bytes 327712 | tf_op jit(solution)/shard_map/ppermute | solution.py:475
  79.8 0.1 add_convert_fusion.2
  79.9 1.8 %collective-permute-start.5 = (bf16[4,16,1280]{2,1,0:T(8,128)(2,1)S(1)}, bf16[4,16,1280]{2,1,0:T(8,128)(2,1)S(1)}, u32[]{:S(2)}, u32[]{:S(2)}) collective-permute-start(bf16[4,16,1280]{2,1,0:T(8,128)(2,1)S(1)} %slice.59), channel_id=1, source_target_pairs={{0,2},{1,3},{2,0},{3,1},{4,6},{5,7},{6,4},{7,5},{8,10},{9,11},{10,... | collective-permute-start | bytes 491528 | tf_op jit(solution)/shard_map/ppermute | solution.py:475
  81.7 7.5 %collective-permute-done.2 = bf16[8,16,1280]{2,1,0:T(8,128)(2,1)S(1)} collective-permute-done((bf16[8,16,1280]{2,1,0:T(8,128)(2,1)S(1)}, bf16[8,16,1280]{2,1,0:T(8,128)(2,1)S(1)}, u32[]{:S(2)}, u32[]{:S(2)}) %collective-permute-start.2) | collective-permute-done | bytes 327712 | tf_op jit(solution)/shard_map/ppermute | solution.py:475
  89.2 0.1 add_convert_fusion.3
  89.3 1.3 collective-permute-start.3
  90.6 1.8 %collective-permute-done.5 = bf16[4,16,1280]{2,1,0:T(8,128)(2,1)S(1)} collective-permute-done((bf16[4,16,1280]{2,1,0:T(8,128)(2,1)S(1)}, bf16[4,16,1280]{2,1,0:T(8,128)(2,1)S(1)}, u32[]{:S(2)}, u32[]{:S(2)}) %collective-permute-start.5) | collective-permute-done | bytes 163872 | tf_op jit(solution)/shard_map/ppermute | solution.py:475
  92.5 2.2 %collective-permute-done.3 = bf16[4,16,1280]{2,1,0:T(8,128)(2,1)S(1)} collective-permute-done((bf16[4,16,1280]{2,1,0:T(8,128)(2,1)S(1)}, bf16[4,16,1280]{2,1,0:T(8,128)(2,1)S(1)}, u32[]{:S(2)}, u32[]{:S(2)}) %collective-permute-start.3) | collective-permute-done | bytes 163872 | tf_op jit(solution)/shard_map/ppermute | solution.py:475
  94.8 1.5 %collective-permute-start.6 = (bf16[2,16,2560]{2,1,0:T(8,128)(2,1)S(1)}, bf16[2,16,2560]{2,1,0:T(8,128)(2,1)S(1)}, u32[]{:S(2)}, u32[]{:S(2)}) collective-permute-start(bf16[2,16,2560]{2,1,0:T(8,128)(2,1)S(1)} %slice.51), channel_id=1, source_target_pairs={{0,8},{1,9},{2,10},{3,11},{4,12},{5,13},{6,14},{7,15},{8,0},{9,1},... | collective-permute-start | bytes 491528 | tf_op jit(solution)/shard_map/ppermute | solution.py:475
  96.3 3.9 %collective-permute-done.6 = bf16[2,16,2560]{2,1,0:T(8,128)(2,1)S(1)} collective-permute-done((bf16[2,16,2560]{2,1,0:T(8,128)(2,1)S(1)}, bf16[2,16,2560]{2,1,0:T(8,128)(2,1)S(1)}, u32[]{:S(2)}, u32[]{:S(2)}) %collective-permute-start.6) | collective-permute-done | bytes 163872 | tf_op jit(solution)/shard_map/ppermute | solution.py:475
  100.2 2.5 %collective-permute-start.7 = (bf16[1,16,2560]{2,1,0:T(8,128)(2,1)S(1)}, bf16[1,16,2560]{2,1,0:T(8,128)(2,1)S(1)}, u32[]{:S(2)}, u32[]{:S(2)}) collective-permute-start(bf16[1,16,2560]{2,1,0:T(8,128)(2,1)S(1)} %slice.61), channel_id=1, source_target_pairs={{0,16},{1,17},{2,18},{3,19},{4,20},{5,21},{6,22},{7,23},{8,24},{9,... | collective-permute-start | bytes 245768 | tf_op jit(solution)/shard_map/ppermute | solution.py:475
  102.7 5.2 %collective-permute-done.7 = bf16[1,16,2560]{2,1,0:T(8,128)(2,1)S(1)} collective-permute-done((bf16[1,16,2560]{2,1,0:T(8,128)(2,1)S(1)}, bf16[1,16,2560]{2,1,0:T(8,128)(2,1)S(1)}, u32[]{:S(2)}, u32[]{:S(2)}) %collective-permute-start.7) | collective-permute-done | bytes 81952 | tf_op jit(solution)/shard_map/ppermute | solution.py:475
  107.9 0.6 collective-permute-start.8
  108.5 5.1 %collective-permute-done.8 = bf16[1,16,2560]{2,1,0:T(8,128)(2,1)S(1)} collective-permute-done((bf16[1,16,2560]{2,1,0:T(8,128)(2,1)S(1)}, bf16[1,16,2560]{2,1,0:T(8,128)(2,1)S(1)}, u32[]{:S(2)}, u32[]{:S(2)}) %collective-permute-start.8) | collective-permute-done | bytes 81952 | tf_op jit(solution)/shard_map/ppermute | solution.py:475
  113.6 1.8 %collective-permute-start.9 = (bf16[2,16,2560]{2,1,0:T(8,128)(2,1)S(1)}, bf16[2,16,2560]{2,1,0:T(8,128)(2,1)S(1)}, u32[]{:S(2)}, u32[]{:S(2)}) collective-permute-start(bf16[2,16,2560]{2,1,0:T(8,128)(2,1)S(1)} %pad_maximum_fusion.6), channel_id=1, source_target_pairs={{0,8},{1,9},{2,10},{3,11},{4,12},{5,13},{6,14},{7,15},{8,0},{9,1},... | collective-permute-start | bytes 491528 | tf_op jit(solution)/shard_map/ppermute | solution.py:475
  115.4 2.2 %shard_map.149 = (f32[1024,512]{1,0:T(8,128)}, f32[1,512]{1,0:T(1,128)}, f32[1,512]{1,0:T(1,128)}) custom-call(bf16[512,640]{1,0:T(8,128)(2,1)S(1)} %bitcast.11), custom_call_target="tpu_custom_call" | custom-call | tf_op jit(solution)/shard_map/pallas_call | solution.py:553
  117.6 1.4 %collective-permute-done.9 = bf16[2,16,2560]{2,1,0:T(8,128)(2,1)S(1)} collective-permute-done((bf16[2,16,2560]{2,1,0:T(8,128)(2,1)S(1)}, bf16[2,16,2560]{2,1,0:T(8,128)(2,1)S(1)}, u32[]{:S(2)}, u32[]{:S(2)}) %collective-permute-start.9) | collective-permute-done | bytes 163872 | tf_op jit(solution)/shard_map/ppermute | solution.py:475
  119.1 1.5 %collective-permute-start.10 = (bf16[4,16,1280]{2,1,0:T(8,128)(2,1)S(1)}, bf16[4,16,1280]{2,1,0:T(8,128)(2,1)S(1)}, u32[]{:S(2)}, u32[]{:S(2)}) collective-permute-start(bf16[4,16,1280]{2,1,0:T(8,128)(2,1)S(1)} %get-tuple-element.68), channel_id=1, source_target_pairs={{0,4},{1,5},{2,6},{3,7},{4,0},{5,1},{6,2},{7,3},{8,12},{9,13},{10,... | collective-permute-start | bytes 491528 | tf_op jit(solution)/shard_map/ppermute | solution.py:475
  120.5 0.7 collective-permute-start.13
  121.2 5.0 %collective-permute-done.10 = bf16[4,16,1280]{2,1,0:T(8,128)(2,1)S(1)} collective-permute-done((bf16[4,16,1280]{2,1,0:T(8,128)(2,1)S(1)}, bf16[4,16,1280]{2,1,0:T(8,128)(2,1)S(1)}, u32[]{:S(2)}, u32[]{:S(2)}) %collective-permute-start.10) | collective-permute-done | bytes 163872 | tf_op jit(solution)/shard_map/ppermute | solution.py:475
  126.3 1.5 %collective-permute-start.11 = (bf16[8,16,1280]{2,1,0:T(8,128)(2,1)S(1)}, bf16[8,16,1280]{2,1,0:T(8,128)(2,1)S(1)}, u32[]{:S(2)}, u32[]{:S(2)}) collective-permute-start(bf16[8,16,1280]{2,1,0:T(8,128)(2,1)S(1)} %pad_maximum_fusion.4), channel_id=1, source_target_pairs={{0,2},{1,3},{2,0},{3,1},{4,6},{5,7},{6,4},{7,5},{8,10},{9,11},{10,... | collective-permute-start | bytes 983048 | tf_op jit(solution)/shard_map/ppermute | solution.py:475
  127.9 0.6 collective-permute-start.14
  128.5 5.0 %collective-permute-done.11 = bf16[8,16,1280]{2,1,0:T(8,128)(2,1)S(1)} collective-permute-done((bf16[8,16,1280]{2,1,0:T(8,128)(2,1)S(1)}, bf16[8,16,1280]{2,1,0:T(8,128)(2,1)S(1)}, u32[]{:S(2)}, u32[]{:S(2)}) %collective-permute-start.11) | collective-permute-done | bytes 327712 | tf_op jit(solution)/shard_map/ppermute | solution.py:475
  133.5 0.1 collective-permute-start.12
  133.6 1.4 %collective-permute-done.14 = bf16[8,16,1280]{2,1,0:T(8,128)(2,1)S(1)} collective-permute-done((bf16[8,16,1280]{2,1,0:T(8,128)(2,1)S(1)}, bf16[8,16,1280]{2,1,0:T(8,128)(2,1)S(1)}, u32[]{:S(2)}, u32[]{:S(2)}) %collective-permute-start.14) | collective-permute-done | bytes 327712 | tf_op jit(solution)/shard_map/ppermute | solution.py:475
  135.1 0.1 collective-permute-start.15
  135.2 0.5 collective-permute-done.12.refs_1_
  135.7 1.6 %collective-permute-done.15.refs_3_ = bf16[16,16,1280]{2,1,0:T(8,128)(2,1)S(1)} collective-permute-done((bf16[16,16,1280]{2,1,0:T(8,128)(2,1)S(1)}, bf16[16,16,1280]{2,1,0:T(8,128)(2,1)S(1)}, u32[]{:S(2)}, u32[]{:S(2)}) %collective-permute-start.15) | collective-permute-done | bytes 655392 | tf_op jit(solution)/shard_map/ppermute | solution.py:475
  137.2 2.6 %shard_map.150 = (f32[512,2048]{1,0:T(8,128)}, f32[512,512]{1,0:T(8,128)}) custom-call(s32[1]{0:T(128)} %bitcast.me_ref, bf16[16,16,1280]{2,1,0:T(8,128)(2,1)S(1)} %pad_maximum_fusion.refs_0_, bf16[16,16,1280]{2,1,0:T(8,128)(2,1)S(1)} %collective-permute-done.12.refs_1_, bf16[16,16,1280]{2,1,0:T(8,128)(2,1)S(1)} %pad_maximum_fusion.1.refs_2_, ...), custom_call_target="tpu_custom_call" | custom-call | tf_op jit(solution)/shard_map/pallas_call | solution.py:570
  (30 shorter events, 0.6 us)
Async XLA Ops:
  0.6 35.7 %copy-start.3 = (s32[256]{0:T(256)S(1)}, s32[256]{0:T(256)}, u32[]{:S(2)}) copy-start(s32[256]{0:T(256)} %param.14) | copy-start | bytes 3076
  0.6 36.5 %copy-start.4 = (s32[256,1]{0,1:T(1,128)S(1)}, s32[256,1]{0,1:T(1,128)}, u32[]{:S(2)}) copy-start(s32[256,1]{0,1:T(1,128)} %param.13) | copy-start | bytes 3076
  0.7 37.3 %copy-start.2 = (s32[512]{0:T(512)S(1)}, s32[512]{0:T(512)}, u32[]{:S(2)}) copy-start(s32[512]{0:T(512)} %param.12) | copy-start | bytes 6148
  32.8 16.9 %all-to-all-start.1 = ((bf16[8,64,512]{2,1,0:T(8,128)(2,1)}), bf16[8,64,512]{2,1,0:T(8,128)(2,1)S(1)}, u32[]{:S(2)}, u32[]{:S(2)}) async-start(bf16[8,64,512]{2,1,0:T(8,128)(2,1)} %shard_map.146), calls=%async_computation.1 | async-start | bytes 1048576 | tf_op jit(solution)/shard_map/all_to_all | solution.py:478
  49.7 0.8 copy-start.1
  63.4 3.6 %copy-start = (bf16[16,16,1280]{2,1,0:T(8,128)(2,1)S(1)}, bf16[16,16,1280]{2,1,0:T(8,128)(2,1)}, u32[]{:S(2)}) copy-start(bf16[16,16,1280]{2,1,0:T(8,128)(2,1)} %get-tuple-element.52) | copy-start | bytes 1966084
  63.4 2.4 %collective-permute-start = (bf16[16,16,1280]{2,1,0:T(8,128)(2,1)}, bf16[16,16,1280]{2,1,0:T(8,128)(2,1)S(1)}, u32[]{:S(2)}, u32[]{:S(2)}) collective-permute-start(bf16[16,16,1280]{2,1,0:T(8,128)(2,1)} %get-tuple-element.51), channel_id=1, source_target_pairs={{0,1},{1,0},{2,3},{3,2},{4,5},{5,4},{6,7},{7,6},{8,9},{9,8},{10,11... | collective-permute-start | bytes 1966088 | tf_op jit(solution)/shard_map/ppermute | solution.py:475
  63.4 3.5 %collective-permute-start.1 = (bf16[16,16,1280]{2,1,0:T(8,128)(2,1)}, bf16[16,16,1280]{2,1,0:T(8,128)(2,1)S(1)}, u32[]{:S(2)}, u32[]{:S(2)}) collective-permute-start(bf16[16,16,1280]{2,1,0:T(8,128)(2,1)} %get-tuple-element.53), channel_id=1, source_target_pairs={{0,1},{1,0},{2,3},{3,2},{4,5},{5,4},{6,7},{7,6},{8,9},{9,8},{10,11... | collective-permute-start | bytes 1966088 | tf_op jit(solution)/shard_map/ppermute | solution.py:475
  67.2 12.6 %collective-permute-start.4 = (bf16[8,16,1280]{2,1,0:T(8,128)(2,1)S(1)}, bf16[8,16,1280]{2,1,0:T(8,128)(2,1)S(1)}, u32[]{:S(2)}, u32[]{:S(2)}) collective-permute-start(bf16[8,16,1280]{2,1,0:T(8,128)(2,1)S(1)} %slice.47), channel_id=1, source_target_pairs={{0,4},{1,5},{2,6},{3,7},{4,0},{5,1},{6,2},{7,3},{8,12},{9,13},{10,... | collective-permute-start | bytes 983048 | tf_op jit(solution)/shard_map/ppermute | solution.py:475
  68.7 26.0 %all-to-all-start.2 = ((bf16[32,16,640]{2,1,0:T(8,128)(2,1)}), bf16[32,16,640]{2,1,0:T(8,128)(2,1)S(1)}, u32[]{:S(2)}, u32[]{:S(2)}) async-start(bf16[32,16,640]{2,1,0:T(8,128)(2,1)} %bitcast.7), calls=%async_computation.2 | async-start | bytes 1310720 | tf_op jit(solution)/shard_map/all_to_all | solution.py:478
  72.2 17.0 %collective-permute-start.2 = (bf16[8,16,1280]{2,1,0:T(8,128)(2,1)S(1)}, bf16[8,16,1280]{2,1,0:T(8,128)(2,1)S(1)}, u32[]{:S(2)}, u32[]{:S(2)}) collective-permute-start(bf16[8,16,1280]{2,1,0:T(8,128)(2,1)S(1)} %slice.43), channel_id=1, source_target_pairs={{0,2},{1,3},{2,0},{3,1},{4,6},{5,7},{6,4},{7,5},{8,10},{9,11},{10,... | collective-permute-start | bytes 983048 | tf_op jit(solution)/shard_map/ppermute | solution.py:475
  79.9 12.6 %collective-permute-start.5 = (bf16[4,16,1280]{2,1,0:T(8,128)(2,1)S(1)}, bf16[4,16,1280]{2,1,0:T(8,128)(2,1)S(1)}, u32[]{:S(2)}, u32[]{:S(2)}) collective-permute-start(bf16[4,16,1280]{2,1,0:T(8,128)(2,1)S(1)} %slice.59), channel_id=1, source_target_pairs={{0,2},{1,3},{2,0},{3,1},{4,6},{5,7},{6,4},{7,5},{8,10},{9,11},{10,... | collective-permute-start | bytes 491528 | tf_op jit(solution)/shard_map/ppermute | solution.py:475
  89.3 5.4 %collective-permute-start.3 = (bf16[4,16,1280]{2,1,0:T(8,128)(2,1)S(1)}, bf16[4,16,1280]{2,1,0:T(8,128)(2,1)S(1)}, u32[]{:S(2)}, u32[]{:S(2)}) collective-permute-start(bf16[4,16,1280]{2,1,0:T(8,128)(2,1)S(1)} %slice.57), channel_id=1, source_target_pairs={{0,4},{1,5},{2,6},{3,7},{4,0},{5,1},{6,2},{7,3},{8,12},{9,13},{10,... | collective-permute-start | bytes 491528 | tf_op jit(solution)/shard_map/ppermute | solution.py:475
  94.8 5.4 %collective-permute-start.6 = (bf16[2,16,2560]{2,1,0:T(8,128)(2,1)S(1)}, bf16[2,16,2560]{2,1,0:T(8,128)(2,1)S(1)}, u32[]{:S(2)}, u32[]{:S(2)}) collective-permute-start(bf16[2,16,2560]{2,1,0:T(8,128)(2,1)S(1)} %slice.51), channel_id=1, source_target_pairs={{0,8},{1,9},{2,10},{3,11},{4,12},{5,13},{6,14},{7,15},{8,0},{9,1},... | collective-permute-start | bytes 491528 | tf_op jit(solution)/shard_map/ppermute | solution.py:475
  100.2 7.7 %collective-permute-start.7 = (bf16[1,16,2560]{2,1,0:T(8,128)(2,1)S(1)}, bf16[1,16,2560]{2,1,0:T(8,128)(2,1)S(1)}, u32[]{:S(2)}, u32[]{:S(2)}) collective-permute-start(bf16[1,16,2560]{2,1,0:T(8,128)(2,1)S(1)} %slice.61), channel_id=1, source_target_pairs={{0,16},{1,17},{2,18},{3,19},{4,20},{5,21},{6,22},{7,23},{8,24},{9,... | collective-permute-start | bytes 245768 | tf_op jit(solution)/shard_map/ppermute | solution.py:475
  107.9 5.7 %collective-permute-start.8 = (bf16[1,16,2560]{2,1,0:T(8,128)(2,1)S(1)}, bf16[1,16,2560]{2,1,0:T(8,128)(2,1)S(1)}, u32[]{:S(2)}, u32[]{:S(2)}) collective-permute-start(bf16[1,16,2560]{2,1,0:T(8,128)(2,1)S(1)} %add_convert_fusion.7), channel_id=1, source_target_pairs={{0,16},{1,17},{2,18},{3,19},{4,20},{5,21},{6,22},{7,23},{8,24},{9,... | collective-permute-start | bytes 245768 | tf_op jit(solution)/shard_map/ppermute | solution.py:475
  113.6 5.4 %collective-permute-start.9 = (bf16[2,16,2560]{2,1,0:T(8,128)(2,1)S(1)}, bf16[2,16,2560]{2,1,0:T(8,128)(2,1)S(1)}, u32[]{:S(2)}, u32[]{:S(2)}) collective-permute-start(bf16[2,16,2560]{2,1,0:T(8,128)(2,1)S(1)} %pad_maximum_fusion.6), channel_id=1, source_target_pairs={{0,8},{1,9},{2,10},{3,11},{4,12},{5,13},{6,14},{7,15},{8,0},{9,1},... | collective-permute-start | bytes 491528 | tf_op jit(solution)/shard_map/ppermute | solution.py:475
  119.1 7.2 %collective-permute-start.10 = (bf16[4,16,1280]{2,1,0:T(8,128)(2,1)S(1)}, bf16[4,16,1280]{2,1,0:T(8,128)(2,1)S(1)}, u32[]{:S(2)}, u32[]{:S(2)}) collective-permute-start(bf16[4,16,1280]{2,1,0:T(8,128)(2,1)S(1)} %get-tuple-element.68), channel_id=1, source_target_pairs={{0,4},{1,5},{2,6},{3,7},{4,0},{5,1},{6,2},{7,3},{8,12},{9,13},{10,... | collective-permute-start | bytes 491528 | tf_op jit(solution)/shard_map/ppermute | solution.py:475
  120.5 7.3 %collective-permute-start.13 = (bf16[4,16,1280]{2,1,0:T(8,128)(2,1)S(1)}, bf16[4,16,1280]{2,1,0:T(8,128)(2,1)S(1)}, u32[]{:S(2)}, u32[]{:S(2)}) collective-permute-start(bf16[4,16,1280]{2,1,0:T(8,128)(2,1)S(1)} %get-tuple-element.67), channel_id=1, source_target_pairs={{0,2},{1,3},{2,0},{3,1},{4,6},{5,7},{6,4},{7,5},{8,10},{9,11},{10,... | collective-permute-start | bytes 491528 | tf_op jit(solution)/shard_map/ppermute | solution.py:475
  126.3 7.1 %collective-permute-start.11 = (bf16[8,16,1280]{2,1,0:T(8,128)(2,1)S(1)}, bf16[8,16,1280]{2,1,0:T(8,128)(2,1)S(1)}, u32[]{:S(2)}, u32[]{:S(2)}) collective-permute-start(bf16[8,16,1280]{2,1,0:T(8,128)(2,1)S(1)} %pad_maximum_fusion.4), channel_id=1, source_target_pairs={{0,2},{1,3},{2,0},{3,1},{4,6},{5,7},{6,4},{7,5},{8,10},{9,11},{10,... | collective-permute-start | bytes 983048 | tf_op jit(solution)/shard_map/ppermute | solution.py:475
  127.9 7.1 %collective-permute-start.14 = (bf16[8,16,1280]{2,1,0:T(8,128)(2,1)S(1)}, bf16[8,16,1280]{2,1,0:T(8,128)(2,1)S(1)}, u32[]{:S(2)}, u32[]{:S(2)}) collective-permute-start(bf16[8,16,1280]{2,1,0:T(8,128)(2,1)S(1)} %pad_maximum_fusion.5), channel_id=1, source_target_pairs={{0,4},{1,5},{2,6},{3,7},{4,0},{5,1},{6,2},{7,3},{8,12},{9,13},{10,... | collective-permute-start | bytes 983048 | tf_op jit(solution)/shard_map/ppermute | solution.py:475
  133.5 2.2 %collective-permute-start.12 = (bf16[16,16,1280]{2,1,0:T(8,128)(2,1)S(1)}, bf16[16,16,1280]{2,1,0:T(8,128)(2,1)S(1)}, u32[]{:S(2)}, u32[]{:S(2)}) collective-permute-start(bf16[16,16,1280]{2,1,0:T(8,128)(2,1)S(1)} %pad_maximum_fusion.refs_0_), channel_id=1, source_target_pairs={{0,1},{1,0},{2,3},{3,2},{4,5},{5,4},{6,7},{7,6},{8,9},{9,8},{10,11... | collective-permute-start | bytes 1966088 | tf_op jit(solution)/shard_map/ppermute | solution.py:475
  135.1 2.2 %collective-permute-start.15 = (bf16[16,16,1280]{2,1,0:T(8,128)(2,1)S(1)}, bf16[16,16,1280]{2,1,0:T(8,128)(2,1)S(1)}, u32[]{:S(2)}, u32[]{:S(2)}) collective-permute-start(bf16[16,16,1280]{2,1,0:T(8,128)(2,1)S(1)} %pad_maximum_fusion.1.refs_2_), channel_id=1, source_target_pairs={{0,1},{1,0},{2,3},{3,2},{4,5},{5,4},{6,7},{7,6},{8,9},{9,8},{10,11... | collective-permute-start | bytes 1966088 | tf_op jit(solution)/shard_map/ppermute | solution.py:475

commit v10 on v9

--- a/solution.py
+++ b/solution.py
@@ -23,12 +23,10 @@
 BF16 = jnp.bfloat16
 VMEM = pl.BlockSpec(memory_space=pltpu.VMEM)
 SMEM = pl.BlockSpec(memory_space=pltpu.SMEM)
-HBM = pl.BlockSpec(memory_space=pltpu.HBM)
-ANY = pl.BlockSpec(memory_space=pl.ANY)
-
-
-def call(body, out_shape, in_specs, flops=0, moved=0, scratch=(), out_space=VMEM, mebibytes=24):
-    outs = jax.tree.map(lambda _: out_space, out_shape)
+
+
+def call(body, out_shape, in_specs, flops=0, moved=0, scratch=(), mebibytes=24):
+    outs = jax.tree.map(lambda _: VMEM, out_shape)
     return pl.pallas_call(
         body,
         out_shape=out_shape,
@@ -56,26 +54,22 @@
 TN = ((0,), (0,))
 
 
-def send_body(lengths_ref, grad_ref, out_ref, sems):
-    peers = out_ref.shape[0]
+def send_body(table_size, me_ref, lengths_ref, grad_ref, *refs):
+    out_refs, begin_ref = refs[:-1], refs[-1]
+    peers = len(out_refs)
     blocks = grad_ref.shape[0] // BLK
     begin = jnp.int32(0)
-    copies = []
     for peer in range(peers):
+        begin_ref[peer] = begin
+        for slot in range(peers):
+            begin = begin + lengths_ref[peer, 0, slot]
+    me = me_ref[0] // table_size
+    for apart, out_ref in enumerate(out_refs):
+        begin = begin_ref[me ^ apart]
         for inner in range(LMAXB):
             block = jnp.minimum(begin + inner, blocks - 1)
-            copies.append(
-                pltpu.make_async_copy(
-                    grad_ref.at[pl.ds(pl.multiple_of(block * BLK, BLK), BLK)],
-                    out_ref.at[peer, pl.ds(inner * BLK, BLK)],
-                    sems.at[peer, inner],
-                )
-            )
-            copies[-1].start()
-        for slot in range(peers):
-            begin = begin + lengths_ref[peer, 0, slot]
-    for copy in copies:
-        copy.wait()
+            rows = grad_ref[pl.ds(pl.multiple_of(block * BLK, BLK), BLK), :]
+            out_ref[inner * BLK : (inner + 1) * BLK, :] = rows
 
 
 def tile_mask():
@@ -134,13 +128,7 @@
     number_ref,
     *refs,
 ):
-    size = len(SAVED)
-    held = dict(zip(SAVED, refs[size : 2 * size]))
-    sems = refs[-1]
-    copies = {
-        name: pltpu.make_async_copy(held[name], refs[index], sems.at[index])
-        for index, name in enumerate(SAVED)
-    }
+    held = dict(zip(SAVED, refs))
     gate_ref, hat_ref, hat_scale_ref, qkv_ref, slope_ref, slope_t_ref = (
         held[name] for name in SAVED[:6]
     )
@@ -159,8 +147,6 @@
     lane = lax.broadcasted_iota(jnp.int32, (count, LANES), 1)
     digits = jnp.where(lane == 0, number >> 5, jnp.where(lane == 1, number & 31, 0))
     digits_ref[...] = digits.astype(F32).astype(BF16)
-    copies["place"].start()
-    copies["digits"].start()
     values = rows_ref[...].astype(F32)
     shifted = values - jnp.mean(values, axis=-1, keepdims=True)
     scale = lax.rsqrt(jnp.mean(shifted * shifted, axis=-1, keepdims=True) + EPSILON)
@@ -170,8 +156,6 @@
     normed = hat * gain_in_ref[...]
     normed_t_ref[...] = normed.T.astype(BF16)
     normed = normed.astype(BF16)
-    for name in ("rows_hat", "rows_scale", "normed_t"):
-        copies[name].start()
     lane = lax.broadcasted_iota(jnp.int32, (tokens, count), 1)
     pick = jnp.where(lane == jnp.broadcast_to(item_ref[...], (tokens, count)), 1.0, 0.0)
     pick = pick.astype(BF16)
@@ -190,8 +174,6 @@
             qkv_ref[:, (part - 1) * width : part * width] = dot(pick, active.astype(BF16)).astype(
                 BF16
             )
-    for name in ("gate", "qkv", "rows_slope"):
-        copies[name].start()
     mask = tile_mask()
     factor = HDIM ** (-0.5)
     for tile in range(tokens // TILE):
@@ -219,23 +201,6 @@
         hat_scale_ref[rows, :] = scale
         mixed = hat * gain_out_ref[...] * gate_ref[rows, :]
         mixed_t_ref[:, rows] = mixed.T.astype(BF16)
-    for name in ("hat", "hat_scale", "slope", "slope_t", "weight_t", "mixed_t"):
-        copies[name].start()
-    for copy in copies.values():
-        copy.wait()
-
-
-def fetch(names, far_refs, near_refs, sems):
-    copies = {}
-    for index, name in enumerate(names):
-        copies[name] = pltpu.make_async_copy(far_refs[index], near_refs[index], sems.at[index])
-        copies[name].start()
-
-    def get(name):
-        copies[name].wait()
-        return near_refs[names.index(name)]
-
-    return get
 
 
 def gather_of(item_ref, count):
@@ -245,8 +210,7 @@
     return jnp.where(hit, 1.0, 0.0).astype(BF16)
 
 
-FETCHED = (
-    "got",
+USED = (
     "w_out",
     "hat",
     "gate",
@@ -267,31 +231,43 @@
 
 
 def backward_body(
-    plan, factor, me_ref, dest_ref, blocks_ref, item_ref, gain_in_ref, gain_out_ref, *refs
+    plan,
+    table_size,
+    factor,
+    me_ref,
+    dest_ref,
+    blocks_ref,
+    item_ref,
+    gain_in_ref,
+    gain_out_ref,
+    *refs,
 ):
-    size = len(FETCHED)
-    far_refs, out_refs, refs = refs[:size], refs[size : size + 5], refs[size + 5 :]
-    near_refs, stage_refs, refs = refs[:size], refs[size : size + 5], refs[size + 5 :]
-    sums_ref, active_ref, grad_y_ref, in_sems, out_sems = refs
-    get = fetch(FETCHED, far_refs, near_refs, in_sems)
-    sends = [
-        pltpu.make_async_copy(stage, out, out_sems.at[index])
-        for index, (stage, out) in enumerate(zip(stage_refs, out_refs))
-    ]
-    got_ref = get("got")
-    for slot in range(got_ref.shape[0]):
-        rows = got_ref[dest_ref[slot]]
+    used, refs = dict(zip(USED, refs)), refs[len(USED) :]
+    got_refs, (table_ref, *part_refs), (wide_ref, sums_ref, active_ref, grad_y_ref) = (
+        refs[:-9],
+        refs[-9:-4],
+        refs[-4:],
+    )
+    w_out_ref, hat_ref, gate_ref, hat_scale_ref, qkv_ref, slope_ref, slope_t_ref = (
+        used[name] for name in USED[:7]
+    )
+    weight_t_ref, mixed_t_ref, normed_t_ref, rows_slope_ref, w_in_ref = (
+        used[name] for name in USED[7:12]
+    )
+    rows_hat_ref, rows_scale_ref, place_ref, digits_ref = (used[name] for name in USED[12:])
+    for apart, got_ref in enumerate(got_refs):
+        wide_ref[apart] = got_ref[...]
+    for slot in range(len(got_refs)):
+        rows = wide_ref[dest_ref[slot] ^ (me_ref[0] // table_size)]
         live = lax.broadcasted_iota(jnp.int32, rows.shape, 0) < blocks_ref[slot] * BLK
         rows = jnp.where(live, rows.astype(F32), 0.0).astype(BF16)
         grad_y_ref[slot * SLOT : (slot + 1) * SLOT, :] = rows
-    w_out_ref = get("w_out")
     tokens, width = grad_y_ref.shape
+    count = normed_t_ref.shape[1]
     gain_total = jnp.zeros((1, width), F32)
     for tile in range(tokens // TILE):
         rows = slice(tile * TILE, (tile + 1) * TILE)
         grad_mixed = dot(grad_y_ref[rows, :], w_out_ref[...], NT)
-        if tile == 0:
-            hat_ref, gate_ref, hat_scale_ref = get("hat"), get("gate"), get("hat_scale")
         hat = hat_ref[rows, :]
         active_ref[rows, :width] = (grad_mixed * hat * gain_out_ref[...]).astype(BF16)
         inner = grad_mixed * gate_ref[rows, :]
@@ -300,8 +276,6 @@
         mean = jnp.mean(inner, axis=-1, keepdims=True)
         along = jnp.mean(inner * hat, axis=-1, keepdims=True)
         grad_att = ((inner - mean - hat * along) * hat_scale_ref[rows, :]).astype(BF16)
-        if tile == 0:
-            qkv_ref, slope_ref, slope_t_ref, weight_t_ref = (get(name) for name in FETCHED[5:9])
         for head in range(HEADS):
             vals, queries, keys = (
                 qkv_ref[rows, part * width + head * HDIM : part * width + (head + 1) * HDIM]
@@ -319,10 +293,7 @@
             ):
                 first = part * width + head * HDIM
                 active_ref[rows, first : first + HDIM] = value.astype(BF16)
-    mixed_t_ref = get("mixed_t")
     sums_ref[:, :width] = (dot(mixed_t_ref[...], grad_y_ref[...]) * factor).astype(BF16)
-    normed_t_ref, rows_slope_ref, w_in_ref = get("normed_t"), get("rows_slope"), get("w_in")
-    count = normed_t_ref.shape[1]
     gather = gather_of(item_ref, count)
     grad_normed = jnp.zeros((count, width), F32)
     for part in range(4):
@@ -333,17 +304,13 @@
             dot(normed_t_ref[...], grad_hidden) * factor
         ).astype(BF16)
         grad_normed = grad_normed + dot(grad_hidden, w_in_ref[:, columns], NT)
-    rows_hat_ref, rows_scale_ref, place_ref, digits_ref = (get(name) for name in FETCHED[13:])
     hat = rows_hat_ref[...]
     gains = (jnp.sum(grad_normed * hat, axis=0, keepdims=True) * factor, gain_total * factor)
-    plan.write(me_ref[0], sums_ref, stage_refs[1:])
-    for copy in sends[1:]:
-        copy.start()
+    plan.write(me_ref[0], sums_ref, part_refs)
     inner = grad_normed * gain_in_ref[...]
     mean = jnp.mean(inner, axis=-1, keepdims=True)
     along = jnp.mean(inner * hat, axis=-1, keepdims=True)
     row_grad = (inner - mean - hat * along) * rows_scale_ref[...] + dot(gather, grad_y_ref[...])
-    table_ref = stage_refs[0]
     places = table_ref.shape[0]
     spots = lax.broadcasted_iota(jnp.int32, (places, count), 0)
     hit = spots == jnp.broadcast_to(place_ref[...], (places, count))
@@ -363,9 +330,6 @@
     repeat = jnp.where(repeat == lane, 1.0, 0.0).astype(BF16)
     table_ref[:, width:] = dot(repeat, lanes).astype(BF16)
     table_ref[:, width : width + LANES] += dot(spread, digits_ref[...]).astype(BF16)
-    sends[0].start()
-    for copy in sends:
-        copy.wait()
 
 
 class Plan:
@@ -480,27 +444,25 @@
     peers = jnp.arange(dp_size, dtype=jnp.int32)[:, None, None]
     lengths = jnp.where(seq_dest[None, None, :] == peers, seq_blocks[None, None, :], 0)
     send = call(
-        send_body,
-        shape_of((dp_size, SLOT, width), BF16),
-        [SMEM, HBM],
-        mebibytes=58,
-        out_space=HBM,
-        scratch=[pltpu.SemaphoreType.DMA((dp_size, LMAXB))],
-    )(exchange(lengths, "dp"), grad_out)
-    got = exchange(send, "dp")
+        functools.partial(send_body, table_size),
+        [shape_of((SLOT, width), BF16)] * dp_size,
+        [SMEM] * 2 + [VMEM],
+        scratch=[pltpu.SMEM((dp_size,), jnp.int32)],
+    )(me, exchange(lengths, "dp"), grad_out)
+    got = list(send)
+    far = [apart for apart in range(1, dp_size) if 2 * apart >= dp_size]
+    for apart in far:
+        got[apart] = swap(send[apart], apart * table_size)
+    *near, touched_rows = lax.optimization_barrier((*send[: far[0]], touched_rows))
 
     shapes = saved_shapes(tokens, count, width)
-    shapes = [shapes[name] for name in SAVED]
-    held = [pltpu.VMEM(item.shape, item.dtype) for item in shapes]
     saved = call(
         functools.partial(forward_body, plan.capacity),
-        shapes,
+        [shapes[name] for name in SAVED],
         [VMEM] * 8,
-        flops=4 * count * width * width * 8,
+        flops=4 * count * width * width * 20,
         moved=10_000_000,
-        mebibytes=58,
-        scratch=held + [pltpu.SemaphoreType.DMA((len(SAVED),))],
-        out_space=HBM,
+        mebibytes=12 + tokens // 32,
     )(
         touched_rows,
         row_of_token.reshape(tokens, 1),
@@ -511,30 +473,38 @@
         row_owner.reshape(1, count),
         owner_row.reshape(count, 1),
     )
-
+    *near, gate = lax.optimization_barrier((*near, saved[0]))
+    saved = [gate, *saved[1:]]
+    got[0] = near[0]
+    for apart in range(1, far[0]):
+        got[apart] = swap(near[apart], apart * table_size)
     saved = dict(zip(SAVED, saved), w_in=w_in, w_out=w_out)
-    saved = dict(saved, got=got)
-    fetched = [saved[name] for name in FETCHED]
     outs = [shape_of((devices_all * plan.capacity, width + plan.extra), BF16)]
     for _, wide in plan.sides:
         outs += [shape_of((devices_all // 2, CHUNK_ROWS, wide), BF16)] * 2
     table_send, *parts = call(
-        functools.partial(backward_body, plan, total_factor),
+        functools.partial(backward_body, plan, table_size, total_factor),
         outs,
-        [SMEM] * 3 + [VMEM] * 3 + [ANY] + [HBM] * (len(FETCHED) - 1),
+        [SMEM] * 3 + [VMEM] * (3 + len(USED) + dp_size),
         flops=4 * count * width * width * 40,
         moved=12_000_000,
-        mebibytes=58,
-        out_space=HBM,
-        scratch=[pltpu.VMEM(item.shape, item.dtype) for item in fetched + outs]
-        + [
+        mebibytes=12 + tokens // 32,
+        scratch=[
+            pltpu.VMEM((dp_size, SLOT, width), BF16),
             pltpu.VMEM((width, plan.column_groups * plan.wide), BF16),
             pltpu.VMEM((tokens, 4 * width), BF16),
             pltpu.VMEM((tokens, width), BF16),
-            pltpu.SemaphoreType.DMA((len(FETCHED),)),
-            pltpu.SemaphoreType.DMA((len(outs),)),
         ],
-    )(me, seq_dest, seq_blocks, row_of_token.reshape(1, tokens), gain_in, gain_out, *fetched)
+    )(
+        me,
+        seq_dest,
+        seq_blocks,
+        row_of_token.reshape(1, tokens),
+        gain_in,
+        gain_out,
+        *(saved[name] for name in USED),
+        *got,
+    )
 
     def reduced(kept, mask):
         middle = kept.shape[0] // 2
@@ -544,7 +514,6 @@
         return jnp.concatenate([kept, swap(kept, mask)])
 
     sides = [add(parts[2 * side], swap(parts[2 * side + 1], 1)) for side in range(2)]
-    *sides, table_send = lax.optimization_barrier((*sides, table_send))
     table_got = exchange(table_send.reshape(devices_all, plan.capacity, -1), both)
     for step in range(plan.near_steps):
         sides = [reduced(sides[side], plan.orders[side][step]) for side in range(2)]

time: 140 us -> 123 us (0.88)
  Pallas kernels: 44.7 us -> 19.9 us
  starting transfers between devices: 24.7 us -> 44.2 us
  blocking collectives: 13.5 us -> 0 us
  local copies, waits for them, and re-layouts: 3.34 us -> 8.11 us
  waiting for transfers between devices: 50 us -> 45.3 us
  other arithmetic: 2.65 us -> 4.32 us
    pallas_call x3, Pallas kernels: 40 us -> 15.1 us  [the longest x1 8.88 us: on_device(): call(functools.partial(backward_body, plan, table_size, total_factor), ou...]
    ppermute x16 -> x23, starting transfers between devices: 17.8 us -> 33.2 us  [swap(): lax.ppermute(values, both, [(here, here ^ mask) for here in range(devices...]
    all_to_all x1 -> x0, blocking collectives: 13.5 us -> none  [exchange(): return lax.all_to_all(values, axes, split_axis=0, concat_axis=0, tiled=True)]
    ppermute x16 -> x23, waiting for transfers between devices: 48.2 us -> 41.4 us  [swap(): lax.ppermute(values, both, [(here, here ^ mask) for here in range(devices...]
    unnamed x11 -> x25, local copies, waits for them, and re-layouts: 1.57 us -> 6.37 us
    all_to_all x2, starting transfers between devices: 6.95 us -> 11 us  [exchange(): return lax.all_to_all(values, axes, split_axis=0, concat_axis=0, tiled=True)]
    all_to_all x2, waiting for transfers between devices: 1.81 us -> 3.92 us  [exchange(): return lax.all_to_all(values, axes, split_axis=0, concat_axis=0, tiled=True)]
  transfers between devices with their start and end apart: 18 -> 25, of which waited for: 15 -> 16; matrix products, arithmetic and copies ran while one was open for 3% -> 4% of each run, Pallas kernels for 8% -> 6%
where the time goes in v10:
time: 123 us
  waiting for transfers between devices  45.3 us (37%)
  starting transfers between devices  44.2 us (36%)
  Pallas kernels  19.9 us (16%)
  local copies, waits for them, and re-layouts  8.11 us (7%)
  other arithmetic  4.32 us (4%)
    ppermute x23, waiting for transfers between devices, swap(): lax.ppermute(values, both, [(here, here ^ mask) for here in range(devices...  41.4 us
    ppermute x23, starting transfers between devices, swap(): lax.ppermute(values, both, [(here, here ^ mask) for here in range(devices...  33.2 us
    all_to_all x2, starting transfers between devices, exchange(): return lax.all_to_all(values, axes, split_axis=0, concat_axis=0, tiled=True)  11 us
    pallas_call x1, Pallas kernels, on_device(): call(functools.partial(backward_body, plan, table_size, total_factor), ou...  8.88 us
    unnamed x25, local copies, waits for them, and re-layouts  6.37 us
    pallas_call x1, Pallas kernels, on_device(): call(functools.partial(forward_body, plan.capacity), [shapes[name] for na...  5.52 us
    all_to_all x2, waiting for transfers between devices, exchange(): return lax.all_to_all(values, axes, split_axis=0, concat_axis=0, tiled=True)  3.92 us
    convert_element_type x8, other arithmetic, add(): return (left.astype(F32) + right.astype(F32)).astype(BF16)  2.78 us
  transfers between devices with their start and end apart: 25, of which 16 were waited for; matrix products, arithmetic and copies ran while one was open for 4% of the time, Pallas kernels for 6%

profile of v10, /device:TPU:0, one launch (start us, length us, event | category | flops | bytes accessed | tf_op | source)
XLA Modules:
  0.0 122.7 jit_solution(17173505085724995409)
XLA Ops:
  0.6 1.3 %compare_select_fusion = s32[8,1,8]{2,1,0:T(1,128)} fusion(s32[8]{0:T(128)} %blocks_ref.1, s32[8]{0:T(128)} %dest_ref.1), kind=kLoop, calls=%fused_computation.15 | loop fusion | flops 128 | bytes 320 | tf_op jit(solution)/shard_map/jit(_where)/select_n | solution.py:445
  1.9 7.3 %all-to-all-start = ((s32[8,1,8]{2,1,0:T(1,128)}), s32[8,1,8]{2,1,0:T(1,128)S(1)}, u32[]{:S(2)}, u32[]{:S(2)}) async-start(s32[8,1,8]{2,1,0:T(1,128)} %compare_select_fusion), calls=%async_computation | async-start | bytes 8192 | tf_op jit(solution)/shard_map/all_to_all | solution.py:442
  9.2 0.8 copy.19.number_ref
  10.0 0.8 copy.18.owner_col_ref
  10.8 0.8 copy.17.item_ref
  11.6 3.9 %all-to-all-done.lengths_ref = s32[8,1,8]{2,1,0:T(1,128)S(1)} async-done(((s32[8,1,8]{2,1,0:T(1,128)}), s32[8,1,8]{2,1,0:T(1,128)S(1)}, u32[]{:S(2)}, u32[]{:S(2)}) %all-to-all-start) | async-done | bytes 288 | tf_op jit(solution)/shard_map/all_to_all | solution.py:442
  15.5 0.9 copy-done
  16.5 0.7 shard_map.146
  17.8 2.4 %collective-permute-start.4 = (bf16[64,512]{1,0:T(8,128)(2,1)S(1)}, bf16[64,512]{1,0:T(8,128)(2,1)S(1)}, u32[]{:S(2)}, u32[]{:S(2)}) collective-permute-start(bf16[64,512]{1,0:T(8,128)(2,1)S(1)} %get-tuple-element.80), channel_id=1, source_target_pairs={{0,20},{1,21},{2,22},{3,23},{4,16},{5,17},{6,18},{7,19},{8,28},{9,... | collective-permute-start | bytes 196616 | tf_op jit(solution)/shard_map/ppermute | solution.py:439
  20.2 0.8 collective-permute-start.5
  21.0 3.9 %collective-permute-start.6 = (bf16[64,512]{1,0:T(8,128)(2,1)S(1)}, bf16[64,512]{1,0:T(8,128)(2,1)S(1)}, u32[]{:S(2)}, u32[]{:S(2)}) collective-permute-start(bf16[64,512]{1,0:T(8,128)(2,1)S(1)} %get-tuple-element.82), channel_id=1, source_target_pairs={{0,28},{1,29},{2,30},{3,31},{4,24},{5,25},{6,26},{7,27},{8,20},{9,... | collective-permute-start | bytes 196616 | tf_op jit(solution)/shard_map/ppermute | solution.py:439
  24.9 0.7 copy-done.2
  25.6 1.6 %copy-done.5 = bf16[512,2048]{1,0:T(8,128)(2,1)S(1)} copy-done((bf16[512,2048]{1,0:T(8,128)(2,1)S(1)}, bf16[512,2048]{1,0:T(8,128)(2,1)}, u32[]{:S(2)}) %copy-start.5) | copy-done | bytes 2097176
  27.2 0.9 copy-done.8
  28.1 0.7 copy-done.9
  28.8 0.7 copy-done.11
  29.5 5.5 %shard_map.147 = (f32[512,512]{1,0:T(8,128)S(1)}, f32[512,512]{1,0:T(8,128)S(1)}, f32[512,1]{1,0:T(8,128)S(1)}, bf16[512,1536]{1,0:T(8,128)(2,1)S(1)}, bf16[16,1...) custom-call(bf16[256,512]{1,0:T(8,128)(2,1)S(1)} %copy-done.8, ...), custom_call_target="tpu_custom_call" | custom-call | flops 5368709120 | bytes 10000000 | tf_op jit(solution)/shard_map/pallas_call | solution.py:459
  35.7 2.9 %collective-permute-start.2 = (bf16[64,512]{1,0:T(8,128)(2,1)S(1)}, bf16[64,512]{1,0:T(8,128)(2,1)S(1)}, u32[]{:S(2)}, u32[]{:S(2)}) collective-permute-start(bf16[64,512]{1,0:T(8,128)(2,1)S(1)} %get-tuple-element.78), channel_id=1, source_target_pairs={{0,12},{1,13},{2,14},{3,15},{4,8},{5,9},{6,10},{7,11},{8,4},{9,5},... | collective-permute-start | bytes 196616 | tf_op jit(solution)/shard_map/ppermute | solution.py:439
  38.6 0.8 collective-permute-done.refs_17_
  40.0 1.6 %collective-permute-done.2.refs_19_ = bf16[64,512]{1,0:T(8,128)(2,1)S(1)} collective-permute-done((bf16[64,512]{1,0:T(8,128)(2,1)S(1)}, bf16[64,512]{1,0:T(8,128)(2,1)S(1)}, u32[]{:S(2)}, u32[]{:S(2)}) %collective-permute-start.2) | collective-permute-done | bytes 65568 | tf_op jit(solution)/shard_map/ppermute | solution.py:439
  41.6 8.9 %shard_map.148 = (bf16[512,640]{1,0:T(8,128)(2,1)}, bf16[16,16,1280]{2,1,0:T(8,128)(2,1)S(1)}, bf16[16,16,1280]{2,1,0:T(8,128)(2,1)S(1)}, bf16[16,16,1280]{2,1,0:T(8,128)(2,1)S(1)}, bf16[16,16,1280]{2,1,0:T(8,128)(2,1)S(1)}) custom-call(s32[1]{0:T(128)} %bitcast.me_ref, s32[8]{0:T(128)S(1)} %copy-done.3, s32[8]{0:T(128)S(1)} %copy-done.4, ...), custom_call_target="tpu_custom_call" | custom-call | flops 10737418240 | bytes 12000000 | tf_op jit(solution)/shard_map/pallas_call | solution.py:485
  51.0 3.7 %all-to-all-start.1 = ((bf16[32,16,640]{2,1,0:T(8,128)(2,1)}), bf16[32,16,640]{2,1,0:T(8,128)(2,1)S(1)}, u32[]{:S(2)}, u32[]{:S(2)}) async-start(bf16[32,16,640]{2,1,0:T(8,128)(2,1)} %bitcast.7), calls=%async_computation.1 | async-start | bytes 1310720 | tf_op jit(solution)/shard_map/all_to_all | solution.py:442
  54.7 1.2 %add_convert_fusion.1 = bf16[16,16,1280]{2,1,0:T(8,128)(2,1)S(1)} fusion(bf16[16,16,1280]{2,1,0:T(8,128)(2,1)} %collective-permute-done.7, bf16[16,16,1280]{2,1,0:T(8,128)(2,1)S(1)} %get-tuple-element.83), kind=kLoop, calls=%fused_computation.1 | loop fusion | flops 1310720 | bytes 1966080 | tf_op jit(solution)/shard_map/convert_element_type | solution.py:412
  56.0 1.7 %collective-permute-start.8 = (bf16[8,16,1280]{2,1,0:T(8,128)(2,1)S(1)}, bf16[8,16,1280]{2,1,0:T(8,128)(2,1)S(1)}, u32[]{:S(2)}, u32[]{:S(2)}) collective-permute-start(bf16[8,16,1280]{2,1,0:T(8,128)(2,1)S(1)} %slice.57), channel_id=1, source_target_pairs={{0,2},{1,3},{2,0},{3,1},{4,6},{5,7},{6,4},{7,5},{8,10},{9,11},{10,... | collective-permute-start | bytes 983048 | tf_op jit(solution)/shard_map/ppermute | solution.py:439
  57.7 1.2 %add_convert_fusion = bf16[16,16,1280]{2,1,0:T(8,128)(2,1)S(1)} fusion(bf16[16,16,1280]{2,1,0:T(8,128)(2,1)} %collective-permute-done.10, bf16[16,16,1280]{2,1,0:T(8,128)(2,1)S(1)} %get-tuple-element.85), kind=kLoop, calls=%fused_computation | loop fusion | flops 1310720 | bytes 1966080 | tf_op jit(solution)/shard_map/convert_element_type | solution.py:412
  59.0 1.5 %collective-permute-start.11 = (bf16[8,16,1280]{2,1,0:T(8,128)(2,1)S(1)}, bf16[8,16,1280]{2,1,0:T(8,128)(2,1)S(1)}, u32[]{:S(2)}, u32[]{:S(2)}) collective-permute-start(bf16[8,16,1280]{2,1,0:T(8,128)(2,1)S(1)} %slice.61), channel_id=1, source_target_pairs={{0,4},{1,5},{2,6},{3,7},{4,0},{5,1},{6,2},{7,3},{8,12},{9,13},{10,... | collective-permute-start | bytes 983048 | tf_op jit(solution)/shard_map/ppermute | solution.py:439
  60.5 10.4 %collective-permute-done.8 = bf16[8,16,1280]{2,1,0:T(8,128)(2,1)S(1)} collective-permute-done((bf16[8,16,1280]{2,1,0:T(8,128)(2,1)S(1)}, bf16[8,16,1280]{2,1,0:T(8,128)(2,1)S(1)}, u32[]{:S(2)}, u32[]{:S(2)}) %collective-permute-start.8) | collective-permute-done | bytes 327712 | tf_op jit(solution)/shard_map/ppermute | solution.py:439
  71.0 1.3 %collective-permute-start.9 = (bf16[4,16,1280]{2,1,0:T(8,128)(2,1)S(1)}, bf16[4,16,1280]{2,1,0:T(8,128)(2,1)S(1)}, u32[]{:S(2)}, u32[]{:S(2)}) collective-permute-start(bf16[4,16,1280]{2,1,0:T(8,128)(2,1)S(1)} %slice.59), channel_id=1, source_target_pairs={{0,4},{1,5},{2,6},{3,7},{4,0},{5,1},{6,2},{7,3},{8,12},{9,13},{10,... | collective-permute-start | bytes 491528 | tf_op jit(solution)/shard_map/ppermute | solution.py:439
  73.0 3.9 %collective-permute-done.9 = bf16[4,16,1280]{2,1,0:T(8,128)(2,1)S(1)} collective-permute-done((bf16[4,16,1280]{2,1,0:T(8,128)(2,1)S(1)}, bf16[4,16,1280]{2,1,0:T(8,128)(2,1)S(1)}, u32[]{:S(2)}, u32[]{:S(2)}) %collective-permute-start.9) | collective-permute-done | bytes 163872 | tf_op jit(solution)/shard_map/ppermute | solution.py:439
  76.9 1.1 collective-permute-done.12
  78.1 1.5 %collective-permute-start.13 = (bf16[2,16,2560]{2,1,0:T(8,128)(2,1)S(1)}, bf16[2,16,2560]{2,1,0:T(8,128)(2,1)S(1)}, u32[]{:S(2)}, u32[]{:S(2)}) collective-permute-start(bf16[2,16,2560]{2,1,0:T(8,128)(2,1)S(1)} %slice.51), channel_id=1, source_target_pairs={{0,8},{1,9},{2,10},{3,11},{4,12},{5,13},{6,14},{7,15},{8,0},{9,1},... | collective-permute-start | bytes 491528 | tf_op jit(solution)/shard_map/ppermute | solution.py:439
  79.6 3.9 %collective-permute-done.13 = bf16[2,16,2560]{2,1,0:T(8,128)(2,1)S(1)} collective-permute-done((bf16[2,16,2560]{2,1,0:T(8,128)(2,1)S(1)}, bf16[2,16,2560]{2,1,0:T(8,128)(2,1)S(1)}, u32[]{:S(2)}, u32[]{:S(2)}) %collective-permute-start.13) | collective-permute-done | bytes 163872 | tf_op jit(solution)/shard_map/ppermute | solution.py:439
  83.5 3.6 %collective-permute-start.14 = (bf16[1,16,2560]{2,1,0:T(8,128)(2,1)S(1)}, bf16[1,16,2560]{2,1,0:T(8,128)(2,1)S(1)}, u32[]{:S(2)}, u32[]{:S(2)}) collective-permute-start(bf16[1,16,2560]{2,1,0:T(8,128)(2,1)S(1)} %slice.65), channel_id=1, source_target_pairs={{0,16},{1,17},{2,18},{3,19},{4,20},{5,21},{6,22},{7,23},{8,24},{9,... | collective-permute-start | bytes 245768 | tf_op jit(solution)/shard_map/ppermute | solution.py:439
  87.2 2.4 %collective-permute-done.14 = bf16[1,16,2560]{2,1,0:T(8,128)(2,1)S(1)} collective-permute-done((bf16[1,16,2560]{2,1,0:T(8,128)(2,1)S(1)}, bf16[1,16,2560]{2,1,0:T(8,128)(2,1)S(1)}, u32[]{:S(2)}, u32[]{:S(2)}) %collective-permute-start.14) | collective-permute-done | bytes 81952 | tf_op jit(solution)/shard_map/ppermute | solution.py:439
  89.6 3.1 %collective-permute-start.15 = (bf16[1,16,2560]{2,1,0:T(8,128)(2,1)S(1)}, bf16[1,16,2560]{2,1,0:T(8,128)(2,1)S(1)}, u32[]{:S(2)}, u32[]{:S(2)}) collective-permute-start(bf16[1,16,2560]{2,1,0:T(8,128)(2,1)S(1)} %add_convert_fusion.7), channel_id=1, source_target_pairs={{0,16},{1,17},{2,18},{3,19},{4,20},{5,21},{6,22},{7,23},{8,24},{9,... | collective-permute-start | bytes 245768 | tf_op jit(solution)/shard_map/ppermute | solution.py:439
  92.7 2.7 %collective-permute-done.15 = bf16[1,16,2560]{2,1,0:T(8,128)(2,1)S(1)} collective-permute-done((bf16[1,16,2560]{2,1,0:T(8,128)(2,1)S(1)}, bf16[1,16,2560]{2,1,0:T(8,128)(2,1)S(1)}, u32[]{:S(2)}, u32[]{:S(2)}) %collective-permute-start.15) | collective-permute-done | bytes 81952 | tf_op jit(solution)/shard_map/ppermute | solution.py:439
  95.5 3.9 %collective-permute-start.16 = (bf16[2,16,2560]{2,1,0:T(8,128)(2,1)S(1)}, bf16[2,16,2560]{2,1,0:T(8,128)(2,1)S(1)}, u32[]{:S(2)}, u32[]{:S(2)}) collective-permute-start(bf16[2,16,2560]{2,1,0:T(8,128)(2,1)S(1)} %pad_maximum_fusion.6), channel_id=1, source_target_pairs={{0,8},{1,9},{2,10},{3,11},{4,12},{5,13},{6,14},{7,15},{8,0},{9,1},... | collective-permute-start | bytes 491528 | tf_op jit(solution)/shard_map/ppermute | solution.py:439
  99.4 2.2 %shard_map.149 = (f32[1024,512]{1,0:T(8,128)}, f32[1,512]{1,0:T(1,128)}, f32[1,512]{1,0:T(1,128)}) custom-call(bf16[512,640]{1,0:T(8,128)(2,1)S(1)} %bitcast.11), custom_call_target="tpu_custom_call" | custom-call | tf_op jit(solution)/shard_map/pallas_call | solution.py:522
  101.5 1.1 collective-permute-done.16
  103.2 1.4 %collective-permute-start.20 = (bf16[4,16,1280]{2,1,0:T(8,128)(2,1)S(1)}, bf16[4,16,1280]{2,1,0:T(8,128)(2,1)S(1)}, u32[]{:S(2)}, u32[]{:S(2)}) collective-permute-start(bf16[4,16,1280]{2,1,0:T(8,128)(2,1)S(1)} %get-tuple-element.97), channel_id=1, source_target_pairs={{0,2},{1,3},{2,0},{3,1},{4,6},{5,7},{6,4},{7,5},{8,10},{9,11},{10,... | collective-permute-start | bytes 491528 | tf_op jit(solution)/shard_map/ppermute | solution.py:439
  104.6 5.0 %collective-permute-done.17 = bf16[4,16,1280]{2,1,0:T(8,128)(2,1)S(1)} collective-permute-done((bf16[4,16,1280]{2,1,0:T(8,128)(2,1)S(1)}, bf16[4,16,1280]{2,1,0:T(8,128)(2,1)S(1)}, u32[]{:S(2)}, u32[]{:S(2)}) %collective-permute-start.17) | collective-permute-done | bytes 163872 | tf_op jit(solution)/shard_map/ppermute | solution.py:439
  109.6 1.1 collective-permute-start.18
  110.7 1.2 collective-permute-start.21
  111.9 4.8 %collective-permute-done.18 = bf16[8,16,1280]{2,1,0:T(8,128)(2,1)S(1)} collective-permute-done((bf16[8,16,1280]{2,1,0:T(8,128)(2,1)S(1)}, bf16[8,16,1280]{2,1,0:T(8,128)(2,1)S(1)}, u32[]{:S(2)}, u32[]{:S(2)}) %collective-permute-start.18) | collective-permute-done | bytes 327712 | tf_op jit(solution)/shard_map/ppermute | solution.py:439
  116.9 1.0 collective-permute-done.21
  118.0 1.0 collective-permute-done.19.refs_1_
  119.0 1.1 collective-permute-done.22.refs_3_
  120.1 2.6 %shard_map.150 = (f32[512,2048]{1,0:T(8,128)}, f32[512,512]{1,0:T(8,128)}) custom-call(s32[1]{0:T(128)} %bitcast.me_ref, bf16[16,16,1280]{2,1,0:T(8,128)(2,1)S(1)} %pad_maximum_fusion.refs_0_, bf16[16,16,1280]{2,1,0:T(8,128)(2,1)S(1)} %collective-permute-done.19.refs_1_, bf16[16,16,1280]{2,1,0:T(8,128)(2,1)S(1)} %pad_maximum_fusion.1.refs_2_, ...), custom_call_target="tpu_custom_call" | custom-call | tf_op jit(solution)/shard_map/pallas_call | solution.py:539
  (57 shorter events, 4.2 us)
Async XLA Ops:
  1.9 13.6 %all-to-all-start = ((s32[8,1,8]{2,1,0:T(1,128)}), s32[8,1,8]{2,1,0:T(1,128)S(1)}, u32[]{:S(2)}, u32[]{:S(2)}) async-start(s32[8,1,8]{2,1,0:T(1,128)} %compare_select_fusion), calls=%async_computation | async-start | bytes 8192 | tf_op jit(solution)/shard_map/all_to_all | solution.py:442
  15.5 1.0 copy-start
  17.2 18.5 %collective-permute-start.3 = (bf16[64,512]{1,0:T(8,128)(2,1)S(1)}, bf16[64,512]{1,0:T(8,128)(2,1)S(1)}, u32[]{:S(2)}, u32[]{:S(2)}) collective-permute-start(bf16[64,512]{1,0:T(8,128)(2,1)S(1)} %get-tuple-element.79), channel_id=1, source_target_pairs={{0,16},{1,17},{2,18},{3,19},{4,20},{5,21},{6,22},{7,23},{8,24},{9,... | collective-permute-start | bytes 196616 | tf_op jit(solution)/shard_map/ppermute | solution.py:439
  17.8 17.9 %collective-permute-start.4 = (bf16[64,512]{1,0:T(8,128)(2,1)S(1)}, bf16[64,512]{1,0:T(8,128)(2,1)S(1)}, u32[]{:S(2)}, u32[]{:S(2)}) collective-permute-start(bf16[64,512]{1,0:T(8,128)(2,1)S(1)} %get-tuple-element.80), channel_id=1, source_target_pairs={{0,20},{1,21},{2,22},{3,23},{4,16},{5,17},{6,18},{7,19},{8,28},{9,... | collective-permute-start | bytes 196616 | tf_op jit(solution)/shard_map/ppermute | solution.py:439
  20.2 18.4 %collective-permute-start.5 = (bf16[64,512]{1,0:T(8,128)(2,1)S(1)}, bf16[64,512]{1,0:T(8,128)(2,1)S(1)}, u32[]{:S(2)}, u32[]{:S(2)}) collective-permute-start(bf16[64,512]{1,0:T(8,128)(2,1)S(1)} %get-tuple-element.81), channel_id=1, source_target_pairs={{0,24},{1,25},{2,26},{3,27},{4,28},{5,29},{6,30},{7,31},{8,16},{9,... | collective-permute-start | bytes 196616 | tf_op jit(solution)/shard_map/ppermute | solution.py:439
  21.0 17.6 %collective-permute-start.6 = (bf16[64,512]{1,0:T(8,128)(2,1)S(1)}, bf16[64,512]{1,0:T(8,128)(2,1)S(1)}, u32[]{:S(2)}, u32[]{:S(2)}) collective-permute-start(bf16[64,512]{1,0:T(8,128)(2,1)S(1)} %get-tuple-element.82), channel_id=1, source_target_pairs={{0,28},{1,29},{2,30},{3,31},{4,24},{5,25},{6,26},{7,27},{8,20},{9,... | collective-permute-start | bytes 196616 | tf_op jit(solution)/shard_map/ppermute | solution.py:439
  24.9 0.7 copy-start.2
  25.6 1.6 %copy-start.5 = (bf16[512,2048]{1,0:T(8,128)(2,1)S(1)}, bf16[512,2048]{1,0:T(8,128)(2,1)}, u32[]{:S(2)}) copy-start(bf16[512,2048]{1,0:T(8,128)(2,1)} %refs_11_.1) | copy-start | bytes 6291460
  27.2 0.9 copy-start.8
  28.1 0.7 copy-start.9
  28.8 0.7 copy-start.11
  29.5 12.1 %copy-start.1 = (s32[512]{0:T(512)S(1)}, s32[512]{0:T(512)}, u32[]{:S(2)}) copy-start(s32[512]{0:T(512)} %param.12) | copy-start | bytes 6148
  29.5 12.1 %copy-start.3 = (s32[8]{0:T(128)S(1)}, s32[8]{0:T(128)}, u32[]{:S(2)}) copy-start(s32[8]{0:T(128)} %dest_ref.1) | copy-start | bytes 100
  29.5 12.1 %copy-start.4 = (s32[8]{0:T(128)S(1)}, s32[8]{0:T(128)}, u32[]{:S(2)}) copy-start(s32[8]{0:T(128)} %blocks_ref.1) | copy-start | bytes 100
  29.5 12.1 %copy-start.6 = (bf16[512,2048]{1,0:T(8,128)(2,1)S(1)}, bf16[512,2048]{1,0:T(8,128)(2,1)}, u32[]{:S(2)}) copy-start(bf16[512,2048]{1,0:T(8,128)(2,1)} %refs_11_.1) | copy-start | bytes 6291460
  29.5 12.1 %copy-start.7 = (bf16[512,512]{1,0:T(8,128)(2,1)S(1)}, bf16[512,512]{1,0:T(8,128)(2,1)}, u32[]{:S(2)}) copy-start(bf16[512,512]{1,0:T(8,128)(2,1)} %refs_0_.1) | copy-start | bytes 1572868
  29.5 12.1 %copy-start.10 = (f32[512]{0:T(512)S(1)}, f32[512]{0:T(512)}, u32[]{:S(2)}) copy-start(f32[512]{0:T(512)} %param.20) | copy-start | bytes 6148
  35.1 4.3 %collective-permute-start = (bf16[64,512]{1,0:T(8,128)(2,1)S(1)}, bf16[64,512]{1,0:T(8,128)(2,1)S(1)}, u32[]{:S(2)}, u32[]{:S(2)}) collective-permute-start(bf16[64,512]{1,0:T(8,128)(2,1)S(1)} %get-tuple-element.76), channel_id=1, source_target_pairs={{0,4},{1,5},{2,6},{3,7},{4,0},{5,1},{6,2},{7,3},{8,12},{9,13},{10,... | collective-permute-start | bytes 196616 | tf_op jit(solution)/shard_map/ppermute | solution.py:439
  35.7 4.3 %collective-permute-start.1 = (bf16[64,512]{1,0:T(8,128)(2,1)S(1)}, bf16[64,512]{1,0:T(8,128)(2,1)S(1)}, u32[]{:S(2)}, u32[]{:S(2)}) collective-permute-start(bf16[64,512]{1,0:T(8,128)(2,1)S(1)} %get-tuple-element.77), channel_id=1, source_target_pairs={{0,8},{1,9},{2,10},{3,11},{4,12},{5,13},{6,14},{7,15},{8,0},{9,1},... | collective-permute-start | bytes 196616 | tf_op jit(solution)/shard_map/ppermute | solution.py:439
  35.7 5.9 %collective-permute-start.2 = (bf16[64,512]{1,0:T(8,128)(2,1)S(1)}, bf16[64,512]{1,0:T(8,128)(2,1)S(1)}, u32[]{:S(2)}, u32[]{:S(2)}) collective-permute-start(bf16[64,512]{1,0:T(8,128)(2,1)S(1)} %get-tuple-element.78), channel_id=1, source_target_pairs={{0,12},{1,13},{2,14},{3,15},{4,8},{5,9},{6,10},{7,11},{8,4},{9,5},... | collective-permute-start | bytes 196616 | tf_op jit(solution)/shard_map/ppermute | solution.py:439
  50.5 4.2 %collective-permute-start.7 = (bf16[16,16,1280]{2,1,0:T(8,128)(2,1)S(1)}, bf16[16,16,1280]{2,1,0:T(8,128)(2,1)}, u32[]{:S(2)}, u32[]{:S(2)}) collective-permute-start(bf16[16,16,1280]{2,1,0:T(8,128)(2,1)S(1)} %get-tuple-element.84), channel_id=1, source_target_pairs={{0,1},{1,0},{2,3},{3,2},{4,5},{5,4},{6,7},{7,6},{8,9},{9,8},{10,11... | collective-permute-start | bytes 1966088 | tf_op jit(solution)/shard_map/ppermute | solution.py:439
  50.5 7.2 %collective-permute-start.10 = (bf16[16,16,1280]{2,1,0:T(8,128)(2,1)S(1)}, bf16[16,16,1280]{2,1,0:T(8,128)(2,1)}, u32[]{:S(2)}, u32[]{:S(2)}) collective-permute-start(bf16[16,16,1280]{2,1,0:T(8,128)(2,1)S(1)} %get-tuple-element.86), channel_id=1, source_target_pairs={{0,1},{1,0},{2,3},{3,2},{4,5},{5,4},{6,7},{7,6},{8,9},{9,8},{10,11... | collective-permute-start | bytes 1966088 | tf_op jit(solution)/shard_map/ppermute | solution.py:439
  51.0 27.1 %all-to-all-start.1 = ((bf16[32,16,640]{2,1,0:T(8,128)(2,1)}), bf16[32,16,640]{2,1,0:T(8,128)(2,1)S(1)}, u32[]{:S(2)}, u32[]{:S(2)}) async-start(bf16[32,16,640]{2,1,0:T(8,128)(2,1)} %bitcast.7), calls=%async_computation.1 | async-start | bytes 1310720 | tf_op jit(solution)/shard_map/all_to_all | solution.py:442
  56.0 14.9 %collective-permute-start.8 = (bf16[8,16,1280]{2,1,0:T(8,128)(2,1)S(1)}, bf16[8,16,1280]{2,1,0:T(8,128)(2,1)S(1)}, u32[]{:S(2)}, u32[]{:S(2)}) collective-permute-start(bf16[8,16,1280]{2,1,0:T(8,128)(2,1)S(1)} %slice.57), channel_id=1, source_target_pairs={{0,2},{1,3},{2,0},{3,1},{4,6},{5,7},{6,4},{7,5},{8,10},{9,11},{10,... | collective-permute-start | bytes 983048 | tf_op jit(solution)/shard_map/ppermute | solution.py:439
  59.0 13.3 %collective-permute-start.11 = (bf16[8,16,1280]{2,1,0:T(8,128)(2,1)S(1)}, bf16[8,16,1280]{2,1,0:T(8,128)(2,1)S(1)}, u32[]{:S(2)}, u32[]{:S(2)}) collective-permute-start(bf16[8,16,1280]{2,1,0:T(8,128)(2,1)S(1)} %slice.61), channel_id=1, source_target_pairs={{0,4},{1,5},{2,6},{3,7},{4,0},{5,1},{6,2},{7,3},{8,12},{9,13},{10,... | collective-permute-start | bytes 983048 | tf_op jit(solution)/shard_map/ppermute | solution.py:439
  71.0 5.8 %collective-permute-start.9 = (bf16[4,16,1280]{2,1,0:T(8,128)(2,1)S(1)}, bf16[4,16,1280]{2,1,0:T(8,128)(2,1)S(1)}, u32[]{:S(2)}, u32[]{:S(2)}) collective-permute-start(bf16[4,16,1280]{2,1,0:T(8,128)(2,1)S(1)} %slice.59), channel_id=1, source_target_pairs={{0,4},{1,5},{2,6},{3,7},{4,0},{5,1},{6,2},{7,3},{8,12},{9,13},{10,... | collective-permute-start | bytes 491528 | tf_op jit(solution)/shard_map/ppermute | solution.py:439
  72.4 5.6 %collective-permute-start.12 = (bf16[4,16,1280]{2,1,0:T(8,128)(2,1)S(1)}, bf16[4,16,1280]{2,1,0:T(8,128)(2,1)S(1)}, u32[]{:S(2)}, u32[]{:S(2)}) collective-permute-start(bf16[4,16,1280]{2,1,0:T(8,128)(2,1)S(1)} %slice.63), channel_id=1, source_target_pairs={{0,2},{1,3},{2,0},{3,1},{4,6},{5,7},{6,4},{7,5},{8,10},{9,11},{10,... | collective-permute-start | bytes 491528 | tf_op jit(solution)/shard_map/ppermute | solution.py:439
  78.1 5.4 %collective-permute-start.13 = (bf16[2,16,2560]{2,1,0:T(8,128)(2,1)S(1)}, bf16[2,16,2560]{2,1,0:T(8,128)(2,1)S(1)}, u32[]{:S(2)}, u32[]{:S(2)}) collective-permute-start(bf16[2,16,2560]{2,1,0:T(8,128)(2,1)S(1)} %slice.51), channel_id=1, source_target_pairs={{0,8},{1,9},{2,10},{3,11},{4,12},{5,13},{6,14},{7,15},{8,0},{9,1},... | collective-permute-start | bytes 491528 | tf_op jit(solution)/shard_map/ppermute | solution.py:439
  83.5 6.1 %collective-permute-start.14 = (bf16[1,16,2560]{2,1,0:T(8,128)(2,1)S(1)}, bf16[1,16,2560]{2,1,0:T(8,128)(2,1)S(1)}, u32[]{:S(2)}, u32[]{:S(2)}) collective-permute-start(bf16[1,16,2560]{2,1,0:T(8,128)(2,1)S(1)} %slice.65), channel_id=1, source_target_pairs={{0,16},{1,17},{2,18},{3,19},{4,20},{5,21},{6,22},{7,23},{8,24},{9,... | collective-permute-start | bytes 245768 | tf_op jit(solution)/shard_map/ppermute | solution.py:439
  89.6 5.8 %collective-permute-start.15 = (bf16[1,16,2560]{2,1,0:T(8,128)(2,1)S(1)}, bf16[1,16,2560]{2,1,0:T(8,128)(2,1)S(1)}, u32[]{:S(2)}, u32[]{:S(2)}) collective-permute-start(bf16[1,16,2560]{2,1,0:T(8,128)(2,1)S(1)} %add_convert_fusion.7), channel_id=1, source_target_pairs={{0,16},{1,17},{2,18},{3,19},{4,20},{5,21},{6,22},{7,23},{8,24},{9,... | collective-permute-start | bytes 245768 | tf_op jit(solution)/shard_map/ppermute | solution.py:439
  95.5 7.2 %collective-permute-start.16 = (bf16[2,16,2560]{2,1,0:T(8,128)(2,1)S(1)}, bf16[2,16,2560]{2,1,0:T(8,128)(2,1)S(1)}, u32[]{:S(2)}, u32[]{:S(2)}) collective-permute-start(bf16[2,16,2560]{2,1,0:T(8,128)(2,1)S(1)} %pad_maximum_fusion.6), channel_id=1, source_target_pairs={{0,8},{1,9},{2,10},{3,11},{4,12},{5,13},{6,14},{7,15},{8,0},{9,1},... | collective-permute-start | bytes 491528 | tf_op jit(solution)/shard_map/ppermute | solution.py:439
  102.7 6.8 %collective-permute-start.17 = (bf16[4,16,1280]{2,1,0:T(8,128)(2,1)S(1)}, bf16[4,16,1280]{2,1,0:T(8,128)(2,1)S(1)}, u32[]{:S(2)}, u32[]{:S(2)}) collective-permute-start(bf16[4,16,1280]{2,1,0:T(8,128)(2,1)S(1)} %get-tuple-element.98), channel_id=1, source_target_pairs={{0,4},{1,5},{2,6},{3,7},{4,0},{5,1},{6,2},{7,3},{8,12},{9,13},{10,... | collective-permute-start | bytes 491528 | tf_op jit(solution)/shard_map/ppermute | solution.py:439
  103.2 7.5 %collective-permute-start.20 = (bf16[4,16,1280]{2,1,0:T(8,128)(2,1)S(1)}, bf16[4,16,1280]{2,1,0:T(8,128)(2,1)S(1)}, u32[]{:S(2)}, u32[]{:S(2)}) collective-permute-start(bf16[4,16,1280]{2,1,0:T(8,128)(2,1)S(1)} %get-tuple-element.97), channel_id=1, source_target_pairs={{0,2},{1,3},{2,0},{3,1},{4,6},{5,7},{6,4},{7,5},{8,10},{9,11},{10,... | collective-permute-start | bytes 491528 | tf_op jit(solution)/shard_map/ppermute | solution.py:439
  109.6 7.1 %collective-permute-start.18 = (bf16[8,16,1280]{2,1,0:T(8,128)(2,1)S(1)}, bf16[8,16,1280]{2,1,0:T(8,128)(2,1)S(1)}, u32[]{:S(2)}, u32[]{:S(2)}) collective-permute-start(bf16[8,16,1280]{2,1,0:T(8,128)(2,1)S(1)} %pad_maximum_fusion.4), channel_id=1, source_target_pairs={{0,2},{1,3},{2,0},{3,1},{4,6},{5,7},{6,4},{7,5},{8,10},{9,11},{10,... | collective-permute-start | bytes 983048 | tf_op jit(solution)/shard_map/ppermute | solution.py:439
  110.7 7.1 %collective-permute-start.21 = (bf16[8,16,1280]{2,1,0:T(8,128)(2,1)S(1)}, bf16[8,16,1280]{2,1,0:T(8,128)(2,1)S(1)}, u32[]{:S(2)}, u32[]{:S(2)}) collective-permute-start(bf16[8,16,1280]{2,1,0:T(8,128)(2,1)S(1)} %pad_maximum_fusion.5), channel_id=1, source_target_pairs={{0,4},{1,5},{2,6},{3,7},{4,0},{5,1},{6,2},{7,3},{8,12},{9,13},{10,... | collective-permute-start | bytes 983048 | tf_op jit(solution)/shard_map/ppermute | solution.py:439
  116.8 2.2 %collective-permute-start.19 = (bf16[16,16,1280]{2,1,0:T(8,128)(2,1)S(1)}, bf16[16,16,1280]{2,1,0:T(8,128)(2,1)S(1)}, u32[]{:S(2)}, u32[]{:S(2)}) collective-permute-start(bf16[16,16,1280]{2,1,0:T(8,128)(2,1)S(1)} %pad_maximum_fusion.refs_0_), channel_id=1, source_target_pairs={{0,1},{1,0},{2,3},{3,2},{4,5},{5,4},{6,7},{7,6},{8,9},{9,8},{10,11... | collective-permute-start | bytes 1966088 | tf_op jit(solution)/shard_map/ppermute | solution.py:439
  117.9 2.2 %collective-permute-start.22 = (bf16[16,16,1280]{2,1,0:T(8,128)(2,1)S(1)}, bf16[16,16,1280]{2,1,0:T(8,128)(2,1)S(1)}, u32[]{:S(2)}, u32[]{:S(2)}) collective-permute-start(bf16[16,16,1280]{2,1,0:T(8,128)(2,1)S(1)} %pad_maximum_fusion.1.refs_2_), channel_id=1, source_target_pairs={{0,1},{1,0},{2,3},{3,2},{4,5},{5,4},{6,7},{7,6},{8,9},{9,8},{10,11... | collective-permute-start | bytes 1966088 | tf_op jit(solution)/shard_map/ppermute | solution.py:439

commit v11 on v10

--- a/solution.py
+++ b/solution.py
@@ -58,12 +58,11 @@
     out_refs, begin_ref = refs[:-1], refs[-1]
     peers = len(out_refs)
     blocks = grad_ref.shape[0] // BLK
+    me = me_ref[0] // table_size
     begin = jnp.int32(0)
     for peer in range(peers):
         begin_ref[peer] = begin
-        for slot in range(peers):
-            begin = begin + lengths_ref[peer, 0, slot]
-    me = me_ref[0] // table_size
+        begin = begin + lengths_ref[peer, me]
     for apart, out_ref in enumerate(out_refs):
         begin = begin_ref[me ^ apart]
         for inner in range(LMAXB):
@@ -121,10 +120,9 @@
     rows_ref,
     item_ref,
     w_in_ref,
-    gain_in_ref,
-    gain_out_ref,
+    gains_ref,
     owner_col_ref,
-    owner_row_ref,
+    ints_ref,
     number_ref,
     *refs,
 ):
@@ -136,13 +134,15 @@
     rows_hat_ref, rows_scale_ref, place_ref, digits_ref = (held[name] for name in SAVED[10:])
     count, width = rows_ref.shape
     tokens = item_ref.shape[0]
-    across = jnp.broadcast_to(owner_row_ref[...], (count, count))
+    gain_in, gain_out = gains_ref[0:1, :], gains_ref[1:2, :]
+    owner_row = ints_ref[:, tokens:]
+    across = jnp.broadcast_to(owner_row, (count, count))
     down = jnp.broadcast_to(owner_col_ref[...], (count, count))
     sub = lax.broadcasted_iota(jnp.int32, (count, count), 0)
     lane = lax.broadcasted_iota(jnp.int32, (count, count), 1)
     earlier = jnp.where((across == down) & (sub < lane), 1.0, 0.0)
     rank = jnp.sum(earlier, axis=0, keepdims=True).astype(jnp.int32)
-    place_ref[...] = owner_row_ref[...] * capacity + rank
+    place_ref[...] = owner_row * capacity + rank
     number = jnp.broadcast_to(number_ref[...], (count, LANES))
     lane = lax.broadcasted_iota(jnp.int32, (count, LANES), 1)
     digits = jnp.where(lane == 0, number >> 5, jnp.where(lane == 1, number & 31, 0))
@@ -153,7 +153,7 @@
     hat = shifted * scale
     rows_hat_ref[...] = hat
     rows_scale_ref[...] = scale
-    normed = hat * gain_in_ref[...]
+    normed = hat * gain_in
     normed_t_ref[...] = normed.T.astype(BF16)
     normed = normed.astype(BF16)
     lane = lax.broadcasted_iota(jnp.int32, (tokens, count), 1)
@@ -199,14 +199,14 @@
         hat = shifted * scale
         hat_ref[rows, :] = hat
         hat_scale_ref[rows, :] = scale
-        mixed = hat * gain_out_ref[...] * gate_ref[rows, :]
+        mixed = hat * gain_out * gate_ref[rows, :]
         mixed_t_ref[:, rows] = mixed.T.astype(BF16)
 
 
-def gather_of(item_ref, count):
-    tokens = item_ref.shape[1]
+def gather_of(items, count):
+    tokens = items.shape[1]
     sub = lax.broadcasted_iota(jnp.int32, (count, tokens), 0)
-    hit = sub == jnp.broadcast_to(item_ref[...], (count, tokens))
+    hit = sub == jnp.broadcast_to(items, (count, tokens))
     return jnp.where(hit, 1.0, 0.0).astype(BF16)
 
 
@@ -237,9 +237,8 @@
     me_ref,
     dest_ref,
     blocks_ref,
-    item_ref,
-    gain_in_ref,
-    gain_out_ref,
+    ints_ref,
+    gains_ref,
     *refs,
 ):
     used, refs = dict(zip(USED, refs)), refs[len(USED) :]
@@ -264,15 +263,16 @@
         grad_y_ref[slot * SLOT : (slot + 1) * SLOT, :] = rows
     tokens, width = grad_y_ref.shape
     count = normed_t_ref.shape[1]
+    gain_in, gain_out = gains_ref[0:1, :], gains_ref[1:2, :]
     gain_total = jnp.zeros((1, width), F32)
     for tile in range(tokens // TILE):
         rows = slice(tile * TILE, (tile + 1) * TILE)
         grad_mixed = dot(grad_y_ref[rows, :], w_out_ref[...], NT)
         hat = hat_ref[rows, :]
-        active_ref[rows, :width] = (grad_mixed * hat * gain_out_ref[...]).astype(BF16)
+        active_ref[rows, :width] = (grad_mixed * hat * gain_out).astype(BF16)
         inner = grad_mixed * gate_ref[rows, :]
         gain_total = gain_total + jnp.sum(inner * hat, axis=0, keepdims=True)
-        inner = inner * gain_out_ref[...]
+        inner = inner * gain_out
         mean = jnp.mean(inner, axis=-1, keepdims=True)
         along = jnp.mean(inner * hat, axis=-1, keepdims=True)
         grad_att = ((inner - mean - hat * along) * hat_scale_ref[rows, :]).astype(BF16)
@@ -294,7 +294,7 @@
                 first = part * width + head * HDIM
                 active_ref[rows, first : first + HDIM] = value.astype(BF16)
     sums_ref[:, :width] = (dot(mixed_t_ref[...], grad_y_ref[...]) * factor).astype(BF16)
-    gather = gather_of(item_ref, count)
+    gather = gather_of(ints_ref[:, :tokens], count)
     grad_normed = jnp.zeros((count, width), F32)
     for part in range(4):
         columns = slice(part * width, (part + 1) * width)
@@ -307,7 +307,7 @@
     hat = rows_hat_ref[...]
     gains = (jnp.sum(grad_normed * hat, axis=0, keepdims=True) * factor, gain_total * factor)
     plan.write(me_ref[0], sums_ref, part_refs)
-    inner = grad_normed * gain_in_ref[...]
+    inner = grad_normed * gain_in
     mean = jnp.mean(inner, axis=-1, keepdims=True)
     along = jnp.mean(inner * hat, axis=-1, keepdims=True)
     row_grad = (inner - mean - hat * along) * rows_scale_ref[...] + dot(gather, grad_y_ref[...])
@@ -432,7 +432,8 @@
     plan = Plan(dp_size, table_size, count, width)
     devices_all = plan.chunks
     total_factor = 1.0 / math.sqrt(grad_out.shape[0] * devices_all)
-    gain_in, gain_out = gain_in[None, :], gain_out[None, :]
+    gain_rows = jnp.stack([gain_in, gain_out])
+    ints = jnp.concatenate([row_of_token, row_owner[:, 0]])[None, :]
     me = lax.axis_index(both).astype(jnp.int32)[None]
 
     def swap(values, mask):
@@ -441,25 +442,28 @@
     def exchange(values, axes):
         return lax.all_to_all(values, axes, split_axis=0, concat_axis=0, tiled=True)
 
-    peers = jnp.arange(dp_size, dtype=jnp.int32)[:, None, None]
-    lengths = jnp.where(seq_dest[None, None, :] == peers, seq_blocks[None, None, :], 0)
+    peers = jnp.arange(dp_size, dtype=jnp.int32)
+    own = jnp.sum(jnp.where(seq_dest[:, None] == peers, seq_blocks[:, None], 0), axis=0)
+    lengths = jnp.where(peers[:, None] == lax.axis_index("dp"), own, 0)
+    for bit in range(dp_size.bit_length() - 1):
+        lengths = lengths + swap(lengths, table_size << bit)
     send = call(
         functools.partial(send_body, table_size),
         [shape_of((SLOT, width), BF16)] * dp_size,
         [SMEM] * 2 + [VMEM],
         scratch=[pltpu.SMEM((dp_size,), jnp.int32)],
-    )(me, exchange(lengths, "dp"), grad_out)
+    )(me, lengths, grad_out)
     got = list(send)
     far = [apart for apart in range(1, dp_size) if 2 * apart >= dp_size]
     for apart in far:
         got[apart] = swap(send[apart], apart * table_size)
-    *near, touched_rows = lax.optimization_barrier((*send[: far[0]], touched_rows))
+    *near, ints = lax.optimization_barrier((*send[: far[0]], ints))
 
     shapes = saved_shapes(tokens, count, width)
     saved = call(
         functools.partial(forward_body, plan.capacity),
         [shapes[name] for name in SAVED],
-        [VMEM] * 8,
+        [VMEM] * 7,
         flops=4 * count * width * width * 20,
         moved=10_000_000,
         mebibytes=12 + tokens // 32,
@@ -467,10 +471,9 @@
         touched_rows,
         row_of_token.reshape(tokens, 1),
         w_in,
-        gain_in,
-        gain_out,
+        gain_rows,
         row_owner,
-        row_owner.reshape(1, count),
+        ints,
         owner_row.reshape(count, 1),
     )
     *near, gate = lax.optimization_barrier((*near, saved[0]))
@@ -485,7 +488,7 @@
     table_send, *parts = call(
         functools.partial(backward_body, plan, table_size, total_factor),
         outs,
-        [SMEM] * 3 + [VMEM] * (3 + len(USED) + dp_size),
+        [SMEM] * 3 + [VMEM] * (2 + len(USED) + dp_size),
         flops=4 * count * width * width * 40,
         moved=12_000_000,
         mebibytes=12 + tokens // 32,
@@ -499,9 +502,8 @@
         me,
         seq_dest,
         seq_blocks,
-        row_of_token.reshape(1, tokens),
-        gain_in,
-        gain_out,
+        ints,
+        gain_rows,
         *(saved[name] for name in USED),
         *got,
     )

time: 123 us -> 123 us (level)
  local copies, waits for them, and re-layouts: 8.11 us -> 6.06 us
  starting transfers between devices: 44.2 us -> 46 us
  waiting for transfers between devices: 45.3 us -> 43.9 us
    ppermute x23 -> x26, starting transfers between devices: 33.2 us -> 40.3 us  [swap(): lax.ppermute(values, both, [(here, here ^ mask) for here in range(devices...]
    all_to_all x2 -> x1, starting transfers between devices: 11 us -> 5.74 us  [exchange(): return lax.all_to_all(values, axes, split_axis=0, concat_axis=0, tiled=True)]
    all_to_all x2 -> x1, waiting for transfers between devices: 3.92 us -> 0.01 us  [exchange(): return lax.all_to_all(values, axes, split_axis=0, concat_axis=0, tiled=True)]
    ppermute x23 -> x26, waiting for transfers between devices: 41.4 us -> 43.9 us  [swap(): lax.ppermute(values, both, [(here, here ^ mask) for here in range(devices...]
    unnamed x25 -> x15, local copies, waits for them, and re-layouts: 6.37 us -> 4.31 us
  transfers between devices with their start and end apart: 25 -> 27, of which waited for: 16 -> 17; matrix products, arithmetic and copies ran while one was open for 4% -> 6% of each run, Pallas kernels for 6% -> 6%
where the time goes in v11:
time: 123 us; the launch traced here: 122 us
  starting transfers between devices  46 us (37%)
  waiting for transfers between devices  43.9 us (36%)
  Pallas kernels  19.8 us (16%)
  local copies, waits for them, and re-layouts  6.06 us (5%)
  other arithmetic  5.45 us (4%)
    ppermute x26, waiting for transfers between devices, swap(): lax.ppermute(values, both, [(here, here ^ mask) for here in range(devices...  43.9 us
    ppermute x26, starting transfers between devices, swap(): lax.ppermute(values, both, [(here, here ^ mask) for here in range(devices...  40.3 us
    pallas_call x1, Pallas kernels, on_device(): call(functools.partial(backward_body, plan, table_size, total_factor), ou...  8.85 us
    all_to_all x1, starting transfers between devices, exchange(): return lax.all_to_all(values, axes, split_axis=0, concat_axis=0, tiled=True)  5.74 us
    pallas_call x1, Pallas kernels, on_device(): call(functools.partial(forward_body, plan.capacity), [shapes[name] for na...  5.48 us
    unnamed x15, local copies, waits for them, and re-layouts  4.31 us
    convert_element_type x8, other arithmetic, add(): return (left.astype(F32) + right.astype(F32)).astype(BF16)  2.78 us
    pallas_call x1, Pallas kernels, on_device(): call(functools.partial(widen_body, plan), (shape_of(w_in.shape, F32), sha...  2.6 us
  transfers between devices with their start and end apart: 27, of which 17 were waited for; matrix products, arithmetic and copies ran while one was open for 6% of the time, Pallas kernels for 6%

profile of v11, /device:TPU:0, one launch (start us, length us, event | category | flops | bytes accessed | tf_op | source)
XLA Modules:
  0.0 122.1 jit_solution(12370757673038324315)
XLA Ops:
  0.6 0.8 select_reduce_fusion
  1.5 2.9 %collective-permute-start = (s32[8,8]{1,0:T(8,128)S(1)}, s32[8,8]{1,0:T(8,128)S(1)}, u32[]{:S(2)}, u32[]{:S(2)}) collective-permute-start(s32[8,8]{1,0:T(8,128)S(1)} %broadcast_select_fusion), channel_id=1, source_target_pairs={{0,4},{1,5},{2,6},{3,7},{4,0},{5,1},{6,2},{7,3},{8,12},{9,13},{10,... | collective-permute-start | bytes 776 | tf_op jit(solution)/shard_map/ppermute | solution.py:440
  5.8 0.8 copy.18.owner_col_ref
  6.7 1.6 %collective-permute-start.1 = (s32[8,8]{1,0:T(8,128)S(1)}, s32[8,8]{1,0:T(8,128)S(1)}, u32[]{:S(2)}, u32[]{:S(2)}) collective-permute-start(s32[8,8]{1,0:T(8,128)S(1)} %fusion), channel_id=1, source_target_pairs={{0,8},{1,9},{2,10},{3,11},{4,12},{5,13},{6,14},{7,15},{8,0},{9,1},... | collective-permute-start | bytes 776 | tf_op jit(solution)/shard_map/ppermute | solution.py:440
  8.3 2.0 %collective-permute-done.1 = s32[8,8]{1,0:T(8,128)S(1)} collective-permute-done((s32[8,8]{1,0:T(8,128)S(1)}, s32[8,8]{1,0:T(8,128)S(1)}, u32[]{:S(2)}, u32[]{:S(2)}) %collective-permute-start.1) | collective-permute-done | bytes 288 | tf_op jit(solution)/shard_map/ppermute | solution.py:440
  10.4 2.6 %collective-permute-start.2 = (s32[8,8]{1,0:T(8,128)S(1)}, s32[8,8]{1,0:T(8,128)S(1)}, u32[]{:S(2)}, u32[]{:S(2)}) collective-permute-start(s32[8,8]{1,0:T(8,128)S(1)} %fusion.2), channel_id=1, source_target_pairs={{0,16},{1,17},{2,18},{3,19},{4,20},{5,21},{6,22},{7,23},{8,24},{9,... | collective-permute-start | bytes 776 | tf_op jit(solution)/shard_map/ppermute | solution.py:440
  13.0 0.8 copy.19.number_ref
  13.8 0.8 copy.17.item_ref
  14.9 0.9 copy-done
  16.6 2.7 %collective-permute-start.6 = (bf16[64,512]{1,0:T(8,128)(2,1)S(1)}, bf16[64,512]{1,0:T(8,128)(2,1)S(1)}, u32[]{:S(2)}, u32[]{:S(2)}) collective-permute-start(bf16[64,512]{1,0:T(8,128)(2,1)S(1)} %get-tuple-element.79), channel_id=1, source_target_pairs={{0,16},{1,17},{2,18},{3,19},{4,20},{5,21},{6,22},{7,23},{8,24},{9,... | collective-permute-start | bytes 196616 | tf_op jit(solution)/shard_map/ppermute | solution.py:440
  19.2 1.1 collective-permute-start.7
  20.4 3.6 %collective-permute-start.8 = (bf16[64,512]{1,0:T(8,128)(2,1)S(1)}, bf16[64,512]{1,0:T(8,128)(2,1)S(1)}, u32[]{:S(2)}, u32[]{:S(2)}) collective-permute-start(bf16[64,512]{1,0:T(8,128)(2,1)S(1)} %get-tuple-element.81), channel_id=1, source_target_pairs={{0,24},{1,25},{2,26},{3,27},{4,28},{5,29},{6,30},{7,31},{8,16},{9,... | collective-permute-start | bytes 196616 | tf_op jit(solution)/shard_map/ppermute | solution.py:440
  24.3 1.6 %copy-done.1 = bf16[512,2048]{1,0:T(8,128)(2,1)S(1)} copy-done((bf16[512,2048]{1,0:T(8,128)(2,1)S(1)}, bf16[512,2048]{1,0:T(8,128)(2,1)}, u32[]{:S(2)}) %copy-start.1) | copy-done | bytes 2097176
  25.9 0.9 copy-done.4
  26.8 5.5 %shard_map.147 = (f32[512,512]{1,0:T(8,128)S(1)}, f32[512,512]{1,0:T(8,128)S(1)}, f32[512,1]{1,0:T(8,128)S(1)}, bf16[512,1536]{1,0:T(8,128)(2,1)S(1)}, bf16[16,1...) custom-call(bf16[256,512]{1,0:T(8,128)(2,1)S(1)} %copy-done.4, ...), custom_call_target="tpu_custom_call" | custom-call | flops 5368709120 | bytes 10000000 | tf_op jit(solution)/shard_map/pallas_call | solution.py:463
  32.3 1.4 %collective-permute-start.3 = (bf16[64,512]{1,0:T(8,128)(2,1)S(1)}, bf16[64,512]{1,0:T(8,128)(2,1)S(1)}, u32[]{:S(2)}, u32[]{:S(2)}) collective-permute-start(bf16[64,512]{1,0:T(8,128)(2,1)S(1)} %get-tuple-element.76), channel_id=1, source_target_pairs={{0,4},{1,5},{2,6},{3,7},{4,0},{5,1},{6,2},{7,3},{8,12},{9,13},{10,... | collective-permute-start | bytes 196616 | tf_op jit(solution)/shard_map/ppermute | solution.py:440
  33.8 2.1 %collective-permute-start.5 = (bf16[64,512]{1,0:T(8,128)(2,1)S(1)}, bf16[64,512]{1,0:T(8,128)(2,1)S(1)}, u32[]{:S(2)}, u32[]{:S(2)}) collective-permute-start(bf16[64,512]{1,0:T(8,128)(2,1)S(1)} %get-tuple-element.78), channel_id=1, source_target_pairs={{0,12},{1,13},{2,14},{3,15},{4,8},{5,9},{6,10},{7,11},{8,4},{9,5},... | collective-permute-start | bytes 196616 | tf_op jit(solution)/shard_map/ppermute | solution.py:440
  35.9 0.8 collective-permute-done.3.refs_17_
  36.7 1.4 %collective-permute-done.4.refs_18_ = bf16[64,512]{1,0:T(8,128)(2,1)S(1)} collective-permute-done((bf16[64,512]{1,0:T(8,128)(2,1)S(1)}, bf16[64,512]{1,0:T(8,128)(2,1)S(1)}, u32[]{:S(2)}, u32[]{:S(2)}) %collective-permute-start.4) | collective-permute-done | bytes 65568 | tf_op jit(solution)/shard_map/ppermute | solution.py:440
  38.0 1.0 collective-permute-done.5.refs_19_
  39.0 8.9 %shard_map.148 = (bf16[512,640]{1,0:T(8,128)(2,1)}, bf16[16,16,1280]{2,1,0:T(8,128)(2,1)S(1)}, bf16[16,16,1280]{2,1,0:T(8,128)(2,1)S(1)}, bf16[16,16,1280]{2,1,0:T(8,128)(2,1)S(1)}, bf16[16,16,1280]{2,1,0:T(8,128)(2,1)S(1)}) custom-call(s32[1]{0:T(128)} %bitcast.me_ref, s32[8]{0:T(128)S(1)} %copy-done.5, s32[8]{0:T(128)S(1)} %copy-done.6, ...), custom_call_target="tpu_custom_call" | custom-call | flops 10737418240 | bytes 12000000 | tf_op jit(solution)/shard_map/pallas_call | solution.py:488
  48.4 5.7 %all-to-all-start = ((bf16[32,16,640]{2,1,0:T(8,128)(2,1)}), bf16[32,16,640]{2,1,0:T(8,128)(2,1)S(1)}, u32[]{:S(2)}, u32[]{:S(2)}) async-start(bf16[32,16,640]{2,1,0:T(8,128)(2,1)} %bitcast.6), calls=%async_computation | async-start | bytes 1310720 | tf_op jit(solution)/shard_map/all_to_all | solution.py:443
  54.1 1.2 %add_convert_fusion.1 = bf16[16,16,1280]{2,1,0:T(8,128)(2,1)S(1)} fusion(bf16[16,16,1280]{2,1,0:T(8,128)(2,1)} %collective-permute-done.10, bf16[16,16,1280]{2,1,0:T(8,128)(2,1)S(1)} %get-tuple-element.83), kind=kLoop, calls=%fused_computation.1 | loop fusion | flops 1310720 | bytes 1966080 | tf_op jit(solution)/shard_map/convert_element_type | solution.py:412
  55.4 1.7 %collective-permute-start.11 = (bf16[8,16,1280]{2,1,0:T(8,128)(2,1)S(1)}, bf16[8,16,1280]{2,1,0:T(8,128)(2,1)S(1)}, u32[]{:S(2)}, u32[]{:S(2)}) collective-permute-start(bf16[8,16,1280]{2,1,0:T(8,128)(2,1)S(1)} %slice.57), channel_id=1, source_target_pairs={{0,2},{1,3},{2,0},{3,1},{4,6},{5,7},{6,4},{7,5},{8,10},{9,11},{10,... | collective-permute-start | bytes 983048 | tf_op jit(solution)/shard_map/ppermute | solution.py:440
  57.1 1.2 %add_convert_fusion = bf16[16,16,1280]{2,1,0:T(8,128)(2,1)S(1)} fusion(bf16[16,16,1280]{2,1,0:T(8,128)(2,1)} %collective-permute-done.13, bf16[16,16,1280]{2,1,0:T(8,128)(2,1)S(1)} %get-tuple-element.85), kind=kLoop, calls=%fused_computation | loop fusion | flops 1310720 | bytes 1966080 | tf_op jit(solution)/shard_map/convert_element_type | solution.py:412
  58.4 1.5 %collective-permute-start.14 = (bf16[8,16,1280]{2,1,0:T(8,128)(2,1)S(1)}, bf16[8,16,1280]{2,1,0:T(8,128)(2,1)S(1)}, u32[]{:S(2)}, u32[]{:S(2)}) collective-permute-start(bf16[8,16,1280]{2,1,0:T(8,128)(2,1)S(1)} %slice.61), channel_id=1, source_target_pairs={{0,4},{1,5},{2,6},{3,7},{4,0},{5,1},{6,2},{7,3},{8,12},{9,13},{10,... | collective-permute-start | bytes 983048 | tf_op jit(solution)/shard_map/ppermute | solution.py:440
  59.9 10.4 %collective-permute-done.11 = bf16[8,16,1280]{2,1,0:T(8,128)(2,1)S(1)} collective-permute-done((bf16[8,16,1280]{2,1,0:T(8,128)(2,1)S(1)}, bf16[8,16,1280]{2,1,0:T(8,128)(2,1)S(1)}, u32[]{:S(2)}, u32[]{:S(2)}) %collective-permute-start.11) | collective-permute-done | bytes 327712 | tf_op jit(solution)/shard_map/ppermute | solution.py:440
  70.4 1.3 %collective-permute-start.12 = (bf16[4,16,1280]{2,1,0:T(8,128)(2,1)S(1)}, bf16[4,16,1280]{2,1,0:T(8,128)(2,1)S(1)}, u32[]{:S(2)}, u32[]{:S(2)}) collective-permute-start(bf16[4,16,1280]{2,1,0:T(8,128)(2,1)S(1)} %slice.59), channel_id=1, source_target_pairs={{0,4},{1,5},{2,6},{3,7},{4,0},{5,1},{6,2},{7,3},{8,12},{9,13},{10,... | collective-permute-start | bytes 491528 | tf_op jit(solution)/shard_map/ppermute | solution.py:440
  72.4 3.9 %collective-permute-done.12 = bf16[4,16,1280]{2,1,0:T(8,128)(2,1)S(1)} collective-permute-done((bf16[4,16,1280]{2,1,0:T(8,128)(2,1)S(1)}, bf16[4,16,1280]{2,1,0:T(8,128)(2,1)S(1)}, u32[]{:S(2)}, u32[]{:S(2)}) %collective-permute-start.12) | collective-permute-done | bytes 163872 | tf_op jit(solution)/shard_map/ppermute | solution.py:440
  76.3 1.1 collective-permute-done.15
  77.5 1.5 %collective-permute-start.16 = (bf16[2,16,2560]{2,1,0:T(8,128)(2,1)S(1)}, bf16[2,16,2560]{2,1,0:T(8,128)(2,1)S(1)}, u32[]{:S(2)}, u32[]{:S(2)}) collective-permute-start(bf16[2,16,2560]{2,1,0:T(8,128)(2,1)S(1)} %slice.51), channel_id=1, source_target_pairs={{0,8},{1,9},{2,10},{3,11},{4,12},{5,13},{6,14},{7,15},{8,0},{9,1},... | collective-permute-start | bytes 491528 | tf_op jit(solution)/shard_map/ppermute | solution.py:440
  79.0 3.9 %collective-permute-done.16 = bf16[2,16,2560]{2,1,0:T(8,128)(2,1)S(1)} collective-permute-done((bf16[2,16,2560]{2,1,0:T(8,128)(2,1)S(1)}, bf16[2,16,2560]{2,1,0:T(8,128)(2,1)S(1)}, u32[]{:S(2)}, u32[]{:S(2)}) %collective-permute-start.16) | collective-permute-done | bytes 163872 | tf_op jit(solution)/shard_map/ppermute | solution.py:440
  83.0 3.6 %collective-permute-start.17 = (bf16[1,16,2560]{2,1,0:T(8,128)(2,1)S(1)}, bf16[1,16,2560]{2,1,0:T(8,128)(2,1)S(1)}, u32[]{:S(2)}, u32[]{:S(2)}) collective-permute-start(bf16[1,16,2560]{2,1,0:T(8,128)(2,1)S(1)} %slice.65), channel_id=1, source_target_pairs={{0,16},{1,17},{2,18},{3,19},{4,20},{5,21},{6,22},{7,23},{8,24},{9,... | collective-permute-start | bytes 245768 | tf_op jit(solution)/shard_map/ppermute | solution.py:440
  86.6 2.4 %collective-permute-done.17 = bf16[1,16,2560]{2,1,0:T(8,128)(2,1)S(1)} collective-permute-done((bf16[1,16,2560]{2,1,0:T(8,128)(2,1)S(1)}, bf16[1,16,2560]{2,1,0:T(8,128)(2,1)S(1)}, u32[]{:S(2)}, u32[]{:S(2)}) %collective-permute-start.17) | collective-permute-done | bytes 81952 | tf_op jit(solution)/shard_map/ppermute | solution.py:440
  89.0 3.1 %collective-permute-start.18 = (bf16[1,16,2560]{2,1,0:T(8,128)(2,1)S(1)}, bf16[1,16,2560]{2,1,0:T(8,128)(2,1)S(1)}, u32[]{:S(2)}, u32[]{:S(2)}) collective-permute-start(bf16[1,16,2560]{2,1,0:T(8,128)(2,1)S(1)} %add_convert_fusion.7), channel_id=1, source_target_pairs={{0,16},{1,17},{2,18},{3,19},{4,20},{5,21},{6,22},{7,23},{8,24},{9,... | collective-permute-start | bytes 245768 | tf_op jit(solution)/shard_map/ppermute | solution.py:440
  92.1 2.7 %collective-permute-done.18 = bf16[1,16,2560]{2,1,0:T(8,128)(2,1)S(1)} collective-permute-done((bf16[1,16,2560]{2,1,0:T(8,128)(2,1)S(1)}, bf16[1,16,2560]{2,1,0:T(8,128)(2,1)S(1)}, u32[]{:S(2)}, u32[]{:S(2)}) %collective-permute-start.18) | collective-permute-done | bytes 81952 | tf_op jit(solution)/shard_map/ppermute | solution.py:440
  94.9 3.9 %collective-permute-start.19 = (bf16[2,16,2560]{2,1,0:T(8,128)(2,1)S(1)}, bf16[2,16,2560]{2,1,0:T(8,128)(2,1)S(1)}, u32[]{:S(2)}, u32[]{:S(2)}) collective-permute-start(bf16[2,16,2560]{2,1,0:T(8,128)(2,1)S(1)} %pad_maximum_fusion.6), channel_id=1, source_target_pairs={{0,8},{1,9},{2,10},{3,11},{4,12},{5,13},{6,14},{7,15},{8,0},{9,1},... | collective-permute-start | bytes 491528 | tf_op jit(solution)/shard_map/ppermute | solution.py:440
  98.8 2.2 %shard_map.149 = (f32[1024,512]{1,0:T(8,128)}, f32[1,512]{1,0:T(1,128)}, f32[1,512]{1,0:T(1,128)}) custom-call(bf16[512,640]{1,0:T(8,128)(2,1)S(1)} %bitcast.10), custom_call_target="tpu_custom_call" | custom-call | tf_op jit(solution)/shard_map/pallas_call | solution.py:524
  100.9 1.1 collective-permute-done.19
  102.6 1.4 %collective-permute-start.23 = (bf16[4,16,1280]{2,1,0:T(8,128)(2,1)S(1)}, bf16[4,16,1280]{2,1,0:T(8,128)(2,1)S(1)}, u32[]{:S(2)}, u32[]{:S(2)}) collective-permute-start(bf16[4,16,1280]{2,1,0:T(8,128)(2,1)S(1)} %get-tuple-element.97), channel_id=1, source_target_pairs={{0,2},{1,3},{2,0},{3,1},{4,6},{5,7},{6,4},{7,5},{8,10},{9,11},{10,... | collective-permute-start | bytes 491528 | tf_op jit(solution)/shard_map/ppermute | solution.py:440
  104.0 5.0 %collective-permute-done.20 = bf16[4,16,1280]{2,1,0:T(8,128)(2,1)S(1)} collective-permute-done((bf16[4,16,1280]{2,1,0:T(8,128)(2,1)S(1)}, bf16[4,16,1280]{2,1,0:T(8,128)(2,1)S(1)}, u32[]{:S(2)}, u32[]{:S(2)}) %collective-permute-start.20) | collective-permute-done | bytes 163872 | tf_op jit(solution)/shard_map/ppermute | solution.py:440
  109.0 1.1 collective-permute-start.21
  110.1 1.2 collective-permute-start.24
  111.3 4.8 %collective-permute-done.21 = bf16[8,16,1280]{2,1,0:T(8,128)(2,1)S(1)} collective-permute-done((bf16[8,16,1280]{2,1,0:T(8,128)(2,1)S(1)}, bf16[8,16,1280]{2,1,0:T(8,128)(2,1)S(1)}, u32[]{:S(2)}, u32[]{:S(2)}) %collective-permute-start.21) | collective-permute-done | bytes 327712 | tf_op jit(solution)/shard_map/ppermute | solution.py:440
  116.3 1.0 collective-permute-done.24
  117.4 1.0 collective-permute-done.22.refs_1_
  118.4 1.1 collective-permute-done.25.refs_3_
  119.5 2.6 %shard_map.150 = (f32[512,2048]{1,0:T(8,128)}, f32[512,512]{1,0:T(8,128)}) custom-call(s32[1]{0:T(128)} %bitcast.me_ref, bf16[16,16,1280]{2,1,0:T(8,128)(2,1)S(1)} %pad_maximum_fusion.refs_0_, bf16[16,16,1280]{2,1,0:T(8,128)(2,1)S(1)} %collective-permute-done.22.refs_1_, bf16[16,16,1280]{2,1,0:T(8,128)(2,1)S(1)} %pad_maximum_fusion.1.refs_2_, ...), custom_call_target="tpu_custom_call" | custom-call | tf_op jit(solution)/shard_map/pallas_call | solution.py:541
  (59 shorter events, 5.4 us)
Async XLA Ops:
  1.5 5.2 %collective-permute-start = (s32[8,8]{1,0:T(8,128)S(1)}, s32[8,8]{1,0:T(8,128)S(1)}, u32[]{:S(2)}, u32[]{:S(2)}) collective-permute-start(s32[8,8]{1,0:T(8,128)S(1)} %broadcast_select_fusion), channel_id=1, source_target_pairs={{0,4},{1,5},{2,6},{3,7},{4,0},{5,1},{6,2},{7,3},{8,12},{9,13},{10,... | collective-permute-start | bytes 776 | tf_op jit(solution)/shard_map/ppermute | solution.py:440
  6.7 3.6 %collective-permute-start.1 = (s32[8,8]{1,0:T(8,128)S(1)}, s32[8,8]{1,0:T(8,128)S(1)}, u32[]{:S(2)}, u32[]{:S(2)}) collective-permute-start(s32[8,8]{1,0:T(8,128)S(1)} %fusion), channel_id=1, source_target_pairs={{0,8},{1,9},{2,10},{3,11},{4,12},{5,13},{6,14},{7,15},{8,0},{9,1},... | collective-permute-start | bytes 776 | tf_op jit(solution)/shard_map/ppermute | solution.py:440
  10.4 4.5 %collective-permute-start.2 = (s32[8,8]{1,0:T(8,128)S(1)}, s32[8,8]{1,0:T(8,128)S(1)}, u32[]{:S(2)}, u32[]{:S(2)}) collective-permute-start(s32[8,8]{1,0:T(8,128)S(1)} %fusion.2), channel_id=1, source_target_pairs={{0,16},{1,17},{2,18},{3,19},{4,20},{5,21},{6,22},{7,23},{8,24},{9,... | collective-permute-start | bytes 776 | tf_op jit(solution)/shard_map/ppermute | solution.py:440
  14.9 1.0 copy-start
  16.6 17.2 %collective-permute-start.6 = (bf16[64,512]{1,0:T(8,128)(2,1)S(1)}, bf16[64,512]{1,0:T(8,128)(2,1)S(1)}, u32[]{:S(2)}, u32[]{:S(2)}) collective-permute-start(bf16[64,512]{1,0:T(8,128)(2,1)S(1)} %get-tuple-element.79), channel_id=1, source_target_pairs={{0,16},{1,17},{2,18},{3,19},{4,20},{5,21},{6,22},{7,23},{8,24},{9,... | collective-permute-start | bytes 196616 | tf_op jit(solution)/shard_map/ppermute | solution.py:440
  19.2 14.5 %collective-permute-start.7 = (bf16[64,512]{1,0:T(8,128)(2,1)S(1)}, bf16[64,512]{1,0:T(8,128)(2,1)S(1)}, u32[]{:S(2)}, u32[]{:S(2)}) collective-permute-start(bf16[64,512]{1,0:T(8,128)(2,1)S(1)} %get-tuple-element.80), channel_id=1, source_target_pairs={{0,20},{1,21},{2,22},{3,23},{4,16},{5,17},{6,18},{7,19},{8,28},{9,... | collective-permute-start | bytes 196616 | tf_op jit(solution)/shard_map/ppermute | solution.py:440
  20.4 15.5 %collective-permute-start.8 = (bf16[64,512]{1,0:T(8,128)(2,1)S(1)}, bf16[64,512]{1,0:T(8,128)(2,1)S(1)}, u32[]{:S(2)}, u32[]{:S(2)}) collective-permute-start(bf16[64,512]{1,0:T(8,128)(2,1)S(1)} %get-tuple-element.81), channel_id=1, source_target_pairs={{0,24},{1,25},{2,26},{3,27},{4,28},{5,29},{6,30},{7,31},{8,16},{9,... | collective-permute-start | bytes 196616 | tf_op jit(solution)/shard_map/ppermute | solution.py:440
  24.0 11.9 %collective-permute-start.9 = (bf16[64,512]{1,0:T(8,128)(2,1)S(1)}, bf16[64,512]{1,0:T(8,128)(2,1)S(1)}, u32[]{:S(2)}, u32[]{:S(2)}) collective-permute-start(bf16[64,512]{1,0:T(8,128)(2,1)S(1)} %get-tuple-element.82), channel_id=1, source_target_pairs={{0,28},{1,29},{2,30},{3,31},{4,24},{5,25},{6,26},{7,27},{8,20},{9,... | collective-permute-start | bytes 196616 | tf_op jit(solution)/shard_map/ppermute | solution.py:440
  24.3 1.6 %copy-start.1 = (bf16[512,2048]{1,0:T(8,128)(2,1)S(1)}, bf16[512,2048]{1,0:T(8,128)(2,1)}, u32[]{:S(2)}) copy-start(bf16[512,2048]{1,0:T(8,128)(2,1)} %refs_11_.1) | copy-start | bytes 6291460
  25.9 0.9 copy-start.4
  26.8 12.2 %copy-start.2 = (bf16[512,2048]{1,0:T(8,128)(2,1)S(1)}, bf16[512,2048]{1,0:T(8,128)(2,1)}, u32[]{:S(2)}) copy-start(bf16[512,2048]{1,0:T(8,128)(2,1)} %refs_11_.1) | copy-start | bytes 6291460
  26.8 12.2 %copy-start.3 = (bf16[512,512]{1,0:T(8,128)(2,1)S(1)}, bf16[512,512]{1,0:T(8,128)(2,1)}, u32[]{:S(2)}) copy-start(bf16[512,512]{1,0:T(8,128)(2,1)} %refs_0_.1) | copy-start | bytes 1572868
  26.8 12.2 %copy-start.5 = (s32[8]{0:T(128)S(1)}, s32[8]{0:T(128)}, u32[]{:S(2)}) copy-start(s32[8]{0:T(128)} %dest_ref.1) | copy-start | bytes 100
  26.8 12.2 %copy-start.6 = (s32[8]{0:T(128)S(1)}, s32[8]{0:T(128)}, u32[]{:S(2)}) copy-start(s32[8]{0:T(128)} %blocks_ref.1) | copy-start | bytes 100
  32.3 4.3 %collective-permute-start.3 = (bf16[64,512]{1,0:T(8,128)(2,1)S(1)}, bf16[64,512]{1,0:T(8,128)(2,1)S(1)}, u32[]{:S(2)}, u32[]{:S(2)}) collective-permute-start(bf16[64,512]{1,0:T(8,128)(2,1)S(1)} %get-tuple-element.76), channel_id=1, source_target_pairs={{0,4},{1,5},{2,6},{3,7},{4,0},{5,1},{6,2},{7,3},{8,12},{9,13},{10,... | collective-permute-start | bytes 196616 | tf_op jit(solution)/shard_map/ppermute | solution.py:440
  33.7 4.3 %collective-permute-start.4 = (bf16[64,512]{1,0:T(8,128)(2,1)S(1)}, bf16[64,512]{1,0:T(8,128)(2,1)S(1)}, u32[]{:S(2)}, u32[]{:S(2)}) collective-permute-start(bf16[64,512]{1,0:T(8,128)(2,1)S(1)} %get-tuple-element.77), channel_id=1, source_target_pairs={{0,8},{1,9},{2,10},{3,11},{4,12},{5,13},{6,14},{7,15},{8,0},{9,1},... | collective-permute-start | bytes 196616 | tf_op jit(solution)/shard_map/ppermute | solution.py:440
  33.8 5.2 %collective-permute-start.5 = (bf16[64,512]{1,0:T(8,128)(2,1)S(1)}, bf16[64,512]{1,0:T(8,128)(2,1)S(1)}, u32[]{:S(2)}, u32[]{:S(2)}) collective-permute-start(bf16[64,512]{1,0:T(8,128)(2,1)S(1)} %get-tuple-element.78), channel_id=1, source_target_pairs={{0,12},{1,13},{2,14},{3,15},{4,8},{5,9},{6,10},{7,11},{8,4},{9,5},... | collective-permute-start | bytes 196616 | tf_op jit(solution)/shard_map/ppermute | solution.py:440
  47.9 6.3 %collective-permute-start.10 = (bf16[16,16,1280]{2,1,0:T(8,128)(2,1)S(1)}, bf16[16,16,1280]{2,1,0:T(8,128)(2,1)}, u32[]{:S(2)}, u32[]{:S(2)}) collective-permute-start(bf16[16,16,1280]{2,1,0:T(8,128)(2,1)S(1)} %get-tuple-element.84), channel_id=1, source_target_pairs={{0,1},{1,0},{2,3},{3,2},{4,5},{5,4},{6,7},{7,6},{8,9},{9,8},{10,11... | collective-permute-start | bytes 1966088 | tf_op jit(solution)/shard_map/ppermute | solution.py:440
  47.9 9.2 %collective-permute-start.13 = (bf16[16,16,1280]{2,1,0:T(8,128)(2,1)S(1)}, bf16[16,16,1280]{2,1,0:T(8,128)(2,1)}, u32[]{:S(2)}, u32[]{:S(2)}) collective-permute-start(bf16[16,16,1280]{2,1,0:T(8,128)(2,1)S(1)} %get-tuple-element.86), channel_id=1, source_target_pairs={{0,1},{1,0},{2,3},{3,2},{4,5},{5,4},{6,7},{7,6},{8,9},{9,8},{10,11... | collective-permute-start | bytes 1966088 | tf_op jit(solution)/shard_map/ppermute | solution.py:440
  48.4 29.1 %all-to-all-start = ((bf16[32,16,640]{2,1,0:T(8,128)(2,1)}), bf16[32,16,640]{2,1,0:T(8,128)(2,1)S(1)}, u32[]{:S(2)}, u32[]{:S(2)}) async-start(bf16[32,16,640]{2,1,0:T(8,128)(2,1)} %bitcast.6), calls=%async_computation | async-start | bytes 1310720 | tf_op jit(solution)/shard_map/all_to_all | solution.py:443
  55.4 14.9 %collective-permute-start.11 = (bf16[8,16,1280]{2,1,0:T(8,128)(2,1)S(1)}, bf16[8,16,1280]{2,1,0:T(8,128)(2,1)S(1)}, u32[]{:S(2)}, u32[]{:S(2)}) collective-permute-start(bf16[8,16,1280]{2,1,0:T(8,128)(2,1)S(1)} %slice.57), channel_id=1, source_target_pairs={{0,2},{1,3},{2,0},{3,1},{4,6},{5,7},{6,4},{7,5},{8,10},{9,11},{10,... | collective-permute-start | bytes 983048 | tf_op jit(solution)/shard_map/ppermute | solution.py:440
  58.4 13.3 %collective-permute-start.14 = (bf16[8,16,1280]{2,1,0:T(8,128)(2,1)S(1)}, bf16[8,16,1280]{2,1,0:T(8,128)(2,1)S(1)}, u32[]{:S(2)}, u32[]{:S(2)}) collective-permute-start(bf16[8,16,1280]{2,1,0:T(8,128)(2,1)S(1)} %slice.61), channel_id=1, source_target_pairs={{0,4},{1,5},{2,6},{3,7},{4,0},{5,1},{6,2},{7,3},{8,12},{9,13},{10,... | collective-permute-start | bytes 983048 | tf_op jit(solution)/shard_map/ppermute | solution.py:440
  70.4 5.8 %collective-permute-start.12 = (bf16[4,16,1280]{2,1,0:T(8,128)(2,1)S(1)}, bf16[4,16,1280]{2,1,0:T(8,128)(2,1)S(1)}, u32[]{:S(2)}, u32[]{:S(2)}) collective-permute-start(bf16[4,16,1280]{2,1,0:T(8,128)(2,1)S(1)} %slice.59), channel_id=1, source_target_pairs={{0,4},{1,5},{2,6},{3,7},{4,0},{5,1},{6,2},{7,3},{8,12},{9,13},{10,... | collective-permute-start | bytes 491528 | tf_op jit(solution)/shard_map/ppermute | solution.py:440
  71.8 5.6 %collective-permute-start.15 = (bf16[4,16,1280]{2,1,0:T(8,128)(2,1)S(1)}, bf16[4,16,1280]{2,1,0:T(8,128)(2,1)S(1)}, u32[]{:S(2)}, u32[]{:S(2)}) collective-permute-start(bf16[4,16,1280]{2,1,0:T(8,128)(2,1)S(1)} %slice.63), channel_id=1, source_target_pairs={{0,2},{1,3},{2,0},{3,1},{4,6},{5,7},{6,4},{7,5},{8,10},{9,11},{10,... | collective-permute-start | bytes 491528 | tf_op jit(solution)/shard_map/ppermute | solution.py:440
  77.5 5.4 %collective-permute-start.16 = (bf16[2,16,2560]{2,1,0:T(8,128)(2,1)S(1)}, bf16[2,16,2560]{2,1,0:T(8,128)(2,1)S(1)}, u32[]{:S(2)}, u32[]{:S(2)}) collective-permute-start(bf16[2,16,2560]{2,1,0:T(8,128)(2,1)S(1)} %slice.51), channel_id=1, source_target_pairs={{0,8},{1,9},{2,10},{3,11},{4,12},{5,13},{6,14},{7,15},{8,0},{9,1},... | collective-permute-start | bytes 491528 | tf_op jit(solution)/shard_map/ppermute | solution.py:440
  83.0 6.1 %collective-permute-start.17 = (bf16[1,16,2560]{2,1,0:T(8,128)(2,1)S(1)}, bf16[1,16,2560]{2,1,0:T(8,128)(2,1)S(1)}, u32[]{:S(2)}, u32[]{:S(2)}) collective-permute-start(bf16[1,16,2560]{2,1,0:T(8,128)(2,1)S(1)} %slice.65), channel_id=1, source_target_pairs={{0,16},{1,17},{2,18},{3,19},{4,20},{5,21},{6,22},{7,23},{8,24},{9,... | collective-permute-start | bytes 245768 | tf_op jit(solution)/shard_map/ppermute | solution.py:440
  89.0 5.8 %collective-permute-start.18 = (bf16[1,16,2560]{2,1,0:T(8,128)(2,1)S(1)}, bf16[1,16,2560]{2,1,0:T(8,128)(2,1)S(1)}, u32[]{:S(2)}, u32[]{:S(2)}) collective-permute-start(bf16[1,16,2560]{2,1,0:T(8,128)(2,1)S(1)} %add_convert_fusion.7), channel_id=1, source_target_pairs={{0,16},{1,17},{2,18},{3,19},{4,20},{5,21},{6,22},{7,23},{8,24},{9,... | collective-permute-start | bytes 245768 | tf_op jit(solution)/shard_map/ppermute | solution.py:440
  94.9 7.2 %collective-permute-start.19 = (bf16[2,16,2560]{2,1,0:T(8,128)(2,1)S(1)}, bf16[2,16,2560]{2,1,0:T(8,128)(2,1)S(1)}, u32[]{:S(2)}, u32[]{:S(2)}) collective-permute-start(bf16[2,16,2560]{2,1,0:T(8,128)(2,1)S(1)} %pad_maximum_fusion.6), channel_id=1, source_target_pairs={{0,8},{1,9},{2,10},{3,11},{4,12},{5,13},{6,14},{7,15},{8,0},{9,1},... | collective-permute-start | bytes 491528 | tf_op jit(solution)/shard_map/ppermute | solution.py:440
  102.1 6.8 %collective-permute-start.20 = (bf16[4,16,1280]{2,1,0:T(8,128)(2,1)S(1)}, bf16[4,16,1280]{2,1,0:T(8,128)(2,1)S(1)}, u32[]{:S(2)}, u32[]{:S(2)}) collective-permute-start(bf16[4,16,1280]{2,1,0:T(8,128)(2,1)S(1)} %get-tuple-element.98), channel_id=1, source_target_pairs={{0,4},{1,5},{2,6},{3,7},{4,0},{5,1},{6,2},{7,3},{8,12},{9,13},{10,... | collective-permute-start | bytes 491528 | tf_op jit(solution)/shard_map/ppermute | solution.py:440
  102.6 7.5 %collective-permute-start.23 = (bf16[4,16,1280]{2,1,0:T(8,128)(2,1)S(1)}, bf16[4,16,1280]{2,1,0:T(8,128)(2,1)S(1)}, u32[]{:S(2)}, u32[]{:S(2)}) collective-permute-start(bf16[4,16,1280]{2,1,0:T(8,128)(2,1)S(1)} %get-tuple-element.97), channel_id=1, source_target_pairs={{0,2},{1,3},{2,0},{3,1},{4,6},{5,7},{6,4},{7,5},{8,10},{9,11},{10,... | collective-permute-start | bytes 491528 | tf_op jit(solution)/shard_map/ppermute | solution.py:440
  109.0 7.1 %collective-permute-start.21 = (bf16[8,16,1280]{2,1,0:T(8,128)(2,1)S(1)}, bf16[8,16,1280]{2,1,0:T(8,128)(2,1)S(1)}, u32[]{:S(2)}, u32[]{:S(2)}) collective-permute-start(bf16[8,16,1280]{2,1,0:T(8,128)(2,1)S(1)} %pad_maximum_fusion.4), channel_id=1, source_target_pairs={{0,2},{1,3},{2,0},{3,1},{4,6},{5,7},{6,4},{7,5},{8,10},{9,11},{10,... | collective-permute-start | bytes 983048 | tf_op jit(solution)/shard_map/ppermute | solution.py:440
  110.1 7.1 %collective-permute-start.24 = (bf16[8,16,1280]{2,1,0:T(8,128)(2,1)S(1)}, bf16[8,16,1280]{2,1,0:T(8,128)(2,1)S(1)}, u32[]{:S(2)}, u32[]{:S(2)}) collective-permute-start(bf16[8,16,1280]{2,1,0:T(8,128)(2,1)S(1)} %pad_maximum_fusion.5), channel_id=1, source_target_pairs={{0,4},{1,5},{2,6},{3,7},{4,0},{5,1},{6,2},{7,3},{8,12},{9,13},{10,... | collective-permute-start | bytes 983048 | tf_op jit(solution)/shard_map/ppermute | solution.py:440
  116.2 2.2 %collective-permute-start.22 = (bf16[16,16,1280]{2,1,0:T(8,128)(2,1)S(1)}, bf16[16,16,1280]{2,1,0:T(8,128)(2,1)S(1)}, u32[]{:S(2)}, u32[]{:S(2)}) collective-permute-start(bf16[16,16,1280]{2,1,0:T(8,128)(2,1)S(1)} %pad_maximum_fusion.refs_0_), channel_id=1, source_target_pairs={{0,1},{1,0},{2,3},{3,2},{4,5},{5,4},{6,7},{7,6},{8,9},{9,8},{10,11... | collective-permute-start | bytes 1966088 | tf_op jit(solution)/shard_map/ppermute | solution.py:440
  117.3 2.2 %collective-permute-start.25 = (bf16[16,16,1280]{2,1,0:T(8,128)(2,1)S(1)}, bf16[16,16,1280]{2,1,0:T(8,128)(2,1)S(1)}, u32[]{:S(2)}, u32[]{:S(2)}) collective-permute-start(bf16[16,16,1280]{2,1,0:T(8,128)(2,1)S(1)} %pad_maximum_fusion.1.refs_2_), channel_id=1, source_target_pairs={{0,1},{1,0},{2,3},{3,2},{4,5},{5,4},{6,7},{7,6},{8,9},{9,8},{10,11... | collective-permute-start | bytes 1966088 | tf_op jit(solution)/shard_map/ppermute | solution.py:440

commit v12 on v11

--- a/solution.py
+++ b/solution.py
@@ -118,12 +118,9 @@
 def forward_body(
     capacity,
     rows_ref,
-    item_ref,
     w_in_ref,
     gains_ref,
-    owner_col_ref,
     ints_ref,
-    number_ref,
     *refs,
 ):
     held = dict(zip(SAVED, refs))
@@ -133,17 +130,24 @@
     weight_t_ref, mixed_t_ref, normed_t_ref, rows_slope_ref = (held[name] for name in SAVED[6:10])
     rows_hat_ref, rows_scale_ref, place_ref, digits_ref = (held[name] for name in SAVED[10:])
     count, width = rows_ref.shape
-    tokens = item_ref.shape[0]
+    tokens = ints_ref.shape[1] - 2 * count
     gain_in, gain_out = gains_ref[0:1, :], gains_ref[1:2, :]
-    owner_row = ints_ref[:, tokens:]
+    columns = jnp.broadcast_to(ints_ref[...].astype(F32), (8, ints_ref.shape[1])).T
+    columns = columns[:, 0:1].astype(jnp.int32)
+    items, owners, numbers = (
+        columns[:tokens],
+        columns[tokens : tokens + count],
+        columns[tokens + count :],
+    )
+    owner_row = ints_ref[:, tokens : tokens + count]
     across = jnp.broadcast_to(owner_row, (count, count))
-    down = jnp.broadcast_to(owner_col_ref[...], (count, count))
+    down = jnp.broadcast_to(owners, (count, count))
     sub = lax.broadcasted_iota(jnp.int32, (count, count), 0)
     lane = lax.broadcasted_iota(jnp.int32, (count, count), 1)
     earlier = jnp.where((across == down) & (sub < lane), 1.0, 0.0)
     rank = jnp.sum(earlier, axis=0, keepdims=True).astype(jnp.int32)
     place_ref[...] = owner_row * capacity + rank
-    number = jnp.broadcast_to(number_ref[...], (count, LANES))
+    number = jnp.broadcast_to(numbers, (count, LANES))
     lane = lax.broadcasted_iota(jnp.int32, (count, LANES), 1)
     digits = jnp.where(lane == 0, number >> 5, jnp.where(lane == 1, number & 31, 0))
     digits_ref[...] = digits.astype(F32).astype(BF16)
@@ -157,7 +161,7 @@
     normed_t_ref[...] = normed.T.astype(BF16)
     normed = normed.astype(BF16)
     lane = lax.broadcasted_iota(jnp.int32, (tokens, count), 1)
-    pick = jnp.where(lane == jnp.broadcast_to(item_ref[...], (tokens, count)), 1.0, 0.0)
+    pick = jnp.where(lane == jnp.broadcast_to(items, (tokens, count)), 1.0, 0.0)
     pick = pick.astype(BF16)
     for part in range(4):
         columns = slice(part * width, (part + 1) * width)
@@ -433,14 +437,16 @@
     devices_all = plan.chunks
     total_factor = 1.0 / math.sqrt(grad_out.shape[0] * devices_all)
     gain_rows = jnp.stack([gain_in, gain_out])
-    ints = jnp.concatenate([row_of_token, row_owner[:, 0]])[None, :]
+    ints = jnp.concatenate([row_of_token, row_owner[:, 0], owner_row])[None, :]
     me = lax.axis_index(both).astype(jnp.int32)[None]
 
     def swap(values, mask):
         return lax.ppermute(values, both, [(here, here ^ mask) for here in range(devices_all)])
 
-    def exchange(values, axes):
-        return lax.all_to_all(values, axes, split_axis=0, concat_axis=0, tiled=True)
+    def exchange(values, axes, groups):
+        return lax.all_to_all(
+            values, axes, split_axis=0, concat_axis=0, tiled=True, axis_index_groups=groups
+        )
 
     peers = jnp.arange(dp_size, dtype=jnp.int32)
     own = jnp.sum(jnp.where(seq_dest[:, None] == peers, seq_blocks[:, None], 0), axis=0)
@@ -463,18 +469,15 @@
     saved = call(
         functools.partial(forward_body, plan.capacity),
         [shapes[name] for name in SAVED],
-        [VMEM] * 7,
+        [VMEM] * 4,
         flops=4 * count * width * width * 20,
         moved=10_000_000,
         mebibytes=12 + tokens // 32,
     )(
         touched_rows,
-        row_of_token.reshape(tokens, 1),
         w_in,
         gain_rows,
-        row_owner,
         ints,
-        owner_row.reshape(count, 1),
     )
     *near, gate = lax.optimization_barrier((*near, saved[0]))
     saved = [gate, *saved[1:]]
@@ -515,12 +518,17 @@
     def gathered(kept, mask):
         return jnp.concatenate([kept, swap(kept, mask)])
 
+    low = min(2, dp_size)
+    high, inside = dp_size // low, low * table_size
+    groups = [[upper * low + lower for upper in range(high)] for lower in range(low)]
+    table_got = exchange(table_send.reshape(high, inside, plan.capacity, -1), "dp", groups)
     sides = [add(parts[2 * side], swap(parts[2 * side + 1], 1)) for side in range(2)]
-    table_got = exchange(table_send.reshape(devices_all, plan.capacity, -1), both)
     for step in range(plan.near_steps):
         sides = [reduced(sides[side], plan.orders[side][step]) for side in range(2)]
     kept = jnp.concatenate(sides, axis=2)
     kept, table_got = lax.optimization_barrier((kept, table_got))
+    groups = [[upper * inside + lower for lower in range(inside)] for upper in range(high)]
+    table_got = exchange(jnp.swapaxes(table_got, 0, 1), both, groups)
     table_part, grad_gain_in, grad_gain_out = call(
         functools.partial(table_body, plan),
         (

time: 123 us -> 126 us (1.024)
  waiting for transfers between devices: 43.9 us -> 48.2 us
  local copies, waits for them, and re-layouts: 6.06 us -> 4.52 us
    all_to_all x1 -> x2, starting transfers between devices: 5.74 us -> 8.9 us  [exchange(): lax.all_to_all(values, axes, split_axis=0, concat_axis=0, tiled=True, axi...]
    ppermute x26, starting transfers between devices: 40.3 us -> 37.3 us  [swap(): lax.ppermute(values, both, [(here, here ^ mask) for here in range(devices...]
    all_to_all x1 -> x2, waiting for transfers between devices: 0.01 us -> 2.35 us  [exchange(): lax.all_to_all(values, axes, split_axis=0, concat_axis=0, tiled=True, axi...]
    ppermute x26, waiting for transfers between devices: 43.9 us -> 45.8 us  [swap(): lax.ppermute(values, both, [(here, here ^ mask) for here in range(devices...]
    reshape x2 -> x0, local copies, waits for them, and re-layouts: 1.63 us -> none  [the longest x1 0.82 us: on_device(): row_of_token.reshape(tokens, 1)]
    unnamed x15 -> x14, local copies, waits for them, and re-layouts: 4.31 us -> 3.51 us
  transfers between devices with their start and end apart: 27 -> 28, of which waited for: 17 -> 19; matrix products, arithmetic and copies ran while one was open for 6% -> 4% of each run, Pallas kernels for 6% -> 4%
where the time goes in v12:
time: 126 us; the launch traced here: 125 us
  waiting for transfers between devices  48.2 us (38%)
  starting transfers between devices  46.2 us (37%)
  Pallas kernels  19.8 us (16%)
  other arithmetic  5.49 us (4%)
  local copies, waits for them, and re-layouts  4.52 us (4%)
    ppermute x26, waiting for transfers between devices, swap(): lax.ppermute(values, both, [(here, here ^ mask) for here in range(devices...  45.8 us
    ppermute x26, starting transfers between devices, swap(): lax.ppermute(values, both, [(here, here ^ mask) for here in range(devices...  37.3 us
    all_to_all x2, starting transfers between devices, exchange(): lax.all_to_all(values, axes, split_axis=0, concat_axis=0, tiled=True, axi...  8.9 us
    pallas_call x1, Pallas kernels, on_device(): call(functools.partial(backward_body, plan, table_size, total_factor), ou...  8.87 us
    pallas_call x1, Pallas kernels, on_device(): call(functools.partial(forward_body, plan.capacity), [shapes[name] for na...  5.48 us
    unnamed x14, local copies, waits for them, and re-layouts  3.51 us
    convert_element_type x8, other arithmetic, add(): return (left.astype(F32) + right.astype(F32)).astype(BF16)  2.8 us
    pallas_call x1, Pallas kernels, on_device(): call(functools.partial(widen_body, plan), (shape_of(w_in.shape, F32), sha...  2.6 us
  transfers between devices with their start and end apart: 28, of which 19 were waited for; matrix products, arithmetic and copies ran while one was open for 4% of the time, Pallas kernels for 4%

profile of v12, /device:TPU:0, one launch (start us, length us, event | category | flops | bytes accessed | tf_op | source)
XLA Modules:
  0.0 125.0 jit_solution(15945043276363381988)
XLA Ops:
  0.6 0.8 select_reduce_fusion
  1.5 2.9 %collective-permute-start = (s32[8,8]{1,0:T(8,128)S(1)}, s32[8,8]{1,0:T(8,128)S(1)}, u32[]{:S(2)}, u32[]{:S(2)}) collective-permute-start(s32[8,8]{1,0:T(8,128)S(1)} %broadcast_select_fusion), channel_id=1, source_target_pairs={{0,4},{1,5},{2,6},{3,7},{4,0},{5,1},{6,2},{7,3},{8,12},{9,13},{10,... | collective-permute-start | bytes 776 | tf_op jit(solution)/shard_map/ppermute | solution.py:444
  5.1 0.9 collective-permute-done
  6.1 2.1 %collective-permute-start.1 = (s32[8,8]{1,0:T(8,128)S(1)}, s32[8,8]{1,0:T(8,128)S(1)}, u32[]{:S(2)}, u32[]{:S(2)}) collective-permute-start(s32[8,8]{1,0:T(8,128)S(1)} %fusion), channel_id=1, source_target_pairs={{0,8},{1,9},{2,10},{3,11},{4,12},{5,13},{6,14},{7,15},{8,0},{9,1},... | collective-permute-start | bytes 776 | tf_op jit(solution)/shard_map/ppermute | solution.py:444
  8.9 0.9 collective-permute-done.1
  9.8 3.0 %collective-permute-start.2 = (s32[8,8]{1,0:T(8,128)S(1)}, s32[8,8]{1,0:T(8,128)S(1)}, u32[]{:S(2)}, u32[]{:S(2)}) collective-permute-start(s32[8,8]{1,0:T(8,128)S(1)} %fusion.2), channel_id=1, source_target_pairs={{0,16},{1,17},{2,18},{3,19},{4,20},{5,21},{6,22},{7,23},{8,24},{9,... | collective-permute-start | bytes 776 | tf_op jit(solution)/shard_map/ppermute | solution.py:444
  12.9 1.6 %collective-permute-done.2 = s32[8,8]{1,0:T(8,128)S(1)} collective-permute-done((s32[8,8]{1,0:T(8,128)S(1)}, s32[8,8]{1,0:T(8,128)S(1)}, u32[]{:S(2)}, u32[]{:S(2)}) %collective-permute-start.2) | collective-permute-done | bytes 288 | tf_op jit(solution)/shard_map/ppermute | solution.py:444
  14.5 0.9 copy-done
  16.1 3.0 %collective-permute-start.6 = (bf16[64,512]{1,0:T(8,128)(2,1)S(1)}, bf16[64,512]{1,0:T(8,128)(2,1)S(1)}, u32[]{:S(2)}, u32[]{:S(2)}) collective-permute-start(bf16[64,512]{1,0:T(8,128)(2,1)S(1)} %get-tuple-element.79), channel_id=1, source_target_pairs={{0,16},{1,17},{2,18},{3,19},{4,20},{5,21},{6,22},{7,23},{8,24},{9,... | collective-permute-start | bytes 196616 | tf_op jit(solution)/shard_map/ppermute | solution.py:444
  19.1 1.3 %collective-permute-start.7 = (bf16[64,512]{1,0:T(8,128)(2,1)S(1)}, bf16[64,512]{1,0:T(8,128)(2,1)S(1)}, u32[]{:S(2)}, u32[]{:S(2)}) collective-permute-start(bf16[64,512]{1,0:T(8,128)(2,1)S(1)} %get-tuple-element.80), channel_id=1, source_target_pairs={{0,20},{1,21},{2,22},{3,23},{4,16},{5,17},{6,18},{7,19},{8,28},{9,... | collective-permute-start | bytes 196616 | tf_op jit(solution)/shard_map/ppermute | solution.py:444
  20.4 3.6 %collective-permute-start.8 = (bf16[64,512]{1,0:T(8,128)(2,1)S(1)}, bf16[64,512]{1,0:T(8,128)(2,1)S(1)}, u32[]{:S(2)}, u32[]{:S(2)}) collective-permute-start(bf16[64,512]{1,0:T(8,128)(2,1)S(1)} %get-tuple-element.81), channel_id=1, source_target_pairs={{0,24},{1,25},{2,26},{3,27},{4,28},{5,29},{6,30},{7,31},{8,16},{9,... | collective-permute-start | bytes 196616 | tf_op jit(solution)/shard_map/ppermute | solution.py:444
  24.0 1.6 %copy-done.1 = bf16[512,2048]{1,0:T(8,128)(2,1)S(1)} copy-done((bf16[512,2048]{1,0:T(8,128)(2,1)S(1)}, bf16[512,2048]{1,0:T(8,128)(2,1)}, u32[]{:S(2)}) %copy-start.1) | copy-done | bytes 2097176
  25.6 0.9 copy-done.4
  26.5 5.5 %shard_map.147 = (f32[512,512]{1,0:T(8,128)S(1)}, f32[512,512]{1,0:T(8,128)S(1)}, f32[512,1]{1,0:T(8,128)S(1)}, bf16[512,1536]{1,0:T(8,128)(2,1)S(1)}, bf16[16,1...) custom-call(bf16[256,512]{1,0:T(8,128)(2,1)S(1)} %copy-done.4, ...), custom_call_target="tpu_custom_call" | custom-call | flops 5368709120 | bytes 10000000 | tf_op jit(solution)/shard_map/pallas_call | solution.py:469
  32.0 1.8 %collective-permute-start.3 = (bf16[64,512]{1,0:T(8,128)(2,1)S(1)}, bf16[64,512]{1,0:T(8,128)(2,1)S(1)}, u32[]{:S(2)}, u32[]{:S(2)}) collective-permute-start(bf16[64,512]{1,0:T(8,128)(2,1)S(1)} %get-tuple-element.76), channel_id=1, source_target_pairs={{0,4},{1,5},{2,6},{3,7},{4,0},{5,1},{6,2},{7,3},{8,12},{9,13},{10,... | collective-permute-start | bytes 196616 | tf_op jit(solution)/shard_map/ppermute | solution.py:444
  33.8 1.8 %collective-permute-start.5 = (bf16[64,512]{1,0:T(8,128)(2,1)S(1)}, bf16[64,512]{1,0:T(8,128)(2,1)S(1)}, u32[]{:S(2)}, u32[]{:S(2)}) collective-permute-start(bf16[64,512]{1,0:T(8,128)(2,1)S(1)} %get-tuple-element.78), channel_id=1, source_target_pairs={{0,12},{1,13},{2,14},{3,15},{4,8},{5,9},{6,10},{7,11},{8,4},{9,5},... | collective-permute-start | bytes 196616 | tf_op jit(solution)/shard_map/ppermute | solution.py:444
  35.6 0.8 collective-permute-done.3.refs_17_
  36.3 1.7 %collective-permute-done.4.refs_18_ = bf16[64,512]{1,0:T(8,128)(2,1)S(1)} collective-permute-done((bf16[64,512]{1,0:T(8,128)(2,1)S(1)}, bf16[64,512]{1,0:T(8,128)(2,1)S(1)}, u32[]{:S(2)}, u32[]{:S(2)}) %collective-permute-start.4) | collective-permute-done | bytes 65568 | tf_op jit(solution)/shard_map/ppermute | solution.py:444
  38.0 1.0 collective-permute-done.5.refs_19_
  39.0 8.9 %shard_map.148 = (bf16[512,640]{1,0:T(8,128)(2,1)}, bf16[16,16,1280]{2,1,0:T(8,128)(2,1)S(1)}, bf16[16,16,1280]{2,1,0:T(8,128)(2,1)S(1)}, bf16[16,16,1280]{2,1,0:T(8,128)(2,1)S(1)}, bf16[16,16,1280]{2,1,0:T(8,128)(2,1)S(1)}) custom-call(s32[1]{0:T(128)} %bitcast.me_ref, s32[8]{0:T(128)S(1)} %copy-done.5, s32[8]{0:T(128)S(1)} %copy-done.6, ...), custom_call_target="tpu_custom_call" | custom-call | flops 10737418240 | bytes 12000000 | tf_op jit(solution)/shard_map/pallas_call | solution.py:491
  48.4 5.4 %all-to-all-start = ((bf16[4,8,16,640]{3,2,1,0:T(8,128)(2,1)}), bf16[4,8,16,640]{3,2,1,0:T(8,128)(2,1)S(1)}, u32[]{:S(2)}, u32[]{:S(2)}) async-start(bf16[4,8,16,640]{3,2,1,0:T(8,128)(2,1)} %bitcast.5), calls=%async_computation | async-start | bytes 1310720 | tf_op jit(solution)/shard_map/all_to_all | solution.py:447
  53.8 1.2 add_convert_fusion.1
  55.0 1.6 %collective-permute-start.11 = (bf16[8,16,1280]{2,1,0:T(8,128)(2,1)S(1)}, bf16[8,16,1280]{2,1,0:T(8,128)(2,1)S(1)}, u32[]{:S(2)}, u32[]{:S(2)}) collective-permute-start(bf16[8,16,1280]{2,1,0:T(8,128)(2,1)S(1)} %slice.57), channel_id=1, source_target_pairs={{0,2},{1,3},{2,0},{3,1},{4,6},{5,7},{6,4},{7,5},{8,10},{9,11},{10,... | collective-permute-start | bytes 983048 | tf_op jit(solution)/shard_map/ppermute | solution.py:444
  56.6 1.2 add_convert_fusion
  57.9 0.8 collective-permute-start.14
  58.7 5.8 %collective-permute-done.11 = bf16[8,16,1280]{2,1,0:T(8,128)(2,1)S(1)} collective-permute-done((bf16[8,16,1280]{2,1,0:T(8,128)(2,1)S(1)}, bf16[8,16,1280]{2,1,0:T(8,128)(2,1)S(1)}, u32[]{:S(2)}, u32[]{:S(2)}) %collective-permute-start.11) | collective-permute-done | bytes 327712 | tf_op jit(solution)/shard_map/ppermute | solution.py:444
  65.3 2.6 %collective-permute-done.14 = bf16[8,16,1280]{2,1,0:T(8,128)(2,1)S(1)} collective-permute-done((bf16[8,16,1280]{2,1,0:T(8,128)(2,1)S(1)}, bf16[8,16,1280]{2,1,0:T(8,128)(2,1)S(1)}, u32[]{:S(2)}, u32[]{:S(2)}) %collective-permute-start.14) | collective-permute-done | bytes 327712 | tf_op jit(solution)/shard_map/ppermute | solution.py:444
  68.1 2.4 %collective-permute-done.12 = bf16[4,16,1280]{2,1,0:T(8,128)(2,1)S(1)} collective-permute-done((bf16[4,16,1280]{2,1,0:T(8,128)(2,1)S(1)}, bf16[4,16,1280]{2,1,0:T(8,128)(2,1)S(1)}, u32[]{:S(2)}, u32[]{:S(2)}) %collective-permute-start.12) | collective-permute-done | bytes 163872 | tf_op jit(solution)/shard_map/ppermute | solution.py:444
  70.6 2.8 %collective-permute-done.15 = bf16[4,16,1280]{2,1,0:T(8,128)(2,1)S(1)} collective-permute-done((bf16[4,16,1280]{2,1,0:T(8,128)(2,1)S(1)}, bf16[4,16,1280]{2,1,0:T(8,128)(2,1)S(1)}, u32[]{:S(2)}, u32[]{:S(2)}) %collective-permute-start.15) | collective-permute-done | bytes 163872 | tf_op jit(solution)/shard_map/ppermute | solution.py:444
  73.5 2.1 %collective-permute-start.16 = (bf16[2,16,2560]{2,1,0:T(8,128)(2,1)S(1)}, bf16[2,16,2560]{2,1,0:T(8,128)(2,1)S(1)}, u32[]{:S(2)}, u32[]{:S(2)}) collective-permute-start(bf16[2,16,2560]{2,1,0:T(8,128)(2,1)S(1)} %slice.51), channel_id=1, source_target_pairs={{0,8},{1,9},{2,10},{3,11},{4,12},{5,13},{6,14},{7,15},{8,0},{9,1},... | collective-permute-start | bytes 491528 | tf_op jit(solution)/shard_map/ppermute | solution.py:444
  75.6 4.2 %collective-permute-done.16 = bf16[2,16,2560]{2,1,0:T(8,128)(2,1)S(1)} collective-permute-done((bf16[2,16,2560]{2,1,0:T(8,128)(2,1)S(1)}, bf16[2,16,2560]{2,1,0:T(8,128)(2,1)S(1)}, u32[]{:S(2)}, u32[]{:S(2)}) %collective-permute-start.16) | collective-permute-done | bytes 163872 | tf_op jit(solution)/shard_map/ppermute | solution.py:444
  79.9 2.5 %collective-permute-start.17 = (bf16[1,16,2560]{2,1,0:T(8,128)(2,1)S(1)}, bf16[1,16,2560]{2,1,0:T(8,128)(2,1)S(1)}, u32[]{:S(2)}, u32[]{:S(2)}) collective-permute-start(bf16[1,16,2560]{2,1,0:T(8,128)(2,1)S(1)} %slice.65), channel_id=1, source_target_pairs={{0,16},{1,17},{2,18},{3,19},{4,20},{5,21},{6,22},{7,23},{8,24},{9,... | collective-permute-start | bytes 245768 | tf_op jit(solution)/shard_map/ppermute | solution.py:444
  82.4 3.3 %collective-permute-done.17 = bf16[1,16,2560]{2,1,0:T(8,128)(2,1)S(1)} collective-permute-done((bf16[1,16,2560]{2,1,0:T(8,128)(2,1)S(1)}, bf16[1,16,2560]{2,1,0:T(8,128)(2,1)S(1)}, u32[]{:S(2)}, u32[]{:S(2)}) %collective-permute-start.17) | collective-permute-done | bytes 81952 | tf_op jit(solution)/shard_map/ppermute | solution.py:444
  85.7 2.1 %collective-permute-start.18 = (bf16[1,16,2560]{2,1,0:T(8,128)(2,1)S(1)}, bf16[1,16,2560]{2,1,0:T(8,128)(2,1)S(1)}, u32[]{:S(2)}, u32[]{:S(2)}) collective-permute-start(bf16[1,16,2560]{2,1,0:T(8,128)(2,1)S(1)} %add_convert_fusion.7), channel_id=1, source_target_pairs={{0,16},{1,17},{2,18},{3,19},{4,20},{5,21},{6,22},{7,23},{8,24},{9,... | collective-permute-start | bytes 245768 | tf_op jit(solution)/shard_map/ppermute | solution.py:444
  87.8 0.9 copy.18
  88.7 3.5 %all-to-all-start.1 = ((bf16[8,4,16,640]{3,2,1,0:T(8,128)(2,1)}), bf16[8,4,16,640]{3,2,1,0:T(8,128)(2,1)S(1)}, u32[]{:S(2)}, u32[]{:S(2)}) async-start(bf16[8,4,16,640]{3,2,1,0:T(8,128)(2,1)} %copy.18), calls=%async_computation.1 | async-start | bytes 1310720 | tf_op jit(solution)/shard_map/all_to_all | solution.py:447
  92.3 3.0 %collective-permute-start.19 = (bf16[2,16,2560]{2,1,0:T(8,128)(2,1)S(1)}, bf16[2,16,2560]{2,1,0:T(8,128)(2,1)S(1)}, u32[]{:S(2)}, u32[]{:S(2)}) collective-permute-start(bf16[2,16,2560]{2,1,0:T(8,128)(2,1)S(1)} %pad_maximum_fusion.6), channel_id=1, source_target_pairs={{0,8},{1,9},{2,10},{3,11},{4,12},{5,13},{6,14},{7,15},{8,0},{9,1},... | collective-permute-start | bytes 491528 | tf_op jit(solution)/shard_map/ppermute | solution.py:444
  95.3 4.7 %collective-permute-done.19 = bf16[2,16,2560]{2,1,0:T(8,128)(2,1)S(1)} collective-permute-done((bf16[2,16,2560]{2,1,0:T(8,128)(2,1)S(1)}, bf16[2,16,2560]{2,1,0:T(8,128)(2,1)S(1)}, u32[]{:S(2)}, u32[]{:S(2)}) %collective-permute-start.19) | collective-permute-done | bytes 163872 | tf_op jit(solution)/shard_map/ppermute | solution.py:444
  100.1 2.3 %all-to-all-done.1 = bf16[8,4,16,640]{3,2,1,0:T(8,128)(2,1)S(1)} async-done(((bf16[8,4,16,640]{3,2,1,0:T(8,128)(2,1)}), bf16[8,4,16,640]{3,2,1,0:T(8,128)(2,1)S(1)}, u32[]{:S(2)}, u32[]{:S(2)}) %all-to-all-start.1) | async-done | bytes 655392 | tf_op jit(solution)/shard_map/all_to_all | solution.py:447
  102.4 2.2 %shard_map.149 = (f32[1024,512]{1,0:T(8,128)}, f32[1,512]{1,0:T(1,128)}, f32[1,512]{1,0:T(1,128)}) custom-call(bf16[512,640]{1,0:T(8,128)(2,1)S(1)} %bitcast.10), custom_call_target="tpu_custom_call" | custom-call | tf_op jit(solution)/shard_map/pallas_call | solution.py:532
  104.6 1.5 %collective-permute-start.20 = (bf16[4,16,1280]{2,1,0:T(8,128)(2,1)S(1)}, bf16[4,16,1280]{2,1,0:T(8,128)(2,1)S(1)}, u32[]{:S(2)}, u32[]{:S(2)}) collective-permute-start(bf16[4,16,1280]{2,1,0:T(8,128)(2,1)S(1)} %get-tuple-element.98), channel_id=1, source_target_pairs={{0,4},{1,5},{2,6},{3,7},{4,0},{5,1},{6,2},{7,3},{8,12},{9,13},{10,... | collective-permute-start | bytes 491528 | tf_op jit(solution)/shard_map/ppermute | solution.py:444
  106.7 3.7 %collective-permute-done.20 = bf16[4,16,1280]{2,1,0:T(8,128)(2,1)S(1)} collective-permute-done((bf16[4,16,1280]{2,1,0:T(8,128)(2,1)S(1)}, bf16[4,16,1280]{2,1,0:T(8,128)(2,1)S(1)}, u32[]{:S(2)}, u32[]{:S(2)}) %collective-permute-start.20) | collective-permute-done | bytes 163872 | tf_op jit(solution)/shard_map/ppermute | solution.py:444
  110.4 1.5 %collective-permute-start.21 = (bf16[8,16,1280]{2,1,0:T(8,128)(2,1)S(1)}, bf16[8,16,1280]{2,1,0:T(8,128)(2,1)S(1)}, u32[]{:S(2)}, u32[]{:S(2)}) collective-permute-start(bf16[8,16,1280]{2,1,0:T(8,128)(2,1)S(1)} %pad_maximum_fusion.4), channel_id=1, source_target_pairs={{0,2},{1,3},{2,0},{3,1},{4,6},{5,7},{6,4},{7,5},{8,10},{9,11},{10,... | collective-permute-start | bytes 983048 | tf_op jit(solution)/shard_map/ppermute | solution.py:444
  112.6 6.2 %collective-permute-done.21 = bf16[8,16,1280]{2,1,0:T(8,128)(2,1)S(1)} collective-permute-done((bf16[8,16,1280]{2,1,0:T(8,128)(2,1)S(1)}, bf16[8,16,1280]{2,1,0:T(8,128)(2,1)S(1)}, u32[]{:S(2)}, u32[]{:S(2)}) %collective-permute-start.21) | collective-permute-done | bytes 327712 | tf_op jit(solution)/shard_map/ppermute | solution.py:444
  119.0 1.2 collective-permute-done.24
  120.3 0.8 collective-permute-done.22.refs_1_
  121.1 1.3 %collective-permute-done.25.refs_3_ = bf16[16,16,1280]{2,1,0:T(8,128)(2,1)S(1)} collective-permute-done((bf16[16,16,1280]{2,1,0:T(8,128)(2,1)S(1)}, bf16[16,16,1280]{2,1,0:T(8,128)(2,1)S(1)}, u32[]{:S(2)}, u32[]{:S(2)}) %collective-permute-start.25) | collective-permute-done | bytes 655392 | tf_op jit(solution)/shard_map/ppermute | solution.py:444
  122.4 2.6 %shard_map.150 = (f32[512,2048]{1,0:T(8,128)}, f32[512,512]{1,0:T(8,128)}) custom-call(s32[1]{0:T(128)} %bitcast.me_ref, bf16[16,16,1280]{2,1,0:T(8,128)(2,1)S(1)} %pad_maximum_fusion.refs_0_, bf16[16,16,1280]{2,1,0:T(8,128)(2,1)S(1)} %collective-permute-done.22.refs_1_, bf16[16,16,1280]{2,1,0:T(8,128)(2,1)S(1)} %pad_maximum_fusion.1.refs_2_, ...), custom_call_target="tpu_custom_call" | custom-call | tf_op jit(solution)/shard_map/pallas_call | solution.py:549
  (58 shorter events, 5.7 us)
Async XLA Ops:
  1.5 4.5 %collective-permute-start = (s32[8,8]{1,0:T(8,128)S(1)}, s32[8,8]{1,0:T(8,128)S(1)}, u32[]{:S(2)}, u32[]{:S(2)}) collective-permute-start(s32[8,8]{1,0:T(8,128)S(1)} %broadcast_select_fusion), channel_id=1, source_target_pairs={{0,4},{1,5},{2,6},{3,7},{4,0},{5,1},{6,2},{7,3},{8,12},{9,13},{10,... | collective-permute-start | bytes 776 | tf_op jit(solution)/shard_map/ppermute | solution.py:444
  6.1 3.7 %collective-permute-start.1 = (s32[8,8]{1,0:T(8,128)S(1)}, s32[8,8]{1,0:T(8,128)S(1)}, u32[]{:S(2)}, u32[]{:S(2)}) collective-permute-start(s32[8,8]{1,0:T(8,128)S(1)} %fusion), channel_id=1, source_target_pairs={{0,8},{1,9},{2,10},{3,11},{4,12},{5,13},{6,14},{7,15},{8,0},{9,1},... | collective-permute-start | bytes 776 | tf_op jit(solution)/shard_map/ppermute | solution.py:444
  9.8 4.6 %collective-permute-start.2 = (s32[8,8]{1,0:T(8,128)S(1)}, s32[8,8]{1,0:T(8,128)S(1)}, u32[]{:S(2)}, u32[]{:S(2)}) collective-permute-start(s32[8,8]{1,0:T(8,128)S(1)} %fusion.2), channel_id=1, source_target_pairs={{0,16},{1,17},{2,18},{3,19},{4,20},{5,21},{6,22},{7,23},{8,24},{9,... | collective-permute-start | bytes 776 | tf_op jit(solution)/shard_map/ppermute | solution.py:444
  14.5 1.0 copy-start
  16.1 17.7 %collective-permute-start.6 = (bf16[64,512]{1,0:T(8,128)(2,1)S(1)}, bf16[64,512]{1,0:T(8,128)(2,1)S(1)}, u32[]{:S(2)}, u32[]{:S(2)}) collective-permute-start(bf16[64,512]{1,0:T(8,128)(2,1)S(1)} %get-tuple-element.79), channel_id=1, source_target_pairs={{0,16},{1,17},{2,18},{3,19},{4,20},{5,21},{6,22},{7,23},{8,24},{9,... | collective-permute-start | bytes 196616 | tf_op jit(solution)/shard_map/ppermute | solution.py:444
  19.1 14.7 %collective-permute-start.7 = (bf16[64,512]{1,0:T(8,128)(2,1)S(1)}, bf16[64,512]{1,0:T(8,128)(2,1)S(1)}, u32[]{:S(2)}, u32[]{:S(2)}) collective-permute-start(bf16[64,512]{1,0:T(8,128)(2,1)S(1)} %get-tuple-element.80), channel_id=1, source_target_pairs={{0,20},{1,21},{2,22},{3,23},{4,16},{5,17},{6,18},{7,19},{8,28},{9,... | collective-permute-start | bytes 196616 | tf_op jit(solution)/shard_map/ppermute | solution.py:444
  20.4 15.2 %collective-permute-start.8 = (bf16[64,512]{1,0:T(8,128)(2,1)S(1)}, bf16[64,512]{1,0:T(8,128)(2,1)S(1)}, u32[]{:S(2)}, u32[]{:S(2)}) collective-permute-start(bf16[64,512]{1,0:T(8,128)(2,1)S(1)} %get-tuple-element.81), channel_id=1, source_target_pairs={{0,24},{1,25},{2,26},{3,27},{4,28},{5,29},{6,30},{7,31},{8,16},{9,... | collective-permute-start | bytes 196616 | tf_op jit(solution)/shard_map/ppermute | solution.py:444
  24.0 11.6 %collective-permute-start.9 = (bf16[64,512]{1,0:T(8,128)(2,1)S(1)}, bf16[64,512]{1,0:T(8,128)(2,1)S(1)}, u32[]{:S(2)}, u32[]{:S(2)}) collective-permute-start(bf16[64,512]{1,0:T(8,128)(2,1)S(1)} %get-tuple-element.82), channel_id=1, source_target_pairs={{0,28},{1,29},{2,30},{3,31},{4,24},{5,25},{6,26},{7,27},{8,20},{9,... | collective-permute-start | bytes 196616 | tf_op jit(solution)/shard_map/ppermute | solution.py:444
  24.0 1.6 %copy-start.1 = (bf16[512,2048]{1,0:T(8,128)(2,1)S(1)}, bf16[512,2048]{1,0:T(8,128)(2,1)}, u32[]{:S(2)}) copy-start(bf16[512,2048]{1,0:T(8,128)(2,1)} %refs_11_.1) | copy-start | bytes 6291460
  25.6 0.9 copy-start.4
  26.5 12.5 %copy-start.2 = (bf16[512,2048]{1,0:T(8,128)(2,1)S(1)}, bf16[512,2048]{1,0:T(8,128)(2,1)}, u32[]{:S(2)}) copy-start(bf16[512,2048]{1,0:T(8,128)(2,1)} %refs_11_.1) | copy-start | bytes 6291460
  26.5 12.5 %copy-start.3 = (bf16[512,512]{1,0:T(8,128)(2,1)S(1)}, bf16[512,512]{1,0:T(8,128)(2,1)}, u32[]{:S(2)}) copy-start(bf16[512,512]{1,0:T(8,128)(2,1)} %refs_0_.1) | copy-start | bytes 1572868
  26.5 12.5 %copy-start.5 = (s32[8]{0:T(128)S(1)}, s32[8]{0:T(128)}, u32[]{:S(2)}) copy-start(s32[8]{0:T(128)} %dest_ref.1) | copy-start | bytes 100
  26.5 12.5 %copy-start.6 = (s32[8]{0:T(128)S(1)}, s32[8]{0:T(128)}, u32[]{:S(2)}) copy-start(s32[8]{0:T(128)} %blocks_ref.1) | copy-start | bytes 100
  32.0 4.3 %collective-permute-start.3 = (bf16[64,512]{1,0:T(8,128)(2,1)S(1)}, bf16[64,512]{1,0:T(8,128)(2,1)S(1)}, u32[]{:S(2)}, u32[]{:S(2)}) collective-permute-start(bf16[64,512]{1,0:T(8,128)(2,1)S(1)} %get-tuple-element.76), channel_id=1, source_target_pairs={{0,4},{1,5},{2,6},{3,7},{4,0},{5,1},{6,2},{7,3},{8,12},{9,13},{10,... | collective-permute-start | bytes 196616 | tf_op jit(solution)/shard_map/ppermute | solution.py:444
  33.8 4.3 %collective-permute-start.4 = (bf16[64,512]{1,0:T(8,128)(2,1)S(1)}, bf16[64,512]{1,0:T(8,128)(2,1)S(1)}, u32[]{:S(2)}, u32[]{:S(2)}) collective-permute-start(bf16[64,512]{1,0:T(8,128)(2,1)S(1)} %get-tuple-element.77), channel_id=1, source_target_pairs={{0,8},{1,9},{2,10},{3,11},{4,12},{5,13},{6,14},{7,15},{8,0},{9,1},... | collective-permute-start | bytes 196616 | tf_op jit(solution)/shard_map/ppermute | solution.py:444
  33.8 5.2 %collective-permute-start.5 = (bf16[64,512]{1,0:T(8,128)(2,1)S(1)}, bf16[64,512]{1,0:T(8,128)(2,1)S(1)}, u32[]{:S(2)}, u32[]{:S(2)}) collective-permute-start(bf16[64,512]{1,0:T(8,128)(2,1)S(1)} %get-tuple-element.78), channel_id=1, source_target_pairs={{0,12},{1,13},{2,14},{3,15},{4,8},{5,9},{6,10},{7,11},{8,4},{9,5},... | collective-permute-start | bytes 196616 | tf_op jit(solution)/shard_map/ppermute | solution.py:444
  47.9 5.9 %collective-permute-start.10 = (bf16[16,16,1280]{2,1,0:T(8,128)(2,1)S(1)}, bf16[16,16,1280]{2,1,0:T(8,128)(2,1)}, u32[]{:S(2)}, u32[]{:S(2)}) collective-permute-start(bf16[16,16,1280]{2,1,0:T(8,128)(2,1)S(1)} %get-tuple-element.84), channel_id=1, source_target_pairs={{0,1},{1,0},{2,3},{3,2},{4,5},{5,4},{6,7},{7,6},{8,9},{9,8},{10,11... | collective-permute-start | bytes 1966088 | tf_op jit(solution)/shard_map/ppermute | solution.py:444
  47.9 8.7 %collective-permute-start.13 = (bf16[16,16,1280]{2,1,0:T(8,128)(2,1)S(1)}, bf16[16,16,1280]{2,1,0:T(8,128)(2,1)}, u32[]{:S(2)}, u32[]{:S(2)}) collective-permute-start(bf16[16,16,1280]{2,1,0:T(8,128)(2,1)S(1)} %get-tuple-element.86), channel_id=1, source_target_pairs={{0,1},{1,0},{2,3},{3,2},{4,5},{5,4},{6,7},{7,6},{8,9},{9,8},{10,11... | collective-permute-start | bytes 1966088 | tf_op jit(solution)/shard_map/ppermute | solution.py:444
  48.4 25.1 %all-to-all-start = ((bf16[4,8,16,640]{3,2,1,0:T(8,128)(2,1)}), bf16[4,8,16,640]{3,2,1,0:T(8,128)(2,1)S(1)}, u32[]{:S(2)}, u32[]{:S(2)}) async-start(bf16[4,8,16,640]{3,2,1,0:T(8,128)(2,1)} %bitcast.5), calls=%async_computation | async-start | bytes 1310720 | tf_op jit(solution)/shard_map/all_to_all | solution.py:447
  55.0 9.4 %collective-permute-start.11 = (bf16[8,16,1280]{2,1,0:T(8,128)(2,1)S(1)}, bf16[8,16,1280]{2,1,0:T(8,128)(2,1)S(1)}, u32[]{:S(2)}, u32[]{:S(2)}) collective-permute-start(bf16[8,16,1280]{2,1,0:T(8,128)(2,1)S(1)} %slice.57), channel_id=1, source_target_pairs={{0,2},{1,3},{2,0},{3,1},{4,6},{5,7},{6,4},{7,5},{8,10},{9,11},{10,... | collective-permute-start | bytes 983048 | tf_op jit(solution)/shard_map/ppermute | solution.py:444
  57.9 10.0 %collective-permute-start.14 = (bf16[8,16,1280]{2,1,0:T(8,128)(2,1)S(1)}, bf16[8,16,1280]{2,1,0:T(8,128)(2,1)S(1)}, u32[]{:S(2)}, u32[]{:S(2)}) collective-permute-start(bf16[8,16,1280]{2,1,0:T(8,128)(2,1)S(1)} %slice.61), channel_id=1, source_target_pairs={{0,4},{1,5},{2,6},{3,7},{4,0},{5,1},{6,2},{7,3},{8,12},{9,13},{10,... | collective-permute-start | bytes 983048 | tf_op jit(solution)/shard_map/ppermute | solution.py:444
  64.6 6.0 %collective-permute-start.12 = (bf16[4,16,1280]{2,1,0:T(8,128)(2,1)S(1)}, bf16[4,16,1280]{2,1,0:T(8,128)(2,1)S(1)}, u32[]{:S(2)}, u32[]{:S(2)}) collective-permute-start(bf16[4,16,1280]{2,1,0:T(8,128)(2,1)S(1)} %slice.59), channel_id=1, source_target_pairs={{0,4},{1,5},{2,6},{3,7},{4,0},{5,1},{6,2},{7,3},{8,12},{9,13},{10,... | collective-permute-start | bytes 491528 | tf_op jit(solution)/shard_map/ppermute | solution.py:444
  68.0 5.4 %collective-permute-start.15 = (bf16[4,16,1280]{2,1,0:T(8,128)(2,1)S(1)}, bf16[4,16,1280]{2,1,0:T(8,128)(2,1)S(1)}, u32[]{:S(2)}, u32[]{:S(2)}) collective-permute-start(bf16[4,16,1280]{2,1,0:T(8,128)(2,1)S(1)} %slice.63), channel_id=1, source_target_pairs={{0,2},{1,3},{2,0},{3,1},{4,6},{5,7},{6,4},{7,5},{8,10},{9,11},{10,... | collective-permute-start | bytes 491528 | tf_op jit(solution)/shard_map/ppermute | solution.py:444
  73.5 6.3 %collective-permute-start.16 = (bf16[2,16,2560]{2,1,0:T(8,128)(2,1)S(1)}, bf16[2,16,2560]{2,1,0:T(8,128)(2,1)S(1)}, u32[]{:S(2)}, u32[]{:S(2)}) collective-permute-start(bf16[2,16,2560]{2,1,0:T(8,128)(2,1)S(1)} %slice.51), channel_id=1, source_target_pairs={{0,8},{1,9},{2,10},{3,11},{4,12},{5,13},{6,14},{7,15},{8,0},{9,1},... | collective-permute-start | bytes 491528 | tf_op jit(solution)/shard_map/ppermute | solution.py:444
  79.9 5.8 %collective-permute-start.17 = (bf16[1,16,2560]{2,1,0:T(8,128)(2,1)S(1)}, bf16[1,16,2560]{2,1,0:T(8,128)(2,1)S(1)}, u32[]{:S(2)}, u32[]{:S(2)}) collective-permute-start(bf16[1,16,2560]{2,1,0:T(8,128)(2,1)S(1)} %slice.65), channel_id=1, source_target_pairs={{0,16},{1,17},{2,18},{3,19},{4,20},{5,21},{6,22},{7,23},{8,24},{9,... | collective-permute-start | bytes 245768 | tf_op jit(solution)/shard_map/ppermute | solution.py:444
  85.7 6.5 %collective-permute-start.18 = (bf16[1,16,2560]{2,1,0:T(8,128)(2,1)S(1)}, bf16[1,16,2560]{2,1,0:T(8,128)(2,1)S(1)}, u32[]{:S(2)}, u32[]{:S(2)}) collective-permute-start(bf16[1,16,2560]{2,1,0:T(8,128)(2,1)S(1)} %add_convert_fusion.7), channel_id=1, source_target_pairs={{0,16},{1,17},{2,18},{3,19},{4,20},{5,21},{6,22},{7,23},{8,24},{9,... | collective-permute-start | bytes 245768 | tf_op jit(solution)/shard_map/ppermute | solution.py:444
  88.7 13.7 %all-to-all-start.1 = ((bf16[8,4,16,640]{3,2,1,0:T(8,128)(2,1)}), bf16[8,4,16,640]{3,2,1,0:T(8,128)(2,1)S(1)}, u32[]{:S(2)}, u32[]{:S(2)}) async-start(bf16[8,4,16,640]{3,2,1,0:T(8,128)(2,1)} %copy.18), calls=%async_computation.1 | async-start | bytes 1310720 | tf_op jit(solution)/shard_map/all_to_all | solution.py:447
  92.3 7.7 %collective-permute-start.19 = (bf16[2,16,2560]{2,1,0:T(8,128)(2,1)S(1)}, bf16[2,16,2560]{2,1,0:T(8,128)(2,1)S(1)}, u32[]{:S(2)}, u32[]{:S(2)}) collective-permute-start(bf16[2,16,2560]{2,1,0:T(8,128)(2,1)S(1)} %pad_maximum_fusion.6), channel_id=1, source_target_pairs={{0,8},{1,9},{2,10},{3,11},{4,12},{5,13},{6,14},{7,15},{8,0},{9,1},... | collective-permute-start | bytes 491528 | tf_op jit(solution)/shard_map/ppermute | solution.py:444
  104.6 5.8 %collective-permute-start.20 = (bf16[4,16,1280]{2,1,0:T(8,128)(2,1)S(1)}, bf16[4,16,1280]{2,1,0:T(8,128)(2,1)S(1)}, u32[]{:S(2)}, u32[]{:S(2)}) collective-permute-start(bf16[4,16,1280]{2,1,0:T(8,128)(2,1)S(1)} %get-tuple-element.98), channel_id=1, source_target_pairs={{0,4},{1,5},{2,6},{3,7},{4,0},{5,1},{6,2},{7,3},{8,12},{9,13},{10,... | collective-permute-start | bytes 491528 | tf_op jit(solution)/shard_map/ppermute | solution.py:444
  106.1 5.8 %collective-permute-start.23 = (bf16[4,16,1280]{2,1,0:T(8,128)(2,1)S(1)}, bf16[4,16,1280]{2,1,0:T(8,128)(2,1)S(1)}, u32[]{:S(2)}, u32[]{:S(2)}) collective-permute-start(bf16[4,16,1280]{2,1,0:T(8,128)(2,1)S(1)} %get-tuple-element.97), channel_id=1, source_target_pairs={{0,2},{1,3},{2,0},{3,1},{4,6},{5,7},{6,4},{7,5},{8,10},{9,11},{10,... | collective-permute-start | bytes 491528 | tf_op jit(solution)/shard_map/ppermute | solution.py:444
  110.4 8.4 %collective-permute-start.21 = (bf16[8,16,1280]{2,1,0:T(8,128)(2,1)S(1)}, bf16[8,16,1280]{2,1,0:T(8,128)(2,1)S(1)}, u32[]{:S(2)}, u32[]{:S(2)}) collective-permute-start(bf16[8,16,1280]{2,1,0:T(8,128)(2,1)S(1)} %pad_maximum_fusion.4), channel_id=1, source_target_pairs={{0,2},{1,3},{2,0},{3,1},{4,6},{5,7},{6,4},{7,5},{8,10},{9,11},{10,... | collective-permute-start | bytes 983048 | tf_op jit(solution)/shard_map/ppermute | solution.py:444
  112.0 8.1 %collective-permute-start.24 = (bf16[8,16,1280]{2,1,0:T(8,128)(2,1)S(1)}, bf16[8,16,1280]{2,1,0:T(8,128)(2,1)S(1)}, u32[]{:S(2)}, u32[]{:S(2)}) collective-permute-start(bf16[8,16,1280]{2,1,0:T(8,128)(2,1)S(1)} %pad_maximum_fusion.5), channel_id=1, source_target_pairs={{0,4},{1,5},{2,6},{3,7},{4,0},{5,1},{6,2},{7,3},{8,12},{9,13},{10,... | collective-permute-start | bytes 983048 | tf_op jit(solution)/shard_map/ppermute | solution.py:444
  118.9 2.2 %collective-permute-start.22 = (bf16[16,16,1280]{2,1,0:T(8,128)(2,1)S(1)}, bf16[16,16,1280]{2,1,0:T(8,128)(2,1)S(1)}, u32[]{:S(2)}, u32[]{:S(2)}) collective-permute-start(bf16[16,16,1280]{2,1,0:T(8,128)(2,1)S(1)} %pad_maximum_fusion.refs_0_), channel_id=1, source_target_pairs={{0,1},{1,0},{2,3},{3,2},{4,5},{5,4},{6,7},{7,6},{8,9},{9,8},{10,11... | collective-permute-start | bytes 1966088 | tf_op jit(solution)/shard_map/ppermute | solution.py:444
  120.2 2.2 %collective-permute-start.25 = (bf16[16,16,1280]{2,1,0:T(8,128)(2,1)S(1)}, bf16[16,16,1280]{2,1,0:T(8,128)(2,1)S(1)}, u32[]{:S(2)}, u32[]{:S(2)}) collective-permute-start(bf16[16,16,1280]{2,1,0:T(8,128)(2,1)S(1)} %pad_maximum_fusion.1.refs_2_), channel_id=1, source_target_pairs={{0,1},{1,0},{2,3},{3,2},{4,5},{5,4},{6,7},{7,6},{8,9},{9,8},{10,11... | collective-permute-start | bytes 1966088 | tf_op jit(solution)/shard_map/ppermute | solution.py:444

commit v13 on v12

--- a/solution.py
+++ b/solution.py
@@ -460,10 +460,9 @@
         scratch=[pltpu.SMEM((dp_size,), jnp.int32)],
     )(me, lengths, grad_out)
     got = list(send)
-    far = [apart for apart in range(1, dp_size) if 2 * apart >= dp_size]
-    for apart in far:
+    for apart in reversed(range(1, dp_size)):
         got[apart] = swap(send[apart], apart * table_size)
-    *near, ints = lax.optimization_barrier((*send[: far[0]], ints))
+    got[0], ints = lax.optimization_barrier((got[0], ints))
 
     shapes = saved_shapes(tokens, count, width)
     saved = call(
@@ -479,11 +478,6 @@
         gain_rows,
         ints,
     )
-    *near, gate = lax.optimization_barrier((*near, saved[0]))
-    saved = [gate, *saved[1:]]
-    got[0] = near[0]
-    for apart in range(1, far[0]):
-        got[apart] = swap(near[apart], apart * table_size)
     saved = dict(zip(SAVED, saved), w_in=w_in, w_out=w_out)
     outs = [shape_of((devices_all * plan.capacity, width + plan.extra), BF16)]
     for _, wide in plan.sides:
@@ -529,6 +523,11 @@
     kept, table_got = lax.optimization_barrier((kept, table_got))
     groups = [[upper * inside + lower for lower in range(inside)] for upper in range(high)]
     table_got = exchange(jnp.swapaxes(table_got, 0, 1), both, groups)
+    for mask in plan.orders[0][plan.near_steps :]:
+        kept = reduced(kept, mask)
+    back = plan.orders[0][: plan.near_steps - 1 : -1]
+    kept = gathered(kept, back[0])
+    kept, table_got = lax.optimization_barrier((kept, table_got))
     table_part, grad_gain_in, grad_gain_out = call(
         functools.partial(table_body, plan),
         (
@@ -538,9 +537,7 @@
         ),
         [VMEM],
     )(table_got.reshape(devices_all * plan.capacity, -1))
-    for mask in plan.orders[0][plan.near_steps :]:
-        kept = reduced(kept, mask)
-    for mask in reversed(plan.orders[0][plan.near_steps :]):
+    for mask in back[1:]:
         kept = gathered(kept, mask)
     kept, table_part = lax.optimization_barrier((kept, table_part))
     sides = [kept[..., : plan.split], kept[..., plan.split :]]

time: 126 us -> 120 us (0.952)
  waiting for transfers between devices: 48.2 us -> 42.1 us
    ppermute x26, waiting for transfers between devices: 45.8 us -> 39.4 us  [swap(): lax.ppermute(values, both, [(here, here ^ mask) for here in range(devices...]
  transfers between devices with their start and end apart: 28 -> 28, of which waited for: 19 -> 16; matrix products, arithmetic and copies ran while one was open for 4% -> 5% of each run, Pallas kernels for 4% -> 6%
where the time goes in v13:
time: 120 us; the launch traced here: 119 us
  starting transfers between devices  46.4 us (39%)
  waiting for transfers between devices  42.1 us (35%)
  Pallas kernels  19.8 us (16%)
  other arithmetic  5.46 us (5%)
  local copies, waits for them, and re-layouts  4.52 us (4%)
    ppermute x26, waiting for transfers between devices, swap(): lax.ppermute(values, both, [(here, here ^ mask) for here in range(devices...  39.4 us
    ppermute x26, starting transfers between devices, swap(): lax.ppermute(values, both, [(here, here ^ mask) for here in range(devices...  37.8 us
    pallas_call x1, Pallas kernels, on_device(): call(functools.partial(backward_body, plan, table_size, total_factor), ou...  8.85 us
    all_to_all x2, starting transfers between devices, exchange(): lax.all_to_all(values, axes, split_axis=0, concat_axis=0, tiled=True, axi...  8.57 us
    pallas_call x1, Pallas kernels, on_device(): call(functools.partial(forward_body, plan.capacity), [shapes[name] for na...  5.51 us
    unnamed x14, local copies, waits for them, and re-layouts  3.5 us
    convert_element_type x8, other arithmetic, add(): return (left.astype(F32) + right.astype(F32)).astype(BF16)  2.78 us
    all_to_all x2, waiting for transfers between devices, exchange(): lax.all_to_all(values, axes, split_axis=0, concat_axis=0, tiled=True, axi...  2.65 us
  transfers between devices with their start and end apart: 28, of which 16 were waited for; matrix products, arithmetic and copies ran while one was open for 5% of the time, Pallas kernels for 6%

profile of v13, /device:TPU:0, one launch (start us, length us, event | category | flops | bytes accessed | tf_op | source)
XLA Modules:
  0.0 119.2 jit_solution(15513832420689108683)
XLA Ops:
  0.6 0.8 select_reduce_fusion
  1.5 2.9 %collective-permute-start = (s32[8,8]{1,0:T(8,128)S(1)}, s32[8,8]{1,0:T(8,128)S(1)}, u32[]{:S(2)}, u32[]{:S(2)}) collective-permute-start(s32[8,8]{1,0:T(8,128)S(1)} %broadcast_select_fusion), channel_id=1, source_target_pairs={{0,4},{1,5},{2,6},{3,7},{4,0},{5,1},{6,2},{7,3},{8,12},{9,13},{10,... | collective-permute-start | bytes 776 | tf_op jit(solution)/shard_map/ppermute | solution.py:444
  4.4 1.6 %collective-permute-done = s32[8,8]{1,0:T(8,128)S(1)} collective-permute-done((s32[8,8]{1,0:T(8,128)S(1)}, s32[8,8]{1,0:T(8,128)S(1)}, u32[]{:S(2)}, u32[]{:S(2)}) %collective-permute-start) | collective-permute-done | bytes 288 | tf_op jit(solution)/shard_map/ppermute | solution.py:444
  6.1 2.1 %collective-permute-start.1 = (s32[8,8]{1,0:T(8,128)S(1)}, s32[8,8]{1,0:T(8,128)S(1)}, u32[]{:S(2)}, u32[]{:S(2)}) collective-permute-start(s32[8,8]{1,0:T(8,128)S(1)} %fusion), channel_id=1, source_target_pairs={{0,8},{1,9},{2,10},{3,11},{4,12},{5,13},{6,14},{7,15},{8,0},{9,1},... | collective-permute-start | bytes 776 | tf_op jit(solution)/shard_map/ppermute | solution.py:444
  8.9 0.9 collective-permute-done.1
  9.8 3.0 %collective-permute-start.2 = (s32[8,8]{1,0:T(8,128)S(1)}, s32[8,8]{1,0:T(8,128)S(1)}, u32[]{:S(2)}, u32[]{:S(2)}) collective-permute-start(s32[8,8]{1,0:T(8,128)S(1)} %fusion.2), channel_id=1, source_target_pairs={{0,16},{1,17},{2,18},{3,19},{4,20},{5,21},{6,22},{7,23},{8,24},{9,... | collective-permute-start | bytes 776 | tf_op jit(solution)/shard_map/ppermute | solution.py:444
  12.9 1.6 %collective-permute-done.2 = s32[8,8]{1,0:T(8,128)S(1)} collective-permute-done((s32[8,8]{1,0:T(8,128)S(1)}, s32[8,8]{1,0:T(8,128)S(1)}, u32[]{:S(2)}, u32[]{:S(2)}) %collective-permute-start.2) | collective-permute-done | bytes 288 | tf_op jit(solution)/shard_map/ppermute | solution.py:444
  14.5 0.9 copy-done
  16.1 1.9 %collective-permute-start.3 = (bf16[64,512]{1,0:T(8,128)(2,1)S(1)}, bf16[64,512]{1,0:T(8,128)(2,1)S(1)}, u32[]{:S(2)}, u32[]{:S(2)}) collective-permute-start(bf16[64,512]{1,0:T(8,128)(2,1)S(1)} %get-tuple-element.62), channel_id=1, source_target_pairs={{0,4},{1,5},{2,6},{3,7},{4,0},{5,1},{6,2},{7,3},{8,12},{9,13},{10,... | collective-permute-start | bytes 196616 | tf_op jit(solution)/shard_map/ppermute | solution.py:444
  18.0 1.6 %collective-permute-start.4 = (bf16[64,512]{1,0:T(8,128)(2,1)S(1)}, bf16[64,512]{1,0:T(8,128)(2,1)S(1)}, u32[]{:S(2)}, u32[]{:S(2)}) collective-permute-start(bf16[64,512]{1,0:T(8,128)(2,1)S(1)} %get-tuple-element.63), channel_id=1, source_target_pairs={{0,8},{1,9},{2,10},{3,11},{4,12},{5,13},{6,14},{7,15},{8,0},{9,1},... | collective-permute-start | bytes 196616 | tf_op jit(solution)/shard_map/ppermute | solution.py:444
  20.4 2.9 %collective-permute-start.6 = (bf16[64,512]{1,0:T(8,128)(2,1)S(1)}, bf16[64,512]{1,0:T(8,128)(2,1)S(1)}, u32[]{:S(2)}, u32[]{:S(2)}) collective-permute-start(bf16[64,512]{1,0:T(8,128)(2,1)S(1)} %get-tuple-element.65), channel_id=1, source_target_pairs={{0,16},{1,17},{2,18},{3,19},{4,20},{5,21},{6,22},{7,23},{8,24},{9,... | collective-permute-start | bytes 196616 | tf_op jit(solution)/shard_map/ppermute | solution.py:444
  23.3 1.3 %collective-permute-start.7 = (bf16[64,512]{1,0:T(8,128)(2,1)S(1)}, bf16[64,512]{1,0:T(8,128)(2,1)S(1)}, u32[]{:S(2)}, u32[]{:S(2)}) collective-permute-start(bf16[64,512]{1,0:T(8,128)(2,1)S(1)} %get-tuple-element.66), channel_id=1, source_target_pairs={{0,20},{1,21},{2,22},{3,23},{4,16},{5,17},{6,18},{7,19},{8,28},{9,... | collective-permute-start | bytes 196616 | tf_op jit(solution)/shard_map/ppermute | solution.py:444
  24.6 3.6 %collective-permute-start.8 = (bf16[64,512]{1,0:T(8,128)(2,1)S(1)}, bf16[64,512]{1,0:T(8,128)(2,1)S(1)}, u32[]{:S(2)}, u32[]{:S(2)}) collective-permute-start(bf16[64,512]{1,0:T(8,128)(2,1)S(1)} %get-tuple-element.67), channel_id=1, source_target_pairs={{0,24},{1,25},{2,26},{3,27},{4,28},{5,29},{6,30},{7,31},{8,16},{9,... | collective-permute-start | bytes 196616 | tf_op jit(solution)/shard_map/ppermute | solution.py:444
  28.2 1.6 %copy-done.1 = bf16[512,2048]{1,0:T(8,128)(2,1)S(1)} copy-done((bf16[512,2048]{1,0:T(8,128)(2,1)S(1)}, bf16[512,2048]{1,0:T(8,128)(2,1)}, u32[]{:S(2)}) %copy-start.1) | copy-done | bytes 2097176
  29.8 0.9 copy-done.4
  30.8 5.5 %shard_map.147 = (f32[512,512]{1,0:T(8,128)S(1)}, f32[512,512]{1,0:T(8,128)S(1)}, f32[512,1]{1,0:T(8,128)S(1)}, bf16[512,1536]{1,0:T(8,128)(2,1)S(1)}, bf16[16,1...) custom-call(bf16[256,512]{1,0:T(8,128)(2,1)S(1)} %copy-done.4, ...), custom_call_target="tpu_custom_call" | custom-call | flops 5368709120 | bytes 10000000 | tf_op jit(solution)/shard_map/pallas_call | solution.py:468
  36.4 8.8 %shard_map.148 = (bf16[512,640]{1,0:T(8,128)(2,1)}, bf16[16,16,1280]{2,1,0:T(8,128)(2,1)S(1)}, bf16[16,16,1280]{2,1,0:T(8,128)(2,1)S(1)}, bf16[16,16,1280]{2,1,0:T(8,128)(2,1)S(1)}, bf16[16,16,1280]{2,1,0:T(8,128)(2,1)S(1)}) custom-call(s32[1]{0:T(128)} %bitcast.me_ref, s32[8]{0:T(128)S(1)} %copy-done.5, s32[8]{0:T(128)S(1)} %copy-done.6, ...), custom_call_target="tpu_custom_call" | custom-call | flops 10737418240 | bytes 12000000 | tf_op jit(solution)/shard_map/pallas_call | solution.py:485
  45.8 5.0 %all-to-all-start = ((bf16[4,8,16,640]{3,2,1,0:T(8,128)(2,1)}), bf16[4,8,16,640]{3,2,1,0:T(8,128)(2,1)S(1)}, u32[]{:S(2)}, u32[]{:S(2)}) async-start(bf16[4,8,16,640]{3,2,1,0:T(8,128)(2,1)} %bitcast.5), calls=%async_computation | async-start | bytes 1310720 | tf_op jit(solution)/shard_map/all_to_all | solution.py:447
  50.8 1.2 %add_convert_fusion.1 = bf16[16,16,1280]{2,1,0:T(8,128)(2,1)S(1)} fusion(bf16[16,16,1280]{2,1,0:T(8,128)(2,1)} %collective-permute-done.10, bf16[16,16,1280]{2,1,0:T(8,128)(2,1)S(1)} %get-tuple-element.69), kind=kLoop, calls=%fused_computation.1 | loop fusion | flops 1310720 | bytes 1966080 | tf_op jit(solution)/shard_map/convert_element_type | solution.py:416
  52.1 1.6 %collective-permute-start.11 = (bf16[8,16,1280]{2,1,0:T(8,128)(2,1)S(1)}, bf16[8,16,1280]{2,1,0:T(8,128)(2,1)S(1)}, u32[]{:S(2)}, u32[]{:S(2)}) collective-permute-start(bf16[8,16,1280]{2,1,0:T(8,128)(2,1)S(1)} %slice.57), channel_id=1, source_target_pairs={{0,2},{1,3},{2,0},{3,1},{4,6},{5,7},{6,4},{7,5},{8,10},{9,11},{10,... | collective-permute-start | bytes 983048 | tf_op jit(solution)/shard_map/ppermute | solution.py:444
  53.6 1.2 %add_convert_fusion = bf16[16,16,1280]{2,1,0:T(8,128)(2,1)S(1)} fusion(bf16[16,16,1280]{2,1,0:T(8,128)(2,1)} %collective-permute-done.13, bf16[16,16,1280]{2,1,0:T(8,128)(2,1)S(1)} %get-tuple-element.71), kind=kLoop, calls=%fused_computation | loop fusion | flops 1310720 | bytes 1966080 | tf_op jit(solution)/shard_map/convert_element_type | solution.py:416
  54.9 1.6 %collective-permute-start.14 = (bf16[8,16,1280]{2,1,0:T(8,128)(2,1)S(1)}, bf16[8,16,1280]{2,1,0:T(8,128)(2,1)S(1)}, u32[]{:S(2)}, u32[]{:S(2)}) collective-permute-start(bf16[8,16,1280]{2,1,0:T(8,128)(2,1)S(1)} %slice.61), channel_id=1, source_target_pairs={{0,4},{1,5},{2,6},{3,7},{4,0},{5,1},{6,2},{7,3},{8,12},{9,13},{10,... | collective-permute-start | bytes 983048 | tf_op jit(solution)/shard_map/ppermute | solution.py:444
  56.5 5.0 %collective-permute-done.11 = bf16[8,16,1280]{2,1,0:T(8,128)(2,1)S(1)} collective-permute-done((bf16[8,16,1280]{2,1,0:T(8,128)(2,1)S(1)}, bf16[8,16,1280]{2,1,0:T(8,128)(2,1)S(1)}, u32[]{:S(2)}, u32[]{:S(2)}) %collective-permute-start.11) | collective-permute-done | bytes 327712 | tf_op jit(solution)/shard_map/ppermute | solution.py:444
  61.6 1.6 %collective-permute-start.12 = (bf16[4,16,1280]{2,1,0:T(8,128)(2,1)S(1)}, bf16[4,16,1280]{2,1,0:T(8,128)(2,1)S(1)}, u32[]{:S(2)}, u32[]{:S(2)}) collective-permute-start(bf16[4,16,1280]{2,1,0:T(8,128)(2,1)S(1)} %slice.59), channel_id=1, source_target_pairs={{0,4},{1,5},{2,6},{3,7},{4,0},{5,1},{6,2},{7,3},{8,12},{9,13},{10,... | collective-permute-start | bytes 491528 | tf_op jit(solution)/shard_map/ppermute | solution.py:444
  63.1 1.8 %collective-permute-done.14 = bf16[8,16,1280]{2,1,0:T(8,128)(2,1)S(1)} collective-permute-done((bf16[8,16,1280]{2,1,0:T(8,128)(2,1)S(1)}, bf16[8,16,1280]{2,1,0:T(8,128)(2,1)S(1)}, u32[]{:S(2)}, u32[]{:S(2)}) %collective-permute-start.14) | collective-permute-done | bytes 327712 | tf_op jit(solution)/shard_map/ppermute | solution.py:444
  65.1 2.4 %collective-permute-done.12 = bf16[4,16,1280]{2,1,0:T(8,128)(2,1)S(1)} collective-permute-done((bf16[4,16,1280]{2,1,0:T(8,128)(2,1)S(1)}, bf16[4,16,1280]{2,1,0:T(8,128)(2,1)S(1)}, u32[]{:S(2)}, u32[]{:S(2)}) %collective-permute-start.12) | collective-permute-done | bytes 163872 | tf_op jit(solution)/shard_map/ppermute | solution.py:444
  67.6 2.9 %collective-permute-done.15 = bf16[4,16,1280]{2,1,0:T(8,128)(2,1)S(1)} collective-permute-done((bf16[4,16,1280]{2,1,0:T(8,128)(2,1)S(1)}, bf16[4,16,1280]{2,1,0:T(8,128)(2,1)S(1)}, u32[]{:S(2)}, u32[]{:S(2)}) %collective-permute-start.15) | collective-permute-done | bytes 163872 | tf_op jit(solution)/shard_map/ppermute | solution.py:444
  70.6 2.1 %collective-permute-start.16 = (bf16[2,16,2560]{2,1,0:T(8,128)(2,1)S(1)}, bf16[2,16,2560]{2,1,0:T(8,128)(2,1)S(1)}, u32[]{:S(2)}, u32[]{:S(2)}) collective-permute-start(bf16[2,16,2560]{2,1,0:T(8,128)(2,1)S(1)} %slice.51), channel_id=1, source_target_pairs={{0,8},{1,9},{2,10},{3,11},{4,12},{5,13},{6,14},{7,15},{8,0},{9,1},... | collective-permute-start | bytes 491528 | tf_op jit(solution)/shard_map/ppermute | solution.py:444
  72.7 4.2 %collective-permute-done.16 = bf16[2,16,2560]{2,1,0:T(8,128)(2,1)S(1)} collective-permute-done((bf16[2,16,2560]{2,1,0:T(8,128)(2,1)S(1)}, bf16[2,16,2560]{2,1,0:T(8,128)(2,1)S(1)}, u32[]{:S(2)}, u32[]{:S(2)}) %collective-permute-start.16) | collective-permute-done | bytes 163872 | tf_op jit(solution)/shard_map/ppermute | solution.py:444
  76.9 2.5 %collective-permute-start.17 = (bf16[1,16,2560]{2,1,0:T(8,128)(2,1)S(1)}, bf16[1,16,2560]{2,1,0:T(8,128)(2,1)S(1)}, u32[]{:S(2)}, u32[]{:S(2)}) collective-permute-start(bf16[1,16,2560]{2,1,0:T(8,128)(2,1)S(1)} %slice.65), channel_id=1, source_target_pairs={{0,16},{1,17},{2,18},{3,19},{4,20},{5,21},{6,22},{7,23},{8,24},{9,... | collective-permute-start | bytes 245768 | tf_op jit(solution)/shard_map/ppermute | solution.py:444
  79.4 0.9 copy.18
  80.3 3.5 %all-to-all-start.1 = ((bf16[8,4,16,640]{3,2,1,0:T(8,128)(2,1)}), bf16[8,4,16,640]{3,2,1,0:T(8,128)(2,1)S(1)}, u32[]{:S(2)}, u32[]{:S(2)}) async-start(bf16[8,4,16,640]{3,2,1,0:T(8,128)(2,1)} %copy.18), calls=%async_computation.1 | async-start | bytes 1310720 | tf_op jit(solution)/shard_map/all_to_all | solution.py:447
  83.9 1.0 collective-permute-start.18
  84.8 6.5 %collective-permute-done.18 = bf16[1,16,2560]{2,1,0:T(8,128)(2,1)S(1)} collective-permute-done((bf16[1,16,2560]{2,1,0:T(8,128)(2,1)S(1)}, bf16[1,16,2560]{2,1,0:T(8,128)(2,1)S(1)}, u32[]{:S(2)}, u32[]{:S(2)}) %collective-permute-start.18) | collective-permute-done | bytes 81952 | tf_op jit(solution)/shard_map/ppermute | solution.py:444
  91.4 2.6 %all-to-all-done.1 = bf16[8,4,16,640]{3,2,1,0:T(8,128)(2,1)S(1)} async-done(((bf16[8,4,16,640]{3,2,1,0:T(8,128)(2,1)}), bf16[8,4,16,640]{3,2,1,0:T(8,128)(2,1)S(1)}, u32[]{:S(2)}, u32[]{:S(2)}) %all-to-all-start.1) | async-done | bytes 655392 | tf_op jit(solution)/shard_map/all_to_all | solution.py:447
  94.0 2.0 %collective-permute-start.19 = (bf16[2,16,2560]{2,1,0:T(8,128)(2,1)S(1)}, bf16[2,16,2560]{2,1,0:T(8,128)(2,1)S(1)}, u32[]{:S(2)}, u32[]{:S(2)}) collective-permute-start(bf16[2,16,2560]{2,1,0:T(8,128)(2,1)S(1)} %pad_maximum_fusion.6), channel_id=1, source_target_pairs={{0,8},{1,9},{2,10},{3,11},{4,12},{5,13},{6,14},{7,15},{8,0},{9,1},... | collective-permute-start | bytes 491528 | tf_op jit(solution)/shard_map/ppermute | solution.py:444
  96.0 2.2 %shard_map.149 = (f32[1024,512]{1,0:T(8,128)}, f32[1,512]{1,0:T(1,128)}, f32[1,512]{1,0:T(1,128)}) custom-call(bf16[512,640]{1,0:T(8,128)(2,1)S(1)} %bitcast.10), custom_call_target="tpu_custom_call" | custom-call | tf_op jit(solution)/shard_map/pallas_call | solution.py:531
  98.1 1.8 %collective-permute-done.19 = bf16[2,16,2560]{2,1,0:T(8,128)(2,1)S(1)} collective-permute-done((bf16[2,16,2560]{2,1,0:T(8,128)(2,1)S(1)}, bf16[2,16,2560]{2,1,0:T(8,128)(2,1)S(1)}, u32[]{:S(2)}, u32[]{:S(2)}) %collective-permute-start.19) | collective-permute-done | bytes 163872 | tf_op jit(solution)/shard_map/ppermute | solution.py:444
  100.1 0.9 collective-permute-start.20
  100.9 1.2 %collective-permute-start.23 = (bf16[4,16,1280]{2,1,0:T(8,128)(2,1)S(1)}, bf16[4,16,1280]{2,1,0:T(8,128)(2,1)S(1)}, u32[]{:S(2)}, u32[]{:S(2)}) collective-permute-start(bf16[4,16,1280]{2,1,0:T(8,128)(2,1)S(1)} %get-tuple-element.85), channel_id=1, source_target_pairs={{0,2},{1,3},{2,0},{3,1},{4,6},{5,7},{6,4},{7,5},{8,10},{9,11},{10,... | collective-permute-start | bytes 491528 | tf_op jit(solution)/shard_map/ppermute | solution.py:444
  102.1 3.3 %collective-permute-done.20 = bf16[4,16,1280]{2,1,0:T(8,128)(2,1)S(1)} collective-permute-done((bf16[4,16,1280]{2,1,0:T(8,128)(2,1)S(1)}, bf16[4,16,1280]{2,1,0:T(8,128)(2,1)S(1)}, u32[]{:S(2)}, u32[]{:S(2)}) %collective-permute-start.20) | collective-permute-done | bytes 163872 | tf_op jit(solution)/shard_map/ppermute | solution.py:444
  105.5 1.5 %collective-permute-start.21 = (bf16[8,16,1280]{2,1,0:T(8,128)(2,1)S(1)}, bf16[8,16,1280]{2,1,0:T(8,128)(2,1)S(1)}, u32[]{:S(2)}, u32[]{:S(2)}) collective-permute-start(bf16[8,16,1280]{2,1,0:T(8,128)(2,1)S(1)} %pad_maximum_fusion.4), channel_id=1, source_target_pairs={{0,2},{1,3},{2,0},{3,1},{4,6},{5,7},{6,4},{7,5},{8,10},{9,11},{10,... | collective-permute-start | bytes 983048 | tf_op jit(solution)/shard_map/ppermute | solution.py:444
  107.1 1.7 %collective-permute-start.24 = (bf16[8,16,1280]{2,1,0:T(8,128)(2,1)S(1)}, bf16[8,16,1280]{2,1,0:T(8,128)(2,1)S(1)}, u32[]{:S(2)}, u32[]{:S(2)}) collective-permute-start(bf16[8,16,1280]{2,1,0:T(8,128)(2,1)S(1)} %pad_maximum_fusion.5), channel_id=1, source_target_pairs={{0,4},{1,5},{2,6},{3,7},{4,0},{5,1},{6,2},{7,3},{8,12},{9,13},{10,... | collective-permute-start | bytes 983048 | tf_op jit(solution)/shard_map/ppermute | solution.py:444
  108.8 4.5 %collective-permute-done.21 = bf16[8,16,1280]{2,1,0:T(8,128)(2,1)S(1)} collective-permute-done((bf16[8,16,1280]{2,1,0:T(8,128)(2,1)S(1)}, bf16[8,16,1280]{2,1,0:T(8,128)(2,1)S(1)}, u32[]{:S(2)}, u32[]{:S(2)}) %collective-permute-start.21) | collective-permute-done | bytes 327712 | tf_op jit(solution)/shard_map/ppermute | solution.py:444
  113.4 0.9 collective-permute-done.24
  114.5 1.0 collective-permute-done.22.refs_1_
  115.5 1.1 collective-permute-done.25.refs_3_
  116.6 2.6 %shard_map.150 = (f32[512,2048]{1,0:T(8,128)}, f32[512,512]{1,0:T(8,128)}) custom-call(s32[1]{0:T(128)} %bitcast.me_ref, bf16[16,16,1280]{2,1,0:T(8,128)(2,1)S(1)} %pad_maximum_fusion.refs_0_, bf16[16,16,1280]{2,1,0:T(8,128)(2,1)S(1)} %collective-permute-done.22.refs_1_, bf16[16,16,1280]{2,1,0:T(8,128)(2,1)S(1)} %pad_maximum_fusion.1.refs_2_, ...), custom_call_target="tpu_custom_call" | custom-call | tf_op jit(solution)/shard_map/pallas_call | solution.py:546
  (58 shorter events, 3.9 us)
Async XLA Ops:
  1.5 4.5 %collective-permute-start = (s32[8,8]{1,0:T(8,128)S(1)}, s32[8,8]{1,0:T(8,128)S(1)}, u32[]{:S(2)}, u32[]{:S(2)}) collective-permute-start(s32[8,8]{1,0:T(8,128)S(1)} %broadcast_select_fusion), channel_id=1, source_target_pairs={{0,4},{1,5},{2,6},{3,7},{4,0},{5,1},{6,2},{7,3},{8,12},{9,13},{10,... | collective-permute-start | bytes 776 | tf_op jit(solution)/shard_map/ppermute | solution.py:444
  6.1 3.7 %collective-permute-start.1 = (s32[8,8]{1,0:T(8,128)S(1)}, s32[8,8]{1,0:T(8,128)S(1)}, u32[]{:S(2)}, u32[]{:S(2)}) collective-permute-start(s32[8,8]{1,0:T(8,128)S(1)} %fusion), channel_id=1, source_target_pairs={{0,8},{1,9},{2,10},{3,11},{4,12},{5,13},{6,14},{7,15},{8,0},{9,1},... | collective-permute-start | bytes 776 | tf_op jit(solution)/shard_map/ppermute | solution.py:444
  9.8 4.6 %collective-permute-start.2 = (s32[8,8]{1,0:T(8,128)S(1)}, s32[8,8]{1,0:T(8,128)S(1)}, u32[]{:S(2)}, u32[]{:S(2)}) collective-permute-start(s32[8,8]{1,0:T(8,128)S(1)} %fusion.2), channel_id=1, source_target_pairs={{0,16},{1,17},{2,18},{3,19},{4,20},{5,21},{6,22},{7,23},{8,24},{9,... | collective-permute-start | bytes 776 | tf_op jit(solution)/shard_map/ppermute | solution.py:444
  14.5 1.0 copy-start
  16.1 8.5 %collective-permute-start.3 = (bf16[64,512]{1,0:T(8,128)(2,1)S(1)}, bf16[64,512]{1,0:T(8,128)(2,1)S(1)}, u32[]{:S(2)}, u32[]{:S(2)}) collective-permute-start(bf16[64,512]{1,0:T(8,128)(2,1)S(1)} %get-tuple-element.62), channel_id=1, source_target_pairs={{0,4},{1,5},{2,6},{3,7},{4,0},{5,1},{6,2},{7,3},{8,12},{9,13},{10,... | collective-permute-start | bytes 196616 | tf_op jit(solution)/shard_map/ppermute | solution.py:444
  18.0 10.2 %collective-permute-start.4 = (bf16[64,512]{1,0:T(8,128)(2,1)S(1)}, bf16[64,512]{1,0:T(8,128)(2,1)S(1)}, u32[]{:S(2)}, u32[]{:S(2)}) collective-permute-start(bf16[64,512]{1,0:T(8,128)(2,1)S(1)} %get-tuple-element.63), channel_id=1, source_target_pairs={{0,8},{1,9},{2,10},{3,11},{4,12},{5,13},{6,14},{7,15},{8,0},{9,1},... | collective-permute-start | bytes 196616 | tf_op jit(solution)/shard_map/ppermute | solution.py:444
  20.3 16.0 %collective-permute-start.5 = (bf16[64,512]{1,0:T(8,128)(2,1)S(1)}, bf16[64,512]{1,0:T(8,128)(2,1)S(1)}, u32[]{:S(2)}, u32[]{:S(2)}) collective-permute-start(bf16[64,512]{1,0:T(8,128)(2,1)S(1)} %get-tuple-element.64), channel_id=1, source_target_pairs={{0,12},{1,13},{2,14},{3,15},{4,8},{5,9},{6,10},{7,11},{8,4},{9,5},... | collective-permute-start | bytes 196616 | tf_op jit(solution)/shard_map/ppermute | solution.py:444
  20.4 15.9 %collective-permute-start.6 = (bf16[64,512]{1,0:T(8,128)(2,1)S(1)}, bf16[64,512]{1,0:T(8,128)(2,1)S(1)}, u32[]{:S(2)}, u32[]{:S(2)}) collective-permute-start(bf16[64,512]{1,0:T(8,128)(2,1)S(1)} %get-tuple-element.65), channel_id=1, source_target_pairs={{0,16},{1,17},{2,18},{3,19},{4,20},{5,21},{6,22},{7,23},{8,24},{9,... | collective-permute-start | bytes 196616 | tf_op jit(solution)/shard_map/ppermute | solution.py:444
  23.3 13.0 %collective-permute-start.7 = (bf16[64,512]{1,0:T(8,128)(2,1)S(1)}, bf16[64,512]{1,0:T(8,128)(2,1)S(1)}, u32[]{:S(2)}, u32[]{:S(2)}) collective-permute-start(bf16[64,512]{1,0:T(8,128)(2,1)S(1)} %get-tuple-element.66), channel_id=1, source_target_pairs={{0,20},{1,21},{2,22},{3,23},{4,16},{5,17},{6,18},{7,19},{8,28},{9,... | collective-permute-start | bytes 196616 | tf_op jit(solution)/shard_map/ppermute | solution.py:444
  24.6 11.8 %collective-permute-start.8 = (bf16[64,512]{1,0:T(8,128)(2,1)S(1)}, bf16[64,512]{1,0:T(8,128)(2,1)S(1)}, u32[]{:S(2)}, u32[]{:S(2)}) collective-permute-start(bf16[64,512]{1,0:T(8,128)(2,1)S(1)} %get-tuple-element.67), channel_id=1, source_target_pairs={{0,24},{1,25},{2,26},{3,27},{4,28},{5,29},{6,30},{7,31},{8,16},{9,... | collective-permute-start | bytes 196616 | tf_op jit(solution)/shard_map/ppermute | solution.py:444
  28.2 8.2 %collective-permute-start.9 = (bf16[64,512]{1,0:T(8,128)(2,1)S(1)}, bf16[64,512]{1,0:T(8,128)(2,1)S(1)}, u32[]{:S(2)}, u32[]{:S(2)}) collective-permute-start(bf16[64,512]{1,0:T(8,128)(2,1)S(1)} %get-tuple-element.68), channel_id=1, source_target_pairs={{0,28},{1,29},{2,30},{3,31},{4,24},{5,25},{6,26},{7,27},{8,20},{9,... | collective-permute-start | bytes 196616 | tf_op jit(solution)/shard_map/ppermute | solution.py:444
  28.2 1.6 %copy-start.1 = (bf16[512,2048]{1,0:T(8,128)(2,1)S(1)}, bf16[512,2048]{1,0:T(8,128)(2,1)}, u32[]{:S(2)}) copy-start(bf16[512,2048]{1,0:T(8,128)(2,1)} %refs_11_.1) | copy-start | bytes 6291460
  29.8 0.9 copy-start.4
  30.8 5.6 %copy-start.2 = (bf16[512,2048]{1,0:T(8,128)(2,1)S(1)}, bf16[512,2048]{1,0:T(8,128)(2,1)}, u32[]{:S(2)}) copy-start(bf16[512,2048]{1,0:T(8,128)(2,1)} %refs_11_.1) | copy-start | bytes 6291460
  30.8 5.6 %copy-start.3 = (bf16[512,512]{1,0:T(8,128)(2,1)S(1)}, bf16[512,512]{1,0:T(8,128)(2,1)}, u32[]{:S(2)}) copy-start(bf16[512,512]{1,0:T(8,128)(2,1)} %refs_0_.1) | copy-start | bytes 1572868
  30.8 5.6 %copy-start.5 = (s32[8]{0:T(128)S(1)}, s32[8]{0:T(128)}, u32[]{:S(2)}) copy-start(s32[8]{0:T(128)} %dest_ref.1) | copy-start | bytes 100
  30.8 5.6 %copy-start.6 = (s32[8]{0:T(128)S(1)}, s32[8]{0:T(128)}, u32[]{:S(2)}) copy-start(s32[8]{0:T(128)} %blocks_ref.1) | copy-start | bytes 100
  45.2 5.5 %collective-permute-start.10 = (bf16[16,16,1280]{2,1,0:T(8,128)(2,1)S(1)}, bf16[16,16,1280]{2,1,0:T(8,128)(2,1)}, u32[]{:S(2)}, u32[]{:S(2)}) collective-permute-start(bf16[16,16,1280]{2,1,0:T(8,128)(2,1)S(1)} %get-tuple-element.70), channel_id=1, source_target_pairs={{0,1},{1,0},{2,3},{3,2},{4,5},{5,4},{6,7},{7,6},{8,9},{9,8},{10,11... | collective-permute-start | bytes 1966088 | tf_op jit(solution)/shard_map/ppermute | solution.py:444
  45.2 8.4 %collective-permute-start.13 = (bf16[16,16,1280]{2,1,0:T(8,128)(2,1)S(1)}, bf16[16,16,1280]{2,1,0:T(8,128)(2,1)}, u32[]{:S(2)}, u32[]{:S(2)}) collective-permute-start(bf16[16,16,1280]{2,1,0:T(8,128)(2,1)S(1)} %get-tuple-element.72), channel_id=1, source_target_pairs={{0,1},{1,0},{2,3},{3,2},{4,5},{5,4},{6,7},{7,6},{8,9},{9,8},{10,11... | collective-permute-start | bytes 1966088 | tf_op jit(solution)/shard_map/ppermute | solution.py:444
  45.8 24.8 %all-to-all-start = ((bf16[4,8,16,640]{3,2,1,0:T(8,128)(2,1)}), bf16[4,8,16,640]{3,2,1,0:T(8,128)(2,1)S(1)}, u32[]{:S(2)}, u32[]{:S(2)}) async-start(bf16[4,8,16,640]{3,2,1,0:T(8,128)(2,1)} %bitcast.5), calls=%async_computation | async-start | bytes 1310720 | tf_op jit(solution)/shard_map/all_to_all | solution.py:447
  52.1 9.4 %collective-permute-start.11 = (bf16[8,16,1280]{2,1,0:T(8,128)(2,1)S(1)}, bf16[8,16,1280]{2,1,0:T(8,128)(2,1)S(1)}, u32[]{:S(2)}, u32[]{:S(2)}) collective-permute-start(bf16[8,16,1280]{2,1,0:T(8,128)(2,1)S(1)} %slice.57), channel_id=1, source_target_pairs={{0,2},{1,3},{2,0},{3,1},{4,6},{5,7},{6,4},{7,5},{8,10},{9,11},{10,... | collective-permute-start | bytes 983048 | tf_op jit(solution)/shard_map/ppermute | solution.py:444
  54.9 10.0 %collective-permute-start.14 = (bf16[8,16,1280]{2,1,0:T(8,128)(2,1)S(1)}, bf16[8,16,1280]{2,1,0:T(8,128)(2,1)S(1)}, u32[]{:S(2)}, u32[]{:S(2)}) collective-permute-start(bf16[8,16,1280]{2,1,0:T(8,128)(2,1)S(1)} %slice.61), channel_id=1, source_target_pairs={{0,4},{1,5},{2,6},{3,7},{4,0},{5,1},{6,2},{7,3},{8,12},{9,13},{10,... | collective-permute-start | bytes 983048 | tf_op jit(solution)/shard_map/ppermute | solution.py:444
  61.6 6.0 %collective-permute-start.12 = (bf16[4,16,1280]{2,1,0:T(8,128)(2,1)S(1)}, bf16[4,16,1280]{2,1,0:T(8,128)(2,1)S(1)}, u32[]{:S(2)}, u32[]{:S(2)}) collective-permute-start(bf16[4,16,1280]{2,1,0:T(8,128)(2,1)S(1)} %slice.59), channel_id=1, source_target_pairs={{0,4},{1,5},{2,6},{3,7},{4,0},{5,1},{6,2},{7,3},{8,12},{9,13},{10,... | collective-permute-start | bytes 491528 | tf_op jit(solution)/shard_map/ppermute | solution.py:444
  65.1 5.4 %collective-permute-start.15 = (bf16[4,16,1280]{2,1,0:T(8,128)(2,1)S(1)}, bf16[4,16,1280]{2,1,0:T(8,128)(2,1)S(1)}, u32[]{:S(2)}, u32[]{:S(2)}) collective-permute-start(bf16[4,16,1280]{2,1,0:T(8,128)(2,1)S(1)} %slice.63), channel_id=1, source_target_pairs={{0,2},{1,3},{2,0},{3,1},{4,6},{5,7},{6,4},{7,5},{8,10},{9,11},{10,... | collective-permute-start | bytes 491528 | tf_op jit(solution)/shard_map/ppermute | solution.py:444
  70.6 6.3 %collective-permute-start.16 = (bf16[2,16,2560]{2,1,0:T(8,128)(2,1)S(1)}, bf16[2,16,2560]{2,1,0:T(8,128)(2,1)S(1)}, u32[]{:S(2)}, u32[]{:S(2)}) collective-permute-start(bf16[2,16,2560]{2,1,0:T(8,128)(2,1)S(1)} %slice.51), channel_id=1, source_target_pairs={{0,8},{1,9},{2,10},{3,11},{4,12},{5,13},{6,14},{7,15},{8,0},{9,1},... | collective-permute-start | bytes 491528 | tf_op jit(solution)/shard_map/ppermute | solution.py:444
  76.9 6.9 %collective-permute-start.17 = (bf16[1,16,2560]{2,1,0:T(8,128)(2,1)S(1)}, bf16[1,16,2560]{2,1,0:T(8,128)(2,1)S(1)}, u32[]{:S(2)}, u32[]{:S(2)}) collective-permute-start(bf16[1,16,2560]{2,1,0:T(8,128)(2,1)S(1)} %slice.65), channel_id=1, source_target_pairs={{0,16},{1,17},{2,18},{3,19},{4,20},{5,21},{6,22},{7,23},{8,24},{9,... | collective-permute-start | bytes 245768 | tf_op jit(solution)/shard_map/ppermute | solution.py:444
  80.3 13.7 %all-to-all-start.1 = ((bf16[8,4,16,640]{3,2,1,0:T(8,128)(2,1)}), bf16[8,4,16,640]{3,2,1,0:T(8,128)(2,1)S(1)}, u32[]{:S(2)}, u32[]{:S(2)}) async-start(bf16[8,4,16,640]{3,2,1,0:T(8,128)(2,1)} %copy.18), calls=%async_computation.1 | async-start | bytes 1310720 | tf_op jit(solution)/shard_map/all_to_all | solution.py:447
  83.9 7.5 %collective-permute-start.18 = (bf16[1,16,2560]{2,1,0:T(8,128)(2,1)S(1)}, bf16[1,16,2560]{2,1,0:T(8,128)(2,1)S(1)}, u32[]{:S(2)}, u32[]{:S(2)}) collective-permute-start(bf16[1,16,2560]{2,1,0:T(8,128)(2,1)S(1)} %add_convert_fusion.7), channel_id=1, source_target_pairs={{0,16},{1,17},{2,18},{3,19},{4,20},{5,21},{6,22},{7,23},{8,24},{9,... | collective-permute-start | bytes 245768 | tf_op jit(solution)/shard_map/ppermute | solution.py:444
  94.0 6.0 %collective-permute-start.19 = (bf16[2,16,2560]{2,1,0:T(8,128)(2,1)S(1)}, bf16[2,16,2560]{2,1,0:T(8,128)(2,1)S(1)}, u32[]{:S(2)}, u32[]{:S(2)}) collective-permute-start(bf16[2,16,2560]{2,1,0:T(8,128)(2,1)S(1)} %pad_maximum_fusion.6), channel_id=1, source_target_pairs={{0,8},{1,9},{2,10},{3,11},{4,12},{5,13},{6,14},{7,15},{8,0},{9,1},... | collective-permute-start | bytes 491528 | tf_op jit(solution)/shard_map/ppermute | solution.py:444
  100.1 5.4 %collective-permute-start.20 = (bf16[4,16,1280]{2,1,0:T(8,128)(2,1)S(1)}, bf16[4,16,1280]{2,1,0:T(8,128)(2,1)S(1)}, u32[]{:S(2)}, u32[]{:S(2)}) collective-permute-start(bf16[4,16,1280]{2,1,0:T(8,128)(2,1)S(1)} %get-tuple-element.86), channel_id=1, source_target_pairs={{0,4},{1,5},{2,6},{3,7},{4,0},{5,1},{6,2},{7,3},{8,12},{9,13},{10,... | collective-permute-start | bytes 491528 | tf_op jit(solution)/shard_map/ppermute | solution.py:444
  100.9 6.1 %collective-permute-start.23 = (bf16[4,16,1280]{2,1,0:T(8,128)(2,1)S(1)}, bf16[4,16,1280]{2,1,0:T(8,128)(2,1)S(1)}, u32[]{:S(2)}, u32[]{:S(2)}) collective-permute-start(bf16[4,16,1280]{2,1,0:T(8,128)(2,1)S(1)} %get-tuple-element.85), channel_id=1, source_target_pairs={{0,2},{1,3},{2,0},{3,1},{4,6},{5,7},{6,4},{7,5},{8,10},{9,11},{10,... | collective-permute-start | bytes 491528 | tf_op jit(solution)/shard_map/ppermute | solution.py:444
  105.5 7.8 %collective-permute-start.21 = (bf16[8,16,1280]{2,1,0:T(8,128)(2,1)S(1)}, bf16[8,16,1280]{2,1,0:T(8,128)(2,1)S(1)}, u32[]{:S(2)}, u32[]{:S(2)}) collective-permute-start(bf16[8,16,1280]{2,1,0:T(8,128)(2,1)S(1)} %pad_maximum_fusion.4), channel_id=1, source_target_pairs={{0,2},{1,3},{2,0},{3,1},{4,6},{5,7},{6,4},{7,5},{8,10},{9,11},{10,... | collective-permute-start | bytes 983048 | tf_op jit(solution)/shard_map/ppermute | solution.py:444
  107.1 7.3 %collective-permute-start.24 = (bf16[8,16,1280]{2,1,0:T(8,128)(2,1)S(1)}, bf16[8,16,1280]{2,1,0:T(8,128)(2,1)S(1)}, u32[]{:S(2)}, u32[]{:S(2)}) collective-permute-start(bf16[8,16,1280]{2,1,0:T(8,128)(2,1)S(1)} %pad_maximum_fusion.5), channel_id=1, source_target_pairs={{0,4},{1,5},{2,6},{3,7},{4,0},{5,1},{6,2},{7,3},{8,12},{9,13},{10,... | collective-permute-start | bytes 983048 | tf_op jit(solution)/shard_map/ppermute | solution.py:444
  113.3 2.2 %collective-permute-start.22 = (bf16[16,16,1280]{2,1,0:T(8,128)(2,1)S(1)}, bf16[16,16,1280]{2,1,0:T(8,128)(2,1)S(1)}, u32[]{:S(2)}, u32[]{:S(2)}) collective-permute-start(bf16[16,16,1280]{2,1,0:T(8,128)(2,1)S(1)} %pad_maximum_fusion.refs_0_), channel_id=1, source_target_pairs={{0,1},{1,0},{2,3},{3,2},{4,5},{5,4},{6,7},{7,6},{8,9},{9,8},{10,11... | collective-permute-start | bytes 1966088 | tf_op jit(solution)/shard_map/ppermute | solution.py:444
  114.4 2.2 %collective-permute-start.25 = (bf16[16,16,1280]{2,1,0:T(8,128)(2,1)S(1)}, bf16[16,16,1280]{2,1,0:T(8,128)(2,1)S(1)}, u32[]{:S(2)}, u32[]{:S(2)}) collective-permute-start(bf16[16,16,1280]{2,1,0:T(8,128)(2,1)S(1)} %pad_maximum_fusion.1.refs_2_), channel_id=1, source_target_pairs={{0,1},{1,0},{2,3},{3,2},{4,5},{5,4},{6,7},{7,6},{8,9},{9,8},{10,11... | collective-permute-start | bytes 1966088 | tf_op jit(solution)/shard_map/ppermute | solution.py:444

commit v14 on v13

--- a/solution.py
+++ b/solution.py
@@ -54,10 +54,10 @@
 TN = ((0,), (0,))
 
 
-def send_body(table_size, me_ref, lengths_ref, grad_ref, *refs):
+def send_body(table_size, count, me_ref, lengths_ref, rows_ref, *refs):
     out_refs, begin_ref = refs[:-1], refs[-1]
     peers = len(out_refs)
-    blocks = grad_ref.shape[0] // BLK
+    blocks = (rows_ref.shape[0] - count) // BLK
     me = me_ref[0] // table_size
     begin = jnp.int32(0)
     for peer in range(peers):
@@ -67,7 +67,7 @@
         begin = begin_ref[me ^ apart]
         for inner in range(LMAXB):
             block = jnp.minimum(begin + inner, blocks - 1)
-            rows = grad_ref[pl.ds(pl.multiple_of(block * BLK, BLK), BLK), :]
+            rows = rows_ref[pl.ds(pl.multiple_of(count + block * BLK, BLK), BLK), :]
             out_ref[inner * BLK : (inner + 1) * BLK, :] = rows
 
 
@@ -77,25 +77,19 @@
     return (sub // SLOT == lane // SLOT) & (lane <= sub)
 
 
-SAVED = (
-    "gate",
-    "hat",
-    "hat_scale",
-    "qkv",
-    "slope",
-    "slope_t",
-    "weight_t",
-    "mixed_t",
-    "normed_t",
-    "rows_slope",
-    "rows_hat",
-    "rows_scale",
-    "place",
-    "digits",
-)
-
-
-def saved_shapes(tokens, count, width):
+def row_shapes(count, width):
+    return dict(
+        rows_active=shape_of((count, 5 * width), BF16),
+        normed_t=shape_of((width, count), BF16),
+        rows_slope=shape_of((count, 4 * width), BF16),
+        rows_hat=shape_of((count, width), F32),
+        rows_scale=shape_of((count, 1), F32),
+        place=shape_of((1, count), jnp.int32),
+        digits=shape_of((count, LANES), BF16),
+    )
+
+
+def token_shapes(tokens, width):
     pairs = tokens // TILE * HEADS
     return dict(
         gate=shape_of((tokens, width), F32),
@@ -106,78 +100,91 @@
         slope_t=shape_of((pairs, TILE, TILE), BF16),
         weight_t=shape_of((pairs, TILE, TILE), BF16),
         mixed_t=shape_of((width, tokens), BF16),
-        normed_t=shape_of((width, count), BF16),
-        rows_slope=shape_of((count, 4 * width), BF16),
-        rows_hat=shape_of((count, width), F32),
-        rows_scale=shape_of((count, 1), F32),
-        place=shape_of((1, count), jnp.int32),
-        digits=shape_of((count, LANES), BF16),
-    )
-
-
-def forward_body(
+    )
+
+
+def column_of(row):
+    wide = jnp.broadcast_to(row.astype(F32), (8, row.shape[1])).T
+    return wide[:, 0:1].astype(jnp.int32)
+
+
+def rows_body(
     capacity,
     rows_ref,
-    w_in_ref,
+    weights_ref,
     gains_ref,
     ints_ref,
-    *refs,
+    rows_active_ref,
+    normed_t_ref,
+    rows_slope_ref,
+    rows_hat_ref,
+    rows_scale_ref,
+    place_ref,
+    digits_ref,
 ):
-    held = dict(zip(SAVED, refs))
-    gate_ref, hat_ref, hat_scale_ref, qkv_ref, slope_ref, slope_t_ref = (
-        held[name] for name in SAVED[:6]
-    )
-    weight_t_ref, mixed_t_ref, normed_t_ref, rows_slope_ref = (held[name] for name in SAVED[6:10])
-    rows_hat_ref, rows_scale_ref, place_ref, digits_ref = (held[name] for name in SAVED[10:])
-    count, width = rows_ref.shape
+    count, width = rows_hat_ref.shape
     tokens = ints_ref.shape[1] - 2 * count
-    gain_in, gain_out = gains_ref[0:1, :], gains_ref[1:2, :]
-    columns = jnp.broadcast_to(ints_ref[...].astype(F32), (8, ints_ref.shape[1])).T
-    columns = columns[:, 0:1].astype(jnp.int32)
-    items, owners, numbers = (
-        columns[:tokens],
-        columns[tokens : tokens + count],
-        columns[tokens + count :],
-    )
     owner_row = ints_ref[:, tokens : tokens + count]
     across = jnp.broadcast_to(owner_row, (count, count))
-    down = jnp.broadcast_to(owners, (count, count))
+    down = jnp.broadcast_to(column_of(owner_row), (count, count))
     sub = lax.broadcasted_iota(jnp.int32, (count, count), 0)
     lane = lax.broadcasted_iota(jnp.int32, (count, count), 1)
     earlier = jnp.where((across == down) & (sub < lane), 1.0, 0.0)
     rank = jnp.sum(earlier, axis=0, keepdims=True).astype(jnp.int32)
     place_ref[...] = owner_row * capacity + rank
-    number = jnp.broadcast_to(numbers, (count, LANES))
+    number = jnp.broadcast_to(column_of(ints_ref[:, tokens + count :]), (count, LANES))
     lane = lax.broadcasted_iota(jnp.int32, (count, LANES), 1)
     digits = jnp.where(lane == 0, number >> 5, jnp.where(lane == 1, number & 31, 0))
     digits_ref[...] = digits.astype(F32).astype(BF16)
-    values = rows_ref[...].astype(F32)
+    values = rows_ref[:count, :].astype(F32)
     shifted = values - jnp.mean(values, axis=-1, keepdims=True)
     scale = lax.rsqrt(jnp.mean(shifted * shifted, axis=-1, keepdims=True) + EPSILON)
     hat = shifted * scale
     rows_hat_ref[...] = hat
     rows_scale_ref[...] = scale
-    normed = hat * gain_in
+    normed = hat * gains_ref[0:1, :]
     normed_t_ref[...] = normed.T.astype(BF16)
     normed = normed.astype(BF16)
-    lane = lax.broadcasted_iota(jnp.int32, (tokens, count), 1)
-    pick = jnp.where(lane == jnp.broadcast_to(items, (tokens, count)), 1.0, 0.0)
-    pick = pick.astype(BF16)
     for part in range(4):
         columns = slice(part * width, (part + 1) * width)
-        hidden = dot(normed, w_in_ref[:, columns])
+        hidden = dot(normed, weights_ref[:, columns])
         sigma = sigmoid(hidden)
         active = hidden * sigma
         slope = sigma * (1.0 + hidden * (1.0 - sigma))
         rows_slope_ref[:, columns] = slope.astype(BF16)
+        high = active.astype(BF16)
+        rows_active_ref[:, columns] = high
         if part == 0:
-            high = active.astype(BF16)
-            low = (active - high.astype(F32)).astype(BF16)
-            gate_ref[...] = dot(pick, high) + dot(pick, low)
-        else:
-            qkv_ref[:, (part - 1) * width : part * width] = dot(pick, active.astype(BF16)).astype(
-                BF16
-            )
+            rows_active_ref[:, 4 * width :] = (active - high.astype(F32)).astype(BF16)
+
+
+def forward_body(
+    rows_active_ref,
+    gains_ref,
+    ints_ref,
+    gate_ref,
+    hat_ref,
+    hat_scale_ref,
+    qkv_ref,
+    slope_ref,
+    slope_t_ref,
+    weight_t_ref,
+    mixed_t_ref,
+):
+    count = rows_active_ref.shape[0]
+    tokens, width = gate_ref.shape
+    items = column_of(ints_ref[:, :tokens])
+    lane = lax.broadcasted_iota(jnp.int32, (tokens, count), 1)
+    pick = jnp.where(lane == jnp.broadcast_to(items, (tokens, count)), 1.0, 0.0).astype(BF16)
+    gate_ref[...] = dot(pick, rows_active_ref[:, :width]) + dot(
+        pick, rows_active_ref[:, 4 * width :]
+    )
+    for part in range(3):
+        columns = slice((part + 1) * width, (part + 2) * width)
+        qkv_ref[:, part * width : (part + 1) * width] = dot(pick, rows_active_ref[:, columns]).astype(
+            BF16
+        )
+    gain_out = gains_ref[1:2, :]
     mask = tile_mask()
     factor = HDIM ** (-0.5)
     for tile in range(tokens // TILE):
@@ -215,7 +222,7 @@
 
 
 USED = (
-    "w_out",
+    "weights",
     "hat",
     "gate",
     "hat_scale",
@@ -226,7 +233,6 @@
     "mixed_t",
     "normed_t",
     "rows_slope",
-    "w_in",
     "rows_hat",
     "rows_scale",
     "place",
@@ -251,13 +257,11 @@
         refs[-9:-4],
         refs[-4:],
     )
-    w_out_ref, hat_ref, gate_ref, hat_scale_ref, qkv_ref, slope_ref, slope_t_ref = (
+    weights_ref, hat_ref, gate_ref, hat_scale_ref, qkv_ref, slope_ref, slope_t_ref = (
         used[name] for name in USED[:7]
     )
-    weight_t_ref, mixed_t_ref, normed_t_ref, rows_slope_ref, w_in_ref = (
-        used[name] for name in USED[7:12]
-    )
-    rows_hat_ref, rows_scale_ref, place_ref, digits_ref = (used[name] for name in USED[12:])
+    weight_t_ref, mixed_t_ref, normed_t_ref, rows_slope_ref = (used[name] for name in USED[7:11])
+    rows_hat_ref, rows_scale_ref, place_ref, digits_ref = (used[name] for name in USED[11:])
     for apart, got_ref in enumerate(got_refs):
         wide_ref[apart] = got_ref[...]
     for slot in range(len(got_refs)):
@@ -271,7 +275,7 @@
     gain_total = jnp.zeros((1, width), F32)
     for tile in range(tokens // TILE):
         rows = slice(tile * TILE, (tile + 1) * TILE)
-        grad_mixed = dot(grad_y_ref[rows, :], w_out_ref[...], NT)
+        grad_mixed = dot(grad_y_ref[rows, :], weights_ref[:, 4 * width :], NT)
         hat = hat_ref[rows, :]
         active_ref[rows, :width] = (grad_mixed * hat * gain_out).astype(BF16)
         inner = grad_mixed * gate_ref[rows, :]
@@ -307,7 +311,7 @@
         sums_ref[:, (part + 1) * width : (part + 2) * width] = (
             dot(normed_t_ref[...], grad_hidden) * factor
         ).astype(BF16)
-        grad_normed = grad_normed + dot(grad_hidden, w_in_ref[:, columns], NT)
+        grad_normed = grad_normed + dot(grad_hidden, weights_ref[:, columns], NT)
     hat = rows_hat_ref[...]
     gains = (jnp.sum(grad_normed * hat, axis=0, keepdims=True) * factor, gain_total * factor)
     plan.write(me_ref[0], sums_ref, part_refs)
@@ -437,6 +441,8 @@
     devices_all = plan.chunks
     total_factor = 1.0 / math.sqrt(grad_out.shape[0] * devices_all)
     gain_rows = jnp.stack([gain_in, gain_out])
+    rows = jnp.concatenate([touched_rows, grad_out])
+    weights = jnp.concatenate([w_in, w_out], axis=1)
     ints = jnp.concatenate([row_of_token, row_owner[:, 0], owner_row])[None, :]
     me = lax.axis_index(both).astype(jnp.int32)[None]
 
@@ -454,31 +460,35 @@
     for bit in range(dp_size.bit_length() - 1):
         lengths = lengths + swap(lengths, table_size << bit)
     send = call(
-        functools.partial(send_body, table_size),
+        functools.partial(send_body, table_size, count),
         [shape_of((SLOT, width), BF16)] * dp_size,
         [SMEM] * 2 + [VMEM],
         scratch=[pltpu.SMEM((dp_size,), jnp.int32)],
-    )(me, lengths, grad_out)
+    )(me, lengths, rows)
     got = list(send)
     for apart in reversed(range(1, dp_size)):
         got[apart] = swap(send[apart], apart * table_size)
-    got[0], ints = lax.optimization_barrier((got[0], ints))
-
-    shapes = saved_shapes(tokens, count, width)
-    saved = call(
-        functools.partial(forward_body, plan.capacity),
-        [shapes[name] for name in SAVED],
+    shapes = row_shapes(count, width)
+    made = call(
+        functools.partial(rows_body, plan.capacity),
+        list(shapes.values()),
         [VMEM] * 4,
-        flops=4 * count * width * width * 20,
-        moved=10_000_000,
+        flops=8 * count * width * width,
+        moved=4_000_000,
+    )(rows, weights, gain_rows, ints)
+    saved = dict(zip(shapes, made), weights=weights)
+    got[0], after = lax.optimization_barrier((got[0], ints))
+    shapes = token_shapes(tokens, width)
+    made = call(
+        forward_body,
+        list(shapes.values()),
+        [VMEM] * 3,
+        flops=4 * count * width * width * 10,
+        moved=8_000_000,
         mebibytes=12 + tokens // 32,
-    )(
-        touched_rows,
-        w_in,
-        gain_rows,
-        ints,
-    )
-    saved = dict(zip(SAVED, saved), w_in=w_in, w_out=w_out)
+    )(saved["rows_active"], gain_rows, after)
+    saved |= dict(zip(shapes, made))
+
     outs = [shape_of((devices_all * plan.capacity, width + plan.extra), BF16)]
     for _, wide in plan.sides:
         outs += [shape_of((devices_all // 2, CHUNK_ROWS, wide), BF16)] * 2
@@ -512,11 +522,12 @@
     def gathered(kept, mask):
         return jnp.concatenate([kept, swap(kept, mask)])
 
+    sides = [add(parts[2 * side], swap(parts[2 * side + 1], 1)) for side in range(2)]
+    *sides, table_send = lax.optimization_barrier((*sides, table_send))
     low = min(2, dp_size)
     high, inside = dp_size // low, low * table_size
     groups = [[upper * low + lower for upper in range(high)] for lower in range(low)]
     table_got = exchange(table_send.reshape(high, inside, plan.capacity, -1), "dp", groups)
-    sides = [add(parts[2 * side], swap(parts[2 * side + 1], 1)) for side in range(2)]
     for step in range(plan.near_steps):
         sides = [reduced(sides[side], plan.orders[side][step]) for side in range(2)]
     kept = jnp.concatenate(sides, axis=2)

time: 120 us -> 117 us (0.975)
  waiting for transfers between devices: 42.1 us -> 47.9 us
  starting transfers between devices: 46.4 us -> 42.1 us
  other arithmetic: 5.46 us -> 1.88 us
    ppermute x26, waiting for transfers between devices: 39.4 us -> 44.1 us  [swap(): lax.ppermute(values, both, [(here, here ^ mask) for here in range(devices...]
    ppermute x26, starting transfers between devices: 37.8 us -> 34.9 us  [swap(): lax.ppermute(values, both, [(here, here ^ mask) for here in range(devices...]
    convert_element_type x8, other arithmetic: 2.78 us -> 0.61 us  [add(): return (left.astype(F32) + right.astype(F32)).astype(BF16)]
    all_to_all x2, starting transfers between devices: 8.57 us -> 7.21 us  [exchange(): lax.all_to_all(values, axes, split_axis=0, concat_axis=0, tiled=True, axi...]
    unnamed x14 -> x20, local copies, waits for them, and re-layouts: 3.5 us -> 2.83 us
    pallas_call x2 -> x3, Pallas kernels: 6.2 us -> 6.02 us  [the longest x1 3.92 us: on_device(): call(forward_body, list(shapes.values()), [VMEM] * 3, flops=4 * count * w...]
  transfers between devices with their start and end apart: 28 -> 28, of which waited for: 16 -> 21; matrix products, arithmetic and copies ran while one was open for 5% -> 4% of each run, Pallas kernels for 6% -> 6%
where the time goes in v14:
time: 117 us; the launch traced here: 116 us
  waiting for transfers between devices  47.9 us (41%)
  starting transfers between devices  42.1 us (36%)
  Pallas kernels  19.6 us (17%)
  local copies, waits for them, and re-layouts  3.91 us (3%)
  other arithmetic  1.88 us (2%)
    ppermute x26, waiting for transfers between devices, swap(): lax.ppermute(values, both, [(here, here ^ mask) for here in range(devices...  44.1 us
    ppermute x26, starting transfers between devices, swap(): lax.ppermute(values, both, [(here, here ^ mask) for here in range(devices...  34.9 us
    pallas_call x1, Pallas kernels, on_device(): call(functools.partial(backward_body, plan, table_size, total_factor), ou...  8.84 us
    all_to_all x2, starting transfers between devices, exchange(): lax.all_to_all(values, axes, split_axis=0, concat_axis=0, tiled=True, axi...  7.21 us
    pallas_call x1, Pallas kernels, on_device(): call(forward_body, list(shapes.values()), [VMEM] * 3, flops=4 * count * w...  3.92 us
    all_to_all x2, waiting for transfers between devices, exchange(): lax.all_to_all(values, axes, split_axis=0, concat_axis=0, tiled=True, axi...  3.77 us
    unnamed x20, local copies, waits for them, and re-layouts  2.83 us
    pallas_call x1, Pallas kernels, on_device(): call(functools.partial(widen_body, plan), (shape_of(w_in.shape, F32), sha...  2.6 us
  transfers between devices with their start and end apart: 28, of which 21 were waited for; matrix products, arithmetic and copies ran while one was open for 4% of the time, Pallas kernels for 6%

profile of v14, /device:TPU:0, one launch (start us, length us, event | category | flops | bytes accessed | tf_op | source)
XLA Modules:
  0.0 116.4 jit_solution(15713811524584394267)
XLA Ops:
  1.5 2.9 %collective-permute-start = (s32[8,8]{1,0:T(8,128)S(1)}, s32[8,8]{1,0:T(8,128)S(1)}, u32[]{:S(2)}, u32[]{:S(2)}) collective-permute-start(s32[8,8]{1,0:T(8,128)S(1)} %broadcast_select_fusion), channel_id=1, source_target_pairs={{0,4},{1,5},{2,6},{3,7},{4,0},{5,1},{6,2},{7,3},{8,12},{9,13},{10,... | collective-permute-start | bytes 776 | tf_op jit(solution)/shard_map/ppermute | solution.py:450
  4.4 1.0 constant_dynamic-update-slice_fusion.3
  5.4 1.8 %constant_dynamic-update-slice_fusion.1 = bf16[512,2560]{1,0:T(8,128)(2,1)S(1)} fusion(bf16[512,2048]{1,0:T(8,128)(2,1)} %param.18), kind=kLoop, calls=%fused_computation.16 | loop fusion | bytes 4194304
  7.5 1.6 %collective-permute-start.1 = (s32[8,8]{1,0:T(8,128)S(1)}, s32[8,8]{1,0:T(8,128)S(1)}, u32[]{:S(2)}, u32[]{:S(2)}) collective-permute-start(s32[8,8]{1,0:T(8,128)S(1)} %fusion), channel_id=1, source_target_pairs={{0,8},{1,9},{2,10},{3,11},{4,12},{5,13},{6,14},{7,15},{8,0},{9,1},... | collective-permute-start | bytes 776 | tf_op jit(solution)/shard_map/ppermute | solution.py:450
  9.1 2.0 %collective-permute-done.1 = s32[8,8]{1,0:T(8,128)S(1)} collective-permute-done((s32[8,8]{1,0:T(8,128)S(1)}, s32[8,8]{1,0:T(8,128)S(1)}, u32[]{:S(2)}, u32[]{:S(2)}) %collective-permute-start.1) | collective-permute-done | bytes 288 | tf_op jit(solution)/shard_map/ppermute | solution.py:450
  11.2 2.6 %collective-permute-start.2 = (s32[8,8]{1,0:T(8,128)S(1)}, s32[8,8]{1,0:T(8,128)S(1)}, u32[]{:S(2)}, u32[]{:S(2)}) collective-permute-start(s32[8,8]{1,0:T(8,128)S(1)} %fusion.2), channel_id=1, source_target_pairs={{0,16},{1,17},{2,18},{3,19},{4,20},{5,21},{6,22},{7,23},{8,24},{9,... | collective-permute-start | bytes 776 | tf_op jit(solution)/shard_map/ppermute | solution.py:450
  13.8 1.9 %collective-permute-done.2 = s32[8,8]{1,0:T(8,128)S(1)} collective-permute-done((s32[8,8]{1,0:T(8,128)S(1)}, s32[8,8]{1,0:T(8,128)S(1)}, u32[]{:S(2)}, u32[]{:S(2)}) %collective-permute-start.2) | collective-permute-done | bytes 288 | tf_op jit(solution)/shard_map/ppermute | solution.py:450
  17.1 1.6 %collective-permute-start.4 = (bf16[64,512]{1,0:T(8,128)(2,1)S(1)}, bf16[64,512]{1,0:T(8,128)(2,1)S(1)}, u32[]{:S(2)}, u32[]{:S(2)}) collective-permute-start(bf16[64,512]{1,0:T(8,128)(2,1)S(1)} %get-tuple-element.68), channel_id=1, source_target_pairs={{0,8},{1,9},{2,10},{3,11},{4,12},{5,13},{6,14},{7,15},{8,0},{9,1},... | collective-permute-start | bytes 196616 | tf_op jit(solution)/shard_map/ppermute | solution.py:450
  18.7 1.4 %shard_map.146 = (bf16[256,2560]{1,0:T(8,128)(2,1)S(1)}, bf16[512,256]{1,0:T(8,128)(2,1)S(1)}, bf16[256,2048]{1,0:T(8,128)(2,1)S(1)}, f32[256,512]{1,0:T(8,128)S...) custom-call(bf16[512,512]{1,0:T(8,128)(2,1)S(1)} %constant_dynamic-update-slice_fusion.2.rows_ref, ...), custom_call_target="tpu_custom_call" | custom-call | flops 536870912 | bytes 4000000 | tf_op jit(solution)/shard_map/pallas_call | solution.py:472
  20.1 1.4 %collective-permute-start.5 = (bf16[64,512]{1,0:T(8,128)(2,1)S(1)}, bf16[64,512]{1,0:T(8,128)(2,1)S(1)}, u32[]{:S(2)}, u32[]{:S(2)}) collective-permute-start(bf16[64,512]{1,0:T(8,128)(2,1)S(1)} %get-tuple-element.69), channel_id=1, source_target_pairs={{0,12},{1,13},{2,14},{3,15},{4,8},{5,9},{6,10},{7,11},{8,4},{9,5},... | collective-permute-start | bytes 196616 | tf_op jit(solution)/shard_map/ppermute | solution.py:450
  21.4 2.6 %collective-permute-start.6 = (bf16[64,512]{1,0:T(8,128)(2,1)S(1)}, bf16[64,512]{1,0:T(8,128)(2,1)S(1)}, u32[]{:S(2)}, u32[]{:S(2)}) collective-permute-start(bf16[64,512]{1,0:T(8,128)(2,1)S(1)} %get-tuple-element.70), channel_id=1, source_target_pairs={{0,16},{1,17},{2,18},{3,19},{4,20},{5,21},{6,22},{7,23},{8,24},{9,... | collective-permute-start | bytes 196616 | tf_op jit(solution)/shard_map/ppermute | solution.py:450
  24.4 3.6 %collective-permute-start.8 = (bf16[64,512]{1,0:T(8,128)(2,1)S(1)}, bf16[64,512]{1,0:T(8,128)(2,1)S(1)}, u32[]{:S(2)}, u32[]{:S(2)}) collective-permute-start(bf16[64,512]{1,0:T(8,128)(2,1)S(1)} %get-tuple-element.72), channel_id=1, source_target_pairs={{0,24},{1,25},{2,26},{3,27},{4,28},{5,29},{6,30},{7,31},{8,16},{9,... | collective-permute-start | bytes 196616 | tf_op jit(solution)/shard_map/ppermute | solution.py:450
  28.0 1.1 collective-permute-start.9
  29.1 3.9 %shard_map.148 = (f32[512,512]{1,0:T(8,128)S(1)}, f32[512,512]{1,0:T(8,128)S(1)}, f32[512,1]{1,0:T(8,128)S(1)}, bf16[512,1536]{1,0:T(8,128)(2,1)S(1)}, bf16[16,1...) custom-call(bf16[256,2560]{1,0:T(8,128)(2,1)S(1)} %get-tuple-element, ...), custom_call_target="tpu_custom_call" | custom-call | flops 2684354560 | bytes 8000000 | tf_op jit(solution)/shard_map/pallas_call | solution.py:482
  33.1 1.9 %collective-permute-done.9.refs_22_ = bf16[64,512]{1,0:T(8,128)(2,1)S(1)} collective-permute-done((bf16[64,512]{1,0:T(8,128)(2,1)S(1)}, bf16[64,512]{1,0:T(8,128)(2,1)S(1)}, u32[]{:S(2)}, u32[]{:S(2)}) %collective-permute-start.9) | collective-permute-done | bytes 65568 | tf_op jit(solution)/shard_map/ppermute | solution.py:450
  35.0 8.8 %shard_map.149 = (bf16[512,640]{1,0:T(8,128)(2,1)}, bf16[16,16,1280]{2,1,0:T(8,128)(2,1)S(1)}, bf16[16,16,1280]{2,1,0:T(8,128)(2,1)S(1)}, bf16[16,16,1280]{2,1,0:T(8,128)(2,1)S(1)}, bf16[16,16,1280]{2,1,0:T(8,128)(2,1)S(1)}) custom-call(s32[1]{0:T(128)} %bitcast.me_ref, s32[8]{0:T(128)S(1)} %copy-done, s32[8]{0:T(128)S(1)} %copy-done.1, ...), custom_call_target="tpu_custom_call" | custom-call | flops 10737418240 | bytes 12000000 | tf_op jit(solution)/shard_map/pallas_call | solution.py:495
  44.3 1.6 %collective-permute-done.10 = bf16[16,16,1280]{2,1,0:T(8,128)(2,1)S(1)} collective-permute-done((bf16[16,16,1280]{2,1,0:T(8,128)(2,1)S(1)}, bf16[16,16,1280]{2,1,0:T(8,128)(2,1)S(1)}, u32[]{:S(2)}, u32[]{:S(2)}) %collective-permute-start.10) | collective-permute-done | bytes 655392 | tf_op jit(solution)/shard_map/ppermute | solution.py:450
  46.1 0.8 collective-permute-done.11
  47.1 1.5 %collective-permute-start.14 = (bf16[8,16,1280]{2,1,0:T(8,128)(2,1)S(1)}, bf16[8,16,1280]{2,1,0:T(8,128)(2,1)S(1)}, u32[]{:S(2)}, u32[]{:S(2)}) collective-permute-start(bf16[8,16,1280]{2,1,0:T(8,128)(2,1)S(1)} %slice.47), channel_id=1, source_target_pairs={{0,4},{1,5},{2,6},{3,7},{4,0},{5,1},{6,2},{7,3},{8,12},{9,13},{10,... | collective-permute-start | bytes 983048 | tf_op jit(solution)/shard_map/ppermute | solution.py:450
  48.5 3.7 %all-to-all-start = ((bf16[4,8,16,640]{3,2,1,0:T(8,128)(2,1)}), bf16[4,8,16,640]{3,2,1,0:T(8,128)(2,1)S(1)}, u32[]{:S(2)}, u32[]{:S(2)}) async-start(bf16[4,8,16,640]{3,2,1,0:T(8,128)(2,1)} %bitcast.5), calls=%async_computation | async-start | bytes 1310720 | tf_op jit(solution)/shard_map/all_to_all | solution.py:453
  52.2 1.6 %collective-permute-start.12 = (bf16[8,16,1280]{2,1,0:T(8,128)(2,1)S(1)}, bf16[8,16,1280]{2,1,0:T(8,128)(2,1)S(1)}, u32[]{:S(2)}, u32[]{:S(2)}) collective-permute-start(bf16[8,16,1280]{2,1,0:T(8,128)(2,1)S(1)} %slice.43), channel_id=1, source_target_pairs={{0,2},{1,3},{2,0},{3,1},{4,6},{5,7},{6,4},{7,5},{8,10},{9,11},{10,... | collective-permute-start | bytes 983048 | tf_op jit(solution)/shard_map/ppermute | solution.py:450
  53.8 3.1 %collective-permute-done.14 = bf16[8,16,1280]{2,1,0:T(8,128)(2,1)S(1)} collective-permute-done((bf16[8,16,1280]{2,1,0:T(8,128)(2,1)S(1)}, bf16[8,16,1280]{2,1,0:T(8,128)(2,1)S(1)}, u32[]{:S(2)}, u32[]{:S(2)}) %collective-permute-start.14) | collective-permute-done | bytes 327712 | tf_op jit(solution)/shard_map/ppermute | solution.py:450
  57.0 1.6 %collective-permute-start.15 = (bf16[4,16,1280]{2,1,0:T(8,128)(2,1)S(1)}, bf16[4,16,1280]{2,1,0:T(8,128)(2,1)S(1)}, u32[]{:S(2)}, u32[]{:S(2)}) collective-permute-start(bf16[4,16,1280]{2,1,0:T(8,128)(2,1)S(1)} %slice.59), channel_id=1, source_target_pairs={{0,2},{1,3},{2,0},{3,1},{4,6},{5,7},{6,4},{7,5},{8,10},{9,11},{10,... | collective-permute-start | bytes 491528 | tf_op jit(solution)/shard_map/ppermute | solution.py:450
  58.6 4.3 %collective-permute-done.12 = bf16[8,16,1280]{2,1,0:T(8,128)(2,1)S(1)} collective-permute-done((bf16[8,16,1280]{2,1,0:T(8,128)(2,1)S(1)}, bf16[8,16,1280]{2,1,0:T(8,128)(2,1)S(1)}, u32[]{:S(2)}, u32[]{:S(2)}) %collective-permute-start.12) | collective-permute-done | bytes 327712 | tf_op jit(solution)/shard_map/ppermute | solution.py:450
  63.7 1.6 %collective-permute-done.15 = bf16[4,16,1280]{2,1,0:T(8,128)(2,1)S(1)} collective-permute-done((bf16[4,16,1280]{2,1,0:T(8,128)(2,1)S(1)}, bf16[4,16,1280]{2,1,0:T(8,128)(2,1)S(1)}, u32[]{:S(2)}, u32[]{:S(2)}) %collective-permute-start.15) | collective-permute-done | bytes 163872 | tf_op jit(solution)/shard_map/ppermute | solution.py:450
  65.3 3.1 %collective-permute-done.13 = bf16[4,16,1280]{2,1,0:T(8,128)(2,1)S(1)} collective-permute-done((bf16[4,16,1280]{2,1,0:T(8,128)(2,1)S(1)}, bf16[4,16,1280]{2,1,0:T(8,128)(2,1)S(1)}, u32[]{:S(2)}, u32[]{:S(2)}) %collective-permute-start.13) | collective-permute-done | bytes 163872 | tf_op jit(solution)/shard_map/ppermute | solution.py:450
  68.5 1.1 all-to-all-done
  69.6 0.8 collective-permute-start.16
  70.4 4.6 %collective-permute-done.16 = bf16[2,16,2560]{2,1,0:T(8,128)(2,1)S(1)} collective-permute-done((bf16[2,16,2560]{2,1,0:T(8,128)(2,1)S(1)}, bf16[2,16,2560]{2,1,0:T(8,128)(2,1)S(1)}, u32[]{:S(2)}, u32[]{:S(2)}) %collective-permute-start.16) | collective-permute-done | bytes 163872 | tf_op jit(solution)/shard_map/ppermute | solution.py:450
  75.0 1.7 %collective-permute-start.17 = (bf16[1,16,2560]{2,1,0:T(8,128)(2,1)S(1)}, bf16[1,16,2560]{2,1,0:T(8,128)(2,1)S(1)}, u32[]{:S(2)}, u32[]{:S(2)}) collective-permute-start(bf16[1,16,2560]{2,1,0:T(8,128)(2,1)S(1)} %slice.61), channel_id=1, source_target_pairs={{0,16},{1,17},{2,18},{3,19},{4,20},{5,21},{6,22},{7,23},{8,24},{9,... | collective-permute-start | bytes 245768 | tf_op jit(solution)/shard_map/ppermute | solution.py:450
  76.7 0.9 copy.18
  77.6 3.5 %all-to-all-start.1 = ((bf16[8,4,16,640]{3,2,1,0:T(8,128)(2,1)}), bf16[8,4,16,640]{3,2,1,0:T(8,128)(2,1)S(1)}, u32[]{:S(2)}, u32[]{:S(2)}) async-start(bf16[8,4,16,640]{3,2,1,0:T(8,128)(2,1)} %copy.18), calls=%async_computation.1 | async-start | bytes 1310720 | tf_op jit(solution)/shard_map/all_to_all | solution.py:453
  81.4 1.3 %collective-permute-start.18 = (bf16[1,16,2560]{2,1,0:T(8,128)(2,1)S(1)}, bf16[1,16,2560]{2,1,0:T(8,128)(2,1)S(1)}, u32[]{:S(2)}, u32[]{:S(2)}) collective-permute-start(bf16[1,16,2560]{2,1,0:T(8,128)(2,1)S(1)} %add_convert_fusion.7), channel_id=1, source_target_pairs={{0,16},{1,17},{2,18},{3,19},{4,20},{5,21},{6,22},{7,23},{8,24},{9,... | collective-permute-start | bytes 245768 | tf_op jit(solution)/shard_map/ppermute | solution.py:450
  82.6 6.1 %collective-permute-done.18 = bf16[1,16,2560]{2,1,0:T(8,128)(2,1)S(1)} collective-permute-done((bf16[1,16,2560]{2,1,0:T(8,128)(2,1)S(1)}, bf16[1,16,2560]{2,1,0:T(8,128)(2,1)S(1)}, u32[]{:S(2)}, u32[]{:S(2)}) %collective-permute-start.18) | collective-permute-done | bytes 81952 | tf_op jit(solution)/shard_map/ppermute | solution.py:450
  88.7 2.6 %all-to-all-done.1 = bf16[8,4,16,640]{3,2,1,0:T(8,128)(2,1)S(1)} async-done(((bf16[8,4,16,640]{3,2,1,0:T(8,128)(2,1)}), bf16[8,4,16,640]{3,2,1,0:T(8,128)(2,1)S(1)}, u32[]{:S(2)}, u32[]{:S(2)}) %all-to-all-start.1) | async-done | bytes 655392 | tf_op jit(solution)/shard_map/all_to_all | solution.py:453
  91.4 1.5 %collective-permute-start.19 = (bf16[2,16,2560]{2,1,0:T(8,128)(2,1)S(1)}, bf16[2,16,2560]{2,1,0:T(8,128)(2,1)S(1)}, u32[]{:S(2)}, u32[]{:S(2)}) collective-permute-start(bf16[2,16,2560]{2,1,0:T(8,128)(2,1)S(1)} %pad_maximum_fusion.6), channel_id=1, source_target_pairs={{0,8},{1,9},{2,10},{3,11},{4,12},{5,13},{6,14},{7,15},{8,0},{9,1},... | collective-permute-start | bytes 491528 | tf_op jit(solution)/shard_map/ppermute | solution.py:450
  92.8 2.2 %shard_map.150 = (f32[1024,512]{1,0:T(8,128)}, f32[1,512]{1,0:T(1,128)}, f32[1,512]{1,0:T(1,128)}) custom-call(bf16[512,640]{1,0:T(8,128)(2,1)S(1)} %bitcast.10), custom_call_target="tpu_custom_call" | custom-call | tf_op jit(solution)/shard_map/pallas_call | solution.py:542
  95.0 2.1 %collective-permute-done.19 = bf16[2,16,2560]{2,1,0:T(8,128)(2,1)S(1)} collective-permute-done((bf16[2,16,2560]{2,1,0:T(8,128)(2,1)S(1)}, bf16[2,16,2560]{2,1,0:T(8,128)(2,1)S(1)}, u32[]{:S(2)}, u32[]{:S(2)}) %collective-permute-start.19) | collective-permute-done | bytes 163872 | tf_op jit(solution)/shard_map/ppermute | solution.py:450
  97.2 1.1 collective-permute-start.20
  98.3 1.0 collective-permute-start.23
  99.3 3.3 %collective-permute-done.20 = bf16[4,16,1280]{2,1,0:T(8,128)(2,1)S(1)} collective-permute-done((bf16[4,16,1280]{2,1,0:T(8,128)(2,1)S(1)}, bf16[4,16,1280]{2,1,0:T(8,128)(2,1)S(1)}, u32[]{:S(2)}, u32[]{:S(2)}) %collective-permute-start.20) | collective-permute-done | bytes 163872 | tf_op jit(solution)/shard_map/ppermute | solution.py:450
  102.6 1.5 %collective-permute-start.21 = (bf16[8,16,1280]{2,1,0:T(8,128)(2,1)S(1)}, bf16[8,16,1280]{2,1,0:T(8,128)(2,1)S(1)}, u32[]{:S(2)}, u32[]{:S(2)}) collective-permute-start(bf16[8,16,1280]{2,1,0:T(8,128)(2,1)S(1)} %pad_maximum_fusion.4), channel_id=1, source_target_pairs={{0,2},{1,3},{2,0},{3,1},{4,6},{5,7},{6,4},{7,5},{8,10},{9,11},{10,... | collective-permute-start | bytes 983048 | tf_op jit(solution)/shard_map/ppermute | solution.py:450
  104.4 1.7 %collective-permute-start.24 = (bf16[8,16,1280]{2,1,0:T(8,128)(2,1)S(1)}, bf16[8,16,1280]{2,1,0:T(8,128)(2,1)S(1)}, u32[]{:S(2)}, u32[]{:S(2)}) collective-permute-start(bf16[8,16,1280]{2,1,0:T(8,128)(2,1)S(1)} %pad_maximum_fusion.5), channel_id=1, source_target_pairs={{0,4},{1,5},{2,6},{3,7},{4,0},{5,1},{6,2},{7,3},{8,12},{9,13},{10,... | collective-permute-start | bytes 983048 | tf_op jit(solution)/shard_map/ppermute | solution.py:450
  106.1 4.5 %collective-permute-done.21 = bf16[8,16,1280]{2,1,0:T(8,128)(2,1)S(1)} collective-permute-done((bf16[8,16,1280]{2,1,0:T(8,128)(2,1)S(1)}, bf16[8,16,1280]{2,1,0:T(8,128)(2,1)S(1)}, u32[]{:S(2)}, u32[]{:S(2)}) %collective-permute-start.21) | collective-permute-done | bytes 327712 | tf_op jit(solution)/shard_map/ppermute | solution.py:450
  110.8 0.8 collective-permute-done.24
  111.7 1.2 collective-permute-done.22.refs_1_
  112.9 0.9 collective-permute-done.25.refs_3_
  113.8 2.6 %shard_map.151 = (f32[512,2048]{1,0:T(8,128)}, f32[512,512]{1,0:T(8,128)}) custom-call(s32[1]{0:T(128)} %bitcast.me_ref, bf16[16,16,1280]{2,1,0:T(8,128)(2,1)S(1)} %pad_maximum_fusion.refs_0_, bf16[16,16,1280]{2,1,0:T(8,128)(2,1)S(1)} %collective-permute-done.22.refs_1_, bf16[16,16,1280]{2,1,0:T(8,128)(2,1)S(1)} %pad_maximum_fusion.1.refs_2_, ...), custom_call_target="tpu_custom_call" | custom-call | tf_op jit(solution)/shard_map/pallas_call | solution.py:557
  (67 shorter events, 5.6 us)
Async XLA Ops:
  1.5 5.9 %collective-permute-start = (s32[8,8]{1,0:T(8,128)S(1)}, s32[8,8]{1,0:T(8,128)S(1)}, u32[]{:S(2)}, u32[]{:S(2)}) collective-permute-start(s32[8,8]{1,0:T(8,128)S(1)} %broadcast_select_fusion), channel_id=1, source_target_pairs={{0,4},{1,5},{2,6},{3,7},{4,0},{5,1},{6,2},{7,3},{8,12},{9,13},{10,... | collective-permute-start | bytes 776 | tf_op jit(solution)/shard_map/ppermute | solution.py:450
  5.4 1.9 %copy-start.2 = (bf16[512,512]{1,0:T(8,128)(2,1)S(1)}, bf16[512,512]{1,0:T(8,128)(2,1)}, u32[]{:S(2)}) copy-start(bf16[512,512]{1,0:T(8,128)(2,1)} %param.19) | copy-start | bytes 1572868
  5.4 2.0 %copy-start.3 = (bf16[256,512]{1,0:T(8,128)(2,1)S(1)}, bf16[256,512]{1,0:T(8,128)(2,1)}, u32[]{:S(2)}) copy-start(bf16[256,512]{1,0:T(8,128)(2,1)} %param.17) | copy-start | bytes 786436
  5.4 3.6 %copy-start.4 = (f32[512]{0:T(512)S(1)}, f32[512]{0:T(512)}, u32[]{:S(2)}) copy-start(f32[512]{0:T(512)} %param.21) | copy-start | bytes 6148
  5.4 3.6 %copy-start.5 = (f32[512]{0:T(512)S(1)}, f32[512]{0:T(512)}, u32[]{:S(2)}) copy-start(f32[512]{0:T(512)} %param.20) | copy-start | bytes 6148
  7.3 11.4 %copy-start.6 = (s32[512]{0:T(512)S(1)}, s32[512]{0:T(512)}, u32[]{:S(2)}) copy-start(s32[512]{0:T(512)} %param.12) | copy-start | bytes 6148
  7.3 11.4 %copy-start.7 = (s32[256]{0:T(256)S(1)}, s32[256]{0:T(256)}, u32[]{:S(2)}) copy-start(s32[256]{0:T(256)} %param.14) | copy-start | bytes 3076
  7.3 11.3 %copy-start.8 = (s32[256,1]{0,1:T(1,128)S(1)}, s32[256,1]{0,1:T(1,128)}, u32[]{:S(2)}) copy-start(s32[256,1]{0,1:T(1,128)} %param.13) | copy-start | bytes 3076
  7.5 3.6 %collective-permute-start.1 = (s32[8,8]{1,0:T(8,128)S(1)}, s32[8,8]{1,0:T(8,128)S(1)}, u32[]{:S(2)}, u32[]{:S(2)}) collective-permute-start(s32[8,8]{1,0:T(8,128)S(1)} %fusion), channel_id=1, source_target_pairs={{0,8},{1,9},{2,10},{3,11},{4,12},{5,13},{6,14},{7,15},{8,0},{9,1},... | collective-permute-start | bytes 776 | tf_op jit(solution)/shard_map/ppermute | solution.py:450
  11.2 4.5 %collective-permute-start.2 = (s32[8,8]{1,0:T(8,128)S(1)}, s32[8,8]{1,0:T(8,128)S(1)}, u32[]{:S(2)}, u32[]{:S(2)}) collective-permute-start(s32[8,8]{1,0:T(8,128)S(1)} %fusion.2), channel_id=1, source_target_pairs={{0,16},{1,17},{2,18},{3,19},{4,20},{5,21},{6,22},{7,23},{8,24},{9,... | collective-permute-start | bytes 776 | tf_op jit(solution)/shard_map/ppermute | solution.py:450
  16.4 8.1 %collective-permute-start.3 = (bf16[64,512]{1,0:T(8,128)(2,1)S(1)}, bf16[64,512]{1,0:T(8,128)(2,1)S(1)}, u32[]{:S(2)}, u32[]{:S(2)}) collective-permute-start(bf16[64,512]{1,0:T(8,128)(2,1)S(1)} %get-tuple-element.67), channel_id=1, source_target_pairs={{0,4},{1,5},{2,6},{3,7},{4,0},{5,1},{6,2},{7,3},{8,12},{9,13},{10,... | collective-permute-start | bytes 196616 | tf_op jit(solution)/shard_map/ppermute | solution.py:450
  17.1 11.0 %collective-permute-start.4 = (bf16[64,512]{1,0:T(8,128)(2,1)S(1)}, bf16[64,512]{1,0:T(8,128)(2,1)S(1)}, u32[]{:S(2)}, u32[]{:S(2)}) collective-permute-start(bf16[64,512]{1,0:T(8,128)(2,1)S(1)} %get-tuple-element.68), channel_id=1, source_target_pairs={{0,8},{1,9},{2,10},{3,11},{4,12},{5,13},{6,14},{7,15},{8,0},{9,1},... | collective-permute-start | bytes 196616 | tf_op jit(solution)/shard_map/ppermute | solution.py:450
  20.1 12.9 %collective-permute-start.5 = (bf16[64,512]{1,0:T(8,128)(2,1)S(1)}, bf16[64,512]{1,0:T(8,128)(2,1)S(1)}, u32[]{:S(2)}, u32[]{:S(2)}) collective-permute-start(bf16[64,512]{1,0:T(8,128)(2,1)S(1)} %get-tuple-element.69), channel_id=1, source_target_pairs={{0,12},{1,13},{2,14},{3,15},{4,8},{5,9},{6,10},{7,11},{8,4},{9,5},... | collective-permute-start | bytes 196616 | tf_op jit(solution)/shard_map/ppermute | solution.py:450
  21.4 11.6 %collective-permute-start.6 = (bf16[64,512]{1,0:T(8,128)(2,1)S(1)}, bf16[64,512]{1,0:T(8,128)(2,1)S(1)}, u32[]{:S(2)}, u32[]{:S(2)}) collective-permute-start(bf16[64,512]{1,0:T(8,128)(2,1)S(1)} %get-tuple-element.70), channel_id=1, source_target_pairs={{0,16},{1,17},{2,18},{3,19},{4,20},{5,21},{6,22},{7,23},{8,24},{9,... | collective-permute-start | bytes 196616 | tf_op jit(solution)/shard_map/ppermute | solution.py:450
  24.0 9.0 %collective-permute-start.7 = (bf16[64,512]{1,0:T(8,128)(2,1)S(1)}, bf16[64,512]{1,0:T(8,128)(2,1)S(1)}, u32[]{:S(2)}, u32[]{:S(2)}) collective-permute-start(bf16[64,512]{1,0:T(8,128)(2,1)S(1)} %get-tuple-element.71), channel_id=1, source_target_pairs={{0,20},{1,21},{2,22},{3,23},{4,16},{5,17},{6,18},{7,19},{8,28},{9,... | collective-permute-start | bytes 196616 | tf_op jit(solution)/shard_map/ppermute | solution.py:450
  24.4 8.6 %collective-permute-start.8 = (bf16[64,512]{1,0:T(8,128)(2,1)S(1)}, bf16[64,512]{1,0:T(8,128)(2,1)S(1)}, u32[]{:S(2)}, u32[]{:S(2)}) collective-permute-start(bf16[64,512]{1,0:T(8,128)(2,1)S(1)} %get-tuple-element.72), channel_id=1, source_target_pairs={{0,24},{1,25},{2,26},{3,27},{4,28},{5,29},{6,30},{7,31},{8,16},{9,... | collective-permute-start | bytes 196616 | tf_op jit(solution)/shard_map/ppermute | solution.py:450
  28.0 7.0 %collective-permute-start.9 = (bf16[64,512]{1,0:T(8,128)(2,1)S(1)}, bf16[64,512]{1,0:T(8,128)(2,1)S(1)}, u32[]{:S(2)}, u32[]{:S(2)}) collective-permute-start(bf16[64,512]{1,0:T(8,128)(2,1)S(1)} %get-tuple-element.73), channel_id=1, source_target_pairs={{0,28},{1,29},{2,30},{3,31},{4,24},{5,25},{6,26},{7,27},{8,20},{9,... | collective-permute-start | bytes 196616 | tf_op jit(solution)/shard_map/ppermute | solution.py:450
  29.1 5.9 %copy-start = (s32[8]{0:T(128)S(1)}, s32[8]{0:T(128)}, u32[]{:S(2)}) copy-start(s32[8]{0:T(128)} %dest_ref.1) | copy-start | bytes 100
  29.1 5.9 %copy-start.1 = (s32[8]{0:T(128)S(1)}, s32[8]{0:T(128)}, u32[]{:S(2)}) copy-start(s32[8]{0:T(128)} %blocks_ref.1) | copy-start | bytes 100
  43.8 2.1 %collective-permute-start.10 = (bf16[16,16,1280]{2,1,0:T(8,128)(2,1)S(1)}, bf16[16,16,1280]{2,1,0:T(8,128)(2,1)S(1)}, u32[]{:S(2)}, u32[]{:S(2)}) collective-permute-start(bf16[16,16,1280]{2,1,0:T(8,128)(2,1)S(1)} %get-tuple-element.75), channel_id=1, source_target_pairs={{0,1},{1,0},{2,3},{3,2},{4,5},{5,4},{6,7},{7,6},{8,9},{9,8},{10,11... | collective-permute-start | bytes 1966088 | tf_op jit(solution)/shard_map/ppermute | solution.py:450
  43.8 3.0 %collective-permute-start.11 = (bf16[16,16,1280]{2,1,0:T(8,128)(2,1)S(1)}, bf16[16,16,1280]{2,1,0:T(8,128)(2,1)S(1)}, u32[]{:S(2)}, u32[]{:S(2)}) collective-permute-start(bf16[16,16,1280]{2,1,0:T(8,128)(2,1)S(1)} %get-tuple-element.77), channel_id=1, source_target_pairs={{0,1},{1,0},{2,3},{3,2},{4,5},{5,4},{6,7},{7,6},{8,9},{9,8},{10,11... | collective-permute-start | bytes 1966088 | tf_op jit(solution)/shard_map/ppermute | solution.py:450
  47.1 9.8 %collective-permute-start.14 = (bf16[8,16,1280]{2,1,0:T(8,128)(2,1)S(1)}, bf16[8,16,1280]{2,1,0:T(8,128)(2,1)S(1)}, u32[]{:S(2)}, u32[]{:S(2)}) collective-permute-start(bf16[8,16,1280]{2,1,0:T(8,128)(2,1)S(1)} %slice.47), channel_id=1, source_target_pairs={{0,4},{1,5},{2,6},{3,7},{4,0},{5,1},{6,2},{7,3},{8,12},{9,13},{10,... | collective-permute-start | bytes 983048 | tf_op jit(solution)/shard_map/ppermute | solution.py:450
  48.5 21.1 %all-to-all-start = ((bf16[4,8,16,640]{3,2,1,0:T(8,128)(2,1)}), bf16[4,8,16,640]{3,2,1,0:T(8,128)(2,1)S(1)}, u32[]{:S(2)}, u32[]{:S(2)}) async-start(bf16[4,8,16,640]{3,2,1,0:T(8,128)(2,1)} %bitcast.5), calls=%async_computation | async-start | bytes 1310720 | tf_op jit(solution)/shard_map/all_to_all | solution.py:453
  52.2 10.7 %collective-permute-start.12 = (bf16[8,16,1280]{2,1,0:T(8,128)(2,1)S(1)}, bf16[8,16,1280]{2,1,0:T(8,128)(2,1)S(1)}, u32[]{:S(2)}, u32[]{:S(2)}) collective-permute-start(bf16[8,16,1280]{2,1,0:T(8,128)(2,1)S(1)} %slice.43), channel_id=1, source_target_pairs={{0,2},{1,3},{2,0},{3,1},{4,6},{5,7},{6,4},{7,5},{8,10},{9,11},{10,... | collective-permute-start | bytes 983048 | tf_op jit(solution)/shard_map/ppermute | solution.py:450
  57.0 8.3 %collective-permute-start.15 = (bf16[4,16,1280]{2,1,0:T(8,128)(2,1)S(1)}, bf16[4,16,1280]{2,1,0:T(8,128)(2,1)S(1)}, u32[]{:S(2)}, u32[]{:S(2)}) collective-permute-start(bf16[4,16,1280]{2,1,0:T(8,128)(2,1)S(1)} %slice.59), channel_id=1, source_target_pairs={{0,2},{1,3},{2,0},{3,1},{4,6},{5,7},{6,4},{7,5},{8,10},{9,11},{10,... | collective-permute-start | bytes 491528 | tf_op jit(solution)/shard_map/ppermute | solution.py:450
  63.0 5.4 %collective-permute-start.13 = (bf16[4,16,1280]{2,1,0:T(8,128)(2,1)S(1)}, bf16[4,16,1280]{2,1,0:T(8,128)(2,1)S(1)}, u32[]{:S(2)}, u32[]{:S(2)}) collective-permute-start(bf16[4,16,1280]{2,1,0:T(8,128)(2,1)S(1)} %slice.57), channel_id=1, source_target_pairs={{0,4},{1,5},{2,6},{3,7},{4,0},{5,1},{6,2},{7,3},{8,12},{9,13},{10,... | collective-permute-start | bytes 491528 | tf_op jit(solution)/shard_map/ppermute | solution.py:450
  69.6 5.4 %collective-permute-start.16 = (bf16[2,16,2560]{2,1,0:T(8,128)(2,1)S(1)}, bf16[2,16,2560]{2,1,0:T(8,128)(2,1)S(1)}, u32[]{:S(2)}, u32[]{:S(2)}) collective-permute-start(bf16[2,16,2560]{2,1,0:T(8,128)(2,1)S(1)} %slice.51), channel_id=1, source_target_pairs={{0,8},{1,9},{2,10},{3,11},{4,12},{5,13},{6,14},{7,15},{8,0},{9,1},... | collective-permute-start | bytes 491528 | tf_op jit(solution)/shard_map/ppermute | solution.py:450
  75.0 6.3 %collective-permute-start.17 = (bf16[1,16,2560]{2,1,0:T(8,128)(2,1)S(1)}, bf16[1,16,2560]{2,1,0:T(8,128)(2,1)S(1)}, u32[]{:S(2)}, u32[]{:S(2)}) collective-permute-start(bf16[1,16,2560]{2,1,0:T(8,128)(2,1)S(1)} %slice.61), channel_id=1, source_target_pairs={{0,16},{1,17},{2,18},{3,19},{4,20},{5,21},{6,22},{7,23},{8,24},{9,... | collective-permute-start | bytes 245768 | tf_op jit(solution)/shard_map/ppermute | solution.py:450
  77.6 13.7 %all-to-all-start.1 = ((bf16[8,4,16,640]{3,2,1,0:T(8,128)(2,1)}), bf16[8,4,16,640]{3,2,1,0:T(8,128)(2,1)S(1)}, u32[]{:S(2)}, u32[]{:S(2)}) async-start(bf16[8,4,16,640]{3,2,1,0:T(8,128)(2,1)} %copy.18), calls=%async_computation.1 | async-start | bytes 1310720 | tf_op jit(solution)/shard_map/all_to_all | solution.py:453
  81.4 7.3 %collective-permute-start.18 = (bf16[1,16,2560]{2,1,0:T(8,128)(2,1)S(1)}, bf16[1,16,2560]{2,1,0:T(8,128)(2,1)S(1)}, u32[]{:S(2)}, u32[]{:S(2)}) collective-permute-start(bf16[1,16,2560]{2,1,0:T(8,128)(2,1)S(1)} %add_convert_fusion.7), channel_id=1, source_target_pairs={{0,16},{1,17},{2,18},{3,19},{4,20},{5,21},{6,22},{7,23},{8,24},{9,... | collective-permute-start | bytes 245768 | tf_op jit(solution)/shard_map/ppermute | solution.py:450
  91.4 5.7 %collective-permute-start.19 = (bf16[2,16,2560]{2,1,0:T(8,128)(2,1)S(1)}, bf16[2,16,2560]{2,1,0:T(8,128)(2,1)S(1)}, u32[]{:S(2)}, u32[]{:S(2)}) collective-permute-start(bf16[2,16,2560]{2,1,0:T(8,128)(2,1)S(1)} %pad_maximum_fusion.6), channel_id=1, source_target_pairs={{0,8},{1,9},{2,10},{3,11},{4,12},{5,13},{6,14},{7,15},{8,0},{9,1},... | collective-permute-start | bytes 491528 | tf_op jit(solution)/shard_map/ppermute | solution.py:450
  97.2 5.4 %collective-permute-start.20 = (bf16[4,16,1280]{2,1,0:T(8,128)(2,1)S(1)}, bf16[4,16,1280]{2,1,0:T(8,128)(2,1)S(1)}, u32[]{:S(2)}, u32[]{:S(2)}) collective-permute-start(bf16[4,16,1280]{2,1,0:T(8,128)(2,1)S(1)} %get-tuple-element.94), channel_id=1, source_target_pairs={{0,4},{1,5},{2,6},{3,7},{4,0},{5,1},{6,2},{7,3},{8,12},{9,13},{10,... | collective-permute-start | bytes 491528 | tf_op jit(solution)/shard_map/ppermute | solution.py:450
  98.3 6.1 %collective-permute-start.23 = (bf16[4,16,1280]{2,1,0:T(8,128)(2,1)S(1)}, bf16[4,16,1280]{2,1,0:T(8,128)(2,1)S(1)}, u32[]{:S(2)}, u32[]{:S(2)}) collective-permute-start(bf16[4,16,1280]{2,1,0:T(8,128)(2,1)S(1)} %get-tuple-element.93), channel_id=1, source_target_pairs={{0,2},{1,3},{2,0},{3,1},{4,6},{5,7},{6,4},{7,5},{8,10},{9,11},{10,... | collective-permute-start | bytes 491528 | tf_op jit(solution)/shard_map/ppermute | solution.py:450
  102.6 8.0 %collective-permute-start.21 = (bf16[8,16,1280]{2,1,0:T(8,128)(2,1)S(1)}, bf16[8,16,1280]{2,1,0:T(8,128)(2,1)S(1)}, u32[]{:S(2)}, u32[]{:S(2)}) collective-permute-start(bf16[8,16,1280]{2,1,0:T(8,128)(2,1)S(1)} %pad_maximum_fusion.4), channel_id=1, source_target_pairs={{0,2},{1,3},{2,0},{3,1},{4,6},{5,7},{6,4},{7,5},{8,10},{9,11},{10,... | collective-permute-start | bytes 983048 | tf_op jit(solution)/shard_map/ppermute | solution.py:450
  104.4 7.1 %collective-permute-start.24 = (bf16[8,16,1280]{2,1,0:T(8,128)(2,1)S(1)}, bf16[8,16,1280]{2,1,0:T(8,128)(2,1)S(1)}, u32[]{:S(2)}, u32[]{:S(2)}) collective-permute-start(bf16[8,16,1280]{2,1,0:T(8,128)(2,1)S(1)} %pad_maximum_fusion.5), channel_id=1, source_target_pairs={{0,4},{1,5},{2,6},{3,7},{4,0},{5,1},{6,2},{7,3},{8,12},{9,13},{10,... | collective-permute-start | bytes 983048 | tf_op jit(solution)/shard_map/ppermute | solution.py:450
  110.7 2.2 %collective-permute-start.22 = (bf16[16,16,1280]{2,1,0:T(8,128)(2,1)S(1)}, bf16[16,16,1280]{2,1,0:T(8,128)(2,1)S(1)}, u32[]{:S(2)}, u32[]{:S(2)}) collective-permute-start(bf16[16,16,1280]{2,1,0:T(8,128)(2,1)S(1)} %pad_maximum_fusion.refs_0_), channel_id=1, source_target_pairs={{0,1},{1,0},{2,3},{3,2},{4,5},{5,4},{6,7},{7,6},{8,9},{9,8},{10,11... | collective-permute-start | bytes 1966088 | tf_op jit(solution)/shard_map/ppermute | solution.py:450
  111.6 2.2 %collective-permute-start.25 = (bf16[16,16,1280]{2,1,0:T(8,128)(2,1)S(1)}, bf16[16,16,1280]{2,1,0:T(8,128)(2,1)S(1)}, u32[]{:S(2)}, u32[]{:S(2)}) collective-permute-start(bf16[16,16,1280]{2,1,0:T(8,128)(2,1)S(1)} %pad_maximum_fusion.1.refs_2_), channel_id=1, source_target_pairs={{0,1},{1,0},{2,3},{3,2},{4,5},{5,4},{6,7},{7,6},{8,9},{9,8},{10,11... | collective-permute-start | bytes 1966088 | tf_op jit(solution)/shard_map/ppermute | solution.py:450

commit v15 on v14

--- a/solution.py
+++ b/solution.py
@@ -441,8 +441,6 @@
     devices_all = plan.chunks
     total_factor = 1.0 / math.sqrt(grad_out.shape[0] * devices_all)
     gain_rows = jnp.stack([gain_in, gain_out])
-    rows = jnp.concatenate([touched_rows, grad_out])
-    weights = jnp.concatenate([w_in, w_out], axis=1)
     ints = jnp.concatenate([row_of_token, row_owner[:, 0], owner_row])[None, :]
     me = lax.axis_index(both).astype(jnp.int32)[None]
 
@@ -457,8 +455,16 @@
     peers = jnp.arange(dp_size, dtype=jnp.int32)
     own = jnp.sum(jnp.where(seq_dest[:, None] == peers, seq_blocks[:, None], 0), axis=0)
     lengths = jnp.where(peers[:, None] == lax.axis_index("dp"), own, 0)
-    for bit in range(dp_size.bit_length() - 1):
-        lengths = lengths + swap(lengths, table_size << bit)
+    steps = [table_size << bit for bit in range(dp_size.bit_length() - 1)]
+    for step, mask in enumerate(steps[::2]):
+        pair = steps[2 * step + 1 : 2 * step + 2]
+        came = [swap(lengths, mask)] + [swap(lengths, far) for far in pair]
+        came += [swap(lengths, far ^ mask) for far in pair]
+        lengths = lengths + sum(came)
+        if step == 0:
+            lengths, touched_rows = lax.optimization_barrier((lengths, touched_rows))
+    rows = jnp.concatenate([touched_rows, grad_out])
+    weights = jnp.concatenate([w_in, w_out], axis=1)
     send = call(
         functools.partial(send_body, table_size, count),
         [shape_of((SLOT, width), BF16)] * dp_size,
@@ -466,7 +472,9 @@
         scratch=[pltpu.SMEM((dp_size,), jnp.int32)],
     )(me, lengths, rows)
     got = list(send)
-    for apart in reversed(range(1, dp_size)):
+    near, far = list(range(dp_size // 2 - 1, 0, -1)), list(range(dp_size - 1, dp_size // 2 - 1, -1))
+    turns = far[:1] + [apart for pair in zip(far[1:], near) for apart in pair]
+    for apart in turns:
         got[apart] = swap(send[apart], apart * table_size)
     shapes = row_shapes(count, width)
     made = call(

time: 117 us -> 115 us (0.983)
    unnamed x20 -> x22, local copies, waits for them, and re-layouts: 2.83 us -> 1.81 us
    ppermute x26 -> x27, waiting for transfers between devices: 44.1 us -> 43.6 us  [swap(): lax.ppermute(values, both, [(here, here ^ mask) for here in range(devices...]
    ppermute x26 -> x27, starting transfers between devices: 34.9 us -> 35 us  [swap(): lax.ppermute(values, both, [(here, here ^ mask) for here in range(devices...]
  transfers between devices with their start and end apart: 28 -> 29, of which waited for: 21 -> 22; matrix products, arithmetic and copies ran while one was open for 4% -> 3% of each run, Pallas kernels for 6% -> 7%
where the time goes in v15:
time: 115 us
  waiting for transfers between devices  47.4 us (41%)
  starting transfers between devices  42.2 us (37%)
  Pallas kernels  19.6 us (17%)
  local copies, waits for them, and re-layouts  2.89 us (3%)
  other arithmetic  1.8 us (2%)
    ppermute x27, waiting for transfers between devices, swap(): lax.ppermute(values, both, [(here, here ^ mask) for here in range(devices...  43.6 us
    ppermute x27, starting transfers between devices, swap(): lax.ppermute(values, both, [(here, here ^ mask) for here in range(devices...  35 us
    pallas_call x1, Pallas kernels, on_device(): call(functools.partial(backward_body, plan, table_size, total_factor), ou...  8.81 us
    all_to_all x2, starting transfers between devices, exchange(): lax.all_to_all(values, axes, split_axis=0, concat_axis=0, tiled=True, axi...  7.21 us
    pallas_call x1, Pallas kernels, on_device(): call(forward_body, list(shapes.values()), [VMEM] * 3, flops=4 * count * w...  3.91 us
    all_to_all x2, waiting for transfers between devices, exchange(): lax.all_to_all(values, axes, split_axis=0, concat_axis=0, tiled=True, axi...  3.77 us
    pallas_call x1, Pallas kernels, on_device(): call(functools.partial(widen_body, plan), (shape_of(w_in.shape, F32), sha...  2.6 us
  transfers between devices with their start and end apart: 29, of which 22 were waited for; matrix products, arithmetic and copies ran while one was open for 3% of the time, Pallas kernels for 7%

profile of v15, /device:TPU:0, one launch (start us, length us, event | category | flops | bytes accessed | tf_op | source)
XLA Modules:
  0.0 114.9 jit_solution(8581439104658533382)
XLA Ops:
  0.6 0.8 select_reduce_fusion
  1.5 4.0 %collective-permute-start.2 = (s32[8,8]{1,0:T(8,128)S(1)}, s32[8,8]{1,0:T(8,128)S(1)}, u32[]{:S(2)}, u32[]{:S(2)}) collective-permute-start(s32[8,8]{1,0:T(8,128)S(1)} %broadcast_select_fusion), channel_id=1, source_target_pairs={{0,12},{1,13},{2,14},{3,15},{4,8},{5,9},{6,10},{7,11},{8,4},{9,5},... | collective-permute-start | bytes 776 | tf_op jit(solution)/shard_map/ppermute | solution.py:448
  6.2 1.7 %constant_dynamic-update-slice_fusion.1 = bf16[512,2560]{1,0:T(8,128)(2,1)S(1)} fusion(bf16[512,2048]{1,0:T(8,128)(2,1)} %param.18), kind=kLoop, calls=%fused_computation.16 | loop fusion | bytes 4194304
  8.1 1.1 collective-permute-done.1
  9.7 2.6 %collective-permute-start.3 = (s32[8,8]{1,0:T(8,128)S(1)}, s32[8,8]{1,0:T(8,128)S(1)}, u32[]{:S(2)}, u32[]{:S(2)}) collective-permute-start(s32[8,8]{1,0:T(8,128)S(1)} %add_add_fusion), channel_id=1, source_target_pairs={{0,16},{1,17},{2,18},{3,19},{4,20},{5,21},{6,22},{7,23},{8,24},{9,... | collective-permute-start | bytes 776 | tf_op jit(solution)/shard_map/ppermute | solution.py:448
  12.3 1.9 %collective-permute-done.3 = s32[8,8]{1,0:T(8,128)S(1)} collective-permute-done((s32[8,8]{1,0:T(8,128)S(1)}, s32[8,8]{1,0:T(8,128)S(1)}, u32[]{:S(2)}, u32[]{:S(2)}) %collective-permute-start.3) | collective-permute-done | bytes 288 | tf_op jit(solution)/shard_map/ppermute | solution.py:448
  14.2 0.7 shard_map.147
  15.3 1.8 %collective-permute-start.5 = (bf16[64,512]{1,0:T(8,128)(2,1)S(1)}, bf16[64,512]{1,0:T(8,128)(2,1)S(1)}, u32[]{:S(2)}, u32[]{:S(2)}) collective-permute-start(bf16[64,512]{1,0:T(8,128)(2,1)S(1)} %get-tuple-element.72), channel_id=1, source_target_pairs={{0,8},{1,9},{2,10},{3,11},{4,12},{5,13},{6,14},{7,15},{8,0},{9,1},... | collective-permute-start | bytes 196616 | tf_op jit(solution)/shard_map/ppermute | solution.py:448
  17.1 1.4 %shard_map.146 = (bf16[256,2560]{1,0:T(8,128)(2,1)S(1)}, bf16[512,256]{1,0:T(8,128)(2,1)S(1)}, bf16[256,2048]{1,0:T(8,128)(2,1)S(1)}, f32[256,512]{1,0:T(8,128)S...) custom-call(bf16[512,512]{1,0:T(8,128)(2,1)S(1)} %constant_dynamic-update-slice_fusion.2.rows_ref, ...), custom_call_target="tpu_custom_call" | custom-call | flops 536870912 | bytes 4000000 | tf_op jit(solution)/shard_map/pallas_call | solution.py:480
  18.5 1.4 %collective-permute-start.6 = (bf16[64,512]{1,0:T(8,128)(2,1)S(1)}, bf16[64,512]{1,0:T(8,128)(2,1)S(1)}, u32[]{:S(2)}, u32[]{:S(2)}) collective-permute-start(bf16[64,512]{1,0:T(8,128)(2,1)S(1)} %get-tuple-element.73), channel_id=1, source_target_pairs={{0,12},{1,13},{2,14},{3,15},{4,8},{5,9},{6,10},{7,11},{8,4},{9,5},... | collective-permute-start | bytes 196616 | tf_op jit(solution)/shard_map/ppermute | solution.py:448
  19.9 2.6 %collective-permute-start.7 = (bf16[64,512]{1,0:T(8,128)(2,1)S(1)}, bf16[64,512]{1,0:T(8,128)(2,1)S(1)}, u32[]{:S(2)}, u32[]{:S(2)}) collective-permute-start(bf16[64,512]{1,0:T(8,128)(2,1)S(1)} %get-tuple-element.74), channel_id=1, source_target_pairs={{0,16},{1,17},{2,18},{3,19},{4,20},{5,21},{6,22},{7,23},{8,24},{9,... | collective-permute-start | bytes 196616 | tf_op jit(solution)/shard_map/ppermute | solution.py:448
  22.6 3.8 %collective-permute-start.9 = (bf16[64,512]{1,0:T(8,128)(2,1)S(1)}, bf16[64,512]{1,0:T(8,128)(2,1)S(1)}, u32[]{:S(2)}, u32[]{:S(2)}) collective-permute-start(bf16[64,512]{1,0:T(8,128)(2,1)S(1)} %get-tuple-element.76), channel_id=1, source_target_pairs={{0,24},{1,25},{2,26},{3,27},{4,28},{5,29},{6,30},{7,31},{8,16},{9,... | collective-permute-start | bytes 196616 | tf_op jit(solution)/shard_map/ppermute | solution.py:448
  26.4 1.2 %collective-permute-start.10 = (bf16[64,512]{1,0:T(8,128)(2,1)S(1)}, bf16[64,512]{1,0:T(8,128)(2,1)S(1)}, u32[]{:S(2)}, u32[]{:S(2)}) collective-permute-start(bf16[64,512]{1,0:T(8,128)(2,1)S(1)} %get-tuple-element.77), channel_id=1, source_target_pairs={{0,28},{1,29},{2,30},{3,31},{4,24},{5,25},{6,26},{7,27},{8,20},{9,... | collective-permute-start | bytes 196616 | tf_op jit(solution)/shard_map/ppermute | solution.py:448
  27.6 3.9 %shard_map.148 = (f32[512,512]{1,0:T(8,128)S(1)}, f32[512,512]{1,0:T(8,128)S(1)}, f32[512,1]{1,0:T(8,128)S(1)}, bf16[512,1536]{1,0:T(8,128)(2,1)S(1)}, bf16[16,1...) custom-call(bf16[256,2560]{1,0:T(8,128)(2,1)S(1)} %get-tuple-element, ...), custom_call_target="tpu_custom_call" | custom-call | flops 2684354560 | bytes 8000000 | tf_op jit(solution)/shard_map/pallas_call | solution.py:490
  31.5 1.8 %collective-permute-done.10.refs_22_ = bf16[64,512]{1,0:T(8,128)(2,1)S(1)} collective-permute-done((bf16[64,512]{1,0:T(8,128)(2,1)S(1)}, bf16[64,512]{1,0:T(8,128)(2,1)S(1)}, u32[]{:S(2)}, u32[]{:S(2)}) %collective-permute-start.10) | collective-permute-done | bytes 65568 | tf_op jit(solution)/shard_map/ppermute | solution.py:448
  33.4 8.8 %shard_map.149 = (bf16[512,640]{1,0:T(8,128)(2,1)}, bf16[16,16,1280]{2,1,0:T(8,128)(2,1)S(1)}, bf16[16,16,1280]{2,1,0:T(8,128)(2,1)S(1)}, bf16[16,16,1280]{2,1,0:T(8,128)(2,1)S(1)}, bf16[16,16,1280]{2,1,0:T(8,128)(2,1)S(1)}) custom-call(s32[1]{0:T(128)} %bitcast.me_ref, s32[8]{0:T(128)S(1)} %copy-done, s32[8]{0:T(128)S(1)} %copy-done.1, ...), custom_call_target="tpu_custom_call" | custom-call | flops 10737418240 | bytes 12000000 | tf_op jit(solution)/shard_map/pallas_call | solution.py:503
  42.7 1.6 %collective-permute-done.11 = bf16[16,16,1280]{2,1,0:T(8,128)(2,1)S(1)} collective-permute-done((bf16[16,16,1280]{2,1,0:T(8,128)(2,1)S(1)}, bf16[16,16,1280]{2,1,0:T(8,128)(2,1)S(1)}, u32[]{:S(2)}, u32[]{:S(2)}) %collective-permute-start.11) | collective-permute-done | bytes 655392 | tf_op jit(solution)/shard_map/ppermute | solution.py:448
  44.5 0.8 collective-permute-done.12
  45.4 1.6 %collective-permute-start.15 = (bf16[8,16,1280]{2,1,0:T(8,128)(2,1)S(1)}, bf16[8,16,1280]{2,1,0:T(8,128)(2,1)S(1)}, u32[]{:S(2)}, u32[]{:S(2)}) collective-permute-start(bf16[8,16,1280]{2,1,0:T(8,128)(2,1)S(1)} %slice.47), channel_id=1, source_target_pairs={{0,4},{1,5},{2,6},{3,7},{4,0},{5,1},{6,2},{7,3},{8,12},{9,13},{10,... | collective-permute-start | bytes 983048 | tf_op jit(solution)/shard_map/ppermute | solution.py:448
  47.0 3.7 %all-to-all-start = ((bf16[4,8,16,640]{3,2,1,0:T(8,128)(2,1)}), bf16[4,8,16,640]{3,2,1,0:T(8,128)(2,1)S(1)}, u32[]{:S(2)}, u32[]{:S(2)}) async-start(bf16[4,8,16,640]{3,2,1,0:T(8,128)(2,1)} %bitcast.5), calls=%async_computation | async-start | bytes 1310720 | tf_op jit(solution)/shard_map/all_to_all | solution.py:451
  50.7 1.6 %collective-permute-start.13 = (bf16[8,16,1280]{2,1,0:T(8,128)(2,1)S(1)}, bf16[8,16,1280]{2,1,0:T(8,128)(2,1)S(1)}, u32[]{:S(2)}, u32[]{:S(2)}) collective-permute-start(bf16[8,16,1280]{2,1,0:T(8,128)(2,1)S(1)} %slice.43), channel_id=1, source_target_pairs={{0,2},{1,3},{2,0},{3,1},{4,6},{5,7},{6,4},{7,5},{8,10},{9,11},{10,... | collective-permute-start | bytes 983048 | tf_op jit(solution)/shard_map/ppermute | solution.py:448
  52.3 3.0 %collective-permute-done.15 = bf16[8,16,1280]{2,1,0:T(8,128)(2,1)S(1)} collective-permute-done((bf16[8,16,1280]{2,1,0:T(8,128)(2,1)S(1)}, bf16[8,16,1280]{2,1,0:T(8,128)(2,1)S(1)}, u32[]{:S(2)}, u32[]{:S(2)}) %collective-permute-start.15) | collective-permute-done | bytes 327712 | tf_op jit(solution)/shard_map/ppermute | solution.py:448
  55.3 1.6 %collective-permute-start.16 = (bf16[4,16,1280]{2,1,0:T(8,128)(2,1)S(1)}, bf16[4,16,1280]{2,1,0:T(8,128)(2,1)S(1)}, u32[]{:S(2)}, u32[]{:S(2)}) collective-permute-start(bf16[4,16,1280]{2,1,0:T(8,128)(2,1)S(1)} %slice.59), channel_id=1, source_target_pairs={{0,2},{1,3},{2,0},{3,1},{4,6},{5,7},{6,4},{7,5},{8,10},{9,11},{10,... | collective-permute-start | bytes 491528 | tf_op jit(solution)/shard_map/ppermute | solution.py:448
  56.9 4.4 %collective-permute-done.13 = bf16[8,16,1280]{2,1,0:T(8,128)(2,1)S(1)} collective-permute-done((bf16[8,16,1280]{2,1,0:T(8,128)(2,1)S(1)}, bf16[8,16,1280]{2,1,0:T(8,128)(2,1)S(1)}, u32[]{:S(2)}, u32[]{:S(2)}) %collective-permute-start.13) | collective-permute-done | bytes 327712 | tf_op jit(solution)/shard_map/ppermute | solution.py:448
  62.1 1.7 %collective-permute-done.16 = bf16[4,16,1280]{2,1,0:T(8,128)(2,1)S(1)} collective-permute-done((bf16[4,16,1280]{2,1,0:T(8,128)(2,1)S(1)}, bf16[4,16,1280]{2,1,0:T(8,128)(2,1)S(1)}, u32[]{:S(2)}, u32[]{:S(2)}) %collective-permute-start.16) | collective-permute-done | bytes 163872 | tf_op jit(solution)/shard_map/ppermute | solution.py:448
  63.8 3.1 %collective-permute-done.14 = bf16[4,16,1280]{2,1,0:T(8,128)(2,1)S(1)} collective-permute-done((bf16[4,16,1280]{2,1,0:T(8,128)(2,1)S(1)}, bf16[4,16,1280]{2,1,0:T(8,128)(2,1)S(1)}, u32[]{:S(2)}, u32[]{:S(2)}) %collective-permute-start.14) | collective-permute-done | bytes 163872 | tf_op jit(solution)/shard_map/ppermute | solution.py:448
  66.9 1.1 all-to-all-done
  68.1 0.8 collective-permute-start.17
  68.9 4.6 %collective-permute-done.17 = bf16[2,16,2560]{2,1,0:T(8,128)(2,1)S(1)} collective-permute-done((bf16[2,16,2560]{2,1,0:T(8,128)(2,1)S(1)}, bf16[2,16,2560]{2,1,0:T(8,128)(2,1)S(1)}, u32[]{:S(2)}, u32[]{:S(2)}) %collective-permute-start.17) | collective-permute-done | bytes 163872 | tf_op jit(solution)/shard_map/ppermute | solution.py:448
  73.5 1.7 %collective-permute-start.18 = (bf16[1,16,2560]{2,1,0:T(8,128)(2,1)S(1)}, bf16[1,16,2560]{2,1,0:T(8,128)(2,1)S(1)}, u32[]{:S(2)}, u32[]{:S(2)}) collective-permute-start(bf16[1,16,2560]{2,1,0:T(8,128)(2,1)S(1)} %slice.61), channel_id=1, source_target_pairs={{0,16},{1,17},{2,18},{3,19},{4,20},{5,21},{6,22},{7,23},{8,24},{9,... | collective-permute-start | bytes 245768 | tf_op jit(solution)/shard_map/ppermute | solution.py:448
  75.2 0.9 copy.18
  76.1 3.5 %all-to-all-start.1 = ((bf16[8,4,16,640]{3,2,1,0:T(8,128)(2,1)}), bf16[8,4,16,640]{3,2,1,0:T(8,128)(2,1)S(1)}, u32[]{:S(2)}, u32[]{:S(2)}) async-start(bf16[8,4,16,640]{3,2,1,0:T(8,128)(2,1)} %copy.18), calls=%async_computation.1 | async-start | bytes 1310720 | tf_op jit(solution)/shard_map/all_to_all | solution.py:451
  79.8 1.3 %collective-permute-start.19 = (bf16[1,16,2560]{2,1,0:T(8,128)(2,1)S(1)}, bf16[1,16,2560]{2,1,0:T(8,128)(2,1)S(1)}, u32[]{:S(2)}, u32[]{:S(2)}) collective-permute-start(bf16[1,16,2560]{2,1,0:T(8,128)(2,1)S(1)} %add_convert_fusion.7), channel_id=1, source_target_pairs={{0,16},{1,17},{2,18},{3,19},{4,20},{5,21},{6,22},{7,23},{8,24},{9,... | collective-permute-start | bytes 245768 | tf_op jit(solution)/shard_map/ppermute | solution.py:448
  81.1 6.1 %collective-permute-done.19 = bf16[1,16,2560]{2,1,0:T(8,128)(2,1)S(1)} collective-permute-done((bf16[1,16,2560]{2,1,0:T(8,128)(2,1)S(1)}, bf16[1,16,2560]{2,1,0:T(8,128)(2,1)S(1)}, u32[]{:S(2)}, u32[]{:S(2)}) %collective-permute-start.19) | collective-permute-done | bytes 81952 | tf_op jit(solution)/shard_map/ppermute | solution.py:448
  87.2 2.6 %all-to-all-done.1 = bf16[8,4,16,640]{3,2,1,0:T(8,128)(2,1)S(1)} async-done(((bf16[8,4,16,640]{3,2,1,0:T(8,128)(2,1)}), bf16[8,4,16,640]{3,2,1,0:T(8,128)(2,1)S(1)}, u32[]{:S(2)}, u32[]{:S(2)}) %all-to-all-start.1) | async-done | bytes 655392 | tf_op jit(solution)/shard_map/all_to_all | solution.py:451
  89.8 1.5 %collective-permute-start.20 = (bf16[2,16,2560]{2,1,0:T(8,128)(2,1)S(1)}, bf16[2,16,2560]{2,1,0:T(8,128)(2,1)S(1)}, u32[]{:S(2)}, u32[]{:S(2)}) collective-permute-start(bf16[2,16,2560]{2,1,0:T(8,128)(2,1)S(1)} %pad_maximum_fusion.6), channel_id=1, source_target_pairs={{0,8},{1,9},{2,10},{3,11},{4,12},{5,13},{6,14},{7,15},{8,0},{9,1},... | collective-permute-start | bytes 491528 | tf_op jit(solution)/shard_map/ppermute | solution.py:448
  91.3 2.2 %shard_map.150 = (f32[1024,512]{1,0:T(8,128)}, f32[1,512]{1,0:T(1,128)}, f32[1,512]{1,0:T(1,128)}) custom-call(bf16[512,640]{1,0:T(8,128)(2,1)S(1)} %bitcast.10), custom_call_target="tpu_custom_call" | custom-call | tf_op jit(solution)/shard_map/pallas_call | solution.py:550
  93.5 2.1 %collective-permute-done.20 = bf16[2,16,2560]{2,1,0:T(8,128)(2,1)S(1)} collective-permute-done((bf16[2,16,2560]{2,1,0:T(8,128)(2,1)S(1)}, bf16[2,16,2560]{2,1,0:T(8,128)(2,1)S(1)}, u32[]{:S(2)}, u32[]{:S(2)}) %collective-permute-start.20) | collective-permute-done | bytes 163872 | tf_op jit(solution)/shard_map/ppermute | solution.py:448
  95.6 1.1 collective-permute-start.21
  96.8 1.0 collective-permute-start.24
  97.7 3.3 %collective-permute-done.21 = bf16[4,16,1280]{2,1,0:T(8,128)(2,1)S(1)} collective-permute-done((bf16[4,16,1280]{2,1,0:T(8,128)(2,1)S(1)}, bf16[4,16,1280]{2,1,0:T(8,128)(2,1)S(1)}, u32[]{:S(2)}, u32[]{:S(2)}) %collective-permute-start.21) | collective-permute-done | bytes 163872 | tf_op jit(solution)/shard_map/ppermute | solution.py:448
  101.1 1.5 %collective-permute-start.22 = (bf16[8,16,1280]{2,1,0:T(8,128)(2,1)S(1)}, bf16[8,16,1280]{2,1,0:T(8,128)(2,1)S(1)}, u32[]{:S(2)}, u32[]{:S(2)}) collective-permute-start(bf16[8,16,1280]{2,1,0:T(8,128)(2,1)S(1)} %pad_maximum_fusion.4), channel_id=1, source_target_pairs={{0,2},{1,3},{2,0},{3,1},{4,6},{5,7},{6,4},{7,5},{8,10},{9,11},{10,... | collective-permute-start | bytes 983048 | tf_op jit(solution)/shard_map/ppermute | solution.py:448
  102.9 1.7 %collective-permute-start.25 = (bf16[8,16,1280]{2,1,0:T(8,128)(2,1)S(1)}, bf16[8,16,1280]{2,1,0:T(8,128)(2,1)S(1)}, u32[]{:S(2)}, u32[]{:S(2)}) collective-permute-start(bf16[8,16,1280]{2,1,0:T(8,128)(2,1)S(1)} %pad_maximum_fusion.5), channel_id=1, source_target_pairs={{0,4},{1,5},{2,6},{3,7},{4,0},{5,1},{6,2},{7,3},{8,12},{9,13},{10,... | collective-permute-start | bytes 983048 | tf_op jit(solution)/shard_map/ppermute | solution.py:448
  104.6 4.5 %collective-permute-done.22 = bf16[8,16,1280]{2,1,0:T(8,128)(2,1)S(1)} collective-permute-done((bf16[8,16,1280]{2,1,0:T(8,128)(2,1)S(1)}, bf16[8,16,1280]{2,1,0:T(8,128)(2,1)S(1)}, u32[]{:S(2)}, u32[]{:S(2)}) %collective-permute-start.22) | collective-permute-done | bytes 327712 | tf_op jit(solution)/shard_map/ppermute | solution.py:448
  109.3 0.8 collective-permute-done.25
  110.2 1.2 %collective-permute-done.23.refs_1_ = bf16[16,16,1280]{2,1,0:T(8,128)(2,1)S(1)} collective-permute-done((bf16[16,16,1280]{2,1,0:T(8,128)(2,1)S(1)}, bf16[16,16,1280]{2,1,0:T(8,128)(2,1)S(1)}, u32[]{:S(2)}, u32[]{:S(2)}) %collective-permute-start.23) | collective-permute-done | bytes 655392 | tf_op jit(solution)/shard_map/ppermute | solution.py:448
  111.3 0.9 collective-permute-done.26.refs_3_
  112.3 2.6 %shard_map.151 = (f32[512,2048]{1,0:T(8,128)}, f32[512,512]{1,0:T(8,128)}) custom-call(s32[1]{0:T(128)} %bitcast.me_ref, bf16[16,16,1280]{2,1,0:T(8,128)(2,1)S(1)} %pad_maximum_fusion.refs_0_, bf16[16,16,1280]{2,1,0:T(8,128)(2,1)S(1)} %collective-permute-done.23.refs_1_, bf16[16,16,1280]{2,1,0:T(8,128)(2,1)S(1)} %pad_maximum_fusion.1.refs_2_, ...), custom_call_target="tpu_custom_call" | custom-call | tf_op jit(solution)/shard_map/pallas_call | solution.py:565
  (70 shorter events, 4.5 us)
Async XLA Ops:
  1.5 6.5 %copy-start.5 = (f32[512]{0:T(512)S(1)}, f32[512]{0:T(512)}, u32[]{:S(2)}) copy-start(f32[512]{0:T(512)} %param.21) | copy-start | bytes 6148
  1.5 6.5 %copy-start.6 = (f32[512]{0:T(512)S(1)}, f32[512]{0:T(512)}, u32[]{:S(2)}) copy-start(f32[512]{0:T(512)} %param.20) | copy-start | bytes 6148
  1.5 6.5 %copy-start.2 = (bf16[512,512]{1,0:T(8,128)(2,1)S(1)}, bf16[512,512]{1,0:T(8,128)(2,1)}, u32[]{:S(2)}) copy-start(bf16[512,512]{1,0:T(8,128)(2,1)} %param.19) | copy-start | bytes 1572868
  1.5 10.8 %copy-start.3 = (bf16[256,512]{1,0:T(8,128)(2,1)S(1)}, bf16[256,512]{1,0:T(8,128)(2,1)}, u32[]{:S(2)}) copy-start(bf16[256,512]{1,0:T(8,128)(2,1)} %param.11) | copy-start | bytes 786436
  1.5 10.8 %copy-start.4 = (bf16[256,512]{1,0:T(8,128)(2,1)S(1)}, bf16[256,512]{1,0:T(8,128)(2,1)}, u32[]{:S(2)}) copy-start(bf16[256,512]{1,0:T(8,128)(2,1)} %param.17) | copy-start | bytes 786436
  1.5 6.6 %collective-permute-start.2 = (s32[8,8]{1,0:T(8,128)S(1)}, s32[8,8]{1,0:T(8,128)S(1)}, u32[]{:S(2)}, u32[]{:S(2)}) collective-permute-start(s32[8,8]{1,0:T(8,128)S(1)} %broadcast_select_fusion), channel_id=1, source_target_pairs={{0,12},{1,13},{2,14},{3,15},{4,8},{5,9},{6,10},{7,11},{8,4},{9,5},... | collective-permute-start | bytes 776 | tf_op jit(solution)/shard_map/ppermute | solution.py:448
  5.5 3.6 %collective-permute-start.1 = (s32[8,8]{1,0:T(8,128)S(1)}, s32[8,8]{1,0:T(8,128)S(1)}, u32[]{:S(2)}, u32[]{:S(2)}) collective-permute-start(s32[8,8]{1,0:T(8,128)S(1)} %broadcast_select_fusion), channel_id=1, source_target_pairs={{0,8},{1,9},{2,10},{3,11},{4,12},{5,13},{6,14},{7,15},{8,0},{9,1},... | collective-permute-start | bytes 776 | tf_op jit(solution)/shard_map/ppermute | solution.py:448
  6.0 3.6 %collective-permute-start = (s32[8,8]{1,0:T(8,128)S(1)}, s32[8,8]{1,0:T(8,128)S(1)}, u32[]{:S(2)}, u32[]{:S(2)}) collective-permute-start(s32[8,8]{1,0:T(8,128)S(1)} %broadcast_select_fusion), channel_id=1, source_target_pairs={{0,4},{1,5},{2,6},{3,7},{4,0},{5,1},{6,2},{7,3},{8,12},{9,13},{10,... | collective-permute-start | bytes 776 | tf_op jit(solution)/shard_map/ppermute | solution.py:448
  7.9 9.1 %copy-start.7 = (s32[512]{0:T(512)S(1)}, s32[512]{0:T(512)}, u32[]{:S(2)}) copy-start(s32[512]{0:T(512)} %param.12) | copy-start | bytes 6148
  7.9 9.1 %copy-start.8 = (s32[256]{0:T(256)S(1)}, s32[256]{0:T(256)}, u32[]{:S(2)}) copy-start(s32[256]{0:T(256)} %param.14) | copy-start | bytes 3076
  7.9 9.1 %copy-start.9 = (s32[256,1]{0,1:T(1,128)S(1)}, s32[256,1]{0,1:T(1,128)}, u32[]{:S(2)}) copy-start(s32[256,1]{0,1:T(1,128)} %param.13) | copy-start | bytes 3076
  9.7 4.5 %collective-permute-start.3 = (s32[8,8]{1,0:T(8,128)S(1)}, s32[8,8]{1,0:T(8,128)S(1)}, u32[]{:S(2)}, u32[]{:S(2)}) collective-permute-start(s32[8,8]{1,0:T(8,128)S(1)} %add_add_fusion), channel_id=1, source_target_pairs={{0,16},{1,17},{2,18},{3,19},{4,20},{5,21},{6,22},{7,23},{8,24},{9,... | collective-permute-start | bytes 776 | tf_op jit(solution)/shard_map/ppermute | solution.py:448
  14.9 7.8 %collective-permute-start.4 = (bf16[64,512]{1,0:T(8,128)(2,1)S(1)}, bf16[64,512]{1,0:T(8,128)(2,1)S(1)}, u32[]{:S(2)}, u32[]{:S(2)}) collective-permute-start(bf16[64,512]{1,0:T(8,128)(2,1)S(1)} %get-tuple-element.71), channel_id=1, source_target_pairs={{0,4},{1,5},{2,6},{3,7},{4,0},{5,1},{6,2},{7,3},{8,12},{9,13},{10,... | collective-permute-start | bytes 196616 | tf_op jit(solution)/shard_map/ppermute | solution.py:448
  15.3 11.1 %collective-permute-start.5 = (bf16[64,512]{1,0:T(8,128)(2,1)S(1)}, bf16[64,512]{1,0:T(8,128)(2,1)S(1)}, u32[]{:S(2)}, u32[]{:S(2)}) collective-permute-start(bf16[64,512]{1,0:T(8,128)(2,1)S(1)} %get-tuple-element.72), channel_id=1, source_target_pairs={{0,8},{1,9},{2,10},{3,11},{4,12},{5,13},{6,14},{7,15},{8,0},{9,1},... | collective-permute-start | bytes 196616 | tf_op jit(solution)/shard_map/ppermute | solution.py:448
  18.5 13.0 %collective-permute-start.6 = (bf16[64,512]{1,0:T(8,128)(2,1)S(1)}, bf16[64,512]{1,0:T(8,128)(2,1)S(1)}, u32[]{:S(2)}, u32[]{:S(2)}) collective-permute-start(bf16[64,512]{1,0:T(8,128)(2,1)S(1)} %get-tuple-element.73), channel_id=1, source_target_pairs={{0,12},{1,13},{2,14},{3,15},{4,8},{5,9},{6,10},{7,11},{8,4},{9,5},... | collective-permute-start | bytes 196616 | tf_op jit(solution)/shard_map/ppermute | solution.py:448
  19.9 11.6 %collective-permute-start.7 = (bf16[64,512]{1,0:T(8,128)(2,1)S(1)}, bf16[64,512]{1,0:T(8,128)(2,1)S(1)}, u32[]{:S(2)}, u32[]{:S(2)}) collective-permute-start(bf16[64,512]{1,0:T(8,128)(2,1)S(1)} %get-tuple-element.74), channel_id=1, source_target_pairs={{0,16},{1,17},{2,18},{3,19},{4,20},{5,21},{6,22},{7,23},{8,24},{9,... | collective-permute-start | bytes 196616 | tf_op jit(solution)/shard_map/ppermute | solution.py:448
  22.5 9.0 %collective-permute-start.8 = (bf16[64,512]{1,0:T(8,128)(2,1)S(1)}, bf16[64,512]{1,0:T(8,128)(2,1)S(1)}, u32[]{:S(2)}, u32[]{:S(2)}) collective-permute-start(bf16[64,512]{1,0:T(8,128)(2,1)S(1)} %get-tuple-element.75), channel_id=1, source_target_pairs={{0,20},{1,21},{2,22},{3,23},{4,16},{5,17},{6,18},{7,19},{8,28},{9,... | collective-permute-start | bytes 196616 | tf_op jit(solution)/shard_map/ppermute | solution.py:448
  22.6 8.9 %collective-permute-start.9 = (bf16[64,512]{1,0:T(8,128)(2,1)S(1)}, bf16[64,512]{1,0:T(8,128)(2,1)S(1)}, u32[]{:S(2)}, u32[]{:S(2)}) collective-permute-start(bf16[64,512]{1,0:T(8,128)(2,1)S(1)} %get-tuple-element.76), channel_id=1, source_target_pairs={{0,24},{1,25},{2,26},{3,27},{4,28},{5,29},{6,30},{7,31},{8,16},{9,... | collective-permute-start | bytes 196616 | tf_op jit(solution)/shard_map/ppermute | solution.py:448
  26.4 7.0 %collective-permute-start.10 = (bf16[64,512]{1,0:T(8,128)(2,1)S(1)}, bf16[64,512]{1,0:T(8,128)(2,1)S(1)}, u32[]{:S(2)}, u32[]{:S(2)}) collective-permute-start(bf16[64,512]{1,0:T(8,128)(2,1)S(1)} %get-tuple-element.77), channel_id=1, source_target_pairs={{0,28},{1,29},{2,30},{3,31},{4,24},{5,25},{6,26},{7,27},{8,20},{9,... | collective-permute-start | bytes 196616 | tf_op jit(solution)/shard_map/ppermute | solution.py:448
  27.6 5.8 %copy-start = (s32[8]{0:T(128)S(1)}, s32[8]{0:T(128)}, u32[]{:S(2)}) copy-start(s32[8]{0:T(128)} %dest_ref.1) | copy-start | bytes 100
  27.6 5.8 %copy-start.1 = (s32[8]{0:T(128)S(1)}, s32[8]{0:T(128)}, u32[]{:S(2)}) copy-start(s32[8]{0:T(128)} %blocks_ref.1) | copy-start | bytes 100
  42.2 2.1 %collective-permute-start.11 = (bf16[16,16,1280]{2,1,0:T(8,128)(2,1)S(1)}, bf16[16,16,1280]{2,1,0:T(8,128)(2,1)S(1)}, u32[]{:S(2)}, u32[]{:S(2)}) collective-permute-start(bf16[16,16,1280]{2,1,0:T(8,128)(2,1)S(1)} %get-tuple-element.79), channel_id=1, source_target_pairs={{0,1},{1,0},{2,3},{3,2},{4,5},{5,4},{6,7},{7,6},{8,9},{9,8},{10,11... | collective-permute-start | bytes 1966088 | tf_op jit(solution)/shard_map/ppermute | solution.py:448
  42.2 3.0 %collective-permute-start.12 = (bf16[16,16,1280]{2,1,0:T(8,128)(2,1)S(1)}, bf16[16,16,1280]{2,1,0:T(8,128)(2,1)S(1)}, u32[]{:S(2)}, u32[]{:S(2)}) collective-permute-start(bf16[16,16,1280]{2,1,0:T(8,128)(2,1)S(1)} %get-tuple-element.81), channel_id=1, source_target_pairs={{0,1},{1,0},{2,3},{3,2},{4,5},{5,4},{6,7},{7,6},{8,9},{9,8},{10,11... | collective-permute-start | bytes 1966088 | tf_op jit(solution)/shard_map/ppermute | solution.py:448
  45.4 9.8 %collective-permute-start.15 = (bf16[8,16,1280]{2,1,0:T(8,128)(2,1)S(1)}, bf16[8,16,1280]{2,1,0:T(8,128)(2,1)S(1)}, u32[]{:S(2)}, u32[]{:S(2)}) collective-permute-start(bf16[8,16,1280]{2,1,0:T(8,128)(2,1)S(1)} %slice.47), channel_id=1, source_target_pairs={{0,4},{1,5},{2,6},{3,7},{4,0},{5,1},{6,2},{7,3},{8,12},{9,13},{10,... | collective-permute-start | bytes 983048 | tf_op jit(solution)/shard_map/ppermute | solution.py:448
  47.0 21.1 %all-to-all-start = ((bf16[4,8,16,640]{3,2,1,0:T(8,128)(2,1)}), bf16[4,8,16,640]{3,2,1,0:T(8,128)(2,1)S(1)}, u32[]{:S(2)}, u32[]{:S(2)}) async-start(bf16[4,8,16,640]{3,2,1,0:T(8,128)(2,1)} %bitcast.5), calls=%async_computation | async-start | bytes 1310720 | tf_op jit(solution)/shard_map/all_to_all | solution.py:451
  50.7 10.7 %collective-permute-start.13 = (bf16[8,16,1280]{2,1,0:T(8,128)(2,1)S(1)}, bf16[8,16,1280]{2,1,0:T(8,128)(2,1)S(1)}, u32[]{:S(2)}, u32[]{:S(2)}) collective-permute-start(bf16[8,16,1280]{2,1,0:T(8,128)(2,1)S(1)} %slice.43), channel_id=1, source_target_pairs={{0,2},{1,3},{2,0},{3,1},{4,6},{5,7},{6,4},{7,5},{8,10},{9,11},{10,... | collective-permute-start | bytes 983048 | tf_op jit(solution)/shard_map/ppermute | solution.py:448
  55.3 8.4 %collective-permute-start.16 = (bf16[4,16,1280]{2,1,0:T(8,128)(2,1)S(1)}, bf16[4,16,1280]{2,1,0:T(8,128)(2,1)S(1)}, u32[]{:S(2)}, u32[]{:S(2)}) collective-permute-start(bf16[4,16,1280]{2,1,0:T(8,128)(2,1)S(1)} %slice.59), channel_id=1, source_target_pairs={{0,2},{1,3},{2,0},{3,1},{4,6},{5,7},{6,4},{7,5},{8,10},{9,11},{10,... | collective-permute-start | bytes 491528 | tf_op jit(solution)/shard_map/ppermute | solution.py:448
  61.5 5.4 %collective-permute-start.14 = (bf16[4,16,1280]{2,1,0:T(8,128)(2,1)S(1)}, bf16[4,16,1280]{2,1,0:T(8,128)(2,1)S(1)}, u32[]{:S(2)}, u32[]{:S(2)}) collective-permute-start(bf16[4,16,1280]{2,1,0:T(8,128)(2,1)S(1)} %slice.57), channel_id=1, source_target_pairs={{0,4},{1,5},{2,6},{3,7},{4,0},{5,1},{6,2},{7,3},{8,12},{9,13},{10,... | collective-permute-start | bytes 491528 | tf_op jit(solution)/shard_map/ppermute | solution.py:448
  68.1 5.4 %collective-permute-start.17 = (bf16[2,16,2560]{2,1,0:T(8,128)(2,1)S(1)}, bf16[2,16,2560]{2,1,0:T(8,128)(2,1)S(1)}, u32[]{:S(2)}, u32[]{:S(2)}) collective-permute-start(bf16[2,16,2560]{2,1,0:T(8,128)(2,1)S(1)} %slice.51), channel_id=1, source_target_pairs={{0,8},{1,9},{2,10},{3,11},{4,12},{5,13},{6,14},{7,15},{8,0},{9,1},... | collective-permute-start | bytes 491528 | tf_op jit(solution)/shard_map/ppermute | solution.py:448
  73.5 6.3 %collective-permute-start.18 = (bf16[1,16,2560]{2,1,0:T(8,128)(2,1)S(1)}, bf16[1,16,2560]{2,1,0:T(8,128)(2,1)S(1)}, u32[]{:S(2)}, u32[]{:S(2)}) collective-permute-start(bf16[1,16,2560]{2,1,0:T(8,128)(2,1)S(1)} %slice.61), channel_id=1, source_target_pairs={{0,16},{1,17},{2,18},{3,19},{4,20},{5,21},{6,22},{7,23},{8,24},{9,... | collective-permute-start | bytes 245768 | tf_op jit(solution)/shard_map/ppermute | solution.py:448
  76.1 13.7 %all-to-all-start.1 = ((bf16[8,4,16,640]{3,2,1,0:T(8,128)(2,1)}), bf16[8,4,16,640]{3,2,1,0:T(8,128)(2,1)S(1)}, u32[]{:S(2)}, u32[]{:S(2)}) async-start(bf16[8,4,16,640]{3,2,1,0:T(8,128)(2,1)} %copy.18), calls=%async_computation.1 | async-start | bytes 1310720 | tf_op jit(solution)/shard_map/all_to_all | solution.py:451
  79.8 7.3 %collective-permute-start.19 = (bf16[1,16,2560]{2,1,0:T(8,128)(2,1)S(1)}, bf16[1,16,2560]{2,1,0:T(8,128)(2,1)S(1)}, u32[]{:S(2)}, u32[]{:S(2)}) collective-permute-start(bf16[1,16,2560]{2,1,0:T(8,128)(2,1)S(1)} %add_convert_fusion.7), channel_id=1, source_target_pairs={{0,16},{1,17},{2,18},{3,19},{4,20},{5,21},{6,22},{7,23},{8,24},{9,... | collective-permute-start | bytes 245768 | tf_op jit(solution)/shard_map/ppermute | solution.py:448
  89.8 5.7 %collective-permute-start.20 = (bf16[2,16,2560]{2,1,0:T(8,128)(2,1)S(1)}, bf16[2,16,2560]{2,1,0:T(8,128)(2,1)S(1)}, u32[]{:S(2)}, u32[]{:S(2)}) collective-permute-start(bf16[2,16,2560]{2,1,0:T(8,128)(2,1)S(1)} %pad_maximum_fusion.6), channel_id=1, source_target_pairs={{0,8},{1,9},{2,10},{3,11},{4,12},{5,13},{6,14},{7,15},{8,0},{9,1},... | collective-permute-start | bytes 491528 | tf_op jit(solution)/shard_map/ppermute | solution.py:448
  95.6 5.4 %collective-permute-start.21 = (bf16[4,16,1280]{2,1,0:T(8,128)(2,1)S(1)}, bf16[4,16,1280]{2,1,0:T(8,128)(2,1)S(1)}, u32[]{:S(2)}, u32[]{:S(2)}) collective-permute-start(bf16[4,16,1280]{2,1,0:T(8,128)(2,1)S(1)} %get-tuple-element.98), channel_id=1, source_target_pairs={{0,4},{1,5},{2,6},{3,7},{4,0},{5,1},{6,2},{7,3},{8,12},{9,13},{10,... | collective-permute-start | bytes 491528 | tf_op jit(solution)/shard_map/ppermute | solution.py:448
  96.8 6.1 %collective-permute-start.24 = (bf16[4,16,1280]{2,1,0:T(8,128)(2,1)S(1)}, bf16[4,16,1280]{2,1,0:T(8,128)(2,1)S(1)}, u32[]{:S(2)}, u32[]{:S(2)}) collective-permute-start(bf16[4,16,1280]{2,1,0:T(8,128)(2,1)S(1)} %get-tuple-element.97), channel_id=1, source_target_pairs={{0,2},{1,3},{2,0},{3,1},{4,6},{5,7},{6,4},{7,5},{8,10},{9,11},{10,... | collective-permute-start | bytes 491528 | tf_op jit(solution)/shard_map/ppermute | solution.py:448
  101.1 8.0 %collective-permute-start.22 = (bf16[8,16,1280]{2,1,0:T(8,128)(2,1)S(1)}, bf16[8,16,1280]{2,1,0:T(8,128)(2,1)S(1)}, u32[]{:S(2)}, u32[]{:S(2)}) collective-permute-start(bf16[8,16,1280]{2,1,0:T(8,128)(2,1)S(1)} %pad_maximum_fusion.4), channel_id=1, source_target_pairs={{0,2},{1,3},{2,0},{3,1},{4,6},{5,7},{6,4},{7,5},{8,10},{9,11},{10,... | collective-permute-start | bytes 983048 | tf_op jit(solution)/shard_map/ppermute | solution.py:448
  102.9 7.1 %collective-permute-start.25 = (bf16[8,16,1280]{2,1,0:T(8,128)(2,1)S(1)}, bf16[8,16,1280]{2,1,0:T(8,128)(2,1)S(1)}, u32[]{:S(2)}, u32[]{:S(2)}) collective-permute-start(bf16[8,16,1280]{2,1,0:T(8,128)(2,1)S(1)} %pad_maximum_fusion.5), channel_id=1, source_target_pairs={{0,4},{1,5},{2,6},{3,7},{4,0},{5,1},{6,2},{7,3},{8,12},{9,13},{10,... | collective-permute-start | bytes 983048 | tf_op jit(solution)/shard_map/ppermute | solution.py:448
  109.2 2.2 %collective-permute-start.23 = (bf16[16,16,1280]{2,1,0:T(8,128)(2,1)S(1)}, bf16[16,16,1280]{2,1,0:T(8,128)(2,1)S(1)}, u32[]{:S(2)}, u32[]{:S(2)}) collective-permute-start(bf16[16,16,1280]{2,1,0:T(8,128)(2,1)S(1)} %pad_maximum_fusion.refs_0_), channel_id=1, source_target_pairs={{0,1},{1,0},{2,3},{3,2},{4,5},{5,4},{6,7},{7,6},{8,9},{9,8},{10,11... | collective-permute-start | bytes 1966088 | tf_op jit(solution)/shard_map/ppermute | solution.py:448
  110.1 2.2 %collective-permute-start.26 = (bf16[16,16,1280]{2,1,0:T(8,128)(2,1)S(1)}, bf16[16,16,1280]{2,1,0:T(8,128)(2,1)S(1)}, u32[]{:S(2)}, u32[]{:S(2)}) collective-permute-start(bf16[16,16,1280]{2,1,0:T(8,128)(2,1)S(1)} %pad_maximum_fusion.1.refs_2_), channel_id=1, source_target_pairs={{0,1},{1,0},{2,3},{3,2},{4,5},{5,4},{6,7},{7,6},{8,9},{9,8},{10,11... | collective-permute-start | bytes 1966088 | tf_op jit(solution)/shard_map/ppermute | solution.py:448

commit v16 on v15

--- a/solution.py
+++ b/solution.py
@@ -54,6 +54,12 @@
 TN = ((0,), (0,))
 
 
+def slot_orders(peers):
+    far = list(range(peers - 1, peers // 2 - 1, -1))
+    near = list(range(peers // 2 - 1, 0, -1))
+    return [0] + far + near, [0] + near + far
+
+
 def send_body(table_size, count, me_ref, lengths_ref, rows_ref, *refs):
     out_refs, begin_ref = refs[:-1], refs[-1]
     peers = len(out_refs)
@@ -63,7 +69,9 @@
     for peer in range(peers):
         begin_ref[peer] = begin
         begin = begin + lengths_ref[peer, me]
-    for apart, out_ref in enumerate(out_refs):
+    orders = slot_orders(peers)
+    for turn, out_ref in enumerate(out_refs):
+        apart = jnp.where((me_ref[0] & 1) == 0, orders[0][turn], orders[1][turn])
         begin = begin_ref[me ^ apart]
         for inner in range(LMAXB):
             block = jnp.minimum(begin + inner, blocks - 1)
@@ -262,7 +270,9 @@
     )
     weight_t_ref, mixed_t_ref, normed_t_ref, rows_slope_ref = (used[name] for name in USED[7:11])
     rows_hat_ref, rows_scale_ref, place_ref, digits_ref = (used[name] for name in USED[11:])
-    for apart, got_ref in enumerate(got_refs):
+    orders = slot_orders(len(got_refs))
+    for turn, got_ref in enumerate(got_refs):
+        apart = jnp.where((me_ref[0] & 1) == 0, orders[0][turn], orders[1][turn])
         wide_ref[apart] = got_ref[...]
     for slot in range(len(got_refs)):
         rows = wide_ref[dest_ref[slot] ^ (me_ref[0] // table_size)]
@@ -350,21 +360,23 @@
         self.wide = -(-5 * width // block) * LANES
         self.gain_lanes = 2 * width // self.capacity
         self.extra = -(-(GAIN_AT + self.gain_lanes) // LANES) * LANES
+        first = -(-3 * self.wide // (5 * LANES)) * LANES
         self.split = -(-self.wide // (2 * LANES)) * LANES
-        self.sides = ((0, self.split), (self.split, self.wide - self.split))
+        self.sides = ((0, first), (first, self.wide - first))
+        self.halves = ((0, self.split), (self.split, self.wide - self.split))
         table_bits = [1 << bit for bit in range(1, table_size.bit_length() - 1)]
         dp_bits = [table_size << bit for bit in range(dp_size.bit_length() - 1)]
         self.near_steps = len(table_bits) + 1
         self.orders = (table_bits + dp_bits, dp_bits[:1] + table_bits + dp_bits[1:])
 
-    def chunk_at(self, me, side, place):
+    def chunk_at(self, me, sides, side, place):
         order = [1] + self.orders[side]
         mask = 0
         for step, bit in enumerate(order):
             if place >> (len(order) - 1 - step) & 1:
                 mask ^= bit
         chunk = me ^ mask
-        begin, size = self.sides[side]
+        begin, size = sides[side]
         first = (chunk & (self.row_groups - 1)) * CHUNK_ROWS
         rows = pl.ds(pl.multiple_of(first, CHUNK_ROWS), CHUNK_ROWS)
         if self.column_groups == 1:
@@ -377,14 +389,14 @@
         for side in range(2):
             for place in range(self.chunks):
                 out_ref = part_refs[2 * side + place // half]
-                out_ref[place % half] = sums_ref[self.chunk_at(me, side, place)]
+                out_ref[place % half] = sums_ref[self.chunk_at(me, self.sides, side, place)]
 
     def read(self, me, part_refs, sums_ref):
         half = self.chunks // 2
         for side in range(2):
             for place in range(self.chunks):
                 in_ref = part_refs[2 * side + place // half]
-                sums_ref[self.chunk_at(me, side, place)] = in_ref[place % half]
+                sums_ref[self.chunk_at(me, self.halves, side, place)] = in_ref[place % half]
 
 
 def table_body(plan, got_ref, out_ref, gain_in_ref, gain_out_ref):
@@ -444,8 +456,9 @@
     ints = jnp.concatenate([row_of_token, row_owner[:, 0], owner_row])[None, :]
     me = lax.axis_index(both).astype(jnp.int32)[None]
 
-    def swap(values, mask):
-        return lax.ppermute(values, both, [(here, here ^ mask) for here in range(devices_all)])
+    def swap(values, *masks):
+        pairs = [(here, here ^ masks[here % len(masks)]) for here in range(devices_all)]
+        return lax.ppermute(values, both, pairs)
 
     def exchange(values, axes, groups):
         return lax.all_to_all(
@@ -472,10 +485,9 @@
         scratch=[pltpu.SMEM((dp_size,), jnp.int32)],
     )(me, lengths, rows)
     got = list(send)
-    near, far = list(range(dp_size // 2 - 1, 0, -1)), list(range(dp_size - 1, dp_size // 2 - 1, -1))
-    turns = far[:1] + [apart for pair in zip(far[1:], near) for apart in pair]
-    for apart in turns:
-        got[apart] = swap(send[apart], apart * table_size)
+    orders = slot_orders(dp_size)
+    for turn in range(1, dp_size):
+        got[turn] = swap(send[turn], *(order[turn] * table_size for order in orders))
     shapes = row_shapes(count, width)
     made = call(
         functools.partial(rows_body, plan.capacity),

time: 115 us -> 114 us (level)
    ppermute x27, waiting for transfers between devices: 43.6 us -> 39.3 us  [swap(): return lax.ppermute(values, both, pairs)]
    all_to_all x2, waiting for transfers between devices: 3.77 us -> 7.14 us  [exchange(): lax.all_to_all(values, axes, split_axis=0, concat_axis=0, tiled=True, axi...]
    ppermute x27, starting transfers between devices: 35 us -> 33.7 us  [swap(): return lax.ppermute(values, both, pairs)]
  transfers between devices with their start and end apart: 29 -> 29, of which waited for: 22 -> 20; matrix products, arithmetic and copies ran while one was open for 3% -> 3% of each run, Pallas kernels for 7% -> 7%
where the time goes in v16:
time: 114 us
  waiting for transfers between devices  46.5 us (41%)
  starting transfers between devices  41.7 us (37%)
  Pallas kernels  19.6 us (17%)
  local copies, waits for them, and re-layouts  2.89 us (3%)
  other arithmetic  1.94 us (2%)
    ppermute x27, waiting for transfers between devices, swap(): return lax.ppermute(values, both, pairs)  39.3 us
    ppermute x27, starting transfers between devices, swap(): return lax.ppermute(values, both, pairs)  33.7 us
    pallas_call x1, Pallas kernels, on_device(): call(functools.partial(backward_body, plan, table_size, total_factor), ou...  8.85 us
    all_to_all x2, starting transfers between devices, exchange(): lax.all_to_all(values, axes, split_axis=0, concat_axis=0, tiled=True, axi...  7.98 us
    all_to_all x2, waiting for transfers between devices, exchange(): lax.all_to_all(values, axes, split_axis=0, concat_axis=0, tiled=True, axi...  7.14 us
    pallas_call x1, Pallas kernels, on_device(): call(forward_body, list(shapes.values()), [VMEM] * 3, flops=4 * count * w...  3.91 us
    pallas_call x1, Pallas kernels, on_device(): call(functools.partial(widen_body, plan), (shape_of(w_in.shape, F32), sha...  2.6 us
  transfers between devices with their start and end apart: 29, of which 20 were waited for; matrix products, arithmetic and copies ran while one was open for 3% of the time, Pallas kernels for 7%

profile of v16, /device:TPU:0, one launch (start us, length us, event | category | flops | bytes accessed | tf_op | source)
XLA Modules:
  0.0 113.6 jit_solution(6870673540062575129)
XLA Ops:
  0.6 0.8 select_reduce_fusion
  1.5 4.0 %collective-permute-start.2 = (s32[8,8]{1,0:T(8,128)S(1)}, s32[8,8]{1,0:T(8,128)S(1)}, u32[]{:S(2)}, u32[]{:S(2)}) collective-permute-start(s32[8,8]{1,0:T(8,128)S(1)} %broadcast_select_fusion), channel_id=1, source_target_pairs={{0,12},{1,13},{2,14},{3,15},{4,8},{5,9},{6,10},{7,11},{8,4},{9,5},... | collective-permute-start | bytes 776 | tf_op jit(solution)/shard_map/ppermute | solution.py:461
  6.2 1.7 %constant_dynamic-update-slice_fusion.1 = bf16[512,2560]{1,0:T(8,128)(2,1)S(1)} fusion(bf16[512,2048]{1,0:T(8,128)(2,1)} %param.18), kind=kLoop, calls=%fused_computation.16 | loop fusion | bytes 4194304
  8.1 1.1 collective-permute-done.1
  9.7 2.6 %collective-permute-start.3 = (s32[8,8]{1,0:T(8,128)S(1)}, s32[8,8]{1,0:T(8,128)S(1)}, u32[]{:S(2)}, u32[]{:S(2)}) collective-permute-start(s32[8,8]{1,0:T(8,128)S(1)} %add_add_fusion), channel_id=1, source_target_pairs={{0,16},{1,17},{2,18},{3,19},{4,20},{5,21},{6,22},{7,23},{8,24},{9,... | collective-permute-start | bytes 776 | tf_op jit(solution)/shard_map/ppermute | solution.py:461
  12.3 1.9 %collective-permute-done.3 = s32[8,8]{1,0:T(8,128)S(1)} collective-permute-done((s32[8,8]{1,0:T(8,128)S(1)}, s32[8,8]{1,0:T(8,128)S(1)}, u32[]{:S(2)}, u32[]{:S(2)}) %collective-permute-start.3) | collective-permute-done | bytes 288 | tf_op jit(solution)/shard_map/ppermute | solution.py:461
  14.2 0.7 shard_map.147
  14.9 3.6 %collective-permute-start.4 = (bf16[64,512]{1,0:T(8,128)(2,1)S(1)}, bf16[64,512]{1,0:T(8,128)(2,1)S(1)}, u32[]{:S(2)}, u32[]{:S(2)}) collective-permute-start(bf16[64,512]{1,0:T(8,128)(2,1)S(1)} %get-tuple-element.71), channel_id=1, source_target_pairs={{0,28},{1,13},{2,30},{3,15},{4,24},{5,9},{6,26},{7,11},{8,20},{9,5... | collective-permute-start | bytes 196616 | tf_op jit(solution)/shard_map/ppermute | solution.py:461
  18.6 1.4 %shard_map.146 = (bf16[256,2560]{1,0:T(8,128)(2,1)S(1)}, bf16[512,256]{1,0:T(8,128)(2,1)S(1)}, bf16[256,2048]{1,0:T(8,128)(2,1)S(1)}, f32[256,512]{1,0:T(8,128)S...) custom-call(bf16[512,512]{1,0:T(8,128)(2,1)S(1)} %constant_dynamic-update-slice_fusion.2.rows_ref, ...), custom_call_target="tpu_custom_call" | custom-call | flops 536870912 | bytes 4000000 | tf_op jit(solution)/shard_map/pallas_call | solution.py:492
  20.1 1.9 %collective-permute-start.6 = (bf16[64,512]{1,0:T(8,128)(2,1)S(1)}, bf16[64,512]{1,0:T(8,128)(2,1)S(1)}, u32[]{:S(2)}, u32[]{:S(2)}) collective-permute-start(bf16[64,512]{1,0:T(8,128)(2,1)S(1)} %get-tuple-element.73), channel_id=1, source_target_pairs={{0,20},{1,5},{2,22},{3,7},{4,16},{5,1},{6,18},{7,3},{8,28},{9,13},... | collective-permute-start | bytes 196616 | tf_op jit(solution)/shard_map/ppermute | solution.py:461
  22.0 2.1 %collective-permute-start.7 = (bf16[64,512]{1,0:T(8,128)(2,1)S(1)}, bf16[64,512]{1,0:T(8,128)(2,1)S(1)}, u32[]{:S(2)}, u32[]{:S(2)}) collective-permute-start(bf16[64,512]{1,0:T(8,128)(2,1)S(1)} %get-tuple-element.74), channel_id=1, source_target_pairs={{0,16},{1,29},{2,18},{3,31},{4,20},{5,25},{6,22},{7,27},{8,24},{9,... | collective-permute-start | bytes 196616 | tf_op jit(solution)/shard_map/ppermute | solution.py:461
  24.1 1.3 %collective-permute-start.8 = (bf16[64,512]{1,0:T(8,128)(2,1)S(1)}, bf16[64,512]{1,0:T(8,128)(2,1)S(1)}, u32[]{:S(2)}, u32[]{:S(2)}) collective-permute-start(bf16[64,512]{1,0:T(8,128)(2,1)S(1)} %get-tuple-element.75), channel_id=1, source_target_pairs={{0,12},{1,25},{2,14},{3,27},{4,8},{5,29},{6,10},{7,31},{8,4},{9,17... | collective-permute-start | bytes 196616 | tf_op jit(solution)/shard_map/ppermute | solution.py:461
  25.4 0.6 collective-permute-start.9
  26.0 1.6 %collective-permute-start.10 = (bf16[64,512]{1,0:T(8,128)(2,1)S(1)}, bf16[64,512]{1,0:T(8,128)(2,1)S(1)}, u32[]{:S(2)}, u32[]{:S(2)}) collective-permute-start(bf16[64,512]{1,0:T(8,128)(2,1)S(1)} %get-tuple-element.77), channel_id=1, source_target_pairs={{0,4},{1,17},{2,6},{3,19},{4,0},{5,21},{6,2},{7,23},{8,12},{9,25},... | collective-permute-start | bytes 196616 | tf_op jit(solution)/shard_map/ppermute | solution.py:461
  27.6 3.9 %shard_map.148 = (f32[512,512]{1,0:T(8,128)S(1)}, f32[512,512]{1,0:T(8,128)S(1)}, f32[512,1]{1,0:T(8,128)S(1)}, bf16[512,1536]{1,0:T(8,128)(2,1)S(1)}, bf16[16,1...) custom-call(bf16[256,2560]{1,0:T(8,128)(2,1)S(1)} %get-tuple-element, ...), custom_call_target="tpu_custom_call" | custom-call | flops 2684354560 | bytes 8000000 | tf_op jit(solution)/shard_map/pallas_call | solution.py:502
  31.6 8.9 %shard_map.149 = (bf16[512,640]{1,0:T(8,128)(2,1)}, bf16[16,16,1536]{2,1,0:T(8,128)(2,1)S(1)}, bf16[16,16,1536]{2,1,0:T(8,128)(2,1)S(1)}, bf16[16,16,1024]{2,1,0:T(8,128)(2,1)S(1)}, bf16[16,16,1024]{2,1,0:T(8,128)(2,1)S(1)}) custom-call(s32[1]{0:T(128)} %bitcast.me_ref, s32[8]{0:T(128)S(1)} %copy-done, s32[8]{0:T(128)S(1)} %copy-done.1, ...), custom_call_target="tpu_custom_call" | custom-call | flops 10737418240 | bytes 12000000 | tf_op jit(solution)/shard_map/pallas_call | solution.py:515
  40.9 1.4 %collective-permute-done.12 = bf16[16,16,1024]{2,1,0:T(8,128)(2,1)S(1)} collective-permute-done((bf16[16,16,1024]{2,1,0:T(8,128)(2,1)S(1)}, bf16[16,16,1024]{2,1,0:T(8,128)(2,1)S(1)}, u32[]{:S(2)}, u32[]{:S(2)}) %collective-permute-start.12) | collective-permute-done | bytes 524320 | tf_op jit(solution)/shard_map/ppermute | solution.py:461
  42.5 0.9 collective-permute-done.11
  43.8 1.4 %collective-permute-start.15 = (bf16[8,16,1024]{2,1,0:T(8,128)(2,1)S(1)}, bf16[8,16,1024]{2,1,0:T(8,128)(2,1)S(1)}, u32[]{:S(2)}, u32[]{:S(2)}) collective-permute-start(bf16[8,16,1024]{2,1,0:T(8,128)(2,1)S(1)} %slice.47), channel_id=1, source_target_pairs={{0,4},{1,5},{2,6},{3,7},{4,0},{5,1},{6,2},{7,3},{8,12},{9,13},{10,... | collective-permute-start | bytes 786440 | tf_op jit(solution)/shard_map/ppermute | solution.py:461
  45.2 1.6 %collective-permute-start.13 = (bf16[8,16,1536]{2,1,0:T(8,128)(2,1)S(1)}, bf16[8,16,1536]{2,1,0:T(8,128)(2,1)S(1)}, u32[]{:S(2)}, u32[]{:S(2)}) collective-permute-start(bf16[8,16,1536]{2,1,0:T(8,128)(2,1)S(1)} %slice.43), channel_id=1, source_target_pairs={{0,2},{1,3},{2,0},{3,1},{4,6},{5,7},{6,4},{7,5},{8,10},{9,11},{10,... | collective-permute-start | bytes 1179656 | tf_op jit(solution)/shard_map/ppermute | solution.py:461
  46.8 4.4 %all-to-all-start = ((bf16[4,8,16,640]{3,2,1,0:T(8,128)(2,1)}), bf16[4,8,16,640]{3,2,1,0:T(8,128)(2,1)S(1)}, u32[]{:S(2)}, u32[]{:S(2)}) async-start(bf16[4,8,16,640]{3,2,1,0:T(8,128)(2,1)} %bitcast.5), calls=%async_computation | async-start | bytes 1310720 | tf_op jit(solution)/shard_map/all_to_all | solution.py:464
  51.2 0.9 collective-permute-done.15
  52.3 1.6 %collective-permute-start.16 = (bf16[4,16,1024]{2,1,0:T(8,128)(2,1)S(1)}, bf16[4,16,1024]{2,1,0:T(8,128)(2,1)S(1)}, u32[]{:S(2)}, u32[]{:S(2)}) collective-permute-start(bf16[4,16,1024]{2,1,0:T(8,128)(2,1)S(1)} %slice.59), channel_id=1, source_target_pairs={{0,2},{1,3},{2,0},{3,1},{4,6},{5,7},{6,4},{7,5},{8,10},{9,11},{10,... | collective-permute-start | bytes 393224 | tf_op jit(solution)/shard_map/ppermute | solution.py:461
  53.9 3.4 %collective-permute-done.13 = bf16[8,16,1536]{2,1,0:T(8,128)(2,1)S(1)} collective-permute-done((bf16[8,16,1536]{2,1,0:T(8,128)(2,1)S(1)}, bf16[8,16,1536]{2,1,0:T(8,128)(2,1)S(1)}, u32[]{:S(2)}, u32[]{:S(2)}) %collective-permute-start.13) | collective-permute-done | bytes 393248 | tf_op jit(solution)/shard_map/ppermute | solution.py:461
  57.4 0.7 collective-permute-start.14
  58.1 0.8 collective-permute-done.16
  59.0 4.1 %collective-permute-done.14 = bf16[4,16,1536]{2,1,0:T(8,128)(2,1)S(1)} collective-permute-done((bf16[4,16,1536]{2,1,0:T(8,128)(2,1)S(1)}, bf16[4,16,1536]{2,1,0:T(8,128)(2,1)S(1)}, u32[]{:S(2)}, u32[]{:S(2)}) %collective-permute-start.14) | collective-permute-done | bytes 196640 | tf_op jit(solution)/shard_map/ppermute | solution.py:461
  63.2 5.1 %all-to-all-done = bf16[4,8,16,640]{3,2,1,0:T(8,128)(2,1)S(1)} async-done(((bf16[4,8,16,640]{3,2,1,0:T(8,128)(2,1)}), bf16[4,8,16,640]{3,2,1,0:T(8,128)(2,1)S(1)}, u32[]{:S(2)}, u32[]{:S(2)}) %all-to-all-start) | async-done | bytes 655392 | tf_op jit(solution)/shard_map/all_to_all | solution.py:464
  68.4 5.3 %collective-permute-done.17 = bf16[2,16,2560]{2,1,0:T(8,128)(2,1)S(1)} collective-permute-done((bf16[2,16,2560]{2,1,0:T(8,128)(2,1)S(1)}, bf16[2,16,2560]{2,1,0:T(8,128)(2,1)S(1)}, u32[]{:S(2)}, u32[]{:S(2)}) %collective-permute-start.17) | collective-permute-done | bytes 163872 | tf_op jit(solution)/shard_map/ppermute | solution.py:461
  73.8 0.9 copy.18
  74.7 3.5 %all-to-all-start.1 = ((bf16[8,4,16,640]{3,2,1,0:T(8,128)(2,1)}), bf16[8,4,16,640]{3,2,1,0:T(8,128)(2,1)S(1)}, u32[]{:S(2)}, u32[]{:S(2)}) async-start(bf16[8,4,16,640]{3,2,1,0:T(8,128)(2,1)} %copy.18), calls=%async_computation.1 | async-start | bytes 1310720 | tf_op jit(solution)/shard_map/all_to_all | solution.py:464
  78.3 1.3 %collective-permute-done.18 = bf16[1,16,2560]{2,1,0:T(8,128)(2,1)S(1)} collective-permute-done((bf16[1,16,2560]{2,1,0:T(8,128)(2,1)S(1)}, bf16[1,16,2560]{2,1,0:T(8,128)(2,1)S(1)}, u32[]{:S(2)}, u32[]{:S(2)}) %collective-permute-start.18) | collective-permute-done | bytes 81952 | tf_op jit(solution)/shard_map/ppermute | solution.py:461
  79.6 1.7 %collective-permute-start.19 = (bf16[1,16,2560]{2,1,0:T(8,128)(2,1)S(1)}, bf16[1,16,2560]{2,1,0:T(8,128)(2,1)S(1)}, u32[]{:S(2)}, u32[]{:S(2)}) collective-permute-start(bf16[1,16,2560]{2,1,0:T(8,128)(2,1)S(1)} %add_convert_fusion.7), channel_id=1, source_target_pairs={{0,16},{1,17},{2,18},{3,19},{4,20},{5,21},{6,22},{7,23},{8,24},{9,... | collective-permute-start | bytes 245768 | tf_op jit(solution)/shard_map/ppermute | solution.py:461
  81.3 5.0 %collective-permute-done.19 = bf16[1,16,2560]{2,1,0:T(8,128)(2,1)S(1)} collective-permute-done((bf16[1,16,2560]{2,1,0:T(8,128)(2,1)S(1)}, bf16[1,16,2560]{2,1,0:T(8,128)(2,1)S(1)}, u32[]{:S(2)}, u32[]{:S(2)}) %collective-permute-start.19) | collective-permute-done | bytes 81952 | tf_op jit(solution)/shard_map/ppermute | solution.py:461
  86.4 2.1 %all-to-all-done.1 = bf16[8,4,16,640]{3,2,1,0:T(8,128)(2,1)S(1)} async-done(((bf16[8,4,16,640]{3,2,1,0:T(8,128)(2,1)}), bf16[8,4,16,640]{3,2,1,0:T(8,128)(2,1)S(1)}, u32[]{:S(2)}, u32[]{:S(2)}) %all-to-all-start.1) | async-done | bytes 655392 | tf_op jit(solution)/shard_map/all_to_all | solution.py:464
  88.4 2.0 %collective-permute-start.20 = (bf16[2,16,2560]{2,1,0:T(8,128)(2,1)S(1)}, bf16[2,16,2560]{2,1,0:T(8,128)(2,1)S(1)}, u32[]{:S(2)}, u32[]{:S(2)}) collective-permute-start(bf16[2,16,2560]{2,1,0:T(8,128)(2,1)S(1)} %pad_maximum_fusion.6), channel_id=1, source_target_pairs={{0,8},{1,9},{2,10},{3,11},{4,12},{5,13},{6,14},{7,15},{8,0},{9,1},... | collective-permute-start | bytes 491528 | tf_op jit(solution)/shard_map/ppermute | solution.py:461
  90.4 2.2 %shard_map.150 = (f32[1024,512]{1,0:T(8,128)}, f32[1,512]{1,0:T(1,128)}, f32[1,512]{1,0:T(1,128)}) custom-call(bf16[512,640]{1,0:T(8,128)(2,1)S(1)} %bitcast.10), custom_call_target="tpu_custom_call" | custom-call | tf_op jit(solution)/shard_map/pallas_call | solution.py:562
  92.6 1.8 %collective-permute-done.20 = bf16[2,16,2560]{2,1,0:T(8,128)(2,1)S(1)} collective-permute-done((bf16[2,16,2560]{2,1,0:T(8,128)(2,1)S(1)}, bf16[2,16,2560]{2,1,0:T(8,128)(2,1)S(1)}, u32[]{:S(2)}, u32[]{:S(2)}) %collective-permute-start.20) | collective-permute-done | bytes 163872 | tf_op jit(solution)/shard_map/ppermute | solution.py:461
  94.5 0.9 collective-permute-start.21
  95.4 1.2 %collective-permute-start.24 = (bf16[4,16,1280]{2,1,0:T(8,128)(2,1)S(1)}, bf16[4,16,1280]{2,1,0:T(8,128)(2,1)S(1)}, u32[]{:S(2)}, u32[]{:S(2)}) collective-permute-start(bf16[4,16,1280]{2,1,0:T(8,128)(2,1)S(1)} %get-tuple-element.97), channel_id=1, source_target_pairs={{0,2},{1,3},{2,0},{3,1},{4,6},{5,7},{6,4},{7,5},{8,10},{9,11},{10,... | collective-permute-start | bytes 491528 | tf_op jit(solution)/shard_map/ppermute | solution.py:461
  96.6 3.3 %collective-permute-done.21 = bf16[4,16,1280]{2,1,0:T(8,128)(2,1)S(1)} collective-permute-done((bf16[4,16,1280]{2,1,0:T(8,128)(2,1)S(1)}, bf16[4,16,1280]{2,1,0:T(8,128)(2,1)S(1)}, u32[]{:S(2)}, u32[]{:S(2)}) %collective-permute-start.21) | collective-permute-done | bytes 163872 | tf_op jit(solution)/shard_map/ppermute | solution.py:461
  99.9 1.5 %collective-permute-start.22 = (bf16[8,16,1280]{2,1,0:T(8,128)(2,1)S(1)}, bf16[8,16,1280]{2,1,0:T(8,128)(2,1)S(1)}, u32[]{:S(2)}, u32[]{:S(2)}) collective-permute-start(bf16[8,16,1280]{2,1,0:T(8,128)(2,1)S(1)} %pad_maximum_fusion.4), channel_id=1, source_target_pairs={{0,2},{1,3},{2,0},{3,1},{4,6},{5,7},{6,4},{7,5},{8,10},{9,11},{10,... | collective-permute-start | bytes 983048 | tf_op jit(solution)/shard_map/ppermute | solution.py:461
  101.5 1.7 %collective-permute-start.25 = (bf16[8,16,1280]{2,1,0:T(8,128)(2,1)S(1)}, bf16[8,16,1280]{2,1,0:T(8,128)(2,1)S(1)}, u32[]{:S(2)}, u32[]{:S(2)}) collective-permute-start(bf16[8,16,1280]{2,1,0:T(8,128)(2,1)S(1)} %pad_maximum_fusion.5), channel_id=1, source_target_pairs={{0,4},{1,5},{2,6},{3,7},{4,0},{5,1},{6,2},{7,3},{8,12},{9,13},{10,... | collective-permute-start | bytes 983048 | tf_op jit(solution)/shard_map/ppermute | solution.py:461
  103.2 4.5 %collective-permute-done.22 = bf16[8,16,1280]{2,1,0:T(8,128)(2,1)S(1)} collective-permute-done((bf16[8,16,1280]{2,1,0:T(8,128)(2,1)S(1)}, bf16[8,16,1280]{2,1,0:T(8,128)(2,1)S(1)}, u32[]{:S(2)}, u32[]{:S(2)}) %collective-permute-start.22) | collective-permute-done | bytes 327712 | tf_op jit(solution)/shard_map/ppermute | solution.py:461
  107.8 1.0 collective-permute-done.25
  108.9 1.0 collective-permute-done.23.refs_1_
  109.9 1.1 collective-permute-done.26.refs_3_
  111.0 2.6 %shard_map.151 = (f32[512,2048]{1,0:T(8,128)}, f32[512,512]{1,0:T(8,128)}) custom-call(s32[1]{0:T(128)} %bitcast.me_ref, bf16[16,16,1280]{2,1,0:T(8,128)(2,1)S(1)} %pad_maximum_fusion.refs_0_, bf16[16,16,1280]{2,1,0:T(8,128)(2,1)S(1)} %collective-permute-done.23.refs_1_, bf16[16,16,1280]{2,1,0:T(8,128)(2,1)S(1)} %pad_maximum_fusion.1.refs_2_, ...), custom_call_target="tpu_custom_call" | custom-call | tf_op jit(solution)/shard_map/pallas_call | solution.py:577
  (70 shorter events, 3.4 us)
Async XLA Ops:
  1.5 6.5 %copy-start.5 = (f32[512]{0:T(512)S(1)}, f32[512]{0:T(512)}, u32[]{:S(2)}) copy-start(f32[512]{0:T(512)} %param.21) | copy-start | bytes 6148
  1.5 6.5 %copy-start.6 = (f32[512]{0:T(512)S(1)}, f32[512]{0:T(512)}, u32[]{:S(2)}) copy-start(f32[512]{0:T(512)} %param.20) | copy-start | bytes 6148
  1.5 6.5 %copy-start.2 = (bf16[512,512]{1,0:T(8,128)(2,1)S(1)}, bf16[512,512]{1,0:T(8,128)(2,1)}, u32[]{:S(2)}) copy-start(bf16[512,512]{1,0:T(8,128)(2,1)} %param.19) | copy-start | bytes 1572868
  1.5 10.8 %copy-start.3 = (bf16[256,512]{1,0:T(8,128)(2,1)S(1)}, bf16[256,512]{1,0:T(8,128)(2,1)}, u32[]{:S(2)}) copy-start(bf16[256,512]{1,0:T(8,128)(2,1)} %param.11) | copy-start | bytes 786436
  1.5 10.8 %copy-start.4 = (bf16[256,512]{1,0:T(8,128)(2,1)S(1)}, bf16[256,512]{1,0:T(8,128)(2,1)}, u32[]{:S(2)}) copy-start(bf16[256,512]{1,0:T(8,128)(2,1)} %param.17) | copy-start | bytes 786436
  1.5 6.6 %collective-permute-start.2 = (s32[8,8]{1,0:T(8,128)S(1)}, s32[8,8]{1,0:T(8,128)S(1)}, u32[]{:S(2)}, u32[]{:S(2)}) collective-permute-start(s32[8,8]{1,0:T(8,128)S(1)} %broadcast_select_fusion), channel_id=1, source_target_pairs={{0,12},{1,13},{2,14},{3,15},{4,8},{5,9},{6,10},{7,11},{8,4},{9,5},... | collective-permute-start | bytes 776 | tf_op jit(solution)/shard_map/ppermute | solution.py:461
  5.5 3.6 %collective-permute-start.1 = (s32[8,8]{1,0:T(8,128)S(1)}, s32[8,8]{1,0:T(8,128)S(1)}, u32[]{:S(2)}, u32[]{:S(2)}) collective-permute-start(s32[8,8]{1,0:T(8,128)S(1)} %broadcast_select_fusion), channel_id=1, source_target_pairs={{0,8},{1,9},{2,10},{3,11},{4,12},{5,13},{6,14},{7,15},{8,0},{9,1},... | collective-permute-start | bytes 776 | tf_op jit(solution)/shard_map/ppermute | solution.py:461
  6.0 3.6 %collective-permute-start = (s32[8,8]{1,0:T(8,128)S(1)}, s32[8,8]{1,0:T(8,128)S(1)}, u32[]{:S(2)}, u32[]{:S(2)}) collective-permute-start(s32[8,8]{1,0:T(8,128)S(1)} %broadcast_select_fusion), channel_id=1, source_target_pairs={{0,4},{1,5},{2,6},{3,7},{4,0},{5,1},{6,2},{7,3},{8,12},{9,13},{10,... | collective-permute-start | bytes 776 | tf_op jit(solution)/shard_map/ppermute | solution.py:461
  7.9 10.7 %copy-start.7 = (s32[512]{0:T(512)S(1)}, s32[512]{0:T(512)}, u32[]{:S(2)}) copy-start(s32[512]{0:T(512)} %param.12) | copy-start | bytes 6148
  7.9 10.7 %copy-start.8 = (s32[256]{0:T(256)S(1)}, s32[256]{0:T(256)}, u32[]{:S(2)}) copy-start(s32[256]{0:T(256)} %param.14) | copy-start | bytes 3076
  7.9 10.7 %copy-start.9 = (s32[256,1]{0,1:T(1,128)S(1)}, s32[256,1]{0,1:T(1,128)}, u32[]{:S(2)}) copy-start(s32[256,1]{0,1:T(1,128)} %param.13) | copy-start | bytes 3076
  9.7 4.5 %collective-permute-start.3 = (s32[8,8]{1,0:T(8,128)S(1)}, s32[8,8]{1,0:T(8,128)S(1)}, u32[]{:S(2)}, u32[]{:S(2)}) collective-permute-start(s32[8,8]{1,0:T(8,128)S(1)} %add_add_fusion), channel_id=1, source_target_pairs={{0,16},{1,17},{2,18},{3,19},{4,20},{5,21},{6,22},{7,23},{8,24},{9,... | collective-permute-start | bytes 776 | tf_op jit(solution)/shard_map/ppermute | solution.py:461
  14.9 10.5 %collective-permute-start.4 = (bf16[64,512]{1,0:T(8,128)(2,1)S(1)}, bf16[64,512]{1,0:T(8,128)(2,1)S(1)}, u32[]{:S(2)}, u32[]{:S(2)}) collective-permute-start(bf16[64,512]{1,0:T(8,128)(2,1)S(1)} %get-tuple-element.71), channel_id=1, source_target_pairs={{0,28},{1,13},{2,30},{3,15},{4,24},{5,9},{6,26},{7,11},{8,20},{9,5... | collective-permute-start | bytes 196616 | tf_op jit(solution)/shard_map/ppermute | solution.py:461
  18.5 7.5 %collective-permute-start.5 = (bf16[64,512]{1,0:T(8,128)(2,1)S(1)}, bf16[64,512]{1,0:T(8,128)(2,1)S(1)}, u32[]{:S(2)}, u32[]{:S(2)}) collective-permute-start(bf16[64,512]{1,0:T(8,128)(2,1)S(1)} %get-tuple-element.72), channel_id=1, source_target_pairs={{0,24},{1,9},{2,26},{3,11},{4,28},{5,13},{6,30},{7,15},{8,16},{9,1... | collective-permute-start | bytes 196616 | tf_op jit(solution)/shard_map/ppermute | solution.py:461
  20.1 11.5 %collective-permute-start.6 = (bf16[64,512]{1,0:T(8,128)(2,1)S(1)}, bf16[64,512]{1,0:T(8,128)(2,1)S(1)}, u32[]{:S(2)}, u32[]{:S(2)}) collective-permute-start(bf16[64,512]{1,0:T(8,128)(2,1)S(1)} %get-tuple-element.73), channel_id=1, source_target_pairs={{0,20},{1,5},{2,22},{3,7},{4,16},{5,1},{6,18},{7,3},{8,28},{9,13},... | collective-permute-start | bytes 196616 | tf_op jit(solution)/shard_map/ppermute | solution.py:461
  22.0 9.5 %collective-permute-start.7 = (bf16[64,512]{1,0:T(8,128)(2,1)S(1)}, bf16[64,512]{1,0:T(8,128)(2,1)S(1)}, u32[]{:S(2)}, u32[]{:S(2)}) collective-permute-start(bf16[64,512]{1,0:T(8,128)(2,1)S(1)} %get-tuple-element.74), channel_id=1, source_target_pairs={{0,16},{1,29},{2,18},{3,31},{4,20},{5,25},{6,22},{7,27},{8,24},{9,... | collective-permute-start | bytes 196616 | tf_op jit(solution)/shard_map/ppermute | solution.py:461
  24.1 7.4 %collective-permute-start.8 = (bf16[64,512]{1,0:T(8,128)(2,1)S(1)}, bf16[64,512]{1,0:T(8,128)(2,1)S(1)}, u32[]{:S(2)}, u32[]{:S(2)}) collective-permute-start(bf16[64,512]{1,0:T(8,128)(2,1)S(1)} %get-tuple-element.75), channel_id=1, source_target_pairs={{0,12},{1,25},{2,14},{3,27},{4,8},{5,29},{6,10},{7,31},{8,4},{9,17... | collective-permute-start | bytes 196616 | tf_op jit(solution)/shard_map/ppermute | solution.py:461
  25.4 6.1 %collective-permute-start.9 = (bf16[64,512]{1,0:T(8,128)(2,1)S(1)}, bf16[64,512]{1,0:T(8,128)(2,1)S(1)}, u32[]{:S(2)}, u32[]{:S(2)}) collective-permute-start(bf16[64,512]{1,0:T(8,128)(2,1)S(1)} %get-tuple-element.76), channel_id=1, source_target_pairs={{0,8},{1,21},{2,10},{3,23},{4,12},{5,17},{6,14},{7,19},{8,0},{9,29... | collective-permute-start | bytes 196616 | tf_op jit(solution)/shard_map/ppermute | solution.py:461
  26.0 5.6 %collective-permute-start.10 = (bf16[64,512]{1,0:T(8,128)(2,1)S(1)}, bf16[64,512]{1,0:T(8,128)(2,1)S(1)}, u32[]{:S(2)}, u32[]{:S(2)}) collective-permute-start(bf16[64,512]{1,0:T(8,128)(2,1)S(1)} %get-tuple-element.77), channel_id=1, source_target_pairs={{0,4},{1,17},{2,6},{3,19},{4,0},{5,21},{6,2},{7,23},{8,12},{9,25},... | collective-permute-start | bytes 196616 | tf_op jit(solution)/shard_map/ppermute | solution.py:461
  27.6 4.0 %copy-start = (s32[8]{0:T(128)S(1)}, s32[8]{0:T(128)}, u32[]{:S(2)}) copy-start(s32[8]{0:T(128)} %dest_ref.1) | copy-start | bytes 100
  27.6 4.0 %copy-start.1 = (s32[8]{0:T(128)S(1)}, s32[8]{0:T(128)}, u32[]{:S(2)}) copy-start(s32[8]{0:T(128)} %blocks_ref.1) | copy-start | bytes 100
  40.4 1.9 %collective-permute-start.12 = (bf16[16,16,1024]{2,1,0:T(8,128)(2,1)S(1)}, bf16[16,16,1024]{2,1,0:T(8,128)(2,1)S(1)}, u32[]{:S(2)}, u32[]{:S(2)}) collective-permute-start(bf16[16,16,1024]{2,1,0:T(8,128)(2,1)S(1)} %get-tuple-element.81), channel_id=1, source_target_pairs={{0,1},{1,0},{2,3},{3,2},{4,5},{5,4},{6,7},{7,6},{8,9},{9,8},{10,11... | collective-permute-start | bytes 1572872 | tf_op jit(solution)/shard_map/ppermute | solution.py:461
  40.4 3.0 %collective-permute-start.11 = (bf16[16,16,1536]{2,1,0:T(8,128)(2,1)S(1)}, bf16[16,16,1536]{2,1,0:T(8,128)(2,1)S(1)}, u32[]{:S(2)}, u32[]{:S(2)}) collective-permute-start(bf16[16,16,1536]{2,1,0:T(8,128)(2,1)S(1)} %get-tuple-element.79), channel_id=1, source_target_pairs={{0,1},{1,0},{2,3},{3,2},{4,5},{5,4},{6,7},{7,6},{8,9},{9,8},{10,11... | collective-permute-start | bytes 2359304 | tf_op jit(solution)/shard_map/ppermute | solution.py:461
  43.8 8.4 %collective-permute-start.15 = (bf16[8,16,1024]{2,1,0:T(8,128)(2,1)S(1)}, bf16[8,16,1024]{2,1,0:T(8,128)(2,1)S(1)}, u32[]{:S(2)}, u32[]{:S(2)}) collective-permute-start(bf16[8,16,1024]{2,1,0:T(8,128)(2,1)S(1)} %slice.47), channel_id=1, source_target_pairs={{0,4},{1,5},{2,6},{3,7},{4,0},{5,1},{6,2},{7,3},{8,12},{9,13},{10,... | collective-permute-start | bytes 786440 | tf_op jit(solution)/shard_map/ppermute | solution.py:461
  45.2 12.1 %collective-permute-start.13 = (bf16[8,16,1536]{2,1,0:T(8,128)(2,1)S(1)}, bf16[8,16,1536]{2,1,0:T(8,128)(2,1)S(1)}, u32[]{:S(2)}, u32[]{:S(2)}) collective-permute-start(bf16[8,16,1536]{2,1,0:T(8,128)(2,1)S(1)} %slice.43), channel_id=1, source_target_pairs={{0,2},{1,3},{2,0},{3,1},{4,6},{5,7},{6,4},{7,5},{8,10},{9,11},{10,... | collective-permute-start | bytes 1179656 | tf_op jit(solution)/shard_map/ppermute | solution.py:461
  46.8 21.5 %all-to-all-start = ((bf16[4,8,16,640]{3,2,1,0:T(8,128)(2,1)}), bf16[4,8,16,640]{3,2,1,0:T(8,128)(2,1)S(1)}, u32[]{:S(2)}, u32[]{:S(2)}) async-start(bf16[4,8,16,640]{3,2,1,0:T(8,128)(2,1)} %bitcast.5), calls=%async_computation | async-start | bytes 1310720 | tf_op jit(solution)/shard_map/all_to_all | solution.py:464
  52.3 6.7 %collective-permute-start.16 = (bf16[4,16,1024]{2,1,0:T(8,128)(2,1)S(1)}, bf16[4,16,1024]{2,1,0:T(8,128)(2,1)S(1)}, u32[]{:S(2)}, u32[]{:S(2)}) collective-permute-start(bf16[4,16,1024]{2,1,0:T(8,128)(2,1)S(1)} %slice.59), channel_id=1, source_target_pairs={{0,2},{1,3},{2,0},{3,1},{4,6},{5,7},{6,4},{7,5},{8,10},{9,11},{10,... | collective-permute-start | bytes 393224 | tf_op jit(solution)/shard_map/ppermute | solution.py:461
  57.4 5.7 %collective-permute-start.14 = (bf16[4,16,1536]{2,1,0:T(8,128)(2,1)S(1)}, bf16[4,16,1536]{2,1,0:T(8,128)(2,1)S(1)}, u32[]{:S(2)}, u32[]{:S(2)}) collective-permute-start(bf16[4,16,1536]{2,1,0:T(8,128)(2,1)S(1)} %slice.57), channel_id=1, source_target_pairs={{0,4},{1,5},{2,6},{3,7},{4,0},{5,1},{6,2},{7,3},{8,12},{9,13},{10,... | collective-permute-start | bytes 589832 | tf_op jit(solution)/shard_map/ppermute | solution.py:461
  68.3 5.4 %collective-permute-start.17 = (bf16[2,16,2560]{2,1,0:T(8,128)(2,1)S(1)}, bf16[2,16,2560]{2,1,0:T(8,128)(2,1)S(1)}, u32[]{:S(2)}, u32[]{:S(2)}) collective-permute-start(bf16[2,16,2560]{2,1,0:T(8,128)(2,1)S(1)} %slice.51), channel_id=1, source_target_pairs={{0,8},{1,9},{2,10},{3,11},{4,12},{5,13},{6,14},{7,15},{8,0},{9,1},... | collective-permute-start | bytes 491528 | tf_op jit(solution)/shard_map/ppermute | solution.py:461
  73.7 5.8 %collective-permute-start.18 = (bf16[1,16,2560]{2,1,0:T(8,128)(2,1)S(1)}, bf16[1,16,2560]{2,1,0:T(8,128)(2,1)S(1)}, u32[]{:S(2)}, u32[]{:S(2)}) collective-permute-start(bf16[1,16,2560]{2,1,0:T(8,128)(2,1)S(1)} %slice.61), channel_id=1, source_target_pairs={{0,16},{1,17},{2,18},{3,19},{4,20},{5,21},{6,22},{7,23},{8,24},{9,... | collective-permute-start | bytes 245768 | tf_op jit(solution)/shard_map/ppermute | solution.py:461
  74.7 13.7 %all-to-all-start.1 = ((bf16[8,4,16,640]{3,2,1,0:T(8,128)(2,1)}), bf16[8,4,16,640]{3,2,1,0:T(8,128)(2,1)S(1)}, u32[]{:S(2)}, u32[]{:S(2)}) async-start(bf16[8,4,16,640]{3,2,1,0:T(8,128)(2,1)} %copy.18), calls=%async_computation.1 | async-start | bytes 1310720 | tf_op jit(solution)/shard_map/all_to_all | solution.py:464
  79.6 6.7 %collective-permute-start.19 = (bf16[1,16,2560]{2,1,0:T(8,128)(2,1)S(1)}, bf16[1,16,2560]{2,1,0:T(8,128)(2,1)S(1)}, u32[]{:S(2)}, u32[]{:S(2)}) collective-permute-start(bf16[1,16,2560]{2,1,0:T(8,128)(2,1)S(1)} %add_convert_fusion.7), channel_id=1, source_target_pairs={{0,16},{1,17},{2,18},{3,19},{4,20},{5,21},{6,22},{7,23},{8,24},{9,... | collective-permute-start | bytes 245768 | tf_op jit(solution)/shard_map/ppermute | solution.py:461
  88.4 6.0 %collective-permute-start.20 = (bf16[2,16,2560]{2,1,0:T(8,128)(2,1)S(1)}, bf16[2,16,2560]{2,1,0:T(8,128)(2,1)S(1)}, u32[]{:S(2)}, u32[]{:S(2)}) collective-permute-start(bf16[2,16,2560]{2,1,0:T(8,128)(2,1)S(1)} %pad_maximum_fusion.6), channel_id=1, source_target_pairs={{0,8},{1,9},{2,10},{3,11},{4,12},{5,13},{6,14},{7,15},{8,0},{9,1},... | collective-permute-start | bytes 491528 | tf_op jit(solution)/shard_map/ppermute | solution.py:461
  94.5 5.4 %collective-permute-start.21 = (bf16[4,16,1280]{2,1,0:T(8,128)(2,1)S(1)}, bf16[4,16,1280]{2,1,0:T(8,128)(2,1)S(1)}, u32[]{:S(2)}, u32[]{:S(2)}) collective-permute-start(bf16[4,16,1280]{2,1,0:T(8,128)(2,1)S(1)} %get-tuple-element.98), channel_id=1, source_target_pairs={{0,4},{1,5},{2,6},{3,7},{4,0},{5,1},{6,2},{7,3},{8,12},{9,13},{10,... | collective-permute-start | bytes 491528 | tf_op jit(solution)/shard_map/ppermute | solution.py:461
  95.4 6.1 %collective-permute-start.24 = (bf16[4,16,1280]{2,1,0:T(8,128)(2,1)S(1)}, bf16[4,16,1280]{2,1,0:T(8,128)(2,1)S(1)}, u32[]{:S(2)}, u32[]{:S(2)}) collective-permute-start(bf16[4,16,1280]{2,1,0:T(8,128)(2,1)S(1)} %get-tuple-element.97), channel_id=1, source_target_pairs={{0,2},{1,3},{2,0},{3,1},{4,6},{5,7},{6,4},{7,5},{8,10},{9,11},{10,... | collective-permute-start | bytes 491528 | tf_op jit(solution)/shard_map/ppermute | solution.py:461
  99.9 7.8 %collective-permute-start.22 = (bf16[8,16,1280]{2,1,0:T(8,128)(2,1)S(1)}, bf16[8,16,1280]{2,1,0:T(8,128)(2,1)S(1)}, u32[]{:S(2)}, u32[]{:S(2)}) collective-permute-start(bf16[8,16,1280]{2,1,0:T(8,128)(2,1)S(1)} %pad_maximum_fusion.4), channel_id=1, source_target_pairs={{0,2},{1,3},{2,0},{3,1},{4,6},{5,7},{6,4},{7,5},{8,10},{9,11},{10,... | collective-permute-start | bytes 983048 | tf_op jit(solution)/shard_map/ppermute | solution.py:461
  101.5 7.3 %collective-permute-start.25 = (bf16[8,16,1280]{2,1,0:T(8,128)(2,1)S(1)}, bf16[8,16,1280]{2,1,0:T(8,128)(2,1)S(1)}, u32[]{:S(2)}, u32[]{:S(2)}) collective-permute-start(bf16[8,16,1280]{2,1,0:T(8,128)(2,1)S(1)} %pad_maximum_fusion.5), channel_id=1, source_target_pairs={{0,4},{1,5},{2,6},{3,7},{4,0},{5,1},{6,2},{7,3},{8,12},{9,13},{10,... | collective-permute-start | bytes 983048 | tf_op jit(solution)/shard_map/ppermute | solution.py:461
  107.8 2.2 %collective-permute-start.23 = (bf16[16,16,1280]{2,1,0:T(8,128)(2,1)S(1)}, bf16[16,16,1280]{2,1,0:T(8,128)(2,1)S(1)}, u32[]{:S(2)}, u32[]{:S(2)}) collective-permute-start(bf16[16,16,1280]{2,1,0:T(8,128)(2,1)S(1)} %pad_maximum_fusion.refs_0_), channel_id=1, source_target_pairs={{0,1},{1,0},{2,3},{3,2},{4,5},{5,4},{6,7},{7,6},{8,9},{9,8},{10,11... | collective-permute-start | bytes 1966088 | tf_op jit(solution)/shard_map/ppermute | solution.py:461
  108.9 2.2 %collective-permute-start.26 = (bf16[16,16,1280]{2,1,0:T(8,128)(2,1)S(1)}, bf16[16,16,1280]{2,1,0:T(8,128)(2,1)S(1)}, u32[]{:S(2)}, u32[]{:S(2)}) collective-permute-start(bf16[16,16,1280]{2,1,0:T(8,128)(2,1)S(1)} %pad_maximum_fusion.1.refs_2_), channel_id=1, source_target_pairs={{0,1},{1,0},{2,3},{3,2},{4,5},{5,4},{6,7},{7,6},{8,9},{9,8},{10,11... | collective-permute-start | bytes 1966088 | tf_op jit(solution)/shard_map/ppermute | solution.py:461

commit v17 on v16

--- a/solution.py
+++ b/solution.py
@@ -23,6 +23,7 @@
 BF16 = jnp.bfloat16
 VMEM = pl.BlockSpec(memory_space=pltpu.VMEM)
 SMEM = pl.BlockSpec(memory_space=pltpu.SMEM)
+ANY = pl.BlockSpec(memory_space=pl.ANY)
 
 
 def call(body, out_shape, in_specs, flops=0, moved=0, scratch=(), mebibytes=24):
@@ -369,34 +370,30 @@
         self.near_steps = len(table_bits) + 1
         self.orders = (table_bits + dp_bits, dp_bits[:1] + table_bits + dp_bits[1:])
 
-    def chunk_at(self, me, sides, side, place):
+    def chunk(self, me, side, place):
         order = [1] + self.orders[side]
         mask = 0
         for step, bit in enumerate(order):
             if place >> (len(order) - 1 - step) & 1:
                 mask ^= bit
-        chunk = me ^ mask
-        begin, size = sides[side]
-        first = (chunk & (self.row_groups - 1)) * CHUNK_ROWS
-        rows = pl.ds(pl.multiple_of(first, CHUNK_ROWS), CHUNK_ROWS)
+        return me ^ mask
+
+    def columns(self, chunk, part):
+        begin, size = part
         if self.column_groups == 1:
-            return rows, slice(begin, begin + size)
+            return slice(begin, begin + size)
         group = chunk >> (self.row_groups.bit_length() - 1)
-        return rows, pl.ds(pl.multiple_of(group * self.wide + begin, LANES), size)
+        return pl.ds(pl.multiple_of(group * self.wide + begin, LANES), size)
 
     def write(self, me, sums_ref, part_refs):
         half = self.chunks // 2
         for side in range(2):
             for place in range(self.chunks):
+                chunk = self.chunk(me, side, place)
+                first = pl.multiple_of((chunk & (self.row_groups - 1)) * CHUNK_ROWS, CHUNK_ROWS)
+                rows = pl.ds(first, CHUNK_ROWS)
                 out_ref = part_refs[2 * side + place // half]
-                out_ref[place % half] = sums_ref[self.chunk_at(me, self.sides, side, place)]
-
-    def read(self, me, part_refs, sums_ref):
-        half = self.chunks // 2
-        for side in range(2):
-            for place in range(self.chunks):
-                in_ref = part_refs[2 * side + place // half]
-                sums_ref[self.chunk_at(me, self.halves, side, place)] = in_ref[place % half]
+                out_ref[place % half] = sums_ref[rows, self.columns(chunk, self.sides[side])]
 
 
 def table_body(plan, got_ref, out_ref, gain_in_ref, gain_out_ref):
@@ -420,12 +417,30 @@
         ]
 
 
-def widen_body(plan, me_ref, *refs):
-    w_in_ref, w_out_ref, sums_ref = refs[4:]
-    plan.read(me_ref[0], refs[:4], sums_ref)
-    width = w_out_ref.shape[0]
-    w_out_ref[...] = sums_ref[:, :width].astype(F32)
-    w_in_ref[...] = sums_ref[:, width : 5 * width].astype(F32)
+def widen_body(plan, came, me_ref, left_ref, right_ref, *refs):
+    w_in_ref, w_out_ref, stage_ref, sems = refs[-4:]
+    side = (me_ref[0] & 1) ^ came
+    half, blocks = plan.chunks // 2, plan.row_groups // 2
+    for part, in_ref in enumerate((left_ref, right_ref)):
+        for place in range(half):
+            chunk = plan.chunk(me_ref[0], part, came * half + place)
+            row = (chunk & (plan.row_groups - 1)) >> 1
+            rows = pl.ds(pl.multiple_of(row * CHUNK_ROWS, CHUNK_ROWS), CHUNK_ROWS)
+            stage_ref[rows, plan.columns(chunk, plan.halves[part])] = in_ref[place].astype(F32)
+    split = w_out_ref.shape[1]
+    copies = []
+    for block in range(blocks):
+        first = pl.multiple_of((2 * block + side) * CHUNK_ROWS, CHUNK_ROWS)
+        here = stage_ref.at[pl.ds(block * CHUNK_ROWS, CHUNK_ROWS)]
+        there = pl.ds(first, CHUNK_ROWS)
+        copies += [
+            pltpu.make_async_copy(here.at[:, split:], w_in_ref.at[there], sems.at[0, block]),
+            pltpu.make_async_copy(here.at[:, :split], w_out_ref.at[there], sems.at[1, block]),
+        ]
+    for copy in copies:
+        copy.start()
+    for copy in copies:
+        copy.wait()
 
 
 def add(left, right):
@@ -551,10 +566,12 @@
     for step in range(plan.near_steps):
         sides = [reduced(sides[side], plan.orders[side][step]) for side in range(2)]
     kept = jnp.concatenate(sides, axis=2)
+    away = plan.orders[0][plan.near_steps :]
+    kept = reduced(kept, away[0])
     kept, table_got = lax.optimization_barrier((kept, table_got))
     groups = [[upper * inside + lower for lower in range(inside)] for upper in range(high)]
     table_got = exchange(jnp.swapaxes(table_got, 0, 1), both, groups)
-    for mask in plan.orders[0][plan.near_steps :]:
+    for mask in away[1:]:
         kept = reduced(kept, mask)
     back = plan.orders[0][: plan.near_steps - 1 : -1]
     kept = gathered(kept, back[0])
@@ -574,12 +591,24 @@
     sides = [kept[..., : plan.split], kept[..., plan.split :]]
     for step in reversed(range(plan.near_steps)):
         sides = [gathered(sides[side], plan.orders[side][step]) for side in range(2)]
-    grad_w_in, grad_w_out = call(
-        functools.partial(widen_body, plan),
-        (shape_of(w_in.shape, F32), shape_of(w_out.shape, F32)),
-        [SMEM] + [VMEM] * 4,
-        scratch=[pltpu.VMEM((width, plan.column_groups * plan.wide), BF16)],
-    )(me, sides[0], swap(sides[0], 1), sides[1], swap(sides[1], 1))
+    came = [swap(side, 1) for side in sides]
+    rows = width // 2
+    outs = [shape_of(w_in.shape, F32), shape_of(w_out.shape, F32)]
+    for turn, parts in enumerate((sides, came)):
+        written = () if turn == 0 else (grad_w_in, grad_w_out)
+        grad_w_in, grad_w_out = pl.pallas_call(
+            functools.partial(widen_body, plan, turn),
+            out_shape=outs,
+            in_specs=[SMEM] + [VMEM] * 2 + [ANY] * len(written),
+            out_specs=[ANY] * 2,
+            scratch_shapes=[
+                pltpu.VMEM((rows, 5 * width), F32),
+                pltpu.SemaphoreType.DMA((2, plan.row_groups // 2)),
+            ],
+            input_output_aliases={3: 0, 4: 1} if written else {},
+            compiler_params=pltpu.CompilerParams(vmem_limit_bytes=24 * 1024 * 1024),
+            cost_estimate=pl.CostEstimate(flops=0, bytes_accessed=4_000_000, transcendentals=0),
+        )(me, *parts, *written)
     return (table_part, grad_w_in, grad_w_out, grad_gain_in[0], grad_gain_out[0])
 
 

time: 114 us -> 111 us (0.974)
  waiting for transfers between devices: 46.5 us -> 39.1 us
  local copies, waits for them, and re-layouts: 2.89 us -> 4.76 us
  Pallas kernels: 19.6 us -> 21 us
    all_to_all x2, waiting for transfers between devices: 7.14 us -> 2.63 us  [exchange(): lax.all_to_all(values, axes, split_axis=0, concat_axis=0, tiled=True, axi...]
    ppermute x27, waiting for transfers between devices: 39.3 us -> 36.5 us  [swap(): return lax.ppermute(values, both, pairs)]
    pallas_call x1 -> x2, Pallas kernels: 2.6 us -> 3.93 us  [on_device(): pl.pallas_call(functools.partial(widen_body, plan, turn), out_shape=outs,...]
    unnamed x22 -> x18, local copies, waits for them, and re-layouts: 1.81 us -> 2.74 us
  transfers between devices with their start and end apart: 29 -> 29, of which waited for: 20 -> 17; matrix products, arithmetic and copies ran while one was open for 3% -> 5% of each run, Pallas kernels for 7% -> 9%
where the time goes in v17:
time: 111 us
  starting transfers between devices  42.6 us (38%)
  waiting for transfers between devices  39.1 us (35%)
  Pallas kernels  21 us (19%)
  local copies, waits for them, and re-layouts  4.76 us (4%)
  other arithmetic  1.99 us (2%)
  between operations  1.19 us (1%)
    ppermute x27, waiting for transfers between devices, swap(): return lax.ppermute(values, both, pairs)  36.5 us
    ppermute x27, starting transfers between devices, swap(): return lax.ppermute(values, both, pairs)  34 us
    pallas_call x1, Pallas kernels, on_device(): call(functools.partial(backward_body, plan, table_size, total_factor), ou...  8.9 us
    all_to_all x2, starting transfers between devices, exchange(): lax.all_to_all(values, axes, split_axis=0, concat_axis=0, tiled=True, axi...  8.63 us
    pallas_call x2, Pallas kernels, on_device(): pl.pallas_call(functools.partial(widen_body, plan, turn), out_shape=outs,...  3.93 us
    pallas_call x1, Pallas kernels, on_device(): call(forward_body, list(shapes.values()), [VMEM] * 3, flops=4 * count * w...  3.92 us
    unnamed x18, local copies, waits for them, and re-layouts  2.74 us
    all_to_all x2, waiting for transfers between devices, exchange(): lax.all_to_all(values, axes, split_axis=0, concat_axis=0, tiled=True, axi...  2.63 us
  transfers between devices with their start and end apart: 29, of which 17 were waited for; matrix products, arithmetic and copies ran while one was open for 5% of the time, Pallas kernels for 9%

profile of v17, /device:TPU:0, one launch (start us, length us, event | category | flops | bytes accessed | tf_op | source)
XLA Modules:
  0.0 110.7 jit_solution(14373820996738804233)
XLA Ops:
  0.7 0.8 select_reduce_fusion
  1.6 4.0 %collective-permute-start.2 = (s32[8,8]{1,0:T(8,128)S(1)}, s32[8,8]{1,0:T(8,128)S(1)}, u32[]{:S(2)}, u32[]{:S(2)}) collective-permute-start(s32[8,8]{1,0:T(8,128)S(1)} %broadcast_select_fusion), channel_id=1, source_target_pairs={{0,12},{1,13},{2,14},{3,15},{4,8},{5,9},{6,10},{7,11},{8,4},{9,5},... | collective-permute-start | bytes 776 | tf_op jit(solution)/shard_map/ppermute | solution.py:476
  6.2 1.7 %constant_dynamic-update-slice_fusion.1 = bf16[512,2560]{1,0:T(8,128)(2,1)S(1)} fusion(bf16[512,2048]{1,0:T(8,128)(2,1)} %param.18), kind=kLoop, calls=%fused_computation.19 | loop fusion | bytes 4194304
  8.1 1.1 collective-permute-done.1
  9.7 2.6 %collective-permute-start.3 = (s32[8,8]{1,0:T(8,128)S(1)}, s32[8,8]{1,0:T(8,128)S(1)}, u32[]{:S(2)}, u32[]{:S(2)}) collective-permute-start(s32[8,8]{1,0:T(8,128)S(1)} %add_add_fusion), channel_id=1, source_target_pairs={{0,16},{1,17},{2,18},{3,19},{4,20},{5,21},{6,22},{7,23},{8,24},{9,... | collective-permute-start | bytes 776 | tf_op jit(solution)/shard_map/ppermute | solution.py:476
  12.3 1.0 constant_dynamic-update-slice_fusion.3
  13.3 1.0 constant_dynamic-update-slice_fusion.2.rows_ref
  14.3 0.7 shard_map.147
  15.0 3.6 %collective-permute-start.4 = (bf16[64,512]{1,0:T(8,128)(2,1)S(1)}, bf16[64,512]{1,0:T(8,128)(2,1)S(1)}, u32[]{:S(2)}, u32[]{:S(2)}) collective-permute-start(bf16[64,512]{1,0:T(8,128)(2,1)S(1)} %get-tuple-element.73), channel_id=1, source_target_pairs={{0,28},{1,13},{2,30},{3,15},{4,24},{5,9},{6,26},{7,11},{8,20},{9,5... | collective-permute-start | bytes 196616 | tf_op jit(solution)/shard_map/ppermute | solution.py:476
  18.8 1.4 %shard_map.146 = (bf16[256,2560]{1,0:T(8,128)(2,1)S(1)}, bf16[512,256]{1,0:T(8,128)(2,1)S(1)}, bf16[256,2048]{1,0:T(8,128)(2,1)S(1)}, f32[256,512]{1,0:T(8,128)S...) custom-call(bf16[512,512]{1,0:T(8,128)(2,1)S(1)} %constant_dynamic-update-slice_fusion.2.rows_ref, ...), custom_call_target="tpu_custom_call" | custom-call | flops 536870912 | bytes 4000000 | tf_op jit(solution)/shard_map/pallas_call | solution.py:507
  20.3 1.7 %collective-permute-start.6 = (bf16[64,512]{1,0:T(8,128)(2,1)S(1)}, bf16[64,512]{1,0:T(8,128)(2,1)S(1)}, u32[]{:S(2)}, u32[]{:S(2)}) collective-permute-start(bf16[64,512]{1,0:T(8,128)(2,1)S(1)} %get-tuple-element.75), channel_id=1, source_target_pairs={{0,20},{1,5},{2,22},{3,7},{4,16},{5,1},{6,18},{7,3},{8,28},{9,13},... | collective-permute-start | bytes 196616 | tf_op jit(solution)/shard_map/ppermute | solution.py:476
  22.0 2.2 %collective-permute-start.7 = (bf16[64,512]{1,0:T(8,128)(2,1)S(1)}, bf16[64,512]{1,0:T(8,128)(2,1)S(1)}, u32[]{:S(2)}, u32[]{:S(2)}) collective-permute-start(bf16[64,512]{1,0:T(8,128)(2,1)S(1)} %get-tuple-element.76), channel_id=1, source_target_pairs={{0,16},{1,29},{2,18},{3,31},{4,20},{5,25},{6,22},{7,27},{8,24},{9,... | collective-permute-start | bytes 196616 | tf_op jit(solution)/shard_map/ppermute | solution.py:476
  24.2 1.3 %collective-permute-start.8 = (bf16[64,512]{1,0:T(8,128)(2,1)S(1)}, bf16[64,512]{1,0:T(8,128)(2,1)S(1)}, u32[]{:S(2)}, u32[]{:S(2)}) collective-permute-start(bf16[64,512]{1,0:T(8,128)(2,1)S(1)} %get-tuple-element.77), channel_id=1, source_target_pairs={{0,12},{1,25},{2,14},{3,27},{4,8},{5,29},{6,10},{7,31},{8,4},{9,17... | collective-permute-start | bytes 196616 | tf_op jit(solution)/shard_map/ppermute | solution.py:476
  25.5 0.7 collective-permute-start.9
  26.2 1.5 %collective-permute-start.10 = (bf16[64,512]{1,0:T(8,128)(2,1)S(1)}, bf16[64,512]{1,0:T(8,128)(2,1)S(1)}, u32[]{:S(2)}, u32[]{:S(2)}) collective-permute-start(bf16[64,512]{1,0:T(8,128)(2,1)S(1)} %get-tuple-element.79), channel_id=1, source_target_pairs={{0,4},{1,17},{2,6},{3,19},{4,0},{5,21},{6,2},{7,23},{8,12},{9,25},... | collective-permute-start | bytes 196616 | tf_op jit(solution)/shard_map/ppermute | solution.py:476
  27.7 3.9 %shard_map.148 = (f32[512,512]{1,0:T(8,128)S(1)}, f32[512,512]{1,0:T(8,128)S(1)}, f32[512,1]{1,0:T(8,128)S(1)}, bf16[512,1536]{1,0:T(8,128)(2,1)S(1)}, bf16[16,1...) custom-call(bf16[256,2560]{1,0:T(8,128)(2,1)S(1)} %get-tuple-element, ...), custom_call_target="tpu_custom_call" | custom-call | flops 2684354560 | bytes 8000000 | tf_op jit(solution)/shard_map/pallas_call | solution.py:517
  31.7 8.9 %shard_map.149 = (bf16[512,640]{1,0:T(8,128)(2,1)}, bf16[16,16,1536]{2,1,0:T(8,128)(2,1)S(1)}, bf16[16,16,1536]{2,1,0:T(8,128)(2,1)S(1)}, bf16[16,16,1024]{2,1,0:T(8,128)(2,1)S(1)}, bf16[16,16,1024]{2,1,0:T(8,128)(2,1)S(1)}) custom-call(s32[1]{0:T(128)} %bitcast.me_ref, s32[8]{0:T(128)S(1)} %copy-done, s32[8]{0:T(128)S(1)} %copy-done.1, ...), custom_call_target="tpu_custom_call" | custom-call | flops 10737418240 | bytes 12000000 | tf_op jit(solution)/shard_map/pallas_call | solution.py:530
  40.6 0.5 collective-permute-start.11
  41.1 1.4 %collective-permute-done.12 = bf16[16,16,1024]{2,1,0:T(8,128)(2,1)S(1)} collective-permute-done((bf16[16,16,1024]{2,1,0:T(8,128)(2,1)S(1)}, bf16[16,16,1024]{2,1,0:T(8,128)(2,1)S(1)}, u32[]{:S(2)}, u32[]{:S(2)}) %collective-permute-start.12) | collective-permute-done | bytes 524320 | tf_op jit(solution)/shard_map/ppermute | solution.py:476
  42.7 0.9 collective-permute-done.11
  43.9 1.5 %collective-permute-start.15 = (bf16[8,16,1024]{2,1,0:T(8,128)(2,1)S(1)}, bf16[8,16,1024]{2,1,0:T(8,128)(2,1)S(1)}, u32[]{:S(2)}, u32[]{:S(2)}) collective-permute-start(bf16[8,16,1024]{2,1,0:T(8,128)(2,1)S(1)} %slice.47), channel_id=1, source_target_pairs={{0,4},{1,5},{2,6},{3,7},{4,0},{5,1},{6,2},{7,3},{8,12},{9,13},{10,... | collective-permute-start | bytes 786440 | tf_op jit(solution)/shard_map/ppermute | solution.py:476
  45.4 1.6 %collective-permute-start.13 = (bf16[8,16,1536]{2,1,0:T(8,128)(2,1)S(1)}, bf16[8,16,1536]{2,1,0:T(8,128)(2,1)S(1)}, u32[]{:S(2)}, u32[]{:S(2)}) collective-permute-start(bf16[8,16,1536]{2,1,0:T(8,128)(2,1)S(1)} %slice.43), channel_id=1, source_target_pairs={{0,2},{1,3},{2,0},{3,1},{4,6},{5,7},{6,4},{7,5},{8,10},{9,11},{10,... | collective-permute-start | bytes 1179656 | tf_op jit(solution)/shard_map/ppermute | solution.py:476
  47.0 4.3 %all-to-all-start = ((bf16[4,8,16,640]{3,2,1,0:T(8,128)(2,1)}), bf16[4,8,16,640]{3,2,1,0:T(8,128)(2,1)S(1)}, u32[]{:S(2)}, u32[]{:S(2)}) async-start(bf16[4,8,16,640]{3,2,1,0:T(8,128)(2,1)} %bitcast.5), calls=%async_computation | async-start | bytes 1310720 | tf_op jit(solution)/shard_map/all_to_all | solution.py:479
  51.3 1.0 collective-permute-done.15
  52.4 1.6 %collective-permute-start.16 = (bf16[4,16,1024]{2,1,0:T(8,128)(2,1)S(1)}, bf16[4,16,1024]{2,1,0:T(8,128)(2,1)S(1)}, u32[]{:S(2)}, u32[]{:S(2)}) collective-permute-start(bf16[4,16,1024]{2,1,0:T(8,128)(2,1)S(1)} %slice.59), channel_id=1, source_target_pairs={{0,2},{1,3},{2,0},{3,1},{4,6},{5,7},{6,4},{7,5},{8,10},{9,11},{10,... | collective-permute-start | bytes 393224 | tf_op jit(solution)/shard_map/ppermute | solution.py:476
  54.0 3.5 %collective-permute-done.13 = bf16[8,16,1536]{2,1,0:T(8,128)(2,1)S(1)} collective-permute-done((bf16[8,16,1536]{2,1,0:T(8,128)(2,1)S(1)}, bf16[8,16,1536]{2,1,0:T(8,128)(2,1)S(1)}, u32[]{:S(2)}, u32[]{:S(2)}) %collective-permute-start.13) | collective-permute-done | bytes 393248 | tf_op jit(solution)/shard_map/ppermute | solution.py:476
  57.6 0.7 collective-permute-start.14
  58.3 0.9 collective-permute-done.16
  59.2 4.1 %collective-permute-done.14 = bf16[4,16,1536]{2,1,0:T(8,128)(2,1)S(1)} collective-permute-done((bf16[4,16,1536]{2,1,0:T(8,128)(2,1)S(1)}, bf16[4,16,1536]{2,1,0:T(8,128)(2,1)S(1)}, u32[]{:S(2)}, u32[]{:S(2)}) %collective-permute-start.14) | collective-permute-done | bytes 196640 | tf_op jit(solution)/shard_map/ppermute | solution.py:476
  63.9 6.2 %collective-permute-done.17 = bf16[2,16,2560]{2,1,0:T(8,128)(2,1)S(1)} collective-permute-done((bf16[2,16,2560]{2,1,0:T(8,128)(2,1)S(1)}, bf16[2,16,2560]{2,1,0:T(8,128)(2,1)S(1)}, u32[]{:S(2)}, u32[]{:S(2)}) %collective-permute-start.17) | collective-permute-done | bytes 163872 | tf_op jit(solution)/shard_map/ppermute | solution.py:476
  70.2 0.5 collective-permute-start.18
  70.7 0.9 copy.20
  71.6 4.3 %all-to-all-start.1 = ((bf16[8,4,16,640]{3,2,1,0:T(8,128)(2,1)}), bf16[8,4,16,640]{3,2,1,0:T(8,128)(2,1)S(1)}, u32[]{:S(2)}, u32[]{:S(2)}) async-start(bf16[8,4,16,640]{3,2,1,0:T(8,128)(2,1)} %copy.20), calls=%async_computation.1 | async-start | bytes 1310720 | tf_op jit(solution)/shard_map/all_to_all | solution.py:479
  75.9 1.8 %collective-permute-start.19 = (bf16[1,16,2560]{2,1,0:T(8,128)(2,1)S(1)}, bf16[1,16,2560]{2,1,0:T(8,128)(2,1)S(1)}, u32[]{:S(2)}, u32[]{:S(2)}) collective-permute-start(bf16[1,16,2560]{2,1,0:T(8,128)(2,1)S(1)} %add_convert_fusion.7), channel_id=1, source_target_pairs={{0,16},{1,17},{2,18},{3,19},{4,20},{5,21},{6,22},{7,23},{8,24},{9,... | collective-permute-start | bytes 245768 | tf_op jit(solution)/shard_map/ppermute | solution.py:476
  77.8 5.7 %collective-permute-done.19 = bf16[1,16,2560]{2,1,0:T(8,128)(2,1)S(1)} collective-permute-done((bf16[1,16,2560]{2,1,0:T(8,128)(2,1)S(1)}, bf16[1,16,2560]{2,1,0:T(8,128)(2,1)S(1)}, u32[]{:S(2)}, u32[]{:S(2)}) %collective-permute-start.19) | collective-permute-done | bytes 81952 | tf_op jit(solution)/shard_map/ppermute | solution.py:476
  83.5 2.6 %all-to-all-done.1 = bf16[8,4,16,640]{3,2,1,0:T(8,128)(2,1)S(1)} async-done(((bf16[8,4,16,640]{3,2,1,0:T(8,128)(2,1)}), bf16[8,4,16,640]{3,2,1,0:T(8,128)(2,1)S(1)}, u32[]{:S(2)}, u32[]{:S(2)}) %all-to-all-start.1) | async-done | bytes 655392 | tf_op jit(solution)/shard_map/all_to_all | solution.py:479
  86.2 1.4 %collective-permute-start.20 = (bf16[2,16,2560]{2,1,0:T(8,128)(2,1)S(1)}, bf16[2,16,2560]{2,1,0:T(8,128)(2,1)S(1)}, u32[]{:S(2)}, u32[]{:S(2)}) collective-permute-start(bf16[2,16,2560]{2,1,0:T(8,128)(2,1)S(1)} %pad_maximum_fusion.6), channel_id=1, source_target_pairs={{0,8},{1,9},{2,10},{3,11},{4,12},{5,13},{6,14},{7,15},{8,0},{9,1},... | collective-permute-start | bytes 491528 | tf_op jit(solution)/shard_map/ppermute | solution.py:476
  87.5 2.2 %shard_map.150 = (f32[1024,512]{1,0:T(8,128)}, f32[1,512]{1,0:T(1,128)}, f32[1,512]{1,0:T(1,128)}) custom-call(bf16[512,640]{1,0:T(8,128)(2,1)S(1)} %bitcast.10), custom_call_target="tpu_custom_call" | custom-call | tf_op jit(solution)/shard_map/pallas_call | solution.py:579
  89.7 2.2 %collective-permute-done.20 = bf16[2,16,2560]{2,1,0:T(8,128)(2,1)S(1)} collective-permute-done((bf16[2,16,2560]{2,1,0:T(8,128)(2,1)S(1)}, bf16[2,16,2560]{2,1,0:T(8,128)(2,1)S(1)}, u32[]{:S(2)}, u32[]{:S(2)}) %collective-permute-start.20) | collective-permute-done | bytes 163872 | tf_op jit(solution)/shard_map/ppermute | solution.py:476
  92.0 1.1 collective-permute-start.21
  93.1 1.0 collective-permute-start.24
  94.1 3.3 %collective-permute-done.21 = bf16[4,16,1280]{2,1,0:T(8,128)(2,1)S(1)} collective-permute-done((bf16[4,16,1280]{2,1,0:T(8,128)(2,1)S(1)}, bf16[4,16,1280]{2,1,0:T(8,128)(2,1)S(1)}, u32[]{:S(2)}, u32[]{:S(2)}) %collective-permute-start.21) | collective-permute-done | bytes 163872 | tf_op jit(solution)/shard_map/ppermute | solution.py:476
  97.4 1.5 %collective-permute-start.22 = (bf16[8,16,1280]{2,1,0:T(8,128)(2,1)S(1)}, bf16[8,16,1280]{2,1,0:T(8,128)(2,1)S(1)}, u32[]{:S(2)}, u32[]{:S(2)}) collective-permute-start(bf16[8,16,1280]{2,1,0:T(8,128)(2,1)S(1)} %pad_maximum_fusion.3), channel_id=1, source_target_pairs={{0,2},{1,3},{2,0},{3,1},{4,6},{5,7},{6,4},{7,5},{8,10},{9,11},{10,... | collective-permute-start | bytes 983048 | tf_op jit(solution)/shard_map/ppermute | solution.py:476
  99.2 1.7 %collective-permute-start.25 = (bf16[8,16,1280]{2,1,0:T(8,128)(2,1)S(1)}, bf16[8,16,1280]{2,1,0:T(8,128)(2,1)S(1)}, u32[]{:S(2)}, u32[]{:S(2)}) collective-permute-start(bf16[8,16,1280]{2,1,0:T(8,128)(2,1)S(1)} %pad_maximum_fusion.4), channel_id=1, source_target_pairs={{0,4},{1,5},{2,6},{3,7},{4,0},{5,1},{6,2},{7,3},{8,12},{9,13},{10,... | collective-permute-start | bytes 983048 | tf_op jit(solution)/shard_map/ppermute | solution.py:476
  100.9 4.5 %collective-permute-done.22 = bf16[8,16,1280]{2,1,0:T(8,128)(2,1)S(1)} collective-permute-done((bf16[8,16,1280]{2,1,0:T(8,128)(2,1)S(1)}, bf16[8,16,1280]{2,1,0:T(8,128)(2,1)S(1)}, u32[]{:S(2)}, u32[]{:S(2)}) %collective-permute-start.22) | collective-permute-done | bytes 327712 | tf_op jit(solution)/shard_map/ppermute | solution.py:476
  105.6 0.8 collective-permute-done.25
  106.5 2.0 %shard_map.151 = (f32[512,2048]{1,0:T(8,128)}, f32[512,512]{1,0:T(8,128)}) custom-call(s32[1]{0:T(128)} %bitcast.me_ref, bf16[16,16,1280]{2,1,0:T(8,128)(2,1)S(1)} %pad_maximum_fusion.left_ref, bf16[16,16,1280]{2,1,0:T(8,128)(2,1)S(1)} %pad_maximum_fusion.1.right_ref), custom_call_target="tpu_custom_call" | custom-call | bytes 4000000 | tf_op jit(solution)/shard_map/pallas_call | solution.py:599
  108.6 2.0 %shard_map.152 = (f32[512,2048]{1,0:T(8,128)}, f32[512,512]{1,0:T(8,128)}) custom-call(s32[1]{0:T(128)} %bitcast.me_ref, bf16[16,16,1280]{2,1,0:T(8,128)(2,1)S(1)} %collective-permute-done.23.left_ref, bf16[16,16,1280]{2,1,0:T(8,128)(2,1)S(1)} %collective-permute-done.26.right_ref, ...), custom_call_target="tpu_custom_call", output_to_operand_aliasing={{0}: (3, {}), {1}: (4, {})} | custom-call | bytes 4000000 | tf_op jit(solution)/shard_map/pallas_call | solution.py:599
  (66 shorter events, 3.7 us)
Async XLA Ops:
  0.6 7.3 %copy-start.3 = (f32[512]{0:T(512)S(1)}, f32[512]{0:T(512)}, u32[]{:S(2)}) copy-start(f32[512]{0:T(512)} %param.21) | copy-start | bytes 6148
  0.6 7.3 %copy-start.4 = (f32[512]{0:T(512)S(1)}, f32[512]{0:T(512)}, u32[]{:S(2)}) copy-start(f32[512]{0:T(512)} %param.20) | copy-start | bytes 6148
  0.7 7.4 %copy-start.2 = (bf16[512,512]{1,0:T(8,128)(2,1)S(1)}, bf16[512,512]{1,0:T(8,128)(2,1)}, u32[]{:S(2)}) copy-start(bf16[512,512]{1,0:T(8,128)(2,1)} %param.19) | copy-start | bytes 1572868
  1.6 17.3 %copy-start.5 = (s32[512]{0:T(512)S(1)}, s32[512]{0:T(512)}, u32[]{:S(2)}) copy-start(s32[512]{0:T(512)} %param.12) | copy-start | bytes 6148
  1.6 17.3 %copy-start.6 = (s32[256]{0:T(256)S(1)}, s32[256]{0:T(256)}, u32[]{:S(2)}) copy-start(s32[256]{0:T(256)} %param.14) | copy-start | bytes 3076
  1.6 17.3 %copy-start.7 = (s32[256,1]{0,1:T(1,128)S(1)}, s32[256,1]{0,1:T(1,128)}, u32[]{:S(2)}) copy-start(s32[256,1]{0,1:T(1,128)} %param.13) | copy-start | bytes 3076
  1.6 6.5 %collective-permute-start.2 = (s32[8,8]{1,0:T(8,128)S(1)}, s32[8,8]{1,0:T(8,128)S(1)}, u32[]{:S(2)}, u32[]{:S(2)}) collective-permute-start(s32[8,8]{1,0:T(8,128)S(1)} %broadcast_select_fusion), channel_id=1, source_target_pairs={{0,12},{1,13},{2,14},{3,15},{4,8},{5,9},{6,10},{7,11},{8,4},{9,5},... | collective-permute-start | bytes 776 | tf_op jit(solution)/shard_map/ppermute | solution.py:476
  5.6 3.6 %collective-permute-start.1 = (s32[8,8]{1,0:T(8,128)S(1)}, s32[8,8]{1,0:T(8,128)S(1)}, u32[]{:S(2)}, u32[]{:S(2)}) collective-permute-start(s32[8,8]{1,0:T(8,128)S(1)} %broadcast_select_fusion), channel_id=1, source_target_pairs={{0,8},{1,9},{2,10},{3,11},{4,12},{5,13},{6,14},{7,15},{8,0},{9,1},... | collective-permute-start | bytes 776 | tf_op jit(solution)/shard_map/ppermute | solution.py:476
  6.0 3.6 %collective-permute-start = (s32[8,8]{1,0:T(8,128)S(1)}, s32[8,8]{1,0:T(8,128)S(1)}, u32[]{:S(2)}, u32[]{:S(2)}) collective-permute-start(s32[8,8]{1,0:T(8,128)S(1)} %broadcast_select_fusion), channel_id=1, source_target_pairs={{0,4},{1,5},{2,6},{3,7},{4,0},{5,1},{6,2},{7,3},{8,12},{9,13},{10,... | collective-permute-start | bytes 776 | tf_op jit(solution)/shard_map/ppermute | solution.py:476
  9.7 4.5 %collective-permute-start.3 = (s32[8,8]{1,0:T(8,128)S(1)}, s32[8,8]{1,0:T(8,128)S(1)}, u32[]{:S(2)}, u32[]{:S(2)}) collective-permute-start(s32[8,8]{1,0:T(8,128)S(1)} %add_add_fusion), channel_id=1, source_target_pairs={{0,16},{1,17},{2,18},{3,19},{4,20},{5,21},{6,22},{7,23},{8,24},{9,... | collective-permute-start | bytes 776 | tf_op jit(solution)/shard_map/ppermute | solution.py:476
  15.0 10.5 %collective-permute-start.4 = (bf16[64,512]{1,0:T(8,128)(2,1)S(1)}, bf16[64,512]{1,0:T(8,128)(2,1)S(1)}, u32[]{:S(2)}, u32[]{:S(2)}) collective-permute-start(bf16[64,512]{1,0:T(8,128)(2,1)S(1)} %get-tuple-element.73), channel_id=1, source_target_pairs={{0,28},{1,13},{2,30},{3,15},{4,24},{5,9},{6,26},{7,11},{8,20},{9,5... | collective-permute-start | bytes 196616 | tf_op jit(solution)/shard_map/ppermute | solution.py:476
  18.6 7.6 %collective-permute-start.5 = (bf16[64,512]{1,0:T(8,128)(2,1)S(1)}, bf16[64,512]{1,0:T(8,128)(2,1)S(1)}, u32[]{:S(2)}, u32[]{:S(2)}) collective-permute-start(bf16[64,512]{1,0:T(8,128)(2,1)S(1)} %get-tuple-element.74), channel_id=1, source_target_pairs={{0,24},{1,9},{2,26},{3,11},{4,28},{5,13},{6,30},{7,15},{8,16},{9,1... | collective-permute-start | bytes 196616 | tf_op jit(solution)/shard_map/ppermute | solution.py:476
  20.3 11.3 %collective-permute-start.6 = (bf16[64,512]{1,0:T(8,128)(2,1)S(1)}, bf16[64,512]{1,0:T(8,128)(2,1)S(1)}, u32[]{:S(2)}, u32[]{:S(2)}) collective-permute-start(bf16[64,512]{1,0:T(8,128)(2,1)S(1)} %get-tuple-element.75), channel_id=1, source_target_pairs={{0,20},{1,5},{2,22},{3,7},{4,16},{5,1},{6,18},{7,3},{8,28},{9,13},... | collective-permute-start | bytes 196616 | tf_op jit(solution)/shard_map/ppermute | solution.py:476
  22.0 9.6 %collective-permute-start.7 = (bf16[64,512]{1,0:T(8,128)(2,1)S(1)}, bf16[64,512]{1,0:T(8,128)(2,1)S(1)}, u32[]{:S(2)}, u32[]{:S(2)}) collective-permute-start(bf16[64,512]{1,0:T(8,128)(2,1)S(1)} %get-tuple-element.76), channel_id=1, source_target_pairs={{0,16},{1,29},{2,18},{3,31},{4,20},{5,25},{6,22},{7,27},{8,24},{9,... | collective-permute-start | bytes 196616 | tf_op jit(solution)/shard_map/ppermute | solution.py:476
  24.2 7.5 %collective-permute-start.8 = (bf16[64,512]{1,0:T(8,128)(2,1)S(1)}, bf16[64,512]{1,0:T(8,128)(2,1)S(1)}, u32[]{:S(2)}, u32[]{:S(2)}) collective-permute-start(bf16[64,512]{1,0:T(8,128)(2,1)S(1)} %get-tuple-element.77), channel_id=1, source_target_pairs={{0,12},{1,25},{2,14},{3,27},{4,8},{5,29},{6,10},{7,31},{8,4},{9,17... | collective-permute-start | bytes 196616 | tf_op jit(solution)/shard_map/ppermute | solution.py:476
  25.5 6.2 %collective-permute-start.9 = (bf16[64,512]{1,0:T(8,128)(2,1)S(1)}, bf16[64,512]{1,0:T(8,128)(2,1)S(1)}, u32[]{:S(2)}, u32[]{:S(2)}) collective-permute-start(bf16[64,512]{1,0:T(8,128)(2,1)S(1)} %get-tuple-element.78), channel_id=1, source_target_pairs={{0,8},{1,21},{2,10},{3,23},{4,12},{5,17},{6,14},{7,19},{8,0},{9,29... | collective-permute-start | bytes 196616 | tf_op jit(solution)/shard_map/ppermute | solution.py:476
  26.2 5.5 %collective-permute-start.10 = (bf16[64,512]{1,0:T(8,128)(2,1)S(1)}, bf16[64,512]{1,0:T(8,128)(2,1)S(1)}, u32[]{:S(2)}, u32[]{:S(2)}) collective-permute-start(bf16[64,512]{1,0:T(8,128)(2,1)S(1)} %get-tuple-element.79), channel_id=1, source_target_pairs={{0,4},{1,17},{2,6},{3,19},{4,0},{5,21},{6,2},{7,23},{8,12},{9,25},... | collective-permute-start | bytes 196616 | tf_op jit(solution)/shard_map/ppermute | solution.py:476
  27.7 4.0 %copy-start = (s32[8]{0:T(128)S(1)}, s32[8]{0:T(128)}, u32[]{:S(2)}) copy-start(s32[8]{0:T(128)} %dest_ref.1) | copy-start | bytes 100
  27.7 4.0 %copy-start.1 = (s32[8]{0:T(128)S(1)}, s32[8]{0:T(128)}, u32[]{:S(2)}) copy-start(s32[8]{0:T(128)} %blocks_ref.1) | copy-start | bytes 100
  40.6 1.9 %collective-permute-start.12 = (bf16[16,16,1024]{2,1,0:T(8,128)(2,1)S(1)}, bf16[16,16,1024]{2,1,0:T(8,128)(2,1)S(1)}, u32[]{:S(2)}, u32[]{:S(2)}) collective-permute-start(bf16[16,16,1024]{2,1,0:T(8,128)(2,1)S(1)} %get-tuple-element.83), channel_id=1, source_target_pairs={{0,1},{1,0},{2,3},{3,2},{4,5},{5,4},{6,7},{7,6},{8,9},{9,8},{10,11... | collective-permute-start | bytes 1572872 | tf_op jit(solution)/shard_map/ppermute | solution.py:476
  40.6 3.0 %collective-permute-start.11 = (bf16[16,16,1536]{2,1,0:T(8,128)(2,1)S(1)}, bf16[16,16,1536]{2,1,0:T(8,128)(2,1)S(1)}, u32[]{:S(2)}, u32[]{:S(2)}) collective-permute-start(bf16[16,16,1536]{2,1,0:T(8,128)(2,1)S(1)} %get-tuple-element.81), channel_id=1, source_target_pairs={{0,1},{1,0},{2,3},{3,2},{4,5},{5,4},{6,7},{7,6},{8,9},{9,8},{10,11... | collective-permute-start | bytes 2359304 | tf_op jit(solution)/shard_map/ppermute | solution.py:476
  43.9 8.4 %collective-permute-start.15 = (bf16[8,16,1024]{2,1,0:T(8,128)(2,1)S(1)}, bf16[8,16,1024]{2,1,0:T(8,128)(2,1)S(1)}, u32[]{:S(2)}, u32[]{:S(2)}) collective-permute-start(bf16[8,16,1024]{2,1,0:T(8,128)(2,1)S(1)} %slice.47), channel_id=1, source_target_pairs={{0,4},{1,5},{2,6},{3,7},{4,0},{5,1},{6,2},{7,3},{8,12},{9,13},{10,... | collective-permute-start | bytes 786440 | tf_op jit(solution)/shard_map/ppermute | solution.py:476
  45.4 12.1 %collective-permute-start.13 = (bf16[8,16,1536]{2,1,0:T(8,128)(2,1)S(1)}, bf16[8,16,1536]{2,1,0:T(8,128)(2,1)S(1)}, u32[]{:S(2)}, u32[]{:S(2)}) collective-permute-start(bf16[8,16,1536]{2,1,0:T(8,128)(2,1)S(1)} %slice.43), channel_id=1, source_target_pairs={{0,2},{1,3},{2,0},{3,1},{4,6},{5,7},{6,4},{7,5},{8,10},{9,11},{10,... | collective-permute-start | bytes 1179656 | tf_op jit(solution)/shard_map/ppermute | solution.py:476
  47.0 23.2 %all-to-all-start = ((bf16[4,8,16,640]{3,2,1,0:T(8,128)(2,1)}), bf16[4,8,16,640]{3,2,1,0:T(8,128)(2,1)S(1)}, u32[]{:S(2)}, u32[]{:S(2)}) async-start(bf16[4,8,16,640]{3,2,1,0:T(8,128)(2,1)} %bitcast.5), calls=%async_computation | async-start | bytes 1310720 | tf_op jit(solution)/shard_map/all_to_all | solution.py:479
  52.4 6.8 %collective-permute-start.16 = (bf16[4,16,1024]{2,1,0:T(8,128)(2,1)S(1)}, bf16[4,16,1024]{2,1,0:T(8,128)(2,1)S(1)}, u32[]{:S(2)}, u32[]{:S(2)}) collective-permute-start(bf16[4,16,1024]{2,1,0:T(8,128)(2,1)S(1)} %slice.59), channel_id=1, source_target_pairs={{0,2},{1,3},{2,0},{3,1},{4,6},{5,7},{6,4},{7,5},{8,10},{9,11},{10,... | collective-permute-start | bytes 393224 | tf_op jit(solution)/shard_map/ppermute | solution.py:476
  57.6 5.7 %collective-permute-start.14 = (bf16[4,16,1536]{2,1,0:T(8,128)(2,1)S(1)}, bf16[4,16,1536]{2,1,0:T(8,128)(2,1)S(1)}, u32[]{:S(2)}, u32[]{:S(2)}) collective-permute-start(bf16[4,16,1536]{2,1,0:T(8,128)(2,1)S(1)} %slice.57), channel_id=1, source_target_pairs={{0,4},{1,5},{2,6},{3,7},{4,0},{5,1},{6,2},{7,3},{8,12},{9,13},{10,... | collective-permute-start | bytes 589832 | tf_op jit(solution)/shard_map/ppermute | solution.py:476
  63.4 6.7 %collective-permute-start.17 = (bf16[2,16,2560]{2,1,0:T(8,128)(2,1)S(1)}, bf16[2,16,2560]{2,1,0:T(8,128)(2,1)S(1)}, u32[]{:S(2)}, u32[]{:S(2)}) collective-permute-start(bf16[2,16,2560]{2,1,0:T(8,128)(2,1)S(1)} %pad_maximum_fusion.5), channel_id=1, source_target_pairs={{0,8},{1,9},{2,10},{3,11},{4,12},{5,13},{6,14},{7,15},{8,0},{9,1},... | collective-permute-start | bytes 491528 | tf_op jit(solution)/shard_map/ppermute | solution.py:476
  70.2 5.7 %collective-permute-start.18 = (bf16[1,16,2560]{2,1,0:T(8,128)(2,1)S(1)}, bf16[1,16,2560]{2,1,0:T(8,128)(2,1)S(1)}, u32[]{:S(2)}, u32[]{:S(2)}) collective-permute-start(bf16[1,16,2560]{2,1,0:T(8,128)(2,1)S(1)} %slice.53), channel_id=1, source_target_pairs={{0,16},{1,17},{2,18},{3,19},{4,20},{5,21},{6,22},{7,23},{8,24},{9,... | collective-permute-start | bytes 245768 | tf_op jit(solution)/shard_map/ppermute | solution.py:476
  71.6 14.6 %all-to-all-start.1 = ((bf16[8,4,16,640]{3,2,1,0:T(8,128)(2,1)}), bf16[8,4,16,640]{3,2,1,0:T(8,128)(2,1)S(1)}, u32[]{:S(2)}, u32[]{:S(2)}) async-start(bf16[8,4,16,640]{3,2,1,0:T(8,128)(2,1)} %copy.20), calls=%async_computation.1 | async-start | bytes 1310720 | tf_op jit(solution)/shard_map/all_to_all | solution.py:479
  75.9 7.6 %collective-permute-start.19 = (bf16[1,16,2560]{2,1,0:T(8,128)(2,1)S(1)}, bf16[1,16,2560]{2,1,0:T(8,128)(2,1)S(1)}, u32[]{:S(2)}, u32[]{:S(2)}) collective-permute-start(bf16[1,16,2560]{2,1,0:T(8,128)(2,1)S(1)} %add_convert_fusion.7), channel_id=1, source_target_pairs={{0,16},{1,17},{2,18},{3,19},{4,20},{5,21},{6,22},{7,23},{8,24},{9,... | collective-permute-start | bytes 245768 | tf_op jit(solution)/shard_map/ppermute | solution.py:476
  86.2 5.7 %collective-permute-start.20 = (bf16[2,16,2560]{2,1,0:T(8,128)(2,1)S(1)}, bf16[2,16,2560]{2,1,0:T(8,128)(2,1)S(1)}, u32[]{:S(2)}, u32[]{:S(2)}) collective-permute-start(bf16[2,16,2560]{2,1,0:T(8,128)(2,1)S(1)} %pad_maximum_fusion.6), channel_id=1, source_target_pairs={{0,8},{1,9},{2,10},{3,11},{4,12},{5,13},{6,14},{7,15},{8,0},{9,1},... | collective-permute-start | bytes 491528 | tf_op jit(solution)/shard_map/ppermute | solution.py:476
  92.0 5.4 %collective-permute-start.21 = (bf16[4,16,1280]{2,1,0:T(8,128)(2,1)S(1)}, bf16[4,16,1280]{2,1,0:T(8,128)(2,1)S(1)}, u32[]{:S(2)}, u32[]{:S(2)}) collective-permute-start(bf16[4,16,1280]{2,1,0:T(8,128)(2,1)S(1)} %get-tuple-element.102), channel_id=1, source_target_pairs={{0,4},{1,5},{2,6},{3,7},{4,0},{5,1},{6,2},{7,3},{8,12},{9,13},{10,... | collective-permute-start | bytes 491528 | tf_op jit(solution)/shard_map/ppermute | solution.py:476
  93.1 6.1 %collective-permute-start.24 = (bf16[4,16,1280]{2,1,0:T(8,128)(2,1)S(1)}, bf16[4,16,1280]{2,1,0:T(8,128)(2,1)S(1)}, u32[]{:S(2)}, u32[]{:S(2)}) collective-permute-start(bf16[4,16,1280]{2,1,0:T(8,128)(2,1)S(1)} %get-tuple-element.101), channel_id=1, source_target_pairs={{0,2},{1,3},{2,0},{3,1},{4,6},{5,7},{6,4},{7,5},{8,10},{9,11},{10,... | collective-permute-start | bytes 491528 | tf_op jit(solution)/shard_map/ppermute | solution.py:476
  97.4 8.0 %collective-permute-start.22 = (bf16[8,16,1280]{2,1,0:T(8,128)(2,1)S(1)}, bf16[8,16,1280]{2,1,0:T(8,128)(2,1)S(1)}, u32[]{:S(2)}, u32[]{:S(2)}) collective-permute-start(bf16[8,16,1280]{2,1,0:T(8,128)(2,1)S(1)} %pad_maximum_fusion.3), channel_id=1, source_target_pairs={{0,2},{1,3},{2,0},{3,1},{4,6},{5,7},{6,4},{7,5},{8,10},{9,11},{10,... | collective-permute-start | bytes 983048 | tf_op jit(solution)/shard_map/ppermute | solution.py:476
  99.2 7.1 %collective-permute-start.25 = (bf16[8,16,1280]{2,1,0:T(8,128)(2,1)S(1)}, bf16[8,16,1280]{2,1,0:T(8,128)(2,1)S(1)}, u32[]{:S(2)}, u32[]{:S(2)}) collective-permute-start(bf16[8,16,1280]{2,1,0:T(8,128)(2,1)S(1)} %pad_maximum_fusion.4), channel_id=1, source_target_pairs={{0,4},{1,5},{2,6},{3,7},{4,0},{5,1},{6,2},{7,3},{8,12},{9,13},{10,... | collective-permute-start | bytes 983048 | tf_op jit(solution)/shard_map/ppermute | solution.py:476
  105.5 3.0 %collective-permute-start.23 = (bf16[16,16,1280]{2,1,0:T(8,128)(2,1)S(1)}, bf16[16,16,1280]{2,1,0:T(8,128)(2,1)S(1)}, u32[]{:S(2)}, u32[]{:S(2)}) collective-permute-start(bf16[16,16,1280]{2,1,0:T(8,128)(2,1)S(1)} %pad_maximum_fusion.left_ref), channel_id=1, source_target_pairs={{0,1},{1,0},{2,3},{3,2},{4,5},{5,4},{6,7},{7,6},{8,9},{9,8},{10,11... | collective-permute-start | bytes 1966088 | tf_op jit(solution)/shard_map/ppermute | solution.py:476
  106.4 2.2 %collective-permute-start.26 = (bf16[16,16,1280]{2,1,0:T(8,128)(2,1)S(1)}, bf16[16,16,1280]{2,1,0:T(8,128)(2,1)S(1)}, u32[]{:S(2)}, u32[]{:S(2)}) collective-permute-start(bf16[16,16,1280]{2,1,0:T(8,128)(2,1)S(1)} %pad_maximum_fusion.1.right_ref), channel_id=1, source_target_pairs={{0,1},{1,0},{2,3},{3,2},{4,5},{5,4},{6,7},{7,6},{8,9},{9,8},{10,11... | collective-permute-start | bytes 1966088 | tf_op jit(solution)/shard_map/ppermute | solution.py:476

commit v18 on v17

--- a/solution.py
+++ b/solution.py
@@ -419,26 +419,34 @@
 
 def widen_body(plan, came, me_ref, left_ref, right_ref, *refs):
     w_in_ref, w_out_ref, stage_ref, sems = refs[-4:]
-    side = (me_ref[0] & 1) ^ came
-    half, blocks = plan.chunks // 2, plan.row_groups // 2
+    half, split = plan.chunks // 2, w_out_ref.shape[1]
+    copies = []
+
+    def send(rows, there, first, size, sem):
+        for out_ref, begin, end in ((w_out_ref, 0, split), (w_in_ref, split, stage_ref.shape[1])):
+            low, high = max(first, begin), min(first + size, end)
+            if low < high:
+                here = stage_ref.at[rows, low:high]
+                target = out_ref.at[there, low - begin : high - begin]
+                copies.append(pltpu.make_async_copy(here, target, sem.at[int(begin > 0)]))
+                copies[-1].start()
+
     for part, in_ref in enumerate((left_ref, right_ref)):
         for place in range(half):
             chunk = plan.chunk(me_ref[0], part, came * half + place)
             row = (chunk & (plan.row_groups - 1)) >> 1
             rows = pl.ds(pl.multiple_of(row * CHUNK_ROWS, CHUNK_ROWS), CHUNK_ROWS)
             stage_ref[rows, plan.columns(chunk, plan.halves[part])] = in_ref[place].astype(F32)
-    split = w_out_ref.shape[1]
-    copies = []
-    for block in range(blocks):
-        first = pl.multiple_of((2 * block + side) * CHUNK_ROWS, CHUNK_ROWS)
-        here = stage_ref.at[pl.ds(block * CHUNK_ROWS, CHUNK_ROWS)]
-        there = pl.ds(first, CHUNK_ROWS)
-        copies += [
-            pltpu.make_async_copy(here.at[:, split:], w_in_ref.at[there], sems.at[0, block]),
-            pltpu.make_async_copy(here.at[:, :split], w_out_ref.at[there], sems.at[1, block]),
-        ]
-    for copy in copies:
-        copy.start()
+            if plan.column_groups == 1:
+                there = pl.ds(pl.multiple_of(chunk * CHUNK_ROWS, CHUNK_ROWS), CHUNK_ROWS)
+                send(rows, there, *plan.halves[part], sems.at[part, place])
+    if plan.column_groups > 1:
+        side = (me_ref[0] & 1) ^ came
+        for block in range(plan.row_groups // 2):
+            first = pl.multiple_of((2 * block + side) * CHUNK_ROWS, CHUNK_ROWS)
+            rows = pl.ds(block * CHUNK_ROWS, CHUNK_ROWS)
+            there = pl.ds(first, CHUNK_ROWS)
+            send(rows, there, 0, stage_ref.shape[1], sems.at[0, block])
     for copy in copies:
         copy.wait()
 
@@ -573,9 +581,6 @@
     table_got = exchange(jnp.swapaxes(table_got, 0, 1), both, groups)
     for mask in away[1:]:
         kept = reduced(kept, mask)
-    back = plan.orders[0][: plan.near_steps - 1 : -1]
-    kept = gathered(kept, back[0])
-    kept, table_got = lax.optimization_barrier((kept, table_got))
     table_part, grad_gain_in, grad_gain_out = call(
         functools.partial(table_body, plan),
         (
@@ -585,11 +590,12 @@
         ),
         [VMEM],
     )(table_got.reshape(devices_all * plan.capacity, -1))
-    for mask in back[1:]:
+    for mask in reversed(away):
         kept = gathered(kept, mask)
-    kept, table_part = lax.optimization_barrier((kept, table_part))
     sides = [kept[..., : plan.split], kept[..., plan.split :]]
     for step in reversed(range(plan.near_steps)):
+        if step == 0:
+            *sides, table_part = lax.optimization_barrier((*sides, table_part))
         sides = [gathered(sides[side], plan.orders[side][step]) for side in range(2)]
     came = [swap(side, 1) for side in sides]
     rows = width // 2
@@ -603,7 +609,7 @@
             out_specs=[ANY] * 2,
             scratch_shapes=[
                 pltpu.VMEM((rows, 5 * width), F32),
-                pltpu.SemaphoreType.DMA((2, plan.row_groups // 2)),
+                pltpu.SemaphoreType.DMA((2, plan.row_groups // 2, 2)),
             ],
             input_output_aliases={3: 0, 4: 1} if written else {},
             compiler_params=pltpu.CompilerParams(vmem_limit_bytes=24 * 1024 * 1024),

time: 111 us -> 127 us (1.14)
  waiting for transfers between devices: 39.1 us -> 57 us
  starting transfers between devices: 42.6 us -> 41.1 us
    ppermute x27, waiting for transfers between devices: 36.5 us -> 57 us  [swap(): return lax.ppermute(values, both, pairs)]
    all_to_all x2, waiting for transfers between devices: 2.63 us -> 0.01 us  [exchange(): lax.all_to_all(values, axes, split_axis=0, concat_axis=0, tiled=True, axi...]
    unnamed x18 -> x22, local copies, waits for them, and re-layouts: 2.74 us -> 1.84 us
  transfers between devices with their start and end apart: 29 -> 29, of which waited for: 17 -> 16; matrix products, arithmetic and copies ran while one was open for 5% -> 3% of each run, Pallas kernels for 9% -> 6%
where the time goes in v18:
time: 127 us; the launch traced here: 126 us
  waiting for transfers between devices  57 us (45%)
  starting transfers between devices  41.1 us (32%)
  Pallas kernels  21.2 us (17%)
  local copies, waits for them, and re-layouts  3.9 us (3%)
  other arithmetic  1.86 us (1%)
    ppermute x27, waiting for transfers between devices, swap(): return lax.ppermute(values, both, pairs)  57 us
    ppermute x27, starting transfers between devices, swap(): return lax.ppermute(values, both, pairs)  33.1 us
    pallas_call x1, Pallas kernels, on_device(): call(functools.partial(backward_body, plan, table_size, total_factor), ou...  8.85 us
    all_to_all x2, starting transfers between devices, exchange(): lax.all_to_all(values, axes, split_axis=0, concat_axis=0, tiled=True, axi...  7.99 us
    pallas_call x2, Pallas kernels, on_device(): pl.pallas_call(functools.partial(widen_body, plan, turn), out_shape=outs,...  4.16 us
    pallas_call x1, Pallas kernels, on_device(): call(forward_body, list(shapes.values()), [VMEM] * 3, flops=4 * count * w...  3.92 us
  transfers between devices with their start and end apart: 29, of which 16 were waited for; matrix products, arithmetic and copies ran while one was open for 3% of the time, Pallas kernels for 6%

profile of v18, /device:TPU:0, one launch (start us, length us, event | category | flops | bytes accessed | tf_op | source)
XLA Modules:
  0.0 126.2 jit_solution(6968747034556064581)
XLA Ops:
  0.7 0.8 select_reduce_fusion
  1.6 4.0 %collective-permute-start.2 = (s32[8,8]{1,0:T(8,128)S(1)}, s32[8,8]{1,0:T(8,128)S(1)}, u32[]{:S(2)}, u32[]{:S(2)}) collective-permute-start(s32[8,8]{1,0:T(8,128)S(1)} %broadcast_select_fusion), channel_id=1, source_target_pairs={{0,12},{1,13},{2,14},{3,15},{4,8},{5,9},{6,10},{7,11},{8,4},{9,5},... | collective-permute-start | bytes 776 | tf_op jit(solution)/shard_map/ppermute | solution.py:484
  5.6 0.4 collective-permute-start.1
  6.2 1.7 %constant_dynamic-update-slice_fusion.1 = bf16[512,2560]{1,0:T(8,128)(2,1)S(1)} fusion(bf16[512,2048]{1,0:T(8,128)(2,1)} %param.18), kind=kLoop, calls=%fused_computation.17 | loop fusion | bytes 4194304
  8.1 1.1 collective-permute-done.1
  9.7 2.6 %collective-permute-start.3 = (s32[8,8]{1,0:T(8,128)S(1)}, s32[8,8]{1,0:T(8,128)S(1)}, u32[]{:S(2)}, u32[]{:S(2)}) collective-permute-start(s32[8,8]{1,0:T(8,128)S(1)} %add_add_fusion), channel_id=1, source_target_pairs={{0,16},{1,17},{2,18},{3,19},{4,20},{5,21},{6,22},{7,23},{8,24},{9,... | collective-permute-start | bytes 776 | tf_op jit(solution)/shard_map/ppermute | solution.py:484
  12.3 1.0 constant_dynamic-update-slice_fusion.2.rows_ref
  13.3 0.9 collective-permute-done.3
  14.2 0.7 shard_map.147
  14.9 3.6 %collective-permute-start.4 = (bf16[64,512]{1,0:T(8,128)(2,1)S(1)}, bf16[64,512]{1,0:T(8,128)(2,1)S(1)}, u32[]{:S(2)}, u32[]{:S(2)}) collective-permute-start(bf16[64,512]{1,0:T(8,128)(2,1)S(1)} %get-tuple-element.72), channel_id=1, source_target_pairs={{0,28},{1,13},{2,30},{3,15},{4,24},{5,9},{6,26},{7,11},{8,20},{9,5... | collective-permute-start | bytes 196616 | tf_op jit(solution)/shard_map/ppermute | solution.py:484
  18.7 1.4 %shard_map.146 = (bf16[256,2560]{1,0:T(8,128)(2,1)S(1)}, bf16[512,256]{1,0:T(8,128)(2,1)S(1)}, bf16[256,2048]{1,0:T(8,128)(2,1)S(1)}, f32[256,512]{1,0:T(8,128)S...) custom-call(bf16[512,512]{1,0:T(8,128)(2,1)S(1)} %constant_dynamic-update-slice_fusion.2.rows_ref, ...), custom_call_target="tpu_custom_call" | custom-call | flops 536870912 | bytes 4000000 | tf_op jit(solution)/shard_map/pallas_call | solution.py:515
  20.1 1.9 %collective-permute-start.6 = (bf16[64,512]{1,0:T(8,128)(2,1)S(1)}, bf16[64,512]{1,0:T(8,128)(2,1)S(1)}, u32[]{:S(2)}, u32[]{:S(2)}) collective-permute-start(bf16[64,512]{1,0:T(8,128)(2,1)S(1)} %get-tuple-element.74), channel_id=1, source_target_pairs={{0,20},{1,5},{2,22},{3,7},{4,16},{5,1},{6,18},{7,3},{8,28},{9,13},... | collective-permute-start | bytes 196616 | tf_op jit(solution)/shard_map/ppermute | solution.py:484
  22.0 2.1 %collective-permute-start.7 = (bf16[64,512]{1,0:T(8,128)(2,1)S(1)}, bf16[64,512]{1,0:T(8,128)(2,1)S(1)}, u32[]{:S(2)}, u32[]{:S(2)}) collective-permute-start(bf16[64,512]{1,0:T(8,128)(2,1)S(1)} %get-tuple-element.75), channel_id=1, source_target_pairs={{0,16},{1,29},{2,18},{3,31},{4,20},{5,25},{6,22},{7,27},{8,24},{9,... | collective-permute-start | bytes 196616 | tf_op jit(solution)/shard_map/ppermute | solution.py:484
  24.2 1.3 %collective-permute-start.8 = (bf16[64,512]{1,0:T(8,128)(2,1)S(1)}, bf16[64,512]{1,0:T(8,128)(2,1)S(1)}, u32[]{:S(2)}, u32[]{:S(2)}) collective-permute-start(bf16[64,512]{1,0:T(8,128)(2,1)S(1)} %get-tuple-element.76), channel_id=1, source_target_pairs={{0,12},{1,25},{2,14},{3,27},{4,8},{5,29},{6,10},{7,31},{8,4},{9,17... | collective-permute-start | bytes 196616 | tf_op jit(solution)/shard_map/ppermute | solution.py:484
  25.5 0.6 collective-permute-start.9
  26.0 1.6 %collective-permute-start.10 = (bf16[64,512]{1,0:T(8,128)(2,1)S(1)}, bf16[64,512]{1,0:T(8,128)(2,1)S(1)}, u32[]{:S(2)}, u32[]{:S(2)}) collective-permute-start(bf16[64,512]{1,0:T(8,128)(2,1)S(1)} %get-tuple-element.78), channel_id=1, source_target_pairs={{0,4},{1,17},{2,6},{3,19},{4,0},{5,21},{6,2},{7,23},{8,12},{9,25},... | collective-permute-start | bytes 196616 | tf_op jit(solution)/shard_map/ppermute | solution.py:484
  27.7 3.9 %shard_map.148 = (f32[512,512]{1,0:T(8,128)S(1)}, f32[512,512]{1,0:T(8,128)S(1)}, f32[512,1]{1,0:T(8,128)S(1)}, bf16[512,1536]{1,0:T(8,128)(2,1)S(1)}, bf16[16,1...) custom-call(bf16[256,2560]{1,0:T(8,128)(2,1)S(1)} %get-tuple-element, ...), custom_call_target="tpu_custom_call" | custom-call | flops 2684354560 | bytes 8000000 | tf_op jit(solution)/shard_map/pallas_call | solution.py:525
  31.7 8.9 %shard_map.149 = (bf16[512,640]{1,0:T(8,128)(2,1)}, bf16[16,16,1536]{2,1,0:T(8,128)(2,1)S(1)}, bf16[16,16,1536]{2,1,0:T(8,128)(2,1)S(1)}, bf16[16,16,1024]{2,1,0:T(8,128)(2,1)S(1)}, bf16[16,16,1024]{2,1,0:T(8,128)(2,1)S(1)}) custom-call(s32[1]{0:T(128)} %bitcast.me_ref, s32[8]{0:T(128)S(1)} %copy-done, s32[8]{0:T(128)S(1)} %copy-done.1, ...), custom_call_target="tpu_custom_call" | custom-call | flops 10737418240 | bytes 12000000 | tf_op jit(solution)/shard_map/pallas_call | solution.py:538
  40.5 0.5 collective-permute-start.11
  41.0 1.4 %collective-permute-done.12 = bf16[16,16,1024]{2,1,0:T(8,128)(2,1)S(1)} collective-permute-done((bf16[16,16,1024]{2,1,0:T(8,128)(2,1)S(1)}, bf16[16,16,1024]{2,1,0:T(8,128)(2,1)S(1)}, u32[]{:S(2)}, u32[]{:S(2)}) %collective-permute-start.12) | collective-permute-done | bytes 524320 | tf_op jit(solution)/shard_map/ppermute | solution.py:484
  42.6 0.9 collective-permute-done.11
  43.8 1.4 %collective-permute-start.15 = (bf16[8,16,1024]{2,1,0:T(8,128)(2,1)S(1)}, bf16[8,16,1024]{2,1,0:T(8,128)(2,1)S(1)}, u32[]{:S(2)}, u32[]{:S(2)}) collective-permute-start(bf16[8,16,1024]{2,1,0:T(8,128)(2,1)S(1)} %slice.47), channel_id=1, source_target_pairs={{0,4},{1,5},{2,6},{3,7},{4,0},{5,1},{6,2},{7,3},{8,12},{9,13},{10,... | collective-permute-start | bytes 786440 | tf_op jit(solution)/shard_map/ppermute | solution.py:484
  45.3 1.6 %collective-permute-start.13 = (bf16[8,16,1536]{2,1,0:T(8,128)(2,1)S(1)}, bf16[8,16,1536]{2,1,0:T(8,128)(2,1)S(1)}, u32[]{:S(2)}, u32[]{:S(2)}) collective-permute-start(bf16[8,16,1536]{2,1,0:T(8,128)(2,1)S(1)} %slice.43), channel_id=1, source_target_pairs={{0,2},{1,3},{2,0},{3,1},{4,6},{5,7},{6,4},{7,5},{8,10},{9,11},{10,... | collective-permute-start | bytes 1179656 | tf_op jit(solution)/shard_map/ppermute | solution.py:484
  46.9 4.5 %all-to-all-start = ((bf16[4,8,16,640]{3,2,1,0:T(8,128)(2,1)}), bf16[4,8,16,640]{3,2,1,0:T(8,128)(2,1)S(1)}, u32[]{:S(2)}, u32[]{:S(2)}) async-start(bf16[4,8,16,640]{3,2,1,0:T(8,128)(2,1)} %bitcast.5), calls=%async_computation | async-start | bytes 1310720 | tf_op jit(solution)/shard_map/all_to_all | solution.py:487
  51.3 0.9 collective-permute-done.15
  52.3 1.6 %collective-permute-start.16 = (bf16[4,16,1024]{2,1,0:T(8,128)(2,1)S(1)}, bf16[4,16,1024]{2,1,0:T(8,128)(2,1)S(1)}, u32[]{:S(2)}, u32[]{:S(2)}) collective-permute-start(bf16[4,16,1024]{2,1,0:T(8,128)(2,1)S(1)} %slice.59), channel_id=1, source_target_pairs={{0,2},{1,3},{2,0},{3,1},{4,6},{5,7},{6,4},{7,5},{8,10},{9,11},{10,... | collective-permute-start | bytes 393224 | tf_op jit(solution)/shard_map/ppermute | solution.py:484
  53.9 3.4 %collective-permute-done.13 = bf16[8,16,1536]{2,1,0:T(8,128)(2,1)S(1)} collective-permute-done((bf16[8,16,1536]{2,1,0:T(8,128)(2,1)S(1)}, bf16[8,16,1536]{2,1,0:T(8,128)(2,1)S(1)}, u32[]{:S(2)}, u32[]{:S(2)}) %collective-permute-start.13) | collective-permute-done | bytes 393248 | tf_op jit(solution)/shard_map/ppermute | solution.py:484
  57.5 0.7 collective-permute-start.14
  58.2 0.8 collective-permute-done.16
  59.1 4.1 %collective-permute-done.14 = bf16[4,16,1536]{2,1,0:T(8,128)(2,1)S(1)} collective-permute-done((bf16[4,16,1536]{2,1,0:T(8,128)(2,1)S(1)}, bf16[4,16,1536]{2,1,0:T(8,128)(2,1)S(1)}, u32[]{:S(2)}, u32[]{:S(2)}) %collective-permute-start.14) | collective-permute-done | bytes 196640 | tf_op jit(solution)/shard_map/ppermute | solution.py:484
  63.3 0.6 collective-permute-start.17
  63.9 6.2 %collective-permute-done.17 = bf16[2,16,2560]{2,1,0:T(8,128)(2,1)S(1)} collective-permute-done((bf16[2,16,2560]{2,1,0:T(8,128)(2,1)S(1)}, bf16[2,16,2560]{2,1,0:T(8,128)(2,1)S(1)}, u32[]{:S(2)}, u32[]{:S(2)}) %collective-permute-start.17) | collective-permute-done | bytes 163872 | tf_op jit(solution)/shard_map/ppermute | solution.py:484
  70.2 0.5 collective-permute-start.18
  70.7 5.5 %collective-permute-done.18 = bf16[1,16,2560]{2,1,0:T(8,128)(2,1)S(1)} collective-permute-done((bf16[1,16,2560]{2,1,0:T(8,128)(2,1)S(1)}, bf16[1,16,2560]{2,1,0:T(8,128)(2,1)S(1)}, u32[]{:S(2)}, u32[]{:S(2)}) %collective-permute-start.18) | collective-permute-done | bytes 81952 | tf_op jit(solution)/shard_map/ppermute | solution.py:484
  76.2 5.4 %collective-permute-done.19 = bf16[1,16,2560]{2,1,0:T(8,128)(2,1)S(1)} collective-permute-done((bf16[1,16,2560]{2,1,0:T(8,128)(2,1)S(1)}, bf16[1,16,2560]{2,1,0:T(8,128)(2,1)S(1)}, u32[]{:S(2)}, u32[]{:S(2)}) %collective-permute-start.19) | collective-permute-done | bytes 81952 | tf_op jit(solution)/shard_map/ppermute | solution.py:484
  81.8 5.3 %collective-permute-done.20 = bf16[2,16,2560]{2,1,0:T(8,128)(2,1)S(1)} collective-permute-done((bf16[2,16,2560]{2,1,0:T(8,128)(2,1)S(1)}, bf16[2,16,2560]{2,1,0:T(8,128)(2,1)S(1)}, u32[]{:S(2)}, u32[]{:S(2)}) %collective-permute-start.20) | collective-permute-done | bytes 163872 | tf_op jit(solution)/shard_map/ppermute | solution.py:484
  87.2 2.9 %collective-permute-start.22 = (bf16[4,16,1280]{2,1,0:T(8,128)(2,1)S(1)}, bf16[4,16,1280]{2,1,0:T(8,128)(2,1)S(1)}, u32[]{:S(2)}, u32[]{:S(2)}) collective-permute-start(bf16[4,16,1280]{2,1,0:T(8,128)(2,1)S(1)} %get-tuple-element.99), channel_id=1, source_target_pairs={{0,2},{1,3},{2,0},{3,1},{4,6},{5,7},{6,4},{7,5},{8,10},{9,11},{10,... | collective-permute-start | bytes 491528 | tf_op jit(solution)/shard_map/ppermute | solution.py:484
  90.1 0.9 copy.20
  91.0 3.5 %all-to-all-start.1 = ((bf16[8,4,16,640]{3,2,1,0:T(8,128)(2,1)}), bf16[8,4,16,640]{3,2,1,0:T(8,128)(2,1)S(1)}, u32[]{:S(2)}, u32[]{:S(2)}) async-start(bf16[8,4,16,640]{3,2,1,0:T(8,128)(2,1)} %copy.20), calls=%async_computation.1 | async-start | bytes 1310720 | tf_op jit(solution)/shard_map/all_to_all | solution.py:487
  94.5 1.9 %collective-permute-start.21 = (bf16[4,16,1280]{2,1,0:T(8,128)(2,1)S(1)}, bf16[4,16,1280]{2,1,0:T(8,128)(2,1)S(1)}, u32[]{:S(2)}, u32[]{:S(2)}) collective-permute-start(bf16[4,16,1280]{2,1,0:T(8,128)(2,1)S(1)} %get-tuple-element.100), channel_id=1, source_target_pairs={{0,4},{1,5},{2,6},{3,7},{4,0},{5,1},{6,2},{7,3},{8,12},{9,13},{10,... | collective-permute-start | bytes 491528 | tf_op jit(solution)/shard_map/ppermute | solution.py:484
  96.5 11.7 %collective-permute-done.21 = bf16[4,16,1280]{2,1,0:T(8,128)(2,1)S(1)} collective-permute-done((bf16[4,16,1280]{2,1,0:T(8,128)(2,1)S(1)}, bf16[4,16,1280]{2,1,0:T(8,128)(2,1)S(1)}, u32[]{:S(2)}, u32[]{:S(2)}) %collective-permute-start.21) | collective-permute-done | bytes 163872 | tf_op jit(solution)/shard_map/ppermute | solution.py:484
  108.3 2.2 %shard_map.150 = (f32[1024,512]{1,0:T(8,128)}, f32[1,512]{1,0:T(1,128)}, f32[1,512]{1,0:T(1,128)}) custom-call(bf16[512,640]{1,0:T(8,128)(2,1)S(1)} %bitcast.10), custom_call_target="tpu_custom_call" | custom-call | tf_op jit(solution)/shard_map/pallas_call | solution.py:584
  110.4 1.5 %collective-permute-start.23 = (bf16[8,16,1280]{2,1,0:T(8,128)(2,1)S(1)}, bf16[8,16,1280]{2,1,0:T(8,128)(2,1)S(1)}, u32[]{:S(2)}, u32[]{:S(2)}) collective-permute-start(bf16[8,16,1280]{2,1,0:T(8,128)(2,1)S(1)} %pad_maximum_fusion.1), channel_id=1, source_target_pairs={{0,2},{1,3},{2,0},{3,1},{4,6},{5,7},{6,4},{7,5},{8,10},{9,11},{10,... | collective-permute-start | bytes 983048 | tf_op jit(solution)/shard_map/ppermute | solution.py:484
  111.9 0.5 collective-permute-start.25
  112.5 8.4 %collective-permute-done.25 = bf16[8,16,1280]{2,1,0:T(8,128)(2,1)S(1)} collective-permute-done((bf16[8,16,1280]{2,1,0:T(8,128)(2,1)S(1)}, bf16[8,16,1280]{2,1,0:T(8,128)(2,1)S(1)}, u32[]{:S(2)}, u32[]{:S(2)}) %collective-permute-start.25) | collective-permute-done | bytes 327712 | tf_op jit(solution)/shard_map/ppermute | solution.py:484
  121.0 0.5 collective-permute-start.24
  121.6 2.1 %shard_map.151 = (f32[512,2048]{1,0:T(8,128)}, f32[512,512]{1,0:T(8,128)}) custom-call(s32[1]{0:T(128)} %bitcast.me_ref, bf16[16,16,1280]{2,1,0:T(8,128)(2,1)S(1)} %constant_dynamic-update-slice_fusion.4.left_ref, bf16[16,16,1280]{2,1,0:T(8,128)(2,1)S(1)} %constant_dynamic-update-slice_fusion.6.right_ref), custom_call_target="tpu_custom_call" | custom-call | bytes 4000000 | tf_op jit(solution)/shard_map/pallas_call | solution.py:605
  124.0 2.1 %shard_map.152 = (f32[512,2048]{1,0:T(8,128)}, f32[512,512]{1,0:T(8,128)}) custom-call(s32[1]{0:T(128)} %bitcast.me_ref, bf16[16,16,1280]{2,1,0:T(8,128)(2,1)S(1)} %collective-permute-done.24.left_ref, bf16[16,16,1280]{2,1,0:T(8,128)(2,1)S(1)} %collective-permute-done.26.right_ref, ...), custom_call_target="tpu_custom_call", output_to_operand_aliasing={{0}: (3, {}), {1}: (4, {})} | custom-call | bytes 4000000 | tf_op jit(solution)/shard_map/pallas_call | solution.py:605
  (70 shorter events, 2.7 us)
Async XLA Ops:
  0.6 7.4 %copy-start.4 = (f32[512]{0:T(512)S(1)}, f32[512]{0:T(512)}, u32[]{:S(2)}) copy-start(f32[512]{0:T(512)} %param.21) | copy-start | bytes 6148
  0.6 7.4 %copy-start.5 = (f32[512]{0:T(512)S(1)}, f32[512]{0:T(512)}, u32[]{:S(2)}) copy-start(f32[512]{0:T(512)} %param.20) | copy-start | bytes 6148
  0.7 7.4 %copy-start.2 = (bf16[512,512]{1,0:T(8,128)(2,1)S(1)}, bf16[512,512]{1,0:T(8,128)(2,1)}, u32[]{:S(2)}) copy-start(bf16[512,512]{1,0:T(8,128)(2,1)} %param.19) | copy-start | bytes 1572868
  1.6 10.8 %copy-start.3 = (bf16[256,512]{1,0:T(8,128)(2,1)S(1)}, bf16[256,512]{1,0:T(8,128)(2,1)}, u32[]{:S(2)}) copy-start(bf16[256,512]{1,0:T(8,128)(2,1)} %param.11) | copy-start | bytes 786436
  1.6 17.1 %copy-start.6 = (s32[512]{0:T(512)S(1)}, s32[512]{0:T(512)}, u32[]{:S(2)}) copy-start(s32[512]{0:T(512)} %param.12) | copy-start | bytes 6148
  1.6 17.1 %copy-start.7 = (s32[256]{0:T(256)S(1)}, s32[256]{0:T(256)}, u32[]{:S(2)}) copy-start(s32[256]{0:T(256)} %param.14) | copy-start | bytes 3076
  1.6 17.1 %copy-start.8 = (s32[256,1]{0,1:T(1,128)S(1)}, s32[256,1]{0,1:T(1,128)}, u32[]{:S(2)}) copy-start(s32[256,1]{0,1:T(1,128)} %param.13) | copy-start | bytes 3076
  1.6 6.5 %collective-permute-start.2 = (s32[8,8]{1,0:T(8,128)S(1)}, s32[8,8]{1,0:T(8,128)S(1)}, u32[]{:S(2)}, u32[]{:S(2)}) collective-permute-start(s32[8,8]{1,0:T(8,128)S(1)} %broadcast_select_fusion), channel_id=1, source_target_pairs={{0,12},{1,13},{2,14},{3,15},{4,8},{5,9},{6,10},{7,11},{8,4},{9,5},... | collective-permute-start | bytes 776 | tf_op jit(solution)/shard_map/ppermute | solution.py:484
  5.6 3.6 %collective-permute-start.1 = (s32[8,8]{1,0:T(8,128)S(1)}, s32[8,8]{1,0:T(8,128)S(1)}, u32[]{:S(2)}, u32[]{:S(2)}) collective-permute-start(s32[8,8]{1,0:T(8,128)S(1)} %broadcast_select_fusion), channel_id=1, source_target_pairs={{0,8},{1,9},{2,10},{3,11},{4,12},{5,13},{6,14},{7,15},{8,0},{9,1},... | collective-permute-start | bytes 776 | tf_op jit(solution)/shard_map/ppermute | solution.py:484
  6.0 3.6 %collective-permute-start = (s32[8,8]{1,0:T(8,128)S(1)}, s32[8,8]{1,0:T(8,128)S(1)}, u32[]{:S(2)}, u32[]{:S(2)}) collective-permute-start(s32[8,8]{1,0:T(8,128)S(1)} %broadcast_select_fusion), channel_id=1, source_target_pairs={{0,4},{1,5},{2,6},{3,7},{4,0},{5,1},{6,2},{7,3},{8,12},{9,13},{10,... | collective-permute-start | bytes 776 | tf_op jit(solution)/shard_map/ppermute | solution.py:484
  9.7 4.5 %collective-permute-start.3 = (s32[8,8]{1,0:T(8,128)S(1)}, s32[8,8]{1,0:T(8,128)S(1)}, u32[]{:S(2)}, u32[]{:S(2)}) collective-permute-start(s32[8,8]{1,0:T(8,128)S(1)} %add_add_fusion), channel_id=1, source_target_pairs={{0,16},{1,17},{2,18},{3,19},{4,20},{5,21},{6,22},{7,23},{8,24},{9,... | collective-permute-start | bytes 776 | tf_op jit(solution)/shard_map/ppermute | solution.py:484
  14.9 10.5 %collective-permute-start.4 = (bf16[64,512]{1,0:T(8,128)(2,1)S(1)}, bf16[64,512]{1,0:T(8,128)(2,1)S(1)}, u32[]{:S(2)}, u32[]{:S(2)}) collective-permute-start(bf16[64,512]{1,0:T(8,128)(2,1)S(1)} %get-tuple-element.72), channel_id=1, source_target_pairs={{0,28},{1,13},{2,30},{3,15},{4,24},{5,9},{6,26},{7,11},{8,20},{9,5... | collective-permute-start | bytes 196616 | tf_op jit(solution)/shard_map/ppermute | solution.py:484
  18.6 7.5 %collective-permute-start.5 = (bf16[64,512]{1,0:T(8,128)(2,1)S(1)}, bf16[64,512]{1,0:T(8,128)(2,1)S(1)}, u32[]{:S(2)}, u32[]{:S(2)}) collective-permute-start(bf16[64,512]{1,0:T(8,128)(2,1)S(1)} %get-tuple-element.73), channel_id=1, source_target_pairs={{0,24},{1,9},{2,26},{3,11},{4,28},{5,13},{6,30},{7,15},{8,16},{9,1... | collective-permute-start | bytes 196616 | tf_op jit(solution)/shard_map/ppermute | solution.py:484
  20.1 11.5 %collective-permute-start.6 = (bf16[64,512]{1,0:T(8,128)(2,1)S(1)}, bf16[64,512]{1,0:T(8,128)(2,1)S(1)}, u32[]{:S(2)}, u32[]{:S(2)}) collective-permute-start(bf16[64,512]{1,0:T(8,128)(2,1)S(1)} %get-tuple-element.74), channel_id=1, source_target_pairs={{0,20},{1,5},{2,22},{3,7},{4,16},{5,1},{6,18},{7,3},{8,28},{9,13},... | collective-permute-start | bytes 196616 | tf_op jit(solution)/shard_map/ppermute | solution.py:484
  22.0 9.6 %collective-permute-start.7 = (bf16[64,512]{1,0:T(8,128)(2,1)S(1)}, bf16[64,512]{1,0:T(8,128)(2,1)S(1)}, u32[]{:S(2)}, u32[]{:S(2)}) collective-permute-start(bf16[64,512]{1,0:T(8,128)(2,1)S(1)} %get-tuple-element.75), channel_id=1, source_target_pairs={{0,16},{1,29},{2,18},{3,31},{4,20},{5,25},{6,22},{7,27},{8,24},{9,... | collective-permute-start | bytes 196616 | tf_op jit(solution)/shard_map/ppermute | solution.py:484
  24.2 7.4 %collective-permute-start.8 = (bf16[64,512]{1,0:T(8,128)(2,1)S(1)}, bf16[64,512]{1,0:T(8,128)(2,1)S(1)}, u32[]{:S(2)}, u32[]{:S(2)}) collective-permute-start(bf16[64,512]{1,0:T(8,128)(2,1)S(1)} %get-tuple-element.76), channel_id=1, source_target_pairs={{0,12},{1,25},{2,14},{3,27},{4,8},{5,29},{6,10},{7,31},{8,4},{9,17... | collective-permute-start | bytes 196616 | tf_op jit(solution)/shard_map/ppermute | solution.py:484
  25.5 6.1 %collective-permute-start.9 = (bf16[64,512]{1,0:T(8,128)(2,1)S(1)}, bf16[64,512]{1,0:T(8,128)(2,1)S(1)}, u32[]{:S(2)}, u32[]{:S(2)}) collective-permute-start(bf16[64,512]{1,0:T(8,128)(2,1)S(1)} %get-tuple-element.77), channel_id=1, source_target_pairs={{0,8},{1,21},{2,10},{3,23},{4,12},{5,17},{6,14},{7,19},{8,0},{9,29... | collective-permute-start | bytes 196616 | tf_op jit(solution)/shard_map/ppermute | solution.py:484
  26.0 5.6 %collective-permute-start.10 = (bf16[64,512]{1,0:T(8,128)(2,1)S(1)}, bf16[64,512]{1,0:T(8,128)(2,1)S(1)}, u32[]{:S(2)}, u32[]{:S(2)}) collective-permute-start(bf16[64,512]{1,0:T(8,128)(2,1)S(1)} %get-tuple-element.78), channel_id=1, source_target_pairs={{0,4},{1,17},{2,6},{3,19},{4,0},{5,21},{6,2},{7,23},{8,12},{9,25},... | collective-permute-start | bytes 196616 | tf_op jit(solution)/shard_map/ppermute | solution.py:484
  27.7 4.0 %copy-start = (s32[8]{0:T(128)S(1)}, s32[8]{0:T(128)}, u32[]{:S(2)}) copy-start(s32[8]{0:T(128)} %dest_ref.1) | copy-start | bytes 100
  27.7 4.0 %copy-start.1 = (s32[8]{0:T(128)S(1)}, s32[8]{0:T(128)}, u32[]{:S(2)}) copy-start(s32[8]{0:T(128)} %blocks_ref.1) | copy-start | bytes 100
  40.5 1.9 %collective-permute-start.12 = (bf16[16,16,1024]{2,1,0:T(8,128)(2,1)S(1)}, bf16[16,16,1024]{2,1,0:T(8,128)(2,1)S(1)}, u32[]{:S(2)}, u32[]{:S(2)}) collective-permute-start(bf16[16,16,1024]{2,1,0:T(8,128)(2,1)S(1)} %get-tuple-element.82), channel_id=1, source_target_pairs={{0,1},{1,0},{2,3},{3,2},{4,5},{5,4},{6,7},{7,6},{8,9},{9,8},{10,11... | collective-permute-start | bytes 1572872 | tf_op jit(solution)/shard_map/ppermute | solution.py:484
  40.5 3.0 %collective-permute-start.11 = (bf16[16,16,1536]{2,1,0:T(8,128)(2,1)S(1)}, bf16[16,16,1536]{2,1,0:T(8,128)(2,1)S(1)}, u32[]{:S(2)}, u32[]{:S(2)}) collective-permute-start(bf16[16,16,1536]{2,1,0:T(8,128)(2,1)S(1)} %get-tuple-element.80), channel_id=1, source_target_pairs={{0,1},{1,0},{2,3},{3,2},{4,5},{5,4},{6,7},{7,6},{8,9},{9,8},{10,11... | collective-permute-start | bytes 2359304 | tf_op jit(solution)/shard_map/ppermute | solution.py:484
  43.8 8.4 %collective-permute-start.15 = (bf16[8,16,1024]{2,1,0:T(8,128)(2,1)S(1)}, bf16[8,16,1024]{2,1,0:T(8,128)(2,1)S(1)}, u32[]{:S(2)}, u32[]{:S(2)}) collective-permute-start(bf16[8,16,1024]{2,1,0:T(8,128)(2,1)S(1)} %slice.47), channel_id=1, source_target_pairs={{0,4},{1,5},{2,6},{3,7},{4,0},{5,1},{6,2},{7,3},{8,12},{9,13},{10,... | collective-permute-start | bytes 786440 | tf_op jit(solution)/shard_map/ppermute | solution.py:484
  45.3 12.1 %collective-permute-start.13 = (bf16[8,16,1536]{2,1,0:T(8,128)(2,1)S(1)}, bf16[8,16,1536]{2,1,0:T(8,128)(2,1)S(1)}, u32[]{:S(2)}, u32[]{:S(2)}) collective-permute-start(bf16[8,16,1536]{2,1,0:T(8,128)(2,1)S(1)} %slice.43), channel_id=1, source_target_pairs={{0,2},{1,3},{2,0},{3,1},{4,6},{5,7},{6,4},{7,5},{8,10},{9,11},{10,... | collective-permute-start | bytes 1179656 | tf_op jit(solution)/shard_map/ppermute | solution.py:484
  46.9 23.3 %all-to-all-start = ((bf16[4,8,16,640]{3,2,1,0:T(8,128)(2,1)}), bf16[4,8,16,640]{3,2,1,0:T(8,128)(2,1)S(1)}, u32[]{:S(2)}, u32[]{:S(2)}) async-start(bf16[4,8,16,640]{3,2,1,0:T(8,128)(2,1)} %bitcast.5), calls=%async_computation | async-start | bytes 1310720 | tf_op jit(solution)/shard_map/all_to_all | solution.py:487
  52.3 6.7 %collective-permute-start.16 = (bf16[4,16,1024]{2,1,0:T(8,128)(2,1)S(1)}, bf16[4,16,1024]{2,1,0:T(8,128)(2,1)S(1)}, u32[]{:S(2)}, u32[]{:S(2)}) collective-permute-start(bf16[4,16,1024]{2,1,0:T(8,128)(2,1)S(1)} %slice.59), channel_id=1, source_target_pairs={{0,2},{1,3},{2,0},{3,1},{4,6},{5,7},{6,4},{7,5},{8,10},{9,11},{10,... | collective-permute-start | bytes 393224 | tf_op jit(solution)/shard_map/ppermute | solution.py:484
  57.5 5.7 %collective-permute-start.14 = (bf16[4,16,1536]{2,1,0:T(8,128)(2,1)S(1)}, bf16[4,16,1536]{2,1,0:T(8,128)(2,1)S(1)}, u32[]{:S(2)}, u32[]{:S(2)}) collective-permute-start(bf16[4,16,1536]{2,1,0:T(8,128)(2,1)S(1)} %slice.57), channel_id=1, source_target_pairs={{0,4},{1,5},{2,6},{3,7},{4,0},{5,1},{6,2},{7,3},{8,12},{9,13},{10,... | collective-permute-start | bytes 589832 | tf_op jit(solution)/shard_map/ppermute | solution.py:484
  63.3 6.8 %collective-permute-start.17 = (bf16[2,16,2560]{2,1,0:T(8,128)(2,1)S(1)}, bf16[2,16,2560]{2,1,0:T(8,128)(2,1)S(1)}, u32[]{:S(2)}, u32[]{:S(2)}) collective-permute-start(bf16[2,16,2560]{2,1,0:T(8,128)(2,1)S(1)} %pad_maximum_fusion.3), channel_id=1, source_target_pairs={{0,8},{1,9},{2,10},{3,11},{4,12},{5,13},{6,14},{7,15},{8,0},{9,1},... | collective-permute-start | bytes 491528 | tf_op jit(solution)/shard_map/ppermute | solution.py:484
  70.2 6.0 %collective-permute-start.18 = (bf16[1,16,2560]{2,1,0:T(8,128)(2,1)S(1)}, bf16[1,16,2560]{2,1,0:T(8,128)(2,1)S(1)}, u32[]{:S(2)}, u32[]{:S(2)}) collective-permute-start(bf16[1,16,2560]{2,1,0:T(8,128)(2,1)S(1)} %slice.53), channel_id=1, source_target_pairs={{0,16},{1,17},{2,18},{3,19},{4,20},{5,21},{6,22},{7,23},{8,24},{9,... | collective-permute-start | bytes 245768 | tf_op jit(solution)/shard_map/ppermute | solution.py:484
  76.2 5.5 %collective-permute-start.19 = (bf16[1,16,2560]{2,1,0:T(8,128)(2,1)S(1)}, bf16[1,16,2560]{2,1,0:T(8,128)(2,1)S(1)}, u32[]{:S(2)}, u32[]{:S(2)}) collective-permute-start(bf16[1,16,2560]{2,1,0:T(8,128)(2,1)S(1)} %add_convert_fusion.7), channel_id=1, source_target_pairs={{0,16},{1,17},{2,18},{3,19},{4,20},{5,21},{6,22},{7,23},{8,24},{9,... | collective-permute-start | bytes 245768 | tf_op jit(solution)/shard_map/ppermute | solution.py:484
  81.7 5.4 %collective-permute-start.20 = (bf16[2,16,2560]{2,1,0:T(8,128)(2,1)S(1)}, bf16[2,16,2560]{2,1,0:T(8,128)(2,1)S(1)}, u32[]{:S(2)}, u32[]{:S(2)}) collective-permute-start(bf16[2,16,2560]{2,1,0:T(8,128)(2,1)S(1)} %pad_maximum_fusion.4), channel_id=1, source_target_pairs={{0,8},{1,9},{2,10},{3,11},{4,12},{5,13},{6,14},{7,15},{8,0},{9,1},... | collective-permute-start | bytes 491528 | tf_op jit(solution)/shard_map/ppermute | solution.py:484
  87.2 9.3 %collective-permute-start.22 = (bf16[4,16,1280]{2,1,0:T(8,128)(2,1)S(1)}, bf16[4,16,1280]{2,1,0:T(8,128)(2,1)S(1)}, u32[]{:S(2)}, u32[]{:S(2)}) collective-permute-start(bf16[4,16,1280]{2,1,0:T(8,128)(2,1)S(1)} %get-tuple-element.99), channel_id=1, source_target_pairs={{0,2},{1,3},{2,0},{3,1},{4,6},{5,7},{6,4},{7,5},{8,10},{9,11},{10,... | collective-permute-start | bytes 491528 | tf_op jit(solution)/shard_map/ppermute | solution.py:484
  91.0 17.3 %all-to-all-start.1 = ((bf16[8,4,16,640]{3,2,1,0:T(8,128)(2,1)}), bf16[8,4,16,640]{3,2,1,0:T(8,128)(2,1)S(1)}, u32[]{:S(2)}, u32[]{:S(2)}) async-start(bf16[8,4,16,640]{3,2,1,0:T(8,128)(2,1)} %copy.20), calls=%async_computation.1 | async-start | bytes 1310720 | tf_op jit(solution)/shard_map/all_to_all | solution.py:487
  94.5 13.7 %collective-permute-start.21 = (bf16[4,16,1280]{2,1,0:T(8,128)(2,1)S(1)}, bf16[4,16,1280]{2,1,0:T(8,128)(2,1)S(1)}, u32[]{:S(2)}, u32[]{:S(2)}) collective-permute-start(bf16[4,16,1280]{2,1,0:T(8,128)(2,1)S(1)} %get-tuple-element.100), channel_id=1, source_target_pairs={{0,4},{1,5},{2,6},{3,7},{4,0},{5,1},{6,2},{7,3},{8,12},{9,13},{10,... | collective-permute-start | bytes 491528 | tf_op jit(solution)/shard_map/ppermute | solution.py:484
  110.4 10.6 %collective-permute-start.23 = (bf16[8,16,1280]{2,1,0:T(8,128)(2,1)S(1)}, bf16[8,16,1280]{2,1,0:T(8,128)(2,1)S(1)}, u32[]{:S(2)}, u32[]{:S(2)}) collective-permute-start(bf16[8,16,1280]{2,1,0:T(8,128)(2,1)S(1)} %pad_maximum_fusion.1), channel_id=1, source_target_pairs={{0,2},{1,3},{2,0},{3,1},{4,6},{5,7},{6,4},{7,5},{8,10},{9,11},{10,... | collective-permute-start | bytes 983048 | tf_op jit(solution)/shard_map/ppermute | solution.py:484
  111.9 9.0 %collective-permute-start.25 = (bf16[8,16,1280]{2,1,0:T(8,128)(2,1)S(1)}, bf16[8,16,1280]{2,1,0:T(8,128)(2,1)S(1)}, u32[]{:S(2)}, u32[]{:S(2)}) collective-permute-start(bf16[8,16,1280]{2,1,0:T(8,128)(2,1)S(1)} %pad_maximum_fusion.2), channel_id=1, source_target_pairs={{0,4},{1,5},{2,6},{3,7},{4,0},{5,1},{6,2},{7,3},{8,12},{9,13},{10,... | collective-permute-start | bytes 983048 | tf_op jit(solution)/shard_map/ppermute | solution.py:484
  120.9 2.8 %collective-permute-start.26 = (bf16[16,16,1280]{2,1,0:T(8,128)(2,1)S(1)}, bf16[16,16,1280]{2,1,0:T(8,128)(2,1)S(1)}, u32[]{:S(2)}, u32[]{:S(2)}) collective-permute-start(bf16[16,16,1280]{2,1,0:T(8,128)(2,1)S(1)} %constant_dynamic-update-slice_fusion.6.right_ref), channel_id=1, source_target_pairs={{0,1},{1,0},{2,3},{3,2},{4,5},{5,4},{6,7},{7,6},{8,9},{9,8},{10,11... | collective-permute-start | bytes 1966088 | tf_op jit(solution)/shard_map/ppermute | solution.py:484
  121.0 3.0 %collective-permute-start.24 = (bf16[16,16,1280]{2,1,0:T(8,128)(2,1)S(1)}, bf16[16,16,1280]{2,1,0:T(8,128)(2,1)S(1)}, u32[]{:S(2)}, u32[]{:S(2)}) collective-permute-start(bf16[16,16,1280]{2,1,0:T(8,128)(2,1)S(1)} %constant_dynamic-update-slice_fusion.4.left_ref), channel_id=1, source_target_pairs={{0,1},{1,0},{2,3},{3,2},{4,5},{5,4},{6,7},{7,6},{8,9},{9,8},{10,11... | collective-permute-start | bytes 1966088 | tf_op jit(solution)/shard_map/ppermute | solution.py:484

commit v19 on v17

--- a/solution.py
+++ b/solution.py
@@ -361,7 +361,7 @@
         self.wide = -(-5 * width // block) * LANES
         self.gain_lanes = 2 * width // self.capacity
         self.extra = -(-(GAIN_AT + self.gain_lanes) // LANES) * LANES
-        first = -(-3 * self.wide // (5 * LANES)) * LANES
+        first = -(-13 * self.wide // (20 * LANES)) * LANES
         self.split = -(-self.wide // (2 * LANES)) * LANES
         self.sides = ((0, first), (first, self.wide - first))
         self.halves = ((0, self.split), (self.split, self.wide - self.split))
@@ -493,6 +493,16 @@
             lengths, touched_rows = lax.optimization_barrier((lengths, touched_rows))
     rows = jnp.concatenate([touched_rows, grad_out])
     weights = jnp.concatenate([w_in, w_out], axis=1)
+    shapes = row_shapes(count, width)
+    made = call(
+        functools.partial(rows_body, plan.capacity),
+        list(shapes.values()),
+        [VMEM] * 4,
+        flops=8 * count * width * width,
+        moved=4_000_000,
+    )(rows, weights, gain_rows, ints)
+    saved = dict(zip(shapes, made), weights=weights)
+    lengths, saved["rows_active"] = lax.optimization_barrier((lengths, saved["rows_active"]))
     send = call(
         functools.partial(send_body, table_size, count),
         [shape_of((SLOT, width), BF16)] * dp_size,
@@ -503,15 +513,6 @@
     orders = slot_orders(dp_size)
     for turn in range(1, dp_size):
         got[turn] = swap(send[turn], *(order[turn] * table_size for order in orders))
-    shapes = row_shapes(count, width)
-    made = call(
-        functools.partial(rows_body, plan.capacity),
-        list(shapes.values()),
-        [VMEM] * 4,
-        flops=8 * count * width * width,
-        moved=4_000_000,
-    )(rows, weights, gain_rows, ints)
-    saved = dict(zip(shapes, made), weights=weights)
     got[0], after = lax.optimization_barrier((got[0], ints))
     shapes = token_shapes(tokens, width)
     made = call(

time: 111 us -> 112 us (level)
  waiting for transfers between devices: 39.1 us -> 40.9 us
    ppermute x27, waiting for transfers between devices: 36.5 us -> 38.3 us  [swap(): return lax.ppermute(values, both, pairs)]
    ppermute x27, starting transfers between devices: 34 us -> 35.2 us  [swap(): return lax.ppermute(values, both, pairs)]
    unnamed x18 -> x20, local copies, waits for them, and re-layouts: 2.74 us -> 1.8 us
  transfers between devices with their start and end apart: 29 -> 29, of which waited for: 17 -> 19; matrix products, arithmetic and copies ran while one was open for 5% -> 4% of each run, Pallas kernels for 9% -> 8%
where the time goes in v19:
time: 112 us
  starting transfers between devices  42.8 us (38%)
  waiting for transfers between devices  40.9 us (37%)
  Pallas kernels  20.9 us (19%)
  local copies, waits for them, and re-layouts  3.82 us (3%)
  other arithmetic  1.87 us (2%)
  between operations  1.19 us (1%)
    ppermute x27, waiting for transfers between devices, swap(): return lax.ppermute(values, both, pairs)  38.3 us
    ppermute x27, starting transfers between devices, swap(): return lax.ppermute(values, both, pairs)  35.2 us
    pallas_call x1, Pallas kernels, on_device(): call(functools.partial(backward_body, plan, table_size, total_factor), ou...  8.81 us
    all_to_all x2, starting transfers between devices, exchange(): lax.all_to_all(values, axes, split_axis=0, concat_axis=0, tiled=True, axi...  7.6 us
    pallas_call x2, Pallas kernels, on_device(): pl.pallas_call(functools.partial(widen_body, plan, turn), out_shape=outs,...  3.93 us
    pallas_call x1, Pallas kernels, on_device(): call(forward_body, list(shapes.values()), [VMEM] * 3, flops=4 * count * w...  3.91 us
    all_to_all x2, waiting for transfers between devices, exchange(): lax.all_to_all(values, axes, split_axis=0, concat_axis=0, tiled=True, axi...  2.63 us
  transfers between devices with their start and end apart: 29, of which 19 were waited for; matrix products, arithmetic and copies ran while one was open for 4% of the time, Pallas kernels for 8%

profile of v19, /device:TPU:0, one launch (start us, length us, event | category | flops | bytes accessed | tf_op | source)
XLA Modules:
  0.0 111.6 jit_solution(18445922490227108454)
XLA Ops:
  0.7 0.8 select_reduce_fusion
  1.6 4.0 %collective-permute-start.2 = (s32[8,8]{1,0:T(8,128)S(1)}, s32[8,8]{1,0:T(8,128)S(1)}, u32[]{:S(2)}, u32[]{:S(2)}) collective-permute-start(s32[8,8]{1,0:T(8,128)S(1)} %broadcast_select_fusion), channel_id=1, source_target_pairs={{0,12},{1,13},{2,14},{3,15},{4,8},{5,9},{6,10},{7,11},{8,4},{9,5},... | collective-permute-start | bytes 776 | tf_op jit(solution)/shard_map/ppermute | solution.py:476
  5.6 0.4 collective-permute-start.1
  6.2 1.7 %constant_dynamic-update-slice_fusion.1 = bf16[512,2560]{1,0:T(8,128)(2,1)S(1)} fusion(bf16[512,2048]{1,0:T(8,128)(2,1)} %param.18), kind=kLoop, calls=%fused_computation.19 | loop fusion | bytes 4194304
  8.1 1.1 collective-permute-done.1
  9.2 0.4 collective-permute-done
  9.7 2.6 %collective-permute-start.3 = (s32[8,8]{1,0:T(8,128)S(1)}, s32[8,8]{1,0:T(8,128)S(1)}, u32[]{:S(2)}, u32[]{:S(2)}) collective-permute-start(s32[8,8]{1,0:T(8,128)S(1)} %add_add_fusion), channel_id=1, source_target_pairs={{0,16},{1,17},{2,18},{3,19},{4,20},{5,21},{6,22},{7,23},{8,24},{9,... | collective-permute-start | bytes 776 | tf_op jit(solution)/shard_map/ppermute | solution.py:476
  12.3 1.0 constant_dynamic-update-slice_fusion.2.rows_ref
  13.3 1.4 %shard_map.146 = (bf16[256,2560]{1,0:T(8,128)(2,1)S(1)}, bf16[512,256]{1,0:T(8,128)(2,1)S(1)}, bf16[256,2048]{1,0:T(8,128)(2,1)S(1)}, f32[256,512]{1,0:T(8,128)S...) custom-call(bf16[512,512]{1,0:T(8,128)(2,1)S(1)} %constant_dynamic-update-slice_fusion.2.rows_ref, ...), custom_call_target="tpu_custom_call" | custom-call | flops 536870912 | bytes 4000000 | tf_op jit(solution)/shard_map/pallas_call | solution.py:497
  14.8 0.7 shard_map.147
  15.5 3.1 %collective-permute-start.4 = (bf16[64,512]{1,0:T(8,128)(2,1)S(1)}, bf16[64,512]{1,0:T(8,128)(2,1)S(1)}, u32[]{:S(2)}, u32[]{:S(2)}) collective-permute-start(bf16[64,512]{1,0:T(8,128)(2,1)S(1)} %get-tuple-element.77), channel_id=1, source_target_pairs={{0,28},{1,13},{2,30},{3,15},{4,24},{5,9},{6,26},{7,11},{8,20},{9,5... | collective-permute-start | bytes 196616 | tf_op jit(solution)/shard_map/ppermute | solution.py:476
  18.6 0.8 collective-permute-start.5
  19.3 1.2 %collective-permute-start.6 = (bf16[64,512]{1,0:T(8,128)(2,1)S(1)}, bf16[64,512]{1,0:T(8,128)(2,1)S(1)}, u32[]{:S(2)}, u32[]{:S(2)}) collective-permute-start(bf16[64,512]{1,0:T(8,128)(2,1)S(1)} %get-tuple-element.79), channel_id=1, source_target_pairs={{0,20},{1,5},{2,22},{3,7},{4,16},{5,1},{6,18},{7,3},{8,28},{9,13},... | collective-permute-start | bytes 196616 | tf_op jit(solution)/shard_map/ppermute | solution.py:476
  20.5 2.7 %collective-permute-start.7 = (bf16[64,512]{1,0:T(8,128)(2,1)S(1)}, bf16[64,512]{1,0:T(8,128)(2,1)S(1)}, u32[]{:S(2)}, u32[]{:S(2)}) collective-permute-start(bf16[64,512]{1,0:T(8,128)(2,1)S(1)} %get-tuple-element.80), channel_id=1, source_target_pairs={{0,16},{1,29},{2,18},{3,31},{4,20},{5,25},{6,22},{7,27},{8,24},{9,... | collective-permute-start | bytes 196616 | tf_op jit(solution)/shard_map/ppermute | solution.py:476
  23.2 0.7 collective-permute-start.8
  23.9 3.9 %collective-permute-start.9 = (bf16[64,512]{1,0:T(8,128)(2,1)S(1)}, bf16[64,512]{1,0:T(8,128)(2,1)S(1)}, u32[]{:S(2)}, u32[]{:S(2)}) collective-permute-start(bf16[64,512]{1,0:T(8,128)(2,1)S(1)} %get-tuple-element.82), channel_id=1, source_target_pairs={{0,8},{1,21},{2,10},{3,23},{4,12},{5,17},{6,14},{7,19},{8,0},{9,29... | collective-permute-start | bytes 196616 | tf_op jit(solution)/shard_map/ppermute | solution.py:476
  27.8 3.9 %shard_map.148 = (f32[512,512]{1,0:T(8,128)S(1)}, f32[512,512]{1,0:T(8,128)S(1)}, f32[512,1]{1,0:T(8,128)S(1)}, bf16[512,1536]{1,0:T(8,128)(2,1)S(1)}, bf16[16,1...) custom-call(bf16[256,2560]{1,0:T(8,128)(2,1)S(1)} %get-tuple-element, ...), custom_call_target="tpu_custom_call" | custom-call | flops 2684354560 | bytes 8000000 | tf_op jit(solution)/shard_map/pallas_call | solution.py:518
  32.1 8.8 %shard_map.149 = (bf16[512,640]{1,0:T(8,128)(2,1)}, bf16[16,16,1664]{2,1,0:T(8,128)(2,1)S(1)}, bf16[16,16,1664]{2,1,0:T(8,128)(2,1)S(1)}, bf16[16,16,896]{2,1,0:T(8,128)(2,1)S(1)}, bf16[16,16,896]{2,1,0:T(8,128)(2,1)S(1)}) custom-call(s32[1]{0:T(128)} %bitcast.me_ref, s32[8]{0:T(128)S(1)} %copy-done, s32[8]{0:T(128)S(1)} %copy-done.1, ...), custom_call_target="tpu_custom_call" | custom-call | flops 10737418240 | bytes 12000000 | tf_op jit(solution)/shard_map/pallas_call | solution.py:531
  40.9 0.5 collective-permute-start.12
  41.4 2.5 %collective-permute-done.12 = bf16[16,16,896]{2,1,0:T(8,128)(2,1)S(1)} collective-permute-done((bf16[16,16,896]{2,1,0:T(8,128)(2,1)S(1)}, bf16[16,16,896]{2,1,0:T(8,128)(2,1)S(1)}, u32[]{:S(2)}, u32[]{:S(2)}) %collective-permute-start.12) | collective-permute-done | bytes 458784 | tf_op jit(solution)/shard_map/ppermute | solution.py:476
  44.3 1.9 %collective-permute-start.15 = (bf16[8,16,896]{2,1,0:T(8,128)(2,1)S(1)}, bf16[8,16,896]{2,1,0:T(8,128)(2,1)S(1)}, u32[]{:S(2)}, u32[]{:S(2)}) collective-permute-start(bf16[8,16,896]{2,1,0:T(8,128)(2,1)S(1)} %slice.47), channel_id=1, source_target_pairs={{0,4},{1,5},{2,6},{3,7},{4,0},{5,1},{6,2},{7,3},{8,12},{9,13},{10,... | collective-permute-start | bytes 688136 | tf_op jit(solution)/shard_map/ppermute | solution.py:476
  46.2 1.6 %collective-permute-start.13 = (bf16[8,16,1664]{2,1,0:T(8,128)(2,1)S(1)}, bf16[8,16,1664]{2,1,0:T(8,128)(2,1)S(1)}, u32[]{:S(2)}, u32[]{:S(2)}) collective-permute-start(bf16[8,16,1664]{2,1,0:T(8,128)(2,1)S(1)} %slice.43), channel_id=1, source_target_pairs={{0,2},{1,3},{2,0},{3,1},{4,6},{5,7},{6,4},{7,5},{8,10},{9,11},{10,... | collective-permute-start | bytes 1277960 | tf_op jit(solution)/shard_map/ppermute | solution.py:476
  47.8 3.7 %all-to-all-start = ((bf16[4,8,16,640]{3,2,1,0:T(8,128)(2,1)}), bf16[4,8,16,640]{3,2,1,0:T(8,128)(2,1)S(1)}, u32[]{:S(2)}, u32[]{:S(2)}) async-start(bf16[4,8,16,640]{3,2,1,0:T(8,128)(2,1)} %bitcast.5), calls=%async_computation | async-start | bytes 1310720 | tf_op jit(solution)/shard_map/all_to_all | solution.py:479
  51.5 0.6 collective-permute-done.15
  52.2 1.6 %collective-permute-start.16 = (bf16[4,16,896]{2,1,0:T(8,128)(2,1)S(1)}, bf16[4,16,896]{2,1,0:T(8,128)(2,1)S(1)}, u32[]{:S(2)}, u32[]{:S(2)}) collective-permute-start(bf16[4,16,896]{2,1,0:T(8,128)(2,1)S(1)} %slice.59), channel_id=1, source_target_pairs={{0,2},{1,3},{2,0},{3,1},{4,6},{5,7},{6,4},{7,5},{8,10},{9,11},{10,... | collective-permute-start | bytes 344072 | tf_op jit(solution)/shard_map/ppermute | solution.py:476
  53.7 5.2 %collective-permute-done.13 = bf16[8,16,1664]{2,1,0:T(8,128)(2,1)S(1)} collective-permute-done((bf16[8,16,1664]{2,1,0:T(8,128)(2,1)S(1)}, bf16[8,16,1664]{2,1,0:T(8,128)(2,1)S(1)}, u32[]{:S(2)}, u32[]{:S(2)}) %collective-permute-start.13) | collective-permute-done | bytes 426016 | tf_op jit(solution)/shard_map/ppermute | solution.py:476
  59.4 0.9 collective-permute-done.16
  60.3 4.7 %collective-permute-done.14 = bf16[4,16,1664]{2,1,0:T(8,128)(2,1)S(1)} collective-permute-done((bf16[4,16,1664]{2,1,0:T(8,128)(2,1)S(1)}, bf16[4,16,1664]{2,1,0:T(8,128)(2,1)S(1)}, u32[]{:S(2)}, u32[]{:S(2)}) %collective-permute-start.14) | collective-permute-done | bytes 213024 | tf_op jit(solution)/shard_map/ppermute | solution.py:476
  65.1 0.9 collective-permute-start.17
  66.0 4.5 %collective-permute-done.17 = bf16[2,16,2560]{2,1,0:T(8,128)(2,1)S(1)} collective-permute-done((bf16[2,16,2560]{2,1,0:T(8,128)(2,1)S(1)}, bf16[2,16,2560]{2,1,0:T(8,128)(2,1)S(1)}, u32[]{:S(2)}, u32[]{:S(2)}) %collective-permute-start.17) | collective-permute-done | bytes 163872 | tf_op jit(solution)/shard_map/ppermute | solution.py:476
  70.6 1.4 %collective-permute-start.18 = (bf16[1,16,2560]{2,1,0:T(8,128)(2,1)S(1)}, bf16[1,16,2560]{2,1,0:T(8,128)(2,1)S(1)}, u32[]{:S(2)}, u32[]{:S(2)}) collective-permute-start(bf16[1,16,2560]{2,1,0:T(8,128)(2,1)S(1)} %slice.53), channel_id=1, source_target_pairs={{0,16},{1,17},{2,18},{3,19},{4,20},{5,21},{6,22},{7,23},{8,24},{9,... | collective-permute-start | bytes 245768 | tf_op jit(solution)/shard_map/ppermute | solution.py:476
  71.9 0.9 copy.20
  72.8 3.9 %all-to-all-start.1 = ((bf16[8,4,16,640]{3,2,1,0:T(8,128)(2,1)}), bf16[8,4,16,640]{3,2,1,0:T(8,128)(2,1)S(1)}, u32[]{:S(2)}, u32[]{:S(2)}) async-start(bf16[8,4,16,640]{3,2,1,0:T(8,128)(2,1)} %copy.20), calls=%async_computation.1 | async-start | bytes 1310720 | tf_op jit(solution)/shard_map/all_to_all | solution.py:479
  76.9 1.3 %collective-permute-start.19 = (bf16[1,16,2560]{2,1,0:T(8,128)(2,1)S(1)}, bf16[1,16,2560]{2,1,0:T(8,128)(2,1)S(1)}, u32[]{:S(2)}, u32[]{:S(2)}) collective-permute-start(bf16[1,16,2560]{2,1,0:T(8,128)(2,1)S(1)} %add_convert_fusion.7), channel_id=1, source_target_pairs={{0,16},{1,17},{2,18},{3,19},{4,20},{5,21},{6,22},{7,23},{8,24},{9,... | collective-permute-start | bytes 245768 | tf_op jit(solution)/shard_map/ppermute | solution.py:476
  78.1 6.2 %collective-permute-done.19 = bf16[1,16,2560]{2,1,0:T(8,128)(2,1)S(1)} collective-permute-done((bf16[1,16,2560]{2,1,0:T(8,128)(2,1)S(1)}, bf16[1,16,2560]{2,1,0:T(8,128)(2,1)S(1)}, u32[]{:S(2)}, u32[]{:S(2)}) %collective-permute-start.19) | collective-permute-done | bytes 81952 | tf_op jit(solution)/shard_map/ppermute | solution.py:476
  84.4 2.6 %all-to-all-done.1 = bf16[8,4,16,640]{3,2,1,0:T(8,128)(2,1)S(1)} async-done(((bf16[8,4,16,640]{3,2,1,0:T(8,128)(2,1)}), bf16[8,4,16,640]{3,2,1,0:T(8,128)(2,1)S(1)}, u32[]{:S(2)}, u32[]{:S(2)}) %all-to-all-start.1) | async-done | bytes 655392 | tf_op jit(solution)/shard_map/all_to_all | solution.py:479
  87.0 0.8 collective-permute-start.20
  87.8 2.2 %shard_map.150 = (f32[1024,512]{1,0:T(8,128)}, f32[1,512]{1,0:T(1,128)}, f32[1,512]{1,0:T(1,128)}) custom-call(bf16[512,640]{1,0:T(8,128)(2,1)S(1)} %bitcast.10), custom_call_target="tpu_custom_call" | custom-call | tf_op jit(solution)/shard_map/pallas_call | solution.py:580
  89.9 2.8 %collective-permute-done.20 = bf16[2,16,2560]{2,1,0:T(8,128)(2,1)S(1)} collective-permute-done((bf16[2,16,2560]{2,1,0:T(8,128)(2,1)S(1)}, bf16[2,16,2560]{2,1,0:T(8,128)(2,1)S(1)}, u32[]{:S(2)}, u32[]{:S(2)}) %collective-permute-start.20) | collective-permute-done | bytes 163872 | tf_op jit(solution)/shard_map/ppermute | solution.py:476
  92.8 1.1 collective-permute-start.21
  93.9 1.0 collective-permute-start.24
  94.9 3.3 %collective-permute-done.21 = bf16[4,16,1280]{2,1,0:T(8,128)(2,1)S(1)} collective-permute-done((bf16[4,16,1280]{2,1,0:T(8,128)(2,1)S(1)}, bf16[4,16,1280]{2,1,0:T(8,128)(2,1)S(1)}, u32[]{:S(2)}, u32[]{:S(2)}) %collective-permute-start.21) | collective-permute-done | bytes 163872 | tf_op jit(solution)/shard_map/ppermute | solution.py:476
  98.2 1.5 %collective-permute-start.22 = (bf16[8,16,1280]{2,1,0:T(8,128)(2,1)S(1)}, bf16[8,16,1280]{2,1,0:T(8,128)(2,1)S(1)}, u32[]{:S(2)}, u32[]{:S(2)}) collective-permute-start(bf16[8,16,1280]{2,1,0:T(8,128)(2,1)S(1)} %pad_maximum_fusion.3), channel_id=1, source_target_pairs={{0,2},{1,3},{2,0},{3,1},{4,6},{5,7},{6,4},{7,5},{8,10},{9,11},{10,... | collective-permute-start | bytes 983048 | tf_op jit(solution)/shard_map/ppermute | solution.py:476
  100.0 1.7 %collective-permute-start.25 = (bf16[8,16,1280]{2,1,0:T(8,128)(2,1)S(1)}, bf16[8,16,1280]{2,1,0:T(8,128)(2,1)S(1)}, u32[]{:S(2)}, u32[]{:S(2)}) collective-permute-start(bf16[8,16,1280]{2,1,0:T(8,128)(2,1)S(1)} %pad_maximum_fusion.4), channel_id=1, source_target_pairs={{0,4},{1,5},{2,6},{3,7},{4,0},{5,1},{6,2},{7,3},{8,12},{9,13},{10,... | collective-permute-start | bytes 983048 | tf_op jit(solution)/shard_map/ppermute | solution.py:476
  101.8 4.5 %collective-permute-done.22 = bf16[8,16,1280]{2,1,0:T(8,128)(2,1)S(1)} collective-permute-done((bf16[8,16,1280]{2,1,0:T(8,128)(2,1)S(1)}, bf16[8,16,1280]{2,1,0:T(8,128)(2,1)S(1)}, u32[]{:S(2)}, u32[]{:S(2)}) %collective-permute-start.22) | collective-permute-done | bytes 327712 | tf_op jit(solution)/shard_map/ppermute | solution.py:476
  106.4 0.8 collective-permute-done.25
  107.3 2.0 %shard_map.151 = (f32[512,2048]{1,0:T(8,128)}, f32[512,512]{1,0:T(8,128)}) custom-call(s32[1]{0:T(128)} %bitcast.me_ref, bf16[16,16,1280]{2,1,0:T(8,128)(2,1)S(1)} %pad_maximum_fusion.left_ref, bf16[16,16,1280]{2,1,0:T(8,128)(2,1)S(1)} %pad_maximum_fusion.1.right_ref), custom_call_target="tpu_custom_call" | custom-call | bytes 4000000 | tf_op jit(solution)/shard_map/pallas_call | solution.py:600
  109.4 2.0 %shard_map.152 = (f32[512,2048]{1,0:T(8,128)}, f32[512,512]{1,0:T(8,128)}) custom-call(s32[1]{0:T(128)} %bitcast.me_ref, bf16[16,16,1280]{2,1,0:T(8,128)(2,1)S(1)} %collective-permute-done.23.left_ref, bf16[16,16,1280]{2,1,0:T(8,128)(2,1)S(1)} %collective-permute-done.26.right_ref, ...), custom_call_target="tpu_custom_call", output_to_operand_aliasing={{0}: (3, {}), {1}: (4, {})} | custom-call | bytes 4000000 | tf_op jit(solution)/shard_map/pallas_call | solution.py:600
  (68 shorter events, 2.6 us)
Async XLA Ops:
  0.6 7.4 %copy-start.4 = (f32[512]{0:T(512)S(1)}, f32[512]{0:T(512)}, u32[]{:S(2)}) copy-start(f32[512]{0:T(512)} %param.21) | copy-start | bytes 6148
  0.6 7.4 %copy-start.5 = (f32[512]{0:T(512)S(1)}, f32[512]{0:T(512)}, u32[]{:S(2)}) copy-start(f32[512]{0:T(512)} %param.20) | copy-start | bytes 6148
  0.7 7.4 %copy-start.2 = (bf16[512,512]{1,0:T(8,128)(2,1)S(1)}, bf16[512,512]{1,0:T(8,128)(2,1)}, u32[]{:S(2)}) copy-start(bf16[512,512]{1,0:T(8,128)(2,1)} %param.19) | copy-start | bytes 1572868
  1.6 6.5 %copy-start.6 = (s32[512]{0:T(512)S(1)}, s32[512]{0:T(512)}, u32[]{:S(2)}) copy-start(s32[512]{0:T(512)} %param.12) | copy-start | bytes 6148
  1.6 6.5 %copy-start.7 = (s32[256]{0:T(256)S(1)}, s32[256]{0:T(256)}, u32[]{:S(2)}) copy-start(s32[256]{0:T(256)} %param.14) | copy-start | bytes 3076
  1.6 6.5 %copy-start.8 = (s32[256,1]{0,1:T(1,128)S(1)}, s32[256,1]{0,1:T(1,128)}, u32[]{:S(2)}) copy-start(s32[256,1]{0,1:T(1,128)} %param.13) | copy-start | bytes 3076
  1.6 10.7 %copy-start.3 = (bf16[256,512]{1,0:T(8,128)(2,1)S(1)}, bf16[256,512]{1,0:T(8,128)(2,1)}, u32[]{:S(2)}) copy-start(bf16[256,512]{1,0:T(8,128)(2,1)} %param.11) | copy-start | bytes 786436
  1.6 6.6 %collective-permute-start.2 = (s32[8,8]{1,0:T(8,128)S(1)}, s32[8,8]{1,0:T(8,128)S(1)}, u32[]{:S(2)}, u32[]{:S(2)}) collective-permute-start(s32[8,8]{1,0:T(8,128)S(1)} %broadcast_select_fusion), channel_id=1, source_target_pairs={{0,12},{1,13},{2,14},{3,15},{4,8},{5,9},{6,10},{7,11},{8,4},{9,5},... | collective-permute-start | bytes 776 | tf_op jit(solution)/shard_map/ppermute | solution.py:476
  5.6 3.6 %collective-permute-start.1 = (s32[8,8]{1,0:T(8,128)S(1)}, s32[8,8]{1,0:T(8,128)S(1)}, u32[]{:S(2)}, u32[]{:S(2)}) collective-permute-start(s32[8,8]{1,0:T(8,128)S(1)} %broadcast_select_fusion), channel_id=1, source_target_pairs={{0,8},{1,9},{2,10},{3,11},{4,12},{5,13},{6,14},{7,15},{8,0},{9,1},... | collective-permute-start | bytes 776 | tf_op jit(solution)/shard_map/ppermute | solution.py:476
  6.0 3.6 %collective-permute-start = (s32[8,8]{1,0:T(8,128)S(1)}, s32[8,8]{1,0:T(8,128)S(1)}, u32[]{:S(2)}, u32[]{:S(2)}) collective-permute-start(s32[8,8]{1,0:T(8,128)S(1)} %broadcast_select_fusion), channel_id=1, source_target_pairs={{0,4},{1,5},{2,6},{3,7},{4,0},{5,1},{6,2},{7,3},{8,12},{9,13},{10,... | collective-permute-start | bytes 776 | tf_op jit(solution)/shard_map/ppermute | solution.py:476
  9.7 5.0 %collective-permute-start.3 = (s32[8,8]{1,0:T(8,128)S(1)}, s32[8,8]{1,0:T(8,128)S(1)}, u32[]{:S(2)}, u32[]{:S(2)}) collective-permute-start(s32[8,8]{1,0:T(8,128)S(1)} %add_add_fusion), channel_id=1, source_target_pairs={{0,16},{1,17},{2,18},{3,19},{4,20},{5,21},{6,22},{7,23},{8,24},{9,... | collective-permute-start | bytes 776 | tf_op jit(solution)/shard_map/ppermute | solution.py:476
  15.5 8.4 %collective-permute-start.4 = (bf16[64,512]{1,0:T(8,128)(2,1)S(1)}, bf16[64,512]{1,0:T(8,128)(2,1)S(1)}, u32[]{:S(2)}, u32[]{:S(2)}) collective-permute-start(bf16[64,512]{1,0:T(8,128)(2,1)S(1)} %get-tuple-element.77), channel_id=1, source_target_pairs={{0,28},{1,13},{2,30},{3,15},{4,24},{5,9},{6,26},{7,11},{8,20},{9,5... | collective-permute-start | bytes 196616 | tf_op jit(solution)/shard_map/ppermute | solution.py:476
  18.6 9.2 %collective-permute-start.5 = (bf16[64,512]{1,0:T(8,128)(2,1)S(1)}, bf16[64,512]{1,0:T(8,128)(2,1)S(1)}, u32[]{:S(2)}, u32[]{:S(2)}) collective-permute-start(bf16[64,512]{1,0:T(8,128)(2,1)S(1)} %get-tuple-element.78), channel_id=1, source_target_pairs={{0,24},{1,9},{2,26},{3,11},{4,28},{5,13},{6,30},{7,15},{8,16},{9,1... | collective-permute-start | bytes 196616 | tf_op jit(solution)/shard_map/ppermute | solution.py:476
  19.3 12.4 %collective-permute-start.6 = (bf16[64,512]{1,0:T(8,128)(2,1)S(1)}, bf16[64,512]{1,0:T(8,128)(2,1)S(1)}, u32[]{:S(2)}, u32[]{:S(2)}) collective-permute-start(bf16[64,512]{1,0:T(8,128)(2,1)S(1)} %get-tuple-element.79), channel_id=1, source_target_pairs={{0,20},{1,5},{2,22},{3,7},{4,16},{5,1},{6,18},{7,3},{8,28},{9,13},... | collective-permute-start | bytes 196616 | tf_op jit(solution)/shard_map/ppermute | solution.py:476
  20.5 11.2 %collective-permute-start.7 = (bf16[64,512]{1,0:T(8,128)(2,1)S(1)}, bf16[64,512]{1,0:T(8,128)(2,1)S(1)}, u32[]{:S(2)}, u32[]{:S(2)}) collective-permute-start(bf16[64,512]{1,0:T(8,128)(2,1)S(1)} %get-tuple-element.80), channel_id=1, source_target_pairs={{0,16},{1,29},{2,18},{3,31},{4,20},{5,25},{6,22},{7,27},{8,24},{9,... | collective-permute-start | bytes 196616 | tf_op jit(solution)/shard_map/ppermute | solution.py:476
  23.2 8.6 %collective-permute-start.8 = (bf16[64,512]{1,0:T(8,128)(2,1)S(1)}, bf16[64,512]{1,0:T(8,128)(2,1)S(1)}, u32[]{:S(2)}, u32[]{:S(2)}) collective-permute-start(bf16[64,512]{1,0:T(8,128)(2,1)S(1)} %get-tuple-element.81), channel_id=1, source_target_pairs={{0,12},{1,25},{2,14},{3,27},{4,8},{5,29},{6,10},{7,31},{8,4},{9,17... | collective-permute-start | bytes 196616 | tf_op jit(solution)/shard_map/ppermute | solution.py:476
  23.9 8.1 %collective-permute-start.9 = (bf16[64,512]{1,0:T(8,128)(2,1)S(1)}, bf16[64,512]{1,0:T(8,128)(2,1)S(1)}, u32[]{:S(2)}, u32[]{:S(2)}) collective-permute-start(bf16[64,512]{1,0:T(8,128)(2,1)S(1)} %get-tuple-element.82), channel_id=1, source_target_pairs={{0,8},{1,21},{2,10},{3,23},{4,12},{5,17},{6,14},{7,19},{8,0},{9,29... | collective-permute-start | bytes 196616 | tf_op jit(solution)/shard_map/ppermute | solution.py:476
  27.8 4.3 %copy-start = (s32[8]{0:T(128)S(1)}, s32[8]{0:T(128)}, u32[]{:S(2)}) copy-start(s32[8]{0:T(128)} %dest_ref.1) | copy-start | bytes 100
  27.8 4.3 %copy-start.1 = (s32[8]{0:T(128)S(1)}, s32[8]{0:T(128)}, u32[]{:S(2)}) copy-start(s32[8]{0:T(128)} %blocks_ref.1) | copy-start | bytes 100
  27.8 4.3 %collective-permute-start.10 = (bf16[64,512]{1,0:T(8,128)(2,1)S(1)}, bf16[64,512]{1,0:T(8,128)(2,1)S(1)}, u32[]{:S(2)}, u32[]{:S(2)}) collective-permute-start(bf16[64,512]{1,0:T(8,128)(2,1)S(1)} %get-tuple-element.83), channel_id=1, source_target_pairs={{0,4},{1,17},{2,6},{3,19},{4,0},{5,21},{6,2},{7,23},{8,12},{9,25},... | collective-permute-start | bytes 196616 | tf_op jit(solution)/shard_map/ppermute | solution.py:476
  40.9 3.2 %collective-permute-start.11 = (bf16[16,16,1664]{2,1,0:T(8,128)(2,1)S(1)}, bf16[16,16,1664]{2,1,0:T(8,128)(2,1)S(1)}, u32[]{:S(2)}, u32[]{:S(2)}) collective-permute-start(bf16[16,16,1664]{2,1,0:T(8,128)(2,1)S(1)} %get-tuple-element.85), channel_id=1, source_target_pairs={{0,1},{1,0},{2,3},{3,2},{4,5},{5,4},{6,7},{7,6},{8,9},{9,8},{10,11... | collective-permute-start | bytes 2555912 | tf_op jit(solution)/shard_map/ppermute | solution.py:476
  40.9 3.0 %collective-permute-start.12 = (bf16[16,16,896]{2,1,0:T(8,128)(2,1)S(1)}, bf16[16,16,896]{2,1,0:T(8,128)(2,1)S(1)}, u32[]{:S(2)}, u32[]{:S(2)}) collective-permute-start(bf16[16,16,896]{2,1,0:T(8,128)(2,1)S(1)} %get-tuple-element.87), channel_id=1, source_target_pairs={{0,1},{1,0},{2,3},{3,2},{4,5},{5,4},{6,7},{7,6},{8,9},{9,8},{10,11... | collective-permute-start | bytes 1376264 | tf_op jit(solution)/shard_map/ppermute | solution.py:476
  44.3 7.8 %collective-permute-start.15 = (bf16[8,16,896]{2,1,0:T(8,128)(2,1)S(1)}, bf16[8,16,896]{2,1,0:T(8,128)(2,1)S(1)}, u32[]{:S(2)}, u32[]{:S(2)}) collective-permute-start(bf16[8,16,896]{2,1,0:T(8,128)(2,1)S(1)} %slice.47), channel_id=1, source_target_pairs={{0,4},{1,5},{2,6},{3,7},{4,0},{5,1},{6,2},{7,3},{8,12},{9,13},{10,... | collective-permute-start | bytes 688136 | tf_op jit(solution)/shard_map/ppermute | solution.py:476
  46.2 12.8 %collective-permute-start.13 = (bf16[8,16,1664]{2,1,0:T(8,128)(2,1)S(1)}, bf16[8,16,1664]{2,1,0:T(8,128)(2,1)S(1)}, u32[]{:S(2)}, u32[]{:S(2)}) collective-permute-start(bf16[8,16,1664]{2,1,0:T(8,128)(2,1)S(1)} %slice.43), channel_id=1, source_target_pairs={{0,2},{1,3},{2,0},{3,1},{4,6},{5,7},{6,4},{7,5},{8,10},{9,11},{10,... | collective-permute-start | bytes 1277960 | tf_op jit(solution)/shard_map/ppermute | solution.py:476
  47.8 22.8 %all-to-all-start = ((bf16[4,8,16,640]{3,2,1,0:T(8,128)(2,1)}), bf16[4,8,16,640]{3,2,1,0:T(8,128)(2,1)S(1)}, u32[]{:S(2)}, u32[]{:S(2)}) async-start(bf16[4,8,16,640]{3,2,1,0:T(8,128)(2,1)} %bitcast.5), calls=%async_computation | async-start | bytes 1310720 | tf_op jit(solution)/shard_map/all_to_all | solution.py:479
  52.2 8.2 %collective-permute-start.16 = (bf16[4,16,896]{2,1,0:T(8,128)(2,1)S(1)}, bf16[4,16,896]{2,1,0:T(8,128)(2,1)S(1)}, u32[]{:S(2)}, u32[]{:S(2)}) collective-permute-start(bf16[4,16,896]{2,1,0:T(8,128)(2,1)S(1)} %slice.59), channel_id=1, source_target_pairs={{0,2},{1,3},{2,0},{3,1},{4,6},{5,7},{6,4},{7,5},{8,10},{9,11},{10,... | collective-permute-start | bytes 344072 | tf_op jit(solution)/shard_map/ppermute | solution.py:476
  59.1 5.9 %collective-permute-start.14 = (bf16[4,16,1664]{2,1,0:T(8,128)(2,1)S(1)}, bf16[4,16,1664]{2,1,0:T(8,128)(2,1)S(1)}, u32[]{:S(2)}, u32[]{:S(2)}) collective-permute-start(bf16[4,16,1664]{2,1,0:T(8,128)(2,1)S(1)} %slice.57), channel_id=1, source_target_pairs={{0,4},{1,5},{2,6},{3,7},{4,0},{5,1},{6,2},{7,3},{8,12},{9,13},{10,... | collective-permute-start | bytes 638984 | tf_op jit(solution)/shard_map/ppermute | solution.py:476
  65.1 5.4 %collective-permute-start.17 = (bf16[2,16,2560]{2,1,0:T(8,128)(2,1)S(1)}, bf16[2,16,2560]{2,1,0:T(8,128)(2,1)S(1)}, u32[]{:S(2)}, u32[]{:S(2)}) collective-permute-start(bf16[2,16,2560]{2,1,0:T(8,128)(2,1)S(1)} %pad_maximum_fusion.5), channel_id=1, source_target_pairs={{0,8},{1,9},{2,10},{3,11},{4,12},{5,13},{6,14},{7,15},{8,0},{9,1},... | collective-permute-start | bytes 491528 | tf_op jit(solution)/shard_map/ppermute | solution.py:476
  70.6 6.3 %collective-permute-start.18 = (bf16[1,16,2560]{2,1,0:T(8,128)(2,1)S(1)}, bf16[1,16,2560]{2,1,0:T(8,128)(2,1)S(1)}, u32[]{:S(2)}, u32[]{:S(2)}) collective-permute-start(bf16[1,16,2560]{2,1,0:T(8,128)(2,1)S(1)} %slice.53), channel_id=1, source_target_pairs={{0,16},{1,17},{2,18},{3,19},{4,20},{5,21},{6,22},{7,23},{8,24},{9,... | collective-permute-start | bytes 245768 | tf_op jit(solution)/shard_map/ppermute | solution.py:476
  72.8 14.2 %all-to-all-start.1 = ((bf16[8,4,16,640]{3,2,1,0:T(8,128)(2,1)}), bf16[8,4,16,640]{3,2,1,0:T(8,128)(2,1)S(1)}, u32[]{:S(2)}, u32[]{:S(2)}) async-start(bf16[8,4,16,640]{3,2,1,0:T(8,128)(2,1)} %copy.20), calls=%async_computation.1 | async-start | bytes 1310720 | tf_op jit(solution)/shard_map/all_to_all | solution.py:479
  76.9 7.5 %collective-permute-start.19 = (bf16[1,16,2560]{2,1,0:T(8,128)(2,1)S(1)}, bf16[1,16,2560]{2,1,0:T(8,128)(2,1)S(1)}, u32[]{:S(2)}, u32[]{:S(2)}) collective-permute-start(bf16[1,16,2560]{2,1,0:T(8,128)(2,1)S(1)} %add_convert_fusion.7), channel_id=1, source_target_pairs={{0,16},{1,17},{2,18},{3,19},{4,20},{5,21},{6,22},{7,23},{8,24},{9,... | collective-permute-start | bytes 245768 | tf_op jit(solution)/shard_map/ppermute | solution.py:476
  87.0 5.7 %collective-permute-start.20 = (bf16[2,16,2560]{2,1,0:T(8,128)(2,1)S(1)}, bf16[2,16,2560]{2,1,0:T(8,128)(2,1)S(1)}, u32[]{:S(2)}, u32[]{:S(2)}) collective-permute-start(bf16[2,16,2560]{2,1,0:T(8,128)(2,1)S(1)} %pad_maximum_fusion.6), channel_id=1, source_target_pairs={{0,8},{1,9},{2,10},{3,11},{4,12},{5,13},{6,14},{7,15},{8,0},{9,1},... | collective-permute-start | bytes 491528 | tf_op jit(solution)/shard_map/ppermute | solution.py:476
  92.8 5.4 %collective-permute-start.21 = (bf16[4,16,1280]{2,1,0:T(8,128)(2,1)S(1)}, bf16[4,16,1280]{2,1,0:T(8,128)(2,1)S(1)}, u32[]{:S(2)}, u32[]{:S(2)}) collective-permute-start(bf16[4,16,1280]{2,1,0:T(8,128)(2,1)S(1)} %get-tuple-element.106), channel_id=1, source_target_pairs={{0,4},{1,5},{2,6},{3,7},{4,0},{5,1},{6,2},{7,3},{8,12},{9,13},{10,... | collective-permute-start | bytes 491528 | tf_op jit(solution)/shard_map/ppermute | solution.py:476
  93.9 6.1 %collective-permute-start.24 = (bf16[4,16,1280]{2,1,0:T(8,128)(2,1)S(1)}, bf16[4,16,1280]{2,1,0:T(8,128)(2,1)S(1)}, u32[]{:S(2)}, u32[]{:S(2)}) collective-permute-start(bf16[4,16,1280]{2,1,0:T(8,128)(2,1)S(1)} %get-tuple-element.105), channel_id=1, source_target_pairs={{0,2},{1,3},{2,0},{3,1},{4,6},{5,7},{6,4},{7,5},{8,10},{9,11},{10,... | collective-permute-start | bytes 491528 | tf_op jit(solution)/shard_map/ppermute | solution.py:476
  98.2 8.0 %collective-permute-start.22 = (bf16[8,16,1280]{2,1,0:T(8,128)(2,1)S(1)}, bf16[8,16,1280]{2,1,0:T(8,128)(2,1)S(1)}, u32[]{:S(2)}, u32[]{:S(2)}) collective-permute-start(bf16[8,16,1280]{2,1,0:T(8,128)(2,1)S(1)} %pad_maximum_fusion.3), channel_id=1, source_target_pairs={{0,2},{1,3},{2,0},{3,1},{4,6},{5,7},{6,4},{7,5},{8,10},{9,11},{10,... | collective-permute-start | bytes 983048 | tf_op jit(solution)/shard_map/ppermute | solution.py:476
  100.0 7.1 %collective-permute-start.25 = (bf16[8,16,1280]{2,1,0:T(8,128)(2,1)S(1)}, bf16[8,16,1280]{2,1,0:T(8,128)(2,1)S(1)}, u32[]{:S(2)}, u32[]{:S(2)}) collective-permute-start(bf16[8,16,1280]{2,1,0:T(8,128)(2,1)S(1)} %pad_maximum_fusion.4), channel_id=1, source_target_pairs={{0,4},{1,5},{2,6},{3,7},{4,0},{5,1},{6,2},{7,3},{8,12},{9,13},{10,... | collective-permute-start | bytes 983048 | tf_op jit(solution)/shard_map/ppermute | solution.py:476
  106.3 3.0 %collective-permute-start.23 = (bf16[16,16,1280]{2,1,0:T(8,128)(2,1)S(1)}, bf16[16,16,1280]{2,1,0:T(8,128)(2,1)S(1)}, u32[]{:S(2)}, u32[]{:S(2)}) collective-permute-start(bf16[16,16,1280]{2,1,0:T(8,128)(2,1)S(1)} %pad_maximum_fusion.left_ref), channel_id=1, source_target_pairs={{0,1},{1,0},{2,3},{3,2},{4,5},{5,4},{6,7},{7,6},{8,9},{9,8},{10,11... | collective-permute-start | bytes 1966088 | tf_op jit(solution)/shard_map/ppermute | solution.py:476
  107.3 2.2 %collective-permute-start.26 = (bf16[16,16,1280]{2,1,0:T(8,128)(2,1)S(1)}, bf16[16,16,1280]{2,1,0:T(8,128)(2,1)S(1)}, u32[]{:S(2)}, u32[]{:S(2)}) collective-permute-start(bf16[16,16,1280]{2,1,0:T(8,128)(2,1)S(1)} %pad_maximum_fusion.1.right_ref), channel_id=1, source_target_pairs={{0,1},{1,0},{2,3},{3,2},{4,5},{5,4},{6,7},{7,6},{8,9},{9,8},{10,11... | collective-permute-start | bytes 1966088 | tf_op jit(solution)/shard_map/ppermute | solution.py:476

commit v20 on v17

--- a/solution.py
+++ b/solution.py
@@ -361,9 +361,7 @@
         self.wide = -(-5 * width // block) * LANES
         self.gain_lanes = 2 * width // self.capacity
         self.extra = -(-(GAIN_AT + self.gain_lanes) // LANES) * LANES
-        first = -(-3 * self.wide // (5 * LANES)) * LANES
         self.split = -(-self.wide // (2 * LANES)) * LANES
-        self.sides = ((0, first), (first, self.wide - first))
         self.halves = ((0, self.split), (self.split, self.wide - self.split))
         table_bits = [1 << bit for bit in range(1, table_size.bit_length() - 1)]
         dp_bits = [table_size << bit for bit in range(dp_size.bit_length() - 1)]
@@ -393,7 +391,7 @@
                 first = pl.multiple_of((chunk & (self.row_groups - 1)) * CHUNK_ROWS, CHUNK_ROWS)
                 rows = pl.ds(first, CHUNK_ROWS)
                 out_ref = part_refs[2 * side + place // half]
-                out_ref[place % half] = sums_ref[rows, self.columns(chunk, self.sides[side])]
+                out_ref[place % half] = sums_ref[rows, self.columns(chunk, self.halves[side])]
 
 
 def table_body(plan, got_ref, out_ref, gain_in_ref, gain_out_ref):
@@ -525,7 +523,7 @@
     saved |= dict(zip(shapes, made))
 
     outs = [shape_of((devices_all * plan.capacity, width + plan.extra), BF16)]
-    for _, wide in plan.sides:
+    for _, wide in plan.halves:
         outs += [shape_of((devices_all // 2, CHUNK_ROWS, wide), BF16)] * 2
     table_send, *parts = call(
         functools.partial(backward_body, plan, table_size, total_factor),

time: 111 us -> 114 us (1.027)
  starting transfers between devices: 42.6 us -> 46.3 us
  local copies, waits for them, and re-layouts: 4.76 us -> 2.87 us
  waiting for transfers between devices: 39.1 us -> 40.7 us
    ppermute x27, starting transfers between devices: 34 us -> 38.3 us  [swap(): return lax.ppermute(values, both, pairs)]
    ppermute x27, waiting for transfers between devices: 36.5 us -> 38.1 us  [swap(): return lax.ppermute(values, both, pairs)]
    unnamed x18 -> x22, local copies, waits for them, and re-layouts: 2.74 us -> 1.81 us
  transfers between devices with their start and end apart: 29 -> 29, of which waited for: 17 -> 17; matrix products, arithmetic and copies ran while one was open for 5% -> 3% of each run, Pallas kernels for 9% -> 8%
where the time goes in v20:
time: 114 us
  starting transfers between devices  46.3 us (41%)
  waiting for transfers between devices  40.7 us (36%)
  Pallas kernels  21 us (18%)
  local copies, waits for them, and re-layouts  2.87 us (3%)
  other arithmetic  1.84 us (2%)
  between operations  1.2 us (1%)
    ppermute x27, starting transfers between devices, swap(): return lax.ppermute(values, both, pairs)  38.3 us
    ppermute x27, waiting for transfers between devices, swap(): return lax.ppermute(values, both, pairs)  38.1 us
    pallas_call x1, Pallas kernels, on_device(): call(functools.partial(backward_body, plan, table_size, total_factor), ou...  8.9 us
    all_to_all x2, starting transfers between devices, exchange(): lax.all_to_all(values, axes, split_axis=0, concat_axis=0, tiled=True, axi...  8.01 us
    pallas_call x2, Pallas kernels, on_device(): pl.pallas_call(functools.partial(widen_body, plan, turn), out_shape=outs,...  3.93 us
    pallas_call x1, Pallas kernels, on_device(): call(forward_body, list(shapes.values()), [VMEM] * 3, flops=4 * count * w...  3.92 us
    all_to_all x2, waiting for transfers between devices, exchange(): lax.all_to_all(values, axes, split_axis=0, concat_axis=0, tiled=True, axi...  2.65 us
  transfers between devices with their start and end apart: 29, of which 17 were waited for; matrix products, arithmetic and copies ran while one was open for 3% of the time, Pallas kernels for 8%

profile of v20, /device:TPU:0, one launch (start us, length us, event | category | flops | bytes accessed | tf_op | source)
XLA Modules:
  0.0 113.9 jit_solution(11036147176511715656)
XLA Ops:
  0.6 0.8 select_reduce_fusion
  1.5 4.0 %collective-permute-start.2 = (s32[8,8]{1,0:T(8,128)S(1)}, s32[8,8]{1,0:T(8,128)S(1)}, u32[]{:S(2)}, u32[]{:S(2)}) collective-permute-start(s32[8,8]{1,0:T(8,128)S(1)} %broadcast_select_fusion), channel_id=1, source_target_pairs={{0,12},{1,13},{2,14},{3,15},{4,8},{5,9},{6,10},{7,11},{8,4},{9,5},... | collective-permute-start | bytes 776 | tf_op jit(solution)/shard_map/ppermute | solution.py:474
  6.2 1.7 %constant_dynamic-update-slice_fusion.1 = bf16[512,2560]{1,0:T(8,128)(2,1)S(1)} fusion(bf16[512,2048]{1,0:T(8,128)(2,1)} %param.18), kind=kLoop, calls=%fused_computation.19 | loop fusion | bytes 4194304
  8.1 1.1 collective-permute-done.1
  9.7 2.6 %collective-permute-start.3 = (s32[8,8]{1,0:T(8,128)S(1)}, s32[8,8]{1,0:T(8,128)S(1)}, u32[]{:S(2)}, u32[]{:S(2)}) collective-permute-start(s32[8,8]{1,0:T(8,128)S(1)} %add_add_fusion), channel_id=1, source_target_pairs={{0,16},{1,17},{2,18},{3,19},{4,20},{5,21},{6,22},{7,23},{8,24},{9,... | collective-permute-start | bytes 776 | tf_op jit(solution)/shard_map/ppermute | solution.py:474
  12.3 1.9 %collective-permute-done.3 = s32[8,8]{1,0:T(8,128)S(1)} collective-permute-done((s32[8,8]{1,0:T(8,128)S(1)}, s32[8,8]{1,0:T(8,128)S(1)}, u32[]{:S(2)}, u32[]{:S(2)}) %collective-permute-start.3) | collective-permute-done | bytes 288 | tf_op jit(solution)/shard_map/ppermute | solution.py:474
  14.2 0.7 shard_map.147
  14.9 3.6 %collective-permute-start.4 = (bf16[64,512]{1,0:T(8,128)(2,1)S(1)}, bf16[64,512]{1,0:T(8,128)(2,1)S(1)}, u32[]{:S(2)}, u32[]{:S(2)}) collective-permute-start(bf16[64,512]{1,0:T(8,128)(2,1)S(1)} %get-tuple-element.73), channel_id=1, source_target_pairs={{0,28},{1,13},{2,30},{3,15},{4,24},{5,9},{6,26},{7,11},{8,20},{9,5... | collective-permute-start | bytes 196616 | tf_op jit(solution)/shard_map/ppermute | solution.py:474
  18.6 1.4 %shard_map.146 = (bf16[256,2560]{1,0:T(8,128)(2,1)S(1)}, bf16[512,256]{1,0:T(8,128)(2,1)S(1)}, bf16[256,2048]{1,0:T(8,128)(2,1)S(1)}, f32[256,512]{1,0:T(8,128)S...) custom-call(bf16[512,512]{1,0:T(8,128)(2,1)S(1)} %constant_dynamic-update-slice_fusion.2.rows_ref, ...), custom_call_target="tpu_custom_call" | custom-call | flops 536870912 | bytes 4000000 | tf_op jit(solution)/shard_map/pallas_call | solution.py:505
  20.0 1.9 %collective-permute-start.6 = (bf16[64,512]{1,0:T(8,128)(2,1)S(1)}, bf16[64,512]{1,0:T(8,128)(2,1)S(1)}, u32[]{:S(2)}, u32[]{:S(2)}) collective-permute-start(bf16[64,512]{1,0:T(8,128)(2,1)S(1)} %get-tuple-element.75), channel_id=1, source_target_pairs={{0,20},{1,5},{2,22},{3,7},{4,16},{5,1},{6,18},{7,3},{8,28},{9,13},... | collective-permute-start | bytes 196616 | tf_op jit(solution)/shard_map/ppermute | solution.py:474
  22.0 2.1 %collective-permute-start.7 = (bf16[64,512]{1,0:T(8,128)(2,1)S(1)}, bf16[64,512]{1,0:T(8,128)(2,1)S(1)}, u32[]{:S(2)}, u32[]{:S(2)}) collective-permute-start(bf16[64,512]{1,0:T(8,128)(2,1)S(1)} %get-tuple-element.76), channel_id=1, source_target_pairs={{0,16},{1,29},{2,18},{3,31},{4,20},{5,25},{6,22},{7,27},{8,24},{9,... | collective-permute-start | bytes 196616 | tf_op jit(solution)/shard_map/ppermute | solution.py:474
  24.1 1.3 %collective-permute-start.8 = (bf16[64,512]{1,0:T(8,128)(2,1)S(1)}, bf16[64,512]{1,0:T(8,128)(2,1)S(1)}, u32[]{:S(2)}, u32[]{:S(2)}) collective-permute-start(bf16[64,512]{1,0:T(8,128)(2,1)S(1)} %get-tuple-element.77), channel_id=1, source_target_pairs={{0,12},{1,25},{2,14},{3,27},{4,8},{5,29},{6,10},{7,31},{8,4},{9,17... | collective-permute-start | bytes 196616 | tf_op jit(solution)/shard_map/ppermute | solution.py:474
  25.4 0.5 collective-permute-start.9
  26.0 1.6 %collective-permute-start.10 = (bf16[64,512]{1,0:T(8,128)(2,1)S(1)}, bf16[64,512]{1,0:T(8,128)(2,1)S(1)}, u32[]{:S(2)}, u32[]{:S(2)}) collective-permute-start(bf16[64,512]{1,0:T(8,128)(2,1)S(1)} %get-tuple-element.79), channel_id=1, source_target_pairs={{0,4},{1,17},{2,6},{3,19},{4,0},{5,21},{6,2},{7,23},{8,12},{9,25},... | collective-permute-start | bytes 196616 | tf_op jit(solution)/shard_map/ppermute | solution.py:474
  27.6 3.9 %shard_map.148 = (f32[512,512]{1,0:T(8,128)S(1)}, f32[512,512]{1,0:T(8,128)S(1)}, f32[512,1]{1,0:T(8,128)S(1)}, bf16[512,1536]{1,0:T(8,128)(2,1)S(1)}, bf16[16,1...) custom-call(bf16[256,2560]{1,0:T(8,128)(2,1)S(1)} %get-tuple-element, ...), custom_call_target="tpu_custom_call" | custom-call | flops 2684354560 | bytes 8000000 | tf_op jit(solution)/shard_map/pallas_call | solution.py:515
  31.6 8.9 %shard_map.149 = (bf16[512,640]{1,0:T(8,128)(2,1)}, bf16[16,16,1280]{2,1,0:T(8,128)(2,1)S(1)}, bf16[16,16,1280]{2,1,0:T(8,128)(2,1)S(1)}, bf16[16,16,1280]{2,1,0:T(8,128)(2,1)S(1)}, bf16[16,16,1280]{2,1,0:T(8,128)(2,1)S(1)}) custom-call(s32[1]{0:T(128)} %bitcast.me_ref, s32[8]{0:T(128)S(1)} %copy-done, s32[8]{0:T(128)S(1)} %copy-done.1, ...), custom_call_target="tpu_custom_call" | custom-call | flops 10737418240 | bytes 12000000 | tf_op jit(solution)/shard_map/pallas_call | solution.py:528
  40.5 0.5 collective-permute-start.12
  41.0 1.6 %collective-permute-done.11 = bf16[16,16,1280]{2,1,0:T(8,128)(2,1)S(1)} collective-permute-done((bf16[16,16,1280]{2,1,0:T(8,128)(2,1)S(1)}, bf16[16,16,1280]{2,1,0:T(8,128)(2,1)S(1)}, u32[]{:S(2)}, u32[]{:S(2)}) %collective-permute-start.11) | collective-permute-done | bytes 655392 | tf_op jit(solution)/shard_map/ppermute | solution.py:474
  42.8 0.8 collective-permute-done.12
  43.7 1.4 %collective-permute-start.15 = (bf16[8,16,1280]{2,1,0:T(8,128)(2,1)S(1)}, bf16[8,16,1280]{2,1,0:T(8,128)(2,1)S(1)}, u32[]{:S(2)}, u32[]{:S(2)}) collective-permute-start(bf16[8,16,1280]{2,1,0:T(8,128)(2,1)S(1)} %slice.47), channel_id=1, source_target_pairs={{0,4},{1,5},{2,6},{3,7},{4,0},{5,1},{6,2},{7,3},{8,12},{9,13},{10,... | collective-permute-start | bytes 983048 | tf_op jit(solution)/shard_map/ppermute | solution.py:474
  45.1 4.5 %all-to-all-start = ((bf16[4,8,16,640]{3,2,1,0:T(8,128)(2,1)}), bf16[4,8,16,640]{3,2,1,0:T(8,128)(2,1)S(1)}, u32[]{:S(2)}, u32[]{:S(2)}) async-start(bf16[4,8,16,640]{3,2,1,0:T(8,128)(2,1)} %bitcast.5), calls=%async_computation | async-start | bytes 1310720 | tf_op jit(solution)/shard_map/all_to_all | solution.py:477
  49.6 1.6 %collective-permute-start.13 = (bf16[8,16,1280]{2,1,0:T(8,128)(2,1)S(1)}, bf16[8,16,1280]{2,1,0:T(8,128)(2,1)S(1)}, u32[]{:S(2)}, u32[]{:S(2)}) collective-permute-start(bf16[8,16,1280]{2,1,0:T(8,128)(2,1)S(1)} %slice.43), channel_id=1, source_target_pairs={{0,2},{1,3},{2,0},{3,1},{4,6},{5,7},{6,4},{7,5},{8,10},{9,11},{10,... | collective-permute-start | bytes 983048 | tf_op jit(solution)/shard_map/ppermute | solution.py:474
  51.2 2.4 %collective-permute-done.15 = bf16[8,16,1280]{2,1,0:T(8,128)(2,1)S(1)} collective-permute-done((bf16[8,16,1280]{2,1,0:T(8,128)(2,1)S(1)}, bf16[8,16,1280]{2,1,0:T(8,128)(2,1)S(1)}, u32[]{:S(2)}, u32[]{:S(2)}) %collective-permute-start.15) | collective-permute-done | bytes 327712 | tf_op jit(solution)/shard_map/ppermute | solution.py:474
  53.7 1.6 %collective-permute-start.16 = (bf16[4,16,1280]{2,1,0:T(8,128)(2,1)S(1)}, bf16[4,16,1280]{2,1,0:T(8,128)(2,1)S(1)}, u32[]{:S(2)}, u32[]{:S(2)}) collective-permute-start(bf16[4,16,1280]{2,1,0:T(8,128)(2,1)S(1)} %slice.59), channel_id=1, source_target_pairs={{0,2},{1,3},{2,0},{3,1},{4,6},{5,7},{6,4},{7,5},{8,10},{9,11},{10,... | collective-permute-start | bytes 491528 | tf_op jit(solution)/shard_map/ppermute | solution.py:474
  55.3 5.1 %collective-permute-done.13 = bf16[8,16,1280]{2,1,0:T(8,128)(2,1)S(1)} collective-permute-done((bf16[8,16,1280]{2,1,0:T(8,128)(2,1)S(1)}, bf16[8,16,1280]{2,1,0:T(8,128)(2,1)S(1)}, u32[]{:S(2)}, u32[]{:S(2)}) %collective-permute-start.13) | collective-permute-done | bytes 327712 | tf_op jit(solution)/shard_map/ppermute | solution.py:474
  60.4 1.2 %collective-permute-start.14 = (bf16[4,16,1280]{2,1,0:T(8,128)(2,1)S(1)}, bf16[4,16,1280]{2,1,0:T(8,128)(2,1)S(1)}, u32[]{:S(2)}, u32[]{:S(2)}) collective-permute-start(bf16[4,16,1280]{2,1,0:T(8,128)(2,1)S(1)} %slice.57), channel_id=1, source_target_pairs={{0,4},{1,5},{2,6},{3,7},{4,0},{5,1},{6,2},{7,3},{8,12},{9,13},{10,... | collective-permute-start | bytes 491528 | tf_op jit(solution)/shard_map/ppermute | solution.py:474
  61.6 0.8 collective-permute-done.16
  62.4 3.4 %collective-permute-done.14 = bf16[4,16,1280]{2,1,0:T(8,128)(2,1)S(1)} collective-permute-done((bf16[4,16,1280]{2,1,0:T(8,128)(2,1)S(1)}, bf16[4,16,1280]{2,1,0:T(8,128)(2,1)S(1)}, u32[]{:S(2)}, u32[]{:S(2)}) %collective-permute-start.14) | collective-permute-done | bytes 163872 | tf_op jit(solution)/shard_map/ppermute | solution.py:474
  65.9 2.1 %collective-permute-start.17 = (bf16[2,16,2560]{2,1,0:T(8,128)(2,1)S(1)}, bf16[2,16,2560]{2,1,0:T(8,128)(2,1)S(1)}, u32[]{:S(2)}, u32[]{:S(2)}) collective-permute-start(bf16[2,16,2560]{2,1,0:T(8,128)(2,1)S(1)} %pad_maximum_fusion.5), channel_id=1, source_target_pairs={{0,8},{1,9},{2,10},{3,11},{4,12},{5,13},{6,14},{7,15},{8,0},{9,1},... | collective-permute-start | bytes 491528 | tf_op jit(solution)/shard_map/ppermute | solution.py:474
  68.0 3.7 %collective-permute-done.17 = bf16[2,16,2560]{2,1,0:T(8,128)(2,1)S(1)} collective-permute-done((bf16[2,16,2560]{2,1,0:T(8,128)(2,1)S(1)}, bf16[2,16,2560]{2,1,0:T(8,128)(2,1)S(1)}, u32[]{:S(2)}, u32[]{:S(2)}) %collective-permute-start.17) | collective-permute-done | bytes 163872 | tf_op jit(solution)/shard_map/ppermute | solution.py:474
  71.8 3.0 %collective-permute-start.18 = (bf16[1,16,2560]{2,1,0:T(8,128)(2,1)S(1)}, bf16[1,16,2560]{2,1,0:T(8,128)(2,1)S(1)}, u32[]{:S(2)}, u32[]{:S(2)}) collective-permute-start(bf16[1,16,2560]{2,1,0:T(8,128)(2,1)S(1)} %slice.53), channel_id=1, source_target_pairs={{0,16},{1,17},{2,18},{3,19},{4,20},{5,21},{6,22},{7,23},{8,24},{9,... | collective-permute-start | bytes 245768 | tf_op jit(solution)/shard_map/ppermute | solution.py:474
  74.7 0.9 copy.20
  75.6 3.5 %all-to-all-start.1 = ((bf16[8,4,16,640]{3,2,1,0:T(8,128)(2,1)}), bf16[8,4,16,640]{3,2,1,0:T(8,128)(2,1)S(1)}, u32[]{:S(2)}, u32[]{:S(2)}) async-start(bf16[8,4,16,640]{3,2,1,0:T(8,128)(2,1)} %copy.20), calls=%async_computation.1 | async-start | bytes 1310720 | tf_op jit(solution)/shard_map/all_to_all | solution.py:477
  79.2 1.0 collective-permute-start.19
  80.2 6.5 %collective-permute-done.19 = bf16[1,16,2560]{2,1,0:T(8,128)(2,1)S(1)} collective-permute-done((bf16[1,16,2560]{2,1,0:T(8,128)(2,1)S(1)}, bf16[1,16,2560]{2,1,0:T(8,128)(2,1)S(1)}, u32[]{:S(2)}, u32[]{:S(2)}) %collective-permute-start.19) | collective-permute-done | bytes 81952 | tf_op jit(solution)/shard_map/ppermute | solution.py:474
  86.7 2.6 %all-to-all-done.1 = bf16[8,4,16,640]{3,2,1,0:T(8,128)(2,1)S(1)} async-done(((bf16[8,4,16,640]{3,2,1,0:T(8,128)(2,1)}), bf16[8,4,16,640]{3,2,1,0:T(8,128)(2,1)S(1)}, u32[]{:S(2)}, u32[]{:S(2)}) %all-to-all-start.1) | async-done | bytes 655392 | tf_op jit(solution)/shard_map/all_to_all | solution.py:477
  89.3 1.9 %collective-permute-start.20 = (bf16[2,16,2560]{2,1,0:T(8,128)(2,1)S(1)}, bf16[2,16,2560]{2,1,0:T(8,128)(2,1)S(1)}, u32[]{:S(2)}, u32[]{:S(2)}) collective-permute-start(bf16[2,16,2560]{2,1,0:T(8,128)(2,1)S(1)} %pad_maximum_fusion.6), channel_id=1, source_target_pairs={{0,8},{1,9},{2,10},{3,11},{4,12},{5,13},{6,14},{7,15},{8,0},{9,1},... | collective-permute-start | bytes 491528 | tf_op jit(solution)/shard_map/ppermute | solution.py:474
  91.3 2.2 %shard_map.150 = (f32[1024,512]{1,0:T(8,128)}, f32[1,512]{1,0:T(1,128)}, f32[1,512]{1,0:T(1,128)}) custom-call(bf16[512,640]{1,0:T(8,128)(2,1)S(1)} %bitcast.10), custom_call_target="tpu_custom_call" | custom-call | tf_op jit(solution)/shard_map/pallas_call | solution.py:577
  93.5 1.8 %collective-permute-done.20 = bf16[2,16,2560]{2,1,0:T(8,128)(2,1)S(1)} collective-permute-done((bf16[2,16,2560]{2,1,0:T(8,128)(2,1)S(1)}, bf16[2,16,2560]{2,1,0:T(8,128)(2,1)S(1)}, u32[]{:S(2)}, u32[]{:S(2)}) %collective-permute-start.20) | collective-permute-done | bytes 163872 | tf_op jit(solution)/shard_map/ppermute | solution.py:474
  95.4 0.9 collective-permute-start.21
  96.3 1.2 %collective-permute-start.24 = (bf16[4,16,1280]{2,1,0:T(8,128)(2,1)S(1)}, bf16[4,16,1280]{2,1,0:T(8,128)(2,1)S(1)}, u32[]{:S(2)}, u32[]{:S(2)}) collective-permute-start(bf16[4,16,1280]{2,1,0:T(8,128)(2,1)S(1)} %get-tuple-element.101), channel_id=1, source_target_pairs={{0,2},{1,3},{2,0},{3,1},{4,6},{5,7},{6,4},{7,5},{8,10},{9,11},{10,... | collective-permute-start | bytes 491528 | tf_op jit(solution)/shard_map/ppermute | solution.py:474
  97.4 3.3 %collective-permute-done.21 = bf16[4,16,1280]{2,1,0:T(8,128)(2,1)S(1)} collective-permute-done((bf16[4,16,1280]{2,1,0:T(8,128)(2,1)S(1)}, bf16[4,16,1280]{2,1,0:T(8,128)(2,1)S(1)}, u32[]{:S(2)}, u32[]{:S(2)}) %collective-permute-start.21) | collective-permute-done | bytes 163872 | tf_op jit(solution)/shard_map/ppermute | solution.py:474
  100.8 1.5 %collective-permute-start.22 = (bf16[8,16,1280]{2,1,0:T(8,128)(2,1)S(1)}, bf16[8,16,1280]{2,1,0:T(8,128)(2,1)S(1)}, u32[]{:S(2)}, u32[]{:S(2)}) collective-permute-start(bf16[8,16,1280]{2,1,0:T(8,128)(2,1)S(1)} %pad_maximum_fusion.3), channel_id=1, source_target_pairs={{0,2},{1,3},{2,0},{3,1},{4,6},{5,7},{6,4},{7,5},{8,10},{9,11},{10,... | collective-permute-start | bytes 983048 | tf_op jit(solution)/shard_map/ppermute | solution.py:474
  102.4 1.8 %collective-permute-start.25 = (bf16[8,16,1280]{2,1,0:T(8,128)(2,1)S(1)}, bf16[8,16,1280]{2,1,0:T(8,128)(2,1)S(1)}, u32[]{:S(2)}, u32[]{:S(2)}) collective-permute-start(bf16[8,16,1280]{2,1,0:T(8,128)(2,1)S(1)} %pad_maximum_fusion.4), channel_id=1, source_target_pairs={{0,4},{1,5},{2,6},{3,7},{4,0},{5,1},{6,2},{7,3},{8,12},{9,13},{10,... | collective-permute-start | bytes 983048 | tf_op jit(solution)/shard_map/ppermute | solution.py:474
  104.2 4.5 %collective-permute-done.22 = bf16[8,16,1280]{2,1,0:T(8,128)(2,1)S(1)} collective-permute-done((bf16[8,16,1280]{2,1,0:T(8,128)(2,1)S(1)}, bf16[8,16,1280]{2,1,0:T(8,128)(2,1)S(1)}, u32[]{:S(2)}, u32[]{:S(2)}) %collective-permute-start.22) | collective-permute-done | bytes 327712 | tf_op jit(solution)/shard_map/ppermute | solution.py:474
  108.8 0.8 collective-permute-done.25
  109.7 2.0 %shard_map.151 = (f32[512,2048]{1,0:T(8,128)}, f32[512,512]{1,0:T(8,128)}) custom-call(s32[1]{0:T(128)} %bitcast.me_ref, bf16[16,16,1280]{2,1,0:T(8,128)(2,1)S(1)} %pad_maximum_fusion.left_ref, bf16[16,16,1280]{2,1,0:T(8,128)(2,1)S(1)} %pad_maximum_fusion.1.right_ref), custom_call_target="tpu_custom_call" | custom-call | bytes 4000000 | tf_op jit(solution)/shard_map/pallas_call | solution.py:597
  111.8 2.0 %shard_map.152 = (f32[512,2048]{1,0:T(8,128)}, f32[512,512]{1,0:T(8,128)}) custom-call(s32[1]{0:T(128)} %bitcast.me_ref, bf16[16,16,1280]{2,1,0:T(8,128)(2,1)S(1)} %collective-permute-done.23.left_ref, bf16[16,16,1280]{2,1,0:T(8,128)(2,1)S(1)} %collective-permute-done.26.right_ref, ...), custom_call_target="tpu_custom_call", output_to_operand_aliasing={{0}: (3, {}), {1}: (4, {})} | custom-call | bytes 4000000 | tf_op jit(solution)/shard_map/pallas_call | solution.py:597
  (70 shorter events, 2.8 us)
Async XLA Ops:
  1.5 6.5 %copy-start.5 = (f32[512]{0:T(512)S(1)}, f32[512]{0:T(512)}, u32[]{:S(2)}) copy-start(f32[512]{0:T(512)} %param.21) | copy-start | bytes 6148
  1.5 6.5 %copy-start.6 = (f32[512]{0:T(512)S(1)}, f32[512]{0:T(512)}, u32[]{:S(2)}) copy-start(f32[512]{0:T(512)} %param.20) | copy-start | bytes 6148
  1.5 6.5 %copy-start.2 = (bf16[512,512]{1,0:T(8,128)(2,1)S(1)}, bf16[512,512]{1,0:T(8,128)(2,1)}, u32[]{:S(2)}) copy-start(bf16[512,512]{1,0:T(8,128)(2,1)} %param.19) | copy-start | bytes 1572868
  1.5 10.8 %copy-start.3 = (bf16[256,512]{1,0:T(8,128)(2,1)S(1)}, bf16[256,512]{1,0:T(8,128)(2,1)}, u32[]{:S(2)}) copy-start(bf16[256,512]{1,0:T(8,128)(2,1)} %param.11) | copy-start | bytes 786436
  1.5 10.8 %copy-start.4 = (bf16[256,512]{1,0:T(8,128)(2,1)S(1)}, bf16[256,512]{1,0:T(8,128)(2,1)}, u32[]{:S(2)}) copy-start(bf16[256,512]{1,0:T(8,128)(2,1)} %param.17) | copy-start | bytes 786436
  1.5 6.6 %collective-permute-start.2 = (s32[8,8]{1,0:T(8,128)S(1)}, s32[8,8]{1,0:T(8,128)S(1)}, u32[]{:S(2)}, u32[]{:S(2)}) collective-permute-start(s32[8,8]{1,0:T(8,128)S(1)} %broadcast_select_fusion), channel_id=1, source_target_pairs={{0,12},{1,13},{2,14},{3,15},{4,8},{5,9},{6,10},{7,11},{8,4},{9,5},... | collective-permute-start | bytes 776 | tf_op jit(solution)/shard_map/ppermute | solution.py:474
  5.5 3.6 %collective-permute-start.1 = (s32[8,8]{1,0:T(8,128)S(1)}, s32[8,8]{1,0:T(8,128)S(1)}, u32[]{:S(2)}, u32[]{:S(2)}) collective-permute-start(s32[8,8]{1,0:T(8,128)S(1)} %broadcast_select_fusion), channel_id=1, source_target_pairs={{0,8},{1,9},{2,10},{3,11},{4,12},{5,13},{6,14},{7,15},{8,0},{9,1},... | collective-permute-start | bytes 776 | tf_op jit(solution)/shard_map/ppermute | solution.py:474
  6.0 3.6 %collective-permute-start = (s32[8,8]{1,0:T(8,128)S(1)}, s32[8,8]{1,0:T(8,128)S(1)}, u32[]{:S(2)}, u32[]{:S(2)}) collective-permute-start(s32[8,8]{1,0:T(8,128)S(1)} %broadcast_select_fusion), channel_id=1, source_target_pairs={{0,4},{1,5},{2,6},{3,7},{4,0},{5,1},{6,2},{7,3},{8,12},{9,13},{10,... | collective-permute-start | bytes 776 | tf_op jit(solution)/shard_map/ppermute | solution.py:474
  7.9 10.7 %copy-start.7 = (s32[512]{0:T(512)S(1)}, s32[512]{0:T(512)}, u32[]{:S(2)}) copy-start(s32[512]{0:T(512)} %param.12) | copy-start | bytes 6148
  7.9 10.7 %copy-start.8 = (s32[256]{0:T(256)S(1)}, s32[256]{0:T(256)}, u32[]{:S(2)}) copy-start(s32[256]{0:T(256)} %param.14) | copy-start | bytes 3076
  7.9 10.7 %copy-start.9 = (s32[256,1]{0,1:T(1,128)S(1)}, s32[256,1]{0,1:T(1,128)}, u32[]{:S(2)}) copy-start(s32[256,1]{0,1:T(1,128)} %param.13) | copy-start | bytes 3076
  9.7 4.5 %collective-permute-start.3 = (s32[8,8]{1,0:T(8,128)S(1)}, s32[8,8]{1,0:T(8,128)S(1)}, u32[]{:S(2)}, u32[]{:S(2)}) collective-permute-start(s32[8,8]{1,0:T(8,128)S(1)} %add_add_fusion), channel_id=1, source_target_pairs={{0,16},{1,17},{2,18},{3,19},{4,20},{5,21},{6,22},{7,23},{8,24},{9,... | collective-permute-start | bytes 776 | tf_op jit(solution)/shard_map/ppermute | solution.py:474
  14.9 10.6 %collective-permute-start.4 = (bf16[64,512]{1,0:T(8,128)(2,1)S(1)}, bf16[64,512]{1,0:T(8,128)(2,1)S(1)}, u32[]{:S(2)}, u32[]{:S(2)}) collective-permute-start(bf16[64,512]{1,0:T(8,128)(2,1)S(1)} %get-tuple-element.73), channel_id=1, source_target_pairs={{0,28},{1,13},{2,30},{3,15},{4,24},{5,9},{6,26},{7,11},{8,20},{9,5... | collective-permute-start | bytes 196616 | tf_op jit(solution)/shard_map/ppermute | solution.py:474
  18.5 7.5 %collective-permute-start.5 = (bf16[64,512]{1,0:T(8,128)(2,1)S(1)}, bf16[64,512]{1,0:T(8,128)(2,1)S(1)}, u32[]{:S(2)}, u32[]{:S(2)}) collective-permute-start(bf16[64,512]{1,0:T(8,128)(2,1)S(1)} %get-tuple-element.74), channel_id=1, source_target_pairs={{0,24},{1,9},{2,26},{3,11},{4,28},{5,13},{6,30},{7,15},{8,16},{9,1... | collective-permute-start | bytes 196616 | tf_op jit(solution)/shard_map/ppermute | solution.py:474
  20.0 11.5 %collective-permute-start.6 = (bf16[64,512]{1,0:T(8,128)(2,1)S(1)}, bf16[64,512]{1,0:T(8,128)(2,1)S(1)}, u32[]{:S(2)}, u32[]{:S(2)}) collective-permute-start(bf16[64,512]{1,0:T(8,128)(2,1)S(1)} %get-tuple-element.75), channel_id=1, source_target_pairs={{0,20},{1,5},{2,22},{3,7},{4,16},{5,1},{6,18},{7,3},{8,28},{9,13},... | collective-permute-start | bytes 196616 | tf_op jit(solution)/shard_map/ppermute | solution.py:474
  22.0 9.6 %collective-permute-start.7 = (bf16[64,512]{1,0:T(8,128)(2,1)S(1)}, bf16[64,512]{1,0:T(8,128)(2,1)S(1)}, u32[]{:S(2)}, u32[]{:S(2)}) collective-permute-start(bf16[64,512]{1,0:T(8,128)(2,1)S(1)} %get-tuple-element.76), channel_id=1, source_target_pairs={{0,16},{1,29},{2,18},{3,31},{4,20},{5,25},{6,22},{7,27},{8,24},{9,... | collective-permute-start | bytes 196616 | tf_op jit(solution)/shard_map/ppermute | solution.py:474
  24.1 7.5 %collective-permute-start.8 = (bf16[64,512]{1,0:T(8,128)(2,1)S(1)}, bf16[64,512]{1,0:T(8,128)(2,1)S(1)}, u32[]{:S(2)}, u32[]{:S(2)}) collective-permute-start(bf16[64,512]{1,0:T(8,128)(2,1)S(1)} %get-tuple-element.77), channel_id=1, source_target_pairs={{0,12},{1,25},{2,14},{3,27},{4,8},{5,29},{6,10},{7,31},{8,4},{9,17... | collective-permute-start | bytes 196616 | tf_op jit(solution)/shard_map/ppermute | solution.py:474
  25.4 6.1 %collective-permute-start.9 = (bf16[64,512]{1,0:T(8,128)(2,1)S(1)}, bf16[64,512]{1,0:T(8,128)(2,1)S(1)}, u32[]{:S(2)}, u32[]{:S(2)}) collective-permute-start(bf16[64,512]{1,0:T(8,128)(2,1)S(1)} %get-tuple-element.78), channel_id=1, source_target_pairs={{0,8},{1,21},{2,10},{3,23},{4,12},{5,17},{6,14},{7,19},{8,0},{9,29... | collective-permute-start | bytes 196616 | tf_op jit(solution)/shard_map/ppermute | solution.py:474
  26.0 5.6 %collective-permute-start.10 = (bf16[64,512]{1,0:T(8,128)(2,1)S(1)}, bf16[64,512]{1,0:T(8,128)(2,1)S(1)}, u32[]{:S(2)}, u32[]{:S(2)}) collective-permute-start(bf16[64,512]{1,0:T(8,128)(2,1)S(1)} %get-tuple-element.79), channel_id=1, source_target_pairs={{0,4},{1,17},{2,6},{3,19},{4,0},{5,21},{6,2},{7,23},{8,12},{9,25},... | collective-permute-start | bytes 196616 | tf_op jit(solution)/shard_map/ppermute | solution.py:474
  27.6 4.0 %copy-start = (s32[8]{0:T(128)S(1)}, s32[8]{0:T(128)}, u32[]{:S(2)}) copy-start(s32[8]{0:T(128)} %dest_ref.1) | copy-start | bytes 100
  27.6 4.0 %copy-start.1 = (s32[8]{0:T(128)S(1)}, s32[8]{0:T(128)}, u32[]{:S(2)}) copy-start(s32[8]{0:T(128)} %blocks_ref.1) | copy-start | bytes 100
  40.5 2.1 %collective-permute-start.11 = (bf16[16,16,1280]{2,1,0:T(8,128)(2,1)S(1)}, bf16[16,16,1280]{2,1,0:T(8,128)(2,1)S(1)}, u32[]{:S(2)}, u32[]{:S(2)}) collective-permute-start(bf16[16,16,1280]{2,1,0:T(8,128)(2,1)S(1)} %get-tuple-element.81), channel_id=1, source_target_pairs={{0,1},{1,0},{2,3},{3,2},{4,5},{5,4},{6,7},{7,6},{8,9},{9,8},{10,11... | collective-permute-start | bytes 1966088 | tf_op jit(solution)/shard_map/ppermute | solution.py:474
  40.5 3.0 %collective-permute-start.12 = (bf16[16,16,1280]{2,1,0:T(8,128)(2,1)S(1)}, bf16[16,16,1280]{2,1,0:T(8,128)(2,1)S(1)}, u32[]{:S(2)}, u32[]{:S(2)}) collective-permute-start(bf16[16,16,1280]{2,1,0:T(8,128)(2,1)S(1)} %get-tuple-element.83), channel_id=1, source_target_pairs={{0,1},{1,0},{2,3},{3,2},{4,5},{5,4},{6,7},{7,6},{8,9},{9,8},{10,11... | collective-permute-start | bytes 1966088 | tf_op jit(solution)/shard_map/ppermute | solution.py:474
  43.7 9.8 %collective-permute-start.15 = (bf16[8,16,1280]{2,1,0:T(8,128)(2,1)S(1)}, bf16[8,16,1280]{2,1,0:T(8,128)(2,1)S(1)}, u32[]{:S(2)}, u32[]{:S(2)}) collective-permute-start(bf16[8,16,1280]{2,1,0:T(8,128)(2,1)S(1)} %slice.47), channel_id=1, source_target_pairs={{0,4},{1,5},{2,6},{3,7},{4,0},{5,1},{6,2},{7,3},{8,12},{9,13},{10,... | collective-permute-start | bytes 983048 | tf_op jit(solution)/shard_map/ppermute | solution.py:474
  45.1 26.6 %all-to-all-start = ((bf16[4,8,16,640]{3,2,1,0:T(8,128)(2,1)}), bf16[4,8,16,640]{3,2,1,0:T(8,128)(2,1)S(1)}, u32[]{:S(2)}, u32[]{:S(2)}) async-start(bf16[4,8,16,640]{3,2,1,0:T(8,128)(2,1)} %bitcast.5), calls=%async_computation | async-start | bytes 1310720 | tf_op jit(solution)/shard_map/all_to_all | solution.py:477
  49.6 10.7 %collective-permute-start.13 = (bf16[8,16,1280]{2,1,0:T(8,128)(2,1)S(1)}, bf16[8,16,1280]{2,1,0:T(8,128)(2,1)S(1)}, u32[]{:S(2)}, u32[]{:S(2)}) collective-permute-start(bf16[8,16,1280]{2,1,0:T(8,128)(2,1)S(1)} %slice.43), channel_id=1, source_target_pairs={{0,2},{1,3},{2,0},{3,1},{4,6},{5,7},{6,4},{7,5},{8,10},{9,11},{10,... | collective-permute-start | bytes 983048 | tf_op jit(solution)/shard_map/ppermute | solution.py:474
  53.7 8.7 %collective-permute-start.16 = (bf16[4,16,1280]{2,1,0:T(8,128)(2,1)S(1)}, bf16[4,16,1280]{2,1,0:T(8,128)(2,1)S(1)}, u32[]{:S(2)}, u32[]{:S(2)}) collective-permute-start(bf16[4,16,1280]{2,1,0:T(8,128)(2,1)S(1)} %slice.59), channel_id=1, source_target_pairs={{0,2},{1,3},{2,0},{3,1},{4,6},{5,7},{6,4},{7,5},{8,10},{9,11},{10,... | collective-permute-start | bytes 491528 | tf_op jit(solution)/shard_map/ppermute | solution.py:474
  60.4 5.4 %collective-permute-start.14 = (bf16[4,16,1280]{2,1,0:T(8,128)(2,1)S(1)}, bf16[4,16,1280]{2,1,0:T(8,128)(2,1)S(1)}, u32[]{:S(2)}, u32[]{:S(2)}) collective-permute-start(bf16[4,16,1280]{2,1,0:T(8,128)(2,1)S(1)} %slice.57), channel_id=1, source_target_pairs={{0,4},{1,5},{2,6},{3,7},{4,0},{5,1},{6,2},{7,3},{8,12},{9,13},{10,... | collective-permute-start | bytes 491528 | tf_op jit(solution)/shard_map/ppermute | solution.py:474
  65.9 5.8 %collective-permute-start.17 = (bf16[2,16,2560]{2,1,0:T(8,128)(2,1)S(1)}, bf16[2,16,2560]{2,1,0:T(8,128)(2,1)S(1)}, u32[]{:S(2)}, u32[]{:S(2)}) collective-permute-start(bf16[2,16,2560]{2,1,0:T(8,128)(2,1)S(1)} %pad_maximum_fusion.5), channel_id=1, source_target_pairs={{0,8},{1,9},{2,10},{3,11},{4,12},{5,13},{6,14},{7,15},{8,0},{9,1},... | collective-permute-start | bytes 491528 | tf_op jit(solution)/shard_map/ppermute | solution.py:474
  71.8 7.4 %collective-permute-start.18 = (bf16[1,16,2560]{2,1,0:T(8,128)(2,1)S(1)}, bf16[1,16,2560]{2,1,0:T(8,128)(2,1)S(1)}, u32[]{:S(2)}, u32[]{:S(2)}) collective-permute-start(bf16[1,16,2560]{2,1,0:T(8,128)(2,1)S(1)} %slice.53), channel_id=1, source_target_pairs={{0,16},{1,17},{2,18},{3,19},{4,20},{5,21},{6,22},{7,23},{8,24},{9,... | collective-permute-start | bytes 245768 | tf_op jit(solution)/shard_map/ppermute | solution.py:474
  75.6 13.7 %all-to-all-start.1 = ((bf16[8,4,16,640]{3,2,1,0:T(8,128)(2,1)}), bf16[8,4,16,640]{3,2,1,0:T(8,128)(2,1)S(1)}, u32[]{:S(2)}, u32[]{:S(2)}) async-start(bf16[8,4,16,640]{3,2,1,0:T(8,128)(2,1)} %copy.20), calls=%async_computation.1 | async-start | bytes 1310720 | tf_op jit(solution)/shard_map/all_to_all | solution.py:477
  79.2 7.5 %collective-permute-start.19 = (bf16[1,16,2560]{2,1,0:T(8,128)(2,1)S(1)}, bf16[1,16,2560]{2,1,0:T(8,128)(2,1)S(1)}, u32[]{:S(2)}, u32[]{:S(2)}) collective-permute-start(bf16[1,16,2560]{2,1,0:T(8,128)(2,1)S(1)} %add_convert_fusion.7), channel_id=1, source_target_pairs={{0,16},{1,17},{2,18},{3,19},{4,20},{5,21},{6,22},{7,23},{8,24},{9,... | collective-permute-start | bytes 245768 | tf_op jit(solution)/shard_map/ppermute | solution.py:474
  89.3 5.9 %collective-permute-start.20 = (bf16[2,16,2560]{2,1,0:T(8,128)(2,1)S(1)}, bf16[2,16,2560]{2,1,0:T(8,128)(2,1)S(1)}, u32[]{:S(2)}, u32[]{:S(2)}) collective-permute-start(bf16[2,16,2560]{2,1,0:T(8,128)(2,1)S(1)} %pad_maximum_fusion.6), channel_id=1, source_target_pairs={{0,8},{1,9},{2,10},{3,11},{4,12},{5,13},{6,14},{7,15},{8,0},{9,1},... | collective-permute-start | bytes 491528 | tf_op jit(solution)/shard_map/ppermute | solution.py:474
  95.4 5.4 %collective-permute-start.21 = (bf16[4,16,1280]{2,1,0:T(8,128)(2,1)S(1)}, bf16[4,16,1280]{2,1,0:T(8,128)(2,1)S(1)}, u32[]{:S(2)}, u32[]{:S(2)}) collective-permute-start(bf16[4,16,1280]{2,1,0:T(8,128)(2,1)S(1)} %get-tuple-element.102), channel_id=1, source_target_pairs={{0,4},{1,5},{2,6},{3,7},{4,0},{5,1},{6,2},{7,3},{8,12},{9,13},{10,... | collective-permute-start | bytes 491528 | tf_op jit(solution)/shard_map/ppermute | solution.py:474
  96.3 6.0 %collective-permute-start.24 = (bf16[4,16,1280]{2,1,0:T(8,128)(2,1)S(1)}, bf16[4,16,1280]{2,1,0:T(8,128)(2,1)S(1)}, u32[]{:S(2)}, u32[]{:S(2)}) collective-permute-start(bf16[4,16,1280]{2,1,0:T(8,128)(2,1)S(1)} %get-tuple-element.101), channel_id=1, source_target_pairs={{0,2},{1,3},{2,0},{3,1},{4,6},{5,7},{6,4},{7,5},{8,10},{9,11},{10,... | collective-permute-start | bytes 491528 | tf_op jit(solution)/shard_map/ppermute | solution.py:474
  100.8 7.8 %collective-permute-start.22 = (bf16[8,16,1280]{2,1,0:T(8,128)(2,1)S(1)}, bf16[8,16,1280]{2,1,0:T(8,128)(2,1)S(1)}, u32[]{:S(2)}, u32[]{:S(2)}) collective-permute-start(bf16[8,16,1280]{2,1,0:T(8,128)(2,1)S(1)} %pad_maximum_fusion.3), channel_id=1, source_target_pairs={{0,2},{1,3},{2,0},{3,1},{4,6},{5,7},{6,4},{7,5},{8,10},{9,11},{10,... | collective-permute-start | bytes 983048 | tf_op jit(solution)/shard_map/ppermute | solution.py:474
  102.4 7.2 %collective-permute-start.25 = (bf16[8,16,1280]{2,1,0:T(8,128)(2,1)S(1)}, bf16[8,16,1280]{2,1,0:T(8,128)(2,1)S(1)}, u32[]{:S(2)}, u32[]{:S(2)}) collective-permute-start(bf16[8,16,1280]{2,1,0:T(8,128)(2,1)S(1)} %pad_maximum_fusion.4), channel_id=1, source_target_pairs={{0,4},{1,5},{2,6},{3,7},{4,0},{5,1},{6,2},{7,3},{8,12},{9,13},{10,... | collective-permute-start | bytes 983048 | tf_op jit(solution)/shard_map/ppermute | solution.py:474
  108.7 3.0 %collective-permute-start.23 = (bf16[16,16,1280]{2,1,0:T(8,128)(2,1)S(1)}, bf16[16,16,1280]{2,1,0:T(8,128)(2,1)S(1)}, u32[]{:S(2)}, u32[]{:S(2)}) collective-permute-start(bf16[16,16,1280]{2,1,0:T(8,128)(2,1)S(1)} %pad_maximum_fusion.left_ref), channel_id=1, source_target_pairs={{0,1},{1,0},{2,3},{3,2},{4,5},{5,4},{6,7},{7,6},{8,9},{9,8},{10,11... | collective-permute-start | bytes 1966088 | tf_op jit(solution)/shard_map/ppermute | solution.py:474
  109.7 2.2 %collective-permute-start.26 = (bf16[16,16,1280]{2,1,0:T(8,128)(2,1)S(1)}, bf16[16,16,1280]{2,1,0:T(8,128)(2,1)S(1)}, u32[]{:S(2)}, u32[]{:S(2)}) collective-permute-start(bf16[16,16,1280]{2,1,0:T(8,128)(2,1)S(1)} %pad_maximum_fusion.1.right_ref), channel_id=1, source_target_pairs={{0,1},{1,0},{2,3},{3,2},{4,5},{5,4},{6,7},{7,6},{8,9},{9,8},{10,11... | collective-permute-start | bytes 1966088 | tf_op jit(solution)/shard_map/ppermute | solution.py:474

commit v21 on v17

--- a/solution.py
+++ b/solution.py
@@ -573,8 +573,8 @@
     table_got = exchange(jnp.swapaxes(table_got, 0, 1), both, groups)
     for mask in away[1:]:
         kept = reduced(kept, mask)
-    back = plan.orders[0][: plan.near_steps - 1 : -1]
-    kept = gathered(kept, back[0])
+    for mask in reversed(away):
+        kept = gathered(kept, mask)
     kept, table_got = lax.optimization_barrier((kept, table_got))
     table_part, grad_gain_in, grad_gain_out = call(
         functools.partial(table_body, plan),
@@ -585,11 +585,10 @@
         ),
         [VMEM],
     )(table_got.reshape(devices_all * plan.capacity, -1))
-    for mask in back[1:]:
-        kept = gathered(kept, mask)
-    kept, table_part = lax.optimization_barrier((kept, table_part))
     sides = [kept[..., : plan.split], kept[..., plan.split :]]
     for step in reversed(range(plan.near_steps)):
+        if step == 0:
+            *sides, table_part = lax.optimization_barrier((*sides, table_part))
         sides = [gathered(sides[side], plan.orders[side][step]) for side in range(2)]
     came = [swap(side, 1) for side in sides]
     rows = width // 2

time: 111 us -> 114 us (1.027)
  waiting for transfers between devices: 39.1 us -> 43.7 us
    ppermute x27, waiting for transfers between devices: 36.5 us -> 40.3 us  [swap(): return lax.ppermute(values, both, pairs)]
    ppermute x27, starting transfers between devices: 34 us -> 32.1 us  [swap(): return lax.ppermute(values, both, pairs)]
    unnamed x18 -> x22, local copies, waits for them, and re-layouts: 2.74 us -> 1.84 us
  transfers between devices with their start and end apart: 29 -> 29, of which waited for: 17 -> 17; matrix products, arithmetic and copies ran while one was open for 5% -> 4% of each run, Pallas kernels for 9% -> 8%
where the time goes in v21:
time: 114 us; the launch traced here: 113 us
  waiting for transfers between devices  43.7 us (38%)
  starting transfers between devices  41.7 us (37%)
  Pallas kernels  21 us (18%)
  local copies, waits for them, and re-layouts  3.9 us (3%)
  other arithmetic  1.86 us (2%)
  between operations  1.2 us (1%)
    ppermute x27, waiting for transfers between devices, swap(): return lax.ppermute(values, both, pairs)  40.3 us
    ppermute x27, starting transfers between devices, swap(): return lax.ppermute(values, both, pairs)  32.1 us
    all_to_all x2, starting transfers between devices, exchange(): lax.all_to_all(values, axes, split_axis=0, concat_axis=0, tiled=True, axi...  9.57 us
    pallas_call x1, Pallas kernels, on_device(): call(functools.partial(backward_body, plan, table_size, total_factor), ou...  8.85 us
    pallas_call x2, Pallas kernels, on_device(): pl.pallas_call(functools.partial(widen_body, plan, turn), out_shape=outs,...  3.92 us
    pallas_call x1, Pallas kernels, on_device(): call(forward_body, list(shapes.values()), [VMEM] * 3, flops=4 * count * w...  3.92 us
    all_to_all x2, waiting for transfers between devices, exchange(): lax.all_to_all(values, axes, split_axis=0, concat_axis=0, tiled=True, axi...  3.36 us
  transfers between devices with their start and end apart: 29, of which 17 were waited for; matrix products, arithmetic and copies ran while one was open for 4% of the time, Pallas kernels for 8%

profile of v21, /device:TPU:0, one launch (start us, length us, event | category | flops | bytes accessed | tf_op | source)
XLA Modules:
  0.0 113.3 jit_solution(6382526497446631543)
XLA Ops:
  0.7 0.8 select_reduce_fusion
  1.6 4.0 %collective-permute-start.2 = (s32[8,8]{1,0:T(8,128)S(1)}, s32[8,8]{1,0:T(8,128)S(1)}, u32[]{:S(2)}, u32[]{:S(2)}) collective-permute-start(s32[8,8]{1,0:T(8,128)S(1)} %broadcast_select_fusion), channel_id=1, source_target_pairs={{0,12},{1,13},{2,14},{3,15},{4,8},{5,9},{6,10},{7,11},{8,4},{9,5},... | collective-permute-start | bytes 776 | tf_op jit(solution)/shard_map/ppermute | solution.py:476
  6.2 1.7 %constant_dynamic-update-slice_fusion.1 = bf16[512,2560]{1,0:T(8,128)(2,1)S(1)} fusion(bf16[512,2048]{1,0:T(8,128)(2,1)} %param.18), kind=kLoop, calls=%fused_computation.17 | loop fusion | bytes 4194304
  8.1 1.1 collective-permute-done.1
  9.7 2.6 %collective-permute-start.3 = (s32[8,8]{1,0:T(8,128)S(1)}, s32[8,8]{1,0:T(8,128)S(1)}, u32[]{:S(2)}, u32[]{:S(2)}) collective-permute-start(s32[8,8]{1,0:T(8,128)S(1)} %add_add_fusion), channel_id=1, source_target_pairs={{0,16},{1,17},{2,18},{3,19},{4,20},{5,21},{6,22},{7,23},{8,24},{9,... | collective-permute-start | bytes 776 | tf_op jit(solution)/shard_map/ppermute | solution.py:476
  12.3 1.0 constant_dynamic-update-slice_fusion.2.rows_ref
  13.3 0.9 collective-permute-done.3
  14.2 0.7 shard_map.147
  14.9 3.6 %collective-permute-start.4 = (bf16[64,512]{1,0:T(8,128)(2,1)S(1)}, bf16[64,512]{1,0:T(8,128)(2,1)S(1)}, u32[]{:S(2)}, u32[]{:S(2)}) collective-permute-start(bf16[64,512]{1,0:T(8,128)(2,1)S(1)} %get-tuple-element.74), channel_id=1, source_target_pairs={{0,28},{1,13},{2,30},{3,15},{4,24},{5,9},{6,26},{7,11},{8,20},{9,5... | collective-permute-start | bytes 196616 | tf_op jit(solution)/shard_map/ppermute | solution.py:476
  18.7 1.4 %shard_map.146 = (bf16[256,2560]{1,0:T(8,128)(2,1)S(1)}, bf16[512,256]{1,0:T(8,128)(2,1)S(1)}, bf16[256,2048]{1,0:T(8,128)(2,1)S(1)}, f32[256,512]{1,0:T(8,128)S...) custom-call(bf16[512,512]{1,0:T(8,128)(2,1)S(1)} %constant_dynamic-update-slice_fusion.2.rows_ref, ...), custom_call_target="tpu_custom_call" | custom-call | flops 536870912 | bytes 4000000 | tf_op jit(solution)/shard_map/pallas_call | solution.py:507
  20.1 1.9 %collective-permute-start.6 = (bf16[64,512]{1,0:T(8,128)(2,1)S(1)}, bf16[64,512]{1,0:T(8,128)(2,1)S(1)}, u32[]{:S(2)}, u32[]{:S(2)}) collective-permute-start(bf16[64,512]{1,0:T(8,128)(2,1)S(1)} %get-tuple-element.76), channel_id=1, source_target_pairs={{0,20},{1,5},{2,22},{3,7},{4,16},{5,1},{6,18},{7,3},{8,28},{9,13},... | collective-permute-start | bytes 196616 | tf_op jit(solution)/shard_map/ppermute | solution.py:476
  22.0 2.1 %collective-permute-start.7 = (bf16[64,512]{1,0:T(8,128)(2,1)S(1)}, bf16[64,512]{1,0:T(8,128)(2,1)S(1)}, u32[]{:S(2)}, u32[]{:S(2)}) collective-permute-start(bf16[64,512]{1,0:T(8,128)(2,1)S(1)} %get-tuple-element.77), channel_id=1, source_target_pairs={{0,16},{1,29},{2,18},{3,31},{4,20},{5,25},{6,22},{7,27},{8,24},{9,... | collective-permute-start | bytes 196616 | tf_op jit(solution)/shard_map/ppermute | solution.py:476
  24.2 1.3 %collective-permute-start.8 = (bf16[64,512]{1,0:T(8,128)(2,1)S(1)}, bf16[64,512]{1,0:T(8,128)(2,1)S(1)}, u32[]{:S(2)}, u32[]{:S(2)}) collective-permute-start(bf16[64,512]{1,0:T(8,128)(2,1)S(1)} %get-tuple-element.78), channel_id=1, source_target_pairs={{0,12},{1,25},{2,14},{3,27},{4,8},{5,29},{6,10},{7,31},{8,4},{9,17... | collective-permute-start | bytes 196616 | tf_op jit(solution)/shard_map/ppermute | solution.py:476
  25.5 0.6 collective-permute-start.9
  26.0 1.6 %collective-permute-start.10 = (bf16[64,512]{1,0:T(8,128)(2,1)S(1)}, bf16[64,512]{1,0:T(8,128)(2,1)S(1)}, u32[]{:S(2)}, u32[]{:S(2)}) collective-permute-start(bf16[64,512]{1,0:T(8,128)(2,1)S(1)} %get-tuple-element.80), channel_id=1, source_target_pairs={{0,4},{1,17},{2,6},{3,19},{4,0},{5,21},{6,2},{7,23},{8,12},{9,25},... | collective-permute-start | bytes 196616 | tf_op jit(solution)/shard_map/ppermute | solution.py:476
  27.7 3.9 %shard_map.148 = (f32[512,512]{1,0:T(8,128)S(1)}, f32[512,512]{1,0:T(8,128)S(1)}, f32[512,1]{1,0:T(8,128)S(1)}, bf16[512,1536]{1,0:T(8,128)(2,1)S(1)}, bf16[16,1...) custom-call(bf16[256,2560]{1,0:T(8,128)(2,1)S(1)} %get-tuple-element, ...), custom_call_target="tpu_custom_call" | custom-call | flops 2684354560 | bytes 8000000 | tf_op jit(solution)/shard_map/pallas_call | solution.py:517
  31.7 8.9 %shard_map.149 = (bf16[512,640]{1,0:T(8,128)(2,1)}, bf16[16,16,1536]{2,1,0:T(8,128)(2,1)S(1)}, bf16[16,16,1536]{2,1,0:T(8,128)(2,1)S(1)}, bf16[16,16,1024]{2,1,0:T(8,128)(2,1)S(1)}, bf16[16,16,1024]{2,1,0:T(8,128)(2,1)S(1)}) custom-call(s32[1]{0:T(128)} %bitcast.me_ref, s32[8]{0:T(128)S(1)} %copy-done, s32[8]{0:T(128)S(1)} %copy-done.1, ...), custom_call_target="tpu_custom_call" | custom-call | flops 10737418240 | bytes 12000000 | tf_op jit(solution)/shard_map/pallas_call | solution.py:530
  41.0 1.4 %collective-permute-done.12 = bf16[16,16,1024]{2,1,0:T(8,128)(2,1)S(1)} collective-permute-done((bf16[16,16,1024]{2,1,0:T(8,128)(2,1)S(1)}, bf16[16,16,1024]{2,1,0:T(8,128)(2,1)S(1)}, u32[]{:S(2)}, u32[]{:S(2)}) %collective-permute-start.12) | collective-permute-done | bytes 524320 | tf_op jit(solution)/shard_map/ppermute | solution.py:476
  42.6 0.9 collective-permute-done.11
  43.8 1.4 %collective-permute-start.15 = (bf16[8,16,1024]{2,1,0:T(8,128)(2,1)S(1)}, bf16[8,16,1024]{2,1,0:T(8,128)(2,1)S(1)}, u32[]{:S(2)}, u32[]{:S(2)}) collective-permute-start(bf16[8,16,1024]{2,1,0:T(8,128)(2,1)S(1)} %slice.47), channel_id=1, source_target_pairs={{0,4},{1,5},{2,6},{3,7},{4,0},{5,1},{6,2},{7,3},{8,12},{9,13},{10,... | collective-permute-start | bytes 786440 | tf_op jit(solution)/shard_map/ppermute | solution.py:476
  45.3 1.6 %collective-permute-start.13 = (bf16[8,16,1536]{2,1,0:T(8,128)(2,1)S(1)}, bf16[8,16,1536]{2,1,0:T(8,128)(2,1)S(1)}, u32[]{:S(2)}, u32[]{:S(2)}) collective-permute-start(bf16[8,16,1536]{2,1,0:T(8,128)(2,1)S(1)} %slice.43), channel_id=1, source_target_pairs={{0,2},{1,3},{2,0},{3,1},{4,6},{5,7},{6,4},{7,5},{8,10},{9,11},{10,... | collective-permute-start | bytes 1179656 | tf_op jit(solution)/shard_map/ppermute | solution.py:476
  46.9 4.5 %all-to-all-start = ((bf16[4,8,16,640]{3,2,1,0:T(8,128)(2,1)}), bf16[4,8,16,640]{3,2,1,0:T(8,128)(2,1)S(1)}, u32[]{:S(2)}, u32[]{:S(2)}) async-start(bf16[4,8,16,640]{3,2,1,0:T(8,128)(2,1)} %bitcast.5), calls=%async_computation | async-start | bytes 1310720 | tf_op jit(solution)/shard_map/all_to_all | solution.py:479
  51.3 0.9 collective-permute-done.15
  52.3 1.6 %collective-permute-start.16 = (bf16[4,16,1024]{2,1,0:T(8,128)(2,1)S(1)}, bf16[4,16,1024]{2,1,0:T(8,128)(2,1)S(1)}, u32[]{:S(2)}, u32[]{:S(2)}) collective-permute-start(bf16[4,16,1024]{2,1,0:T(8,128)(2,1)S(1)} %slice.59), channel_id=1, source_target_pairs={{0,2},{1,3},{2,0},{3,1},{4,6},{5,7},{6,4},{7,5},{8,10},{9,11},{10,... | collective-permute-start | bytes 393224 | tf_op jit(solution)/shard_map/ppermute | solution.py:476
  53.9 3.4 %collective-permute-done.13 = bf16[8,16,1536]{2,1,0:T(8,128)(2,1)S(1)} collective-permute-done((bf16[8,16,1536]{2,1,0:T(8,128)(2,1)S(1)}, bf16[8,16,1536]{2,1,0:T(8,128)(2,1)S(1)}, u32[]{:S(2)}, u32[]{:S(2)}) %collective-permute-start.13) | collective-permute-done | bytes 393248 | tf_op jit(solution)/shard_map/ppermute | solution.py:476
  57.5 0.7 collective-permute-start.14
  58.2 0.8 collective-permute-done.16
  59.1 4.1 %collective-permute-done.14 = bf16[4,16,1536]{2,1,0:T(8,128)(2,1)S(1)} collective-permute-done((bf16[4,16,1536]{2,1,0:T(8,128)(2,1)S(1)}, bf16[4,16,1536]{2,1,0:T(8,128)(2,1)S(1)}, u32[]{:S(2)}, u32[]{:S(2)}) %collective-permute-start.14) | collective-permute-done | bytes 196640 | tf_op jit(solution)/shard_map/ppermute | solution.py:476
  63.3 0.6 collective-permute-start.17
  63.9 6.2 %collective-permute-done.17 = bf16[2,16,2560]{2,1,0:T(8,128)(2,1)S(1)} collective-permute-done((bf16[2,16,2560]{2,1,0:T(8,128)(2,1)S(1)}, bf16[2,16,2560]{2,1,0:T(8,128)(2,1)S(1)}, u32[]{:S(2)}, u32[]{:S(2)}) %collective-permute-start.17) | collective-permute-done | bytes 163872 | tf_op jit(solution)/shard_map/ppermute | solution.py:476
  70.2 0.5 collective-permute-start.18
  70.7 5.5 %collective-permute-done.18 = bf16[1,16,2560]{2,1,0:T(8,128)(2,1)S(1)} collective-permute-done((bf16[1,16,2560]{2,1,0:T(8,128)(2,1)S(1)}, bf16[1,16,2560]{2,1,0:T(8,128)(2,1)S(1)}, u32[]{:S(2)}, u32[]{:S(2)}) %collective-permute-start.18) | collective-permute-done | bytes 81952 | tf_op jit(solution)/shard_map/ppermute | solution.py:476
  76.2 0.9 copy.20
  77.1 5.1 %all-to-all-start.1 = ((bf16[8,4,16,640]{3,2,1,0:T(8,128)(2,1)}), bf16[8,4,16,640]{3,2,1,0:T(8,128)(2,1)S(1)}, u32[]{:S(2)}, u32[]{:S(2)}) async-start(bf16[8,4,16,640]{3,2,1,0:T(8,128)(2,1)} %copy.20), calls=%async_computation.1 | async-start | bytes 1310720 | tf_op jit(solution)/shard_map/all_to_all | solution.py:479
  82.3 2.0 %collective-permute-start.20 = (bf16[2,16,2560]{2,1,0:T(8,128)(2,1)S(1)}, bf16[2,16,2560]{2,1,0:T(8,128)(2,1)S(1)}, u32[]{:S(2)}, u32[]{:S(2)}) collective-permute-start(bf16[2,16,2560]{2,1,0:T(8,128)(2,1)S(1)} %pad_maximum_fusion.4), channel_id=1, source_target_pairs={{0,8},{1,9},{2,10},{3,11},{4,12},{5,13},{6,14},{7,15},{8,0},{9,1},... | collective-permute-start | bytes 491528 | tf_op jit(solution)/shard_map/ppermute | solution.py:476
  84.3 4.9 %collective-permute-done.20 = bf16[2,16,2560]{2,1,0:T(8,128)(2,1)S(1)} collective-permute-done((bf16[2,16,2560]{2,1,0:T(8,128)(2,1)S(1)}, bf16[2,16,2560]{2,1,0:T(8,128)(2,1)S(1)}, u32[]{:S(2)}, u32[]{:S(2)}) %collective-permute-start.20) | collective-permute-done | bytes 163872 | tf_op jit(solution)/shard_map/ppermute | solution.py:476
  89.2 3.4 %all-to-all-done.1 = bf16[8,4,16,640]{3,2,1,0:T(8,128)(2,1)S(1)} async-done(((bf16[8,4,16,640]{3,2,1,0:T(8,128)(2,1)}), bf16[8,4,16,640]{3,2,1,0:T(8,128)(2,1)S(1)}, u32[]{:S(2)}, u32[]{:S(2)}) %all-to-all-start.1) | async-done | bytes 655392 | tf_op jit(solution)/shard_map/all_to_all | solution.py:479
  92.5 1.5 %collective-permute-start.22 = (bf16[4,16,1280]{2,1,0:T(8,128)(2,1)S(1)}, bf16[4,16,1280]{2,1,0:T(8,128)(2,1)S(1)}, u32[]{:S(2)}, u32[]{:S(2)}) collective-permute-start(bf16[4,16,1280]{2,1,0:T(8,128)(2,1)S(1)} %get-tuple-element.103), channel_id=1, source_target_pairs={{0,2},{1,3},{2,0},{3,1},{4,6},{5,7},{6,4},{7,5},{8,10},{9,11},{10,... | collective-permute-start | bytes 491528 | tf_op jit(solution)/shard_map/ppermute | solution.py:476
  94.1 0.6 collective-permute-start.21
  94.6 2.2 %shard_map.150 = (f32[1024,512]{1,0:T(8,128)}, f32[1,512]{1,0:T(1,128)}, f32[1,512]{1,0:T(1,128)}) custom-call(bf16[512,640]{1,0:T(8,128)(2,1)S(1)} %bitcast.10), custom_call_target="tpu_custom_call" | custom-call | tf_op jit(solution)/shard_map/pallas_call | solution.py:579
  96.8 1.6 %collective-permute-done.22 = bf16[4,16,1280]{2,1,0:T(8,128)(2,1)S(1)} collective-permute-done((bf16[4,16,1280]{2,1,0:T(8,128)(2,1)S(1)}, bf16[4,16,1280]{2,1,0:T(8,128)(2,1)S(1)}, u32[]{:S(2)}, u32[]{:S(2)}) %collective-permute-start.22) | collective-permute-done | bytes 163872 | tf_op jit(solution)/shard_map/ppermute | solution.py:476
  98.4 1.1 %collective-permute-done.21 = bf16[4,16,1280]{2,1,0:T(8,128)(2,1)S(1)} collective-permute-done((bf16[4,16,1280]{2,1,0:T(8,128)(2,1)S(1)}, bf16[4,16,1280]{2,1,0:T(8,128)(2,1)S(1)}, u32[]{:S(2)}, u32[]{:S(2)}) %collective-permute-start.21) | collective-permute-done | bytes 163872 | tf_op jit(solution)/shard_map/ppermute | solution.py:476
  99.6 0.6 collective-permute-start.23
  100.2 1.3 %collective-permute-start.25 = (bf16[8,16,1280]{2,1,0:T(8,128)(2,1)S(1)}, bf16[8,16,1280]{2,1,0:T(8,128)(2,1)S(1)}, u32[]{:S(2)}, u32[]{:S(2)}) collective-permute-start(bf16[8,16,1280]{2,1,0:T(8,128)(2,1)S(1)} %pad_maximum_fusion.2), channel_id=1, source_target_pairs={{0,4},{1,5},{2,6},{3,7},{4,0},{5,1},{6,2},{7,3},{8,12},{9,13},{10,... | collective-permute-start | bytes 983048 | tf_op jit(solution)/shard_map/ppermute | solution.py:476
  101.6 6.5 %collective-permute-done.25 = bf16[8,16,1280]{2,1,0:T(8,128)(2,1)S(1)} collective-permute-done((bf16[8,16,1280]{2,1,0:T(8,128)(2,1)S(1)}, bf16[8,16,1280]{2,1,0:T(8,128)(2,1)S(1)}, u32[]{:S(2)}, u32[]{:S(2)}) %collective-permute-start.25) | collective-permute-done | bytes 327712 | tf_op jit(solution)/shard_map/ppermute | solution.py:476
  108.2 0.5 collective-permute-start.24
  108.7 2.0 %shard_map.151 = (f32[512,2048]{1,0:T(8,128)}, f32[512,512]{1,0:T(8,128)}) custom-call(s32[1]{0:T(128)} %bitcast.me_ref, bf16[16,16,1280]{2,1,0:T(8,128)(2,1)S(1)} %constant_dynamic-update-slice_fusion.4.left_ref, bf16[16,16,1280]{2,1,0:T(8,128)(2,1)S(1)} %constant_dynamic-update-slice_fusion.6.right_ref), custom_call_target="tpu_custom_call" | custom-call | bytes 4000000 | tf_op jit(solution)/shard_map/pallas_call | solution.py:598
  111.2 2.0 %shard_map.152 = (f32[512,2048]{1,0:T(8,128)}, f32[512,512]{1,0:T(8,128)}) custom-call(s32[1]{0:T(128)} %bitcast.me_ref, bf16[16,16,1280]{2,1,0:T(8,128)(2,1)S(1)} %collective-permute-done.24.left_ref, bf16[16,16,1280]{2,1,0:T(8,128)(2,1)S(1)} %collective-permute-done.26.right_ref, ...), custom_call_target="tpu_custom_call", output_to_operand_aliasing={{0}: (3, {}), {1}: (4, {})} | custom-call | bytes 4000000 | tf_op jit(solution)/shard_map/pallas_call | solution.py:598
  (70 shorter events, 3.7 us)
Async XLA Ops:
  0.6 7.4 %copy-start.4 = (f32[512]{0:T(512)S(1)}, f32[512]{0:T(512)}, u32[]{:S(2)}) copy-start(f32[512]{0:T(512)} %param.21) | copy-start | bytes 6148
  0.6 7.4 %copy-start.5 = (f32[512]{0:T(512)S(1)}, f32[512]{0:T(512)}, u32[]{:S(2)}) copy-start(f32[512]{0:T(512)} %param.20) | copy-start | bytes 6148
  0.7 7.4 %copy-start.2 = (bf16[512,512]{1,0:T(8,128)(2,1)S(1)}, bf16[512,512]{1,0:T(8,128)(2,1)}, u32[]{:S(2)}) copy-start(bf16[512,512]{1,0:T(8,128)(2,1)} %param.19) | copy-start | bytes 1572868
  1.6 10.8 %copy-start.3 = (bf16[256,512]{1,0:T(8,128)(2,1)S(1)}, bf16[256,512]{1,0:T(8,128)(2,1)}, u32[]{:S(2)}) copy-start(bf16[256,512]{1,0:T(8,128)(2,1)} %param.11) | copy-start | bytes 786436
  1.6 17.1 %copy-start.6 = (s32[512]{0:T(512)S(1)}, s32[512]{0:T(512)}, u32[]{:S(2)}) copy-start(s32[512]{0:T(512)} %param.12) | copy-start | bytes 6148
  1.6 17.1 %copy-start.7 = (s32[256]{0:T(256)S(1)}, s32[256]{0:T(256)}, u32[]{:S(2)}) copy-start(s32[256]{0:T(256)} %param.14) | copy-start | bytes 3076
  1.6 17.1 %copy-start.8 = (s32[256,1]{0,1:T(1,128)S(1)}, s32[256,1]{0,1:T(1,128)}, u32[]{:S(2)}) copy-start(s32[256,1]{0,1:T(1,128)} %param.13) | copy-start | bytes 3076
  1.6 6.5 %collective-permute-start.2 = (s32[8,8]{1,0:T(8,128)S(1)}, s32[8,8]{1,0:T(8,128)S(1)}, u32[]{:S(2)}, u32[]{:S(2)}) collective-permute-start(s32[8,8]{1,0:T(8,128)S(1)} %broadcast_select_fusion), channel_id=1, source_target_pairs={{0,12},{1,13},{2,14},{3,15},{4,8},{5,9},{6,10},{7,11},{8,4},{9,5},... | collective-permute-start | bytes 776 | tf_op jit(solution)/shard_map/ppermute | solution.py:476
  5.6 3.6 %collective-permute-start.1 = (s32[8,8]{1,0:T(8,128)S(1)}, s32[8,8]{1,0:T(8,128)S(1)}, u32[]{:S(2)}, u32[]{:S(2)}) collective-permute-start(s32[8,8]{1,0:T(8,128)S(1)} %broadcast_select_fusion), channel_id=1, source_target_pairs={{0,8},{1,9},{2,10},{3,11},{4,12},{5,13},{6,14},{7,15},{8,0},{9,1},... | collective-permute-start | bytes 776 | tf_op jit(solution)/shard_map/ppermute | solution.py:476
  6.0 3.6 %collective-permute-start = (s32[8,8]{1,0:T(8,128)S(1)}, s32[8,8]{1,0:T(8,128)S(1)}, u32[]{:S(2)}, u32[]{:S(2)}) collective-permute-start(s32[8,8]{1,0:T(8,128)S(1)} %broadcast_select_fusion), channel_id=1, source_target_pairs={{0,4},{1,5},{2,6},{3,7},{4,0},{5,1},{6,2},{7,3},{8,12},{9,13},{10,... | collective-permute-start | bytes 776 | tf_op jit(solution)/shard_map/ppermute | solution.py:476
  9.7 4.5 %collective-permute-start.3 = (s32[8,8]{1,0:T(8,128)S(1)}, s32[8,8]{1,0:T(8,128)S(1)}, u32[]{:S(2)}, u32[]{:S(2)}) collective-permute-start(s32[8,8]{1,0:T(8,128)S(1)} %add_add_fusion), channel_id=1, source_target_pairs={{0,16},{1,17},{2,18},{3,19},{4,20},{5,21},{6,22},{7,23},{8,24},{9,... | collective-permute-start | bytes 776 | tf_op jit(solution)/shard_map/ppermute | solution.py:476
  14.9 10.5 %collective-permute-start.4 = (bf16[64,512]{1,0:T(8,128)(2,1)S(1)}, bf16[64,512]{1,0:T(8,128)(2,1)S(1)}, u32[]{:S(2)}, u32[]{:S(2)}) collective-permute-start(bf16[64,512]{1,0:T(8,128)(2,1)S(1)} %get-tuple-element.74), channel_id=1, source_target_pairs={{0,28},{1,13},{2,30},{3,15},{4,24},{5,9},{6,26},{7,11},{8,20},{9,5... | collective-permute-start | bytes 196616 | tf_op jit(solution)/shard_map/ppermute | solution.py:476
  18.6 7.5 %collective-permute-start.5 = (bf16[64,512]{1,0:T(8,128)(2,1)S(1)}, bf16[64,512]{1,0:T(8,128)(2,1)S(1)}, u32[]{:S(2)}, u32[]{:S(2)}) collective-permute-start(bf16[64,512]{1,0:T(8,128)(2,1)S(1)} %get-tuple-element.75), channel_id=1, source_target_pairs={{0,24},{1,9},{2,26},{3,11},{4,28},{5,13},{6,30},{7,15},{8,16},{9,1... | collective-permute-start | bytes 196616 | tf_op jit(solution)/shard_map/ppermute | solution.py:476
  20.1 11.5 %collective-permute-start.6 = (bf16[64,512]{1,0:T(8,128)(2,1)S(1)}, bf16[64,512]{1,0:T(8,128)(2,1)S(1)}, u32[]{:S(2)}, u32[]{:S(2)}) collective-permute-start(bf16[64,512]{1,0:T(8,128)(2,1)S(1)} %get-tuple-element.76), channel_id=1, source_target_pairs={{0,20},{1,5},{2,22},{3,7},{4,16},{5,1},{6,18},{7,3},{8,28},{9,13},... | collective-permute-start | bytes 196616 | tf_op jit(solution)/shard_map/ppermute | solution.py:476
  22.0 9.6 %collective-permute-start.7 = (bf16[64,512]{1,0:T(8,128)(2,1)S(1)}, bf16[64,512]{1,0:T(8,128)(2,1)S(1)}, u32[]{:S(2)}, u32[]{:S(2)}) collective-permute-start(bf16[64,512]{1,0:T(8,128)(2,1)S(1)} %get-tuple-element.77), channel_id=1, source_target_pairs={{0,16},{1,29},{2,18},{3,31},{4,20},{5,25},{6,22},{7,27},{8,24},{9,... | collective-permute-start | bytes 196616 | tf_op jit(solution)/shard_map/ppermute | solution.py:476
  24.2 7.4 %collective-permute-start.8 = (bf16[64,512]{1,0:T(8,128)(2,1)S(1)}, bf16[64,512]{1,0:T(8,128)(2,1)S(1)}, u32[]{:S(2)}, u32[]{:S(2)}) collective-permute-start(bf16[64,512]{1,0:T(8,128)(2,1)S(1)} %get-tuple-element.78), channel_id=1, source_target_pairs={{0,12},{1,25},{2,14},{3,27},{4,8},{5,29},{6,10},{7,31},{8,4},{9,17... | collective-permute-start | bytes 196616 | tf_op jit(solution)/shard_map/ppermute | solution.py:476
  25.5 6.1 %collective-permute-start.9 = (bf16[64,512]{1,0:T(8,128)(2,1)S(1)}, bf16[64,512]{1,0:T(8,128)(2,1)S(1)}, u32[]{:S(2)}, u32[]{:S(2)}) collective-permute-start(bf16[64,512]{1,0:T(8,128)(2,1)S(1)} %get-tuple-element.79), channel_id=1, source_target_pairs={{0,8},{1,21},{2,10},{3,23},{4,12},{5,17},{6,14},{7,19},{8,0},{9,29... | collective-permute-start | bytes 196616 | tf_op jit(solution)/shard_map/ppermute | solution.py:476
  26.0 5.6 %collective-permute-start.10 = (bf16[64,512]{1,0:T(8,128)(2,1)S(1)}, bf16[64,512]{1,0:T(8,128)(2,1)S(1)}, u32[]{:S(2)}, u32[]{:S(2)}) collective-permute-start(bf16[64,512]{1,0:T(8,128)(2,1)S(1)} %get-tuple-element.80), channel_id=1, source_target_pairs={{0,4},{1,17},{2,6},{3,19},{4,0},{5,21},{6,2},{7,23},{8,12},{9,25},... | collective-permute-start | bytes 196616 | tf_op jit(solution)/shard_map/ppermute | solution.py:476
  27.7 4.0 %copy-start = (s32[8]{0:T(128)S(1)}, s32[8]{0:T(128)}, u32[]{:S(2)}) copy-start(s32[8]{0:T(128)} %dest_ref.1) | copy-start | bytes 100
  27.7 4.0 %copy-start.1 = (s32[8]{0:T(128)S(1)}, s32[8]{0:T(128)}, u32[]{:S(2)}) copy-start(s32[8]{0:T(128)} %blocks_ref.1) | copy-start | bytes 100
  40.5 1.9 %collective-permute-start.12 = (bf16[16,16,1024]{2,1,0:T(8,128)(2,1)S(1)}, bf16[16,16,1024]{2,1,0:T(8,128)(2,1)S(1)}, u32[]{:S(2)}, u32[]{:S(2)}) collective-permute-start(bf16[16,16,1024]{2,1,0:T(8,128)(2,1)S(1)} %get-tuple-element.84), channel_id=1, source_target_pairs={{0,1},{1,0},{2,3},{3,2},{4,5},{5,4},{6,7},{7,6},{8,9},{9,8},{10,11... | collective-permute-start | bytes 1572872 | tf_op jit(solution)/shard_map/ppermute | solution.py:476
  40.5 3.0 %collective-permute-start.11 = (bf16[16,16,1536]{2,1,0:T(8,128)(2,1)S(1)}, bf16[16,16,1536]{2,1,0:T(8,128)(2,1)S(1)}, u32[]{:S(2)}, u32[]{:S(2)}) collective-permute-start(bf16[16,16,1536]{2,1,0:T(8,128)(2,1)S(1)} %get-tuple-element.82), channel_id=1, source_target_pairs={{0,1},{1,0},{2,3},{3,2},{4,5},{5,4},{6,7},{7,6},{8,9},{9,8},{10,11... | collective-permute-start | bytes 2359304 | tf_op jit(solution)/shard_map/ppermute | solution.py:476
  43.8 8.4 %collective-permute-start.15 = (bf16[8,16,1024]{2,1,0:T(8,128)(2,1)S(1)}, bf16[8,16,1024]{2,1,0:T(8,128)(2,1)S(1)}, u32[]{:S(2)}, u32[]{:S(2)}) collective-permute-start(bf16[8,16,1024]{2,1,0:T(8,128)(2,1)S(1)} %slice.47), channel_id=1, source_target_pairs={{0,4},{1,5},{2,6},{3,7},{4,0},{5,1},{6,2},{7,3},{8,12},{9,13},{10,... | collective-permute-start | bytes 786440 | tf_op jit(solution)/shard_map/ppermute | solution.py:476
  45.3 12.1 %collective-permute-start.13 = (bf16[8,16,1536]{2,1,0:T(8,128)(2,1)S(1)}, bf16[8,16,1536]{2,1,0:T(8,128)(2,1)S(1)}, u32[]{:S(2)}, u32[]{:S(2)}) collective-permute-start(bf16[8,16,1536]{2,1,0:T(8,128)(2,1)S(1)} %slice.43), channel_id=1, source_target_pairs={{0,2},{1,3},{2,0},{3,1},{4,6},{5,7},{6,4},{7,5},{8,10},{9,11},{10,... | collective-permute-start | bytes 1179656 | tf_op jit(solution)/shard_map/ppermute | solution.py:476
  46.9 23.3 %all-to-all-start = ((bf16[4,8,16,640]{3,2,1,0:T(8,128)(2,1)}), bf16[4,8,16,640]{3,2,1,0:T(8,128)(2,1)S(1)}, u32[]{:S(2)}, u32[]{:S(2)}) async-start(bf16[4,8,16,640]{3,2,1,0:T(8,128)(2,1)} %bitcast.5), calls=%async_computation | async-start | bytes 1310720 | tf_op jit(solution)/shard_map/all_to_all | solution.py:479
  52.3 6.7 %collective-permute-start.16 = (bf16[4,16,1024]{2,1,0:T(8,128)(2,1)S(1)}, bf16[4,16,1024]{2,1,0:T(8,128)(2,1)S(1)}, u32[]{:S(2)}, u32[]{:S(2)}) collective-permute-start(bf16[4,16,1024]{2,1,0:T(8,128)(2,1)S(1)} %slice.59), channel_id=1, source_target_pairs={{0,2},{1,3},{2,0},{3,1},{4,6},{5,7},{6,4},{7,5},{8,10},{9,11},{10,... | collective-permute-start | bytes 393224 | tf_op jit(solution)/shard_map/ppermute | solution.py:476
  57.5 5.7 %collective-permute-start.14 = (bf16[4,16,1536]{2,1,0:T(8,128)(2,1)S(1)}, bf16[4,16,1536]{2,1,0:T(8,128)(2,1)S(1)}, u32[]{:S(2)}, u32[]{:S(2)}) collective-permute-start(bf16[4,16,1536]{2,1,0:T(8,128)(2,1)S(1)} %slice.57), channel_id=1, source_target_pairs={{0,4},{1,5},{2,6},{3,7},{4,0},{5,1},{6,2},{7,3},{8,12},{9,13},{10,... | collective-permute-start | bytes 589832 | tf_op jit(solution)/shard_map/ppermute | solution.py:476
  63.3 6.8 %collective-permute-start.17 = (bf16[2,16,2560]{2,1,0:T(8,128)(2,1)S(1)}, bf16[2,16,2560]{2,1,0:T(8,128)(2,1)S(1)}, u32[]{:S(2)}, u32[]{:S(2)}) collective-permute-start(bf16[2,16,2560]{2,1,0:T(8,128)(2,1)S(1)} %pad_maximum_fusion.3), channel_id=1, source_target_pairs={{0,8},{1,9},{2,10},{3,11},{4,12},{5,13},{6,14},{7,15},{8,0},{9,1},... | collective-permute-start | bytes 491528 | tf_op jit(solution)/shard_map/ppermute | solution.py:476
  70.2 6.0 %collective-permute-start.18 = (bf16[1,16,2560]{2,1,0:T(8,128)(2,1)S(1)}, bf16[1,16,2560]{2,1,0:T(8,128)(2,1)S(1)}, u32[]{:S(2)}, u32[]{:S(2)}) collective-permute-start(bf16[1,16,2560]{2,1,0:T(8,128)(2,1)S(1)} %slice.53), channel_id=1, source_target_pairs={{0,16},{1,17},{2,18},{3,19},{4,20},{5,21},{6,22},{7,23},{8,24},{9,... | collective-permute-start | bytes 245768 | tf_op jit(solution)/shard_map/ppermute | solution.py:476
  76.2 6.1 %collective-permute-start.19 = (bf16[1,16,2560]{2,1,0:T(8,128)(2,1)S(1)}, bf16[1,16,2560]{2,1,0:T(8,128)(2,1)S(1)}, u32[]{:S(2)}, u32[]{:S(2)}) collective-permute-start(bf16[1,16,2560]{2,1,0:T(8,128)(2,1)S(1)} %add_convert_fusion.7), channel_id=1, source_target_pairs={{0,16},{1,17},{2,18},{3,19},{4,20},{5,21},{6,22},{7,23},{8,24},{9,... | collective-permute-start | bytes 245768 | tf_op jit(solution)/shard_map/ppermute | solution.py:476
  77.1 15.4 %all-to-all-start.1 = ((bf16[8,4,16,640]{3,2,1,0:T(8,128)(2,1)}), bf16[8,4,16,640]{3,2,1,0:T(8,128)(2,1)S(1)}, u32[]{:S(2)}, u32[]{:S(2)}) async-start(bf16[8,4,16,640]{3,2,1,0:T(8,128)(2,1)} %copy.20), calls=%async_computation.1 | async-start | bytes 1310720 | tf_op jit(solution)/shard_map/all_to_all | solution.py:479
  82.3 6.8 %collective-permute-start.20 = (bf16[2,16,2560]{2,1,0:T(8,128)(2,1)S(1)}, bf16[2,16,2560]{2,1,0:T(8,128)(2,1)S(1)}, u32[]{:S(2)}, u32[]{:S(2)}) collective-permute-start(bf16[2,16,2560]{2,1,0:T(8,128)(2,1)S(1)} %pad_maximum_fusion.4), channel_id=1, source_target_pairs={{0,8},{1,9},{2,10},{3,11},{4,12},{5,13},{6,14},{7,15},{8,0},{9,1},... | collective-permute-start | bytes 491528 | tf_op jit(solution)/shard_map/ppermute | solution.py:476
  92.5 5.8 %collective-permute-start.22 = (bf16[4,16,1280]{2,1,0:T(8,128)(2,1)S(1)}, bf16[4,16,1280]{2,1,0:T(8,128)(2,1)S(1)}, u32[]{:S(2)}, u32[]{:S(2)}) collective-permute-start(bf16[4,16,1280]{2,1,0:T(8,128)(2,1)S(1)} %get-tuple-element.103), channel_id=1, source_target_pairs={{0,2},{1,3},{2,0},{3,1},{4,6},{5,7},{6,4},{7,5},{8,10},{9,11},{10,... | collective-permute-start | bytes 491528 | tf_op jit(solution)/shard_map/ppermute | solution.py:476
  94.1 5.5 %collective-permute-start.21 = (bf16[4,16,1280]{2,1,0:T(8,128)(2,1)S(1)}, bf16[4,16,1280]{2,1,0:T(8,128)(2,1)S(1)}, u32[]{:S(2)}, u32[]{:S(2)}) collective-permute-start(bf16[4,16,1280]{2,1,0:T(8,128)(2,1)S(1)} %get-tuple-element.104), channel_id=1, source_target_pairs={{0,4},{1,5},{2,6},{3,7},{4,0},{5,1},{6,2},{7,3},{8,12},{9,13},{10,... | collective-permute-start | bytes 491528 | tf_op jit(solution)/shard_map/ppermute | solution.py:476
  99.6 8.6 %collective-permute-start.23 = (bf16[8,16,1280]{2,1,0:T(8,128)(2,1)S(1)}, bf16[8,16,1280]{2,1,0:T(8,128)(2,1)S(1)}, u32[]{:S(2)}, u32[]{:S(2)}) collective-permute-start(bf16[8,16,1280]{2,1,0:T(8,128)(2,1)S(1)} %pad_maximum_fusion.1), channel_id=1, source_target_pairs={{0,2},{1,3},{2,0},{3,1},{4,6},{5,7},{6,4},{7,5},{8,10},{9,11},{10,... | collective-permute-start | bytes 983048 | tf_op jit(solution)/shard_map/ppermute | solution.py:476
  100.2 7.8 %collective-permute-start.25 = (bf16[8,16,1280]{2,1,0:T(8,128)(2,1)S(1)}, bf16[8,16,1280]{2,1,0:T(8,128)(2,1)S(1)}, u32[]{:S(2)}, u32[]{:S(2)}) collective-permute-start(bf16[8,16,1280]{2,1,0:T(8,128)(2,1)S(1)} %pad_maximum_fusion.2), channel_id=1, source_target_pairs={{0,4},{1,5},{2,6},{3,7},{4,0},{5,1},{6,2},{7,3},{8,12},{9,13},{10,... | collective-permute-start | bytes 983048 | tf_op jit(solution)/shard_map/ppermute | solution.py:476
  108.1 2.6 %collective-permute-start.26 = (bf16[16,16,1280]{2,1,0:T(8,128)(2,1)S(1)}, bf16[16,16,1280]{2,1,0:T(8,128)(2,1)S(1)}, u32[]{:S(2)}, u32[]{:S(2)}) collective-permute-start(bf16[16,16,1280]{2,1,0:T(8,128)(2,1)S(1)} %constant_dynamic-update-slice_fusion.6.right_ref), channel_id=1, source_target_pairs={{0,1},{1,0},{2,3},{3,2},{4,5},{5,4},{6,7},{7,6},{8,9},{9,8},{10,11... | collective-permute-start | bytes 1966088 | tf_op jit(solution)/shard_map/ppermute | solution.py:476
  108.2 3.0 %collective-permute-start.24 = (bf16[16,16,1280]{2,1,0:T(8,128)(2,1)S(1)}, bf16[16,16,1280]{2,1,0:T(8,128)(2,1)S(1)}, u32[]{:S(2)}, u32[]{:S(2)}) collective-permute-start(bf16[16,16,1280]{2,1,0:T(8,128)(2,1)S(1)} %constant_dynamic-update-slice_fusion.4.left_ref), channel_id=1, source_target_pairs={{0,1},{1,0},{2,3},{3,2},{4,5},{5,4},{6,7},{7,6},{8,9},{9,8},{10,11... | collective-permute-start | bytes 1966088 | tf_op jit(solution)/shard_map/ppermute | solution.py:476

commit v22 on v19

--- a/solution.py
+++ b/solution.py
@@ -361,7 +361,7 @@
         self.wide = -(-5 * width // block) * LANES
         self.gain_lanes = 2 * width // self.capacity
         self.extra = -(-(GAIN_AT + self.gain_lanes) // LANES) * LANES
-        first = -(-13 * self.wide // (20 * LANES)) * LANES
+        first = -(-3 * self.wide // (5 * LANES)) * LANES
         self.split = -(-self.wide // (2 * LANES)) * LANES
         self.sides = ((0, first), (first, self.wide - first))
         self.halves = ((0, self.split), (self.split, self.wide - self.split))

time: 112 us -> 111 us (level)
  transfers between devices with their start and end apart: 29 -> 29, of which waited for: 19 -> 20; matrix products, arithmetic and copies ran while one was open for 4% -> 4% of each run, Pallas kernels for 8% -> 9%
where the time goes in v22:
time: 111 us
  starting transfers between devices  42.6 us (38%)
  waiting for transfers between devices  40.1 us (36%)
  Pallas kernels  20.9 us (19%)
  local copies, waits for them, and re-layouts  3.81 us (3%)
  other arithmetic  1.99 us (2%)
  between operations  1.2 us (1%)
    ppermute x27, waiting for transfers between devices, swap(): return lax.ppermute(values, both, pairs)  37.4 us
    ppermute x27, starting transfers between devices, swap(): return lax.ppermute(values, both, pairs)  34.9 us
    pallas_call x1, Pallas kernels, on_device(): call(functools.partial(backward_body, plan, table_size, total_factor), ou...  8.81 us
    all_to_all x2, starting transfers between devices, exchange(): lax.all_to_all(values, axes, split_axis=0, concat_axis=0, tiled=True, axi...  7.74 us
    pallas_call x2, Pallas kernels, on_device(): pl.pallas_call(functools.partial(widen_body, plan, turn), out_shape=outs,...  3.93 us
    pallas_call x1, Pallas kernels, on_device(): call(forward_body, list(shapes.values()), [VMEM] * 3, flops=4 * count * w...  3.91 us
    all_to_all x2, waiting for transfers between devices, exchange(): lax.all_to_all(values, axes, split_axis=0, concat_axis=0, tiled=True, axi...  2.63 us
  transfers between devices with their start and end apart: 29, of which 20 were waited for; matrix products, arithmetic and copies ran while one was open for 4% of the time, Pallas kernels for 9%

profile of v22, /device:TPU:0, one launch (start us, length us, event | category | flops | bytes accessed | tf_op | source)
XLA Modules:
  0.0 110.6 jit_solution(1471982023487723325)
XLA Ops:
  0.7 0.8 select_reduce_fusion
  1.6 4.0 %collective-permute-start.2 = (s32[8,8]{1,0:T(8,128)S(1)}, s32[8,8]{1,0:T(8,128)S(1)}, u32[]{:S(2)}, u32[]{:S(2)}) collective-permute-start(s32[8,8]{1,0:T(8,128)S(1)} %broadcast_select_fusion), channel_id=1, source_target_pairs={{0,12},{1,13},{2,14},{3,15},{4,8},{5,9},{6,10},{7,11},{8,4},{9,5},... | collective-permute-start | bytes 776 | tf_op jit(solution)/shard_map/ppermute | solution.py:476
  5.6 0.4 collective-permute-start.1
  6.2 1.7 %constant_dynamic-update-slice_fusion.1 = bf16[512,2560]{1,0:T(8,128)(2,1)S(1)} fusion(bf16[512,2048]{1,0:T(8,128)(2,1)} %param.18), kind=kLoop, calls=%fused_computation.19 | loop fusion | bytes 4194304
  8.1 1.1 collective-permute-done.1
  9.7 2.6 %collective-permute-start.3 = (s32[8,8]{1,0:T(8,128)S(1)}, s32[8,8]{1,0:T(8,128)S(1)}, u32[]{:S(2)}, u32[]{:S(2)}) collective-permute-start(s32[8,8]{1,0:T(8,128)S(1)} %add_add_fusion), channel_id=1, source_target_pairs={{0,16},{1,17},{2,18},{3,19},{4,20},{5,21},{6,22},{7,23},{8,24},{9,... | collective-permute-start | bytes 776 | tf_op jit(solution)/shard_map/ppermute | solution.py:476
  12.3 1.0 constant_dynamic-update-slice_fusion.2.rows_ref
  13.3 1.4 %shard_map.146 = (bf16[256,2560]{1,0:T(8,128)(2,1)S(1)}, bf16[512,256]{1,0:T(8,128)(2,1)S(1)}, bf16[256,2048]{1,0:T(8,128)(2,1)S(1)}, f32[256,512]{1,0:T(8,128)S...) custom-call(bf16[512,512]{1,0:T(8,128)(2,1)S(1)} %constant_dynamic-update-slice_fusion.2.rows_ref, ...), custom_call_target="tpu_custom_call" | custom-call | flops 536870912 | bytes 4000000 | tf_op jit(solution)/shard_map/pallas_call | solution.py:497
  14.8 0.7 shard_map.147
  15.5 3.1 %collective-permute-start.4 = (bf16[64,512]{1,0:T(8,128)(2,1)S(1)}, bf16[64,512]{1,0:T(8,128)(2,1)S(1)}, u32[]{:S(2)}, u32[]{:S(2)}) collective-permute-start(bf16[64,512]{1,0:T(8,128)(2,1)S(1)} %get-tuple-element.77), channel_id=1, source_target_pairs={{0,28},{1,13},{2,30},{3,15},{4,24},{5,9},{6,26},{7,11},{8,20},{9,5... | collective-permute-start | bytes 196616 | tf_op jit(solution)/shard_map/ppermute | solution.py:476
  18.6 0.8 collective-permute-start.5
  19.3 1.2 %collective-permute-start.6 = (bf16[64,512]{1,0:T(8,128)(2,1)S(1)}, bf16[64,512]{1,0:T(8,128)(2,1)S(1)}, u32[]{:S(2)}, u32[]{:S(2)}) collective-permute-start(bf16[64,512]{1,0:T(8,128)(2,1)S(1)} %get-tuple-element.79), channel_id=1, source_target_pairs={{0,20},{1,5},{2,22},{3,7},{4,16},{5,1},{6,18},{7,3},{8,28},{9,13},... | collective-permute-start | bytes 196616 | tf_op jit(solution)/shard_map/ppermute | solution.py:476
  20.5 2.7 %collective-permute-start.7 = (bf16[64,512]{1,0:T(8,128)(2,1)S(1)}, bf16[64,512]{1,0:T(8,128)(2,1)S(1)}, u32[]{:S(2)}, u32[]{:S(2)}) collective-permute-start(bf16[64,512]{1,0:T(8,128)(2,1)S(1)} %get-tuple-element.80), channel_id=1, source_target_pairs={{0,16},{1,29},{2,18},{3,31},{4,20},{5,25},{6,22},{7,27},{8,24},{9,... | collective-permute-start | bytes 196616 | tf_op jit(solution)/shard_map/ppermute | solution.py:476
  23.2 0.7 collective-permute-start.8
  23.9 3.9 %collective-permute-start.9 = (bf16[64,512]{1,0:T(8,128)(2,1)S(1)}, bf16[64,512]{1,0:T(8,128)(2,1)S(1)}, u32[]{:S(2)}, u32[]{:S(2)}) collective-permute-start(bf16[64,512]{1,0:T(8,128)(2,1)S(1)} %get-tuple-element.82), channel_id=1, source_target_pairs={{0,8},{1,21},{2,10},{3,23},{4,12},{5,17},{6,14},{7,19},{8,0},{9,29... | collective-permute-start | bytes 196616 | tf_op jit(solution)/shard_map/ppermute | solution.py:476
  27.8 3.9 %shard_map.148 = (f32[512,512]{1,0:T(8,128)S(1)}, f32[512,512]{1,0:T(8,128)S(1)}, f32[512,1]{1,0:T(8,128)S(1)}, bf16[512,1536]{1,0:T(8,128)(2,1)S(1)}, bf16[16,1...) custom-call(bf16[256,2560]{1,0:T(8,128)(2,1)S(1)} %get-tuple-element, ...), custom_call_target="tpu_custom_call" | custom-call | flops 2684354560 | bytes 8000000 | tf_op jit(solution)/shard_map/pallas_call | solution.py:518
  32.1 8.8 %shard_map.149 = (bf16[512,640]{1,0:T(8,128)(2,1)}, bf16[16,16,1536]{2,1,0:T(8,128)(2,1)S(1)}, bf16[16,16,1536]{2,1,0:T(8,128)(2,1)S(1)}, bf16[16,16,1024]{2,1,0:T(8,128)(2,1)S(1)}, bf16[16,16,1024]{2,1,0:T(8,128)(2,1)S(1)}) custom-call(s32[1]{0:T(128)} %bitcast.me_ref, s32[8]{0:T(128)S(1)} %copy-done, s32[8]{0:T(128)S(1)} %copy-done.1, ...), custom_call_target="tpu_custom_call" | custom-call | flops 10737418240 | bytes 12000000 | tf_op jit(solution)/shard_map/pallas_call | solution.py:531
  40.9 0.5 collective-permute-start.11
  41.4 1.4 %collective-permute-done.12 = bf16[16,16,1024]{2,1,0:T(8,128)(2,1)S(1)} collective-permute-done((bf16[16,16,1024]{2,1,0:T(8,128)(2,1)S(1)}, bf16[16,16,1024]{2,1,0:T(8,128)(2,1)S(1)}, u32[]{:S(2)}, u32[]{:S(2)}) %collective-permute-start.12) | collective-permute-done | bytes 524320 | tf_op jit(solution)/shard_map/ppermute | solution.py:476
  43.0 0.9 collective-permute-done.11
  44.2 1.9 %collective-permute-start.15 = (bf16[8,16,1024]{2,1,0:T(8,128)(2,1)S(1)}, bf16[8,16,1024]{2,1,0:T(8,128)(2,1)S(1)}, u32[]{:S(2)}, u32[]{:S(2)}) collective-permute-start(bf16[8,16,1024]{2,1,0:T(8,128)(2,1)S(1)} %slice.47), channel_id=1, source_target_pairs={{0,4},{1,5},{2,6},{3,7},{4,0},{5,1},{6,2},{7,3},{8,12},{9,13},{10,... | collective-permute-start | bytes 786440 | tf_op jit(solution)/shard_map/ppermute | solution.py:476
  46.1 1.6 %collective-permute-start.13 = (bf16[8,16,1536]{2,1,0:T(8,128)(2,1)S(1)}, bf16[8,16,1536]{2,1,0:T(8,128)(2,1)S(1)}, u32[]{:S(2)}, u32[]{:S(2)}) collective-permute-start(bf16[8,16,1536]{2,1,0:T(8,128)(2,1)S(1)} %slice.43), channel_id=1, source_target_pairs={{0,2},{1,3},{2,0},{3,1},{4,6},{5,7},{6,4},{7,5},{8,10},{9,11},{10,... | collective-permute-start | bytes 1179656 | tf_op jit(solution)/shard_map/ppermute | solution.py:476
  47.7 3.7 %all-to-all-start = ((bf16[4,8,16,640]{3,2,1,0:T(8,128)(2,1)}), bf16[4,8,16,640]{3,2,1,0:T(8,128)(2,1)S(1)}, u32[]{:S(2)}, u32[]{:S(2)}) async-start(bf16[4,8,16,640]{3,2,1,0:T(8,128)(2,1)} %bitcast.5), calls=%async_computation | async-start | bytes 1310720 | tf_op jit(solution)/shard_map/all_to_all | solution.py:479
  51.4 1.3 %collective-permute-done.15 = bf16[8,16,1024]{2,1,0:T(8,128)(2,1)S(1)} collective-permute-done((bf16[8,16,1024]{2,1,0:T(8,128)(2,1)S(1)}, bf16[8,16,1024]{2,1,0:T(8,128)(2,1)S(1)}, u32[]{:S(2)}, u32[]{:S(2)}) %collective-permute-start.15) | collective-permute-done | bytes 262176 | tf_op jit(solution)/shard_map/ppermute | solution.py:476
  52.8 1.6 %collective-permute-start.16 = (bf16[4,16,1024]{2,1,0:T(8,128)(2,1)S(1)}, bf16[4,16,1024]{2,1,0:T(8,128)(2,1)S(1)}, u32[]{:S(2)}, u32[]{:S(2)}) collective-permute-start(bf16[4,16,1024]{2,1,0:T(8,128)(2,1)S(1)} %slice.59), channel_id=1, source_target_pairs={{0,2},{1,3},{2,0},{3,1},{4,6},{5,7},{6,4},{7,5},{8,10},{9,11},{10,... | collective-permute-start | bytes 393224 | tf_op jit(solution)/shard_map/ppermute | solution.py:476
  54.4 3.8 %collective-permute-done.13 = bf16[8,16,1536]{2,1,0:T(8,128)(2,1)S(1)} collective-permute-done((bf16[8,16,1536]{2,1,0:T(8,128)(2,1)S(1)}, bf16[8,16,1536]{2,1,0:T(8,128)(2,1)S(1)}, u32[]{:S(2)}, u32[]{:S(2)}) %collective-permute-start.13) | collective-permute-done | bytes 393248 | tf_op jit(solution)/shard_map/ppermute | solution.py:476
  58.4 1.5 %collective-permute-done.16 = bf16[4,16,1024]{2,1,0:T(8,128)(2,1)S(1)} collective-permute-done((bf16[4,16,1024]{2,1,0:T(8,128)(2,1)S(1)}, bf16[4,16,1024]{2,1,0:T(8,128)(2,1)S(1)}, u32[]{:S(2)}, u32[]{:S(2)}) %collective-permute-start.16) | collective-permute-done | bytes 131104 | tf_op jit(solution)/shard_map/ppermute | solution.py:476
  59.9 4.1 %collective-permute-done.14 = bf16[4,16,1536]{2,1,0:T(8,128)(2,1)S(1)} collective-permute-done((bf16[4,16,1536]{2,1,0:T(8,128)(2,1)S(1)}, bf16[4,16,1536]{2,1,0:T(8,128)(2,1)S(1)}, u32[]{:S(2)}, u32[]{:S(2)}) %collective-permute-start.14) | collective-permute-done | bytes 196640 | tf_op jit(solution)/shard_map/ppermute | solution.py:476
  64.1 0.7 collective-permute-start.17
  64.8 5.4 %collective-permute-done.17 = bf16[2,16,2560]{2,1,0:T(8,128)(2,1)S(1)} collective-permute-done((bf16[2,16,2560]{2,1,0:T(8,128)(2,1)S(1)}, bf16[2,16,2560]{2,1,0:T(8,128)(2,1)S(1)}, u32[]{:S(2)}, u32[]{:S(2)}) %collective-permute-start.17) | collective-permute-done | bytes 163872 | tf_op jit(solution)/shard_map/ppermute | solution.py:476
  70.3 0.5 collective-permute-start.18
  70.8 0.9 copy.20
  71.7 4.1 %all-to-all-start.1 = ((bf16[8,4,16,640]{3,2,1,0:T(8,128)(2,1)}), bf16[8,4,16,640]{3,2,1,0:T(8,128)(2,1)S(1)}, u32[]{:S(2)}, u32[]{:S(2)}) async-start(bf16[8,4,16,640]{3,2,1,0:T(8,128)(2,1)} %copy.20), calls=%async_computation.1 | async-start | bytes 1310720 | tf_op jit(solution)/shard_map/all_to_all | solution.py:479
  75.9 1.9 %collective-permute-start.19 = (bf16[1,16,2560]{2,1,0:T(8,128)(2,1)S(1)}, bf16[1,16,2560]{2,1,0:T(8,128)(2,1)S(1)}, u32[]{:S(2)}, u32[]{:S(2)}) collective-permute-start(bf16[1,16,2560]{2,1,0:T(8,128)(2,1)S(1)} %add_convert_fusion.7), channel_id=1, source_target_pairs={{0,16},{1,17},{2,18},{3,19},{4,20},{5,21},{6,22},{7,23},{8,24},{9,... | collective-permute-start | bytes 245768 | tf_op jit(solution)/shard_map/ppermute | solution.py:476
  77.9 5.5 %collective-permute-done.19 = bf16[1,16,2560]{2,1,0:T(8,128)(2,1)S(1)} collective-permute-done((bf16[1,16,2560]{2,1,0:T(8,128)(2,1)S(1)}, bf16[1,16,2560]{2,1,0:T(8,128)(2,1)S(1)}, u32[]{:S(2)}, u32[]{:S(2)}) %collective-permute-start.19) | collective-permute-done | bytes 81952 | tf_op jit(solution)/shard_map/ppermute | solution.py:476
  83.4 2.6 %all-to-all-done.1 = bf16[8,4,16,640]{3,2,1,0:T(8,128)(2,1)S(1)} async-done(((bf16[8,4,16,640]{3,2,1,0:T(8,128)(2,1)}), bf16[8,4,16,640]{3,2,1,0:T(8,128)(2,1)S(1)}, u32[]{:S(2)}, u32[]{:S(2)}) %all-to-all-start.1) | async-done | bytes 655392 | tf_op jit(solution)/shard_map/all_to_all | solution.py:479
  86.0 1.0 collective-permute-start.20
  87.1 2.2 %shard_map.150 = (f32[1024,512]{1,0:T(8,128)}, f32[1,512]{1,0:T(1,128)}, f32[1,512]{1,0:T(1,128)}) custom-call(bf16[512,640]{1,0:T(8,128)(2,1)S(1)} %bitcast.10), custom_call_target="tpu_custom_call" | custom-call | tf_op jit(solution)/shard_map/pallas_call | solution.py:580
  89.2 2.6 %collective-permute-done.20 = bf16[2,16,2560]{2,1,0:T(8,128)(2,1)S(1)} collective-permute-done((bf16[2,16,2560]{2,1,0:T(8,128)(2,1)S(1)}, bf16[2,16,2560]{2,1,0:T(8,128)(2,1)S(1)}, u32[]{:S(2)}, u32[]{:S(2)}) %collective-permute-start.20) | collective-permute-done | bytes 163872 | tf_op jit(solution)/shard_map/ppermute | solution.py:476
  91.8 1.1 collective-permute-start.21
  92.9 1.0 collective-permute-start.24
  93.9 3.3 %collective-permute-done.21 = bf16[4,16,1280]{2,1,0:T(8,128)(2,1)S(1)} collective-permute-done((bf16[4,16,1280]{2,1,0:T(8,128)(2,1)S(1)}, bf16[4,16,1280]{2,1,0:T(8,128)(2,1)S(1)}, u32[]{:S(2)}, u32[]{:S(2)}) %collective-permute-start.21) | collective-permute-done | bytes 163872 | tf_op jit(solution)/shard_map/ppermute | solution.py:476
  97.3 1.5 %collective-permute-start.22 = (bf16[8,16,1280]{2,1,0:T(8,128)(2,1)S(1)}, bf16[8,16,1280]{2,1,0:T(8,128)(2,1)S(1)}, u32[]{:S(2)}, u32[]{:S(2)}) collective-permute-start(bf16[8,16,1280]{2,1,0:T(8,128)(2,1)S(1)} %pad_maximum_fusion.3), channel_id=1, source_target_pairs={{0,2},{1,3},{2,0},{3,1},{4,6},{5,7},{6,4},{7,5},{8,10},{9,11},{10,... | collective-permute-start | bytes 983048 | tf_op jit(solution)/shard_map/ppermute | solution.py:476
  99.1 1.7 %collective-permute-start.25 = (bf16[8,16,1280]{2,1,0:T(8,128)(2,1)S(1)}, bf16[8,16,1280]{2,1,0:T(8,128)(2,1)S(1)}, u32[]{:S(2)}, u32[]{:S(2)}) collective-permute-start(bf16[8,16,1280]{2,1,0:T(8,128)(2,1)S(1)} %pad_maximum_fusion.4), channel_id=1, source_target_pairs={{0,4},{1,5},{2,6},{3,7},{4,0},{5,1},{6,2},{7,3},{8,12},{9,13},{10,... | collective-permute-start | bytes 983048 | tf_op jit(solution)/shard_map/ppermute | solution.py:476
  100.8 4.5 %collective-permute-done.22 = bf16[8,16,1280]{2,1,0:T(8,128)(2,1)S(1)} collective-permute-done((bf16[8,16,1280]{2,1,0:T(8,128)(2,1)S(1)}, bf16[8,16,1280]{2,1,0:T(8,128)(2,1)S(1)}, u32[]{:S(2)}, u32[]{:S(2)}) %collective-permute-start.22) | collective-permute-done | bytes 327712 | tf_op jit(solution)/shard_map/ppermute | solution.py:476
  105.4 0.8 collective-permute-done.25
  106.4 2.0 %shard_map.151 = (f32[512,2048]{1,0:T(8,128)}, f32[512,512]{1,0:T(8,128)}) custom-call(s32[1]{0:T(128)} %bitcast.me_ref, bf16[16,16,1280]{2,1,0:T(8,128)(2,1)S(1)} %pad_maximum_fusion.left_ref, bf16[16,16,1280]{2,1,0:T(8,128)(2,1)S(1)} %pad_maximum_fusion.1.right_ref), custom_call_target="tpu_custom_call" | custom-call | bytes 4000000 | tf_op jit(solution)/shard_map/pallas_call | solution.py:600
  108.5 2.0 %shard_map.152 = (f32[512,2048]{1,0:T(8,128)}, f32[512,512]{1,0:T(8,128)}) custom-call(s32[1]{0:T(128)} %bitcast.me_ref, bf16[16,16,1280]{2,1,0:T(8,128)(2,1)S(1)} %collective-permute-done.23.left_ref, bf16[16,16,1280]{2,1,0:T(8,128)(2,1)S(1)} %collective-permute-done.26.right_ref, ...), custom_call_target="tpu_custom_call", output_to_operand_aliasing={{0}: (3, {}), {1}: (4, {})} | custom-call | bytes 4000000 | tf_op jit(solution)/shard_map/pallas_call | solution.py:600
  (68 shorter events, 3.1 us)
Async XLA Ops:
  0.6 7.4 %copy-start.4 = (f32[512]{0:T(512)S(1)}, f32[512]{0:T(512)}, u32[]{:S(2)}) copy-start(f32[512]{0:T(512)} %param.21) | copy-start | bytes 6148
  0.6 7.4 %copy-start.5 = (f32[512]{0:T(512)S(1)}, f32[512]{0:T(512)}, u32[]{:S(2)}) copy-start(f32[512]{0:T(512)} %param.20) | copy-start | bytes 6148
  0.7 7.4 %copy-start.2 = (bf16[512,512]{1,0:T(8,128)(2,1)S(1)}, bf16[512,512]{1,0:T(8,128)(2,1)}, u32[]{:S(2)}) copy-start(bf16[512,512]{1,0:T(8,128)(2,1)} %param.19) | copy-start | bytes 1572868
  1.6 6.5 %copy-start.6 = (s32[512]{0:T(512)S(1)}, s32[512]{0:T(512)}, u32[]{:S(2)}) copy-start(s32[512]{0:T(512)} %param.12) | copy-start | bytes 6148
  1.6 6.5 %copy-start.7 = (s32[256]{0:T(256)S(1)}, s32[256]{0:T(256)}, u32[]{:S(2)}) copy-start(s32[256]{0:T(256)} %param.14) | copy-start | bytes 3076
  1.6 6.5 %copy-start.8 = (s32[256,1]{0,1:T(1,128)S(1)}, s32[256,1]{0,1:T(1,128)}, u32[]{:S(2)}) copy-start(s32[256,1]{0,1:T(1,128)} %param.13) | copy-start | bytes 3076
  1.6 10.7 %copy-start.3 = (bf16[256,512]{1,0:T(8,128)(2,1)S(1)}, bf16[256,512]{1,0:T(8,128)(2,1)}, u32[]{:S(2)}) copy-start(bf16[256,512]{1,0:T(8,128)(2,1)} %param.11) | copy-start | bytes 786436
  1.6 6.6 %collective-permute-start.2 = (s32[8,8]{1,0:T(8,128)S(1)}, s32[8,8]{1,0:T(8,128)S(1)}, u32[]{:S(2)}, u32[]{:S(2)}) collective-permute-start(s32[8,8]{1,0:T(8,128)S(1)} %broadcast_select_fusion), channel_id=1, source_target_pairs={{0,12},{1,13},{2,14},{3,15},{4,8},{5,9},{6,10},{7,11},{8,4},{9,5},... | collective-permute-start | bytes 776 | tf_op jit(solution)/shard_map/ppermute | solution.py:476
  5.6 3.6 %collective-permute-start.1 = (s32[8,8]{1,0:T(8,128)S(1)}, s32[8,8]{1,0:T(8,128)S(1)}, u32[]{:S(2)}, u32[]{:S(2)}) collective-permute-start(s32[8,8]{1,0:T(8,128)S(1)} %broadcast_select_fusion), channel_id=1, source_target_pairs={{0,8},{1,9},{2,10},{3,11},{4,12},{5,13},{6,14},{7,15},{8,0},{9,1},... | collective-permute-start | bytes 776 | tf_op jit(solution)/shard_map/ppermute | solution.py:476
  6.0 3.6 %collective-permute-start = (s32[8,8]{1,0:T(8,128)S(1)}, s32[8,8]{1,0:T(8,128)S(1)}, u32[]{:S(2)}, u32[]{:S(2)}) collective-permute-start(s32[8,8]{1,0:T(8,128)S(1)} %broadcast_select_fusion), channel_id=1, source_target_pairs={{0,4},{1,5},{2,6},{3,7},{4,0},{5,1},{6,2},{7,3},{8,12},{9,13},{10,... | collective-permute-start | bytes 776 | tf_op jit(solution)/shard_map/ppermute | solution.py:476
  9.7 5.0 %collective-permute-start.3 = (s32[8,8]{1,0:T(8,128)S(1)}, s32[8,8]{1,0:T(8,128)S(1)}, u32[]{:S(2)}, u32[]{:S(2)}) collective-permute-start(s32[8,8]{1,0:T(8,128)S(1)} %add_add_fusion), channel_id=1, source_target_pairs={{0,16},{1,17},{2,18},{3,19},{4,20},{5,21},{6,22},{7,23},{8,24},{9,... | collective-permute-start | bytes 776 | tf_op jit(solution)/shard_map/ppermute | solution.py:476
  15.5 8.4 %collective-permute-start.4 = (bf16[64,512]{1,0:T(8,128)(2,1)S(1)}, bf16[64,512]{1,0:T(8,128)(2,1)S(1)}, u32[]{:S(2)}, u32[]{:S(2)}) collective-permute-start(bf16[64,512]{1,0:T(8,128)(2,1)S(1)} %get-tuple-element.77), channel_id=1, source_target_pairs={{0,28},{1,13},{2,30},{3,15},{4,24},{5,9},{6,26},{7,11},{8,20},{9,5... | collective-permute-start | bytes 196616 | tf_op jit(solution)/shard_map/ppermute | solution.py:476
  18.6 9.2 %collective-permute-start.5 = (bf16[64,512]{1,0:T(8,128)(2,1)S(1)}, bf16[64,512]{1,0:T(8,128)(2,1)S(1)}, u32[]{:S(2)}, u32[]{:S(2)}) collective-permute-start(bf16[64,512]{1,0:T(8,128)(2,1)S(1)} %get-tuple-element.78), channel_id=1, source_target_pairs={{0,24},{1,9},{2,26},{3,11},{4,28},{5,13},{6,30},{7,15},{8,16},{9,1... | collective-permute-start | bytes 196616 | tf_op jit(solution)/shard_map/ppermute | solution.py:476
  19.3 12.4 %collective-permute-start.6 = (bf16[64,512]{1,0:T(8,128)(2,1)S(1)}, bf16[64,512]{1,0:T(8,128)(2,1)S(1)}, u32[]{:S(2)}, u32[]{:S(2)}) collective-permute-start(bf16[64,512]{1,0:T(8,128)(2,1)S(1)} %get-tuple-element.79), channel_id=1, source_target_pairs={{0,20},{1,5},{2,22},{3,7},{4,16},{5,1},{6,18},{7,3},{8,28},{9,13},... | collective-permute-start | bytes 196616 | tf_op jit(solution)/shard_map/ppermute | solution.py:476
  20.5 11.2 %collective-permute-start.7 = (bf16[64,512]{1,0:T(8,128)(2,1)S(1)}, bf16[64,512]{1,0:T(8,128)(2,1)S(1)}, u32[]{:S(2)}, u32[]{:S(2)}) collective-permute-start(bf16[64,512]{1,0:T(8,128)(2,1)S(1)} %get-tuple-element.80), channel_id=1, source_target_pairs={{0,16},{1,29},{2,18},{3,31},{4,20},{5,25},{6,22},{7,27},{8,24},{9,... | collective-permute-start | bytes 196616 | tf_op jit(solution)/shard_map/ppermute | solution.py:476
  23.2 8.6 %collective-permute-start.8 = (bf16[64,512]{1,0:T(8,128)(2,1)S(1)}, bf16[64,512]{1,0:T(8,128)(2,1)S(1)}, u32[]{:S(2)}, u32[]{:S(2)}) collective-permute-start(bf16[64,512]{1,0:T(8,128)(2,1)S(1)} %get-tuple-element.81), channel_id=1, source_target_pairs={{0,12},{1,25},{2,14},{3,27},{4,8},{5,29},{6,10},{7,31},{8,4},{9,17... | collective-permute-start | bytes 196616 | tf_op jit(solution)/shard_map/ppermute | solution.py:476
  23.9 8.1 %collective-permute-start.9 = (bf16[64,512]{1,0:T(8,128)(2,1)S(1)}, bf16[64,512]{1,0:T(8,128)(2,1)S(1)}, u32[]{:S(2)}, u32[]{:S(2)}) collective-permute-start(bf16[64,512]{1,0:T(8,128)(2,1)S(1)} %get-tuple-element.82), channel_id=1, source_target_pairs={{0,8},{1,21},{2,10},{3,23},{4,12},{5,17},{6,14},{7,19},{8,0},{9,29... | collective-permute-start | bytes 196616 | tf_op jit(solution)/shard_map/ppermute | solution.py:476
  27.8 4.3 %copy-start = (s32[8]{0:T(128)S(1)}, s32[8]{0:T(128)}, u32[]{:S(2)}) copy-start(s32[8]{0:T(128)} %dest_ref.1) | copy-start | bytes 100
  27.8 4.3 %copy-start.1 = (s32[8]{0:T(128)S(1)}, s32[8]{0:T(128)}, u32[]{:S(2)}) copy-start(s32[8]{0:T(128)} %blocks_ref.1) | copy-start | bytes 100
  27.8 4.3 %collective-permute-start.10 = (bf16[64,512]{1,0:T(8,128)(2,1)S(1)}, bf16[64,512]{1,0:T(8,128)(2,1)S(1)}, u32[]{:S(2)}, u32[]{:S(2)}) collective-permute-start(bf16[64,512]{1,0:T(8,128)(2,1)S(1)} %get-tuple-element.83), channel_id=1, source_target_pairs={{0,4},{1,17},{2,6},{3,19},{4,0},{5,21},{6,2},{7,23},{8,12},{9,25},... | collective-permute-start | bytes 196616 | tf_op jit(solution)/shard_map/ppermute | solution.py:476
  40.9 1.9 %collective-permute-start.12 = (bf16[16,16,1024]{2,1,0:T(8,128)(2,1)S(1)}, bf16[16,16,1024]{2,1,0:T(8,128)(2,1)S(1)}, u32[]{:S(2)}, u32[]{:S(2)}) collective-permute-start(bf16[16,16,1024]{2,1,0:T(8,128)(2,1)S(1)} %get-tuple-element.87), channel_id=1, source_target_pairs={{0,1},{1,0},{2,3},{3,2},{4,5},{5,4},{6,7},{7,6},{8,9},{9,8},{10,11... | collective-permute-start | bytes 1572872 | tf_op jit(solution)/shard_map/ppermute | solution.py:476
  40.9 3.0 %collective-permute-start.11 = (bf16[16,16,1536]{2,1,0:T(8,128)(2,1)S(1)}, bf16[16,16,1536]{2,1,0:T(8,128)(2,1)S(1)}, u32[]{:S(2)}, u32[]{:S(2)}) collective-permute-start(bf16[16,16,1536]{2,1,0:T(8,128)(2,1)S(1)} %get-tuple-element.85), channel_id=1, source_target_pairs={{0,1},{1,0},{2,3},{3,2},{4,5},{5,4},{6,7},{7,6},{8,9},{9,8},{10,11... | collective-permute-start | bytes 2359304 | tf_op jit(solution)/shard_map/ppermute | solution.py:476
  44.2 8.5 %collective-permute-start.15 = (bf16[8,16,1024]{2,1,0:T(8,128)(2,1)S(1)}, bf16[8,16,1024]{2,1,0:T(8,128)(2,1)S(1)}, u32[]{:S(2)}, u32[]{:S(2)}) collective-permute-start(bf16[8,16,1024]{2,1,0:T(8,128)(2,1)S(1)} %slice.47), channel_id=1, source_target_pairs={{0,4},{1,5},{2,6},{3,7},{4,0},{5,1},{6,2},{7,3},{8,12},{9,13},{10,... | collective-permute-start | bytes 786440 | tf_op jit(solution)/shard_map/ppermute | solution.py:476
  46.1 12.1 %collective-permute-start.13 = (bf16[8,16,1536]{2,1,0:T(8,128)(2,1)S(1)}, bf16[8,16,1536]{2,1,0:T(8,128)(2,1)S(1)}, u32[]{:S(2)}, u32[]{:S(2)}) collective-permute-start(bf16[8,16,1536]{2,1,0:T(8,128)(2,1)S(1)} %slice.43), channel_id=1, source_target_pairs={{0,2},{1,3},{2,0},{3,1},{4,6},{5,7},{6,4},{7,5},{8,10},{9,11},{10,... | collective-permute-start | bytes 1179656 | tf_op jit(solution)/shard_map/ppermute | solution.py:476
  47.7 22.6 %all-to-all-start = ((bf16[4,8,16,640]{3,2,1,0:T(8,128)(2,1)}), bf16[4,8,16,640]{3,2,1,0:T(8,128)(2,1)S(1)}, u32[]{:S(2)}, u32[]{:S(2)}) async-start(bf16[4,8,16,640]{3,2,1,0:T(8,128)(2,1)} %bitcast.5), calls=%async_computation | async-start | bytes 1310720 | tf_op jit(solution)/shard_map/all_to_all | solution.py:479
  52.8 7.1 %collective-permute-start.16 = (bf16[4,16,1024]{2,1,0:T(8,128)(2,1)S(1)}, bf16[4,16,1024]{2,1,0:T(8,128)(2,1)S(1)}, u32[]{:S(2)}, u32[]{:S(2)}) collective-permute-start(bf16[4,16,1024]{2,1,0:T(8,128)(2,1)S(1)} %slice.59), channel_id=1, source_target_pairs={{0,2},{1,3},{2,0},{3,1},{4,6},{5,7},{6,4},{7,5},{8,10},{9,11},{10,... | collective-permute-start | bytes 393224 | tf_op jit(solution)/shard_map/ppermute | solution.py:476
  58.3 5.7 %collective-permute-start.14 = (bf16[4,16,1536]{2,1,0:T(8,128)(2,1)S(1)}, bf16[4,16,1536]{2,1,0:T(8,128)(2,1)S(1)}, u32[]{:S(2)}, u32[]{:S(2)}) collective-permute-start(bf16[4,16,1536]{2,1,0:T(8,128)(2,1)S(1)} %slice.57), channel_id=1, source_target_pairs={{0,4},{1,5},{2,6},{3,7},{4,0},{5,1},{6,2},{7,3},{8,12},{9,13},{10,... | collective-permute-start | bytes 589832 | tf_op jit(solution)/shard_map/ppermute | solution.py:476
  64.1 6.1 %collective-permute-start.17 = (bf16[2,16,2560]{2,1,0:T(8,128)(2,1)S(1)}, bf16[2,16,2560]{2,1,0:T(8,128)(2,1)S(1)}, u32[]{:S(2)}, u32[]{:S(2)}) collective-permute-start(bf16[2,16,2560]{2,1,0:T(8,128)(2,1)S(1)} %pad_maximum_fusion.5), channel_id=1, source_target_pairs={{0,8},{1,9},{2,10},{3,11},{4,12},{5,13},{6,14},{7,15},{8,0},{9,1},... | collective-permute-start | bytes 491528 | tf_op jit(solution)/shard_map/ppermute | solution.py:476
  70.3 5.6 %collective-permute-start.18 = (bf16[1,16,2560]{2,1,0:T(8,128)(2,1)S(1)}, bf16[1,16,2560]{2,1,0:T(8,128)(2,1)S(1)}, u32[]{:S(2)}, u32[]{:S(2)}) collective-permute-start(bf16[1,16,2560]{2,1,0:T(8,128)(2,1)S(1)} %slice.53), channel_id=1, source_target_pairs={{0,16},{1,17},{2,18},{3,19},{4,20},{5,21},{6,22},{7,23},{8,24},{9,... | collective-permute-start | bytes 245768 | tf_op jit(solution)/shard_map/ppermute | solution.py:476
  71.7 14.3 %all-to-all-start.1 = ((bf16[8,4,16,640]{3,2,1,0:T(8,128)(2,1)}), bf16[8,4,16,640]{3,2,1,0:T(8,128)(2,1)S(1)}, u32[]{:S(2)}, u32[]{:S(2)}) async-start(bf16[8,4,16,640]{3,2,1,0:T(8,128)(2,1)} %copy.20), calls=%async_computation.1 | async-start | bytes 1310720 | tf_op jit(solution)/shard_map/all_to_all | solution.py:479
  75.9 7.4 %collective-permute-start.19 = (bf16[1,16,2560]{2,1,0:T(8,128)(2,1)S(1)}, bf16[1,16,2560]{2,1,0:T(8,128)(2,1)S(1)}, u32[]{:S(2)}, u32[]{:S(2)}) collective-permute-start(bf16[1,16,2560]{2,1,0:T(8,128)(2,1)S(1)} %add_convert_fusion.7), channel_id=1, source_target_pairs={{0,16},{1,17},{2,18},{3,19},{4,20},{5,21},{6,22},{7,23},{8,24},{9,... | collective-permute-start | bytes 245768 | tf_op jit(solution)/shard_map/ppermute | solution.py:476
  86.0 5.7 %collective-permute-start.20 = (bf16[2,16,2560]{2,1,0:T(8,128)(2,1)S(1)}, bf16[2,16,2560]{2,1,0:T(8,128)(2,1)S(1)}, u32[]{:S(2)}, u32[]{:S(2)}) collective-permute-start(bf16[2,16,2560]{2,1,0:T(8,128)(2,1)S(1)} %pad_maximum_fusion.6), channel_id=1, source_target_pairs={{0,8},{1,9},{2,10},{3,11},{4,12},{5,13},{6,14},{7,15},{8,0},{9,1},... | collective-permute-start | bytes 491528 | tf_op jit(solution)/shard_map/ppermute | solution.py:476
  91.8 5.4 %collective-permute-start.21 = (bf16[4,16,1280]{2,1,0:T(8,128)(2,1)S(1)}, bf16[4,16,1280]{2,1,0:T(8,128)(2,1)S(1)}, u32[]{:S(2)}, u32[]{:S(2)}) collective-permute-start(bf16[4,16,1280]{2,1,0:T(8,128)(2,1)S(1)} %get-tuple-element.106), channel_id=1, source_target_pairs={{0,4},{1,5},{2,6},{3,7},{4,0},{5,1},{6,2},{7,3},{8,12},{9,13},{10,... | collective-permute-start | bytes 491528 | tf_op jit(solution)/shard_map/ppermute | solution.py:476
  92.9 6.1 %collective-permute-start.24 = (bf16[4,16,1280]{2,1,0:T(8,128)(2,1)S(1)}, bf16[4,16,1280]{2,1,0:T(8,128)(2,1)S(1)}, u32[]{:S(2)}, u32[]{:S(2)}) collective-permute-start(bf16[4,16,1280]{2,1,0:T(8,128)(2,1)S(1)} %get-tuple-element.105), channel_id=1, source_target_pairs={{0,2},{1,3},{2,0},{3,1},{4,6},{5,7},{6,4},{7,5},{8,10},{9,11},{10,... | collective-permute-start | bytes 491528 | tf_op jit(solution)/shard_map/ppermute | solution.py:476
  97.3 8.0 %collective-permute-start.22 = (bf16[8,16,1280]{2,1,0:T(8,128)(2,1)S(1)}, bf16[8,16,1280]{2,1,0:T(8,128)(2,1)S(1)}, u32[]{:S(2)}, u32[]{:S(2)}) collective-permute-start(bf16[8,16,1280]{2,1,0:T(8,128)(2,1)S(1)} %pad_maximum_fusion.3), channel_id=1, source_target_pairs={{0,2},{1,3},{2,0},{3,1},{4,6},{5,7},{6,4},{7,5},{8,10},{9,11},{10,... | collective-permute-start | bytes 983048 | tf_op jit(solution)/shard_map/ppermute | solution.py:476
  99.1 7.1 %collective-permute-start.25 = (bf16[8,16,1280]{2,1,0:T(8,128)(2,1)S(1)}, bf16[8,16,1280]{2,1,0:T(8,128)(2,1)S(1)}, u32[]{:S(2)}, u32[]{:S(2)}) collective-permute-start(bf16[8,16,1280]{2,1,0:T(8,128)(2,1)S(1)} %pad_maximum_fusion.4), channel_id=1, source_target_pairs={{0,4},{1,5},{2,6},{3,7},{4,0},{5,1},{6,2},{7,3},{8,12},{9,13},{10,... | collective-permute-start | bytes 983048 | tf_op jit(solution)/shard_map/ppermute | solution.py:476
  105.4 3.0 %collective-permute-start.23 = (bf16[16,16,1280]{2,1,0:T(8,128)(2,1)S(1)}, bf16[16,16,1280]{2,1,0:T(8,128)(2,1)S(1)}, u32[]{:S(2)}, u32[]{:S(2)}) collective-permute-start(bf16[16,16,1280]{2,1,0:T(8,128)(2,1)S(1)} %pad_maximum_fusion.left_ref), channel_id=1, source_target_pairs={{0,1},{1,0},{2,3},{3,2},{4,5},{5,4},{6,7},{7,6},{8,9},{9,8},{10,11... | collective-permute-start | bytes 1966088 | tf_op jit(solution)/shard_map/ppermute | solution.py:476
  106.3 2.2 %collective-permute-start.26 = (bf16[16,16,1280]{2,1,0:T(8,128)(2,1)S(1)}, bf16[16,16,1280]{2,1,0:T(8,128)(2,1)S(1)}, u32[]{:S(2)}, u32[]{:S(2)}) collective-permute-start(bf16[16,16,1280]{2,1,0:T(8,128)(2,1)S(1)} %pad_maximum_fusion.1.right_ref), channel_id=1, source_target_pairs={{0,1},{1,0},{2,3},{3,2},{4,5},{5,4},{6,7},{7,6},{8,9},{9,8},{10,11... | collective-permute-start | bytes 1966088 | tf_op jit(solution)/shard_map/ppermute | solution.py:476
